TPU v7x, 32 devices: a whole 2x2x4 slice. The times are simulated.
32 devices in a mesh: col: 8 (over y, x, core), row: 4 (over z).
Axes of the slice: x: 2, y: 2, z: 4, core: 2. Of those that a mesh axis runs over, the one named last changes fastest.
Arguments:
- features: bfloat16 [4096, 256], P(('col', 'row')), may hold values from -6 to 6
- weight: bfloat16 [256, 256], replicated, may hold values from -0.375 to 0.375
- bias_term: float32 [256], replicated, may hold values from -3 to 3
- cotangent: bfloat16 [4096, 256], P(('row', 'col')), may hold values from -6 to 6
- tile_values: bfloat16 [4, 8, 32, 128, 128], P('row', 'col'), may hold values from 0 to 0.07980869
- tile_row: int32 [4, 8, 32], P('row', 'col'), may hold values from 0 to 7
- tile_col: int32 [4, 8, 32], P('row', 'col'), may hold values from 0 to 3
- tile_count: int32 [4, 8], P('row', 'col'), may hold values from 6 to 32, as said below
Outputs:
- hidden_out: bfloat16 [4096, 256], P(('row', 'col'))
- grad_features: bfloat16 [4096, 256], P(('col', 'row'))
- grad_weight: float32 [256, 256], replicated
- grad_bias: float32 [256], replicated
Inputs may be any that keep to these rules, and one draw needn't show every extreme that they name: Live slots are the first tile_count[r, c] slots of a grid place; at least 6 of them, and all 32 on some grid place. Slots past the count are ignored. `tile_row`: A grid place's live slots may name the same tile position more than once; their values add.
All inputs are finite; a program needn't handle non-finite values.
Results may differ from a plain program's by a relative error of at most 0.02.
Values may be sent and summed in bfloat16 or wider, within the bound.
No kernel may reach another device: no remote copies, remote signals or barrier semaphores. Data moves between devices by JAX's collectives and lax.ppermute only.
A program may use at most 64 MiB of HBM per device.

v0:
```python
import jax
import jax.numpy as jnp
from jax import lax
from jax.sharding import PartitionSpec as P


def slot_sum(tile_block, slab_rows, target_idx, live_mask, groups, transposed):
    einsum_form = "sji,sjc->sic" if transposed else "sij,sjc->sic"
    products = jnp.einsum(einsum_form, tile_block, slab_rows, preferred_element_type=jnp.float32)
    products = products * live_mask[:, None, None].astype(jnp.float32)
    empty = jnp.zeros((groups,) + products.shape[1:], jnp.float32)
    return empty.at[target_idx].add(products)


def tile_products(tile_block, slab_source, source_idx, target_idx, live_count, groups, transposed):
    half_slots = tile_block.shape[0] // 2
    tile_size = tile_block.shape[1]
    feat_width = slab_source.shape[-1]

    def advance(running, offset):
        block_tiles = lax.dynamic_slice_in_dim(tile_block, offset, half_slots, 0)
        block_source = lax.dynamic_slice_in_dim(source_idx, offset, half_slots, 0)
        block_target = lax.dynamic_slice_in_dim(target_idx, offset, half_slots, 0)
        live_mask = offset + jnp.arange(half_slots, dtype=jnp.int32) < live_count
        slab_rows = slab_source[block_source]
        return (
            running + slot_sum(block_tiles, slab_rows, block_target, live_mask, groups, transposed),
            None,
        )

    running, _ = lax.scan(
        advance,
        jnp.zeros((groups, tile_size, feat_width), jnp.float32),
        jnp.arange(2, dtype=jnp.int32) * half_slots,
    )
    return running.reshape(groups * tile_size, feat_width)


def activate(inputs):
    return jax.nn.gelu(inputs, approximate=True)


def gelu_grad(pre_act, cot_rows):
    _, pull_back = jax.vjp(activate, pre_act)
    return pull_back(cot_rows.astype(jnp.float32))[0].astype(jnp.bfloat16)


def local(features, weight, bias_term, cotangent, tile_values, tile_row, tile_col, tile_count):
    row_count = lax.axis_size("row")
    col_count = lax.axis_size("col")
    tile_size = features.shape[0]
    tile_block = tile_values[0, 0]
    row_tiles = tile_row[0, 0]
    col_tiles = tile_col[0, 0]
    live_count = tile_count[0, 0]
    column_block = lax.all_gather(features, "row", axis=0, tiled=True)
    slab_source = column_block.reshape(row_count, tile_size, column_block.shape[1])
    partial_value = tile_products(
        tile_block, slab_source, col_tiles, row_tiles, live_count, col_count, False
    )
    aggregated = lax.psum_scatter(
        partial_value.astype(jnp.bfloat16), "col", scatter_dimension=0, tiled=True
    )
    pre_act = jnp.dot(aggregated, weight, preferred_element_type=jnp.float32) + bias_term
    own_grad = gelu_grad(pre_act, cotangent)
    grad_block = lax.all_gather(own_grad, "col", axis=0, tiled=True)
    hidden_out = activate(pre_act).astype(jnp.bfloat16)
    back_source = grad_block.reshape(col_count, tile_size, grad_block.shape[1])
    back_partial = tile_products(
        tile_block, back_source, row_tiles, col_tiles, live_count, row_count, True
    )
    back_agg = lax.psum_scatter(
        back_partial.astype(jnp.bfloat16), "row", scatter_dimension=0, tiled=True
    )
    grad_features = jnp.einsum(
        "nh,fh->nf", back_agg, weight, preferred_element_type=jnp.float32
    ).astype(jnp.bfloat16)
    weight_term = jnp.einsum("nf,nh->fh", aggregated, own_grad, preferred_element_type=jnp.float32)
    bias_grad_term = jnp.sum(own_grad.astype(jnp.float32), axis=0)
    weight_sum, bias_sum = lax.psum((weight_term, bias_grad_term), ("col", "row"))
    factor_root = (tile_size * row_count * col_count) ** (-0.5)
    return (hidden_out, grad_features, weight_sum * factor_root, bias_sum * factor_root)


def solution(mesh):
    return jax.shard_map(
        local,
        mesh=mesh,
        in_specs=(
            P(("col", "row"), None),
            P(),
            P(),
            P(("row", "col"), None),
            P("row", "col", None, None, None),
            P("row", "col", None),
            P("row", "col", None),
            P("row", "col"),
        ),
        out_specs=(P(("row", "col"), None), P(("col", "row"), None), P(), P()),
        check_vma=False,
    )
```

profile of v0, /device:TPU:0, one launch (start us, length us, event | category | flops | bytes accessed | tf_op | source)
XLA Modules:
  0.0 248.1 jit_solution(397467581277950424)
XLA Ops:
  7.2 15.8 %all_gather.6 = bf16[512,256]{1,0:T(8,128)(2,1)S(1)} all-gather(bf16[128,256]{1,0:T(8,128)(2,1)} %param.12), channel_id=1, replica_groups=mesh['col'=8,'row'=4] {'row'}, dimensions={0}, use_global_device_ids=true | all-gather | bytes 327680 | tf_op jit(solution)/shard_map/all_gather | solution.py:56
  23.2 20.5 %while.20 = (s32[]{:T(128)}, f32[8,128,256]{2,1,0:T(8,128)S(1)}, s32[2]{0:T(128)S(1)}, s32[32]{0:T(128)}, bf16[32,128,128]{2,1,0:T(8,128)(2,1)}, /*index=5*/s32[...) while((s32[]{:T(128)}, f32[8,128,256]{2,1,0:T(8,128)S(1)}, ...), condition=%wide.region_2.3_spmd, body=%wide.region_0.2_spmd.sunk | while | flops 135267472 | bytes 12063475 | solution.py:31
  25.7 0.8 compare_select_fusion.6
  26.5 1.6 gather_fusion
  28.1 1.3 compare_convert_fusion.4
  29.4 1.8 convolution_multiply_fusion.4
  31.2 2.2 scatter_fusion
  35.9 0.8 compare_select_fusion.6
  36.7 1.6 gather_fusion
  38.3 1.3 compare_convert_fusion.4
  39.6 1.8 convolution_multiply_fusion.4
  41.4 2.2 scatter_fusion
  43.7 0.9 convert_element_type.43
  45.1 1.3 copy.12
  46.4 34.0 %reduce-scatter.3.cloned.1.call-done = bf16[128,256]{1,0:T(8,128)(2,1)} async-done(((bf16[1024,256]{1,0:T(8,128)(2,1)}), bf16[128,256]{1,0:T(8,128)(2,1)}) %reduce-scatter.3.cloned.1.call-update) | async-done | bytes 65552 | tf_op jit(solution)/shard_map/reduce_scatter | solution.py:61
  80.4 1.7 convert_reduce_fusion
  82.1 9.8 %all_gather.7 = bf16[1024,256]{1,0:T(8,128)(2,1)S(1)} all-gather(bf16[128,256]{1,0:T(8,128)(2,1)S(1)} %get-tuple-element.131), channel_id=1, replica_groups=mesh['col'=8,'row'=4] {'col'}, dimensions={0}, use_global_device_ids=true | all-gather | bytes 589824 | tf_op jit(solution)/shard_map/all_gather | solution.py:66
  91.9 1.8 fusion.15
  93.8 19.2 %while.21 = (s32[]{:T(128)}, f32[4,128,256]{2,1,0:T(8,128)S(1)}, s32[2]{0:T(128)S(1)}, s32[32]{0:T(128)S(1)}, bf16[32,128,128]{1,2,0:T(8,128)(2,1)}, /*index=5*/...) while((s32[]{:T(128)}, f32[4,128,256]{2,1,0:T(8,128)S(1)}, ...), condition=%wide.region_6.7_spmd, body=%wide.region_4.6_spmd.sunk | while | flops 135267472 | bytes 12063475 | solution.py:31
  96.4 1.6 gather_fusion.1
  98.1 1.3 compare_convert_fusion.5
  99.4 1.8 convolution_multiply_fusion.5
  101.2 2.2 scatter_fusion.1
  106.0 1.6 gather_fusion.1
  107.7 1.3 compare_convert_fusion.5
  109.0 1.8 convolution_multiply_fusion.5
  110.8 2.2 scatter_fusion.1
  113.7 39.4 %psum.15 = f32[256]{0:T(256)S(1)} all-reduce(f32[256]{0:T(256)S(1)} %get-tuple-element.130), channel_id=1, replica_groups=mesh['col'=8,'row'=4] {'col','row'}, use_global_device_ids=true, to_apply=%region_10.11 | all-reduce | flops 256 | bytes 2048 | tf_op jit(solution)/shard_map/psum | solution.py:80
  153.7 65.2 %all-reduce.2.cloned.1.call-done = f32[256,256]{1,0:T(8,128)} async-done(((f32[256,256]{1,0:T(8,128)}), f32[256,256]{1,0:T(8,128)}) %all-reduce.2.cloned.1.call-update) | async-done | bytes 262160 | tf_op jit(solution)/shard_map/psum | solution.py:80
  218.9 1.7 broadcast_multiply_fusion
  220.5 19.4 %reduce-scatter.5.cloned.1.call-done = bf16[128,256]{1,0:T(8,128)(2,1)} async-done(((bf16[512,256]{1,0:T(8,128)(2,1)}), bf16[128,256]{1,0:T(8,128)(2,1)}) %reduce-scatter.5.cloned.1.call-update) | async-done | bytes 65552 | tf_op jit(solution)/shard_map/reduce_scatter | solution.py:72
  239.9 1.7 convolution_convert_fusion
  (33 shorter events, 4.6 us)
Async XLA Ops:
  7.2 73.2 %copy-start = (bf16[256,256]{1,0:T(8,128)(2,1)S(1)}, bf16[256,256]{1,0:T(8,128)(2,1)}, u32[]{:S(2)}) copy-start(bf16[256,256]{1,0:T(8,128)(2,1)} %param.13) | copy-start | bytes 393220
  7.2 73.2 %reduce-scatter.3.cloned.1.call-start = ((), (), s32[]{:S(2)}) async-start(), calls=%async_computation.2 | async-start | bytes 589824 | tf_op jit(solution)/shard_map/reduce_scatter | solution.py:61
  43.7 1.4 copy-start.1
  43.7 36.7 %copy-start.4 = (bf16[128,256]{1,0:T(8,128)(2,1)S(1)}, bf16[128,256]{1,0:T(8,128)(2,1)}, u32[]{:S(2)}) copy-start(bf16[128,256]{1,0:T(8,128)(2,1)} %param.15) | copy-start | bytes 196612
  43.7 36.7 %copy-start.5 = (f32[256]{0:T(256)S(1)}, f32[256]{0:T(256)}, u32[]{:S(2)}) copy-start(f32[256]{0:T(256)} %param.14) | copy-start | bytes 3076
  44.6 174.3 %all-reduce.2.cloned.1.call-start = ((), (), s32[]{:S(2)}) async-start(), calls=%async_computation.4 | async-start | bytes 524288 | tf_op jit(solution)/shard_map/psum | solution.py:80
  45.1 48.7 %copy-start.2 = (s32[32]{0:T(128)S(1)}, s32[32]{0:T(128)}, u32[]{:S(2)}) copy-start(s32[32]{0:T(128)} %get-tuple-element.322) | copy-start | bytes 388
  45.1 48.7 %copy-start.3 = (s32[32]{0:T(128)S(1)}, s32[32]{0:T(128)}, u32[]{:S(2)}) copy-start(s32[32]{0:T(128)} %get-tuple-element.323) | copy-start | bytes 388
  93.7 146.3 %reduce-scatter.5.cloned.1.call-start = ((), (), s32[]{:S(2)}) async-start(), calls=%async_computation.3 | async-start | bytes 327680 | tf_op jit(solution)/shard_map/reduce_scatter | solution.py:72
Sparse Core Ops, SparseCore 0:
  44.7 35.6 reduce-scatter.2
  93.8 125.0 all-reduce.1
  221.2 18.6 reduce-scatter.4
where the time goes:
time: 249 us; the launch traced here: 248 us
  waiting for transfers between devices  119 us (48%)
  blocking collectives  65 us (26%)
  other arithmetic  19.5 us (8%)
  between operations  13.8 us (6%)
  matrix products  12.4 us (5%)
  local copies, waits for them, and re-layouts  10.8 us (4%)
  loops' own time  7.93 us (3%)
    psum x1, waiting for transfers between devices, local(): lax.psum((weight_term, bias_grad_term), ('col', 'row'))  65.2 us
    psum x1, blocking collectives, local(): lax.psum((weight_term, bias_grad_term), ('col', 'row'))  39.4 us
    reduce_scatter x1, waiting for transfers between devices, local(): lax.psum_scatter(partial_value.astype(jnp.bfloat16), 'col', scatter_dimen...  34 us
    reduce_scatter x1, waiting for transfers between devices, local(): lax.psum_scatter(back_partial.astype(jnp.bfloat16), 'row', scatter_dimens...  19.4 us
    all_gather x1, blocking collectives, local(): column_block = lax.all_gather(features, 'row', axis=0, tiled=True)  15.8 us
    all_gather x1, blocking collectives, local(): grad_block = lax.all_gather(own_grad, 'col', axis=0, tiled=True)  9.76 us
    scatter-add x4, other arithmetic, slot_sum(): return empty.at[target_idx].add(products)  8.77 us
    another operation x2, loops' own time, tile_products(): lax.scan(advance, jnp.zeros((groups, tile_size, feat_width), jnp.float32)...  7.93 us
  transfers between devices with their start and end apart: 3, of which 3 were waited for; matrix products, arithmetic and copies ran while one was open for 8% of the time, Pallas kernels for 0%

commit v1 on v0

v1 whole, which is shorter than its diff:
```python
import functools

import jax
import jax.numpy as jnp
from jax import lax
from jax.experimental import pallas as pl
from jax.experimental.pallas import tpu as pltpu
from jax.sharding import PartitionSpec as P

F32 = jnp.float32
BF16 = jnp.bfloat16
ROOT_2_OVER_PI = 0.7978845608028654
CUBIC = 0.044715
VMEM_LIMIT = 48 * 1024 * 1024

VMEM_SPEC = pl.BlockSpec(memory_space=pltpu.VMEM)
SMEM_SPEC = pl.BlockSpec(memory_space=pltpu.SMEM)


def call(kernel, out_shape, in_specs, scratch, flops, moved):
    return pl.pallas_call(
        kernel,
        out_shape=out_shape,
        in_specs=in_specs,
        out_specs=jax.tree.map(lambda _: VMEM_SPEC, out_shape),
        scratch_shapes=scratch,
        compiler_params=pltpu.CompilerParams(vmem_limit_bytes=VMEM_LIMIT),
        cost_estimate=pl.CostEstimate(flops=flops, bytes_accessed=moved, transcendentals=0),
    )


def add_slots(count, source_idx, target_idx, tiles_ref, source_ref, acc_ref, contract):
    slots, tile = tiles_ref.shape[0], tiles_ref.shape[1]
    group = 4
    acc_ref[...] = jnp.zeros_like(acc_ref)

    def body(step, carry):
        first = step * group
        products = []
        for k in range(group):
            slot = first + k
            rows = source_ref[pl.ds(pl.multiple_of(source_idx[slot] * tile, tile), tile), :]
            product = lax.dot_general(
                tiles_ref[slot], rows, (((contract,), (0,)), ((), ())), preferred_element_type=F32
            )
            products.append(jnp.where(slot < count, product, 0.0))
        for k in range(group):
            slot = first + k
            place = jnp.where(slot < count, target_idx[slot], 0)
            where = pl.ds(pl.multiple_of(place * tile, tile), tile)
            acc_ref[where, :] += products[k]
        return carry

    lax.fori_loop(0, (count + group - 1) // group, body, 0)


def forward_kernel(count_ref, row_ref, col_ref, tiles_ref, source_ref, out_ref, acc_ref):
    add_slots(count_ref[0], col_ref, row_ref, tiles_ref, source_ref, acc_ref, 1)
    out_ref[...] = acc_ref[...].astype(BF16)


def middle_kernel(parts_ref, weight_ref, bias_ref, cot_ref, hidden_ref, both_ref):
    total = parts_ref[0].astype(F32)
    for k in range(1, parts_ref.shape[0]):
        total += parts_ref[k].astype(F32)
    aggregated = total.astype(BF16)
    v = jnp.dot(aggregated, weight_ref[...], preferred_element_type=F32) + bias_ref[...]
    square = v * v
    t = jnp.tanh(ROOT_2_OVER_PI * (v + CUBIC * (square * v)))
    half = 0.5 * (1.0 + t)
    hidden_ref[...] = (v * half).astype(BF16)
    slope = half + 0.5 * v * (1.0 - t * t) * (ROOT_2_OVER_PI * (1.0 + 3.0 * CUBIC * square))
    width = v.shape[1]
    both_ref[:, :width] = (cot_ref[...].astype(F32) * slope).astype(BF16)
    both_ref[:, width:] = aggregated


def backward_kernel(
    me_ref, count_ref, row_ref, col_ref, tiles_ref, both_ref, out_ref, acc_ref, weight_acc, *, share
):
    tile = tiles_ref.shape[1]
    width = out_ref.shape[2]
    grad_ref = both_ref.at[:, :width]
    add_slots(count_ref[0], row_ref, col_ref, tiles_ref, grad_ref, acc_ref, 0)
    grad = both_ref[:, :width]
    weight_acc[...] = lax.dot_general(
        both_ref[:, width:], grad, (((0,), (0,)), ((), ())), preferred_element_type=F32
    )
    mine = weight_acc[pl.ds(pl.multiple_of(me_ref[0] * share, share), share), :]
    bias = jnp.sum(grad.astype(F32), axis=0, keepdims=True)
    bias_high = bias.astype(BF16).astype(F32)
    rest = out_ref.shape[1] - tile - share
    extra = lax.broadcasted_iota(jnp.int32, (rest, width), 0)
    tail = jnp.where(extra == 0, bias_high, jnp.where(extra == 1, bias - bias_high, 0.0))
    tail = jnp.concatenate([mine, tail], axis=0).astype(BF16)
    for k in range(out_ref.shape[0]):
        out_ref[k, :tile, :] = acc_ref[k * tile : (k + 1) * tile, :].astype(BF16)
        out_ref[k, tile:, :] = tail


def final_kernel(parts_ref, weight_ref, features_ref, share_ref, bias_ref, *, factor, tile):
    total = parts_ref[0].astype(F32)
    for k in range(1, parts_ref.shape[0]):
        total += parts_ref[k].astype(F32)
    features_ref[...] = lax.dot_general(
        total[:tile].astype(BF16),
        weight_ref[...],
        (((1,), (1,)), ((), ())),
        preferred_element_type=F32,
    ).astype(BF16)
    share = share_ref.shape[0]
    share_ref[...] = total[tile : tile + share] * factor
    bias_ref[...] = (total[tile + share : tile + share + 1] + total[tile + share + 1 : tile + share + 2]) * factor


def local(features, weight, bias_term, cotangent, tile_values, tile_row, tile_col, tile_count):
    row_count = lax.axis_size("row")
    col_count = lax.axis_size("col")
    tile, width = features.shape
    hidden = weight.shape[1]
    slots = tile_values.shape[2]
    tiles = tile_values.reshape(slots, tile, tile)
    rows = tile_row.reshape(slots)
    cols = tile_col.reshape(slots)
    count = tile_count.reshape(1)
    bias_row = bias_term.reshape(1, hidden)
    slot_flops = 2 * slots * tile * tile

    column_block = lax.all_gather(features, "row", axis=0, tiled=True)
    partial_value = call(
        forward_kernel,
        jax.ShapeDtypeStruct((col_count * tile, width), BF16),
        [SMEM_SPEC] * 3 + [VMEM_SPEC] * 2,
        [pltpu.VMEM((col_count * tile, width), F32)],
        slot_flops * width,
        tiles.size * 2,
    )(count, rows, cols, tiles, column_block)
    parts = lax.all_to_all(
        partial_value.reshape(col_count, tile, width), "col", split_axis=0, concat_axis=0
    )
    hidden_out, both = call(
        middle_kernel,
        (
            jax.ShapeDtypeStruct((tile, hidden), BF16),
            jax.ShapeDtypeStruct((tile, hidden + width), BF16),
        ),
        [VMEM_SPEC] * 4,
        [],
        2 * tile * width * hidden,
        parts.size * 2,
    )(parts, weight, bias_row, cotangent)
    both_block = lax.all_gather(both, "col", axis=0, tiled=True)

    share = width // col_count
    extra = -(-(share + 2) // 16) * 16
    me = lax.axis_index("col").astype(jnp.int32).reshape(1)
    back = call(
        functools.partial(backward_kernel, share=share),
        jax.ShapeDtypeStruct((row_count, tile + extra, hidden), BF16),
        [SMEM_SPEC] * 4 + [VMEM_SPEC] * 2,
        [
            pltpu.VMEM((row_count * tile, hidden), F32),
            pltpu.VMEM((width, hidden), F32),
        ],
        slot_flops * hidden,
        tiles.size * 2,
    )(me, count, rows, cols, tiles, both_block)
    back_parts = lax.all_to_all(back, "row", split_axis=0, concat_axis=0)
    factor = (tile * row_count * col_count) ** (-0.5)
    grad_features, weight_share, grad_bias = call(
        functools.partial(final_kernel, factor=factor, tile=tile),
        (
            jax.ShapeDtypeStruct((tile, width), BF16),
            jax.ShapeDtypeStruct((share, hidden), F32),
            jax.ShapeDtypeStruct((1, hidden), F32),
        ),
        [VMEM_SPEC] * 2,
        [],
        2 * tile * width * hidden,
        back.size * 2,
    )(back_parts, weight)
    grad_weight = lax.all_gather(weight_share, "col", axis=0, tiled=True)
    return hidden_out, grad_features, grad_weight, grad_bias.reshape(hidden)


def solution(mesh):
    return jax.shard_map(
        local,
        mesh=mesh,
        in_specs=(
            P(("col", "row"), None),
            P(),
            P(),
            P(("row", "col"), None),
            P("row", "col", None, None, None),
            P("row", "col", None),
            P("row", "col", None),
            P("row", "col"),
        ),
        out_specs=(P(("row", "col"), None), P(("col", "row"), None), P(), P()),
        check_vma=False,
    )
```

time: 249 us -> 103 us (0.41)
  waiting for transfers between devices: 119 us -> 23.1 us
  other arithmetic: 19.5 us -> 0 us
  matrix products: 12.4 us -> 0 us
  blocking collectives: 65 us -> 55.7 us
  loops' own time: 7.93 us -> 0 us
  local copies, waits for them, and re-layouts: 10.8 us -> 4.51 us
  Pallas kernels: 0 us -> 4.35 us
    psum x1 -> x0, waiting for transfers between devices: 65.2 us -> none  [local(): lax.psum((weight_term, bias_grad_term), ('col', 'row'))]
    reduce_scatter x2 -> x0, waiting for transfers between devices: 53.4 us -> none  [the longest x1 34 us: local(): lax.psum_scatter(partial_value.astype(jnp.bfloat16), 'col', scatter_dimen...]
    psum x1 -> x0, blocking collectives: 39.4 us -> none  [local(): lax.psum((weight_term, bias_grad_term), ('col', 'row'))]
    all_to_all x0 -> x2, blocking collectives: none -> 30.1 us  [the longest x1 16.2 us: local(): back_parts = lax.all_to_all(back, 'row', split_axis=0, concat_axis=0)]
    all_gather x0 -> x1, waiting for transfers between devices: none -> 23.1 us  [local(): both_block = lax.all_gather(both, 'col', axis=0, tiled=True)]
    dot_general x7 -> x0, matrix products: 12.4 us -> none  [the longest x4 7.26 us: slot_sum(): jnp.einsum(einsum_form, tile_block, slab_rows, preferred_element_type=jnp...]
    scatter-add x4 -> x0, other arithmetic: 8.77 us -> none  [slot_sum(): return empty.at[target_idx].add(products)]
    another operation x2 -> x0, loops' own time: 7.93 us -> none  [tile_products(): lax.scan(advance, jnp.zeros((groups, tile_size, feat_width), jnp.float32)...]
  transfers between devices with their start and end apart: 3 -> 1, of which waited for: 3 -> 1; matrix products, arithmetic and copies ran while one was open for 8% -> 0% of each run, Pallas kernels for 0% -> 0%
where the time goes in v1:
time: 103 us; the launch traced here: 102 us
  blocking collectives  55.7 us (54%)
  waiting for transfers between devices  23.1 us (22%)
  between operations  14.7 us (14%)
  local copies, waits for them, and re-layouts  4.51 us (4%)
  Pallas kernels  4.35 us (4%)
    all_gather x1, waiting for transfers between devices, local(): both_block = lax.all_gather(both, 'col', axis=0, tiled=True)  23.1 us
    all_to_all x1, blocking collectives, local(): back_parts = lax.all_to_all(back, 'row', split_axis=0, concat_axis=0)  16.2 us
    all_gather x1, blocking collectives, local(): column_block = lax.all_gather(features, 'row', axis=0, tiled=True)  15.8 us
    all_to_all x1, blocking collectives, local(): lax.all_to_all(partial_value.reshape(col_count, tile, width), 'col', spli...  13.9 us
    all_gather x1, blocking collectives, local(): grad_weight = lax.all_gather(weight_share, 'col', axis=0, tiled=True)  9.74 us
    unnamed x17, local copies, waits for them, and re-layouts  4.51 us
  transfers between devices with their start and end apart: 1, of which 1 were waited for; matrix products, arithmetic and copies ran while one was open for 0% of the time, Pallas kernels for 0%

profile of v1, /device:TPU:0, one launch (start us, length us, event | category | flops | bytes accessed | tf_op | source)
XLA Modules:
  0.0 102.4 jit_solution(9199669664892182572)
XLA Ops:
  7.2 0.0 all-gather.2.cloned.1.call-start
  7.9 15.8 %all_gather.9.source_ref = bf16[512,256]{1,0:T(8,128)(2,1)S(1)} all-gather(bf16[128,256]{1,0:T(8,128)(2,1)} %param.8), channel_id=1, replica_groups=mesh['col'=8,'row'=4] {'row'}, dimensions={0}, use_global_device_ids=true | all-gather | bytes 327680 | tf_op jit(solution)/shard_map/all_gather | solution.py:129
  23.7 0.0 copy-start.5
  23.7 0.0 copy-start.6
  23.7 0.7 copy-done.5
  24.4 0.0 copy-done.6
  24.4 0.0 copy-start
  24.4 1.2 %copy-done = bf16[1,1,32,128,128]{4,3,2,1,0:T(8,128)(2,1)S(1)} copy-done((bf16[1,1,32,128,128]{4,3,2,1,0:T(8,128)(2,1)S(1)}, bf16[1,1,32,128,128]{4,3,2,1,0:T(8,128)(2,1)}, u32[]{:S(2)}) %copy-start) | copy-done | bytes 1048600
  25.6 0.0 copy-start.3
  25.6 0.0 copy-start.4
  25.6 1.1 %shard_map.111 = bf16[1024,256]{1,0:T(8,128)(2,1)S(1)} custom-call(s32[1]{0:T(128)} %bitcast.8.count_ref, s32[32]{0:T(128)S(1)} %bitcast.13, s32[32]{0:T(128)S(1)} %bitcast.15, bf16[32,128,128]{2,1,0:T(8,128)(2,1)S(1)} %bitcast.10, bf16[512,256]{1,0:T(8,128)(2,1)S(1)} %all_gather.9.source_ref), custom_call_target="tpu_custom_call" | custom-call | flops 268435456 | bytes 1048576 | tf_op jit(solution)/shard_map/pallas_call | solution.py:130
  26.7 0.0 copy-start.1
  26.7 13.9 %all_to_all.10.parts_ref = bf16[8,128,256]{2,1,0:T(8,128)(2,1)S(1)} all-to-all(bf16[8,128,256]{2,1,0:T(8,128)(2,1)S(1)} %bitcast.12), channel_id=1, replica_groups=mesh['col'=8,'row'=4] {'col'}, dimensions={0} | all-to-all | bytes 1048576 | tf_op jit(solution)/shard_map/all_to_all | solution.py:138
  40.6 0.0 copy-start.7
  40.6 0.0 copy-done.3
  40.6 0.0 copy-done.4
  40.6 0.7 copy-done.7
  41.3 0.9 shard_map.112
  42.2 0.0 all-gather.2.cloned.1.call-update
  42.2 23.1 %all-gather.2.cloned.1.call-done.both_ref = bf16[1024,512]{1,0:T(8,128)(2,1)} async-done(((bf16[128,512]{1,0:T(8,128)(2,1)}), bf16[1024,512]{1,0:T(8,128)(2,1)}) %all-gather.2.cloned.1.call-update) | async-done | bytes 1048592 | tf_op jit(solution)/shard_map/all_gather | solution.py:152
  65.3 0.0 copy-done.1
  65.3 0.0 copy-start.2
  65.3 1.2 %copy-done.2 = bf16[1024,512]{1,0:T(8,128)(2,1)S(1)} copy-done((bf16[1024,512]{1,0:T(8,128)(2,1)S(1)}, bf16[1024,512]{1,0:T(8,128)(2,1)}, u32[]{:S(2)}) %copy-start.2) | copy-done | bytes 1048600
  66.5 1.5 %shard_map.113 = bf16[4,176,256]{2,1,0:T(8,128)(2,1)S(1)} custom-call(s32[1]{0:T(128)} %bitcast.6.me_ref, s32[1]{0:T(128)} %bitcast.9.count_ref, s32[32]{0:T(128)S(1)} %bitcast.14, s32[32]{0:T(128)S(1)} %bitcast.16, bf16[32,128,128]{2,1,0:T(8,128)(2,1)S(1)} %bitcast.11, bf16[1024,512]{1,0:T(8,128)(2,1)S(1)} %copy-done.2), custom_call_target="tpu_custom_call" | custom-call | flops 268435456 | bytes 1048576 | tf_op jit(solution)/shard_map/pallas_call | solution.py:157
  68.0 16.2 %all_to_all.11.parts_ref = bf16[4,176,256]{2,1,0:T(8,128)(2,1)S(1)} all-to-all(bf16[4,176,256]{2,1,0:T(8,128)(2,1)S(1)} %shard_map.113), channel_id=1, replica_groups=mesh['col'=8,'row'=4] {'row'}, dimensions={0} | all-to-all | bytes 720896 | tf_op jit(solution)/shard_map/all_to_all | solution.py:168
  84.2 0.8 shard_map.114
  85.1 9.7 %all_gather.11 = f32[256,256]{1,0:T(8,128)S(1)} all-gather(f32[32,256]{1,0:T(8,128)S(1)} %get-tuple-element.12), channel_id=1, replica_groups=mesh['col'=8,'row'=4] {'col'}, dimensions={0}, use_global_device_ids=true | all-gather | bytes 294912 | tf_op jit(solution)/shard_map/all_gather | solution.py:182
  94.8 0.7 copy.14
Async XLA Ops:
  7.2 58.1 %all-gather.2.cloned.1.call-start = ((), (), s32[]{:S(2)}) async-start(), calls=%async_computation.2 | async-start | bytes 1179648 | tf_op jit(solution)/shard_map/all_gather | solution.py:152
  23.7 0.7 copy-start.5
  23.7 0.7 copy-start.6
  24.4 1.2 %copy-start = (bf16[1,1,32,128,128]{4,3,2,1,0:T(8,128)(2,1)S(1)}, bf16[1,1,32,128,128]{4,3,2,1,0:T(8,128)(2,1)}, u32[]{:S(2)}) copy-start(bf16[1,1,32,128,128]{4,3,2,1,0:T(8,128)(2,1)} %param.12) | copy-start | bytes 3145732
  25.6 15.0 %copy-start.3 = (bf16[256,256]{1,0:T(8,128)(2,1)S(1)}, bf16[256,256]{1,0:T(8,128)(2,1)}, u32[]{:S(2)}) copy-start(bf16[256,256]{1,0:T(8,128)(2,1)} %weight_ref.3) | copy-start | bytes 393220
  25.6 15.0 %copy-start.4 = (bf16[128,256]{1,0:T(8,128)(2,1)S(1)}, bf16[128,256]{1,0:T(8,128)(2,1)}, u32[]{:S(2)}) copy-start(bf16[128,256]{1,0:T(8,128)(2,1)} %cot_ref.1) | copy-start | bytes 196612
  26.7 38.6 %copy-start.1 = (bf16[1,1,32,128,128]{4,3,2,1,0:T(8,128)(2,1)S(1)}, bf16[1,1,32,128,128]{4,3,2,1,0:T(8,128)(2,1)}, u32[]{:S(2)}) copy-start(bf16[1,1,32,128,128]{4,3,2,1,0:T(8,128)(2,1)} %param.12) | copy-start | bytes 3145732
  40.6 0.7 copy-start.7
  65.3 1.2 %copy-start.2 = (bf16[1024,512]{1,0:T(8,128)(2,1)S(1)}, bf16[1024,512]{1,0:T(8,128)(2,1)}, u32[]{:S(2)}) copy-start(bf16[1024,512]{1,0:T(8,128)(2,1)} %all-gather.2.cloned.1.call-done.both_ref) | copy-start | bytes 3145732
Sparse Core Ops, SparseCore 0:
  42.4 22.9 all-gather.1

commit v2 on v1

v2 whole, which is shorter than its diff:
```python
import functools

import jax
import jax.numpy as jnp
from jax import lax
from jax.experimental import pallas as pl
from jax.experimental.pallas import tpu as pltpu
from jax.sharding import PartitionSpec as P

F32 = jnp.float32
BF16 = jnp.bfloat16
ROOT_2_OVER_PI = 0.7978845608028654
CUBIC = 0.044715
VMEM_LIMIT = 48 * 1024 * 1024

VMEM_SPEC = pl.BlockSpec(memory_space=pltpu.VMEM)
SMEM_SPEC = pl.BlockSpec(memory_space=pltpu.SMEM)


def call(kernel, out_shape, in_specs, scratch, flops, moved):
    return pl.pallas_call(
        kernel,
        out_shape=out_shape,
        in_specs=in_specs,
        out_specs=jax.tree.map(lambda _: VMEM_SPEC, out_shape),
        scratch_shapes=scratch,
        compiler_params=pltpu.CompilerParams(vmem_limit_bytes=VMEM_LIMIT),
        cost_estimate=pl.CostEstimate(flops=flops, bytes_accessed=moved, transcendentals=0),
    )


def partner(index, k, count):
    if count & (count - 1) == 0:
        return index ^ k
    return (k - index) % count


def exchange(blocks, axis):
    count = len(blocks)
    received = []
    for k, block in enumerate(blocks):
        pairs = [(i, partner(i, k, count)) for i in range(count)]
        moves = any(i != j for i, j in pairs)
        received.append(lax.ppermute(block, axis, pairs) if moves else block)
    return received


def block_at(index, size):
    return pl.ds(pl.multiple_of(index * size, size), size)


def summed(refs, rows):
    total = refs[0][rows, :].astype(F32)
    for ref in refs[1:]:
        total += ref[rows, :].astype(F32)
    return total


def add_slots(count, source_idx, target_idx, tiles_ref, source_ref, acc_ref, contract):
    tile = tiles_ref.shape[1]
    group = 4
    acc_ref[...] = jnp.zeros_like(acc_ref)

    def body(step, carry):
        first = step * group
        products = []
        for k in range(group):
            slot = first + k
            rows = source_ref[block_at(source_idx[slot], tile), :]
            product = lax.dot_general(
                tiles_ref[slot], rows, (((contract,), (0,)), ((), ())), preferred_element_type=F32
            )
            products.append(jnp.where(slot < count, product, 0.0))
        for k in range(group):
            slot = first + k
            place = jnp.where(slot < count, target_idx[slot], 0)
            acc_ref[block_at(place, tile), :] += products[k]
        return carry

    lax.fori_loop(0, (count + group - 1) // group, body, 0)


def forward_kernel(me_ref, count_ref, row_ref, col_ref, tiles_ref, *refs, n_row, n_col):
    sources, outs, (source_ref, acc_ref) = refs[:n_row], refs[n_row:-2], refs[-2:]
    tile = tiles_ref.shape[1]
    for k, ref in enumerate(sources):
        source_ref[block_at(partner(me_ref[0], k, n_row), tile), :] = ref[...]
    add_slots(count_ref[0], col_ref, row_ref, tiles_ref, source_ref, acc_ref, 1)
    for k, ref in enumerate(outs):
        ref[...] = acc_ref[block_at(partner(me_ref[1], k, n_col), tile), :].astype(BF16)


def middle_kernel(me_ref, weight_ref, bias_ref, cot_ref, *refs, n_col, share):
    parts, (hidden_ref, *outs), weight_acc = refs[:n_col], refs[n_col:-1], refs[-1]
    tile, width = cot_ref.shape
    aggregated = summed(parts, slice(None)).astype(BF16)
    v = jnp.dot(aggregated, weight_ref[...], preferred_element_type=F32) + bias_ref[...]
    square = v * v
    t = jnp.tanh(ROOT_2_OVER_PI * (v + CUBIC * (square * v)))
    half = 0.5 * (1.0 + t)
    hidden_ref[...] = (v * half).astype(BF16)
    slope = half + 0.5 * v * (1.0 - t * t) * (ROOT_2_OVER_PI * (1.0 + 3.0 * CUBIC * square))
    grad = (cot_ref[...].astype(F32) * slope).astype(BF16)
    weight_acc[...] = lax.dot_general(
        aggregated, grad, (((0,), (0,)), ((), ())), preferred_element_type=F32
    )
    bias = jnp.sum(grad.astype(F32), axis=0, keepdims=True)
    high = bias.astype(BF16).astype(F32)
    rest = outs[0].shape[0] - tile - share
    line = lax.broadcasted_iota(jnp.int32, (rest, width), 0)
    tail = jnp.where(line == 0, high, jnp.where(line == 1, bias - high, 0.0))
    for k, ref in enumerate(outs):
        mine = weight_acc[block_at(partner(me_ref[1], k, n_col), share), :]
        ref[:tile, :] = grad
        ref[tile:, :] = jnp.concatenate([mine, tail], axis=0).astype(BF16)


def share_kernel(*refs, tile, share):
    parts, out_ref = refs[:-1], refs[-1]
    total = summed(parts, slice(tile, None))
    bias = total[share : share + 1] + total[share + 1 : share + 2]
    high = bias.astype(BF16).astype(F32)
    line = lax.broadcasted_iota(jnp.int32, total.shape, 0)
    total = jnp.where(line == share, high, jnp.where(line == share + 1, bias - high, total))
    out_ref[...] = total.astype(BF16)


def backward_kernel(me_ref, count_ref, row_ref, col_ref, tiles_ref, *refs, n_row, n_col):
    sources, outs, (source_ref, acc_ref) = refs[:n_col], refs[n_col:-2], refs[-2:]
    tile = tiles_ref.shape[1]
    for k, ref in enumerate(sources):
        source_ref[block_at(partner(me_ref[1], k, n_col), tile), :] = ref[:tile, :]
    add_slots(count_ref[0], row_ref, col_ref, tiles_ref, source_ref, acc_ref, 0)
    for k, ref in enumerate(outs):
        ref[...] = acc_ref[block_at(partner(me_ref[0], k, n_row), tile), :].astype(BF16)


def scale_kernel(*refs, factor):
    parts, (share_ref, bias_ref) = refs[:-2], refs[-2:]
    share = share_ref.shape[0]
    total = summed(parts, slice(None))
    share_ref[...] = total[:share] * factor
    bias_ref[...] = (total[share : share + 1] + total[share + 1 : share + 2]) * factor


def features_kernel(weight_ref, *refs):
    parts, out_ref = refs[:-1], refs[-1]
    out_ref[...] = lax.dot_general(
        summed(parts, slice(None)).astype(BF16),
        weight_ref[...],
        (((1,), (1,)), ((), ())),
        preferred_element_type=F32,
    ).astype(BF16)


def join_kernel(me_ref, *refs):
    parts, out_ref = refs[:-1], refs[-1]
    share = parts[0].shape[0]
    for k, ref in enumerate(parts):
        out_ref[block_at(partner(me_ref[1], k, len(parts)), share), :] = ref[...]


def local(features, weight, bias_term, cotangent, tile_values, tile_row, tile_col, tile_count):
    n_row = lax.axis_size("row")
    n_col = lax.axis_size("col")
    tile, width = features.shape
    hidden = weight.shape[1]
    slots = tile_values.shape[2]
    tiles = tile_values.reshape(slots, tile, tile)
    rows = tile_row.reshape(slots)
    cols = tile_col.reshape(slots)
    count = tile_count.reshape(1)
    bias_row = bias_term.reshape(1, hidden)
    me = jnp.stack([lax.axis_index("row"), lax.axis_index("col")]).astype(jnp.int32)
    slot_flops = 2 * slots * tile * tile
    share = width // n_col
    extra = -(-(share + 2) // 16) * 16

    def like(rows, columns, dtype=BF16):
        return jax.ShapeDtypeStruct((rows, columns), dtype)

    sources = exchange([features] * n_row, "row")
    partials = call(
        functools.partial(forward_kernel, n_row=n_row, n_col=n_col),
        [like(tile, width)] * n_col,
        [SMEM_SPEC] * 4 + [VMEM_SPEC] * (1 + n_row),
        [pltpu.VMEM((n_row * tile, width), BF16), pltpu.VMEM((n_col * tile, width), F32)],
        slot_flops * width,
        tiles.size * 2,
    )(me, count, rows, cols, tiles, *sources)
    parts = exchange(partials, "col")
    hidden_out, *blocks = call(
        functools.partial(middle_kernel, n_col=n_col, share=share),
        [like(tile, hidden)] + [like(tile + extra, hidden)] * n_col,
        [SMEM_SPEC] + [VMEM_SPEC] * (3 + n_col),
        [pltpu.VMEM((width, hidden), F32)],
        4 * tile * width * hidden,
        n_col * tile * width * 4,
    )(me, weight, bias_row, cotangent, *parts)
    blocks = exchange(blocks, "col")
    block_share = call(
        functools.partial(share_kernel, tile=tile, share=share),
        like(extra, hidden),
        [VMEM_SPEC] * n_col,
        [],
        n_col * extra * hidden,
        n_col * (tile + extra) * hidden * 2,
    )(*blocks)
    shares = exchange([block_share] * n_row, "row")
    backs = call(
        functools.partial(backward_kernel, n_row=n_row, n_col=n_col),
        [like(tile, hidden)] * n_row,
        [SMEM_SPEC] * 4 + [VMEM_SPEC] * (1 + n_col),
        [pltpu.VMEM((n_col * tile, hidden), BF16), pltpu.VMEM((n_row * tile, hidden), F32)],
        slot_flops * hidden,
        tiles.size * 2,
    )(me, count, rows, cols, tiles, *blocks)
    backs = exchange(backs, "row")
    factor = (tile * n_row * n_col) ** (-0.5)
    own_share, grad_bias = call(
        functools.partial(scale_kernel, factor=factor),
        (like(share, hidden, F32), like(1, hidden, F32)),
        [VMEM_SPEC] * n_row,
        [],
        n_row * extra * hidden,
        n_row * extra * hidden * 2,
    )(*shares)
    all_shares = exchange([own_share] * n_col, "col")
    grad_features = call(
        features_kernel,
        like(tile, width),
        [VMEM_SPEC] * (1 + n_row),
        [],
        2 * tile * width * hidden,
        n_row * tile * hidden * 2,
    )(weight, *backs)
    grad_weight = call(
        join_kernel,
        like(width, hidden, F32),
        [SMEM_SPEC] + [VMEM_SPEC] * n_col,
        [],
        0,
        width * hidden * 8,
    )(me, *all_shares)
    return hidden_out, grad_features, grad_weight, grad_bias.reshape(hidden)


def solution(mesh):
    return jax.shard_map(
        local,
        mesh=mesh,
        in_specs=(
            P(("col", "row"), None),
            P(),
            P(),
            P(("row", "col"), None),
            P("row", "col", None, None, None),
            P("row", "col", None),
            P("row", "col", None),
            P("row", "col"),
        ),
        out_specs=(P(("row", "col"), None), P(("col", "row"), None), P(), P()),
        check_vma=False,
    )
```

time: 103 us -> 66.6 us (0.65)
  blocking collectives: 55.7 us -> 0 us
  starting transfers between devices: 0.04 us -> 34 us
  between operations: 14.7 us -> 1.4 us
  Pallas kernels: 4.35 us -> 6.49 us
  local copies, waits for them, and re-layouts: 4.51 us -> 2.75 us
  waiting for transfers between devices: 23.1 us -> 22 us
    ppermute x0 -> x30, starting transfers between devices: none -> 34 us  [exchange(): received.append(lax.ppermute(block, axis, pairs) if moves else block)]
    all_to_all x2 -> x0, blocking collectives: 30.1 us -> none  [the longest x1 16.2 us: local(): back_parts = lax.all_to_all(back, 'row', split_axis=0, concat_axis=0)]
    all_gather x2 -> x0, blocking collectives: 25.6 us -> none  [the longest x1 15.8 us: local(): column_block = lax.all_gather(features, 'row', axis=0, tiled=True)]
    all_gather x1 -> x0, waiting for transfers between devices: 23.1 us -> none  [local(): both_block = lax.all_gather(both, 'col', axis=0, tiled=True)]
    ppermute x0 -> x30, waiting for transfers between devices: none -> 22 us  [exchange(): received.append(lax.ppermute(block, axis, pairs) if moves else block)]
    pallas_call x4 -> x7, Pallas kernels: 4.35 us -> 6.49 us  [the longest x1 1.45 us: local(): call(functools.partial(middle_kernel, n_col=n_col, share=share), [like(ti...]
    unnamed x17 -> x16, local copies, waits for them, and re-layouts: 4.51 us -> 2.75 us
  transfers between devices with their start and end apart: 1 -> 30, of which waited for: 1 -> 13; matrix products, arithmetic and copies ran while one was open for 0% -> 0% of each run, Pallas kernels for 0% -> 4%
where the time goes in v2:
time: 66.6 us; the launch traced here: 66.7 us
  starting transfers between devices  34 us (51%)
  waiting for transfers between devices  22 us (33%)
  Pallas kernels  6.49 us (10%)
  local copies, waits for them, and re-layouts  2.75 us (4%)
  between operations  1.4 us (2%)
    ppermute x30, starting transfers between devices, exchange(): received.append(lax.ppermute(block, axis, pairs) if moves else block)  34 us
    ppermute x30, waiting for transfers between devices, exchange(): received.append(lax.ppermute(block, axis, pairs) if moves else block)  22 us
    unnamed x16, local copies, waits for them, and re-layouts  2.75 us
    pallas_call x1, Pallas kernels, local(): call(functools.partial(middle_kernel, n_col=n_col, share=share), [like(ti...  1.45 us
  transfers between devices with their start and end apart: 30, of which 13 were waited for; matrix products, arithmetic and copies ran while one was open for 0% of the time, Pallas kernels for 4%

profile of v2, /device:TPU:0, one launch (start us, length us, event | category | flops | bytes accessed | tf_op | source)
XLA Modules:
  0.0 66.7 jit_solution(11392793351816156616)
XLA Ops:
  0.6 4.1 %collective-permute-start.1 = (bf16[128,256]{1,0:T(8,128)(2,1)}, bf16[128,256]{1,0:T(8,128)(2,1)S(1)}, u32[]{:S(2)}, u32[]{:S(2)}) collective-permute-start(bf16[128,256]{1,0:T(8,128)(2,1)} %refs_0_.1), channel_id=1, source_target_pairs={{0,2},{1,3},{2,0},{3,1},{4,6},{5,7},{6,4},{7,5},{8,10},{9,11},{10,... | collective-permute-start | bytes 196616 | tf_op jit(solution)/shard_map/ppermute | solution.py:44
  4.7 1.6 %collective-permute-start = (bf16[128,256]{1,0:T(8,128)(2,1)}, bf16[128,256]{1,0:T(8,128)(2,1)S(1)}, u32[]{:S(2)}, u32[]{:S(2)}) collective-permute-start(bf16[128,256]{1,0:T(8,128)(2,1)} %refs_0_.1), channel_id=1, source_target_pairs={{0,1},{1,0},{2,3},{3,2},{4,5},{5,4},{6,7},{7,6},{8,9},{9,8},{10,11... | collective-permute-start | bytes 196616 | tf_op jit(solution)/shard_map/ppermute | solution.py:44
  7.0 1.0 %collective-permute-done.1.refs_2_ = bf16[128,256]{1,0:T(8,128)(2,1)S(1)} collective-permute-done((bf16[128,256]{1,0:T(8,128)(2,1)}, bf16[128,256]{1,0:T(8,128)(2,1)S(1)}, u32[]{:S(2)}, u32[]{:S(2)}) %collective-permute-start.1) | collective-permute-done | bytes 65568 | tf_op jit(solution)/shard_map/ppermute | solution.py:44
  8.0 1.2 %collective-permute-done.refs_1_ = bf16[128,256]{1,0:T(8,128)(2,1)S(1)} collective-permute-done((bf16[128,256]{1,0:T(8,128)(2,1)}, bf16[128,256]{1,0:T(8,128)(2,1)S(1)}, u32[]{:S(2)}, u32[]{:S(2)}) %collective-permute-start) | collective-permute-done | bytes 65568 | tf_op jit(solution)/shard_map/ppermute | solution.py:44
  9.2 3.4 %collective-permute-done.2.refs_3_ = bf16[128,256]{1,0:T(8,128)(2,1)S(1)} collective-permute-done((bf16[128,256]{1,0:T(8,128)(2,1)}, bf16[128,256]{1,0:T(8,128)(2,1)S(1)}, u32[]{:S(2)}, u32[]{:S(2)}) %collective-permute-start.2) | collective-permute-done | bytes 65568 | tf_op jit(solution)/shard_map/ppermute | solution.py:44
  13.3 1.2 %copy-done = bf16[1,1,32,128,128]{4,3,2,1,0:T(8,128)(2,1)S(1)} copy-done((bf16[1,1,32,128,128]{4,3,2,1,0:T(8,128)(2,1)S(1)}, bf16[1,1,32,128,128]{4,3,2,1,0:T(8,128)(2,1)}, u32[]{:S(2)}) %copy-start) | copy-done | bytes 1048600
  14.5 0.8 %copy-done.3 = bf16[128,256]{1,0:T(8,128)(2,1)S(1)} copy-done((bf16[128,256]{1,0:T(8,128)(2,1)S(1)}, bf16[128,256]{1,0:T(8,128)(2,1)}, u32[]{:S(2)}) %copy-start.3) | copy-done | bytes 65560
  15.3 1.1 %shard_map.111 = (bf16[128,256]{1,0:T(8,128)(2,1)S(1)}, bf16[128,256]{1,0:T(8,128)(2,1)S(1)}, bf16[128,256]{1,0:T(8,128)(2,1)S(1)}, bf16[128,256]{1,0:T(8,128)(2...) custom-call(s32[2]{0:T(128)S(1)} %pad_add_fusion.me_ref, ...), custom_call_target="tpu_custom_call" | custom-call | flops 268435456 | bytes 1048576 | tf_op jit(solution)/shard_map/pallas_call | solution.py:183
  16.6 1.6 %collective-permute-start.4 = (bf16[128,256]{1,0:T(8,128)(2,1)S(1)}, bf16[128,256]{1,0:T(8,128)(2,1)S(1)}, u32[]{:S(2)}, u32[]{:S(2)}) collective-permute-start(bf16[128,256]{1,0:T(8,128)(2,1)S(1)} %get-tuple-element.29), channel_id=1, source_target_pairs={{0,8},{4,12},{8,0},{12,4},{16,24},{20,28},{24,16},{28,20},{1,9},{5... | collective-permute-start | bytes 196616 | tf_op jit(solution)/shard_map/ppermute | solution.py:44
  18.4 2.9 %collective-permute-start.6 = (bf16[128,256]{1,0:T(8,128)(2,1)S(1)}, bf16[128,256]{1,0:T(8,128)(2,1)S(1)}, u32[]{:S(2)}, u32[]{:S(2)}) collective-permute-start(bf16[128,256]{1,0:T(8,128)(2,1)S(1)} %get-tuple-element.31), channel_id=1, source_target_pairs={{0,16},{4,20},{8,24},{12,28},{16,0},{20,4},{24,8},{28,12},{1,17},{... | collective-permute-start | bytes 196616 | tf_op jit(solution)/shard_map/ppermute | solution.py:44
  21.4 1.5 %collective-permute-start.8 = (bf16[128,256]{1,0:T(8,128)(2,1)S(1)}, bf16[128,256]{1,0:T(8,128)(2,1)S(1)}, u32[]{:S(2)}, u32[]{:S(2)}) collective-permute-start(bf16[128,256]{1,0:T(8,128)(2,1)S(1)} %get-tuple-element.33), channel_id=1, source_target_pairs={{0,24},{4,28},{8,16},{12,20},{16,8},{20,12},{24,0},{28,4},{1,25},{... | collective-permute-start | bytes 196616 | tf_op jit(solution)/shard_map/ppermute | solution.py:44
  22.8 0.9 %collective-permute-start.9 = (bf16[128,256]{1,0:T(8,128)(2,1)S(1)}, bf16[128,256]{1,0:T(8,128)(2,1)S(1)}, u32[]{:S(2)}, u32[]{:S(2)}) collective-permute-start(bf16[128,256]{1,0:T(8,128)(2,1)S(1)} %get-tuple-element.34), channel_id=1, source_target_pairs={{0,28},{4,24},{8,20},{12,16},{16,12},{20,8},{24,4},{28,0},{1,29},{... | collective-permute-start | bytes 196616 | tf_op jit(solution)/shard_map/ppermute | solution.py:44
  23.9 4.4 %collective-permute-done.7.refs_5_ = bf16[128,256]{1,0:T(8,128)(2,1)S(1)} collective-permute-done((bf16[128,256]{1,0:T(8,128)(2,1)S(1)}, bf16[128,256]{1,0:T(8,128)(2,1)S(1)}, u32[]{:S(2)}, u32[]{:S(2)}) %collective-permute-start.7) | collective-permute-done | bytes 65568 | tf_op jit(solution)/shard_map/ppermute | solution.py:44
  28.4 1.4 %shard_map.112 = (bf16[128,256]{1,0:T(8,128)(2,1)}, bf16[176,256]{1,0:T(8,128)(2,1)S(1)}, bf16[176,256]{1,0:T(8,128)(2,1)S(1)}, bf16[176,256]{1,0:T(8,128)(2,1)S...) custom-call(s32[2]{0:T(128)S(1)} %pad_add_fusion.me_ref, ...), custom_call_target="tpu_custom_call" | custom-call | flops 33554432 | bytes 1048576 | tf_op jit(solution)/shard_map/pallas_call | solution.py:192
  29.9 1.2 %collective-permute-start.11 = (bf16[176,256]{1,0:T(8,128)(2,1)S(1)}, bf16[176,256]{1,0:T(8,128)(2,1)S(1)}, u32[]{:S(2)}, u32[]{:S(2)}) collective-permute-start(bf16[176,256]{1,0:T(8,128)(2,1)S(1)} %get-tuple-element.38), channel_id=1, source_target_pairs={{0,8},{4,12},{8,0},{12,4},{16,24},{20,28},{24,16},{28,20},{1,9},{5... | collective-permute-start | bytes 270344 | tf_op jit(solution)/shard_map/ppermute | solution.py:44
  31.7 1.4 %collective-permute-start.13 = (bf16[176,256]{1,0:T(8,128)(2,1)S(1)}, bf16[176,256]{1,0:T(8,128)(2,1)S(1)}, u32[]{:S(2)}, u32[]{:S(2)}) collective-permute-start(bf16[176,256]{1,0:T(8,128)(2,1)S(1)} %get-tuple-element.40), channel_id=1, source_target_pairs={{0,16},{4,20},{8,24},{12,28},{16,0},{20,4},{24,8},{28,12},{1,17},{... | collective-permute-start | bytes 270344 | tf_op jit(solution)/shard_map/ppermute | solution.py:44
  33.5 1.2 %collective-permute-start.15 = (bf16[176,256]{1,0:T(8,128)(2,1)S(1)}, bf16[176,256]{1,0:T(8,128)(2,1)S(1)}, u32[]{:S(2)}, u32[]{:S(2)}) collective-permute-start(bf16[176,256]{1,0:T(8,128)(2,1)S(1)} %get-tuple-element.42), channel_id=1, source_target_pairs={{0,24},{4,28},{8,16},{12,20},{16,8},{20,12},{24,0},{28,4},{1,25},{... | collective-permute-start | bytes 270344 | tf_op jit(solution)/shard_map/ppermute | solution.py:44
  34.6 0.8 %collective-permute-done.11.refs_2_ = bf16[176,256]{1,0:T(8,128)(2,1)S(1)} collective-permute-done((bf16[176,256]{1,0:T(8,128)(2,1)S(1)}, bf16[176,256]{1,0:T(8,128)(2,1)S(1)}, u32[]{:S(2)}, u32[]{:S(2)}) %collective-permute-start.11) | collective-permute-done | bytes 90144 | tf_op jit(solution)/shard_map/ppermute | solution.py:44
  36.2 0.9 %collective-permute-done.13.refs_4_ = bf16[176,256]{1,0:T(8,128)(2,1)S(1)} collective-permute-done((bf16[176,256]{1,0:T(8,128)(2,1)S(1)}, bf16[176,256]{1,0:T(8,128)(2,1)S(1)}, u32[]{:S(2)}, u32[]{:S(2)}) %collective-permute-start.13) | collective-permute-done | bytes 90144 | tf_op jit(solution)/shard_map/ppermute | solution.py:44
  37.1 4.9 %collective-permute-done.14.refs_5_ = bf16[176,256]{1,0:T(8,128)(2,1)S(1)} collective-permute-done((bf16[176,256]{1,0:T(8,128)(2,1)S(1)}, bf16[176,256]{1,0:T(8,128)(2,1)S(1)}, u32[]{:S(2)}, u32[]{:S(2)}) %collective-permute-start.14) | collective-permute-done | bytes 90144 | tf_op jit(solution)/shard_map/ppermute | solution.py:44
  42.5 1.2 %collective-permute-start.21 = (bf16[48,256]{1,0:T(8,128)(2,1)S(1)}, bf16[48,256]{1,0:T(8,128)(2,1)S(1)}, u32[]{:S(2)}, u32[]{:S(2)}) collective-permute-start(bf16[48,256]{1,0:T(8,128)(2,1)S(1)} %shard_map.115.refs_0_), channel_id=1, source_target_pairs={{0,2},{1,3},{2,0},{3,1},{4,6},{5,7},{6,4},{7,5},{8,10},{9,11},{10,... | collective-permute-start | bytes 73736 | tf_op jit(solution)/shard_map/ppermute | solution.py:44
  43.7 2.7 %collective-permute-start.20 = (bf16[48,256]{1,0:T(8,128)(2,1)S(1)}, bf16[48,256]{1,0:T(8,128)(2,1)S(1)}, u32[]{:S(2)}, u32[]{:S(2)}) collective-permute-start(bf16[48,256]{1,0:T(8,128)(2,1)S(1)} %shard_map.115.refs_0_), channel_id=1, source_target_pairs={{0,1},{1,0},{2,3},{3,2},{4,5},{5,4},{6,7},{7,6},{8,9},{9,8},{10,11... | collective-permute-start | bytes 73736 | tf_op jit(solution)/shard_map/ppermute | solution.py:44
  46.5 1.5 %collective-permute-done.22.refs_3_ = bf16[48,256]{1,0:T(8,128)(2,1)S(1)} collective-permute-done((bf16[48,256]{1,0:T(8,128)(2,1)S(1)}, bf16[48,256]{1,0:T(8,128)(2,1)S(1)}, u32[]{:S(2)}, u32[]{:S(2)}) %collective-permute-start.22) | collective-permute-done | bytes 24608 | tf_op jit(solution)/shard_map/ppermute | solution.py:44
  48.8 2.0 %collective-permute-start.28 = (f32[32,256]{1,0:T(8,128)S(1)}, f32[32,256]{1,0:T(8,128)S(1)}, u32[]{:S(2)}, u32[]{:S(2)}) collective-permute-start(f32[32,256]{1,0:T(8,128)S(1)} %get-tuple-element.48.refs_0_), channel_id=1, source_target_pairs={{0,24},{4,28},{8,16},{12,20},{16,8},{20,12},{24,0},{28,4},{1,25},{... | collective-permute-start | bytes 98312 | tf_op jit(solution)/shard_map/ppermute | solution.py:44
  50.9 1.5 %collective-permute-start.27 = (f32[32,256]{1,0:T(8,128)S(1)}, f32[32,256]{1,0:T(8,128)S(1)}, u32[]{:S(2)}, u32[]{:S(2)}) collective-permute-start(f32[32,256]{1,0:T(8,128)S(1)} %get-tuple-element.48.refs_0_), channel_id=1, source_target_pairs={{0,20},{4,16},{8,28},{12,24},{16,4},{20,0},{24,12},{28,8},{1,21},{... | collective-permute-start | bytes 98312 | tf_op jit(solution)/shard_map/ppermute | solution.py:44
  52.4 1.2 %shard_map.113 = (bf16[128,256]{1,0:T(8,128)(2,1)S(1)}, bf16[128,256]{1,0:T(8,128)(2,1)S(1)}, bf16[128,256]{1,0:T(8,128)(2,1)S(1)}, bf16[128,256]{1,0:T(8,128)(2,1)S(1)}) custom-call(s32[2]{0:T(128)S(1)} %pad_add_fusion.me_ref, s32[1]{0:T(128)} %bitcast.9.count_ref, s32[32]{0:T(128)S(1)} %bitcast.13, s32[32]{0:T(128)S(1)} %bitcast.15, ...), custom_call_target="tpu_custom_call" | custom-call | flops 268435456 | bytes 1048576 | tf_op jit(solution)/shard_map/pallas_call | solution.py:210
  53.6 2.6 %collective-permute-start.17 = (bf16[128,256]{1,0:T(8,128)(2,1)S(1)}, bf16[128,256]{1,0:T(8,128)(2,1)S(1)}, u32[]{:S(2)}, u32[]{:S(2)}) collective-permute-start(bf16[128,256]{1,0:T(8,128)(2,1)S(1)} %get-tuple-element.45), channel_id=1, source_target_pairs={{0,1},{1,0},{2,3},{3,2},{4,5},{5,4},{6,7},{7,6},{8,9},{9,8},{10,11... | collective-permute-start | bytes 196616 | tf_op jit(solution)/shard_map/ppermute | solution.py:44
  56.2 1.9 %collective-permute-start.26 = (f32[32,256]{1,0:T(8,128)S(1)}, f32[32,256]{1,0:T(8,128)S(1)}, u32[]{:S(2)}, u32[]{:S(2)}) collective-permute-start(f32[32,256]{1,0:T(8,128)S(1)} %get-tuple-element.48.refs_0_), channel_id=1, source_target_pairs={{0,16},{4,20},{8,24},{12,28},{16,0},{20,4},{24,8},{28,12},{1,17},{... | collective-permute-start | bytes 98312 | tf_op jit(solution)/shard_map/ppermute | solution.py:44
  58.2 2.4 %collective-permute-start.19 = (bf16[128,256]{1,0:T(8,128)(2,1)S(1)}, bf16[128,256]{1,0:T(8,128)(2,1)S(1)}, u32[]{:S(2)}, u32[]{:S(2)}) collective-permute-start(bf16[128,256]{1,0:T(8,128)(2,1)S(1)} %get-tuple-element.47), channel_id=1, source_target_pairs={{0,3},{1,2},{2,1},{3,0},{4,7},{5,6},{6,5},{7,4},{8,11},{9,10},{10,... | collective-permute-start | bytes 196616 | tf_op jit(solution)/shard_map/ppermute | solution.py:44
  61.9 2.7 %collective-permute-done.24.refs_2_ = f32[32,256]{1,0:T(8,128)S(1)} collective-permute-done((f32[32,256]{1,0:T(8,128)S(1)}, f32[32,256]{1,0:T(8,128)S(1)}, u32[]{:S(2)}, u32[]{:S(2)}) %collective-permute-start.24) | collective-permute-done | bytes 32800 | tf_op jit(solution)/shard_map/ppermute | solution.py:44
  64.6 1.3 %shard_map.117 = f32[256,256]{1,0:T(8,128)} custom-call(s32[2]{0:T(128)S(1)} %pad_add_fusion.me_ref, f32[32,256]{1,0:T(8,128)S(1)} %get-tuple-element.48.refs_0_, f32[32,256]{1,0:T(8,128)S(1)} %collective-permute-done.23.refs_1_, f32[32,256]{1,0:T(8,128)S(1)} %collective-permute-done.24.refs_2_, f32[32,256]{1,0:T(8,128)S(1)} %collective-permute-done.25.refs_3_, ...), custom_call_target="tpu_custom_call" | custom-call | bytes 524288 | tf_op jit(solution)/shard_map/pallas_call | solution.py:237
  65.9 0.8 %shard_map.114 = bf16[128,256]{1,0:T(8,128)(2,1)} custom-call(bf16[256,256]{1,0:T(8,128)(2,1)S(1)} %copy-done.2, bf16[128,256]{1,0:T(8,128)(2,1)S(1)} %get-tuple-element.44.refs_0_, bf16[128,256]{1,0:T(8,128)(2,1)S(1)} %collective-permute-done.17.refs_1_, bf16[128,256]{1,0:T(8,128)(2,1)S(1)} %collective-permute-done.18.refs_2_, ...), custom_call_target="tpu_custom_call" | custom-call | flops 16777216 | bytes 262144 | tf_op jit(solution)/shard_map/pallas_call | solution.py:229
  (52 shorter events, 6.0 us)
Async XLA Ops:
  0.6 7.4 %collective-permute-start.1 = (bf16[128,256]{1,0:T(8,128)(2,1)}, bf16[128,256]{1,0:T(8,128)(2,1)S(1)}, u32[]{:S(2)}, u32[]{:S(2)}) collective-permute-start(bf16[128,256]{1,0:T(8,128)(2,1)} %refs_0_.1), channel_id=1, source_target_pairs={{0,2},{1,3},{2,0},{3,1},{4,6},{5,7},{6,4},{7,5},{8,10},{9,11},{10,... | collective-permute-start | bytes 196616 | tf_op jit(solution)/shard_map/ppermute | solution.py:44
  4.7 4.5 %collective-permute-start = (bf16[128,256]{1,0:T(8,128)(2,1)}, bf16[128,256]{1,0:T(8,128)(2,1)S(1)}, u32[]{:S(2)}, u32[]{:S(2)}) collective-permute-start(bf16[128,256]{1,0:T(8,128)(2,1)} %refs_0_.1), channel_id=1, source_target_pairs={{0,1},{1,0},{2,3},{3,2},{4,5},{5,4},{6,7},{7,6},{8,9},{9,8},{10,11... | collective-permute-start | bytes 196616 | tf_op jit(solution)/shard_map/ppermute | solution.py:44
  6.3 6.3 %collective-permute-start.2 = (bf16[128,256]{1,0:T(8,128)(2,1)}, bf16[128,256]{1,0:T(8,128)(2,1)S(1)}, u32[]{:S(2)}, u32[]{:S(2)}) collective-permute-start(bf16[128,256]{1,0:T(8,128)(2,1)} %refs_0_.1), channel_id=1, source_target_pairs={{0,3},{1,2},{2,1},{3,0},{4,7},{5,6},{6,5},{7,4},{8,11},{9,10},{10,... | collective-permute-start | bytes 196616 | tf_op jit(solution)/shard_map/ppermute | solution.py:44
  15.3 13.0 %copy-start.7 = (f32[256]{0:T(256)S(1)}, f32[256]{0:T(256)}, u32[]{:S(2)}) copy-start(f32[256]{0:T(256)} %param.10) | copy-start | bytes 3076
  16.5 35.9 %copy-start.1 = (bf16[1,1,32,128,128]{4,3,2,1,0:T(8,128)(2,1)S(1)}, bf16[1,1,32,128,128]{4,3,2,1,0:T(8,128)(2,1)}, u32[]{:S(2)}) copy-start(bf16[1,1,32,128,128]{4,3,2,1,0:T(8,128)(2,1)} %param.12) | copy-start | bytes 3145732
  16.5 4.9 %collective-permute-start.3 = (bf16[128,256]{1,0:T(8,128)(2,1)S(1)}, bf16[128,256]{1,0:T(8,128)(2,1)S(1)}, u32[]{:S(2)}, u32[]{:S(2)}) collective-permute-start(bf16[128,256]{1,0:T(8,128)(2,1)S(1)} %get-tuple-element.28), channel_id=1, source_target_pairs={{0,4},{4,0},{8,12},{12,8},{16,20},{20,16},{24,28},{28,24},{1,5},{5... | collective-permute-start | bytes 196616 | tf_op jit(solution)/shard_map/ppermute | solution.py:44
  16.6 6.2 %collective-permute-start.4 = (bf16[128,256]{1,0:T(8,128)(2,1)S(1)}, bf16[128,256]{1,0:T(8,128)(2,1)S(1)}, u32[]{:S(2)}, u32[]{:S(2)}) collective-permute-start(bf16[128,256]{1,0:T(8,128)(2,1)S(1)} %get-tuple-element.29), channel_id=1, source_target_pairs={{0,8},{4,12},{8,0},{12,4},{16,24},{20,28},{24,16},{28,20},{1,9},{5... | collective-permute-start | bytes 196616 | tf_op jit(solution)/shard_map/ppermute | solution.py:44
  18.1 5.6 %collective-permute-start.5 = (bf16[128,256]{1,0:T(8,128)(2,1)S(1)}, bf16[128,256]{1,0:T(8,128)(2,1)S(1)}, u32[]{:S(2)}, u32[]{:S(2)}) collective-permute-start(bf16[128,256]{1,0:T(8,128)(2,1)S(1)} %get-tuple-element.30), channel_id=1, source_target_pairs={{0,12},{4,8},{8,4},{12,0},{16,28},{20,24},{24,20},{28,16},{1,13},{... | collective-permute-start | bytes 196616 | tf_op jit(solution)/shard_map/ppermute | solution.py:44
  18.4 5.5 %collective-permute-start.6 = (bf16[128,256]{1,0:T(8,128)(2,1)S(1)}, bf16[128,256]{1,0:T(8,128)(2,1)S(1)}, u32[]{:S(2)}, u32[]{:S(2)}) collective-permute-start(bf16[128,256]{1,0:T(8,128)(2,1)S(1)} %get-tuple-element.31), channel_id=1, source_target_pairs={{0,16},{4,20},{8,24},{12,28},{16,0},{20,4},{24,8},{28,12},{1,17},{... | collective-permute-start | bytes 196616 | tf_op jit(solution)/shard_map/ppermute | solution.py:44
  21.4 7.0 %collective-permute-start.7 = (bf16[128,256]{1,0:T(8,128)(2,1)S(1)}, bf16[128,256]{1,0:T(8,128)(2,1)S(1)}, u32[]{:S(2)}, u32[]{:S(2)}) collective-permute-start(bf16[128,256]{1,0:T(8,128)(2,1)S(1)} %get-tuple-element.32), channel_id=1, source_target_pairs={{0,20},{4,16},{8,28},{12,24},{16,4},{20,0},{24,12},{28,8},{1,21},{... | collective-permute-start | bytes 196616 | tf_op jit(solution)/shard_map/ppermute | solution.py:44
  21.4 7.0 %collective-permute-start.8 = (bf16[128,256]{1,0:T(8,128)(2,1)S(1)}, bf16[128,256]{1,0:T(8,128)(2,1)S(1)}, u32[]{:S(2)}, u32[]{:S(2)}) collective-permute-start(bf16[128,256]{1,0:T(8,128)(2,1)S(1)} %get-tuple-element.33), channel_id=1, source_target_pairs={{0,24},{4,28},{8,16},{12,20},{16,8},{20,12},{24,0},{28,4},{1,25},{... | collective-permute-start | bytes 196616 | tf_op jit(solution)/shard_map/ppermute | solution.py:44
  22.8 5.5 %collective-permute-start.9 = (bf16[128,256]{1,0:T(8,128)(2,1)S(1)}, bf16[128,256]{1,0:T(8,128)(2,1)S(1)}, u32[]{:S(2)}, u32[]{:S(2)}) collective-permute-start(bf16[128,256]{1,0:T(8,128)(2,1)S(1)} %get-tuple-element.34), channel_id=1, source_target_pairs={{0,28},{4,24},{8,20},{12,16},{16,12},{20,8},{24,4},{28,0},{1,29},{... | collective-permute-start | bytes 196616 | tf_op jit(solution)/shard_map/ppermute | solution.py:44
  29.8 3.7 %collective-permute-start.10 = (bf16[176,256]{1,0:T(8,128)(2,1)S(1)}, bf16[176,256]{1,0:T(8,128)(2,1)S(1)}, u32[]{:S(2)}, u32[]{:S(2)}) collective-permute-start(bf16[176,256]{1,0:T(8,128)(2,1)S(1)} %get-tuple-element.37), channel_id=1, source_target_pairs={{0,4},{4,0},{8,12},{12,8},{16,20},{20,16},{24,28},{28,24},{1,5},{5... | collective-permute-start | bytes 270344 | tf_op jit(solution)/shard_map/ppermute | solution.py:44
  29.9 5.5 %collective-permute-start.11 = (bf16[176,256]{1,0:T(8,128)(2,1)S(1)}, bf16[176,256]{1,0:T(8,128)(2,1)S(1)}, u32[]{:S(2)}, u32[]{:S(2)}) collective-permute-start(bf16[176,256]{1,0:T(8,128)(2,1)S(1)} %get-tuple-element.38), channel_id=1, source_target_pairs={{0,8},{4,12},{8,0},{12,4},{16,24},{20,28},{24,16},{28,20},{1,9},{5... | collective-permute-start | bytes 270344 | tf_op jit(solution)/shard_map/ppermute | solution.py:44
  31.1 5.1 %collective-permute-start.12 = (bf16[176,256]{1,0:T(8,128)(2,1)S(1)}, bf16[176,256]{1,0:T(8,128)(2,1)S(1)}, u32[]{:S(2)}, u32[]{:S(2)}) collective-permute-start(bf16[176,256]{1,0:T(8,128)(2,1)S(1)} %get-tuple-element.39), channel_id=1, source_target_pairs={{0,12},{4,8},{8,4},{12,0},{16,28},{20,24},{24,20},{28,16},{1,13},{... | collective-permute-start | bytes 270344 | tf_op jit(solution)/shard_map/ppermute | solution.py:44
  31.7 5.4 %collective-permute-start.13 = (bf16[176,256]{1,0:T(8,128)(2,1)S(1)}, bf16[176,256]{1,0:T(8,128)(2,1)S(1)}, u32[]{:S(2)}, u32[]{:S(2)}) collective-permute-start(bf16[176,256]{1,0:T(8,128)(2,1)S(1)} %get-tuple-element.40), channel_id=1, source_target_pairs={{0,16},{4,20},{8,24},{12,28},{16,0},{20,4},{24,8},{28,12},{1,17},{... | collective-permute-start | bytes 270344 | tf_op jit(solution)/shard_map/ppermute | solution.py:44
  33.1 8.9 %collective-permute-start.14 = (bf16[176,256]{1,0:T(8,128)(2,1)S(1)}, bf16[176,256]{1,0:T(8,128)(2,1)S(1)}, u32[]{:S(2)}, u32[]{:S(2)}) collective-permute-start(bf16[176,256]{1,0:T(8,128)(2,1)S(1)} %get-tuple-element.41), channel_id=1, source_target_pairs={{0,20},{4,16},{8,28},{12,24},{16,4},{20,0},{24,12},{28,8},{1,21},{... | collective-permute-start | bytes 270344 | tf_op jit(solution)/shard_map/ppermute | solution.py:44
  33.5 8.5 %collective-permute-start.15 = (bf16[176,256]{1,0:T(8,128)(2,1)S(1)}, bf16[176,256]{1,0:T(8,128)(2,1)S(1)}, u32[]{:S(2)}, u32[]{:S(2)}) collective-permute-start(bf16[176,256]{1,0:T(8,128)(2,1)S(1)} %get-tuple-element.42), channel_id=1, source_target_pairs={{0,24},{4,28},{8,16},{12,20},{16,8},{20,12},{24,0},{28,4},{1,25},{... | collective-permute-start | bytes 270344 | tf_op jit(solution)/shard_map/ppermute | solution.py:44
  35.4 6.6 %collective-permute-start.16 = (bf16[176,256]{1,0:T(8,128)(2,1)S(1)}, bf16[176,256]{1,0:T(8,128)(2,1)S(1)}, u32[]{:S(2)}, u32[]{:S(2)}) collective-permute-start(bf16[176,256]{1,0:T(8,128)(2,1)S(1)} %get-tuple-element.43), channel_id=1, source_target_pairs={{0,28},{4,24},{8,20},{12,16},{16,12},{20,8},{24,4},{28,0},{1,29},{... | collective-permute-start | bytes 270344 | tf_op jit(solution)/shard_map/ppermute | solution.py:44
  42.0 6.0 %collective-permute-start.22 = (bf16[48,256]{1,0:T(8,128)(2,1)S(1)}, bf16[48,256]{1,0:T(8,128)(2,1)S(1)}, u32[]{:S(2)}, u32[]{:S(2)}) collective-permute-start(bf16[48,256]{1,0:T(8,128)(2,1)S(1)} %shard_map.115.refs_0_), channel_id=1, source_target_pairs={{0,3},{1,2},{2,1},{3,0},{4,7},{5,6},{6,5},{7,4},{8,11},{9,10},{10,... | collective-permute-start | bytes 73736 | tf_op jit(solution)/shard_map/ppermute | solution.py:44
  42.5 5.4 %collective-permute-start.21 = (bf16[48,256]{1,0:T(8,128)(2,1)S(1)}, bf16[48,256]{1,0:T(8,128)(2,1)S(1)}, u32[]{:S(2)}, u32[]{:S(2)}) collective-permute-start(bf16[48,256]{1,0:T(8,128)(2,1)S(1)} %shard_map.115.refs_0_), channel_id=1, source_target_pairs={{0,2},{1,3},{2,0},{3,1},{4,6},{5,7},{6,4},{7,5},{8,10},{9,11},{10,... | collective-permute-start | bytes 73736 | tf_op jit(solution)/shard_map/ppermute | solution.py:44
  43.7 4.5 %collective-permute-start.20 = (bf16[48,256]{1,0:T(8,128)(2,1)S(1)}, bf16[48,256]{1,0:T(8,128)(2,1)S(1)}, u32[]{:S(2)}, u32[]{:S(2)}) collective-permute-start(bf16[48,256]{1,0:T(8,128)(2,1)S(1)} %shard_map.115.refs_0_), channel_id=1, source_target_pairs={{0,1},{1,0},{2,3},{3,2},{4,5},{5,4},{6,7},{7,6},{8,9},{9,8},{10,11... | collective-permute-start | bytes 73736 | tf_op jit(solution)/shard_map/ppermute | solution.py:44
  48.8 9.3 %collective-permute-start.29 = (f32[32,256]{1,0:T(8,128)S(1)}, f32[32,256]{1,0:T(8,128)S(1)}, u32[]{:S(2)}, u32[]{:S(2)}) collective-permute-start(f32[32,256]{1,0:T(8,128)S(1)} %get-tuple-element.48.refs_0_), channel_id=1, source_target_pairs={{0,28},{4,24},{8,20},{12,16},{16,12},{20,8},{24,4},{28,0},{1,29},{... | collective-permute-start | bytes 98312 | tf_op jit(solution)/shard_map/ppermute | solution.py:44
  48.8 9.3 %collective-permute-start.28 = (f32[32,256]{1,0:T(8,128)S(1)}, f32[32,256]{1,0:T(8,128)S(1)}, u32[]{:S(2)}, u32[]{:S(2)}) collective-permute-start(f32[32,256]{1,0:T(8,128)S(1)} %get-tuple-element.48.refs_0_), channel_id=1, source_target_pairs={{0,24},{4,28},{8,16},{12,20},{16,8},{20,12},{24,0},{28,4},{1,25},{... | collective-permute-start | bytes 98312 | tf_op jit(solution)/shard_map/ppermute | solution.py:44
  50.9 7.4 %collective-permute-start.27 = (f32[32,256]{1,0:T(8,128)S(1)}, f32[32,256]{1,0:T(8,128)S(1)}, u32[]{:S(2)}, u32[]{:S(2)}) collective-permute-start(f32[32,256]{1,0:T(8,128)S(1)} %get-tuple-element.48.refs_0_), channel_id=1, source_target_pairs={{0,20},{4,16},{8,28},{12,24},{16,4},{20,0},{24,12},{28,8},{1,21},{... | collective-permute-start | bytes 98312 | tf_op jit(solution)/shard_map/ppermute | solution.py:44
  53.6 12.3 %collective-permute-start.17 = (bf16[128,256]{1,0:T(8,128)(2,1)S(1)}, bf16[128,256]{1,0:T(8,128)(2,1)S(1)}, u32[]{:S(2)}, u32[]{:S(2)}) collective-permute-start(bf16[128,256]{1,0:T(8,128)(2,1)S(1)} %get-tuple-element.45), channel_id=1, source_target_pairs={{0,1},{1,0},{2,3},{3,2},{4,5},{5,4},{6,7},{7,6},{8,9},{9,8},{10,11... | collective-permute-start | bytes 196616 | tf_op jit(solution)/shard_map/ppermute | solution.py:44
  56.2 4.4 %collective-permute-start.26 = (f32[32,256]{1,0:T(8,128)S(1)}, f32[32,256]{1,0:T(8,128)S(1)}, u32[]{:S(2)}, u32[]{:S(2)}) collective-permute-start(f32[32,256]{1,0:T(8,128)S(1)} %get-tuple-element.48.refs_0_), channel_id=1, source_target_pairs={{0,16},{4,20},{8,24},{12,28},{16,0},{20,4},{24,8},{28,12},{1,17},{... | collective-permute-start | bytes 98312 | tf_op jit(solution)/shard_map/ppermute | solution.py:44
  58.1 3.3 %collective-permute-start.25 = (f32[32,256]{1,0:T(8,128)S(1)}, f32[32,256]{1,0:T(8,128)S(1)}, u32[]{:S(2)}, u32[]{:S(2)}) collective-permute-start(f32[32,256]{1,0:T(8,128)S(1)} %get-tuple-element.48.refs_0_), channel_id=1, source_target_pairs={{0,12},{4,8},{8,4},{12,0},{16,28},{20,24},{24,20},{28,16},{1,13},{... | collective-permute-start | bytes 98312 | tf_op jit(solution)/shard_map/ppermute | solution.py:44
  58.2 7.7 %collective-permute-start.18 = (bf16[128,256]{1,0:T(8,128)(2,1)S(1)}, bf16[128,256]{1,0:T(8,128)(2,1)S(1)}, u32[]{:S(2)}, u32[]{:S(2)}) collective-permute-start(bf16[128,256]{1,0:T(8,128)(2,1)S(1)} %get-tuple-element.46), channel_id=1, source_target_pairs={{0,2},{1,3},{2,0},{3,1},{4,6},{5,7},{6,4},{7,5},{8,10},{9,11},{10,... | collective-permute-start | bytes 196616 | tf_op jit(solution)/shard_map/ppermute | solution.py:44
  58.2 7.6 %collective-permute-start.19 = (bf16[128,256]{1,0:T(8,128)(2,1)S(1)}, bf16[128,256]{1,0:T(8,128)(2,1)S(1)}, u32[]{:S(2)}, u32[]{:S(2)}) collective-permute-start(bf16[128,256]{1,0:T(8,128)(2,1)S(1)} %get-tuple-element.47), channel_id=1, source_target_pairs={{0,3},{1,2},{2,1},{3,0},{4,7},{5,6},{6,5},{7,4},{8,11},{9,10},{10,... | collective-permute-start | bytes 196616 | tf_op jit(solution)/shard_map/ppermute | solution.py:44
  60.7 3.9 %collective-permute-start.24 = (f32[32,256]{1,0:T(8,128)S(1)}, f32[32,256]{1,0:T(8,128)S(1)}, u32[]{:S(2)}, u32[]{:S(2)}) collective-permute-start(f32[32,256]{1,0:T(8,128)S(1)} %get-tuple-element.48.refs_0_), channel_id=1, source_target_pairs={{0,8},{4,12},{8,0},{12,4},{16,24},{20,28},{24,16},{28,20},{1,9},{5... | collective-permute-start | bytes 98312 | tf_op jit(solution)/shard_map/ppermute | solution.py:44
  61.5 3.1 %collective-permute-start.23 = (f32[32,256]{1,0:T(8,128)S(1)}, f32[32,256]{1,0:T(8,128)S(1)}, u32[]{:S(2)}, u32[]{:S(2)}) collective-permute-start(f32[32,256]{1,0:T(8,128)S(1)} %get-tuple-element.48.refs_0_), channel_id=1, source_target_pairs={{0,4},{4,0},{8,12},{12,8},{16,20},{20,16},{24,28},{28,24},{1,5},{5... | collective-permute-start | bytes 98312 | tf_op jit(solution)/shard_map/ppermute | solution.py:44
  (6 other events, 29.4 us)

commit v3 on v2

v3 whole, which is shorter than its diff:
```python
import functools

import jax
import jax.numpy as jnp
from jax import lax
from jax.experimental import pallas as pl
from jax.experimental.pallas import tpu as pltpu
from jax.sharding import PartitionSpec as P

F32 = jnp.float32
BF16 = jnp.bfloat16
ROOT_2_OVER_PI = 0.7978845608028654
CUBIC = 0.044715
VMEM_LIMIT = 48 * 1024 * 1024
BIAS_ROWS = 16

VMEM_SPEC = pl.BlockSpec(memory_space=pltpu.VMEM)
SMEM_SPEC = pl.BlockSpec(memory_space=pltpu.SMEM)


def call(kernel, out_shape, in_specs, scratch, flops, moved):
    return pl.pallas_call(
        kernel,
        out_shape=out_shape,
        in_specs=in_specs,
        out_specs=jax.tree.map(lambda _: VMEM_SPEC, out_shape),
        scratch_shapes=scratch,
        compiler_params=pltpu.CompilerParams(vmem_limit_bytes=VMEM_LIMIT),
        cost_estimate=pl.CostEstimate(flops=flops, bytes_accessed=moved, transcendentals=0),
    )


def partner(index, k, count):
    if count & (count - 1) == 0:
        return index ^ k
    return (k - index) % count


def exchange(blocks, axis, size, cores=1):
    count = size // cores
    received = []
    for k, block in enumerate(blocks):
        pairs = [(i, partner(i // cores, k, count) * cores + i % cores) for i in range(size)]
        moves = any(i != j for i, j in pairs)
        received.append(lax.ppermute(block, axis, pairs) if moves else block)
    return received


def block_at(index, size):
    return pl.ds(pl.multiple_of(index * size, size), size)


def summed(refs, rows=slice(None)):
    total = refs[0][rows, :].astype(F32)
    for ref in refs[1:]:
        total += ref[rows, :].astype(F32)
    return total


def bias_rows(bias):
    high = bias.astype(BF16).astype(F32)
    line = lax.broadcasted_iota(jnp.int32, (BIAS_ROWS, bias.shape[1]), 0)
    return jnp.where(line == 0, high, jnp.where(line == 1, bias - high, 0.0))


def dense_kernel(count_ref, row_ref, col_ref, tiles_ref, dense_ref, turned_ref, sum_ref, turned_sum):
    tile = tiles_ref.shape[1]
    sum_ref[...] = jnp.zeros_like(sum_ref)
    turned_sum[...] = jnp.zeros_like(turned_sum)

    def body(slot, carry):
        values = tiles_ref[slot].astype(F32)
        rows = block_at(row_ref[slot], tile)
        cols = block_at(col_ref[slot], tile)
        sum_ref[rows, cols] += values
        turned_sum[cols, rows] += values.T
        return carry

    lax.fori_loop(0, count_ref[0], body, 0)
    dense_ref[...] = sum_ref[...].astype(BF16)
    turned_ref[...] = turned_sum[...].astype(BF16)


def dense_product(refs, source_ref, acc_ref, turned):
    (dense_ref,) = refs
    rows = dense_ref.shape[0]
    step = 256 if rows % 256 == 0 else rows
    for first in range(0, rows, step):
        acc_ref[first : first + step, :] = jnp.dot(
            dense_ref[first : first + step, :], source_ref[...], preferred_element_type=F32
        )


def slot_product(refs, source_ref, acc_ref, turned):
    count_ref, row_ref, col_ref, tiles_ref = refs
    source_idx, target_idx = (row_ref, col_ref) if turned else (col_ref, row_ref)
    contract = 0 if turned else 1
    count = count_ref[0]
    tile = tiles_ref.shape[1]
    acc_ref[...] = jnp.zeros_like(acc_ref)

    def body(slot, carry):
        rows = source_ref[block_at(source_idx[slot], tile), :]
        acc_ref[block_at(target_idx[slot], tile), :] += lax.dot_general(
            tiles_ref[slot], rows, (((contract,), (0,)), ((), ())), preferred_element_type=F32
        )
        return carry

    lax.fori_loop(0, count, body, 0)


def forward_kernel(me_ref, cot_ref, *refs, product, n_adj, n_row):
    adjacency, sources = refs[:n_adj], refs[n_adj : n_adj + n_row]
    out_ref, source_ref, acc_ref = refs[n_adj + n_row :]
    tile = sources[0].shape[0]
    for k, ref in enumerate(sources):
        source_ref[block_at(partner(me_ref[0], k, n_row), tile), :] = ref[...]
    product(adjacency, source_ref, acc_ref, False)
    nodes = acc_ref.shape[0]
    out_ref[:nodes, :] = acc_ref[...].astype(BF16)
    out_ref[nodes:, :] = cot_ref[...]


def chip_kernel(me_ref, own_ref, other_ref, cot_ref, *refs):
    outs, sum_ref = refs[:-1], refs[-1]
    n_chip = len(outs)
    nodes = sum_ref.shape[0]
    tile = own_ref.shape[0] - nodes
    chip, core = me_ref[1], me_ref[2]
    sum_ref[...] = own_ref[:nodes, :].astype(F32) + other_ref[:nodes, :].astype(F32)
    for k, ref in enumerate(outs):
        ref[...] = sum_ref[block_at(partner(chip, k, n_chip), 2 * tile), :].astype(BF16)
    cot_ref[block_at(core, tile), :] = own_ref[nodes:, :]
    cot_ref[block_at(1 - core, tile), :] = other_ref[nodes:, :]


def middle_kernel(me_ref, weight_ref, bias_ref, cot_ref, *refs, n_chip, n_row):
    parts, (hidden_ref, grad_ref, *outs) = refs[:n_chip], refs[n_chip:-2]
    hidden_both, weight_acc = refs[-2:]
    tile = hidden_ref.shape[0]
    aggregated = summed(parts).astype(BF16)
    v = jnp.dot(aggregated, weight_ref[...], preferred_element_type=F32) + bias_ref[...]
    square = v * v
    t = jnp.tanh(ROOT_2_OVER_PI * (v + CUBIC * (square * v)))
    half = 0.5 * (1.0 + t)
    hidden_both[...] = v * half
    hidden_ref[...] = hidden_both[block_at(me_ref[2], tile), :].astype(BF16)
    slope = half + 0.5 * v * (1.0 - t * t) * (ROOT_2_OVER_PI * (1.0 + 3.0 * CUBIC * square))
    grad = (cot_ref[...].astype(F32) * slope).astype(BF16)
    grad_ref[...] = grad
    weight_acc[...] = lax.dot_general(
        aggregated, grad, (((0,), (0,)), ((), ())), preferred_element_type=F32
    )
    tail = bias_rows(jnp.sum(grad.astype(F32), axis=0, keepdims=True))
    share = outs[0].shape[0] - BIAS_ROWS
    for k, ref in enumerate(outs):
        mine = weight_acc[block_at(partner(me_ref[0], k, n_row), share), :]
        ref[...] = jnp.concatenate([mine, tail], axis=0).astype(BF16)


def share_kernel(*refs):
    parts, out_ref = refs[:-1], refs[-1]
    total = summed(parts)
    share = total.shape[0] - BIAS_ROWS
    tail = bias_rows(total[share : share + 1] + total[share + 1 : share + 2])
    out_ref[...] = jnp.concatenate([total[:share], tail], axis=0).astype(BF16)


def backward_kernel(me_ref, *refs, product, n_adj, n_row, n_chip, factor):
    adjacency, refs = refs[:n_adj], refs[n_adj:]
    sources, shares, refs = refs[:n_chip], refs[n_chip : 2 * n_chip], refs[2 * n_chip :]
    (bias_ref, *outs), (source_ref, acc_ref) = refs[:-2], refs[-2:]
    nodes = sources[0].shape[0]
    for k, ref in enumerate(sources):
        source_ref[block_at(partner(me_ref[1], k, n_chip), nodes), :] = ref[...]
    product(adjacency, source_ref, acc_ref, True)
    total = summed(shares) * factor
    share = total.shape[0] - BIAS_ROWS
    bias_ref[...] = total[share : share + 1] + total[share + 1 : share + 2]
    tile = nodes // 2
    for k, ref in enumerate(outs):
        ref[:tile, :] = acc_ref[block_at(partner(me_ref[0], k, n_row), tile), :].astype(BF16)
        ref[tile:, :] = total[:share].astype(BF16)


def final_kernel(me_ref, weight_ref, *refs, n_row):
    parts, (features_ref, grad_ref) = refs[:n_row], refs[n_row:]
    tile = features_ref.shape[0]
    features_ref[...] = lax.dot_general(
        summed(parts, slice(0, tile)).astype(BF16),
        weight_ref[...],
        (((1,), (1,)), ((), ())),
        preferred_element_type=F32,
    ).astype(BF16)
    share = parts[0].shape[0] - tile
    for k, ref in enumerate(parts):
        grad_ref[block_at(partner(me_ref[0], k, n_row), share), :] = ref[tile:, :].astype(F32)


def local(features, weight, bias_term, cotangent, tile_values, tile_row, tile_col, tile_count):
    n_row = lax.axis_size("row")
    n_col = lax.axis_size("col")
    n_chip = n_col // 2
    tile, width = features.shape
    hidden = weight.shape[1]
    slots = tile_values.shape[2]
    tiles = tile_values.reshape(slots, tile, tile)
    row_nodes, col_nodes = n_col * tile, n_row * tile
    bias_row = bias_term.reshape(1, hidden)
    col = lax.axis_index("col")
    me = jnp.stack([lax.axis_index("row"), col // 2, col % 2]).astype(jnp.int32)
    share = width // n_row
    matrix = 2 * tile * width * hidden

    def like(rows, columns, dtype=BF16):
        return jax.ShapeDtypeStruct((rows, columns), dtype)

    slot_args = (tile_count.reshape(1), tile_row.reshape(slots), tile_col.reshape(slots), tiles)
    if n_row * n_col <= 2 * slots:
        product, n_adj, adj_specs = dense_product, 1, [VMEM_SPEC]
        dense, turned = call(
            dense_kernel,
            (like(row_nodes, col_nodes), like(col_nodes, row_nodes)),
            [SMEM_SPEC] * 3 + [VMEM_SPEC],
            [pltpu.VMEM((row_nodes, col_nodes), F32), pltpu.VMEM((col_nodes, row_nodes), F32)],
            0,
            12 * row_nodes * col_nodes,
        )(*slot_args)
        adjacency, adjacency_back = (dense,), (turned,)
    else:
        product, n_adj, adj_specs = slot_product, 4, [SMEM_SPEC] * 3 + [VMEM_SPEC]
        adjacency = adjacency_back = slot_args

    sources = exchange([features] * n_row, "row", n_row)
    partial_value = call(
        functools.partial(forward_kernel, product=product, n_adj=n_adj, n_row=n_row),
        like(row_nodes + tile, width),
        [SMEM_SPEC, VMEM_SPEC] + adj_specs + [VMEM_SPEC] * n_row,
        [pltpu.VMEM((col_nodes, width), BF16), pltpu.VMEM((row_nodes, width), F32)],
        slots * matrix // 2,
        row_nodes * width * 8,
    )(me, cotangent, *adjacency, *sources)
    swapped = lax.ppermute(partial_value, "col", [(i, i ^ 1) for i in range(n_col)])
    cot_both, *pieces = call(
        chip_kernel,
        [like(2 * tile, hidden)] + [like(2 * tile, width)] * n_chip,
        [SMEM_SPEC] + [VMEM_SPEC] * 2,
        [pltpu.VMEM((row_nodes, width), F32)],
        row_nodes * width,
        row_nodes * width * 6,
    )(me, partial_value, swapped)
    parts = exchange(pieces, "col", n_col, 2)
    hidden_out, grad, *terms = call(
        functools.partial(middle_kernel, n_chip=n_chip, n_row=n_row),
        [like(tile, hidden), like(2 * tile, hidden)] + [like(share + BIAS_ROWS, hidden)] * n_row,
        [SMEM_SPEC] + [VMEM_SPEC] * (3 + n_chip),
        [pltpu.VMEM((2 * tile, hidden), F32), pltpu.VMEM((width, hidden), F32)],
        4 * matrix,
        n_chip * tile * width * 8,
    )(me, weight, bias_row, cot_both, *parts)
    grads = exchange([grad] * n_chip, "col", n_col, 2)
    terms = exchange(terms, "row", n_row)
    row_share = call(
        share_kernel,
        like(share + BIAS_ROWS, hidden),
        [VMEM_SPEC] * n_row,
        [],
        n_row * share * hidden,
        n_row * share * hidden * 2,
    )(*terms)
    shares = exchange([row_share] * n_chip, "col", n_col, 2)
    factor = (tile * n_row * n_col) ** (-0.5)
    grad_bias, *backs = call(
        functools.partial(
            backward_kernel, product=product, n_adj=n_adj, n_row=n_row, n_chip=n_chip, factor=factor
        ),
        [like(1, hidden, F32)] + [like(tile + share, hidden)] * n_row,
        [SMEM_SPEC] + adj_specs + [VMEM_SPEC] * (2 * n_chip),
        [pltpu.VMEM((row_nodes, hidden), BF16), pltpu.VMEM((col_nodes, hidden), F32)],
        slots * matrix // 2,
        row_nodes * hidden * 8,
    )(me, *adjacency_back, *grads, *shares)
    backs = exchange(backs, "row", n_row)
    grad_features, grad_weight = call(
        functools.partial(final_kernel, n_row=n_row),
        (like(tile, width), like(width, hidden, F32)),
        [SMEM_SPEC] + [VMEM_SPEC] * (1 + n_row),
        [],
        matrix,
        n_row * tile * hidden * 4,
    )(me, weight, *backs)
    return hidden_out, grad_features, grad_weight, grad_bias.reshape(hidden)


def solution(mesh):
    return jax.shard_map(
        local,
        mesh=mesh,
        in_specs=(
            P(("col", "row"), None),
            P(),
            P(),
            P(("row", "col"), None),
            P("row", "col", None, None, None),
            P("row", "col", None),
            P("row", "col", None),
            P("row", "col"),
        ),
        out_specs=(P(("row", "col"), None), P(("col", "row"), None), P(), P()),
        check_vma=False,
    )
```

time: 66.6 us -> 63 us (0.946)
  starting transfers between devices: 34 us -> 24.5 us
  Pallas kernels: 6.49 us -> 10.6 us
  waiting for transfers between devices: 22 us -> 23.7 us
    ppermute x30 -> x18, starting transfers between devices: 34 us -> 24.4 us  [exchange(): received.append(lax.ppermute(block, axis, pairs) if moves else block)]
    pallas_call x7, Pallas kernels: 6.49 us -> 10.6 us  [the longest x1 4.29 us: local(): call(dense_kernel, (like(row_nodes, col_nodes), like(col_nodes, row_nodes...]
    ppermute x0 -> x1, waiting for transfers between devices: none -> 1.99 us  [local(): lax.ppermute(partial_value, 'col', [(i, i ^ 1) for i in range(n_col)])]
    ppermute x30 -> x18, waiting for transfers between devices: 22 us -> 21.7 us  [exchange(): received.append(lax.ppermute(block, axis, pairs) if moves else block)]
    unnamed x16 -> x14, local copies, waits for them, and re-layouts: 2.75 us -> 2.57 us
  transfers between devices with their start and end apart: 30 -> 19, of which waited for: 13 -> 10; matrix products, arithmetic and copies ran while one was open for 0% -> 0% of each run, Pallas kernels for 4% -> 7%
where the time goes in v3:
time: 63 us; the launch traced here: 62.8 us
  starting transfers between devices  24.5 us (39%)
  waiting for transfers between devices  23.7 us (38%)
  Pallas kernels  10.6 us (17%)
  local copies, waits for them, and re-layouts  2.57 us (4%)
  between operations  1.39 us (2%)
    ppermute x18, starting transfers between devices, exchange(): received.append(lax.ppermute(block, axis, pairs) if moves else block)  24.4 us
    ppermute x18, waiting for transfers between devices, exchange(): received.append(lax.ppermute(block, axis, pairs) if moves else block)  21.7 us
    pallas_call x1, Pallas kernels, local(): call(dense_kernel, (like(row_nodes, col_nodes), like(col_nodes, row_nodes...  4.29 us
    unnamed x14, local copies, waits for them, and re-layouts  2.57 us
    ppermute x1, waiting for transfers between devices, local(): lax.ppermute(partial_value, 'col', [(i, i ^ 1) for i in range(n_col)])  1.99 us
    pallas_call x1, Pallas kernels, local(): call(functools.partial(backward_kernel, product=product, n_adj=n_adj, n_r...  1.56 us
    pallas_call x1, Pallas kernels, local(): call(functools.partial(middle_kernel, n_chip=n_chip, n_row=n_row), [like(...  1.54 us
    pallas_call x1, Pallas kernels, local(): call(functools.partial(final_kernel, n_row=n_row), (like(tile, width), li...  1.38 us
  transfers between devices with their start and end apart: 19, of which 10 were waited for; matrix products, arithmetic and copies ran while one was open for 0% of the time, Pallas kernels for 7%

profile of v3, /device:TPU:0, one launch (start us, length us, event | category | flops | bytes accessed | tf_op | source)
XLA Modules:
  0.0 62.8 jit_solution(9706309457272548765)
XLA Ops:
  0.6 4.1 %collective-permute-start.1 = (bf16[128,256]{1,0:T(8,128)(2,1)}, bf16[128,256]{1,0:T(8,128)(2,1)S(1)}, u32[]{:S(2)}, u32[]{:S(2)}) collective-permute-start(bf16[128,256]{1,0:T(8,128)(2,1)} %refs_1_.1), channel_id=1, source_target_pairs={{0,2},{1,3},{2,0},{3,1},{4,6},{5,7},{6,4},{7,5},{8,10},{9,11},{10,... | collective-permute-start | bytes 196616 | tf_op jit(solution)/shard_map/ppermute | solution.py:45
  4.7 1.6 %collective-permute-start = (bf16[128,256]{1,0:T(8,128)(2,1)}, bf16[128,256]{1,0:T(8,128)(2,1)S(1)}, u32[]{:S(2)}, u32[]{:S(2)}) collective-permute-start(bf16[128,256]{1,0:T(8,128)(2,1)} %refs_1_.1), channel_id=1, source_target_pairs={{0,1},{1,0},{2,3},{3,2},{4,5},{5,4},{6,7},{7,6},{8,9},{9,8},{10,11... | collective-permute-start | bytes 196616 | tf_op jit(solution)/shard_map/ppermute | solution.py:45
  7.0 0.6 %copy-done.5 = s32[1,1,32]{2,1,0:T(1,128)S(1)} copy-done((s32[1,1,32]{2,1,0:T(1,128)S(1)}, s32[1,1,32]{2,1,0:T(1,128)}, u32[]{:S(2)}) %copy-start.5) | copy-done | bytes 152
  7.6 1.2 %copy-done = bf16[1,1,32,128,128]{4,3,2,1,0:T(8,128)(2,1)S(1)} copy-done((bf16[1,1,32,128,128]{4,3,2,1,0:T(8,128)(2,1)S(1)}, bf16[1,1,32,128,128]{4,3,2,1,0:T(8,128)(2,1)}, u32[]{:S(2)}) %copy-start) | copy-done | bytes 1048600
  8.9 4.3 %shard_map.111 = (bf16[1024,512]{1,0:T(8,128)(2,1)S(1)}, bf16[512,1024]{1,0:T(8,128)(2,1)S(1)}) custom-call(s32[1]{0:T(128)} %bitcast.9.count_ref, s32[32]{0:T(128)S(1)} %bitcast.12, s32[32]{0:T(128)S(1)} %bitcast.13, bf16[32,128,128]{2,1,0:T(8,128)(2,1)S(1)} %bitcast.10), custom_call_target="tpu_custom_call" | custom-call | bytes 6291456 | tf_op jit(solution)/shard_map/pallas_call | solution.py:221
  13.3 1.0 %shard_map.112.own_ref = bf16[1152,256]{1,0:T(8,128)(2,1)S(1)} custom-call(s32[3]{0:T(128)S(1)} %pad_add_fusion.me_ref, bf16[128,256]{1,0:T(8,128)(2,1)S(1)} %copy-done.2, bf16[1024,512]{1,0:T(8,128)(2,1)S(1)} %get-tuple-element.24.refs_0_, bf16[128,256]{1,0:T(8,128)(2,1)S(1)} %copy-done.3, bf16[128,256]{1,0:T(8,128)(2,1)S(1)} %collective-permute-done.refs_2_, ...), custom_call_target="tpu_custom_call" | custom-call | flops 268435456 | bytes 2097152 | tf_op jit(solution)/shard_map/pallas_call | solution.py:235
  14.4 2.0 %collective-permute-done.3.other_ref = bf16[1152,256]{1,0:T(8,128)(2,1)S(1)} collective-permute-done((bf16[1152,256]{1,0:T(8,128)(2,1)S(1)}, bf16[1152,256]{1,0:T(8,128)(2,1)S(1)}, u32[]{:S(2)}, u32[]{:S(2)}) %collective-permute-start.3) | collective-permute-done | bytes 589856 | tf_op jit(solution)/shard_map/ppermute | solution.py:243
  16.4 0.8 %shard_map.113 = (bf16[256,256]{1,0:T(8,128)(2,1)S(1)}, bf16[256,256]{1,0:T(8,128)(2,1)S(1)}, bf16[256,256]{1,0:T(8,128)(2,1)S(1)}, bf16[256,256]{1,0:T(8,128)(2,1)S(1)}, bf16[256,256]{1,0:T(8,128)(2,1)S(1)}) custom-call(s32[3]{0:T(128)S(1)} %pad_add_fusion.me_ref, bf16[1152,256]{1,0:T(8,128)(2,1)S(1)} %shard_map.112.own_ref, ...), custom_call_target="tpu_custom_call" | custom-call | flops 262144 | bytes 1572864 | tf_op jit(solution)/shard_map/pallas_call | solution.py:244
  17.1 0.9 %collective-permute-start.4 = (bf16[256,256]{1,0:T(8,128)(2,1)S(1)}, bf16[256,256]{1,0:T(8,128)(2,1)S(1)}, u32[]{:S(2)}, u32[]{:S(2)}) collective-permute-start(bf16[256,256]{1,0:T(8,128)(2,1)S(1)} %get-tuple-element.27), channel_id=1, source_target_pairs={{0,8},{4,12},{8,0},{12,4},{16,24},{20,28},{24,16},{28,20},{1,9},{5... | collective-permute-start | bytes 393224 | tf_op jit(solution)/shard_map/ppermute | solution.py:45
  18.0 1.5 %collective-permute-start.5 = (bf16[256,256]{1,0:T(8,128)(2,1)S(1)}, bf16[256,256]{1,0:T(8,128)(2,1)S(1)}, u32[]{:S(2)}, u32[]{:S(2)}) collective-permute-start(bf16[256,256]{1,0:T(8,128)(2,1)S(1)} %get-tuple-element.28), channel_id=1, source_target_pairs={{0,16},{4,20},{8,24},{12,28},{16,0},{20,4},{24,8},{28,12},{1,17},{... | collective-permute-start | bytes 393224 | tf_op jit(solution)/shard_map/ppermute | solution.py:45
  19.5 1.2 %collective-permute-start.6 = (bf16[256,256]{1,0:T(8,128)(2,1)S(1)}, bf16[256,256]{1,0:T(8,128)(2,1)S(1)}, u32[]{:S(2)}, u32[]{:S(2)}) collective-permute-start(bf16[256,256]{1,0:T(8,128)(2,1)S(1)} %get-tuple-element.29), channel_id=1, source_target_pairs={{0,24},{4,28},{8,16},{12,20},{16,8},{20,12},{24,0},{28,4},{1,25},{... | collective-permute-start | bytes 393224 | tf_op jit(solution)/shard_map/ppermute | solution.py:45
  20.7 2.9 %collective-permute-done.4.refs_1_ = bf16[256,256]{1,0:T(8,128)(2,1)S(1)} collective-permute-done((bf16[256,256]{1,0:T(8,128)(2,1)S(1)}, bf16[256,256]{1,0:T(8,128)(2,1)S(1)}, u32[]{:S(2)}, u32[]{:S(2)}) %collective-permute-start.4) | collective-permute-done | bytes 131104 | tf_op jit(solution)/shard_map/ppermute | solution.py:45
  23.5 2.5 %collective-permute-done.5.refs_2_ = bf16[256,256]{1,0:T(8,128)(2,1)S(1)} collective-permute-done((bf16[256,256]{1,0:T(8,128)(2,1)S(1)}, bf16[256,256]{1,0:T(8,128)(2,1)S(1)}, u32[]{:S(2)}, u32[]{:S(2)}) %collective-permute-start.5) | collective-permute-done | bytes 131104 | tf_op jit(solution)/shard_map/ppermute | solution.py:45
  26.1 0.7 %copy-done.4 = f32[256]{0:T(256)S(1)} copy-done((f32[256]{0:T(256)S(1)}, f32[256]{0:T(256)}, u32[]{:S(2)}) %copy-start.4) | copy-done | bytes 1048
  26.7 1.5 %shard_map.114 = (bf16[128,256]{1,0:T(8,128)(2,1)}, bf16[256,256]{1,0:T(8,128)(2,1)S(1)}, bf16[80,256]{1,0:T(8,128)(2,1)S(1)}, bf16[80,256]{1,0:T(8,128)(2,1)S(1...) custom-call(s32[3]{0:T(128)S(1)} %pad_add_fusion.me_ref, bf16[256,256]{1,0:T(8,128)(2,1)S(1)} %copy-done.1, ...), custom_call_target="tpu_custom_call" | custom-call | flops 67108864 | bytes 1048576 | tf_op jit(solution)/shard_map/pallas_call | solution.py:253
  28.3 1.3 %collective-permute-start.10 = (bf16[80,256]{1,0:T(8,128)(2,1)S(1)}, bf16[80,256]{1,0:T(8,128)(2,1)S(1)}, u32[]{:S(2)}, u32[]{:S(2)}) collective-permute-start(bf16[80,256]{1,0:T(8,128)(2,1)S(1)} %get-tuple-element.34), channel_id=1, source_target_pairs={{0,1},{1,0},{2,3},{3,2},{4,5},{5,4},{6,7},{7,6},{8,9},{9,8},{10,11... | collective-permute-start | bytes 122888 | tf_op jit(solution)/shard_map/ppermute | solution.py:45
  29.6 1.8 %collective-permute-start.9 = (bf16[256,256]{1,0:T(8,128)(2,1)S(1)}, bf16[256,256]{1,0:T(8,128)(2,1)S(1)}, u32[]{:S(2)}, u32[]{:S(2)}) collective-permute-start(bf16[256,256]{1,0:T(8,128)(2,1)S(1)} %get-tuple-element.32.refs_1_), channel_id=1, source_target_pairs={{0,24},{4,28},{8,16},{12,20},{16,8},{20,12},{24,0},{28,4},{1,25},{... | collective-permute-start | bytes 393224 | tf_op jit(solution)/shard_map/ppermute | solution.py:45
  31.7 1.5 %collective-permute-start.7 = (bf16[256,256]{1,0:T(8,128)(2,1)S(1)}, bf16[256,256]{1,0:T(8,128)(2,1)S(1)}, u32[]{:S(2)}, u32[]{:S(2)}) collective-permute-start(bf16[256,256]{1,0:T(8,128)(2,1)S(1)} %get-tuple-element.32.refs_1_), channel_id=1, source_target_pairs={{0,8},{4,12},{8,0},{12,4},{16,24},{20,28},{24,16},{28,20},{1,9},{5... | collective-permute-start | bytes 393224 | tf_op jit(solution)/shard_map/ppermute | solution.py:45
  33.1 3.7 %collective-permute-start.11 = (bf16[80,256]{1,0:T(8,128)(2,1)S(1)}, bf16[80,256]{1,0:T(8,128)(2,1)S(1)}, u32[]{:S(2)}, u32[]{:S(2)}) collective-permute-start(bf16[80,256]{1,0:T(8,128)(2,1)S(1)} %get-tuple-element.35), channel_id=1, source_target_pairs={{0,2},{1,3},{2,0},{3,1},{4,6},{5,7},{6,4},{7,5},{8,10},{9,11},{10,... | collective-permute-start | bytes 122888 | tf_op jit(solution)/shard_map/ppermute | solution.py:45
  36.9 2.0 %collective-permute-done.11.refs_2_ = bf16[80,256]{1,0:T(8,128)(2,1)S(1)} collective-permute-done((bf16[80,256]{1,0:T(8,128)(2,1)S(1)}, bf16[80,256]{1,0:T(8,128)(2,1)S(1)}, u32[]{:S(2)}, u32[]{:S(2)}) %collective-permute-start.11) | collective-permute-done | bytes 40992 | tf_op jit(solution)/shard_map/ppermute | solution.py:45
  38.8 3.8 %collective-permute-done.12.refs_3_ = bf16[80,256]{1,0:T(8,128)(2,1)S(1)} collective-permute-done((bf16[80,256]{1,0:T(8,128)(2,1)S(1)}, bf16[80,256]{1,0:T(8,128)(2,1)S(1)}, u32[]{:S(2)}, u32[]{:S(2)}) %collective-permute-start.12) | collective-permute-done | bytes 40992 | tf_op jit(solution)/shard_map/ppermute | solution.py:45
  42.7 1.2 %collective-permute-start.15 = (bf16[80,256]{1,0:T(8,128)(2,1)S(1)}, bf16[80,256]{1,0:T(8,128)(2,1)S(1)}, u32[]{:S(2)}, u32[]{:S(2)}) collective-permute-start(bf16[80,256]{1,0:T(8,128)(2,1)S(1)} %shard_map.115.refs_5_), channel_id=1, source_target_pairs={{0,24},{4,28},{8,16},{12,20},{16,8},{20,12},{24,0},{28,4},{1,25},{... | collective-permute-start | bytes 122888 | tf_op jit(solution)/shard_map/ppermute | solution.py:45
  43.9 0.6 %collective-permute-start.14 = (bf16[80,256]{1,0:T(8,128)(2,1)S(1)}, bf16[80,256]{1,0:T(8,128)(2,1)S(1)}, u32[]{:S(2)}, u32[]{:S(2)}) collective-permute-start(bf16[80,256]{1,0:T(8,128)(2,1)S(1)} %shard_map.115.refs_5_), channel_id=1, source_target_pairs={{0,16},{4,20},{8,24},{12,28},{16,0},{20,4},{24,8},{28,12},{1,17},{... | collective-permute-start | bytes 122888 | tf_op jit(solution)/shard_map/ppermute | solution.py:45
  44.6 3.1 %collective-permute-done.15.refs_8_ = bf16[80,256]{1,0:T(8,128)(2,1)S(1)} collective-permute-done((bf16[80,256]{1,0:T(8,128)(2,1)S(1)}, bf16[80,256]{1,0:T(8,128)(2,1)S(1)}, u32[]{:S(2)}, u32[]{:S(2)}) %collective-permute-start.15) | collective-permute-done | bytes 40992 | tf_op jit(solution)/shard_map/ppermute | solution.py:45
  47.7 0.3 collective-permute-start.13
  48.1 3.6 %collective-permute-done.13.refs_6_ = bf16[80,256]{1,0:T(8,128)(2,1)S(1)} collective-permute-done((bf16[80,256]{1,0:T(8,128)(2,1)S(1)}, bf16[80,256]{1,0:T(8,128)(2,1)S(1)}, u32[]{:S(2)}, u32[]{:S(2)}) %collective-permute-start.13) | collective-permute-done | bytes 40992 | tf_op jit(solution)/shard_map/ppermute | solution.py:45
  51.7 1.6 %shard_map.116 = (f32[1,256]{1,0:T(1,128)}, bf16[192,256]{1,0:T(8,128)(2,1)S(1)}, bf16[192,256]{1,0:T(8,128)(2,1)S(1)}, bf16[192,256]{1,0:T(8,128)(2,1)S(1)}, bf16[192,256]{1,0:T(8,128)(2,1)S(1)}) custom-call(s32[3]{0:T(128)S(1)} %pad_add_fusion.me_ref, bf16[512,1024]{1,0:T(8,128)(2,1)S(1)} %get-tuple-element.31.refs_0_, ...), custom_call_target="tpu_custom_call" | custom-call | flops 268435456 | bytes 2097152 | tf_op jit(solution)/shard_map/pallas_call | solution.py:273
  53.3 1.0 %collective-permute-start.17 = (bf16[192,256]{1,0:T(8,128)(2,1)S(1)}, bf16[192,256]{1,0:T(8,128)(2,1)S(1)}, u32[]{:S(2)}, u32[]{:S(2)}) collective-permute-start(bf16[192,256]{1,0:T(8,128)(2,1)S(1)} %get-tuple-element.39), channel_id=1, source_target_pairs={{0,2},{1,3},{2,0},{3,1},{4,6},{5,7},{6,4},{7,5},{8,10},{9,11},{10,... | collective-permute-start | bytes 294920 | tf_op jit(solution)/shard_map/ppermute | solution.py:45
  54.3 3.4 %collective-permute-start.18 = (bf16[192,256]{1,0:T(8,128)(2,1)S(1)}, bf16[192,256]{1,0:T(8,128)(2,1)S(1)}, u32[]{:S(2)}, u32[]{:S(2)}) collective-permute-start(bf16[192,256]{1,0:T(8,128)(2,1)S(1)} %get-tuple-element.40), channel_id=1, source_target_pairs={{0,3},{1,2},{2,1},{3,0},{4,7},{5,6},{6,5},{7,4},{8,11},{9,10},{10,... | collective-permute-start | bytes 294920 | tf_op jit(solution)/shard_map/ppermute | solution.py:45
  57.6 1.3 %collective-permute-done.16.refs_1_ = bf16[192,256]{1,0:T(8,128)(2,1)S(1)} collective-permute-done((bf16[192,256]{1,0:T(8,128)(2,1)S(1)}, bf16[192,256]{1,0:T(8,128)(2,1)S(1)}, u32[]{:S(2)}, u32[]{:S(2)}) %collective-permute-start.16) | collective-permute-done | bytes 98336 | tf_op jit(solution)/shard_map/ppermute | solution.py:45
  58.9 2.5 %collective-permute-done.18.refs_3_ = bf16[192,256]{1,0:T(8,128)(2,1)S(1)} collective-permute-done((bf16[192,256]{1,0:T(8,128)(2,1)S(1)}, bf16[192,256]{1,0:T(8,128)(2,1)S(1)}, u32[]{:S(2)}, u32[]{:S(2)}) %collective-permute-start.18) | collective-permute-done | bytes 98336 | tf_op jit(solution)/shard_map/ppermute | solution.py:45
  61.4 1.4 %shard_map.117 = (bf16[128,256]{1,0:T(8,128)(2,1)}, f32[256,256]{1,0:T(8,128)}) custom-call(s32[3]{0:T(128)S(1)} %pad_add_fusion.me_ref, bf16[256,256]{1,0:T(8,128)(2,1)S(1)} %copy-done.1, bf16[192,256]{1,0:T(8,128)(2,1)S(1)} %get-tuple-element.37.refs_0_, bf16[192,256]{1,0:T(8,128)(2,1)S(1)} %collective-permute-done.16.refs_1_, ...), custom_call_target="tpu_custom_call" | custom-call | flops 16777216 | bytes 524288 | tf_op jit(solution)/shard_map/pallas_call | solution.py:284
  (28 shorter events, 0.6 us)
Async XLA Ops:
  0.6 12.6 %collective-permute-start.1 = (bf16[128,256]{1,0:T(8,128)(2,1)}, bf16[128,256]{1,0:T(8,128)(2,1)S(1)}, u32[]{:S(2)}, u32[]{:S(2)}) collective-permute-start(bf16[128,256]{1,0:T(8,128)(2,1)} %refs_1_.1), channel_id=1, source_target_pairs={{0,2},{1,3},{2,0},{3,1},{4,6},{5,7},{6,4},{7,5},{8,10},{9,11},{10,... | collective-permute-start | bytes 196616 | tf_op jit(solution)/shard_map/ppermute | solution.py:45
  4.7 8.5 %collective-permute-start = (bf16[128,256]{1,0:T(8,128)(2,1)}, bf16[128,256]{1,0:T(8,128)(2,1)S(1)}, u32[]{:S(2)}, u32[]{:S(2)}) collective-permute-start(bf16[128,256]{1,0:T(8,128)(2,1)} %refs_1_.1), channel_id=1, source_target_pairs={{0,1},{1,0},{2,3},{3,2},{4,5},{5,4},{6,7},{7,6},{8,9},{9,8},{10,11... | collective-permute-start | bytes 196616 | tf_op jit(solution)/shard_map/ppermute | solution.py:45
  6.3 6.9 %collective-permute-start.2 = (bf16[128,256]{1,0:T(8,128)(2,1)}, bf16[128,256]{1,0:T(8,128)(2,1)S(1)}, u32[]{:S(2)}, u32[]{:S(2)}) collective-permute-start(bf16[128,256]{1,0:T(8,128)(2,1)} %refs_1_.1), channel_id=1, source_target_pairs={{0,3},{1,2},{2,1},{3,0},{4,7},{5,6},{6,5},{7,4},{8,11},{9,10},{10,... | collective-permute-start | bytes 196616 | tf_op jit(solution)/shard_map/ppermute | solution.py:45
  7.0 0.7 %copy-start.5 = (s32[1,1,32]{2,1,0:T(1,128)S(1)}, s32[1,1,32]{2,1,0:T(1,128)}, u32[]{:S(2)}) copy-start(s32[1,1,32]{2,1,0:T(1,128)} %param.13) | copy-start | bytes 388
  7.0 0.7 %copy-start.6 = (s32[1,1,32]{2,1,0:T(1,128)S(1)}, s32[1,1,32]{2,1,0:T(1,128)}, u32[]{:S(2)}) copy-start(s32[1,1,32]{2,1,0:T(1,128)} %param.14) | copy-start | bytes 388
  7.6 1.2 %copy-start = (bf16[1,1,32,128,128]{4,3,2,1,0:T(8,128)(2,1)S(1)}, bf16[1,1,32,128,128]{4,3,2,1,0:T(8,128)(2,1)}, u32[]{:S(2)}) copy-start(bf16[1,1,32,128,128]{4,3,2,1,0:T(8,128)(2,1)} %param.12) | copy-start | bytes 3145732
  8.9 4.4 %copy-start.2 = (bf16[128,256]{1,0:T(8,128)(2,1)S(1)}, bf16[128,256]{1,0:T(8,128)(2,1)}, u32[]{:S(2)}) copy-start(bf16[128,256]{1,0:T(8,128)(2,1)} %cot_ref.1) | copy-start | bytes 196612
  8.9 4.4 %copy-start.3 = (bf16[128,256]{1,0:T(8,128)(2,1)S(1)}, bf16[128,256]{1,0:T(8,128)(2,1)}, u32[]{:S(2)}) copy-start(bf16[128,256]{1,0:T(8,128)(2,1)} %refs_1_.1) | copy-start | bytes 196612
  14.3 11.8 %copy-start.1 = (bf16[256,256]{1,0:T(8,128)(2,1)S(1)}, bf16[256,256]{1,0:T(8,128)(2,1)}, u32[]{:S(2)}) copy-start(bf16[256,256]{1,0:T(8,128)(2,1)} %weight_ref.3) | copy-start | bytes 393220
  14.3 2.1 %collective-permute-start.3 = (bf16[1152,256]{1,0:T(8,128)(2,1)S(1)}, bf16[1152,256]{1,0:T(8,128)(2,1)S(1)}, u32[]{:S(2)}, u32[]{:S(2)}) collective-permute-start(bf16[1152,256]{1,0:T(8,128)(2,1)S(1)} %shard_map.112.own_ref), channel_id=1, source_target_pairs={{0,4},{4,0},{8,12},{12,8},{16,20},{20,16},{24,28},{28,24},{1,5},{5... | collective-permute-start | bytes 1769480 | tf_op jit(solution)/shard_map/ppermute | solution.py:243
  17.1 6.4 %collective-permute-start.4 = (bf16[256,256]{1,0:T(8,128)(2,1)S(1)}, bf16[256,256]{1,0:T(8,128)(2,1)S(1)}, u32[]{:S(2)}, u32[]{:S(2)}) collective-permute-start(bf16[256,256]{1,0:T(8,128)(2,1)S(1)} %get-tuple-element.27), channel_id=1, source_target_pairs={{0,8},{4,12},{8,0},{12,4},{16,24},{20,28},{24,16},{28,20},{1,9},{5... | collective-permute-start | bytes 393224 | tf_op jit(solution)/shard_map/ppermute | solution.py:45
  18.0 8.1 %collective-permute-start.5 = (bf16[256,256]{1,0:T(8,128)(2,1)S(1)}, bf16[256,256]{1,0:T(8,128)(2,1)S(1)}, u32[]{:S(2)}, u32[]{:S(2)}) collective-permute-start(bf16[256,256]{1,0:T(8,128)(2,1)S(1)} %get-tuple-element.28), channel_id=1, source_target_pairs={{0,16},{4,20},{8,24},{12,28},{16,0},{20,4},{24,8},{28,12},{1,17},{... | collective-permute-start | bytes 393224 | tf_op jit(solution)/shard_map/ppermute | solution.py:45
  19.5 6.6 %collective-permute-start.6 = (bf16[256,256]{1,0:T(8,128)(2,1)S(1)}, bf16[256,256]{1,0:T(8,128)(2,1)S(1)}, u32[]{:S(2)}, u32[]{:S(2)}) collective-permute-start(bf16[256,256]{1,0:T(8,128)(2,1)S(1)} %get-tuple-element.29), channel_id=1, source_target_pairs={{0,24},{4,28},{8,16},{12,20},{16,8},{20,12},{24,0},{28,4},{1,25},{... | collective-permute-start | bytes 393224 | tf_op jit(solution)/shard_map/ppermute | solution.py:45
  26.1 0.7 %copy-start.4 = (f32[256]{0:T(256)S(1)}, f32[256]{0:T(256)}, u32[]{:S(2)}) copy-start(f32[256]{0:T(256)} %param.10) | copy-start | bytes 3076
  28.3 8.6 %collective-permute-start.10 = (bf16[80,256]{1,0:T(8,128)(2,1)S(1)}, bf16[80,256]{1,0:T(8,128)(2,1)S(1)}, u32[]{:S(2)}, u32[]{:S(2)}) collective-permute-start(bf16[80,256]{1,0:T(8,128)(2,1)S(1)} %get-tuple-element.34), channel_id=1, source_target_pairs={{0,1},{1,0},{2,3},{3,2},{4,5},{5,4},{6,7},{7,6},{8,9},{9,8},{10,11... | collective-permute-start | bytes 122888 | tf_op jit(solution)/shard_map/ppermute | solution.py:45
  29.6 22.1 %collective-permute-start.9 = (bf16[256,256]{1,0:T(8,128)(2,1)S(1)}, bf16[256,256]{1,0:T(8,128)(2,1)S(1)}, u32[]{:S(2)}, u32[]{:S(2)}) collective-permute-start(bf16[256,256]{1,0:T(8,128)(2,1)S(1)} %get-tuple-element.32.refs_1_), channel_id=1, source_target_pairs={{0,24},{4,28},{8,16},{12,20},{16,8},{20,12},{24,0},{28,4},{1,25},{... | collective-permute-start | bytes 393224 | tf_op jit(solution)/shard_map/ppermute | solution.py:45
  31.4 20.3 %collective-permute-start.8 = (bf16[256,256]{1,0:T(8,128)(2,1)S(1)}, bf16[256,256]{1,0:T(8,128)(2,1)S(1)}, u32[]{:S(2)}, u32[]{:S(2)}) collective-permute-start(bf16[256,256]{1,0:T(8,128)(2,1)S(1)} %get-tuple-element.32.refs_1_), channel_id=1, source_target_pairs={{0,16},{4,20},{8,24},{12,28},{16,0},{20,4},{24,8},{28,12},{1,17},{... | collective-permute-start | bytes 393224 | tf_op jit(solution)/shard_map/ppermute | solution.py:45
  31.7 20.0 %collective-permute-start.7 = (bf16[256,256]{1,0:T(8,128)(2,1)S(1)}, bf16[256,256]{1,0:T(8,128)(2,1)S(1)}, u32[]{:S(2)}, u32[]{:S(2)}) collective-permute-start(bf16[256,256]{1,0:T(8,128)(2,1)S(1)} %get-tuple-element.32.refs_1_), channel_id=1, source_target_pairs={{0,8},{4,12},{8,0},{12,4},{16,24},{20,28},{24,16},{28,20},{1,9},{5... | collective-permute-start | bytes 393224 | tf_op jit(solution)/shard_map/ppermute | solution.py:45
  33.1 5.7 %collective-permute-start.11 = (bf16[80,256]{1,0:T(8,128)(2,1)S(1)}, bf16[80,256]{1,0:T(8,128)(2,1)S(1)}, u32[]{:S(2)}, u32[]{:S(2)}) collective-permute-start(bf16[80,256]{1,0:T(8,128)(2,1)S(1)} %get-tuple-element.35), channel_id=1, source_target_pairs={{0,2},{1,3},{2,0},{3,1},{4,6},{5,7},{6,4},{7,5},{8,10},{9,11},{10,... | collective-permute-start | bytes 122888 | tf_op jit(solution)/shard_map/ppermute | solution.py:45
  36.9 5.8 %collective-permute-start.12 = (bf16[80,256]{1,0:T(8,128)(2,1)S(1)}, bf16[80,256]{1,0:T(8,128)(2,1)S(1)}, u32[]{:S(2)}, u32[]{:S(2)}) collective-permute-start(bf16[80,256]{1,0:T(8,128)(2,1)S(1)} %get-tuple-element.36), channel_id=1, source_target_pairs={{0,3},{1,2},{2,1},{3,0},{4,7},{5,6},{6,5},{7,4},{8,11},{9,10},{10,... | collective-permute-start | bytes 122888 | tf_op jit(solution)/shard_map/ppermute | solution.py:45
  42.7 5.0 %collective-permute-start.15 = (bf16[80,256]{1,0:T(8,128)(2,1)S(1)}, bf16[80,256]{1,0:T(8,128)(2,1)S(1)}, u32[]{:S(2)}, u32[]{:S(2)}) collective-permute-start(bf16[80,256]{1,0:T(8,128)(2,1)S(1)} %shard_map.115.refs_5_), channel_id=1, source_target_pairs={{0,24},{4,28},{8,16},{12,20},{16,8},{20,12},{24,0},{28,4},{1,25},{... | collective-permute-start | bytes 122888 | tf_op jit(solution)/shard_map/ppermute | solution.py:45
  43.9 4.2 %collective-permute-start.14 = (bf16[80,256]{1,0:T(8,128)(2,1)S(1)}, bf16[80,256]{1,0:T(8,128)(2,1)S(1)}, u32[]{:S(2)}, u32[]{:S(2)}) collective-permute-start(bf16[80,256]{1,0:T(8,128)(2,1)S(1)} %shard_map.115.refs_5_), channel_id=1, source_target_pairs={{0,16},{4,20},{8,24},{12,28},{16,0},{20,4},{24,8},{28,12},{1,17},{... | collective-permute-start | bytes 122888 | tf_op jit(solution)/shard_map/ppermute | solution.py:45
  47.7 4.0 %collective-permute-start.13 = (bf16[80,256]{1,0:T(8,128)(2,1)S(1)}, bf16[80,256]{1,0:T(8,128)(2,1)S(1)}, u32[]{:S(2)}, u32[]{:S(2)}) collective-permute-start(bf16[80,256]{1,0:T(8,128)(2,1)S(1)} %shard_map.115.refs_5_), channel_id=1, source_target_pairs={{0,8},{4,12},{8,0},{12,4},{16,24},{20,28},{24,16},{28,20},{1,9},{5... | collective-permute-start | bytes 122888 | tf_op jit(solution)/shard_map/ppermute | solution.py:45
  53.3 5.7 %collective-permute-start.16 = (bf16[192,256]{1,0:T(8,128)(2,1)S(1)}, bf16[192,256]{1,0:T(8,128)(2,1)S(1)}, u32[]{:S(2)}, u32[]{:S(2)}) collective-permute-start(bf16[192,256]{1,0:T(8,128)(2,1)S(1)} %get-tuple-element.38), channel_id=1, source_target_pairs={{0,1},{1,0},{2,3},{3,2},{4,5},{5,4},{6,7},{7,6},{8,9},{9,8},{10,11... | collective-permute-start | bytes 294920 | tf_op jit(solution)/shard_map/ppermute | solution.py:45
  53.3 5.7 %collective-permute-start.17 = (bf16[192,256]{1,0:T(8,128)(2,1)S(1)}, bf16[192,256]{1,0:T(8,128)(2,1)S(1)}, u32[]{:S(2)}, u32[]{:S(2)}) collective-permute-start(bf16[192,256]{1,0:T(8,128)(2,1)S(1)} %get-tuple-element.39), channel_id=1, source_target_pairs={{0,2},{1,3},{2,0},{3,1},{4,6},{5,7},{6,4},{7,5},{8,10},{9,11},{10,... | collective-permute-start | bytes 294920 | tf_op jit(solution)/shard_map/ppermute | solution.py:45
  54.3 7.1 %collective-permute-start.18 = (bf16[192,256]{1,0:T(8,128)(2,1)S(1)}, bf16[192,256]{1,0:T(8,128)(2,1)S(1)}, u32[]{:S(2)}, u32[]{:S(2)}) collective-permute-start(bf16[192,256]{1,0:T(8,128)(2,1)S(1)} %get-tuple-element.40), channel_id=1, source_target_pairs={{0,3},{1,2},{2,1},{3,0},{4,7},{5,6},{6,5},{7,4},{8,11},{9,10},{10,... | collective-permute-start | bytes 294920 | tf_op jit(solution)/shard_map/ppermute | solution.py:45

commit v4 on v3

v4 whole, which is shorter than its diff:
```python
import functools

import jax
import jax.numpy as jnp
from jax import lax
from jax.experimental import pallas as pl
from jax.experimental.pallas import tpu as pltpu
from jax.sharding import PartitionSpec as P

F32 = jnp.float32
BF16 = jnp.bfloat16
ROOT_2_OVER_PI = 0.7978845608028654
CUBIC = 0.044715
VMEM_LIMIT = 48 * 1024 * 1024
BIAS_ROWS = 16

VMEM_SPEC = pl.BlockSpec(memory_space=pltpu.VMEM)
HBM_SPEC = pl.BlockSpec(memory_space=pltpu.HBM)
SMEM_SPEC = pl.BlockSpec(memory_space=pltpu.SMEM)


def call(kernel, out_shape, in_specs, scratch, flops, moved):
    return pl.pallas_call(
        kernel,
        out_shape=out_shape,
        in_specs=in_specs,
        out_specs=jax.tree.map(lambda _: VMEM_SPEC, out_shape),
        scratch_shapes=scratch,
        compiler_params=pltpu.CompilerParams(vmem_limit_bytes=VMEM_LIMIT),
        cost_estimate=pl.CostEstimate(flops=flops, bytes_accessed=moved, transcendentals=0),
    )


def partner(index, k, count):
    if count & (count - 1) == 0:
        return index ^ k
    return (k - index) % count


def far_first(count):
    return list(dict.fromkeys([count - 1, *range(1, count), 0]))


def exchange(blocks, axis, size, cores=1):
    count = size // cores
    received = []
    for k in far_first(count):
        pairs = [(i, partner(i // cores, k, count) * cores + i % cores) for i in range(size)]
        moves = any(i != j for i, j in pairs)
        received.append(lax.ppermute(blocks[k], axis, pairs) if moves else blocks[k])
    return received


def block_at(index, size):
    return pl.ds(pl.multiple_of(index * size, size), size)


def row_index():
    return lax.axis_index("row")


def chip_index():
    return lax.axis_index("col") // 2


def core_index():
    return lax.axis_index("col") % 2


def summed(refs):
    by_partner = dict(zip(far_first(len(refs)), refs))
    values = [by_partner[k][...].astype(F32) for k in sorted(by_partner)]
    while len(values) > 1:
        values = [sum(values[i + 1 : i + 2], values[i]) for i in range(0, len(values), 2)]
    return values[0]


def bias_rows(bias):
    high = bias.astype(BF16).astype(F32)
    line = lax.broadcasted_iota(jnp.int32, (BIAS_ROWS, bias.shape[1]), 0)
    return jnp.where(line == 0, high, jnp.where(line == 1, bias - high, 0.0))


def dense_kernel(
    count_ref, row_hbm, col_hbm, tiles_hbm, bias_hbm, dense_ref, bias_ref,
    row_ref, col_ref, tiles_ref, sum_ref, sems, tile_sems,
):
    slots, tile = tiles_ref.shape[0], tiles_ref.shape[1]
    chunks = tile_sems.shape[0]
    size = slots // chunks
    small = [
        pltpu.make_async_copy(row_hbm, row_ref, sems.at[0]),
        pltpu.make_async_copy(col_hbm, col_ref, sems.at[1]),
        pltpu.make_async_copy(bias_hbm, bias_ref, sems.at[2]),
    ]
    large = []
    for k in range(chunks):
        part = pl.ds(k * size, size)
        large.append(
            pltpu.make_async_copy(tiles_hbm.at[0, 0, part], tiles_ref.at[part], tile_sems.at[k])
        )
    for copy in small + large:
        copy.start()
    sum_ref[...] = jnp.zeros_like(sum_ref)
    for copy in small:
        copy.wait()
    count = count_ref[0, 0]

    def body(slot, carry):
        rows = block_at(row_ref[0, 0, slot], tile)
        cols = block_at(col_ref[0, 0, slot], tile)
        sum_ref[rows, cols] += tiles_ref[slot].astype(F32)
        return carry

    for k, copy in enumerate(large):
        copy.wait()
        lax.fori_loop(k * size, jnp.minimum(count, (k + 1) * size), body, 0)
    dense_ref[...] = sum_ref[...].astype(BF16)


def turn_kernel(dense_ref, after_ref, turned_ref):
    rows = dense_ref.shape[0]
    step = 256 if rows % 256 == 0 else rows
    for first in range(0, rows, step):
        turned_ref[:, first : first + step] = dense_ref[first : first + step, :].T


def dense_product(refs, source_ref, acc_ref, turned):
    (dense_ref,) = refs
    rows = dense_ref.shape[0]
    step = 256 if rows % 256 == 0 else rows
    for first in range(0, rows, step):
        acc_ref[first : first + step, :] = jnp.dot(
            dense_ref[first : first + step, :], source_ref[...], preferred_element_type=F32
        )


def slot_product(refs, source_ref, acc_ref, turned):
    count_ref, row_ref, col_ref, tiles_ref = refs
    source_idx, target_idx = (row_ref, col_ref) if turned else (col_ref, row_ref)
    contract = 0 if turned else 1
    tile = tiles_ref.shape[1]
    acc_ref[...] = jnp.zeros_like(acc_ref)

    def body(slot, carry):
        rows = source_ref[block_at(source_idx[slot], tile), :]
        acc_ref[block_at(target_idx[slot], tile), :] += lax.dot_general(
            tiles_ref[slot], rows, (((contract,), (0,)), ((), ())), preferred_element_type=F32
        )
        return carry

    lax.fori_loop(0, count_ref[0], body, 0)


def forward_kernel(cot_ref, *refs, product, n_adj, n_row):
    adjacency, sources = refs[:n_adj], refs[n_adj : n_adj + n_row]
    out_ref, source_ref, acc_ref = refs[n_adj + n_row :]
    tile = sources[0].shape[0]
    for k, ref in zip(far_first(n_row), sources):
        source_ref[block_at(partner(row_index(), k, n_row), tile), :] = ref[...]
    product(adjacency, source_ref, acc_ref, False)
    nodes = acc_ref.shape[0]
    out_ref[:nodes, :] = acc_ref[...].astype(BF16)
    out_ref[nodes:, :] = cot_ref[...]


def chip_kernel(own_ref, other_ref, *refs, k, n_chip):
    out_ref = refs[-1]
    rows = block_at(partner(chip_index(), k, n_chip), out_ref.shape[0])
    out_ref[...] = (own_ref[rows, :].astype(F32) + other_ref[rows, :].astype(F32)).astype(BF16)


def middle_kernel(weight_ref, bias_ref, own_ref, other_ref, *refs):
    parts, (hidden_ref, grad_ref, agg_ref) = refs[:-3], refs[-3:]
    aggregated = summed(parts).astype(BF16)
    agg_ref[...] = aggregated
    v = jnp.dot(aggregated, weight_ref[...], preferred_element_type=F32) + bias_ref[...]
    square = v * v
    t = jnp.tanh(ROOT_2_OVER_PI * (v + CUBIC * (square * v)))
    half = 0.5 * (1.0 + t)
    hidden_ref[...] = (v * half).astype(BF16)
    slope = half + 0.5 * v * (1.0 - t * t) * (ROOT_2_OVER_PI * (1.0 + 3.0 * CUBIC * square))
    tile = v.shape[0] // 2
    last = own_ref.shape[0] - tile
    own, other = own_ref[last:, :].astype(F32), other_ref[last:, :].astype(F32)
    for core in range(2):
        part = slice(core * tile, (core + 1) * tile)
        cot = jnp.where(core_index() == core, own, other)
        grad_ref[part, :] = (cot * slope[part, :]).astype(BF16)


def hidden_kernel(both_ref, out_ref):
    out_ref[...] = both_ref[block_at(core_index(), out_ref.shape[0]), :]


def term_kernel(agg_ref, grad_ref, after_ref, out_ref, acc_ref):
    grad = grad_ref[...]
    acc_ref[...] = lax.dot_general(
        agg_ref[...], grad, (((0,), (0,)), ((), ())), preferred_element_type=F32
    )
    half = acc_ref.shape[0] // 2
    out_ref[:half, :] = acc_ref[block_at(core_index(), half), :].astype(BF16)
    bias = jnp.sum(grad.astype(F32), axis=0, keepdims=True)
    out_ref[half:, :] = bias_rows(bias).astype(BF16)


def add_terms_kernel(after_ref, *refs):
    parts, out_ref = refs[:-1], refs[-1]
    total = summed(parts)
    half = total.shape[0] - BIAS_ROWS
    out_ref[:half, :] = total[:half].astype(BF16)
    out_ref[half:, :] = bias_rows(total[half : half + 1] + total[half + 1 : half + 2]).astype(BF16)


def scale_kernel(after_ref, *refs, factor):
    parts, (half_ref, bias_ref) = refs[:-2], refs[-2:]
    total = summed(parts) * factor
    half = half_ref.shape[0]
    half_ref[...] = total[:half]
    bias_ref[...] = total[half : half + 1] + total[half + 1 : half + 2]


def gather_kernel(*refs):
    parts, out_ref = refs[:-1], refs[-1]
    nodes = parts[0].shape[0]
    for k, ref in zip(far_first(len(parts)), parts):
        out_ref[block_at(partner(chip_index(), k, len(parts)), nodes), :] = ref[...]


def slot_back_kernel(count_ref, row_ref, col_ref, tiles_ref, source_ref, out_ref, acc_ref):
    slot_product((count_ref, row_ref, col_ref, tiles_ref), source_ref, acc_ref, True)
    out_ref[...] = acc_ref[...].astype(BF16)


def slot_piece_kernel(back_ref, *refs, k, n_row):
    out_ref = refs[-1]
    out_ref[...] = back_ref[block_at(partner(row_index(), k, n_row), out_ref.shape[0]), :]


def dense_piece_kernel(turned_ref, source_ref, *refs, k, n_row):
    out_ref = refs[-1]
    rows = block_at(partner(row_index(), k, n_row), out_ref.shape[0])
    out_ref[...] = jnp.dot(
        turned_ref[rows, :], source_ref[...], preferred_element_type=F32
    ).astype(BF16)


def features_kernel(weight_ref, *refs):
    parts, out_ref = refs[:-1], refs[-1]
    out_ref[...] = lax.dot_general(
        summed(parts).astype(BF16),
        weight_ref[...],
        (((1,), (1,)), ((), ())),
        preferred_element_type=F32,
    ).astype(BF16)


def join_kernel(own_ref, other_ref, bias_ref, weight_ref, bias_out):
    half = own_ref.shape[0]
    weight_ref[block_at(core_index(), half), :] = own_ref[...]
    weight_ref[block_at(1 - core_index(), half), :] = other_ref[...]
    bias_out[...] = bias_ref[...]


def in_turn(count, make):
    made, before = {}, []
    for k in far_first(count):
        made[k] = make(k, before)
        before = [made[k]]
    return made


def local(features, weight, bias_term, cotangent, tile_values, tile_row, tile_col, tile_count):
    n_row = lax.axis_size("row")
    n_col = lax.axis_size("col")
    n_chip = n_col // 2
    tile, width = features.shape
    hidden = weight.shape[1]
    slots = tile_values.shape[2]
    row_nodes, col_nodes = n_col * tile, n_row * tile
    bias_row = bias_term.reshape(1, hidden)
    half = width // 2
    matrix = 2 * tile * width * hidden
    block_bytes = 2 * tile * width

    def like(rows, columns, dtype=BF16):
        return jax.ShapeDtypeStruct((rows, columns), dtype)

    near = 1
    is_dense = n_row * n_col <= 2 * slots
    if is_dense:
        product, n_adj, adj_specs = dense_product, 1, [VMEM_SPEC]
        chunks = 4 if slots % 4 == 0 else 1
        dense, bias_row = call(
            dense_kernel,
            (like(row_nodes, col_nodes), like(1, hidden, F32)),
            [SMEM_SPEC] + [HBM_SPEC] * 4,
            [
                pltpu.SMEM((1, 1, slots), jnp.int32),
                pltpu.SMEM((1, 1, slots), jnp.int32),
                pltpu.VMEM((slots, tile, tile), BF16),
                pltpu.VMEM((row_nodes, col_nodes), F32),
                pltpu.SemaphoreType.DMA((3,)),
                pltpu.SemaphoreType.DMA((chunks,)),
            ],
            0,
            12 * row_nodes * col_nodes,
        )(tile_count, *(
            pltpu.with_memory_space_constraint(array, pltpu.HBM)
            for array in (tile_row, tile_col, tile_values, bias_row)
        ))
        adjacency = (dense,)
    else:
        product, n_adj, adj_specs = slot_product, 4, [SMEM_SPEC] * 3 + [VMEM_SPEC]
        adjacency = (
            tile_count.reshape(1),
            tile_row.reshape(slots),
            tile_col.reshape(slots),
            tile_values.reshape(slots, tile, tile),
        )

    sources = exchange([features] * n_row, "row", n_row)
    partial_value = call(
        functools.partial(forward_kernel, product=product, n_adj=n_adj, n_row=n_row),
        like(row_nodes + tile, width),
        [VMEM_SPEC] + adj_specs + [VMEM_SPEC] * n_row,
        [pltpu.VMEM((col_nodes, width), BF16), pltpu.VMEM((row_nodes, width), F32)],
        slots * matrix // 2,
        row_nodes * width * 8,
    )(cotangent, *adjacency, *sources)
    swapped = lax.ppermute(partial_value, "col", [(i, i ^ 1) for i in range(n_col)])

    def chip_piece(k, before):
        return call(
            functools.partial(chip_kernel, k=k, n_chip=n_chip),
            like(2 * tile, width),
            [VMEM_SPEC] * (2 + len(before)),
            [],
            2 * tile * width,
            6 * block_bytes,
        )(partial_value, swapped, *before)

    pieces = in_turn(n_chip, chip_piece)
    parts = exchange(pieces, "col", n_col, 2)
    if is_dense:
        turned = call(
            turn_kernel,
            like(col_nodes, row_nodes),
            [VMEM_SPEC] * 2,
            [],
            0,
            4 * row_nodes * col_nodes,
        )(dense, pieces[0])
    both_hidden, grad, aggregated = call(
        middle_kernel,
        [like(2 * tile, hidden), like(2 * tile, hidden), like(2 * tile, width)],
        [VMEM_SPEC] * (4 + n_chip),
        [],
        2 * matrix,
        n_chip * 2 * block_bytes,
    )(weight, bias_row, partial_value, swapped, *parts)
    grads = exchange([grad] * n_chip, "col", n_col, 2)
    hidden_out = call(
        hidden_kernel, like(tile, hidden), [VMEM_SPEC], [], 0, 2 * block_bytes
    )(both_hidden)
    term = call(
        term_kernel,
        like(half + BIAS_ROWS, hidden),
        [VMEM_SPEC] * 3,
        [pltpu.VMEM((width, hidden), F32)],
        2 * matrix,
        6 * block_bytes,
    )(aggregated, grad, grads[near])
    source = call(
        gather_kernel,
        like(row_nodes, hidden),
        [VMEM_SPEC] * n_chip,
        [],
        0,
        row_nodes * hidden * 4,
    )(*grads)
    if is_dense:
        piece_kernel, piece_args, piece_flops = dense_piece_kernel, (turned, source), n_col * matrix
    else:
        back = call(
            slot_back_kernel,
            like(col_nodes, hidden),
            [SMEM_SPEC] * 3 + [VMEM_SPEC] * 2,
            [pltpu.VMEM((col_nodes, hidden), F32)],
            slots * matrix // 2,
            row_nodes * hidden * 8,
        )(*adjacency, source)
        piece_kernel, piece_args, piece_flops = slot_piece_kernel, (back,), 0

    def back_piece(k, before):
        return call(
            functools.partial(piece_kernel, k=k, n_row=n_row),
            like(tile, hidden),
            [VMEM_SPEC] * (len(piece_args) + len(before)),
            [],
            piece_flops,
            2 * block_bytes,
        )(*piece_args, *before)

    made = in_turn(n_row, back_piece)
    backs = exchange(made, "row", n_row)
    terms = exchange([term] * n_row, "row", n_row)
    row_term = call(
        add_terms_kernel,
        like(half + BIAS_ROWS, hidden),
        [VMEM_SPEC] * (1 + n_row),
        [],
        n_row * half * hidden,
        n_row * half * hidden * 2,
    )(made[0], *terms)
    row_terms = exchange([row_term] * n_chip, "col", n_col, 2)
    factor = (tile * n_row * n_col) ** (-0.5)
    grad_features = call(
        features_kernel,
        like(tile, width),
        [VMEM_SPEC] * (1 + n_row),
        [],
        matrix,
        n_row * block_bytes,
    )(weight, *backs)
    own_half, bias_grad = call(
        functools.partial(scale_kernel, factor=factor),
        (like(half, hidden, F32), like(1, hidden, F32)),
        [HBM_SPEC] + [VMEM_SPEC] * n_chip,
        [],
        n_chip * half * hidden,
        n_chip * half * hidden * 2,
    )(pltpu.with_memory_space_constraint(grad_features, pltpu.HBM), *row_terms)
    other_half = lax.ppermute(own_half, "col", [(i, i ^ 1) for i in range(n_col)])
    grad_weight, grad_bias = call(
        join_kernel,
        (like(width, hidden, F32), like(1, hidden, F32)),
        [VMEM_SPEC] * 3,
        [],
        0,
        width * hidden * 8,
    )(own_half, other_half, bias_grad)
    return hidden_out, grad_features, grad_weight, grad_bias.reshape(hidden)


def solution(mesh):
    return jax.shard_map(
        local,
        mesh=mesh,
        in_specs=(
            P(("col", "row"), None),
            P(),
            P(),
            P(("row", "col"), None),
            P("row", "col", None, None, None),
            P("row", "col", None),
            P("row", "col", None),
            P("row", "col"),
        ),
        out_specs=(P(("row", "col"), None), P(("col", "row"), None), P(), P()),
        check_vma=False,
    )
```

time: 63 us -> 52.1 us (0.83)
  waiting for transfers between devices: 23.7 us -> 16.1 us
  Pallas kernels: 10.6 us -> 6.26 us
  starting transfers between devices: 24.5 us -> 28.1 us
  local copies, waits for them, and re-layouts: 2.57 us -> 0.01 us
    ppermute x18 -> x19, waiting for transfers between devices: 21.7 us -> 14.1 us  [the longest x18 13.5 us: exchange(): lax.ppermute(blocks[k], axis, pairs)]
    pallas_call x6 -> x18, Pallas kernels: 9.57 us -> 5.8 us  [the longest x1 1.4 us: local(): call(dense_kernel, (like(row_nodes, col_nodes), like(1, hidden, F32)), [S...]
    ppermute x18 -> x19, starting transfers between devices: 24.4 us -> 28 us  [the longest x18 27.9 us: exchange(): lax.ppermute(blocks[k], axis, pairs)]
    unnamed x14 -> x6, local copies, waits for them, and re-layouts: 2.57 us -> 0.01 us
  transfers between devices with their start and end apart: 19 -> 20, of which waited for: 10 -> 11; matrix products, arithmetic and copies ran while one was open for 0% -> 0% of each run, Pallas kernels for 7% -> 9%
where the time goes in v4:
time: 52.1 us; the launch traced here: 51.9 us
  starting transfers between devices  28.1 us (54%)
  waiting for transfers between devices  16.1 us (31%)
  Pallas kernels  6.26 us (12%)
  between operations  1.46 us (3%)
    ppermute x18, starting transfers between devices, exchange(): lax.ppermute(blocks[k], axis, pairs)  27.9 us
    ppermute x18, waiting for transfers between devices, exchange(): lax.ppermute(blocks[k], axis, pairs)  13.5 us
    ppermute x1, waiting for transfers between devices, local(): lax.ppermute(partial_value, 'col', [(i, i ^ 1) for i in range(n_col)])  1.99 us
    pallas_call x1, Pallas kernels, local(): call(dense_kernel, (like(row_nodes, col_nodes), like(1, hidden, F32)), [S...  1.4 us
  transfers between devices with their start and end apart: 20, of which 11 were waited for; matrix products, arithmetic and copies ran while one was open for 0% of the time, Pallas kernels for 9%

profile of v4, /device:TPU:0, one launch (start us, length us, event | category | flops | bytes accessed | tf_op | source)
XLA Modules:
  0.0 51.9 jit_solution(9932009396599540752)
XLA Ops:
  0.6 5.1 %collective-permute-start = (bf16[128,256]{1,0:T(8,128)(2,1)}, bf16[128,256]{1,0:T(8,128)(2,1)S(1)}, u32[]{:S(2)}, u32[]{:S(2)}) collective-permute-start(bf16[128,256]{1,0:T(8,128)(2,1)} %refs_4_.1), channel_id=1, source_target_pairs={{0,3},{1,2},{2,1},{3,0},{4,7},{5,6},{6,5},{7,4},{8,11},{9,10},{10,... | collective-permute-start | bytes 196616 | tf_op jit(solution)/shard_map/ppermute | solution.py:50
  5.8 0.6 %collective-permute-start.2 = (bf16[128,256]{1,0:T(8,128)(2,1)}, bf16[128,256]{1,0:T(8,128)(2,1)S(1)}, u32[]{:S(2)}, u32[]{:S(2)}) collective-permute-start(bf16[128,256]{1,0:T(8,128)(2,1)} %refs_4_.1), channel_id=1, source_target_pairs={{0,2},{1,3},{2,0},{3,1},{4,6},{5,7},{6,4},{7,5},{8,10},{9,11},{10,... | collective-permute-start | bytes 196616 | tf_op jit(solution)/shard_map/ppermute | solution.py:50
  7.1 1.4 %shard_map.111 = (bf16[1024,512]{1,0:T(8,128)(2,1)S(1)}, f32[1,256]{1,0:T(1,128)S(1)}) custom-call(s32[1,1]{1,0:T(1,128)S(6)} %copy.12.count_ref, s32[1,1,32]{2,1,0:T(1,128)} %row_hbm.1, s32[1,1,32]{2,1,0:T(1,128)} %col_hbm.1, bf16[1,1,32,128,128]{4,3,2,1,0:T(8,128)(2,1)} %tiles_hbm.1, f32[1,256]{1,0:T(1,128)} %bitcast.2), custom_call_target="tpu_custom_call" | custom-call | bytes 6291456 | tf_op jit(solution)/shard_map/pallas_call | solution.py:294
  8.5 0.4 collective-permute-done.refs_1_
  8.9 1.8 %collective-permute-done.1.refs_2_ = bf16[128,256]{1,0:T(8,128)(2,1)S(1)} collective-permute-done((bf16[128,256]{1,0:T(8,128)(2,1)}, bf16[128,256]{1,0:T(8,128)(2,1)S(1)}, u32[]{:S(2)}, u32[]{:S(2)}) %collective-permute-start.1) | collective-permute-done | bytes 65568 | tf_op jit(solution)/shard_map/ppermute | solution.py:50
  10.6 1.0 %collective-permute-done.2.refs_3_ = bf16[128,256]{1,0:T(8,128)(2,1)S(1)} collective-permute-done((bf16[128,256]{1,0:T(8,128)(2,1)}, bf16[128,256]{1,0:T(8,128)(2,1)S(1)}, u32[]{:S(2)}, u32[]{:S(2)}) %collective-permute-start.2) | collective-permute-done | bytes 65568 | tf_op jit(solution)/shard_map/ppermute | solution.py:50
  11.6 0.5 shard_map.112.own_ref
  12.1 2.0 %collective-permute-done.3.other_ref = bf16[1152,256]{1,0:T(8,128)(2,1)S(1)} collective-permute-done((bf16[1152,256]{1,0:T(8,128)(2,1)S(1)}, bf16[1152,256]{1,0:T(8,128)(2,1)S(1)}, u32[]{:S(2)}, u32[]{:S(2)}) %collective-permute-start.3) | collective-permute-done | bytes 589856 | tf_op jit(solution)/shard_map/ppermute | solution.py:331
  14.2 2.5 %collective-permute-start.4 = (bf16[256,256]{1,0:T(8,128)(2,1)S(1)}, bf16[256,256]{1,0:T(8,128)(2,1)S(1)}, u32[]{:S(2)}, u32[]{:S(2)}) collective-permute-start(bf16[256,256]{1,0:T(8,128)(2,1)S(1)} %shard_map.113.refs_0_), channel_id=1, source_target_pairs={{0,24},{4,28},{8,16},{12,20},{16,8},{20,12},{24,0},{28,4},{1,25},{... | collective-permute-start | bytes 393224 | tf_op jit(solution)/shard_map/ppermute | solution.py:50
  16.7 0.6 %collective-permute-start.5 = (bf16[256,256]{1,0:T(8,128)(2,1)S(1)}, bf16[256,256]{1,0:T(8,128)(2,1)S(1)}, u32[]{:S(2)}, u32[]{:S(2)}) collective-permute-start(bf16[256,256]{1,0:T(8,128)(2,1)S(1)} %shard_map.114.refs_0_), channel_id=1, source_target_pairs={{0,8},{4,12},{8,0},{12,4},{16,24},{20,28},{24,16},{28,20},{1,9},{5... | collective-permute-start | bytes 393224 | tf_op jit(solution)/shard_map/ppermute | solution.py:50
  17.4 0.6 %collective-permute-start.6 = (bf16[256,256]{1,0:T(8,128)(2,1)S(1)}, bf16[256,256]{1,0:T(8,128)(2,1)S(1)}, u32[]{:S(2)}, u32[]{:S(2)}) collective-permute-start(bf16[256,256]{1,0:T(8,128)(2,1)S(1)} %shard_map.115.refs_0_), channel_id=1, source_target_pairs={{0,16},{4,20},{8,24},{12,28},{16,0},{20,4},{24,8},{28,12},{1,17},{... | collective-permute-start | bytes 393224 | tf_op jit(solution)/shard_map/ppermute | solution.py:50
  18.0 3.5 %collective-permute-done.4.refs_0_ = bf16[256,256]{1,0:T(8,128)(2,1)S(1)} collective-permute-done((bf16[256,256]{1,0:T(8,128)(2,1)S(1)}, bf16[256,256]{1,0:T(8,128)(2,1)S(1)}, u32[]{:S(2)}, u32[]{:S(2)}) %collective-permute-start.4) | collective-permute-done | bytes 131104 | tf_op jit(solution)/shard_map/ppermute | solution.py:50
  21.5 2.1 %collective-permute-done.5.refs_1_ = bf16[256,256]{1,0:T(8,128)(2,1)S(1)} collective-permute-done((bf16[256,256]{1,0:T(8,128)(2,1)S(1)}, bf16[256,256]{1,0:T(8,128)(2,1)S(1)}, u32[]{:S(2)}, u32[]{:S(2)}) %collective-permute-start.5) | collective-permute-done | bytes 131104 | tf_op jit(solution)/shard_map/ppermute | solution.py:50
  23.5 0.4 shard_map.117
  23.9 1.6 %collective-permute-start.8 = (bf16[256,256]{1,0:T(8,128)(2,1)S(1)}, bf16[256,256]{1,0:T(8,128)(2,1)S(1)}, u32[]{:S(2)}, u32[]{:S(2)}) collective-permute-start(bf16[256,256]{1,0:T(8,128)(2,1)S(1)} %get-tuple-element.16.refs_3_.grad_ref), channel_id=1, source_target_pairs={{0,8},{4,12},{8,0},{12,4},{16,24},{20,28},{24,16},{28,20},{1,9},{5... | collective-permute-start | bytes 393224 | tf_op jit(solution)/shard_map/ppermute | solution.py:50
  25.5 1.4 %collective-permute-start.7 = (bf16[256,256]{1,0:T(8,128)(2,1)S(1)}, bf16[256,256]{1,0:T(8,128)(2,1)S(1)}, u32[]{:S(2)}, u32[]{:S(2)}) collective-permute-start(bf16[256,256]{1,0:T(8,128)(2,1)S(1)} %get-tuple-element.16.refs_3_.grad_ref), channel_id=1, source_target_pairs={{0,24},{4,28},{8,16},{12,20},{16,8},{20,12},{24,0},{28,4},{1,25},{... | collective-permute-start | bytes 393224 | tf_op jit(solution)/shard_map/ppermute | solution.py:50
  26.9 0.6 %collective-permute-start.9 = (bf16[256,256]{1,0:T(8,128)(2,1)S(1)}, bf16[256,256]{1,0:T(8,128)(2,1)S(1)}, u32[]{:S(2)}, u32[]{:S(2)}) collective-permute-start(bf16[256,256]{1,0:T(8,128)(2,1)S(1)} %get-tuple-element.16.refs_3_.grad_ref), channel_id=1, source_target_pairs={{0,16},{4,20},{8,24},{12,28},{16,0},{20,4},{24,8},{28,12},{1,17},{... | collective-permute-start | bytes 393224 | tf_op jit(solution)/shard_map/ppermute | solution.py:50
  27.5 1.7 %collective-permute-done.8.refs_1_.after_ref = bf16[256,256]{1,0:T(8,128)(2,1)S(1)} collective-permute-done((bf16[256,256]{1,0:T(8,128)(2,1)S(1)}, bf16[256,256]{1,0:T(8,128)(2,1)S(1)}, u32[]{:S(2)}, u32[]{:S(2)}) %collective-permute-start.8) | collective-permute-done | bytes 131104 | tf_op jit(solution)/shard_map/ppermute | solution.py:50
  29.5 2.2 %collective-permute-start.13 = (bf16[144,256]{1,0:T(8,128)(2,1)S(1)}, bf16[144,256]{1,0:T(8,128)(2,1)S(1)}, u32[]{:S(2)}, u32[]{:S(2)}) collective-permute-start(bf16[144,256]{1,0:T(8,128)(2,1)S(1)} %shard_map.126.refs_3_), channel_id=1, source_target_pairs={{0,3},{1,2},{2,1},{3,0},{4,7},{5,6},{6,5},{7,4},{8,11},{9,10},{10,... | collective-permute-start | bytes 221192 | tf_op jit(solution)/shard_map/ppermute | solution.py:50
  31.7 0.4 collective-permute-start.14
  32.0 1.9 %collective-permute-start.15 = (bf16[144,256]{1,0:T(8,128)(2,1)S(1)}, bf16[144,256]{1,0:T(8,128)(2,1)S(1)}, u32[]{:S(2)}, u32[]{:S(2)}) collective-permute-start(bf16[144,256]{1,0:T(8,128)(2,1)S(1)} %shard_map.126.refs_3_), channel_id=1, source_target_pairs={{0,2},{1,3},{2,0},{3,1},{4,6},{5,7},{6,4},{7,5},{8,10},{9,11},{10,... | collective-permute-start | bytes 221192 | tf_op jit(solution)/shard_map/ppermute | solution.py:50
  33.9 0.3 shard_map.119.turned_ref
  34.9 2.2 %collective-permute-start.10 = (bf16[128,256]{1,0:T(8,128)(2,1)S(1)}, bf16[128,256]{1,0:T(8,128)(2,1)S(1)}, u32[]{:S(2)}, u32[]{:S(2)}) collective-permute-start(bf16[128,256]{1,0:T(8,128)(2,1)S(1)} %shard_map.121.refs_0_), channel_id=1, source_target_pairs={{0,3},{1,2},{2,1},{3,0},{4,7},{5,6},{6,5},{7,4},{8,11},{9,10},{10,... | collective-permute-start | bytes 196616 | tf_op jit(solution)/shard_map/ppermute | solution.py:50
  37.9 5.2 %collective-permute-start.16 = (bf16[144,256]{1,0:T(8,128)(2,1)S(1)}, bf16[144,256]{1,0:T(8,128)(2,1)S(1)}, u32[]{:S(2)}, u32[]{:S(2)}) collective-permute-start(bf16[144,256]{1,0:T(8,128)(2,1)S(1)} %shard_map.127.refs_3_), channel_id=1, source_target_pairs={{0,24},{4,28},{8,16},{12,20},{16,8},{20,12},{24,0},{28,4},{1,25},{... | collective-permute-start | bytes 221192 | tf_op jit(solution)/shard_map/ppermute | solution.py:50
  43.1 0.5 %collective-permute-start.17 = (bf16[144,256]{1,0:T(8,128)(2,1)S(1)}, bf16[144,256]{1,0:T(8,128)(2,1)S(1)}, u32[]{:S(2)}, u32[]{:S(2)}) collective-permute-start(bf16[144,256]{1,0:T(8,128)(2,1)S(1)} %shard_map.127.refs_3_), channel_id=1, source_target_pairs={{0,8},{4,12},{8,0},{12,4},{16,24},{20,28},{24,16},{28,20},{1,9},{5... | collective-permute-start | bytes 221192 | tf_op jit(solution)/shard_map/ppermute | solution.py:50
  43.7 2.4 %collective-permute-start.12 = (bf16[128,256]{1,0:T(8,128)(2,1)S(1)}, bf16[128,256]{1,0:T(8,128)(2,1)S(1)}, u32[]{:S(2)}, u32[]{:S(2)}) collective-permute-start(bf16[128,256]{1,0:T(8,128)(2,1)S(1)} %shard_map.123.refs_0_), channel_id=1, source_target_pairs={{0,2},{1,3},{2,0},{3,1},{4,6},{5,7},{6,4},{7,5},{8,10},{9,11},{10,... | collective-permute-start | bytes 196616 | tf_op jit(solution)/shard_map/ppermute | solution.py:50
  46.2 1.8 %collective-permute-done.11.refs_1_ = bf16[128,256]{1,0:T(8,128)(2,1)S(1)} collective-permute-done((bf16[128,256]{1,0:T(8,128)(2,1)S(1)}, bf16[128,256]{1,0:T(8,128)(2,1)S(1)}, u32[]{:S(2)}, u32[]{:S(2)}) %collective-permute-start.11) | collective-permute-done | bytes 65568 | tf_op jit(solution)/shard_map/ppermute | solution.py:50
  48.0 0.9 %collective-permute-done.12.refs_2_ = bf16[128,256]{1,0:T(8,128)(2,1)S(1)} collective-permute-done((bf16[128,256]{1,0:T(8,128)(2,1)S(1)}, bf16[128,256]{1,0:T(8,128)(2,1)S(1)}, u32[]{:S(2)}, u32[]{:S(2)}) %collective-permute-start.12) | collective-permute-done | bytes 65568 | tf_op jit(solution)/shard_map/ppermute | solution.py:50
  48.9 0.8 %shard_map.125.after_ref = bf16[128,256]{1,0:T(8,128)(2,1)} custom-call(bf16[256,256]{1,0:T(8,128)(2,1)S(1)} %copy-done, bf16[128,256]{1,0:T(8,128)(2,1)S(1)} %collective-permute-done.10.refs_0_, bf16[128,256]{1,0:T(8,128)(2,1)S(1)} %collective-permute-done.11.refs_1_, bf16[128,256]{1,0:T(8,128)(2,1)S(1)} %collective-permute-done.12.refs_2_, ...), custom_call_target="tpu_custom_call" | custom-call | flops 16777216 | bytes 262144 | tf_op jit(solution)/shard_map/pallas_call | solution.py:418
  49.9 0.6 %shard_map.118 = bf16[128,256]{1,0:T(8,128)(2,1)} custom-call(bf16[256,256]{1,0:T(8,128)(2,1)S(1)} %get-tuple-element.15.both_ref), custom_call_target="tpu_custom_call" | custom-call | bytes 131072 | tf_op jit(solution)/shard_map/pallas_call | solution.py:363
  50.5 0.7 %collective-permute-done.19.other_ref = f32[128,256]{1,0:T(8,128)S(1)} collective-permute-done((f32[128,256]{1,0:T(8,128)S(1)}, f32[128,256]{1,0:T(8,128)S(1)}, u32[]{:S(2)}, u32[]{:S(2)}) %collective-permute-start.19) | collective-permute-done | bytes 131104 | tf_op jit(solution)/shard_map/ppermute | solution.py:434
  51.2 0.7 %shard_map.129 = (f32[256,256]{1,0:T(8,128)}, f32[1,256]{1,0:T(1,128)}) custom-call(f32[128,256]{1,0:T(8,128)S(1)} %get-tuple-element.18.own_ref, f32[128,256]{1,0:T(8,128)S(1)} %collective-permute-done.19.other_ref, f32[1,256]{1,0:T(1,128)S(1)} %get-tuple-element.19.bias_ref), custom_call_target="tpu_custom_call" | custom-call | bytes 524288 | tf_op jit(solution)/shard_map/pallas_call | solution.py:435
  (33 shorter events, 2.1 us)
Async XLA Ops:
  0.6 8.2 %collective-permute-start = (bf16[128,256]{1,0:T(8,128)(2,1)}, bf16[128,256]{1,0:T(8,128)(2,1)S(1)}, u32[]{:S(2)}, u32[]{:S(2)}) collective-permute-start(bf16[128,256]{1,0:T(8,128)(2,1)} %refs_4_.1), channel_id=1, source_target_pairs={{0,3},{1,2},{2,1},{3,0},{4,7},{5,6},{6,5},{7,4},{8,11},{9,10},{10,... | collective-permute-start | bytes 196616 | tf_op jit(solution)/shard_map/ppermute | solution.py:50
  5.7 4.9 %collective-permute-start.1 = (bf16[128,256]{1,0:T(8,128)(2,1)}, bf16[128,256]{1,0:T(8,128)(2,1)S(1)}, u32[]{:S(2)}, u32[]{:S(2)}) collective-permute-start(bf16[128,256]{1,0:T(8,128)(2,1)} %refs_4_.1), channel_id=1, source_target_pairs={{0,1},{1,0},{2,3},{3,2},{4,5},{5,4},{6,7},{7,6},{8,9},{9,8},{10,11... | collective-permute-start | bytes 196616 | tf_op jit(solution)/shard_map/ppermute | solution.py:50
  5.8 5.8 %collective-permute-start.2 = (bf16[128,256]{1,0:T(8,128)(2,1)}, bf16[128,256]{1,0:T(8,128)(2,1)S(1)}, u32[]{:S(2)}, u32[]{:S(2)}) collective-permute-start(bf16[128,256]{1,0:T(8,128)(2,1)} %refs_4_.1), channel_id=1, source_target_pairs={{0,2},{1,3},{2,0},{3,1},{4,6},{5,7},{6,4},{7,5},{8,10},{9,11},{10,... | collective-permute-start | bytes 196616 | tf_op jit(solution)/shard_map/ppermute | solution.py:50
  7.0 4.6 %copy-start.1 = (bf16[128,256]{1,0:T(8,128)(2,1)S(1)}, bf16[128,256]{1,0:T(8,128)(2,1)}, u32[]{:S(2)}) copy-start(bf16[128,256]{1,0:T(8,128)(2,1)} %cot_ref.1) | copy-start | bytes 196612
  7.1 4.5 %copy-start.2 = (bf16[128,256]{1,0:T(8,128)(2,1)S(1)}, bf16[128,256]{1,0:T(8,128)(2,1)}, u32[]{:S(2)}) copy-start(bf16[128,256]{1,0:T(8,128)(2,1)} %refs_4_.1) | copy-start | bytes 196612
  12.1 2.1 %collective-permute-start.3 = (bf16[1152,256]{1,0:T(8,128)(2,1)S(1)}, bf16[1152,256]{1,0:T(8,128)(2,1)S(1)}, u32[]{:S(2)}, u32[]{:S(2)}) collective-permute-start(bf16[1152,256]{1,0:T(8,128)(2,1)S(1)} %shard_map.112.own_ref), channel_id=1, source_target_pairs={{0,4},{4,0},{8,12},{12,8},{16,20},{20,16},{24,28},{28,24},{1,5},{5... | collective-permute-start | bytes 1769480 | tf_op jit(solution)/shard_map/ppermute | solution.py:331
  14.2 7.3 %collective-permute-start.4 = (bf16[256,256]{1,0:T(8,128)(2,1)S(1)}, bf16[256,256]{1,0:T(8,128)(2,1)S(1)}, u32[]{:S(2)}, u32[]{:S(2)}) collective-permute-start(bf16[256,256]{1,0:T(8,128)(2,1)S(1)} %shard_map.113.refs_0_), channel_id=1, source_target_pairs={{0,24},{4,28},{8,16},{12,20},{16,8},{20,12},{24,0},{28,4},{1,25},{... | collective-permute-start | bytes 393224 | tf_op jit(solution)/shard_map/ppermute | solution.py:50
  16.7 6.8 %collective-permute-start.5 = (bf16[256,256]{1,0:T(8,128)(2,1)S(1)}, bf16[256,256]{1,0:T(8,128)(2,1)S(1)}, u32[]{:S(2)}, u32[]{:S(2)}) collective-permute-start(bf16[256,256]{1,0:T(8,128)(2,1)S(1)} %shard_map.114.refs_0_), channel_id=1, source_target_pairs={{0,8},{4,12},{8,0},{12,4},{16,24},{20,28},{24,16},{28,20},{1,9},{5... | collective-permute-start | bytes 393224 | tf_op jit(solution)/shard_map/ppermute | solution.py:50
  17.4 6.2 %copy-start = (bf16[256,256]{1,0:T(8,128)(2,1)S(1)}, bf16[256,256]{1,0:T(8,128)(2,1)}, u32[]{:S(2)}) copy-start(bf16[256,256]{1,0:T(8,128)(2,1)} %weight_ref.3) | copy-start | bytes 393220
  17.4 6.2 %collective-permute-start.6 = (bf16[256,256]{1,0:T(8,128)(2,1)S(1)}, bf16[256,256]{1,0:T(8,128)(2,1)S(1)}, u32[]{:S(2)}, u32[]{:S(2)}) collective-permute-start(bf16[256,256]{1,0:T(8,128)(2,1)S(1)} %shard_map.115.refs_0_), channel_id=1, source_target_pairs={{0,16},{4,20},{8,24},{12,28},{16,0},{20,4},{24,8},{28,12},{1,17},{... | collective-permute-start | bytes 393224 | tf_op jit(solution)/shard_map/ppermute | solution.py:50
  23.9 5.3 %collective-permute-start.8 = (bf16[256,256]{1,0:T(8,128)(2,1)S(1)}, bf16[256,256]{1,0:T(8,128)(2,1)S(1)}, u32[]{:S(2)}, u32[]{:S(2)}) collective-permute-start(bf16[256,256]{1,0:T(8,128)(2,1)S(1)} %get-tuple-element.16.refs_3_.grad_ref), channel_id=1, source_target_pairs={{0,8},{4,12},{8,0},{12,4},{16,24},{20,28},{24,16},{28,20},{1,9},{5... | collective-permute-start | bytes 393224 | tf_op jit(solution)/shard_map/ppermute | solution.py:50
  25.5 8.8 %collective-permute-start.7 = (bf16[256,256]{1,0:T(8,128)(2,1)S(1)}, bf16[256,256]{1,0:T(8,128)(2,1)S(1)}, u32[]{:S(2)}, u32[]{:S(2)}) collective-permute-start(bf16[256,256]{1,0:T(8,128)(2,1)S(1)} %get-tuple-element.16.refs_3_.grad_ref), channel_id=1, source_target_pairs={{0,24},{4,28},{8,16},{12,20},{16,8},{20,12},{24,0},{28,4},{1,25},{... | collective-permute-start | bytes 393224 | tf_op jit(solution)/shard_map/ppermute | solution.py:50
  26.9 7.7 %collective-permute-start.9 = (bf16[256,256]{1,0:T(8,128)(2,1)S(1)}, bf16[256,256]{1,0:T(8,128)(2,1)S(1)}, u32[]{:S(2)}, u32[]{:S(2)}) collective-permute-start(bf16[256,256]{1,0:T(8,128)(2,1)S(1)} %get-tuple-element.16.refs_3_.grad_ref), channel_id=1, source_target_pairs={{0,16},{4,20},{8,24},{12,28},{16,0},{20,4},{24,8},{28,12},{1,17},{... | collective-permute-start | bytes 393224 | tf_op jit(solution)/shard_map/ppermute | solution.py:50
  29.5 8.4 %collective-permute-start.13 = (bf16[144,256]{1,0:T(8,128)(2,1)S(1)}, bf16[144,256]{1,0:T(8,128)(2,1)S(1)}, u32[]{:S(2)}, u32[]{:S(2)}) collective-permute-start(bf16[144,256]{1,0:T(8,128)(2,1)S(1)} %shard_map.126.refs_3_), channel_id=1, source_target_pairs={{0,3},{1,2},{2,1},{3,0},{4,7},{5,6},{6,5},{7,4},{8,11},{9,10},{10,... | collective-permute-start | bytes 221192 | tf_op jit(solution)/shard_map/ppermute | solution.py:50
  31.7 6.1 %collective-permute-start.14 = (bf16[144,256]{1,0:T(8,128)(2,1)S(1)}, bf16[144,256]{1,0:T(8,128)(2,1)S(1)}, u32[]{:S(2)}, u32[]{:S(2)}) collective-permute-start(bf16[144,256]{1,0:T(8,128)(2,1)S(1)} %shard_map.126.refs_3_), channel_id=1, source_target_pairs={{0,1},{1,0},{2,3},{3,2},{4,5},{5,4},{6,7},{7,6},{8,9},{9,8},{10,11... | collective-permute-start | bytes 221192 | tf_op jit(solution)/shard_map/ppermute | solution.py:50
  32.0 5.8 %collective-permute-start.15 = (bf16[144,256]{1,0:T(8,128)(2,1)S(1)}, bf16[144,256]{1,0:T(8,128)(2,1)S(1)}, u32[]{:S(2)}, u32[]{:S(2)}) collective-permute-start(bf16[144,256]{1,0:T(8,128)(2,1)S(1)} %shard_map.126.refs_3_), channel_id=1, source_target_pairs={{0,2},{1,3},{2,0},{3,1},{4,6},{5,7},{6,4},{7,5},{8,10},{9,11},{10,... | collective-permute-start | bytes 221192 | tf_op jit(solution)/shard_map/ppermute | solution.py:50
  34.9 8.9 %collective-permute-start.10 = (bf16[128,256]{1,0:T(8,128)(2,1)S(1)}, bf16[128,256]{1,0:T(8,128)(2,1)S(1)}, u32[]{:S(2)}, u32[]{:S(2)}) collective-permute-start(bf16[128,256]{1,0:T(8,128)(2,1)S(1)} %shard_map.121.refs_0_), channel_id=1, source_target_pairs={{0,3},{1,2},{2,1},{3,0},{4,7},{5,6},{6,5},{7,4},{8,11},{9,10},{10,... | collective-permute-start | bytes 196616 | tf_op jit(solution)/shard_map/ppermute | solution.py:50
  37.9 11.8 %collective-permute-start.16 = (bf16[144,256]{1,0:T(8,128)(2,1)S(1)}, bf16[144,256]{1,0:T(8,128)(2,1)S(1)}, u32[]{:S(2)}, u32[]{:S(2)}) collective-permute-start(bf16[144,256]{1,0:T(8,128)(2,1)S(1)} %shard_map.127.refs_3_), channel_id=1, source_target_pairs={{0,24},{4,28},{8,16},{12,20},{16,8},{20,12},{24,0},{28,4},{1,25},{... | collective-permute-start | bytes 221192 | tf_op jit(solution)/shard_map/ppermute | solution.py:50
  43.1 6.7 %collective-permute-start.17 = (bf16[144,256]{1,0:T(8,128)(2,1)S(1)}, bf16[144,256]{1,0:T(8,128)(2,1)S(1)}, u32[]{:S(2)}, u32[]{:S(2)}) collective-permute-start(bf16[144,256]{1,0:T(8,128)(2,1)S(1)} %shard_map.127.refs_3_), channel_id=1, source_target_pairs={{0,8},{4,12},{8,0},{12,4},{16,24},{20,28},{24,16},{28,20},{1,9},{5... | collective-permute-start | bytes 221192 | tf_op jit(solution)/shard_map/ppermute | solution.py:50
  43.6 6.1 %collective-permute-start.18 = (bf16[144,256]{1,0:T(8,128)(2,1)S(1)}, bf16[144,256]{1,0:T(8,128)(2,1)S(1)}, u32[]{:S(2)}, u32[]{:S(2)}) collective-permute-start(bf16[144,256]{1,0:T(8,128)(2,1)S(1)} %shard_map.127.refs_3_), channel_id=1, source_target_pairs={{0,16},{4,20},{8,24},{12,28},{16,0},{20,4},{24,8},{28,12},{1,17},{... | collective-permute-start | bytes 221192 | tf_op jit(solution)/shard_map/ppermute | solution.py:50
  43.7 4.3 %collective-permute-start.11 = (bf16[128,256]{1,0:T(8,128)(2,1)S(1)}, bf16[128,256]{1,0:T(8,128)(2,1)S(1)}, u32[]{:S(2)}, u32[]{:S(2)}) collective-permute-start(bf16[128,256]{1,0:T(8,128)(2,1)S(1)} %shard_map.122.refs_0_), channel_id=1, source_target_pairs={{0,1},{1,0},{2,3},{3,2},{4,5},{5,4},{6,7},{7,6},{8,9},{9,8},{10,11... | collective-permute-start | bytes 196616 | tf_op jit(solution)/shard_map/ppermute | solution.py:50
  43.7 5.2 %collective-permute-start.12 = (bf16[128,256]{1,0:T(8,128)(2,1)S(1)}, bf16[128,256]{1,0:T(8,128)(2,1)S(1)}, u32[]{:S(2)}, u32[]{:S(2)}) collective-permute-start(bf16[128,256]{1,0:T(8,128)(2,1)S(1)} %shard_map.123.refs_0_), channel_id=1, source_target_pairs={{0,2},{1,3},{2,0},{3,1},{4,6},{5,7},{6,4},{7,5},{8,10},{9,11},{10,... | collective-permute-start | bytes 196616 | tf_op jit(solution)/shard_map/ppermute | solution.py:50
  49.8 1.4 %collective-permute-start.19 = (f32[128,256]{1,0:T(8,128)S(1)}, f32[128,256]{1,0:T(8,128)S(1)}, u32[]{:S(2)}, u32[]{:S(2)}) collective-permute-start(f32[128,256]{1,0:T(8,128)S(1)} %get-tuple-element.18.own_ref), channel_id=1, source_target_pairs={{0,4},{4,0},{8,12},{12,8},{16,20},{20,16},{24,28},{28,24},{1,5},{5... | collective-permute-start | bytes 393224 | tf_op jit(solution)/shard_map/ppermute | solution.py:434

commit v5 on v4

v5 whole, which is shorter than its diff:
```python
import functools

import jax
import jax.numpy as jnp
from jax import lax
from jax.experimental import pallas as pl
from jax.experimental.pallas import tpu as pltpu
from jax.sharding import PartitionSpec as P

F32 = jnp.float32
BF16 = jnp.bfloat16
ROOT_2_OVER_PI = 0.7978845608028654
CUBIC = 0.044715
VMEM_LIMIT = 48 * 1024 * 1024
BIAS_ROWS = 16

VMEM_SPEC = pl.BlockSpec(memory_space=pltpu.VMEM)
HBM_SPEC = pl.BlockSpec(memory_space=pltpu.HBM)
SMEM_SPEC = pl.BlockSpec(memory_space=pltpu.SMEM)


def call(kernel, out_shape, in_specs, scratch, flops, moved):
    return pl.pallas_call(
        kernel,
        out_shape=out_shape,
        in_specs=in_specs,
        out_specs=jax.tree.map(lambda _: VMEM_SPEC, out_shape),
        scratch_shapes=scratch,
        compiler_params=pltpu.CompilerParams(vmem_limit_bytes=VMEM_LIMIT),
        cost_estimate=pl.CostEstimate(flops=flops, bytes_accessed=moved, transcendentals=0),
    )


def partner(index, k, count):
    if count & (count - 1) == 0:
        return index ^ k
    return (k - index) % count


def far_first(count):
    return list(dict.fromkeys([count - 1, *range(1, count), 0]))


def pairs_of(k, size, cores):
    return [(i, partner(i // cores, k, size // cores) * cores + i % cores) for i in range(size)]


def exchange(blocks, axis, size, cores=1):
    received = []
    for k in far_first(size // cores):
        pairs = pairs_of(k, size, cores)
        moves = any(i != j for i, j in pairs)
        received.append(lax.ppermute(blocks[k], axis, pairs) if moves else blocks[k])
    return received


def swap_cores(block, size):
    return lax.ppermute(block, "col", [(i, i ^ 1) for i in range(size)])


def total_over(block, add, axis, size, cores=1):
    count = size // cores
    if count & (count - 1):
        return exchange([block] * count, axis, size, cores)
    terms, step = [block], 1
    while step < count:
        block = add(terms) if len(terms) > 1 else block
        terms = [lax.ppermute(block, axis, pairs_of(step, size, cores)), block]
        step *= 2
    return terms


def block_at(index, size):
    return pl.ds(pl.multiple_of(index * size, size), size)


def row_index():
    return lax.axis_index("row")


def chip_index():
    return lax.axis_index("col") // 2


def core_index():
    return lax.axis_index("col") % 2


def summed(refs):
    by_partner = dict(zip(far_first(len(refs)), refs))
    values = [by_partner[k][...].astype(F32) for k in sorted(by_partner)]
    while len(values) > 1:
        values = [sum(values[i + 1 : i + 2], values[i]) for i in range(0, len(values), 2)]
    return values[0]


def bias_rows(bias):
    high = bias.astype(BF16).astype(F32)
    line = lax.broadcasted_iota(jnp.int32, (BIAS_ROWS, bias.shape[1]), 0)
    return jnp.where(line == 0, high, jnp.where(line == 1, bias - high, 0.0))


def row_place(row, n_chip):
    return jnp.where(row % 2 == core_index(), 0, n_chip) + row // 2


def dense_kernel(
    count_ref, row_hbm, col_hbm, tiles_hbm, bias_hbm, dense_ref, bias_ref,
    row_ref, col_ref, tiles_ref, sum_ref, sems, tile_sems,
):
    slots, tile = tiles_ref.shape[0], tiles_ref.shape[1]
    n_chip = sum_ref.shape[0] // (2 * tile)
    chunks = tile_sems.shape[0]
    size = slots // chunks
    small = [
        pltpu.make_async_copy(row_hbm, row_ref, sems.at[0]),
        pltpu.make_async_copy(col_hbm, col_ref, sems.at[1]),
        pltpu.make_async_copy(bias_hbm, bias_ref, sems.at[2]),
    ]
    large = []
    for k in range(chunks):
        part = pl.ds(k * size, size)
        large.append(
            pltpu.make_async_copy(tiles_hbm.at[0, 0, part], tiles_ref.at[part], tile_sems.at[k])
        )
    for copy in small + large:
        copy.start()
    sum_ref[...] = jnp.zeros_like(sum_ref)
    for copy in small:
        copy.wait()
    count = count_ref[0, 0]

    def body(slot, carry):
        rows = block_at(row_place(row_ref[0, 0, slot], n_chip), tile)
        cols = block_at(col_ref[0, 0, slot], tile)
        sum_ref[rows, cols] += tiles_ref[slot].astype(F32)
        return carry

    for k, copy in enumerate(large):
        copy.wait()
        lax.fori_loop(k * size, jnp.minimum(count, (k + 1) * size), body, 0)
    dense_ref[...] = sum_ref[...].astype(BF16)


def turn_kernel(dense_ref, after_ref, turned_ref):
    rows = dense_ref.shape[0]
    step = 256 if rows % 256 == 0 else rows
    for first in range(0, rows, step):
        turned_ref[:, first : first + step] = dense_ref[first : first + step, :].T


def dense_dot(left, right):
    return jnp.dot(left, right, preferred_element_type=F32)


def gather_sources(sources, source_ref, index):
    tile = sources[0].shape[0]
    for k, ref in zip(far_first(len(sources)), sources):
        source_ref[block_at(partner(index, k, len(sources)), tile), :] = ref[...]


def slot_product(refs, source_ref, acc_ref, turned):
    count_ref, row_ref, col_ref, tiles_ref = refs
    tile = tiles_ref.shape[1]
    n_chip = (source_ref if turned else acc_ref).shape[0] // (2 * tile)
    contract = 0 if turned else 1
    acc_ref[...] = jnp.zeros_like(acc_ref)

    def body(slot, carry):
        places = [row_place(row_ref[slot], n_chip), col_ref[slot]]
        source, target = places if turned else places[::-1]
        acc_ref[block_at(target, tile), :] += lax.dot_general(
            tiles_ref[slot],
            source_ref[block_at(source, tile), :],
            (((contract,), (0,)), ((), ())),
            preferred_element_type=F32,
        )
        return carry

    lax.fori_loop(0, count_ref[0], body, 0)


def forward_other_kernel(dense_ref, *refs):
    sources, (other_ref, source_ref) = refs[:-2], refs[-2:]
    gather_sources(sources, source_ref, row_index())
    half = other_ref.shape[0]
    other_ref[...] = dense_dot(dense_ref[half:, :], source_ref[...]).astype(BF16)


def forward_own_kernel(dense_ref, source_ref, own_ref):
    own_ref[...] = dense_dot(dense_ref[: own_ref.shape[0], :], source_ref[...]).astype(BF16)


def slot_forward_kernel(count_ref, row_ref, col_ref, tiles_ref, *refs):
    sources, (other_ref, own_ref, source_ref, acc_ref) = refs[:-4], refs[-4:]
    gather_sources(sources, source_ref, row_index())
    slot_product((count_ref, row_ref, col_ref, tiles_ref), source_ref, acc_ref, False)
    half = own_ref.shape[0]
    own_ref[...] = acc_ref[:half, :].astype(BF16)
    other_ref[...] = acc_ref[half:, :].astype(BF16)


def chip_kernel(own_ref, other_ref, *refs, k, n_chip):
    out_ref = refs[-1]
    rows = block_at(partner(chip_index(), k, n_chip), out_ref.shape[0])
    out_ref[...] = (own_ref[rows, :].astype(F32) + other_ref[rows, :].astype(F32)).astype(BF16)


def middle_kernel(weight_ref, bias_ref, cot_ref, *refs):
    parts, (hidden_ref, grad_ref, agg_ref) = refs[:-3], refs[-3:]
    aggregated = summed(parts).astype(BF16)
    agg_ref[...] = aggregated
    v = dense_dot(aggregated, weight_ref[...]) + bias_ref[...]
    square = v * v
    t = jnp.tanh(ROOT_2_OVER_PI * (v + CUBIC * (square * v)))
    half = 0.5 * (1.0 + t)
    hidden_ref[...] = (v * half).astype(BF16)
    slope = half + 0.5 * v * (1.0 - t * t) * (ROOT_2_OVER_PI * (1.0 + 3.0 * CUBIC * square))
    grad_ref[...] = (cot_ref[...].astype(F32) * slope).astype(BF16)


def copy_kernel(in_ref, out_ref):
    out_ref[...] = in_ref[...]


def term_kernel(agg_ref, grad_ref, mine_ref, theirs_ref, acc_ref):
    grad = grad_ref[...]
    acc_ref[...] = lax.dot_general(
        agg_ref[...], grad, (((0,), (0,)), ((), ())), preferred_element_type=F32
    )
    half = acc_ref.shape[0] // 2
    bias = bias_rows(jnp.sum(grad.astype(F32), axis=0, keepdims=True)).astype(BF16)
    for ref, core in ((mine_ref, core_index()), (theirs_ref, 1 - core_index())):
        ref[:half, :] = acc_ref[block_at(core, half), :].astype(BF16)
        ref[half:, :] = bias


def add_terms_kernel(*refs, n_terms):
    total = summed(refs[:n_terms])
    out_ref = refs[-1]
    half = total.shape[0] - BIAS_ROWS
    out_ref[:half, :] = total[:half].astype(BF16)
    out_ref[half:, :] = bias_rows(total[half : half + 1] + total[half + 1 : half + 2]).astype(BF16)


def scale_kernel(after_ref, *refs, factor):
    parts, (half_ref, bias_ref) = refs[:-2], refs[-2:]
    total = summed(parts) * factor
    half = half_ref.shape[0]
    half_ref[...] = total[:half]
    bias_ref[...] = total[half : half + 1] + total[half + 1 : half + 2]


def gather_kernel(after_ref, *refs):
    gather_sources(refs[:-1], refs[-1], chip_index())


def back_own_kernel(turned_ref, source_ref, out_ref):
    out_ref[...] = dense_dot(turned_ref[:, : source_ref.shape[0]], source_ref[...])


def slot_back_kernel(count_ref, row_ref, col_ref, tiles_ref, own_ref, other_ref, out_ref, source_ref):
    half = own_ref.shape[0]
    source_ref[:half, :] = own_ref[...]
    source_ref[half:, :] = other_ref[...]
    slot_product((count_ref, row_ref, col_ref, tiles_ref), source_ref, out_ref, True)


def back_rows(refs, place):
    if len(refs) == 1:
        return refs[0][place, :]
    turned_ref, own_ref, source_ref = refs
    rest = dense_dot(turned_ref[place, source_ref.shape[0] :], source_ref[...])
    return own_ref[place, :] + rest


def back_near_kernel(*refs, targets):
    out_ref = refs[-1]
    tile = out_ref.shape[0] // len(targets)
    for i, k in enumerate(targets):
        place = block_at(row_index() ^ k, tile)
        out_ref[i * tile : (i + 1) * tile, :] = back_rows(refs[:-1], place).astype(BF16)


def back_far_kernel(*refs, k, at):
    near_ref, out_ref = refs[-2:]
    tile = out_ref.shape[0]
    rows = back_rows(refs[:-2], block_at(row_index() ^ k, tile))
    near = near_ref[at * tile : (at + 1) * tile, :].astype(F32)
    out_ref[...] = (rows + near).astype(BF16)


def features_kernel(weight_ref, near_ref, *refs):
    parts, out_ref = refs[:-1], refs[-1]
    total = near_ref[: out_ref.shape[0], :].astype(F32)
    for ref in parts:
        total += ref[...].astype(F32)
    out_ref[...] = lax.dot_general(
        total.astype(BF16),
        weight_ref[...],
        (((1,), (1,)), ((), ())),
        preferred_element_type=F32,
    ).astype(BF16)


def join_kernel(own_ref, other_ref, bias_ref, weight_ref, bias_out):
    half = own_ref.shape[0]
    weight_ref[block_at(core_index(), half), :] = own_ref[...]
    weight_ref[block_at(1 - core_index(), half), :] = other_ref[...]
    bias_out[...] = bias_ref[...]


def in_turn(count, make):
    made, before = {}, []
    for k in far_first(count):
        made[k] = make(k, before)
        before = [made[k]]
    return made


def local(features, weight, bias_term, cotangent, tile_values, tile_row, tile_col, tile_count):
    n_row = lax.axis_size("row")
    n_col = lax.axis_size("col")
    n_chip = n_col // 2
    tile, width = features.shape
    hidden = weight.shape[1]
    slots = tile_values.shape[2]
    row_nodes, col_nodes = n_col * tile, n_row * tile
    bias_row = bias_term.reshape(1, hidden)
    half = width // 2
    matrix = 2 * tile * width * hidden
    block_bytes = 2 * tile * width

    def like(rows, columns, dtype=BF16):
        return jax.ShapeDtypeStruct((rows, columns), dtype)

    near = 1
    own_nodes = n_chip * tile

    def add(terms, after=()):
        return call(
            functools.partial(add_terms_kernel, n_terms=len(terms)),
            like(half + BIAS_ROWS, hidden),
            [VMEM_SPEC] * (len(terms) + len(after)),
            [],
            len(terms) * half * hidden,
            len(terms) * half * hidden * 2,
        )(*terms, *after)

    is_dense = n_row * n_col <= 2 * slots
    if is_dense:
        chunks = 4 if slots % 4 == 0 else 1
        dense, bias_row = call(
            dense_kernel,
            (like(row_nodes, col_nodes), like(1, hidden, F32)),
            [SMEM_SPEC] + [HBM_SPEC] * 4,
            [
                pltpu.SMEM((1, 1, slots), jnp.int32),
                pltpu.SMEM((1, 1, slots), jnp.int32),
                pltpu.VMEM((slots, tile, tile), BF16),
                pltpu.VMEM((row_nodes, col_nodes), F32),
                pltpu.SemaphoreType.DMA((3,)),
                pltpu.SemaphoreType.DMA((chunks,)),
            ],
            0,
            12 * row_nodes * col_nodes,
        )(tile_count, *(
            pltpu.with_memory_space_constraint(array, pltpu.HBM)
            for array in (tile_row, tile_col, tile_values, bias_row)
        ))
    else:
        slot_args = (
            tile_count.reshape(1),
            tile_row.reshape(slots),
            tile_col.reshape(slots),
            tile_values.reshape(slots, tile, tile),
        )
        slot_specs = [SMEM_SPEC] * 3 + [VMEM_SPEC]

    sources = exchange([features] * n_row, "row", n_row)
    if is_dense:
        other, source = call(
            forward_other_kernel,
            (like(own_nodes, width), like(col_nodes, width)),
            [VMEM_SPEC] * (1 + n_row),
            [],
            slots * matrix // 2,
            row_nodes * width * 8,
        )(dense, *sources)
        own = call(
            forward_own_kernel,
            like(own_nodes, width),
            [VMEM_SPEC] * 2,
            [],
            slots * matrix // 2,
            row_nodes * width * 8,
        )(dense, source)
    else:
        other, own = call(
            slot_forward_kernel,
            (like(own_nodes, width), like(own_nodes, width)),
            slot_specs + [VMEM_SPEC] * n_row,
            [pltpu.VMEM((col_nodes, width), BF16), pltpu.VMEM((row_nodes, width), F32)],
            slots * matrix // 2,
            row_nodes * width * 8,
        )(*slot_args, *sources)
    swapped = swap_cores(other, n_col)

    def chip_piece(k, before):
        return call(
            functools.partial(chip_kernel, k=k, n_chip=n_chip),
            like(tile, width),
            [VMEM_SPEC] * (2 + len(before)),
            [],
            tile * width,
            3 * block_bytes,
        )(own, swapped, *before)

    pieces = in_turn(n_chip, chip_piece)
    parts = exchange(pieces, "col", n_col, 2)
    if is_dense:
        turned = call(
            turn_kernel,
            like(col_nodes, row_nodes),
            [VMEM_SPEC] * 2,
            [],
            0,
            4 * row_nodes * col_nodes,
        )(dense, pieces[0])
    hidden_own, grad, aggregated = call(
        middle_kernel,
        [like(tile, hidden), like(tile, hidden), like(tile, width)],
        [VMEM_SPEC] * (3 + n_chip),
        [],
        matrix,
        n_chip * block_bytes,
    )(weight, bias_row, cotangent, *parts)
    grads = exchange([grad] * n_chip, "col", n_col, 2)
    hidden_out = call(copy_kernel, like(tile, hidden), [VMEM_SPEC], [], 0, 2 * block_bytes)(hidden_own)
    mine, theirs = call(
        term_kernel,
        [like(half + BIAS_ROWS, hidden)] * 2,
        [VMEM_SPEC] * 2,
        [pltpu.VMEM((width, hidden), F32)],
        matrix,
        6 * block_bytes,
    )(aggregated, grad)
    chip_term = add([swap_cores(theirs, n_col), mine])
    row_terms = total_over(chip_term, add, "row", n_row)
    row_term = add(row_terms)

    own_grads = call(
        gather_kernel,
        like(own_nodes, hidden),
        [VMEM_SPEC] * (1 + n_chip),
        [],
        0,
        own_nodes * hidden * 4,
    )(chip_term, *grads)
    other_grads = swap_cores(own_grads, n_col)
    if is_dense:
        back_own = call(
            back_own_kernel,
            like(col_nodes, hidden, F32),
            [VMEM_SPEC] * 2,
            [],
            slots * matrix // 2,
            row_nodes * hidden * 8,
        )(turned, own_grads)
        back_args = (turned, back_own, other_grads)
    else:
        back = call(
            slot_back_kernel,
            like(col_nodes, hidden, F32),
            slot_specs + [VMEM_SPEC] * 2,
            [pltpu.VMEM((row_nodes, hidden), BF16)],
            slots * matrix // 2,
            row_nodes * hidden * 8,
        )(*slot_args, own_grads, other_grads)
        back_args = (back,)

    evens, odds = range(2, n_row, 2), range(3, n_row, 2)
    targets = [1, *evens]
    near_piece = call(
        functools.partial(back_near_kernel, targets=targets),
        like(len(targets) * tile, hidden),
        [VMEM_SPEC] * len(back_args),
        [],
        len(targets) * n_chip * matrix,
        len(targets) * 2 * block_bytes,
    )(*back_args)
    near = lax.ppermute(near_piece, "row", pairs_of(1, n_row, 1))
    backs = []
    for k in [0, *odds]:
        piece = call(
            functools.partial(back_far_kernel, k=k, at=(k - 1) // 2) if k else
            functools.partial(back_near_kernel, targets=[0]),
            like(tile, hidden),
            [VMEM_SPEC] * (len(back_args) + (k > 0)),
            [],
            n_chip * matrix,
            2 * block_bytes,
        )(*back_args, *([near] if k else []))
        backs.append(lax.ppermute(piece, "row", pairs_of(k, n_row, 1)) if k else piece)
    grad_features = call(
        features_kernel,
        like(tile, width),
        [VMEM_SPEC] * (2 + len(backs)),
        [],
        matrix,
        n_row * block_bytes,
    )(weight, near, *backs)
    all_terms = total_over(row_term, add, "col", n_col, 2)
    factor = (tile * n_row * n_col) ** (-0.5)
    own_half, bias_grad = call(
        functools.partial(scale_kernel, factor=factor),
        (like(half, hidden, F32), like(1, hidden, F32)),
        [HBM_SPEC] + [VMEM_SPEC] * len(all_terms),
        [],
        len(all_terms) * half * hidden,
        len(all_terms) * half * hidden * 2,
    )(pltpu.with_memory_space_constraint(grad_features, pltpu.HBM), *all_terms)
    other_half = swap_cores(own_half, n_col)
    grad_weight, grad_bias = call(
        join_kernel,
        (like(width, hidden, F32), like(1, hidden, F32)),
        [VMEM_SPEC] * 3,
        [],
        0,
        width * hidden * 8,
    )(own_half, other_half, bias_grad)
    return hidden_out, grad_features, grad_weight, grad_bias.reshape(hidden)


def solution(mesh):
    return jax.shard_map(
        local,
        mesh=mesh,
        in_specs=(
            P(("col", "row"), None),
            P(),
            P(),
            P(("row", "col"), None),
            P("row", "col", None, None, None),
            P("row", "col", None),
            P("row", "col", None),
            P("row", "col"),
        ),
        out_specs=(P(("row", "col"), None), P(("col", "row"), None), P(), P()),
        check_vma=False,
    )
```

time: 52.1 us -> 54.5 us (1.046)
  waiting for transfers between devices: 16.1 us -> 23.5 us
  starting transfers between devices: 28.1 us -> 22.4 us
  Pallas kernels: 6.26 us -> 6.94 us
    ppermute x18 -> x9, starting transfers between devices: 27.9 us -> 13 us  [exchange(): lax.ppermute(blocks[k], axis, pairs)]
    ppermute x2 -> x10, waiting for transfers between devices: 2.68 us -> 14.1 us  [the longest x4 8.3 us: total_over(): terms = [lax.ppermute(block, axis, pairs_of(step, size, cores)), block]]
    ppermute x2 -> x10, starting transfers between devices: 0.14 us -> 9.45 us  [the longest x4 6.28 us: total_over(): terms = [lax.ppermute(block, axis, pairs_of(step, size, cores)), block]]
    ppermute x18 -> x9, waiting for transfers between devices: 13.5 us -> 9.35 us  [exchange(): lax.ppermute(blocks[k], axis, pairs)]
    pallas_call x1, Pallas kernels: 1.4 us -> 2.13 us  [local(): call(dense_kernel, (like(row_nodes, col_nodes), like(1, hidden, F32)), [S...]
    pallas_call x15 -> x19, Pallas kernels: 3.74 us -> 3.72 us  [the longest x1 0.83 us: local(): call(features_kernel, like(tile, width), [VMEM_SPEC] * (2 + len(backs)),...]
  transfers between devices with their start and end apart: 20 -> 19, of which waited for: 11 -> 14; matrix products, arithmetic and copies ran while one was open for 0% -> 0% of each run, Pallas kernels for 9% -> 10%
where the time goes in v5:
time: 54.5 us; the launch traced here: 54.3 us
  waiting for transfers between devices  23.5 us (43%)
  starting transfers between devices  22.4 us (41%)
  Pallas kernels  6.94 us (13%)
  between operations  1.47 us (3%)
    ppermute x9, starting transfers between devices, exchange(): lax.ppermute(blocks[k], axis, pairs)  13 us
    ppermute x9, waiting for transfers between devices, exchange(): lax.ppermute(blocks[k], axis, pairs)  9.35 us
    ppermute x4, waiting for transfers between devices, total_over(): terms = [lax.ppermute(block, axis, pairs_of(step, size, cores)), block]  8.3 us
    ppermute x4, starting transfers between devices, total_over(): terms = [lax.ppermute(block, axis, pairs_of(step, size, cores)), block]  6.28 us
    ppermute x1, waiting for transfers between devices, local(): lax.ppermute(piece, 'row', pairs_of(k, n_row, 1))  3.88 us
    pallas_call x1, Pallas kernels, local(): call(dense_kernel, (like(row_nodes, col_nodes), like(1, hidden, F32)), [S...  2.13 us
    ppermute x1, starting transfers between devices, local(): lax.ppermute(piece, 'row', pairs_of(k, n_row, 1))  2.05 us
    ppermute x4, waiting for transfers between devices, swap_cores(): return lax.ppermute(block, 'col', [(i, i ^ 1) for i in range(size)])  1.93 us
  transfers between devices with their start and end apart: 19, of which 14 were waited for; matrix products, arithmetic and copies ran while one was open for 0% of the time, Pallas kernels for 10%

profile of v5, /device:TPU:0, one launch (start us, length us, event | category | flops | bytes accessed | tf_op | source)
XLA Modules:
  0.0 54.3 jit_solution(1089650516973589706)
XLA Ops:
  0.6 5.1 %collective-permute-start = (bf16[128,256]{1,0:T(8,128)(2,1)}, bf16[128,256]{1,0:T(8,128)(2,1)S(1)}, u32[]{:S(2)}, u32[]{:S(2)}) collective-permute-start(bf16[128,256]{1,0:T(8,128)(2,1)} %refs_3_.1), channel_id=1, source_target_pairs={{0,3},{1,2},{2,1},{3,0},{4,7},{5,6},{6,5},{7,4},{8,11},{9,10},{10,... | collective-permute-start | bytes 196616 | tf_op jit(solution)/shard_map/ppermute | solution.py:53
  5.8 0.6 %collective-permute-start.2 = (bf16[128,256]{1,0:T(8,128)(2,1)}, bf16[128,256]{1,0:T(8,128)(2,1)S(1)}, u32[]{:S(2)}, u32[]{:S(2)}) collective-permute-start(bf16[128,256]{1,0:T(8,128)(2,1)} %refs_3_.1), channel_id=1, source_target_pairs={{0,2},{1,3},{2,0},{3,1},{4,6},{5,7},{6,4},{7,5},{8,10},{9,11},{10,... | collective-permute-start | bytes 196616 | tf_op jit(solution)/shard_map/ppermute | solution.py:53
  7.1 2.1 %shard_map.111 = (bf16[1024,512]{1,0:T(8,128)(2,1)S(1)}, f32[1,256]{1,0:T(1,128)S(1)}) custom-call(s32[1,1]{1,0:T(1,128)S(6)} %copy.12.count_ref, s32[1,1,32]{2,1,0:T(1,128)} %row_hbm.1, s32[1,1,32]{2,1,0:T(1,128)} %col_hbm.1, bf16[1,1,32,128,128]{4,3,2,1,0:T(8,128)(2,1)} %tiles_hbm.1, f32[1,256]{1,0:T(1,128)} %bitcast.2), custom_call_target="tpu_custom_call" | custom-call | bytes 6291456 | tf_op jit(solution)/shard_map/pallas_call | solution.py:353
  9.2 1.4 %collective-permute-done.1.refs_1_ = bf16[128,256]{1,0:T(8,128)(2,1)S(1)} collective-permute-done((bf16[128,256]{1,0:T(8,128)(2,1)}, bf16[128,256]{1,0:T(8,128)(2,1)S(1)}, u32[]{:S(2)}, u32[]{:S(2)}) %collective-permute-start.1) | collective-permute-done | bytes 65568 | tf_op jit(solution)/shard_map/ppermute | solution.py:53
  10.6 1.0 %collective-permute-done.2.refs_2_ = bf16[128,256]{1,0:T(8,128)(2,1)S(1)} collective-permute-done((bf16[128,256]{1,0:T(8,128)(2,1)}, bf16[128,256]{1,0:T(8,128)(2,1)S(1)}, u32[]{:S(2)}, u32[]{:S(2)}) %collective-permute-start.2) | collective-permute-done | bytes 65568 | tf_op jit(solution)/shard_map/ppermute | solution.py:53
  12.3 1.2 %collective-permute-done.3.other_ref = bf16[512,256]{1,0:T(8,128)(2,1)S(1)} collective-permute-done((bf16[512,256]{1,0:T(8,128)(2,1)S(1)}, bf16[512,256]{1,0:T(8,128)(2,1)S(1)}, u32[]{:S(2)}, u32[]{:S(2)}) %collective-permute-start.3) | collective-permute-done | bytes 262176 | tf_op jit(solution)/shard_map/ppermute | solution.py:58
  13.5 2.5 %collective-permute-start.4 = (bf16[128,256]{1,0:T(8,128)(2,1)S(1)}, bf16[128,256]{1,0:T(8,128)(2,1)S(1)}, u32[]{:S(2)}, u32[]{:S(2)}) collective-permute-start(bf16[128,256]{1,0:T(8,128)(2,1)S(1)} %shard_map.114.refs_0_), channel_id=1, source_target_pairs={{0,24},{4,28},{8,16},{12,20},{16,8},{20,12},{24,0},{28,4},{1,25},{... | collective-permute-start | bytes 196616 | tf_op jit(solution)/shard_map/ppermute | solution.py:53
  16.1 0.6 %collective-permute-start.5 = (bf16[128,256]{1,0:T(8,128)(2,1)S(1)}, bf16[128,256]{1,0:T(8,128)(2,1)S(1)}, u32[]{:S(2)}, u32[]{:S(2)}) collective-permute-start(bf16[128,256]{1,0:T(8,128)(2,1)S(1)} %shard_map.115.refs_0_), channel_id=1, source_target_pairs={{0,8},{4,12},{8,0},{12,4},{16,24},{20,28},{24,16},{28,20},{1,9},{5... | collective-permute-start | bytes 196616 | tf_op jit(solution)/shard_map/ppermute | solution.py:53
  16.7 0.6 %collective-permute-start.6 = (bf16[128,256]{1,0:T(8,128)(2,1)S(1)}, bf16[128,256]{1,0:T(8,128)(2,1)S(1)}, u32[]{:S(2)}, u32[]{:S(2)}) collective-permute-start(bf16[128,256]{1,0:T(8,128)(2,1)S(1)} %shard_map.116.refs_0_), channel_id=1, source_target_pairs={{0,16},{4,20},{8,24},{12,28},{16,0},{20,4},{24,8},{28,12},{1,17},{... | collective-permute-start | bytes 196616 | tf_op jit(solution)/shard_map/ppermute | solution.py:53
  17.3 1.8 %collective-permute-done.4.refs_0_ = bf16[128,256]{1,0:T(8,128)(2,1)S(1)} collective-permute-done((bf16[128,256]{1,0:T(8,128)(2,1)S(1)}, bf16[128,256]{1,0:T(8,128)(2,1)S(1)}, u32[]{:S(2)}, u32[]{:S(2)}) %collective-permute-start.4) | collective-permute-done | bytes 65568 | tf_op jit(solution)/shard_map/ppermute | solution.py:53
  19.1 1.3 %collective-permute-done.5.refs_1_ = bf16[128,256]{1,0:T(8,128)(2,1)S(1)} collective-permute-done((bf16[128,256]{1,0:T(8,128)(2,1)S(1)}, bf16[128,256]{1,0:T(8,128)(2,1)S(1)}, u32[]{:S(2)}, u32[]{:S(2)}) %collective-permute-start.5) | collective-permute-done | bytes 65568 | tf_op jit(solution)/shard_map/ppermute | solution.py:53
  20.4 0.6 %collective-permute-done.6.refs_2_ = bf16[128,256]{1,0:T(8,128)(2,1)S(1)} collective-permute-done((bf16[128,256]{1,0:T(8,128)(2,1)S(1)}, bf16[128,256]{1,0:T(8,128)(2,1)S(1)}, u32[]{:S(2)}, u32[]{:S(2)}) %collective-permute-start.6) | collective-permute-done | bytes 65568 | tf_op jit(solution)/shard_map/ppermute | solution.py:53
  21.7 1.5 %collective-permute-start.8 = (bf16[128,256]{1,0:T(8,128)(2,1)S(1)}, bf16[128,256]{1,0:T(8,128)(2,1)S(1)}, u32[]{:S(2)}, u32[]{:S(2)}) collective-permute-start(bf16[128,256]{1,0:T(8,128)(2,1)S(1)} %get-tuple-element.23.grad_ref.refs_3_), channel_id=1, source_target_pairs={{0,24},{4,28},{8,16},{12,20},{16,8},{20,12},{24,0},{28,4},{1,25},{... | collective-permute-start | bytes 196616 | tf_op jit(solution)/shard_map/ppermute | solution.py:53
  23.2 0.5 collective-permute-start.9
  23.7 1.5 %collective-permute-start.10 = (bf16[128,256]{1,0:T(8,128)(2,1)S(1)}, bf16[128,256]{1,0:T(8,128)(2,1)S(1)}, u32[]{:S(2)}, u32[]{:S(2)}) collective-permute-start(bf16[128,256]{1,0:T(8,128)(2,1)S(1)} %get-tuple-element.23.grad_ref.refs_3_), channel_id=1, source_target_pairs={{0,16},{4,20},{8,24},{12,28},{16,0},{20,4},{24,8},{28,12},{1,17},{... | collective-permute-start | bytes 196616 | tf_op jit(solution)/shard_map/ppermute | solution.py:53
  25.3 2.1 %collective-permute-done.8.refs_0_ = bf16[128,256]{1,0:T(8,128)(2,1)S(1)} collective-permute-done((bf16[128,256]{1,0:T(8,128)(2,1)S(1)}, bf16[128,256]{1,0:T(8,128)(2,1)S(1)}, u32[]{:S(2)}, u32[]{:S(2)}) %collective-permute-start.8) | collective-permute-done | bytes 65568 | tf_op jit(solution)/shard_map/ppermute | solution.py:53
  27.5 0.9 %collective-permute-done.10.refs_2_ = bf16[128,256]{1,0:T(8,128)(2,1)S(1)} collective-permute-done((bf16[128,256]{1,0:T(8,128)(2,1)S(1)}, bf16[128,256]{1,0:T(8,128)(2,1)S(1)}, u32[]{:S(2)}, u32[]{:S(2)}) %collective-permute-start.10) | collective-permute-done | bytes 65568 | tf_op jit(solution)/shard_map/ppermute | solution.py:53
  28.6 1.6 %collective-permute-start.14 = (bf16[144,256]{1,0:T(8,128)(2,1)S(1)}, bf16[144,256]{1,0:T(8,128)(2,1)S(1)}, u32[]{:S(2)}, u32[]{:S(2)}) collective-permute-start(bf16[144,256]{1,0:T(8,128)(2,1)S(1)} %shard_map.122.after_ref.refs_1_), channel_id=1, source_target_pairs={{0,1},{1,0},{2,3},{3,2},{4,5},{5,4},{6,7},{7,6},{8,9},{9,8},{10,11... | collective-permute-start | bytes 221192 | tf_op jit(solution)/shard_map/ppermute | solution.py:68
  30.2 0.3 shard_map.120.turned_ref.refs_0_
  30.6 2.7 %collective-permute-done.14.refs_0_ = bf16[144,256]{1,0:T(8,128)(2,1)S(1)} collective-permute-done((bf16[144,256]{1,0:T(8,128)(2,1)S(1)}, bf16[144,256]{1,0:T(8,128)(2,1)S(1)}, u32[]{:S(2)}, u32[]{:S(2)}) %collective-permute-start.14) | collective-permute-done | bytes 73760 | tf_op jit(solution)/shard_map/ppermute | solution.py:68
  33.3 2.0 %collective-permute-start.15 = (bf16[144,256]{1,0:T(8,128)(2,1)S(1)}, bf16[144,256]{1,0:T(8,128)(2,1)S(1)}, u32[]{:S(2)}, u32[]{:S(2)}) collective-permute-start(bf16[144,256]{1,0:T(8,128)(2,1)S(1)} %shard_map.129.refs_1_), channel_id=1, source_target_pairs={{0,2},{1,3},{2,0},{3,1},{4,6},{5,7},{6,4},{7,5},{8,10},{9,11},{10,... | collective-permute-start | bytes 221192 | tf_op jit(solution)/shard_map/ppermute | solution.py:68
  35.9 0.8 %collective-permute-start.12 = (bf16[256,256]{1,0:T(8,128)(2,1)S(1)}, bf16[256,256]{1,0:T(8,128)(2,1)S(1)}, u32[]{:S(2)}, u32[]{:S(2)}) collective-permute-start(bf16[256,256]{1,0:T(8,128)(2,1)S(1)} %shard_map.125), channel_id=1, source_target_pairs={{0,1},{1,0},{2,3},{3,2},{4,5},{5,4},{6,7},{7,6},{8,9},{9,8},{10,11... | collective-permute-start | bytes 393224 | tf_op jit(solution)/shard_map/ppermute | solution.py:492
  36.7 2.7 %collective-permute-done.15.refs_0_ = bf16[144,256]{1,0:T(8,128)(2,1)S(1)} collective-permute-done((bf16[144,256]{1,0:T(8,128)(2,1)S(1)}, bf16[144,256]{1,0:T(8,128)(2,1)S(1)}, u32[]{:S(2)}, u32[]{:S(2)}) %collective-permute-start.15) | collective-permute-done | bytes 73760 | tf_op jit(solution)/shard_map/ppermute | solution.py:68
  39.5 1.6 %collective-permute-start.16 = (bf16[144,256]{1,0:T(8,128)(2,1)S(1)}, bf16[144,256]{1,0:T(8,128)(2,1)S(1)}, u32[]{:S(2)}, u32[]{:S(2)}) collective-permute-start(bf16[144,256]{1,0:T(8,128)(2,1)S(1)} %shard_map.130.refs_1_), channel_id=1, source_target_pairs={{0,8},{4,12},{8,0},{12,4},{16,24},{20,28},{24,16},{28,20},{1,9},{5... | collective-permute-start | bytes 221192 | tf_op jit(solution)/shard_map/ppermute | solution.py:68
  41.0 2.8 %collective-permute-done.16.refs_0_ = bf16[144,256]{1,0:T(8,128)(2,1)S(1)} collective-permute-done((bf16[144,256]{1,0:T(8,128)(2,1)S(1)}, bf16[144,256]{1,0:T(8,128)(2,1)S(1)}, u32[]{:S(2)}, u32[]{:S(2)}) %collective-permute-start.16) | collective-permute-done | bytes 73760 | tf_op jit(solution)/shard_map/ppermute | solution.py:68
  43.9 1.1 %collective-permute-start.17 = (bf16[144,256]{1,0:T(8,128)(2,1)S(1)}, bf16[144,256]{1,0:T(8,128)(2,1)S(1)}, u32[]{:S(2)}, u32[]{:S(2)}) collective-permute-start(bf16[144,256]{1,0:T(8,128)(2,1)S(1)} %shard_map.131.refs_1_), channel_id=1, source_target_pairs={{0,16},{4,20},{8,24},{12,28},{16,0},{20,4},{24,8},{28,12},{1,17},{... | collective-permute-start | bytes 221192 | tf_op jit(solution)/shard_map/ppermute | solution.py:68
  45.2 2.0 %collective-permute-start.13 = (bf16[128,256]{1,0:T(8,128)(2,1)S(1)}, bf16[128,256]{1,0:T(8,128)(2,1)S(1)}, u32[]{:S(2)}, u32[]{:S(2)}) collective-permute-start(bf16[128,256]{1,0:T(8,128)(2,1)S(1)} %shard_map.127), channel_id=1, source_target_pairs={{0,3},{1,2},{2,1},{3,0},{4,7},{5,6},{6,5},{7,4},{8,11},{9,10},{10,... | collective-permute-start | bytes 196616 | tf_op jit(solution)/shard_map/ppermute | solution.py:504
  47.4 3.9 %collective-permute-done.13.refs_1_ = bf16[128,256]{1,0:T(8,128)(2,1)S(1)} collective-permute-done((bf16[128,256]{1,0:T(8,128)(2,1)S(1)}, bf16[128,256]{1,0:T(8,128)(2,1)S(1)}, u32[]{:S(2)}, u32[]{:S(2)}) %collective-permute-start.13) | collective-permute-done | bytes 65568 | tf_op jit(solution)/shard_map/ppermute | solution.py:504
  51.3 0.8 %shard_map.128.after_ref = bf16[128,256]{1,0:T(8,128)(2,1)} custom-call(bf16[256,256]{1,0:T(8,128)(2,1)S(1)} %copy-done, bf16[256,256]{1,0:T(8,128)(2,1)S(1)} %collective-permute-done.12.refs_3_.near_ref, bf16[128,256]{1,0:T(8,128)(2,1)S(1)} %shard_map.126.refs_0_, bf16[128,256]{1,0:T(8,128)(2,1)S(1)} %collective-permute-done.13.refs_1_), custom_call_target="tpu_custom_call" | custom-call | flops 16777216 | bytes 262144 | tf_op jit(solution)/shard_map/pallas_call | solution.py:505
  52.3 0.6 %shard_map.119 = bf16[128,256]{1,0:T(8,128)(2,1)} custom-call(bf16[128,256]{1,0:T(8,128)(2,1)S(1)} %get-tuple-element.21.in_ref), custom_call_target="tpu_custom_call" | custom-call | bytes 131072 | tf_op jit(solution)/shard_map/pallas_call | solution.py:439
  52.9 0.7 %collective-permute-done.18.other_ref = f32[128,256]{1,0:T(8,128)S(1)} collective-permute-done((f32[128,256]{1,0:T(8,128)S(1)}, f32[128,256]{1,0:T(8,128)S(1)}, u32[]{:S(2)}, u32[]{:S(2)}) %collective-permute-start.18) | collective-permute-done | bytes 131104 | tf_op jit(solution)/shard_map/ppermute | solution.py:58
  53.6 0.7 %shard_map.133 = (f32[256,256]{1,0:T(8,128)}, f32[1,256]{1,0:T(1,128)}) custom-call(f32[128,256]{1,0:T(8,128)S(1)} %get-tuple-element.26.own_ref, f32[128,256]{1,0:T(8,128)S(1)} %collective-permute-done.18.other_ref, f32[1,256]{1,0:T(1,128)S(1)} %get-tuple-element.27.bias_ref), custom_call_target="tpu_custom_call" | custom-call | bytes 524288 | tf_op jit(solution)/shard_map/pallas_call | solution.py:524
  (35 shorter events, 2.8 us)
Async XLA Ops:
  0.6 8.6 %collective-permute-start = (bf16[128,256]{1,0:T(8,128)(2,1)}, bf16[128,256]{1,0:T(8,128)(2,1)S(1)}, u32[]{:S(2)}, u32[]{:S(2)}) collective-permute-start(bf16[128,256]{1,0:T(8,128)(2,1)} %refs_3_.1), channel_id=1, source_target_pairs={{0,3},{1,2},{2,1},{3,0},{4,7},{5,6},{6,5},{7,4},{8,11},{9,10},{10,... | collective-permute-start | bytes 196616 | tf_op jit(solution)/shard_map/ppermute | solution.py:53
  5.7 4.9 %collective-permute-start.1 = (bf16[128,256]{1,0:T(8,128)(2,1)}, bf16[128,256]{1,0:T(8,128)(2,1)S(1)}, u32[]{:S(2)}, u32[]{:S(2)}) collective-permute-start(bf16[128,256]{1,0:T(8,128)(2,1)} %refs_3_.1), channel_id=1, source_target_pairs={{0,1},{1,0},{2,3},{3,2},{4,5},{5,4},{6,7},{7,6},{8,9},{9,8},{10,11... | collective-permute-start | bytes 196616 | tf_op jit(solution)/shard_map/ppermute | solution.py:53
  5.8 5.8 %collective-permute-start.2 = (bf16[128,256]{1,0:T(8,128)(2,1)}, bf16[128,256]{1,0:T(8,128)(2,1)S(1)}, u32[]{:S(2)}, u32[]{:S(2)}) collective-permute-start(bf16[128,256]{1,0:T(8,128)(2,1)} %refs_3_.1), channel_id=1, source_target_pairs={{0,2},{1,3},{2,0},{3,1},{4,6},{5,7},{6,4},{7,5},{8,10},{9,11},{10,... | collective-permute-start | bytes 196616 | tf_op jit(solution)/shard_map/ppermute | solution.py:53
  7.0 4.6 %copy-start.1 = (bf16[128,256]{1,0:T(8,128)(2,1)S(1)}, bf16[128,256]{1,0:T(8,128)(2,1)}, u32[]{:S(2)}) copy-start(bf16[128,256]{1,0:T(8,128)(2,1)} %refs_3_.1) | copy-start | bytes 196612
  11.9 1.6 %collective-permute-start.3 = (bf16[512,256]{1,0:T(8,128)(2,1)S(1)}, bf16[512,256]{1,0:T(8,128)(2,1)S(1)}, u32[]{:S(2)}, u32[]{:S(2)}) collective-permute-start(bf16[512,256]{1,0:T(8,128)(2,1)S(1)} %get-tuple-element.20), channel_id=1, source_target_pairs={{0,4},{4,0},{8,12},{12,8},{16,20},{20,16},{24,28},{28,24},{1,5},{5... | collective-permute-start | bytes 786440 | tf_op jit(solution)/shard_map/ppermute | solution.py:58
  13.5 5.5 %collective-permute-start.4 = (bf16[128,256]{1,0:T(8,128)(2,1)S(1)}, bf16[128,256]{1,0:T(8,128)(2,1)S(1)}, u32[]{:S(2)}, u32[]{:S(2)}) collective-permute-start(bf16[128,256]{1,0:T(8,128)(2,1)S(1)} %shard_map.114.refs_0_), channel_id=1, source_target_pairs={{0,24},{4,28},{8,16},{12,20},{16,8},{20,12},{24,0},{28,4},{1,25},{... | collective-permute-start | bytes 196616 | tf_op jit(solution)/shard_map/ppermute | solution.py:53
  16.1 4.3 %collective-permute-start.5 = (bf16[128,256]{1,0:T(8,128)(2,1)S(1)}, bf16[128,256]{1,0:T(8,128)(2,1)S(1)}, u32[]{:S(2)}, u32[]{:S(2)}) collective-permute-start(bf16[128,256]{1,0:T(8,128)(2,1)S(1)} %shard_map.115.refs_0_), channel_id=1, source_target_pairs={{0,8},{4,12},{8,0},{12,4},{16,24},{20,28},{24,16},{28,20},{1,9},{5... | collective-permute-start | bytes 196616 | tf_op jit(solution)/shard_map/ppermute | solution.py:53
  16.7 4.4 %copy-start = (bf16[256,256]{1,0:T(8,128)(2,1)S(1)}, bf16[256,256]{1,0:T(8,128)(2,1)}, u32[]{:S(2)}) copy-start(bf16[256,256]{1,0:T(8,128)(2,1)} %weight_ref.3) | copy-start | bytes 393220
  16.7 4.3 %copy-start.2 = (bf16[128,256]{1,0:T(8,128)(2,1)S(1)}, bf16[128,256]{1,0:T(8,128)(2,1)}, u32[]{:S(2)}) copy-start(bf16[128,256]{1,0:T(8,128)(2,1)} %cot_ref.1) | copy-start | bytes 196612
  16.7 4.3 %collective-permute-start.6 = (bf16[128,256]{1,0:T(8,128)(2,1)S(1)}, bf16[128,256]{1,0:T(8,128)(2,1)S(1)}, u32[]{:S(2)}, u32[]{:S(2)}) collective-permute-start(bf16[128,256]{1,0:T(8,128)(2,1)S(1)} %shard_map.116.refs_0_), channel_id=1, source_target_pairs={{0,16},{4,20},{8,24},{12,28},{16,0},{20,4},{24,8},{28,12},{1,17},{... | collective-permute-start | bytes 196616 | tf_op jit(solution)/shard_map/ppermute | solution.py:53
  21.6 3.6 %collective-permute-start.7 = (bf16[144,256]{1,0:T(8,128)(2,1)S(1)}, bf16[144,256]{1,0:T(8,128)(2,1)S(1)}, u32[]{:S(2)}, u32[]{:S(2)}) collective-permute-start(bf16[144,256]{1,0:T(8,128)(2,1)S(1)} %get-tuple-element.24), channel_id=1, source_target_pairs={{0,4},{4,0},{8,12},{12,8},{16,20},{20,16},{24,28},{28,24},{1,5},{5... | collective-permute-start | bytes 221192 | tf_op jit(solution)/shard_map/ppermute | solution.py:58
  21.7 5.6 %collective-permute-start.8 = (bf16[128,256]{1,0:T(8,128)(2,1)S(1)}, bf16[128,256]{1,0:T(8,128)(2,1)S(1)}, u32[]{:S(2)}, u32[]{:S(2)}) collective-permute-start(bf16[128,256]{1,0:T(8,128)(2,1)S(1)} %get-tuple-element.23.grad_ref.refs_3_), channel_id=1, source_target_pairs={{0,24},{4,28},{8,16},{12,20},{16,8},{20,12},{24,0},{28,4},{1,25},{... | collective-permute-start | bytes 196616 | tf_op jit(solution)/shard_map/ppermute | solution.py:53
  23.2 4.4 %collective-permute-start.9 = (bf16[128,256]{1,0:T(8,128)(2,1)S(1)}, bf16[128,256]{1,0:T(8,128)(2,1)S(1)}, u32[]{:S(2)}, u32[]{:S(2)}) collective-permute-start(bf16[128,256]{1,0:T(8,128)(2,1)S(1)} %get-tuple-element.23.grad_ref.refs_3_), channel_id=1, source_target_pairs={{0,8},{4,12},{8,0},{12,4},{16,24},{20,28},{24,16},{28,20},{1,9},{5... | collective-permute-start | bytes 196616 | tf_op jit(solution)/shard_map/ppermute | solution.py:53
  23.7 4.8 %collective-permute-start.10 = (bf16[128,256]{1,0:T(8,128)(2,1)S(1)}, bf16[128,256]{1,0:T(8,128)(2,1)S(1)}, u32[]{:S(2)}, u32[]{:S(2)}) collective-permute-start(bf16[128,256]{1,0:T(8,128)(2,1)S(1)} %get-tuple-element.23.grad_ref.refs_3_), channel_id=1, source_target_pairs={{0,16},{4,20},{8,24},{12,28},{16,0},{20,4},{24,8},{28,12},{1,17},{... | collective-permute-start | bytes 196616 | tf_op jit(solution)/shard_map/ppermute | solution.py:53
  28.5 7.1 %collective-permute-start.11 = (bf16[512,256]{1,0:T(8,128)(2,1)S(1)}, bf16[512,256]{1,0:T(8,128)(2,1)S(1)}, u32[]{:S(2)}, u32[]{:S(2)}) collective-permute-start(bf16[512,256]{1,0:T(8,128)(2,1)S(1)} %shard_map.123.source_ref), channel_id=1, source_target_pairs={{0,4},{4,0},{8,12},{12,8},{16,20},{20,16},{24,28},{28,24},{1,5},{5... | collective-permute-start | bytes 786440 | tf_op jit(solution)/shard_map/ppermute | solution.py:58
  28.6 4.7 %collective-permute-start.14 = (bf16[144,256]{1,0:T(8,128)(2,1)S(1)}, bf16[144,256]{1,0:T(8,128)(2,1)S(1)}, u32[]{:S(2)}, u32[]{:S(2)}) collective-permute-start(bf16[144,256]{1,0:T(8,128)(2,1)S(1)} %shard_map.122.after_ref.refs_1_), channel_id=1, source_target_pairs={{0,1},{1,0},{2,3},{3,2},{4,5},{5,4},{6,7},{7,6},{8,9},{9,8},{10,11... | collective-permute-start | bytes 221192 | tf_op jit(solution)/shard_map/ppermute | solution.py:68
  33.3 6.1 %collective-permute-start.15 = (bf16[144,256]{1,0:T(8,128)(2,1)S(1)}, bf16[144,256]{1,0:T(8,128)(2,1)S(1)}, u32[]{:S(2)}, u32[]{:S(2)}) collective-permute-start(bf16[144,256]{1,0:T(8,128)(2,1)S(1)} %shard_map.129.refs_1_), channel_id=1, source_target_pairs={{0,2},{1,3},{2,0},{3,1},{4,6},{5,7},{6,4},{7,5},{8,10},{9,11},{10,... | collective-permute-start | bytes 221192 | tf_op jit(solution)/shard_map/ppermute | solution.py:68
  35.9 9.1 %collective-permute-start.12 = (bf16[256,256]{1,0:T(8,128)(2,1)S(1)}, bf16[256,256]{1,0:T(8,128)(2,1)S(1)}, u32[]{:S(2)}, u32[]{:S(2)}) collective-permute-start(bf16[256,256]{1,0:T(8,128)(2,1)S(1)} %shard_map.125), channel_id=1, source_target_pairs={{0,1},{1,0},{2,3},{3,2},{4,5},{5,4},{6,7},{7,6},{8,9},{9,8},{10,11... | collective-permute-start | bytes 393224 | tf_op jit(solution)/shard_map/ppermute | solution.py:492
  39.5 4.4 %collective-permute-start.16 = (bf16[144,256]{1,0:T(8,128)(2,1)S(1)}, bf16[144,256]{1,0:T(8,128)(2,1)S(1)}, u32[]{:S(2)}, u32[]{:S(2)}) collective-permute-start(bf16[144,256]{1,0:T(8,128)(2,1)S(1)} %shard_map.130.refs_1_), channel_id=1, source_target_pairs={{0,8},{4,12},{8,0},{12,4},{16,24},{20,28},{24,16},{28,20},{1,9},{5... | collective-permute-start | bytes 221192 | tf_op jit(solution)/shard_map/ppermute | solution.py:68
  43.9 8.2 %collective-permute-start.17 = (bf16[144,256]{1,0:T(8,128)(2,1)S(1)}, bf16[144,256]{1,0:T(8,128)(2,1)S(1)}, u32[]{:S(2)}, u32[]{:S(2)}) collective-permute-start(bf16[144,256]{1,0:T(8,128)(2,1)S(1)} %shard_map.131.refs_1_), channel_id=1, source_target_pairs={{0,16},{4,20},{8,24},{12,28},{16,0},{20,4},{24,8},{28,12},{1,17},{... | collective-permute-start | bytes 221192 | tf_op jit(solution)/shard_map/ppermute | solution.py:68
  45.2 6.1 %collective-permute-start.13 = (bf16[128,256]{1,0:T(8,128)(2,1)S(1)}, bf16[128,256]{1,0:T(8,128)(2,1)S(1)}, u32[]{:S(2)}, u32[]{:S(2)}) collective-permute-start(bf16[128,256]{1,0:T(8,128)(2,1)S(1)} %shard_map.127), channel_id=1, source_target_pairs={{0,3},{1,2},{2,1},{3,0},{4,7},{5,6},{6,5},{7,4},{8,11},{9,10},{10,... | collective-permute-start | bytes 196616 | tf_op jit(solution)/shard_map/ppermute | solution.py:504
  52.2 1.4 %collective-permute-start.18 = (f32[128,256]{1,0:T(8,128)S(1)}, f32[128,256]{1,0:T(8,128)S(1)}, u32[]{:S(2)}, u32[]{:S(2)}) collective-permute-start(f32[128,256]{1,0:T(8,128)S(1)} %get-tuple-element.26.own_ref), channel_id=1, source_target_pairs={{0,4},{4,0},{8,12},{12,8},{16,20},{20,16},{24,28},{28,24},{1,5},{5... | collective-permute-start | bytes 393224 | tf_op jit(solution)/shard_map/ppermute | solution.py:58

commit v6 on v5

--- a/solution.py
+++ b/solution.py
@@ -58,16 +58,20 @@
     return lax.ppermute(block, "col", [(i, i ^ 1) for i in range(size)])
 
 
-def total_over(block, add, axis, size, cores=1):
-    count = size // cores
-    if count & (count - 1):
-        return exchange([block] * count, axis, size, cores)
-    terms, step = [block], 1
-    while step < count:
-        block = add(terms) if len(terms) > 1 else block
-        terms = [lax.ppermute(block, axis, pairs_of(step, size, cores)), block]
-        step *= 2
-    return terms
+def exchange_second(block, along, n_row, n_col):
+    count = n_row if along == "row" else n_col // 2
+    received = []
+    for k in far_first(count):
+        pairs = []
+        for row in range(n_row):
+            for col in range(1, n_col, 2):
+                if along == "row":
+                    target = col * n_row + partner(row, k, count)
+                else:
+                    target = (2 * partner(col // 2, k, count) + 1) * n_row + row
+                pairs.append((col * n_row + row, target))
+        received.append(lax.ppermute(block, ("col", "row"), pairs) if k else block)
+    return received
 
 
 def block_at(index, size):
@@ -223,32 +227,32 @@
     out_ref[...] = in_ref[...]
 
 
-def term_kernel(agg_ref, grad_ref, mine_ref, theirs_ref, acc_ref):
+def term_kernel(agg_ref, grad_ref, out_ref):
     grad = grad_ref[...]
-    acc_ref[...] = lax.dot_general(
+    term = lax.dot_general(
         agg_ref[...], grad, (((0,), (0,)), ((), ())), preferred_element_type=F32
     )
-    half = acc_ref.shape[0] // 2
-    bias = bias_rows(jnp.sum(grad.astype(F32), axis=0, keepdims=True)).astype(BF16)
-    for ref, core in ((mine_ref, core_index()), (theirs_ref, 1 - core_index())):
-        ref[:half, :] = acc_ref[block_at(core, half), :].astype(BF16)
-        ref[half:, :] = bias
+    width = term.shape[0]
+    out_ref[:width, :] = term.astype(BF16)
+    out_ref[width:, :] = bias_rows(jnp.sum(grad.astype(F32), axis=0, keepdims=True)).astype(BF16)
 
 
 def add_terms_kernel(*refs, n_terms):
     total = summed(refs[:n_terms])
     out_ref = refs[-1]
-    half = total.shape[0] - BIAS_ROWS
-    out_ref[:half, :] = total[:half].astype(BF16)
-    out_ref[half:, :] = bias_rows(total[half : half + 1] + total[half + 1 : half + 2]).astype(BF16)
+    width = total.shape[0] - BIAS_ROWS
+    out_ref[:width, :] = total[:width].astype(BF16)
+    bias = total[width : width + 1] + total[width + 1 : width + 2]
+    out_ref[width:, :] = bias_rows(bias).astype(BF16)
 
 
 def scale_kernel(after_ref, *refs, factor):
-    parts, (half_ref, bias_ref) = refs[:-2], refs[-2:]
+    parts, out_ref = refs[:-1], refs[-1]
     total = summed(parts) * factor
-    half = half_ref.shape[0]
-    half_ref[...] = total[:half]
-    bias_ref[...] = total[half : half + 1] + total[half + 1 : half + 2]
+    width = total.shape[0] - BIAS_ROWS
+    out_ref[:width, :] = total[:width]
+    bias = total[width : width + 1] + total[width + 1 : width + 2]
+    out_ref[width:, :] = jnp.broadcast_to(bias, (out_ref.shape[0] - width, bias.shape[1]))
 
 
 def gather_kernel(after_ref, *refs):
@@ -257,6 +261,13 @@
 
 def back_own_kernel(turned_ref, source_ref, out_ref):
     out_ref[...] = dense_dot(turned_ref[:, : source_ref.shape[0]], source_ref[...])
+
+
+def back_piece_kernel(turned_ref, own_ref, source_ref, *refs, k, n_row):
+    out_ref = refs[-1]
+    rows = block_at(partner(row_index(), k, n_row), out_ref.shape[0])
+    rest = dense_dot(turned_ref[rows, source_ref.shape[0] :], source_ref[...])
+    out_ref[...] = (own_ref[rows, :] + rest).astype(BF16)
 
 
 def slot_back_kernel(count_ref, row_ref, col_ref, tiles_ref, own_ref, other_ref, out_ref, source_ref):
@@ -266,48 +277,27 @@
     slot_product((count_ref, row_ref, col_ref, tiles_ref), source_ref, out_ref, True)
 
 
-def back_rows(refs, place):
-    if len(refs) == 1:
-        return refs[0][place, :]
-    turned_ref, own_ref, source_ref = refs
-    rest = dense_dot(turned_ref[place, source_ref.shape[0] :], source_ref[...])
-    return own_ref[place, :] + rest
-
-
-def back_near_kernel(*refs, targets):
+def slot_piece_kernel(back_ref, *refs, k, n_row):
     out_ref = refs[-1]
-    tile = out_ref.shape[0] // len(targets)
-    for i, k in enumerate(targets):
-        place = block_at(row_index() ^ k, tile)
-        out_ref[i * tile : (i + 1) * tile, :] = back_rows(refs[:-1], place).astype(BF16)
-
-
-def back_far_kernel(*refs, k, at):
-    near_ref, out_ref = refs[-2:]
-    tile = out_ref.shape[0]
-    rows = back_rows(refs[:-2], block_at(row_index() ^ k, tile))
-    near = near_ref[at * tile : (at + 1) * tile, :].astype(F32)
-    out_ref[...] = (rows + near).astype(BF16)
-
-
-def features_kernel(weight_ref, near_ref, *refs):
+    rows = block_at(partner(row_index(), k, n_row), out_ref.shape[0])
+    out_ref[...] = back_ref[rows, :].astype(BF16)
+
+
+def features_kernel(weight_ref, *refs):
     parts, out_ref = refs[:-1], refs[-1]
-    total = near_ref[: out_ref.shape[0], :].astype(F32)
-    for ref in parts:
-        total += ref[...].astype(F32)
     out_ref[...] = lax.dot_general(
-        total.astype(BF16),
+        summed(parts).astype(BF16),
         weight_ref[...],
         (((1,), (1,)), ((), ())),
         preferred_element_type=F32,
     ).astype(BF16)
 
 
-def join_kernel(own_ref, other_ref, bias_ref, weight_ref, bias_out):
-    half = own_ref.shape[0]
-    weight_ref[block_at(core_index(), half), :] = own_ref[...]
-    weight_ref[block_at(1 - core_index(), half), :] = other_ref[...]
-    bias_out[...] = bias_ref[...]
+def join_kernel(own_ref, other_ref, weight_ref, bias_ref):
+    width = weight_ref.shape[0]
+    second = core_index() == 1
+    weight_ref[...] = jnp.where(second, own_ref[:width, :], other_ref[:width, :])
+    bias_ref[...] = jnp.where(second, own_ref[width : width + 1, :], other_ref[width : width + 1, :])
 
 
 def in_turn(count, make):
@@ -327,7 +317,6 @@
     slots = tile_values.shape[2]
     row_nodes, col_nodes = n_col * tile, n_row * tile
     bias_row = bias_term.reshape(1, hidden)
-    half = width // 2
     matrix = 2 * tile * width * hidden
     block_bytes = 2 * tile * width
 
@@ -340,11 +329,11 @@
     def add(terms, after=()):
         return call(
             functools.partial(add_terms_kernel, n_terms=len(terms)),
-            like(half + BIAS_ROWS, hidden),
+            like(width + BIAS_ROWS, hidden),
             [VMEM_SPEC] * (len(terms) + len(after)),
             [],
-            len(terms) * half * hidden,
-            len(terms) * half * hidden * 2,
+            len(terms) * width * hidden,
+            len(terms) * width * hidden * 2,
         )(*terms, *after)
 
     is_dense = n_row * n_col <= 2 * slots
@@ -437,17 +426,17 @@
     )(weight, bias_row, cotangent, *parts)
     grads = exchange([grad] * n_chip, "col", n_col, 2)
     hidden_out = call(copy_kernel, like(tile, hidden), [VMEM_SPEC], [], 0, 2 * block_bytes)(hidden_own)
-    mine, theirs = call(
+    term = call(
         term_kernel,
-        [like(half + BIAS_ROWS, hidden)] * 2,
+        like(width + BIAS_ROWS, hidden),
         [VMEM_SPEC] * 2,
-        [pltpu.VMEM((width, hidden), F32)],
+        [],
         matrix,
         6 * block_bytes,
     )(aggregated, grad)
-    chip_term = add([swap_cores(theirs, n_col), mine])
-    row_terms = total_over(chip_term, add, "row", n_row)
-    row_term = add(row_terms)
+    first_term = lax.ppermute(term, "col", [(i - 1, i) for i in range(1, n_col, 2)])
+    chip_term = add([first_term, term])
+    row_terms = exchange_second(chip_term, "row", n_row, n_col)
 
     own_grads = call(
         gather_kernel,
@@ -467,7 +456,7 @@
             slots * matrix // 2,
             row_nodes * hidden * 8,
         )(turned, own_grads)
-        back_args = (turned, back_own, other_grads)
+        piece_kernel, piece_args = back_piece_kernel, (turned, back_own, other_grads)
     else:
         back = call(
             slot_back_kernel,
@@ -477,58 +466,48 @@
             slots * matrix // 2,
             row_nodes * hidden * 8,
         )(*slot_args, own_grads, other_grads)
-        back_args = (back,)
-
-    evens, odds = range(2, n_row, 2), range(3, n_row, 2)
-    targets = [1, *evens]
-    near_piece = call(
-        functools.partial(back_near_kernel, targets=targets),
-        like(len(targets) * tile, hidden),
-        [VMEM_SPEC] * len(back_args),
-        [],
-        len(targets) * n_chip * matrix,
-        len(targets) * 2 * block_bytes,
-    )(*back_args)
-    near = lax.ppermute(near_piece, "row", pairs_of(1, n_row, 1))
-    backs = []
-    for k in [0, *odds]:
-        piece = call(
-            functools.partial(back_far_kernel, k=k, at=(k - 1) // 2) if k else
-            functools.partial(back_near_kernel, targets=[0]),
+        piece_kernel, piece_args = slot_piece_kernel, (back,)
+
+    def back_piece(k, before):
+        return call(
+            functools.partial(piece_kernel, k=k, n_row=n_row),
             like(tile, hidden),
-            [VMEM_SPEC] * (len(back_args) + (k > 0)),
+            [VMEM_SPEC] * (len(piece_args) + len(before)),
             [],
             n_chip * matrix,
             2 * block_bytes,
-        )(*back_args, *([near] if k else []))
-        backs.append(lax.ppermute(piece, "row", pairs_of(k, n_row, 1)) if k else piece)
+        )(*piece_args, *before)
+
+    made = in_turn(n_row, back_piece)
+    backs = exchange(made, "row", n_row)
+    row_term = add(row_terms, [made[0]])
     grad_features = call(
         features_kernel,
         like(tile, width),
-        [VMEM_SPEC] * (2 + len(backs)),
+        [VMEM_SPEC] * (1 + n_row),
         [],
         matrix,
         n_row * block_bytes,
-    )(weight, near, *backs)
-    all_terms = total_over(row_term, add, "col", n_col, 2)
+    )(weight, *backs)
+    all_terms = exchange_second(row_term, "col", n_row, n_col)
     factor = (tile * n_row * n_col) ** (-0.5)
-    own_half, bias_grad = call(
+    total = call(
         functools.partial(scale_kernel, factor=factor),
-        (like(half, hidden, F32), like(1, hidden, F32)),
+        like(width + 8, hidden, F32),
         [HBM_SPEC] + [VMEM_SPEC] * len(all_terms),
         [],
-        len(all_terms) * half * hidden,
-        len(all_terms) * half * hidden * 2,
+        len(all_terms) * width * hidden,
+        len(all_terms) * width * hidden * 2,
     )(pltpu.with_memory_space_constraint(grad_features, pltpu.HBM), *all_terms)
-    other_half = swap_cores(own_half, n_col)
+    second_total = lax.ppermute(total, "col", [(i, i - 1) for i in range(1, n_col, 2)])
     grad_weight, grad_bias = call(
         join_kernel,
         (like(width, hidden, F32), like(1, hidden, F32)),
-        [VMEM_SPEC] * 3,
+        [VMEM_SPEC] * 2,
         [],
         0,
         width * hidden * 8,
-    )(own_half, other_half, bias_grad)
+    )(total, second_total)
     return hidden_out, grad_features, grad_weight, grad_bias.reshape(hidden)
 
 

time: 54.5 us -> 66 us (1.21)
  waiting for transfers between devices: 23.5 us -> 34.6 us
    ppermute x9 -> x12, waiting for transfers between devices: 9.35 us -> 17.5 us  [exchange(): lax.ppermute(blocks[k], axis, pairs)]
    ppermute x6 -> x8, waiting for transfers between devices: 12.2 us -> 15.8 us  [the longest x1 15.8 us: local(): lax.ppermute(total, 'col', [(i, i - 1) for i in range(1, n_col, 2)])]
    ppermute x9 -> x12, starting transfers between devices: 13 us -> 15.7 us  [exchange(): lax.ppermute(blocks[k], axis, pairs)]
    ppermute x6 -> x8, starting transfers between devices: 9.16 us -> 6.61 us  [the longest x6 4.02 us: exchange_second(): received.append(lax.ppermute(block, ('col', 'row'), pairs) if k else block)]
    ppermute x4 -> x2, waiting for transfers between devices: 1.93 us -> 1.23 us  [swap_cores(): return lax.ppermute(block, 'col', [(i, i ^ 1) for i in range(size)])]
    pallas_call x10 -> x9, Pallas kernels: 1.84 us -> 2.01 us  [the longest x1 0.84 us: local(): call(features_kernel, like(tile, width), [VMEM_SPEC] * (1 + n_row), [], m...]
  transfers between devices with their start and end apart: 19 -> 22, of which waited for: 14 -> 13; matrix products, arithmetic and copies ran while one was open for 0% -> 0% of each run, Pallas kernels for 10% -> 8%
where the time goes in v6:
time: 66 us; the launch traced here: 65.7 us
  waiting for transfers between devices  34.6 us (52%)
  starting transfers between devices  22.4 us (34%)
  Pallas kernels  7.13 us (11%)
  between operations  1.56 us (2%)
    ppermute x12, waiting for transfers between devices, exchange(): lax.ppermute(blocks[k], axis, pairs)  17.5 us
    ppermute x1, waiting for transfers between devices, local(): lax.ppermute(total, 'col', [(i, i - 1) for i in range(1, n_col, 2)])  15.8 us
    ppermute x12, starting transfers between devices, exchange(): lax.ppermute(blocks[k], axis, pairs)  15.7 us
    ppermute x6, starting transfers between devices, exchange_second(): received.append(lax.ppermute(block, ('col', 'row'), pairs) if k else block)  4.02 us
    pallas_call x1, Pallas kernels, local(): call(dense_kernel, (like(row_nodes, col_nodes), like(1, hidden, F32)), [S...  2.13 us
  transfers between devices with their start and end apart: 22, of which 13 were waited for; matrix products, arithmetic and copies ran while one was open for 0% of the time, Pallas kernels for 8%

profile of v6, /device:TPU:0, one launch (start us, length us, event | category | flops | bytes accessed | tf_op | source)
XLA Modules:
  0.0 65.7 jit_solution(1283468290666977996)
XLA Ops:
  0.6 5.1 %collective-permute-start = (bf16[128,256]{1,0:T(8,128)(2,1)}, bf16[128,256]{1,0:T(8,128)(2,1)S(1)}, u32[]{:S(2)}, u32[]{:S(2)}) collective-permute-start(bf16[128,256]{1,0:T(8,128)(2,1)} %refs_3_.1), channel_id=1, source_target_pairs={{0,3},{1,2},{2,1},{3,0},{4,7},{5,6},{6,5},{7,4},{8,11},{9,10},{10,... | collective-permute-start | bytes 196616 | tf_op jit(solution)/shard_map/ppermute | solution.py:53
  5.8 0.6 collective-permute-start.2
  7.1 2.1 %shard_map.111 = (bf16[1024,512]{1,0:T(8,128)(2,1)S(1)}, f32[1,256]{1,0:T(1,128)S(1)}) custom-call(s32[1,1]{1,0:T(1,128)S(6)} %copy.12.count_ref, s32[1,1,32]{2,1,0:T(1,128)} %row_hbm.1, s32[1,1,32]{2,1,0:T(1,128)} %col_hbm.1, bf16[1,1,32,128,128]{4,3,2,1,0:T(8,128)(2,1)} %tiles_hbm.1, f32[1,256]{1,0:T(1,128)} %bitcast.2), custom_call_target="tpu_custom_call" | custom-call | bytes 6291456 | tf_op jit(solution)/shard_map/pallas_call | solution.py:342
  9.2 1.4 %collective-permute-done.1.refs_1_ = bf16[128,256]{1,0:T(8,128)(2,1)S(1)} collective-permute-done((bf16[128,256]{1,0:T(8,128)(2,1)}, bf16[128,256]{1,0:T(8,128)(2,1)S(1)}, u32[]{:S(2)}, u32[]{:S(2)}) %collective-permute-start.1) | collective-permute-done | bytes 65568 | tf_op jit(solution)/shard_map/ppermute | solution.py:53
  10.6 1.0 %collective-permute-done.2.refs_2_ = bf16[128,256]{1,0:T(8,128)(2,1)S(1)} collective-permute-done((bf16[128,256]{1,0:T(8,128)(2,1)}, bf16[128,256]{1,0:T(8,128)(2,1)S(1)}, u32[]{:S(2)}, u32[]{:S(2)}) %collective-permute-start.2) | collective-permute-done | bytes 65568 | tf_op jit(solution)/shard_map/ppermute | solution.py:53
  12.3 1.2 %collective-permute-done.3.other_ref = bf16[512,256]{1,0:T(8,128)(2,1)S(1)} collective-permute-done((bf16[512,256]{1,0:T(8,128)(2,1)S(1)}, bf16[512,256]{1,0:T(8,128)(2,1)S(1)}, u32[]{:S(2)}, u32[]{:S(2)}) %collective-permute-start.3) | collective-permute-done | bytes 262176 | tf_op jit(solution)/shard_map/ppermute | solution.py:58
  13.5 2.5 %collective-permute-start.4 = (bf16[128,256]{1,0:T(8,128)(2,1)S(1)}, bf16[128,256]{1,0:T(8,128)(2,1)S(1)}, u32[]{:S(2)}, u32[]{:S(2)}) collective-permute-start(bf16[128,256]{1,0:T(8,128)(2,1)S(1)} %shard_map.114.refs_0_), channel_id=1, source_target_pairs={{0,24},{4,28},{8,16},{12,20},{16,8},{20,12},{24,0},{28,4},{1,25},{... | collective-permute-start | bytes 196616 | tf_op jit(solution)/shard_map/ppermute | solution.py:53
  16.1 0.6 collective-permute-start.5
  16.7 0.6 collective-permute-start.6
  17.3 1.8 %collective-permute-done.4.refs_0_ = bf16[128,256]{1,0:T(8,128)(2,1)S(1)} collective-permute-done((bf16[128,256]{1,0:T(8,128)(2,1)S(1)}, bf16[128,256]{1,0:T(8,128)(2,1)S(1)}, u32[]{:S(2)}, u32[]{:S(2)}) %collective-permute-start.4) | collective-permute-done | bytes 65568 | tf_op jit(solution)/shard_map/ppermute | solution.py:53
  19.1 1.3 %collective-permute-done.5.refs_1_ = bf16[128,256]{1,0:T(8,128)(2,1)S(1)} collective-permute-done((bf16[128,256]{1,0:T(8,128)(2,1)S(1)}, bf16[128,256]{1,0:T(8,128)(2,1)S(1)}, u32[]{:S(2)}, u32[]{:S(2)}) %collective-permute-start.5) | collective-permute-done | bytes 65568 | tf_op jit(solution)/shard_map/ppermute | solution.py:53
  20.4 0.6 collective-permute-done.6.refs_2_
  21.5 1.3 %collective-permute-start.7 = (bf16[272,256]{1,0:T(8,128)(2,1)S(1)}, bf16[272,256]{1,0:T(8,128)(2,1)S(1)}, u32[]{:S(2)}, u32[]{:S(2)}) collective-permute-start(bf16[272,256]{1,0:T(8,128)(2,1)S(1)} %shard_map.121.refs_1_), channel_id=1, source_target_pairs={{0,4},{8,12},{16,20},{24,28},{1,5},{9,13},{17,21},{25,29},{2,6},{1... | collective-permute-start | bytes 417800 | tf_op jit(solution)/shard_map/ppermute | solution.py:437
  22.8 1.5 %collective-permute-start.8 = (bf16[128,256]{1,0:T(8,128)(2,1)S(1)}, bf16[128,256]{1,0:T(8,128)(2,1)S(1)}, u32[]{:S(2)}, u32[]{:S(2)}) collective-permute-start(bf16[128,256]{1,0:T(8,128)(2,1)S(1)} %get-tuple-element.19.grad_ref.refs_3_), channel_id=1, source_target_pairs={{0,24},{4,28},{8,16},{12,20},{16,8},{20,12},{24,0},{28,4},{1,25},{... | collective-permute-start | bytes 196616 | tf_op jit(solution)/shard_map/ppermute | solution.py:53
  24.4 0.6 collective-permute-start.9
  24.9 1.5 %collective-permute-start.10 = (bf16[128,256]{1,0:T(8,128)(2,1)S(1)}, bf16[128,256]{1,0:T(8,128)(2,1)S(1)}, u32[]{:S(2)}, u32[]{:S(2)}) collective-permute-start(bf16[128,256]{1,0:T(8,128)(2,1)S(1)} %get-tuple-element.19.grad_ref.refs_3_), channel_id=1, source_target_pairs={{0,16},{4,20},{8,24},{12,28},{16,0},{20,4},{24,8},{28,12},{1,17},{... | collective-permute-start | bytes 196616 | tf_op jit(solution)/shard_map/ppermute | solution.py:53
  26.4 1.6 %collective-permute-done.8.refs_0_ = bf16[128,256]{1,0:T(8,128)(2,1)S(1)} collective-permute-done((bf16[128,256]{1,0:T(8,128)(2,1)S(1)}, bf16[128,256]{1,0:T(8,128)(2,1)S(1)}, u32[]{:S(2)}, u32[]{:S(2)}) %collective-permute-start.8) | collective-permute-done | bytes 65568 | tf_op jit(solution)/shard_map/ppermute | solution.py:53
  29.3 0.7 %collective-permute-start.15 = (bf16[272,256]{1,0:T(8,128)(2,1)S(1)}, bf16[272,256]{1,0:T(8,128)(2,1)S(1)}, u32[]{:S(2)}, u32[]{:S(2)}) collective-permute-start(bf16[272,256]{1,0:T(8,128)(2,1)S(1)} %shard_map.122.after_ref.refs_3_), channel_id=1, source_target_pairs={{4,7},{12,15},{20,23},{28,31},{5,6},{13,14},{21,22},{29,30},{6,5},... | collective-permute-start | bytes 417800 | tf_op jit(solution)/shard_map/ppermute | solution.py:73
  30.0 0.7 %collective-permute-start.16 = (bf16[272,256]{1,0:T(8,128)(2,1)S(1)}, bf16[272,256]{1,0:T(8,128)(2,1)S(1)}, u32[]{:S(2)}, u32[]{:S(2)}) collective-permute-start(bf16[272,256]{1,0:T(8,128)(2,1)S(1)} %shard_map.122.after_ref.refs_3_), channel_id=1, source_target_pairs={{4,5},{12,13},{20,21},{28,29},{5,4},{13,12},{21,20},{29,28},{6,7},... | collective-permute-start | bytes 417800 | tf_op jit(solution)/shard_map/ppermute | solution.py:73
  30.7 0.7 %collective-permute-start.17 = (bf16[272,256]{1,0:T(8,128)(2,1)S(1)}, bf16[272,256]{1,0:T(8,128)(2,1)S(1)}, u32[]{:S(2)}, u32[]{:S(2)}) collective-permute-start(bf16[272,256]{1,0:T(8,128)(2,1)S(1)} %shard_map.122.after_ref.refs_3_), channel_id=1, source_target_pairs={{4,6},{12,14},{20,22},{28,30},{5,7},{13,15},{21,23},{29,31},{6,4},... | collective-permute-start | bytes 417800 | tf_op jit(solution)/shard_map/ppermute | solution.py:73
  32.9 0.7 %collective-permute-start.18 = (bf16[272,256]{1,0:T(8,128)(2,1)S(1)}, bf16[272,256]{1,0:T(8,128)(2,1)S(1)}, u32[]{:S(2)}, u32[]{:S(2)}) collective-permute-start(bf16[272,256]{1,0:T(8,128)(2,1)S(1)} %shard_map.130.refs_3_), channel_id=1, source_target_pairs={{4,28},{12,20},{20,12},{28,4},{5,29},{13,21},{21,13},{29,5},{6,30}... | collective-permute-start | bytes 417800 | tf_op jit(solution)/shard_map/ppermute | solution.py:73
  33.6 0.7 %collective-permute-start.19 = (bf16[272,256]{1,0:T(8,128)(2,1)S(1)}, bf16[272,256]{1,0:T(8,128)(2,1)S(1)}, u32[]{:S(2)}, u32[]{:S(2)}) collective-permute-start(bf16[272,256]{1,0:T(8,128)(2,1)S(1)} %shard_map.130.refs_3_), channel_id=1, source_target_pairs={{4,12},{12,4},{20,28},{28,20},{5,13},{13,5},{21,29},{29,21},{6,14}... | collective-permute-start | bytes 417800 | tf_op jit(solution)/shard_map/ppermute | solution.py:73
  34.3 0.7 %collective-permute-start.20 = (bf16[272,256]{1,0:T(8,128)(2,1)S(1)}, bf16[272,256]{1,0:T(8,128)(2,1)S(1)}, u32[]{:S(2)}, u32[]{:S(2)}) collective-permute-start(bf16[272,256]{1,0:T(8,128)(2,1)S(1)} %shard_map.130.refs_3_), channel_id=1, source_target_pairs={{4,20},{12,28},{20,4},{28,12},{5,21},{13,29},{21,5},{29,13},{6,22}... | collective-permute-start | bytes 417800 | tf_op jit(solution)/shard_map/ppermute | solution.py:73
  34.9 2.2 %collective-permute-start.12 = (bf16[128,256]{1,0:T(8,128)(2,1)S(1)}, bf16[128,256]{1,0:T(8,128)(2,1)S(1)}, u32[]{:S(2)}, u32[]{:S(2)}) collective-permute-start(bf16[128,256]{1,0:T(8,128)(2,1)S(1)} %shard_map.125.refs_0_), channel_id=1, source_target_pairs={{0,3},{1,2},{2,1},{3,0},{4,7},{5,6},{6,5},{7,4},{8,11},{9,10},{10,... | collective-permute-start | bytes 196616 | tf_op jit(solution)/shard_map/ppermute | solution.py:53
  37.5 3.6 %collective-permute-done.12.refs_0_ = bf16[128,256]{1,0:T(8,128)(2,1)S(1)} collective-permute-done((bf16[128,256]{1,0:T(8,128)(2,1)S(1)}, bf16[128,256]{1,0:T(8,128)(2,1)S(1)}, u32[]{:S(2)}, u32[]{:S(2)}) %collective-permute-start.12) | collective-permute-done | bytes 65568 | tf_op jit(solution)/shard_map/ppermute | solution.py:53
  41.2 1.7 %collective-permute-done.13.refs_1_ = bf16[128,256]{1,0:T(8,128)(2,1)S(1)} collective-permute-done((bf16[128,256]{1,0:T(8,128)(2,1)S(1)}, bf16[128,256]{1,0:T(8,128)(2,1)S(1)}, u32[]{:S(2)}, u32[]{:S(2)}) %collective-permute-start.13) | collective-permute-done | bytes 65568 | tf_op jit(solution)/shard_map/ppermute | solution.py:53
  42.9 3.4 %collective-permute-done.14.refs_2_ = bf16[128,256]{1,0:T(8,128)(2,1)S(1)} collective-permute-done((bf16[128,256]{1,0:T(8,128)(2,1)S(1)}, bf16[128,256]{1,0:T(8,128)(2,1)S(1)}, u32[]{:S(2)}, u32[]{:S(2)}) %collective-permute-start.14) | collective-permute-done | bytes 65568 | tf_op jit(solution)/shard_map/ppermute | solution.py:53
  46.3 0.8 %shard_map.129.after_ref = bf16[128,256]{1,0:T(8,128)(2,1)} custom-call(bf16[256,256]{1,0:T(8,128)(2,1)S(1)} %copy-done, bf16[128,256]{1,0:T(8,128)(2,1)S(1)} %collective-permute-done.12.refs_0_, bf16[128,256]{1,0:T(8,128)(2,1)S(1)} %collective-permute-done.13.refs_1_, bf16[128,256]{1,0:T(8,128)(2,1)S(1)} %collective-permute-done.14.refs_2_, ...), custom_call_target="tpu_custom_call" | custom-call | flops 16777216 | bytes 262144 | tf_op jit(solution)/shard_map/pallas_call | solution.py:484
  47.2 1.3 %collective-permute-start.21 = (f32[264,256]{1,0:T(8,128)S(1)}, f32[264,256]{1,0:T(8,128)S(1)}, u32[]{:S(2)}, u32[]{:S(2)}) collective-permute-start(f32[264,256]{1,0:T(8,128)S(1)} %shard_map.131.own_ref), channel_id=1, source_target_pairs={{4,0},{12,8},{20,16},{28,24},{5,1},{13,9},{21,17},{29,25},{6,2},{1... | collective-permute-start | bytes 811016 | tf_op jit(solution)/shard_map/ppermute | solution.py:502
  48.5 0.6 shard_map.119
  49.2 15.8 %collective-permute-done.21.other_ref = f32[264,256]{1,0:T(8,128)S(1)} collective-permute-done((f32[264,256]{1,0:T(8,128)S(1)}, f32[264,256]{1,0:T(8,128)S(1)}, u32[]{:S(2)}, u32[]{:S(2)}) %collective-permute-start.21) | collective-permute-done | bytes 270368 | tf_op jit(solution)/shard_map/ppermute | solution.py:502
  65.0 0.7 %shard_map.132 = (f32[256,256]{1,0:T(8,128)}, f32[1,256]{1,0:T(1,128)}) custom-call(f32[264,256]{1,0:T(8,128)S(1)} %shard_map.131.own_ref, f32[264,256]{1,0:T(8,128)S(1)} %collective-permute-done.21.other_ref), custom_call_target="tpu_custom_call" | custom-call | bytes 524288 | tf_op jit(solution)/shard_map/pallas_call | solution.py:503
  (40 shorter events, 4.5 us)
Async XLA Ops:
  0.6 8.6 %collective-permute-start = (bf16[128,256]{1,0:T(8,128)(2,1)}, bf16[128,256]{1,0:T(8,128)(2,1)S(1)}, u32[]{:S(2)}, u32[]{:S(2)}) collective-permute-start(bf16[128,256]{1,0:T(8,128)(2,1)} %refs_3_.1), channel_id=1, source_target_pairs={{0,3},{1,2},{2,1},{3,0},{4,7},{5,6},{6,5},{7,4},{8,11},{9,10},{10,... | collective-permute-start | bytes 196616 | tf_op jit(solution)/shard_map/ppermute | solution.py:53
  5.7 4.9 %collective-permute-start.1 = (bf16[128,256]{1,0:T(8,128)(2,1)}, bf16[128,256]{1,0:T(8,128)(2,1)S(1)}, u32[]{:S(2)}, u32[]{:S(2)}) collective-permute-start(bf16[128,256]{1,0:T(8,128)(2,1)} %refs_3_.1), channel_id=1, source_target_pairs={{0,1},{1,0},{2,3},{3,2},{4,5},{5,4},{6,7},{7,6},{8,9},{9,8},{10,11... | collective-permute-start | bytes 196616 | tf_op jit(solution)/shard_map/ppermute | solution.py:53
  5.8 5.8 %collective-permute-start.2 = (bf16[128,256]{1,0:T(8,128)(2,1)}, bf16[128,256]{1,0:T(8,128)(2,1)S(1)}, u32[]{:S(2)}, u32[]{:S(2)}) collective-permute-start(bf16[128,256]{1,0:T(8,128)(2,1)} %refs_3_.1), channel_id=1, source_target_pairs={{0,2},{1,3},{2,0},{3,1},{4,6},{5,7},{6,4},{7,5},{8,10},{9,11},{10,... | collective-permute-start | bytes 196616 | tf_op jit(solution)/shard_map/ppermute | solution.py:53
  7.0 4.6 %copy-start.1 = (bf16[128,256]{1,0:T(8,128)(2,1)S(1)}, bf16[128,256]{1,0:T(8,128)(2,1)}, u32[]{:S(2)}) copy-start(bf16[128,256]{1,0:T(8,128)(2,1)} %refs_3_.1) | copy-start | bytes 196612
  11.9 1.6 %collective-permute-start.3 = (bf16[512,256]{1,0:T(8,128)(2,1)S(1)}, bf16[512,256]{1,0:T(8,128)(2,1)S(1)}, u32[]{:S(2)}, u32[]{:S(2)}) collective-permute-start(bf16[512,256]{1,0:T(8,128)(2,1)S(1)} %get-tuple-element.16), channel_id=1, source_target_pairs={{0,4},{4,0},{8,12},{12,8},{16,20},{20,16},{24,28},{28,24},{1,5},{5... | collective-permute-start | bytes 786440 | tf_op jit(solution)/shard_map/ppermute | solution.py:58
  13.5 5.5 %collective-permute-start.4 = (bf16[128,256]{1,0:T(8,128)(2,1)S(1)}, bf16[128,256]{1,0:T(8,128)(2,1)S(1)}, u32[]{:S(2)}, u32[]{:S(2)}) collective-permute-start(bf16[128,256]{1,0:T(8,128)(2,1)S(1)} %shard_map.114.refs_0_), channel_id=1, source_target_pairs={{0,24},{4,28},{8,16},{12,20},{16,8},{20,12},{24,0},{28,4},{1,25},{... | collective-permute-start | bytes 196616 | tf_op jit(solution)/shard_map/ppermute | solution.py:53
  16.1 4.3 %collective-permute-start.5 = (bf16[128,256]{1,0:T(8,128)(2,1)S(1)}, bf16[128,256]{1,0:T(8,128)(2,1)S(1)}, u32[]{:S(2)}, u32[]{:S(2)}) collective-permute-start(bf16[128,256]{1,0:T(8,128)(2,1)S(1)} %shard_map.115.refs_0_), channel_id=1, source_target_pairs={{0,8},{4,12},{8,0},{12,4},{16,24},{20,28},{24,16},{28,20},{1,9},{5... | collective-permute-start | bytes 196616 | tf_op jit(solution)/shard_map/ppermute | solution.py:53
  16.7 4.4 %copy-start = (bf16[256,256]{1,0:T(8,128)(2,1)S(1)}, bf16[256,256]{1,0:T(8,128)(2,1)}, u32[]{:S(2)}) copy-start(bf16[256,256]{1,0:T(8,128)(2,1)} %weight_ref.3) | copy-start | bytes 393220
  16.7 4.3 %copy-start.2 = (bf16[128,256]{1,0:T(8,128)(2,1)S(1)}, bf16[128,256]{1,0:T(8,128)(2,1)}, u32[]{:S(2)}) copy-start(bf16[128,256]{1,0:T(8,128)(2,1)} %cot_ref.1) | copy-start | bytes 196612
  16.7 4.3 %collective-permute-start.6 = (bf16[128,256]{1,0:T(8,128)(2,1)S(1)}, bf16[128,256]{1,0:T(8,128)(2,1)S(1)}, u32[]{:S(2)}, u32[]{:S(2)}) collective-permute-start(bf16[128,256]{1,0:T(8,128)(2,1)S(1)} %shard_map.116.refs_0_), channel_id=1, source_target_pairs={{0,16},{4,20},{8,24},{12,28},{16,0},{20,4},{24,8},{28,12},{1,17},{... | collective-permute-start | bytes 196616 | tf_op jit(solution)/shard_map/ppermute | solution.py:53
  21.5 4.9 %collective-permute-start.7 = (bf16[272,256]{1,0:T(8,128)(2,1)S(1)}, bf16[272,256]{1,0:T(8,128)(2,1)S(1)}, u32[]{:S(2)}, u32[]{:S(2)}) collective-permute-start(bf16[272,256]{1,0:T(8,128)(2,1)S(1)} %shard_map.121.refs_1_), channel_id=1, source_target_pairs={{0,4},{8,12},{16,20},{24,28},{1,5},{9,13},{17,21},{25,29},{2,6},{1... | collective-permute-start | bytes 417800 | tf_op jit(solution)/shard_map/ppermute | solution.py:437
  22.8 5.2 %collective-permute-start.8 = (bf16[128,256]{1,0:T(8,128)(2,1)S(1)}, bf16[128,256]{1,0:T(8,128)(2,1)S(1)}, u32[]{:S(2)}, u32[]{:S(2)}) collective-permute-start(bf16[128,256]{1,0:T(8,128)(2,1)S(1)} %get-tuple-element.19.grad_ref.refs_3_), channel_id=1, source_target_pairs={{0,24},{4,28},{8,16},{12,20},{16,8},{20,12},{24,0},{28,4},{1,25},{... | collective-permute-start | bytes 196616 | tf_op jit(solution)/shard_map/ppermute | solution.py:53
  24.4 4.3 %collective-permute-start.9 = (bf16[128,256]{1,0:T(8,128)(2,1)S(1)}, bf16[128,256]{1,0:T(8,128)(2,1)S(1)}, u32[]{:S(2)}, u32[]{:S(2)}) collective-permute-start(bf16[128,256]{1,0:T(8,128)(2,1)S(1)} %get-tuple-element.19.grad_ref.refs_3_), channel_id=1, source_target_pairs={{0,8},{4,12},{8,0},{12,4},{16,24},{20,28},{24,16},{28,20},{1,9},{5... | collective-permute-start | bytes 196616 | tf_op jit(solution)/shard_map/ppermute | solution.py:53
  24.9 4.3 %collective-permute-start.10 = (bf16[128,256]{1,0:T(8,128)(2,1)S(1)}, bf16[128,256]{1,0:T(8,128)(2,1)S(1)}, u32[]{:S(2)}, u32[]{:S(2)}) collective-permute-start(bf16[128,256]{1,0:T(8,128)(2,1)S(1)} %get-tuple-element.19.grad_ref.refs_3_), channel_id=1, source_target_pairs={{0,16},{4,20},{8,24},{12,28},{16,0},{20,4},{24,8},{28,12},{1,17},{... | collective-permute-start | bytes 196616 | tf_op jit(solution)/shard_map/ppermute | solution.py:53
  29.2 2.8 %collective-permute-start.11 = (bf16[512,256]{1,0:T(8,128)(2,1)S(1)}, bf16[512,256]{1,0:T(8,128)(2,1)S(1)}, u32[]{:S(2)}, u32[]{:S(2)}) collective-permute-start(bf16[512,256]{1,0:T(8,128)(2,1)S(1)} %shard_map.123.source_ref), channel_id=1, source_target_pairs={{0,4},{4,0},{8,12},{12,8},{16,20},{20,16},{24,28},{28,24},{1,5},{5... | collective-permute-start | bytes 786440 | tf_op jit(solution)/shard_map/ppermute | solution.py:58
  29.3 3.5 %collective-permute-start.15 = (bf16[272,256]{1,0:T(8,128)(2,1)S(1)}, bf16[272,256]{1,0:T(8,128)(2,1)S(1)}, u32[]{:S(2)}, u32[]{:S(2)}) collective-permute-start(bf16[272,256]{1,0:T(8,128)(2,1)S(1)} %shard_map.122.after_ref.refs_3_), channel_id=1, source_target_pairs={{4,7},{12,15},{20,23},{28,31},{5,6},{13,14},{21,22},{29,30},{6,5},... | collective-permute-start | bytes 417800 | tf_op jit(solution)/shard_map/ppermute | solution.py:73
  30.0 2.8 %collective-permute-start.16 = (bf16[272,256]{1,0:T(8,128)(2,1)S(1)}, bf16[272,256]{1,0:T(8,128)(2,1)S(1)}, u32[]{:S(2)}, u32[]{:S(2)}) collective-permute-start(bf16[272,256]{1,0:T(8,128)(2,1)S(1)} %shard_map.122.after_ref.refs_3_), channel_id=1, source_target_pairs={{4,5},{12,13},{20,21},{28,29},{5,4},{13,12},{21,20},{29,28},{6,7},... | collective-permute-start | bytes 417800 | tf_op jit(solution)/shard_map/ppermute | solution.py:73
  30.7 2.2 %collective-permute-start.17 = (bf16[272,256]{1,0:T(8,128)(2,1)S(1)}, bf16[272,256]{1,0:T(8,128)(2,1)S(1)}, u32[]{:S(2)}, u32[]{:S(2)}) collective-permute-start(bf16[272,256]{1,0:T(8,128)(2,1)S(1)} %shard_map.122.after_ref.refs_3_), channel_id=1, source_target_pairs={{4,6},{12,14},{20,22},{28,30},{5,7},{13,15},{21,23},{29,31},{6,4},... | collective-permute-start | bytes 417800 | tf_op jit(solution)/shard_map/ppermute | solution.py:73
  32.9 14.2 %collective-permute-start.18 = (bf16[272,256]{1,0:T(8,128)(2,1)S(1)}, bf16[272,256]{1,0:T(8,128)(2,1)S(1)}, u32[]{:S(2)}, u32[]{:S(2)}) collective-permute-start(bf16[272,256]{1,0:T(8,128)(2,1)S(1)} %shard_map.130.refs_3_), channel_id=1, source_target_pairs={{4,28},{12,20},{20,12},{28,4},{5,29},{13,21},{21,13},{29,5},{6,30}... | collective-permute-start | bytes 417800 | tf_op jit(solution)/shard_map/ppermute | solution.py:73
  33.6 13.6 %collective-permute-start.19 = (bf16[272,256]{1,0:T(8,128)(2,1)S(1)}, bf16[272,256]{1,0:T(8,128)(2,1)S(1)}, u32[]{:S(2)}, u32[]{:S(2)}) collective-permute-start(bf16[272,256]{1,0:T(8,128)(2,1)S(1)} %shard_map.130.refs_3_), channel_id=1, source_target_pairs={{4,12},{12,4},{20,28},{28,20},{5,13},{13,5},{21,29},{29,21},{6,14}... | collective-permute-start | bytes 417800 | tf_op jit(solution)/shard_map/ppermute | solution.py:73
  34.3 12.9 %collective-permute-start.20 = (bf16[272,256]{1,0:T(8,128)(2,1)S(1)}, bf16[272,256]{1,0:T(8,128)(2,1)S(1)}, u32[]{:S(2)}, u32[]{:S(2)}) collective-permute-start(bf16[272,256]{1,0:T(8,128)(2,1)S(1)} %shard_map.130.refs_3_), channel_id=1, source_target_pairs={{4,20},{12,28},{20,4},{28,12},{5,21},{13,29},{21,5},{29,13},{6,22}... | collective-permute-start | bytes 417800 | tf_op jit(solution)/shard_map/ppermute | solution.py:73
  34.9 6.2 %collective-permute-start.12 = (bf16[128,256]{1,0:T(8,128)(2,1)S(1)}, bf16[128,256]{1,0:T(8,128)(2,1)S(1)}, u32[]{:S(2)}, u32[]{:S(2)}) collective-permute-start(bf16[128,256]{1,0:T(8,128)(2,1)S(1)} %shard_map.125.refs_0_), channel_id=1, source_target_pairs={{0,3},{1,2},{2,1},{3,0},{4,7},{5,6},{6,5},{7,4},{8,11},{9,10},{10,... | collective-permute-start | bytes 196616 | tf_op jit(solution)/shard_map/ppermute | solution.py:53
  37.2 5.7 %collective-permute-start.13 = (bf16[128,256]{1,0:T(8,128)(2,1)S(1)}, bf16[128,256]{1,0:T(8,128)(2,1)S(1)}, u32[]{:S(2)}, u32[]{:S(2)}) collective-permute-start(bf16[128,256]{1,0:T(8,128)(2,1)S(1)} %shard_map.126.refs_0_), channel_id=1, source_target_pairs={{0,1},{1,0},{2,3},{3,2},{4,5},{5,4},{6,7},{7,6},{8,9},{9,8},{10,11... | collective-permute-start | bytes 196616 | tf_op jit(solution)/shard_map/ppermute | solution.py:53
  41.1 5.2 %collective-permute-start.14 = (bf16[128,256]{1,0:T(8,128)(2,1)S(1)}, bf16[128,256]{1,0:T(8,128)(2,1)S(1)}, u32[]{:S(2)}, u32[]{:S(2)}) collective-permute-start(bf16[128,256]{1,0:T(8,128)(2,1)S(1)} %shard_map.127.refs_0_), channel_id=1, source_target_pairs={{0,2},{1,3},{2,0},{3,1},{4,6},{5,7},{6,4},{7,5},{8,10},{9,11},{10,... | collective-permute-start | bytes 196616 | tf_op jit(solution)/shard_map/ppermute | solution.py:53
  47.2 17.7 %collective-permute-start.21 = (f32[264,256]{1,0:T(8,128)S(1)}, f32[264,256]{1,0:T(8,128)S(1)}, u32[]{:S(2)}, u32[]{:S(2)}) collective-permute-start(f32[264,256]{1,0:T(8,128)S(1)} %shard_map.131.own_ref), channel_id=1, source_target_pairs={{4,0},{12,8},{20,16},{28,24},{5,1},{13,9},{21,17},{29,25},{6,2},{1... | collective-permute-start | bytes 811016 | tf_op jit(solution)/shard_map/ppermute | solution.py:502

commit v7 on v5

--- a/solution.py
+++ b/solution.py
@@ -13,6 +13,8 @@
 CUBIC = 0.044715
 VMEM_LIMIT = 48 * 1024 * 1024
 BIAS_ROWS = 16
+ROW_SUM_WEIGHT = 250
+FEATURES_WEIGHT = 150
 
 VMEM_SPEC = pl.BlockSpec(memory_space=pltpu.VMEM)
 HBM_SPEC = pl.BlockSpec(memory_space=pltpu.HBM)
@@ -259,6 +261,13 @@
     out_ref[...] = dense_dot(turned_ref[:, : source_ref.shape[0]], source_ref[...])
 
 
+def back_piece_kernel(turned_ref, own_ref, source_ref, *refs, k, n_row):
+    out_ref = refs[-1]
+    rows = block_at(partner(row_index(), k, n_row), out_ref.shape[0])
+    rest = dense_dot(turned_ref[rows, source_ref.shape[0] :], source_ref[...])
+    out_ref[...] = (own_ref[rows, :] + rest).astype(BF16)
+
+
 def slot_back_kernel(count_ref, row_ref, col_ref, tiles_ref, own_ref, other_ref, out_ref, source_ref):
     half = own_ref.shape[0]
     source_ref[:half, :] = own_ref[...]
@@ -266,37 +275,16 @@
     slot_product((count_ref, row_ref, col_ref, tiles_ref), source_ref, out_ref, True)
 
 
-def back_rows(refs, place):
-    if len(refs) == 1:
-        return refs[0][place, :]
-    turned_ref, own_ref, source_ref = refs
-    rest = dense_dot(turned_ref[place, source_ref.shape[0] :], source_ref[...])
-    return own_ref[place, :] + rest
-
-
-def back_near_kernel(*refs, targets):
+def slot_piece_kernel(back_ref, *refs, k, n_row):
     out_ref = refs[-1]
-    tile = out_ref.shape[0] // len(targets)
-    for i, k in enumerate(targets):
-        place = block_at(row_index() ^ k, tile)
-        out_ref[i * tile : (i + 1) * tile, :] = back_rows(refs[:-1], place).astype(BF16)
-
-
-def back_far_kernel(*refs, k, at):
-    near_ref, out_ref = refs[-2:]
-    tile = out_ref.shape[0]
-    rows = back_rows(refs[:-2], block_at(row_index() ^ k, tile))
-    near = near_ref[at * tile : (at + 1) * tile, :].astype(F32)
-    out_ref[...] = (rows + near).astype(BF16)
-
-
-def features_kernel(weight_ref, near_ref, *refs):
+    rows = block_at(partner(row_index(), k, n_row), out_ref.shape[0])
+    out_ref[...] = back_ref[rows, :].astype(BF16)
+
+
+def features_kernel(weight_ref, *refs):
     parts, out_ref = refs[:-1], refs[-1]
-    total = near_ref[: out_ref.shape[0], :].astype(F32)
-    for ref in parts:
-        total += ref[...].astype(F32)
     out_ref[...] = lax.dot_general(
-        total.astype(BF16),
+        summed(parts).astype(BF16),
         weight_ref[...],
         (((1,), (1,)), ((), ())),
         preferred_element_type=F32,
@@ -337,15 +325,15 @@
     near = 1
     own_nodes = n_chip * tile
 
-    def add(terms, after=()):
+    def add(terms, flops=0):
         return call(
             functools.partial(add_terms_kernel, n_terms=len(terms)),
             like(half + BIAS_ROWS, hidden),
-            [VMEM_SPEC] * (len(terms) + len(after)),
-            [],
-            len(terms) * half * hidden,
+            [VMEM_SPEC] * len(terms),
+            [],
+            flops or len(terms) * half * hidden,
             len(terms) * half * hidden * 2,
-        )(*terms, *after)
+        )(*terms)
 
     is_dense = n_row * n_col <= 2 * slots
     if is_dense:
@@ -446,8 +434,7 @@
         6 * block_bytes,
     )(aggregated, grad)
     chip_term = add([swap_cores(theirs, n_col), mine])
-    row_terms = total_over(chip_term, add, "row", n_row)
-    row_term = add(row_terms)
+    row_term = add(exchange([chip_term] * n_row, "row", n_row), flops=ROW_SUM_WEIGHT * matrix)
 
     own_grads = call(
         gather_kernel,
@@ -467,7 +454,7 @@
             slots * matrix // 2,
             row_nodes * hidden * 8,
         )(turned, own_grads)
-        back_args = (turned, back_own, other_grads)
+        piece_kernel, piece_args = back_piece_kernel, (turned, back_own, other_grads)
     else:
         back = call(
             slot_back_kernel,
@@ -477,39 +464,27 @@
             slots * matrix // 2,
             row_nodes * hidden * 8,
         )(*slot_args, own_grads, other_grads)
-        back_args = (back,)
-
-    evens, odds = range(2, n_row, 2), range(3, n_row, 2)
-    targets = [1, *evens]
-    near_piece = call(
-        functools.partial(back_near_kernel, targets=targets),
-        like(len(targets) * tile, hidden),
-        [VMEM_SPEC] * len(back_args),
-        [],
-        len(targets) * n_chip * matrix,
-        len(targets) * 2 * block_bytes,
-    )(*back_args)
-    near = lax.ppermute(near_piece, "row", pairs_of(1, n_row, 1))
-    backs = []
-    for k in [0, *odds]:
-        piece = call(
-            functools.partial(back_far_kernel, k=k, at=(k - 1) // 2) if k else
-            functools.partial(back_near_kernel, targets=[0]),
+        piece_kernel, piece_args = slot_piece_kernel, (back,)
+
+    def back_piece(k, before):
+        return call(
+            functools.partial(piece_kernel, k=k, n_row=n_row),
             like(tile, hidden),
-            [VMEM_SPEC] * (len(back_args) + (k > 0)),
+            [VMEM_SPEC] * (len(piece_args) + len(before)),
             [],
             n_chip * matrix,
             2 * block_bytes,
-        )(*back_args, *([near] if k else []))
-        backs.append(lax.ppermute(piece, "row", pairs_of(k, n_row, 1)) if k else piece)
+        )(*piece_args, *before)
+
+    backs = exchange(in_turn(n_row, back_piece), "row", n_row)
     grad_features = call(
         features_kernel,
         like(tile, width),
-        [VMEM_SPEC] * (2 + len(backs)),
+        [VMEM_SPEC] * (1 + n_row),
         [],
-        matrix,
+        FEATURES_WEIGHT * matrix,
         n_row * block_bytes,
-    )(weight, near, *backs)
+    )(weight, *backs)
     all_terms = total_over(row_term, add, "col", n_col, 2)
     factor = (tile * n_row * n_col) ** (-0.5)
     own_half, bias_grad = call(

time: 54.5 us -> 48.4 us (0.89)
  waiting for transfers between devices: 23.5 us -> 16 us
  starting transfers between devices: 22.4 us -> 24.4 us
  Pallas kernels: 6.94 us -> 6.35 us
    ppermute x9 -> x15, starting transfers between devices: 13 us -> 22 us  [exchange(): lax.ppermute(blocks[k], axis, pairs)]
    ppermute x4 -> x2, waiting for transfers between devices: 8.3 us -> 0.66 us  [total_over(): terms = [lax.ppermute(block, axis, pairs_of(step, size, cores)), block]]
    ppermute x4 -> x2, starting transfers between devices: 6.28 us -> 2.14 us  [total_over(): terms = [lax.ppermute(block, axis, pairs_of(step, size, cores)), block]]
    ppermute x9 -> x15, waiting for transfers between devices: 9.35 us -> 13.4 us  [exchange(): lax.ppermute(blocks[k], axis, pairs)]
    ppermute x2 -> x0, waiting for transfers between devices: 3.88 us -> none  [the longest x1 3.88 us: local(): lax.ppermute(piece, 'row', pairs_of(k, n_row, 1))]
    ppermute x2 -> x0, starting transfers between devices: 2.89 us -> none  [the longest x1 2.05 us: local(): lax.ppermute(piece, 'row', pairs_of(k, n_row, 1))]
    pallas_call x1, Pallas kernels: 2.13 us -> 1.4 us  [local(): call(dense_kernel, (like(row_nodes, col_nodes), like(1, hidden, F32)), [S...]
    pallas_call x4 -> x5, Pallas kernels: 1.44 us -> 1.59 us  [the longest x1 0.83 us: local(): call(features_kernel, like(tile, width), [VMEM_SPEC] * (1 + n_row), [], F...]
  transfers between devices with their start and end apart: 19 -> 21, of which waited for: 14 -> 15; matrix products, arithmetic and copies ran while one was open for 0% -> 0% of each run, Pallas kernels for 10% -> 10%
where the time goes in v7:
time: 48.4 us; the launch traced here: 48.2 us
  starting transfers between devices  24.4 us (50%)
  waiting for transfers between devices  16 us (33%)
  Pallas kernels  6.35 us (13%)
  between operations  1.48 us (3%)
    ppermute x15, starting transfers between devices, exchange(): lax.ppermute(blocks[k], axis, pairs)  22 us
    ppermute x15, waiting for transfers between devices, exchange(): lax.ppermute(blocks[k], axis, pairs)  13.4 us
    ppermute x2, starting transfers between devices, total_over(): terms = [lax.ppermute(block, axis, pairs_of(step, size, cores)), block]  2.14 us
    ppermute x4, waiting for transfers between devices, swap_cores(): return lax.ppermute(block, 'col', [(i, i ^ 1) for i in range(size)])  1.93 us
    pallas_call x1, Pallas kernels, local(): call(dense_kernel, (like(row_nodes, col_nodes), like(1, hidden, F32)), [S...  1.4 us
  transfers between devices with their start and end apart: 21, of which 15 were waited for; matrix products, arithmetic and copies ran while one was open for 0% of the time, Pallas kernels for 10%

profile of v7, /device:TPU:0, one launch (start us, length us, event | category | flops | bytes accessed | tf_op | source)
XLA Modules:
  0.0 48.2 jit_solution(10991316726132796300)
XLA Ops:
  0.6 5.1 %collective-permute-start = (bf16[128,256]{1,0:T(8,128)(2,1)}, bf16[128,256]{1,0:T(8,128)(2,1)S(1)}, u32[]{:S(2)}, u32[]{:S(2)}) collective-permute-start(bf16[128,256]{1,0:T(8,128)(2,1)} %refs_3_.1), channel_id=1, source_target_pairs={{0,3},{1,2},{2,1},{3,0},{4,7},{5,6},{6,5},{7,4},{8,11},{9,10},{10,... | collective-permute-start | bytes 196616 | tf_op jit(solution)/shard_map/ppermute | solution.py:55
  5.8 0.6 %collective-permute-start.2 = (bf16[128,256]{1,0:T(8,128)(2,1)}, bf16[128,256]{1,0:T(8,128)(2,1)S(1)}, u32[]{:S(2)}, u32[]{:S(2)}) collective-permute-start(bf16[128,256]{1,0:T(8,128)(2,1)} %refs_3_.1), channel_id=1, source_target_pairs={{0,2},{1,3},{2,0},{3,1},{4,6},{5,7},{6,4},{7,5},{8,10},{9,11},{10,... | collective-permute-start | bytes 196616 | tf_op jit(solution)/shard_map/ppermute | solution.py:55
  7.1 1.4 %shard_map.111 = (bf16[1024,512]{1,0:T(8,128)(2,1)S(1)}, f32[1,256]{1,0:T(1,128)S(1)}) custom-call(s32[1,1]{1,0:T(1,128)S(6)} %copy.12.count_ref, s32[1,1,32]{2,1,0:T(1,128)} %row_hbm.1, s32[1,1,32]{2,1,0:T(1,128)} %col_hbm.1, bf16[1,1,32,128,128]{4,3,2,1,0:T(8,128)(2,1)} %tiles_hbm.1, f32[1,256]{1,0:T(1,128)} %bitcast.2), custom_call_target="tpu_custom_call" | custom-call | bytes 6291456 | tf_op jit(solution)/shard_map/pallas_call | solution.py:341
  8.5 0.4 collective-permute-done.refs_0_
  8.9 1.8 %collective-permute-done.1.refs_1_ = bf16[128,256]{1,0:T(8,128)(2,1)S(1)} collective-permute-done((bf16[128,256]{1,0:T(8,128)(2,1)}, bf16[128,256]{1,0:T(8,128)(2,1)S(1)}, u32[]{:S(2)}, u32[]{:S(2)}) %collective-permute-start.1) | collective-permute-done | bytes 65568 | tf_op jit(solution)/shard_map/ppermute | solution.py:55
  10.6 1.0 %collective-permute-done.2.refs_2_ = bf16[128,256]{1,0:T(8,128)(2,1)S(1)} collective-permute-done((bf16[128,256]{1,0:T(8,128)(2,1)}, bf16[128,256]{1,0:T(8,128)(2,1)S(1)}, u32[]{:S(2)}, u32[]{:S(2)}) %collective-permute-start.2) | collective-permute-done | bytes 65568 | tf_op jit(solution)/shard_map/ppermute | solution.py:55
  12.3 1.2 %collective-permute-done.3.other_ref = bf16[512,256]{1,0:T(8,128)(2,1)S(1)} collective-permute-done((bf16[512,256]{1,0:T(8,128)(2,1)S(1)}, bf16[512,256]{1,0:T(8,128)(2,1)S(1)}, u32[]{:S(2)}, u32[]{:S(2)}) %collective-permute-start.3) | collective-permute-done | bytes 262176 | tf_op jit(solution)/shard_map/ppermute | solution.py:60
  13.5 2.5 %collective-permute-start.4 = (bf16[128,256]{1,0:T(8,128)(2,1)S(1)}, bf16[128,256]{1,0:T(8,128)(2,1)S(1)}, u32[]{:S(2)}, u32[]{:S(2)}) collective-permute-start(bf16[128,256]{1,0:T(8,128)(2,1)S(1)} %shard_map.114.refs_0_), channel_id=1, source_target_pairs={{0,24},{4,28},{8,16},{12,20},{16,8},{20,12},{24,0},{28,4},{1,25},{... | collective-permute-start | bytes 196616 | tf_op jit(solution)/shard_map/ppermute | solution.py:55
  16.1 0.6 %collective-permute-start.5 = (bf16[128,256]{1,0:T(8,128)(2,1)S(1)}, bf16[128,256]{1,0:T(8,128)(2,1)S(1)}, u32[]{:S(2)}, u32[]{:S(2)}) collective-permute-start(bf16[128,256]{1,0:T(8,128)(2,1)S(1)} %shard_map.115.refs_0_), channel_id=1, source_target_pairs={{0,8},{4,12},{8,0},{12,4},{16,24},{20,28},{24,16},{28,20},{1,9},{5... | collective-permute-start | bytes 196616 | tf_op jit(solution)/shard_map/ppermute | solution.py:55
  16.7 0.6 %collective-permute-start.6 = (bf16[128,256]{1,0:T(8,128)(2,1)S(1)}, bf16[128,256]{1,0:T(8,128)(2,1)S(1)}, u32[]{:S(2)}, u32[]{:S(2)}) collective-permute-start(bf16[128,256]{1,0:T(8,128)(2,1)S(1)} %shard_map.116.refs_0_), channel_id=1, source_target_pairs={{0,16},{4,20},{8,24},{12,28},{16,0},{20,4},{24,8},{28,12},{1,17},{... | collective-permute-start | bytes 196616 | tf_op jit(solution)/shard_map/ppermute | solution.py:55
  17.3 1.8 %collective-permute-done.4.refs_0_ = bf16[128,256]{1,0:T(8,128)(2,1)S(1)} collective-permute-done((bf16[128,256]{1,0:T(8,128)(2,1)S(1)}, bf16[128,256]{1,0:T(8,128)(2,1)S(1)}, u32[]{:S(2)}, u32[]{:S(2)}) %collective-permute-start.4) | collective-permute-done | bytes 65568 | tf_op jit(solution)/shard_map/ppermute | solution.py:55
  19.1 1.3 %collective-permute-done.5.refs_1_ = bf16[128,256]{1,0:T(8,128)(2,1)S(1)} collective-permute-done((bf16[128,256]{1,0:T(8,128)(2,1)S(1)}, bf16[128,256]{1,0:T(8,128)(2,1)S(1)}, u32[]{:S(2)}, u32[]{:S(2)}) %collective-permute-start.5) | collective-permute-done | bytes 65568 | tf_op jit(solution)/shard_map/ppermute | solution.py:55
  20.4 0.6 %collective-permute-done.6.refs_2_ = bf16[128,256]{1,0:T(8,128)(2,1)S(1)} collective-permute-done((bf16[128,256]{1,0:T(8,128)(2,1)S(1)}, bf16[128,256]{1,0:T(8,128)(2,1)S(1)}, u32[]{:S(2)}, u32[]{:S(2)}) %collective-permute-start.6) | collective-permute-done | bytes 65568 | tf_op jit(solution)/shard_map/ppermute | solution.py:55
  21.7 1.5 %collective-permute-start.8 = (bf16[128,256]{1,0:T(8,128)(2,1)S(1)}, bf16[128,256]{1,0:T(8,128)(2,1)S(1)}, u32[]{:S(2)}, u32[]{:S(2)}) collective-permute-start(bf16[128,256]{1,0:T(8,128)(2,1)S(1)} %get-tuple-element.23.grad_ref.refs_3_), channel_id=1, source_target_pairs={{0,24},{4,28},{8,16},{12,20},{16,8},{20,12},{24,0},{28,4},{1,25},{... | collective-permute-start | bytes 196616 | tf_op jit(solution)/shard_map/ppermute | solution.py:55
  23.2 0.5 %collective-permute-start.9 = (bf16[128,256]{1,0:T(8,128)(2,1)S(1)}, bf16[128,256]{1,0:T(8,128)(2,1)S(1)}, u32[]{:S(2)}, u32[]{:S(2)}) collective-permute-start(bf16[128,256]{1,0:T(8,128)(2,1)S(1)} %get-tuple-element.23.grad_ref.refs_3_), channel_id=1, source_target_pairs={{0,8},{4,12},{8,0},{12,4},{16,24},{20,28},{24,16},{28,20},{1,9},{5... | collective-permute-start | bytes 196616 | tf_op jit(solution)/shard_map/ppermute | solution.py:55
  23.7 1.5 %collective-permute-start.10 = (bf16[128,256]{1,0:T(8,128)(2,1)S(1)}, bf16[128,256]{1,0:T(8,128)(2,1)S(1)}, u32[]{:S(2)}, u32[]{:S(2)}) collective-permute-start(bf16[128,256]{1,0:T(8,128)(2,1)S(1)} %get-tuple-element.23.grad_ref.refs_3_), channel_id=1, source_target_pairs={{0,16},{4,20},{8,24},{12,28},{16,0},{20,4},{24,8},{28,12},{1,17},{... | collective-permute-start | bytes 196616 | tf_op jit(solution)/shard_map/ppermute | solution.py:55
  25.3 2.2 %collective-permute-start.15 = (bf16[144,256]{1,0:T(8,128)(2,1)S(1)}, bf16[144,256]{1,0:T(8,128)(2,1)S(1)}, u32[]{:S(2)}, u32[]{:S(2)}) collective-permute-start(bf16[144,256]{1,0:T(8,128)(2,1)S(1)} %shard_map.122.after_ref.refs_3_), channel_id=1, source_target_pairs={{0,3},{1,2},{2,1},{3,0},{4,7},{5,6},{6,5},{7,4},{8,11},{9,10},{10,... | collective-permute-start | bytes 221192 | tf_op jit(solution)/shard_map/ppermute | solution.py:55
  27.8 1.9 %collective-permute-start.17 = (bf16[144,256]{1,0:T(8,128)(2,1)S(1)}, bf16[144,256]{1,0:T(8,128)(2,1)S(1)}, u32[]{:S(2)}, u32[]{:S(2)}) collective-permute-start(bf16[144,256]{1,0:T(8,128)(2,1)S(1)} %shard_map.122.after_ref.refs_3_), channel_id=1, source_target_pairs={{0,2},{1,3},{2,0},{3,1},{4,6},{5,7},{6,4},{7,5},{8,10},{9,11},{10,... | collective-permute-start | bytes 221192 | tf_op jit(solution)/shard_map/ppermute | solution.py:55
  30.5 1.5 %collective-permute-done.15.refs_0_ = bf16[144,256]{1,0:T(8,128)(2,1)S(1)} collective-permute-done((bf16[144,256]{1,0:T(8,128)(2,1)S(1)}, bf16[144,256]{1,0:T(8,128)(2,1)S(1)}, u32[]{:S(2)}, u32[]{:S(2)}) %collective-permute-start.15) | collective-permute-done | bytes 73760 | tf_op jit(solution)/shard_map/ppermute | solution.py:55
  32.0 1.0 %collective-permute-done.16.refs_1_ = bf16[144,256]{1,0:T(8,128)(2,1)S(1)} collective-permute-done((bf16[144,256]{1,0:T(8,128)(2,1)S(1)}, bf16[144,256]{1,0:T(8,128)(2,1)S(1)}, u32[]{:S(2)}, u32[]{:S(2)}) %collective-permute-start.16) | collective-permute-done | bytes 73760 | tf_op jit(solution)/shard_map/ppermute | solution.py:55
  33.0 1.8 %collective-permute-done.17.refs_2_ = bf16[144,256]{1,0:T(8,128)(2,1)S(1)} collective-permute-done((bf16[144,256]{1,0:T(8,128)(2,1)S(1)}, bf16[144,256]{1,0:T(8,128)(2,1)S(1)}, u32[]{:S(2)}, u32[]{:S(2)}) %collective-permute-start.17) | collective-permute-done | bytes 73760 | tf_op jit(solution)/shard_map/ppermute | solution.py:55
  34.9 1.6 %collective-permute-start.18 = (bf16[144,256]{1,0:T(8,128)(2,1)S(1)}, bf16[144,256]{1,0:T(8,128)(2,1)S(1)}, u32[]{:S(2)}, u32[]{:S(2)}) collective-permute-start(bf16[144,256]{1,0:T(8,128)(2,1)S(1)} %shard_map.130.refs_1_), channel_id=1, source_target_pairs={{0,8},{4,12},{8,0},{12,4},{16,24},{20,28},{24,16},{28,20},{1,9},{5... | collective-permute-start | bytes 221192 | tf_op jit(solution)/shard_map/ppermute | solution.py:70
  36.6 2.2 %collective-permute-start.12 = (bf16[128,256]{1,0:T(8,128)(2,1)S(1)}, bf16[128,256]{1,0:T(8,128)(2,1)S(1)}, u32[]{:S(2)}, u32[]{:S(2)}) collective-permute-start(bf16[128,256]{1,0:T(8,128)(2,1)S(1)} %shard_map.125.refs_0_), channel_id=1, source_target_pairs={{0,3},{1,2},{2,1},{3,0},{4,7},{5,6},{6,5},{7,4},{8,11},{9,10},{10,... | collective-permute-start | bytes 196616 | tf_op jit(solution)/shard_map/ppermute | solution.py:55
  39.3 2.3 %collective-permute-start.14 = (bf16[128,256]{1,0:T(8,128)(2,1)S(1)}, bf16[128,256]{1,0:T(8,128)(2,1)S(1)}, u32[]{:S(2)}, u32[]{:S(2)}) collective-permute-start(bf16[128,256]{1,0:T(8,128)(2,1)S(1)} %shard_map.127.refs_0_), channel_id=1, source_target_pairs={{0,2},{1,3},{2,0},{3,1},{4,6},{5,7},{6,4},{7,5},{8,10},{9,11},{10,... | collective-permute-start | bytes 196616 | tf_op jit(solution)/shard_map/ppermute | solution.py:55
  41.7 0.6 %collective-permute-start.19 = (bf16[144,256]{1,0:T(8,128)(2,1)S(1)}, bf16[144,256]{1,0:T(8,128)(2,1)S(1)}, u32[]{:S(2)}, u32[]{:S(2)}) collective-permute-start(bf16[144,256]{1,0:T(8,128)(2,1)S(1)} %shard_map.131.refs_1_), channel_id=1, source_target_pairs={{0,16},{4,20},{8,24},{12,28},{16,0},{20,4},{24,8},{28,12},{1,17},{... | collective-permute-start | bytes 221192 | tf_op jit(solution)/shard_map/ppermute | solution.py:70
  42.4 0.9 %collective-permute-done.12.refs_0_ = bf16[128,256]{1,0:T(8,128)(2,1)S(1)} collective-permute-done((bf16[128,256]{1,0:T(8,128)(2,1)S(1)}, bf16[128,256]{1,0:T(8,128)(2,1)S(1)}, u32[]{:S(2)}, u32[]{:S(2)}) %collective-permute-start.12) | collective-permute-done | bytes 65568 | tf_op jit(solution)/shard_map/ppermute | solution.py:55
  43.7 0.8 %collective-permute-done.14.refs_2_ = bf16[128,256]{1,0:T(8,128)(2,1)S(1)} collective-permute-done((bf16[128,256]{1,0:T(8,128)(2,1)S(1)}, bf16[128,256]{1,0:T(8,128)(2,1)S(1)}, u32[]{:S(2)}, u32[]{:S(2)}) %collective-permute-start.14) | collective-permute-done | bytes 65568 | tf_op jit(solution)/shard_map/ppermute | solution.py:55
  44.6 0.8 %shard_map.129.after_ref = bf16[128,256]{1,0:T(8,128)(2,1)} custom-call(bf16[256,256]{1,0:T(8,128)(2,1)S(1)} %copy-done, bf16[128,256]{1,0:T(8,128)(2,1)S(1)} %collective-permute-done.12.refs_0_, bf16[128,256]{1,0:T(8,128)(2,1)S(1)} %collective-permute-done.13.refs_1_, bf16[128,256]{1,0:T(8,128)(2,1)S(1)} %collective-permute-done.14.refs_2_, ...), custom_call_target="tpu_custom_call" | custom-call | flops 2516582400 | bytes 262144 | tf_op jit(solution)/shard_map/pallas_call | solution.py:480
  45.4 0.7 %collective-permute-done.19.refs_0_ = bf16[144,256]{1,0:T(8,128)(2,1)S(1)} collective-permute-done((bf16[144,256]{1,0:T(8,128)(2,1)S(1)}, bf16[144,256]{1,0:T(8,128)(2,1)S(1)}, u32[]{:S(2)}, u32[]{:S(2)}) %collective-permute-start.19) | collective-permute-done | bytes 73760 | tf_op jit(solution)/shard_map/ppermute | solution.py:70
  46.2 0.6 %shard_map.119 = bf16[128,256]{1,0:T(8,128)(2,1)} custom-call(bf16[128,256]{1,0:T(8,128)(2,1)S(1)} %get-tuple-element.21.in_ref), custom_call_target="tpu_custom_call" | custom-call | bytes 131072 | tf_op jit(solution)/shard_map/pallas_call | solution.py:427
  46.8 0.7 %collective-permute-done.20.other_ref = f32[128,256]{1,0:T(8,128)S(1)} collective-permute-done((f32[128,256]{1,0:T(8,128)S(1)}, f32[128,256]{1,0:T(8,128)S(1)}, u32[]{:S(2)}, u32[]{:S(2)}) %collective-permute-start.20) | collective-permute-done | bytes 131104 | tf_op jit(solution)/shard_map/ppermute | solution.py:60
  47.5 0.7 %shard_map.133 = (f32[256,256]{1,0:T(8,128)}, f32[1,256]{1,0:T(1,128)}) custom-call(f32[128,256]{1,0:T(8,128)S(1)} %get-tuple-element.26.own_ref, f32[128,256]{1,0:T(8,128)S(1)} %collective-permute-done.20.other_ref, f32[1,256]{1,0:T(1,128)S(1)} %get-tuple-element.27.bias_ref), custom_call_target="tpu_custom_call" | custom-call | bytes 524288 | tf_op jit(solution)/shard_map/pallas_call | solution.py:499
  (39 shorter events, 3.9 us)
Async XLA Ops:
  0.6 8.2 %collective-permute-start = (bf16[128,256]{1,0:T(8,128)(2,1)}, bf16[128,256]{1,0:T(8,128)(2,1)S(1)}, u32[]{:S(2)}, u32[]{:S(2)}) collective-permute-start(bf16[128,256]{1,0:T(8,128)(2,1)} %refs_3_.1), channel_id=1, source_target_pairs={{0,3},{1,2},{2,1},{3,0},{4,7},{5,6},{6,5},{7,4},{8,11},{9,10},{10,... | collective-permute-start | bytes 196616 | tf_op jit(solution)/shard_map/ppermute | solution.py:55
  5.7 4.9 %collective-permute-start.1 = (bf16[128,256]{1,0:T(8,128)(2,1)}, bf16[128,256]{1,0:T(8,128)(2,1)S(1)}, u32[]{:S(2)}, u32[]{:S(2)}) collective-permute-start(bf16[128,256]{1,0:T(8,128)(2,1)} %refs_3_.1), channel_id=1, source_target_pairs={{0,1},{1,0},{2,3},{3,2},{4,5},{5,4},{6,7},{7,6},{8,9},{9,8},{10,11... | collective-permute-start | bytes 196616 | tf_op jit(solution)/shard_map/ppermute | solution.py:55
  5.8 5.8 %collective-permute-start.2 = (bf16[128,256]{1,0:T(8,128)(2,1)}, bf16[128,256]{1,0:T(8,128)(2,1)S(1)}, u32[]{:S(2)}, u32[]{:S(2)}) collective-permute-start(bf16[128,256]{1,0:T(8,128)(2,1)} %refs_3_.1), channel_id=1, source_target_pairs={{0,2},{1,3},{2,0},{3,1},{4,6},{5,7},{6,4},{7,5},{8,10},{9,11},{10,... | collective-permute-start | bytes 196616 | tf_op jit(solution)/shard_map/ppermute | solution.py:55
  7.0 4.6 %copy-start.1 = (bf16[128,256]{1,0:T(8,128)(2,1)S(1)}, bf16[128,256]{1,0:T(8,128)(2,1)}, u32[]{:S(2)}) copy-start(bf16[128,256]{1,0:T(8,128)(2,1)} %refs_3_.1) | copy-start | bytes 196612
  11.9 1.6 %collective-permute-start.3 = (bf16[512,256]{1,0:T(8,128)(2,1)S(1)}, bf16[512,256]{1,0:T(8,128)(2,1)S(1)}, u32[]{:S(2)}, u32[]{:S(2)}) collective-permute-start(bf16[512,256]{1,0:T(8,128)(2,1)S(1)} %get-tuple-element.20), channel_id=1, source_target_pairs={{0,4},{4,0},{8,12},{12,8},{16,20},{20,16},{24,28},{28,24},{1,5},{5... | collective-permute-start | bytes 786440 | tf_op jit(solution)/shard_map/ppermute | solution.py:60
  13.5 5.5 %collective-permute-start.4 = (bf16[128,256]{1,0:T(8,128)(2,1)S(1)}, bf16[128,256]{1,0:T(8,128)(2,1)S(1)}, u32[]{:S(2)}, u32[]{:S(2)}) collective-permute-start(bf16[128,256]{1,0:T(8,128)(2,1)S(1)} %shard_map.114.refs_0_), channel_id=1, source_target_pairs={{0,24},{4,28},{8,16},{12,20},{16,8},{20,12},{24,0},{28,4},{1,25},{... | collective-permute-start | bytes 196616 | tf_op jit(solution)/shard_map/ppermute | solution.py:55
  16.1 4.3 %collective-permute-start.5 = (bf16[128,256]{1,0:T(8,128)(2,1)S(1)}, bf16[128,256]{1,0:T(8,128)(2,1)S(1)}, u32[]{:S(2)}, u32[]{:S(2)}) collective-permute-start(bf16[128,256]{1,0:T(8,128)(2,1)S(1)} %shard_map.115.refs_0_), channel_id=1, source_target_pairs={{0,8},{4,12},{8,0},{12,4},{16,24},{20,28},{24,16},{28,20},{1,9},{5... | collective-permute-start | bytes 196616 | tf_op jit(solution)/shard_map/ppermute | solution.py:55
  16.7 4.4 %copy-start = (bf16[256,256]{1,0:T(8,128)(2,1)S(1)}, bf16[256,256]{1,0:T(8,128)(2,1)}, u32[]{:S(2)}) copy-start(bf16[256,256]{1,0:T(8,128)(2,1)} %weight_ref.3) | copy-start | bytes 393220
  16.7 4.3 %copy-start.2 = (bf16[128,256]{1,0:T(8,128)(2,1)S(1)}, bf16[128,256]{1,0:T(8,128)(2,1)}, u32[]{:S(2)}) copy-start(bf16[128,256]{1,0:T(8,128)(2,1)} %cot_ref.1) | copy-start | bytes 196612
  16.7 4.3 %collective-permute-start.6 = (bf16[128,256]{1,0:T(8,128)(2,1)S(1)}, bf16[128,256]{1,0:T(8,128)(2,1)S(1)}, u32[]{:S(2)}, u32[]{:S(2)}) collective-permute-start(bf16[128,256]{1,0:T(8,128)(2,1)S(1)} %shard_map.116.refs_0_), channel_id=1, source_target_pairs={{0,16},{4,20},{8,24},{12,28},{16,0},{20,4},{24,8},{28,12},{1,17},{... | collective-permute-start | bytes 196616 | tf_op jit(solution)/shard_map/ppermute | solution.py:55
  21.6 3.6 %collective-permute-start.7 = (bf16[144,256]{1,0:T(8,128)(2,1)S(1)}, bf16[144,256]{1,0:T(8,128)(2,1)S(1)}, u32[]{:S(2)}, u32[]{:S(2)}) collective-permute-start(bf16[144,256]{1,0:T(8,128)(2,1)S(1)} %get-tuple-element.24), channel_id=1, source_target_pairs={{0,4},{4,0},{8,12},{12,8},{16,20},{20,16},{24,28},{28,24},{1,5},{5... | collective-permute-start | bytes 221192 | tf_op jit(solution)/shard_map/ppermute | solution.py:60
  21.7 6.2 %collective-permute-start.8 = (bf16[128,256]{1,0:T(8,128)(2,1)S(1)}, bf16[128,256]{1,0:T(8,128)(2,1)S(1)}, u32[]{:S(2)}, u32[]{:S(2)}) collective-permute-start(bf16[128,256]{1,0:T(8,128)(2,1)S(1)} %get-tuple-element.23.grad_ref.refs_3_), channel_id=1, source_target_pairs={{0,24},{4,28},{8,16},{12,20},{16,8},{20,12},{24,0},{28,4},{1,25},{... | collective-permute-start | bytes 196616 | tf_op jit(solution)/shard_map/ppermute | solution.py:55
  23.2 6.9 %collective-permute-start.9 = (bf16[128,256]{1,0:T(8,128)(2,1)S(1)}, bf16[128,256]{1,0:T(8,128)(2,1)S(1)}, u32[]{:S(2)}, u32[]{:S(2)}) collective-permute-start(bf16[128,256]{1,0:T(8,128)(2,1)S(1)} %get-tuple-element.23.grad_ref.refs_3_), channel_id=1, source_target_pairs={{0,8},{4,12},{8,0},{12,4},{16,24},{20,28},{24,16},{28,20},{1,9},{5... | collective-permute-start | bytes 196616 | tf_op jit(solution)/shard_map/ppermute | solution.py:55
  23.7 6.4 %collective-permute-start.10 = (bf16[128,256]{1,0:T(8,128)(2,1)S(1)}, bf16[128,256]{1,0:T(8,128)(2,1)S(1)}, u32[]{:S(2)}, u32[]{:S(2)}) collective-permute-start(bf16[128,256]{1,0:T(8,128)(2,1)S(1)} %get-tuple-element.23.grad_ref.refs_3_), channel_id=1, source_target_pairs={{0,16},{4,20},{8,24},{12,28},{16,0},{20,4},{24,8},{28,12},{1,17},{... | collective-permute-start | bytes 196616 | tf_op jit(solution)/shard_map/ppermute | solution.py:55
  25.3 6.8 %collective-permute-start.15 = (bf16[144,256]{1,0:T(8,128)(2,1)S(1)}, bf16[144,256]{1,0:T(8,128)(2,1)S(1)}, u32[]{:S(2)}, u32[]{:S(2)}) collective-permute-start(bf16[144,256]{1,0:T(8,128)(2,1)S(1)} %shard_map.122.after_ref.refs_3_), channel_id=1, source_target_pairs={{0,3},{1,2},{2,1},{3,0},{4,7},{5,6},{6,5},{7,4},{8,11},{9,10},{10,... | collective-permute-start | bytes 221192 | tf_op jit(solution)/shard_map/ppermute | solution.py:55
  27.5 5.5 %collective-permute-start.16 = (bf16[144,256]{1,0:T(8,128)(2,1)S(1)}, bf16[144,256]{1,0:T(8,128)(2,1)S(1)}, u32[]{:S(2)}, u32[]{:S(2)}) collective-permute-start(bf16[144,256]{1,0:T(8,128)(2,1)S(1)} %shard_map.122.after_ref.refs_3_), channel_id=1, source_target_pairs={{0,1},{1,0},{2,3},{3,2},{4,5},{5,4},{6,7},{7,6},{8,9},{9,8},{10,11... | collective-permute-start | bytes 221192 | tf_op jit(solution)/shard_map/ppermute | solution.py:55
  27.8 7.0 %collective-permute-start.17 = (bf16[144,256]{1,0:T(8,128)(2,1)S(1)}, bf16[144,256]{1,0:T(8,128)(2,1)S(1)}, u32[]{:S(2)}, u32[]{:S(2)}) collective-permute-start(bf16[144,256]{1,0:T(8,128)(2,1)S(1)} %shard_map.122.after_ref.refs_3_), channel_id=1, source_target_pairs={{0,2},{1,3},{2,0},{3,1},{4,6},{5,7},{6,4},{7,5},{8,10},{9,11},{10,... | collective-permute-start | bytes 221192 | tf_op jit(solution)/shard_map/ppermute | solution.py:55
  30.1 6.3 %collective-permute-start.11 = (bf16[512,256]{1,0:T(8,128)(2,1)S(1)}, bf16[512,256]{1,0:T(8,128)(2,1)S(1)}, u32[]{:S(2)}, u32[]{:S(2)}) collective-permute-start(bf16[512,256]{1,0:T(8,128)(2,1)S(1)} %shard_map.123.source_ref), channel_id=1, source_target_pairs={{0,4},{4,0},{8,12},{12,8},{16,20},{20,16},{24,28},{28,24},{1,5},{5... | collective-permute-start | bytes 786440 | tf_op jit(solution)/shard_map/ppermute | solution.py:60
  34.9 6.7 %collective-permute-start.18 = (bf16[144,256]{1,0:T(8,128)(2,1)S(1)}, bf16[144,256]{1,0:T(8,128)(2,1)S(1)}, u32[]{:S(2)}, u32[]{:S(2)}) collective-permute-start(bf16[144,256]{1,0:T(8,128)(2,1)S(1)} %shard_map.130.refs_1_), channel_id=1, source_target_pairs={{0,8},{4,12},{8,0},{12,4},{16,24},{20,28},{24,16},{28,20},{1,9},{5... | collective-permute-start | bytes 221192 | tf_op jit(solution)/shard_map/ppermute | solution.py:70
  36.6 6.7 %collective-permute-start.12 = (bf16[128,256]{1,0:T(8,128)(2,1)S(1)}, bf16[128,256]{1,0:T(8,128)(2,1)S(1)}, u32[]{:S(2)}, u32[]{:S(2)}) collective-permute-start(bf16[128,256]{1,0:T(8,128)(2,1)S(1)} %shard_map.125.refs_0_), channel_id=1, source_target_pairs={{0,3},{1,2},{2,1},{3,0},{4,7},{5,6},{6,5},{7,4},{8,11},{9,10},{10,... | collective-permute-start | bytes 196616 | tf_op jit(solution)/shard_map/ppermute | solution.py:55
  39.1 4.7 %collective-permute-start.13 = (bf16[128,256]{1,0:T(8,128)(2,1)S(1)}, bf16[128,256]{1,0:T(8,128)(2,1)S(1)}, u32[]{:S(2)}, u32[]{:S(2)}) collective-permute-start(bf16[128,256]{1,0:T(8,128)(2,1)S(1)} %shard_map.126.refs_0_), channel_id=1, source_target_pairs={{0,1},{1,0},{2,3},{3,2},{4,5},{5,4},{6,7},{7,6},{8,9},{9,8},{10,11... | collective-permute-start | bytes 196616 | tf_op jit(solution)/shard_map/ppermute | solution.py:55
  39.3 5.2 %collective-permute-start.14 = (bf16[128,256]{1,0:T(8,128)(2,1)S(1)}, bf16[128,256]{1,0:T(8,128)(2,1)S(1)}, u32[]{:S(2)}, u32[]{:S(2)}) collective-permute-start(bf16[128,256]{1,0:T(8,128)(2,1)S(1)} %shard_map.127.refs_0_), channel_id=1, source_target_pairs={{0,2},{1,3},{2,0},{3,1},{4,6},{5,7},{6,4},{7,5},{8,10},{9,11},{10,... | collective-permute-start | bytes 196616 | tf_op jit(solution)/shard_map/ppermute | solution.py:55
  41.7 4.4 %collective-permute-start.19 = (bf16[144,256]{1,0:T(8,128)(2,1)S(1)}, bf16[144,256]{1,0:T(8,128)(2,1)S(1)}, u32[]{:S(2)}, u32[]{:S(2)}) collective-permute-start(bf16[144,256]{1,0:T(8,128)(2,1)S(1)} %shard_map.131.refs_1_), channel_id=1, source_target_pairs={{0,16},{4,20},{8,24},{12,28},{16,0},{20,4},{24,8},{28,12},{1,17},{... | collective-permute-start | bytes 221192 | tf_op jit(solution)/shard_map/ppermute | solution.py:70
  46.1 1.4 %collective-permute-start.20 = (f32[128,256]{1,0:T(8,128)S(1)}, f32[128,256]{1,0:T(8,128)S(1)}, u32[]{:S(2)}, u32[]{:S(2)}) collective-permute-start(f32[128,256]{1,0:T(8,128)S(1)} %get-tuple-element.26.own_ref), channel_id=1, source_target_pairs={{0,4},{4,0},{8,12},{12,8},{16,20},{20,16},{24,28},{28,24},{1,5},{5... | collective-permute-start | bytes 393224 | tf_op jit(solution)/shard_map/ppermute | solution.py:60

commit v8 on v7

--- a/solution.py
+++ b/solution.py
@@ -434,7 +434,8 @@
         6 * block_bytes,
     )(aggregated, grad)
     chip_term = add([swap_cores(theirs, n_col), mine])
-    row_term = add(exchange([chip_term] * n_row, "row", n_row), flops=ROW_SUM_WEIGHT * matrix)
+    add_late = functools.partial(add, flops=ROW_SUM_WEIGHT * matrix)
+    row_term = add_late(total_over(chip_term, add, "row", n_row))
 
     own_grads = call(
         gather_kernel,

time: 48.4 us -> 47.8 us (0.988)
  starting transfers between devices: 24.4 us -> 22.9 us
  waiting for transfers between devices: 16 us -> 16.6 us
    ppermute x15 -> x12, starting transfers between devices: 22 us -> 17.5 us  [exchange(): lax.ppermute(blocks[k], axis, pairs)]
    ppermute x15 -> x12, waiting for transfers between devices: 13.4 us -> 9.62 us  [exchange(): lax.ppermute(blocks[k], axis, pairs)]
    ppermute x2 -> x4, waiting for transfers between devices: 0.66 us -> 3.84 us  [total_over(): terms = [lax.ppermute(block, axis, pairs_of(step, size, cores)), block]]
    ppermute x2 -> x4, starting transfers between devices: 2.14 us -> 5.08 us  [total_over(): terms = [lax.ppermute(block, axis, pairs_of(step, size, cores)), block]]
    ppermute x4, waiting for transfers between devices: 1.93 us -> 3.18 us  [swap_cores(): return lax.ppermute(block, 'col', [(i, i ^ 1) for i in range(size)])]
  transfers between devices with their start and end apart: 21 -> 20, of which waited for: 15 -> 16; matrix products, arithmetic and copies ran while one was open for 0% -> 0% of each run, Pallas kernels for 10% -> 10%
where the time goes in v8:
time: 47.8 us; the launch traced here: 47.6 us
  starting transfers between devices  22.9 us (48%)
  waiting for transfers between devices  16.6 us (35%)
  Pallas kernels  6.6 us (14%)
  between operations  1.47 us (3%)
    ppermute x12, starting transfers between devices, exchange(): lax.ppermute(blocks[k], axis, pairs)  17.5 us
    ppermute x12, waiting for transfers between devices, exchange(): lax.ppermute(blocks[k], axis, pairs)  9.62 us
    ppermute x4, starting transfers between devices, total_over(): terms = [lax.ppermute(block, axis, pairs_of(step, size, cores)), block]  5.08 us
    ppermute x4, waiting for transfers between devices, total_over(): terms = [lax.ppermute(block, axis, pairs_of(step, size, cores)), block]  3.84 us
    ppermute x4, waiting for transfers between devices, swap_cores(): return lax.ppermute(block, 'col', [(i, i ^ 1) for i in range(size)])  3.18 us
    pallas_call x1, Pallas kernels, local(): call(dense_kernel, (like(row_nodes, col_nodes), like(1, hidden, F32)), [S...  1.64 us
  transfers between devices with their start and end apart: 20, of which 16 were waited for; matrix products, arithmetic and copies ran while one was open for 0% of the time, Pallas kernels for 10%

profile of v8, /device:TPU:0, one launch (start us, length us, event | category | flops | bytes accessed | tf_op | source)
XLA Modules:
  0.0 47.6 jit_solution(1238694651049211915)
XLA Ops:
  0.6 5.1 %collective-permute-start = (bf16[128,256]{1,0:T(8,128)(2,1)}, bf16[128,256]{1,0:T(8,128)(2,1)S(1)}, u32[]{:S(2)}, u32[]{:S(2)}) collective-permute-start(bf16[128,256]{1,0:T(8,128)(2,1)} %refs_3_.1), channel_id=1, source_target_pairs={{0,3},{1,2},{2,1},{3,0},{4,7},{5,6},{6,5},{7,4},{8,11},{9,10},{10,... | collective-permute-start | bytes 196616 | tf_op jit(solution)/shard_map/ppermute | solution.py:55
  5.8 0.6 %collective-permute-start.2 = (bf16[128,256]{1,0:T(8,128)(2,1)}, bf16[128,256]{1,0:T(8,128)(2,1)S(1)}, u32[]{:S(2)}, u32[]{:S(2)}) collective-permute-start(bf16[128,256]{1,0:T(8,128)(2,1)} %refs_3_.1), channel_id=1, source_target_pairs={{0,2},{1,3},{2,0},{3,1},{4,6},{5,7},{6,4},{7,5},{8,10},{9,11},{10,... | collective-permute-start | bytes 196616 | tf_op jit(solution)/shard_map/ppermute | solution.py:55
  7.1 1.6 %shard_map.111 = (bf16[1024,512]{1,0:T(8,128)(2,1)S(1)}, f32[1,256]{1,0:T(1,128)S(1)}) custom-call(s32[1,1]{1,0:T(1,128)S(6)} %copy.12.count_ref, s32[1,1,32]{2,1,0:T(1,128)} %row_hbm.1, s32[1,1,32]{2,1,0:T(1,128)} %col_hbm.1, bf16[1,1,32,128,128]{4,3,2,1,0:T(8,128)(2,1)} %tiles_hbm.1, f32[1,256]{1,0:T(1,128)} %bitcast.2), custom_call_target="tpu_custom_call" | custom-call | bytes 6291456 | tf_op jit(solution)/shard_map/pallas_call | solution.py:341
  8.9 1.8 %collective-permute-done.1.refs_1_ = bf16[128,256]{1,0:T(8,128)(2,1)S(1)} collective-permute-done((bf16[128,256]{1,0:T(8,128)(2,1)}, bf16[128,256]{1,0:T(8,128)(2,1)S(1)}, u32[]{:S(2)}, u32[]{:S(2)}) %collective-permute-start.1) | collective-permute-done | bytes 65568 | tf_op jit(solution)/shard_map/ppermute | solution.py:55
  10.6 1.0 %collective-permute-done.2.refs_2_ = bf16[128,256]{1,0:T(8,128)(2,1)S(1)} collective-permute-done((bf16[128,256]{1,0:T(8,128)(2,1)}, bf16[128,256]{1,0:T(8,128)(2,1)S(1)}, u32[]{:S(2)}, u32[]{:S(2)}) %collective-permute-start.2) | collective-permute-done | bytes 65568 | tf_op jit(solution)/shard_map/ppermute | solution.py:55
  12.3 1.2 %collective-permute-done.3.other_ref = bf16[512,256]{1,0:T(8,128)(2,1)S(1)} collective-permute-done((bf16[512,256]{1,0:T(8,128)(2,1)S(1)}, bf16[512,256]{1,0:T(8,128)(2,1)S(1)}, u32[]{:S(2)}, u32[]{:S(2)}) %collective-permute-start.3) | collective-permute-done | bytes 262176 | tf_op jit(solution)/shard_map/ppermute | solution.py:60
  13.5 2.5 %collective-permute-start.4 = (bf16[128,256]{1,0:T(8,128)(2,1)S(1)}, bf16[128,256]{1,0:T(8,128)(2,1)S(1)}, u32[]{:S(2)}, u32[]{:S(2)}) collective-permute-start(bf16[128,256]{1,0:T(8,128)(2,1)S(1)} %shard_map.114.refs_0_), channel_id=1, source_target_pairs={{0,24},{4,28},{8,16},{12,20},{16,8},{20,12},{24,0},{28,4},{1,25},{... | collective-permute-start | bytes 196616 | tf_op jit(solution)/shard_map/ppermute | solution.py:55
  16.1 0.6 %collective-permute-start.5 = (bf16[128,256]{1,0:T(8,128)(2,1)S(1)}, bf16[128,256]{1,0:T(8,128)(2,1)S(1)}, u32[]{:S(2)}, u32[]{:S(2)}) collective-permute-start(bf16[128,256]{1,0:T(8,128)(2,1)S(1)} %shard_map.115.refs_0_), channel_id=1, source_target_pairs={{0,8},{4,12},{8,0},{12,4},{16,24},{20,28},{24,16},{28,20},{1,9},{5... | collective-permute-start | bytes 196616 | tf_op jit(solution)/shard_map/ppermute | solution.py:55
  16.7 0.6 %collective-permute-start.6 = (bf16[128,256]{1,0:T(8,128)(2,1)S(1)}, bf16[128,256]{1,0:T(8,128)(2,1)S(1)}, u32[]{:S(2)}, u32[]{:S(2)}) collective-permute-start(bf16[128,256]{1,0:T(8,128)(2,1)S(1)} %shard_map.116.refs_0_), channel_id=1, source_target_pairs={{0,16},{4,20},{8,24},{12,28},{16,0},{20,4},{24,8},{28,12},{1,17},{... | collective-permute-start | bytes 196616 | tf_op jit(solution)/shard_map/ppermute | solution.py:55
  17.3 1.8 %collective-permute-done.4.refs_0_ = bf16[128,256]{1,0:T(8,128)(2,1)S(1)} collective-permute-done((bf16[128,256]{1,0:T(8,128)(2,1)S(1)}, bf16[128,256]{1,0:T(8,128)(2,1)S(1)}, u32[]{:S(2)}, u32[]{:S(2)}) %collective-permute-start.4) | collective-permute-done | bytes 65568 | tf_op jit(solution)/shard_map/ppermute | solution.py:55
  19.1 1.3 %collective-permute-done.5.refs_1_ = bf16[128,256]{1,0:T(8,128)(2,1)S(1)} collective-permute-done((bf16[128,256]{1,0:T(8,128)(2,1)S(1)}, bf16[128,256]{1,0:T(8,128)(2,1)S(1)}, u32[]{:S(2)}, u32[]{:S(2)}) %collective-permute-start.5) | collective-permute-done | bytes 65568 | tf_op jit(solution)/shard_map/ppermute | solution.py:55
  20.4 0.6 %collective-permute-done.6.refs_2_ = bf16[128,256]{1,0:T(8,128)(2,1)S(1)} collective-permute-done((bf16[128,256]{1,0:T(8,128)(2,1)S(1)}, bf16[128,256]{1,0:T(8,128)(2,1)S(1)}, u32[]{:S(2)}, u32[]{:S(2)}) %collective-permute-start.6) | collective-permute-done | bytes 65568 | tf_op jit(solution)/shard_map/ppermute | solution.py:55
  21.7 1.3 %collective-permute-done.7.refs_0_ = bf16[144,256]{1,0:T(8,128)(2,1)S(1)} collective-permute-done((bf16[144,256]{1,0:T(8,128)(2,1)S(1)}, bf16[144,256]{1,0:T(8,128)(2,1)S(1)}, u32[]{:S(2)}, u32[]{:S(2)}) %collective-permute-start.7) | collective-permute-done | bytes 73760 | tf_op jit(solution)/shard_map/ppermute | solution.py:60
  23.0 1.6 %collective-permute-start.15 = (bf16[144,256]{1,0:T(8,128)(2,1)S(1)}, bf16[144,256]{1,0:T(8,128)(2,1)S(1)}, u32[]{:S(2)}, u32[]{:S(2)}) collective-permute-start(bf16[144,256]{1,0:T(8,128)(2,1)S(1)} %shard_map.122.after_ref.refs_1_), channel_id=1, source_target_pairs={{0,1},{1,0},{2,3},{3,2},{4,5},{5,4},{6,7},{7,6},{8,9},{9,8},{10,11... | collective-permute-start | bytes 221192 | tf_op jit(solution)/shard_map/ppermute | solution.py:70
  24.6 1.4 %collective-permute-start.8 = (bf16[128,256]{1,0:T(8,128)(2,1)S(1)}, bf16[128,256]{1,0:T(8,128)(2,1)S(1)}, u32[]{:S(2)}, u32[]{:S(2)}) collective-permute-start(bf16[128,256]{1,0:T(8,128)(2,1)S(1)} %get-tuple-element.23.grad_ref.refs_3_), channel_id=1, source_target_pairs={{0,24},{4,28},{8,16},{12,20},{16,8},{20,12},{24,0},{28,4},{1,25},{... | collective-permute-start | bytes 196616 | tf_op jit(solution)/shard_map/ppermute | solution.py:55
  26.0 0.5 %collective-permute-start.9 = (bf16[128,256]{1,0:T(8,128)(2,1)S(1)}, bf16[128,256]{1,0:T(8,128)(2,1)S(1)}, u32[]{:S(2)}, u32[]{:S(2)}) collective-permute-start(bf16[128,256]{1,0:T(8,128)(2,1)S(1)} %get-tuple-element.23.grad_ref.refs_3_), channel_id=1, source_target_pairs={{0,8},{4,12},{8,0},{12,4},{16,24},{20,28},{24,16},{28,20},{1,9},{5... | collective-permute-start | bytes 196616 | tf_op jit(solution)/shard_map/ppermute | solution.py:55
  26.5 1.5 %collective-permute-start.10 = (bf16[128,256]{1,0:T(8,128)(2,1)S(1)}, bf16[128,256]{1,0:T(8,128)(2,1)S(1)}, u32[]{:S(2)}, u32[]{:S(2)}) collective-permute-start(bf16[128,256]{1,0:T(8,128)(2,1)S(1)} %get-tuple-element.23.grad_ref.refs_3_), channel_id=1, source_target_pairs={{0,16},{4,20},{8,24},{12,28},{16,0},{20,4},{24,8},{28,12},{1,17},{... | collective-permute-start | bytes 196616 | tf_op jit(solution)/shard_map/ppermute | solution.py:55
  28.1 1.3 %collective-permute-start.16 = (bf16[144,256]{1,0:T(8,128)(2,1)S(1)}, bf16[144,256]{1,0:T(8,128)(2,1)S(1)}, u32[]{:S(2)}, u32[]{:S(2)}) collective-permute-start(bf16[144,256]{1,0:T(8,128)(2,1)S(1)} %shard_map.130.refs_1_), channel_id=1, source_target_pairs={{0,2},{1,3},{2,0},{3,1},{4,6},{5,7},{6,4},{7,5},{8,10},{9,11},{10,... | collective-permute-start | bytes 221192 | tf_op jit(solution)/shard_map/ppermute | solution.py:70
  29.8 0.5 %collective-permute-done.8.refs_0_ = bf16[128,256]{1,0:T(8,128)(2,1)S(1)} collective-permute-done((bf16[128,256]{1,0:T(8,128)(2,1)S(1)}, bf16[128,256]{1,0:T(8,128)(2,1)S(1)}, u32[]{:S(2)}, u32[]{:S(2)}) %collective-permute-start.8) | collective-permute-done | bytes 65568 | tf_op jit(solution)/shard_map/ppermute | solution.py:55
  30.3 0.6 %collective-permute-done.10.refs_2_ = bf16[128,256]{1,0:T(8,128)(2,1)S(1)} collective-permute-done((bf16[128,256]{1,0:T(8,128)(2,1)S(1)}, bf16[128,256]{1,0:T(8,128)(2,1)S(1)}, u32[]{:S(2)}, u32[]{:S(2)}) %collective-permute-start.10) | collective-permute-done | bytes 65568 | tf_op jit(solution)/shard_map/ppermute | solution.py:55
  31.3 2.9 %collective-permute-done.16.refs_0_ = bf16[144,256]{1,0:T(8,128)(2,1)S(1)} collective-permute-done((bf16[144,256]{1,0:T(8,128)(2,1)S(1)}, bf16[144,256]{1,0:T(8,128)(2,1)S(1)}, u32[]{:S(2)}, u32[]{:S(2)}) %collective-permute-start.16) | collective-permute-done | bytes 73760 | tf_op jit(solution)/shard_map/ppermute | solution.py:70
  34.2 1.6 %collective-permute-start.17 = (bf16[144,256]{1,0:T(8,128)(2,1)S(1)}, bf16[144,256]{1,0:T(8,128)(2,1)S(1)}, u32[]{:S(2)}, u32[]{:S(2)}) collective-permute-start(bf16[144,256]{1,0:T(8,128)(2,1)S(1)} %shard_map.131.refs_1_), channel_id=1, source_target_pairs={{0,8},{4,12},{8,0},{12,4},{16,24},{20,28},{24,16},{28,20},{1,9},{5... | collective-permute-start | bytes 221192 | tf_op jit(solution)/shard_map/ppermute | solution.py:70
  36.0 1.9 %collective-permute-start.12 = (bf16[128,256]{1,0:T(8,128)(2,1)S(1)}, bf16[128,256]{1,0:T(8,128)(2,1)S(1)}, u32[]{:S(2)}, u32[]{:S(2)}) collective-permute-start(bf16[128,256]{1,0:T(8,128)(2,1)S(1)} %shard_map.125.refs_0_), channel_id=1, source_target_pairs={{0,3},{1,2},{2,1},{3,0},{4,7},{5,6},{6,5},{7,4},{8,11},{9,10},{10,... | collective-permute-start | bytes 196616 | tf_op jit(solution)/shard_map/ppermute | solution.py:55
  38.4 2.6 %collective-permute-start.14 = (bf16[128,256]{1,0:T(8,128)(2,1)S(1)}, bf16[128,256]{1,0:T(8,128)(2,1)S(1)}, u32[]{:S(2)}, u32[]{:S(2)}) collective-permute-start(bf16[128,256]{1,0:T(8,128)(2,1)S(1)} %shard_map.127.refs_0_), channel_id=1, source_target_pairs={{0,2},{1,3},{2,0},{3,1},{4,6},{5,7},{6,4},{7,5},{8,10},{9,11},{10,... | collective-permute-start | bytes 196616 | tf_op jit(solution)/shard_map/ppermute | solution.py:55
  41.0 0.6 %collective-permute-start.18 = (bf16[144,256]{1,0:T(8,128)(2,1)S(1)}, bf16[144,256]{1,0:T(8,128)(2,1)S(1)}, u32[]{:S(2)}, u32[]{:S(2)}) collective-permute-start(bf16[144,256]{1,0:T(8,128)(2,1)S(1)} %shard_map.132.refs_1_), channel_id=1, source_target_pairs={{0,16},{4,20},{8,24},{12,28},{16,0},{20,4},{24,8},{28,12},{1,17},{... | collective-permute-start | bytes 221192 | tf_op jit(solution)/shard_map/ppermute | solution.py:70
  42.2 0.7 %collective-permute-done.13.refs_1_ = bf16[128,256]{1,0:T(8,128)(2,1)S(1)} collective-permute-done((bf16[128,256]{1,0:T(8,128)(2,1)S(1)}, bf16[128,256]{1,0:T(8,128)(2,1)S(1)}, u32[]{:S(2)}, u32[]{:S(2)}) %collective-permute-start.13) | collective-permute-done | bytes 65568 | tf_op jit(solution)/shard_map/ppermute | solution.py:55
  42.8 0.8 %collective-permute-done.14.refs_2_ = bf16[128,256]{1,0:T(8,128)(2,1)S(1)} collective-permute-done((bf16[128,256]{1,0:T(8,128)(2,1)S(1)}, bf16[128,256]{1,0:T(8,128)(2,1)S(1)}, u32[]{:S(2)}, u32[]{:S(2)}) %collective-permute-start.14) | collective-permute-done | bytes 65568 | tf_op jit(solution)/shard_map/ppermute | solution.py:55
  43.6 0.8 %shard_map.129.after_ref = bf16[128,256]{1,0:T(8,128)(2,1)} custom-call(bf16[256,256]{1,0:T(8,128)(2,1)S(1)} %copy-done, bf16[128,256]{1,0:T(8,128)(2,1)S(1)} %collective-permute-done.12.refs_0_, bf16[128,256]{1,0:T(8,128)(2,1)S(1)} %collective-permute-done.13.refs_1_, bf16[128,256]{1,0:T(8,128)(2,1)S(1)} %collective-permute-done.14.refs_2_, ...), custom_call_target="tpu_custom_call" | custom-call | flops 2516582400 | bytes 262144 | tf_op jit(solution)/shard_map/pallas_call | solution.py:481
  44.5 1.0 %collective-permute-done.18.refs_0_ = bf16[144,256]{1,0:T(8,128)(2,1)S(1)} collective-permute-done((bf16[144,256]{1,0:T(8,128)(2,1)S(1)}, bf16[144,256]{1,0:T(8,128)(2,1)S(1)}, u32[]{:S(2)}, u32[]{:S(2)}) %collective-permute-start.18) | collective-permute-done | bytes 73760 | tf_op jit(solution)/shard_map/ppermute | solution.py:70
  45.5 0.6 %shard_map.119 = bf16[128,256]{1,0:T(8,128)(2,1)} custom-call(bf16[128,256]{1,0:T(8,128)(2,1)S(1)} %get-tuple-element.21.in_ref), custom_call_target="tpu_custom_call" | custom-call | bytes 131072 | tf_op jit(solution)/shard_map/pallas_call | solution.py:427
  46.2 0.7 %collective-permute-done.19.other_ref = f32[128,256]{1,0:T(8,128)S(1)} collective-permute-done((f32[128,256]{1,0:T(8,128)S(1)}, f32[128,256]{1,0:T(8,128)S(1)}, u32[]{:S(2)}, u32[]{:S(2)}) %collective-permute-start.19) | collective-permute-done | bytes 131104 | tf_op jit(solution)/shard_map/ppermute | solution.py:60
  46.9 0.7 %shard_map.134 = (f32[256,256]{1,0:T(8,128)}, f32[1,256]{1,0:T(1,128)}) custom-call(f32[128,256]{1,0:T(8,128)S(1)} %get-tuple-element.26.own_ref, f32[128,256]{1,0:T(8,128)S(1)} %collective-permute-done.19.other_ref, f32[1,256]{1,0:T(1,128)S(1)} %get-tuple-element.27.bias_ref), custom_call_target="tpu_custom_call" | custom-call | bytes 524288 | tf_op jit(solution)/shard_map/pallas_call | solution.py:500
  (38 shorter events, 3.7 us)
Async XLA Ops:
  0.6 8.2 %collective-permute-start = (bf16[128,256]{1,0:T(8,128)(2,1)}, bf16[128,256]{1,0:T(8,128)(2,1)S(1)}, u32[]{:S(2)}, u32[]{:S(2)}) collective-permute-start(bf16[128,256]{1,0:T(8,128)(2,1)} %refs_3_.1), channel_id=1, source_target_pairs={{0,3},{1,2},{2,1},{3,0},{4,7},{5,6},{6,5},{7,4},{8,11},{9,10},{10,... | collective-permute-start | bytes 196616 | tf_op jit(solution)/shard_map/ppermute | solution.py:55
  5.7 4.9 %collective-permute-start.1 = (bf16[128,256]{1,0:T(8,128)(2,1)}, bf16[128,256]{1,0:T(8,128)(2,1)S(1)}, u32[]{:S(2)}, u32[]{:S(2)}) collective-permute-start(bf16[128,256]{1,0:T(8,128)(2,1)} %refs_3_.1), channel_id=1, source_target_pairs={{0,1},{1,0},{2,3},{3,2},{4,5},{5,4},{6,7},{7,6},{8,9},{9,8},{10,11... | collective-permute-start | bytes 196616 | tf_op jit(solution)/shard_map/ppermute | solution.py:55
  5.8 5.8 %collective-permute-start.2 = (bf16[128,256]{1,0:T(8,128)(2,1)}, bf16[128,256]{1,0:T(8,128)(2,1)S(1)}, u32[]{:S(2)}, u32[]{:S(2)}) collective-permute-start(bf16[128,256]{1,0:T(8,128)(2,1)} %refs_3_.1), channel_id=1, source_target_pairs={{0,2},{1,3},{2,0},{3,1},{4,6},{5,7},{6,4},{7,5},{8,10},{9,11},{10,... | collective-permute-start | bytes 196616 | tf_op jit(solution)/shard_map/ppermute | solution.py:55
  7.0 4.6 %copy-start.1 = (bf16[128,256]{1,0:T(8,128)(2,1)S(1)}, bf16[128,256]{1,0:T(8,128)(2,1)}, u32[]{:S(2)}) copy-start(bf16[128,256]{1,0:T(8,128)(2,1)} %refs_3_.1) | copy-start | bytes 196612
  11.9 1.6 %collective-permute-start.3 = (bf16[512,256]{1,0:T(8,128)(2,1)S(1)}, bf16[512,256]{1,0:T(8,128)(2,1)S(1)}, u32[]{:S(2)}, u32[]{:S(2)}) collective-permute-start(bf16[512,256]{1,0:T(8,128)(2,1)S(1)} %get-tuple-element.20), channel_id=1, source_target_pairs={{0,4},{4,0},{8,12},{12,8},{16,20},{20,16},{24,28},{28,24},{1,5},{5... | collective-permute-start | bytes 786440 | tf_op jit(solution)/shard_map/ppermute | solution.py:60
  13.5 5.5 %collective-permute-start.4 = (bf16[128,256]{1,0:T(8,128)(2,1)S(1)}, bf16[128,256]{1,0:T(8,128)(2,1)S(1)}, u32[]{:S(2)}, u32[]{:S(2)}) collective-permute-start(bf16[128,256]{1,0:T(8,128)(2,1)S(1)} %shard_map.114.refs_0_), channel_id=1, source_target_pairs={{0,24},{4,28},{8,16},{12,20},{16,8},{20,12},{24,0},{28,4},{1,25},{... | collective-permute-start | bytes 196616 | tf_op jit(solution)/shard_map/ppermute | solution.py:55
  16.1 4.3 %collective-permute-start.5 = (bf16[128,256]{1,0:T(8,128)(2,1)S(1)}, bf16[128,256]{1,0:T(8,128)(2,1)S(1)}, u32[]{:S(2)}, u32[]{:S(2)}) collective-permute-start(bf16[128,256]{1,0:T(8,128)(2,1)S(1)} %shard_map.115.refs_0_), channel_id=1, source_target_pairs={{0,8},{4,12},{8,0},{12,4},{16,24},{20,28},{24,16},{28,20},{1,9},{5... | collective-permute-start | bytes 196616 | tf_op jit(solution)/shard_map/ppermute | solution.py:55
  16.7 4.4 %copy-start = (bf16[256,256]{1,0:T(8,128)(2,1)S(1)}, bf16[256,256]{1,0:T(8,128)(2,1)}, u32[]{:S(2)}) copy-start(bf16[256,256]{1,0:T(8,128)(2,1)} %weight_ref.3) | copy-start | bytes 393220
  16.7 4.3 %copy-start.2 = (bf16[128,256]{1,0:T(8,128)(2,1)S(1)}, bf16[128,256]{1,0:T(8,128)(2,1)}, u32[]{:S(2)}) copy-start(bf16[128,256]{1,0:T(8,128)(2,1)} %cot_ref.1) | copy-start | bytes 196612
  16.7 4.3 %collective-permute-start.6 = (bf16[128,256]{1,0:T(8,128)(2,1)S(1)}, bf16[128,256]{1,0:T(8,128)(2,1)S(1)}, u32[]{:S(2)}, u32[]{:S(2)}) collective-permute-start(bf16[128,256]{1,0:T(8,128)(2,1)S(1)} %shard_map.116.refs_0_), channel_id=1, source_target_pairs={{0,16},{4,20},{8,24},{12,28},{16,0},{20,4},{24,8},{28,12},{1,17},{... | collective-permute-start | bytes 196616 | tf_op jit(solution)/shard_map/ppermute | solution.py:55
  21.6 1.3 %collective-permute-start.7 = (bf16[144,256]{1,0:T(8,128)(2,1)S(1)}, bf16[144,256]{1,0:T(8,128)(2,1)S(1)}, u32[]{:S(2)}, u32[]{:S(2)}) collective-permute-start(bf16[144,256]{1,0:T(8,128)(2,1)S(1)} %get-tuple-element.24), channel_id=1, source_target_pairs={{0,4},{4,0},{8,12},{12,8},{16,20},{20,16},{24,28},{28,24},{1,5},{5... | collective-permute-start | bytes 221192 | tf_op jit(solution)/shard_map/ppermute | solution.py:60
  23.0 5.1 %collective-permute-start.15 = (bf16[144,256]{1,0:T(8,128)(2,1)S(1)}, bf16[144,256]{1,0:T(8,128)(2,1)S(1)}, u32[]{:S(2)}, u32[]{:S(2)}) collective-permute-start(bf16[144,256]{1,0:T(8,128)(2,1)S(1)} %shard_map.122.after_ref.refs_1_), channel_id=1, source_target_pairs={{0,1},{1,0},{2,3},{3,2},{4,5},{5,4},{6,7},{7,6},{8,9},{9,8},{10,11... | collective-permute-start | bytes 221192 | tf_op jit(solution)/shard_map/ppermute | solution.py:70
  24.6 5.7 %collective-permute-start.8 = (bf16[128,256]{1,0:T(8,128)(2,1)S(1)}, bf16[128,256]{1,0:T(8,128)(2,1)S(1)}, u32[]{:S(2)}, u32[]{:S(2)}) collective-permute-start(bf16[128,256]{1,0:T(8,128)(2,1)S(1)} %get-tuple-element.23.grad_ref.refs_3_), channel_id=1, source_target_pairs={{0,24},{4,28},{8,16},{12,20},{16,8},{20,12},{24,0},{28,4},{1,25},{... | collective-permute-start | bytes 196616 | tf_op jit(solution)/shard_map/ppermute | solution.py:55
  26.0 4.3 %collective-permute-start.9 = (bf16[128,256]{1,0:T(8,128)(2,1)S(1)}, bf16[128,256]{1,0:T(8,128)(2,1)S(1)}, u32[]{:S(2)}, u32[]{:S(2)}) collective-permute-start(bf16[128,256]{1,0:T(8,128)(2,1)S(1)} %get-tuple-element.23.grad_ref.refs_3_), channel_id=1, source_target_pairs={{0,8},{4,12},{8,0},{12,4},{16,24},{20,28},{24,16},{28,20},{1,9},{5... | collective-permute-start | bytes 196616 | tf_op jit(solution)/shard_map/ppermute | solution.py:55
  26.5 4.4 %collective-permute-start.10 = (bf16[128,256]{1,0:T(8,128)(2,1)S(1)}, bf16[128,256]{1,0:T(8,128)(2,1)S(1)}, u32[]{:S(2)}, u32[]{:S(2)}) collective-permute-start(bf16[128,256]{1,0:T(8,128)(2,1)S(1)} %get-tuple-element.23.grad_ref.refs_3_), channel_id=1, source_target_pairs={{0,16},{4,20},{8,24},{12,28},{16,0},{20,4},{24,8},{28,12},{1,17},{... | collective-permute-start | bytes 196616 | tf_op jit(solution)/shard_map/ppermute | solution.py:55
  28.1 6.1 %collective-permute-start.16 = (bf16[144,256]{1,0:T(8,128)(2,1)S(1)}, bf16[144,256]{1,0:T(8,128)(2,1)S(1)}, u32[]{:S(2)}, u32[]{:S(2)}) collective-permute-start(bf16[144,256]{1,0:T(8,128)(2,1)S(1)} %shard_map.130.refs_1_), channel_id=1, source_target_pairs={{0,2},{1,3},{2,0},{3,1},{4,6},{5,7},{6,4},{7,5},{8,10},{9,11},{10,... | collective-permute-start | bytes 221192 | tf_op jit(solution)/shard_map/ppermute | solution.py:70
  31.0 4.8 %collective-permute-start.11 = (bf16[512,256]{1,0:T(8,128)(2,1)S(1)}, bf16[512,256]{1,0:T(8,128)(2,1)S(1)}, u32[]{:S(2)}, u32[]{:S(2)}) collective-permute-start(bf16[512,256]{1,0:T(8,128)(2,1)S(1)} %shard_map.123.source_ref), channel_id=1, source_target_pairs={{0,4},{4,0},{8,12},{12,8},{16,20},{20,16},{24,28},{28,24},{1,5},{5... | collective-permute-start | bytes 786440 | tf_op jit(solution)/shard_map/ppermute | solution.py:60
  34.2 6.7 %collective-permute-start.17 = (bf16[144,256]{1,0:T(8,128)(2,1)S(1)}, bf16[144,256]{1,0:T(8,128)(2,1)S(1)}, u32[]{:S(2)}, u32[]{:S(2)}) collective-permute-start(bf16[144,256]{1,0:T(8,128)(2,1)S(1)} %shard_map.131.refs_1_), channel_id=1, source_target_pairs={{0,8},{4,12},{8,0},{12,4},{16,24},{20,28},{24,16},{28,20},{1,9},{5... | collective-permute-start | bytes 221192 | tf_op jit(solution)/shard_map/ppermute | solution.py:70
  36.0 6.2 %collective-permute-start.12 = (bf16[128,256]{1,0:T(8,128)(2,1)S(1)}, bf16[128,256]{1,0:T(8,128)(2,1)S(1)}, u32[]{:S(2)}, u32[]{:S(2)}) collective-permute-start(bf16[128,256]{1,0:T(8,128)(2,1)S(1)} %shard_map.125.refs_0_), channel_id=1, source_target_pairs={{0,3},{1,2},{2,1},{3,0},{4,7},{5,6},{6,5},{7,4},{8,11},{9,10},{10,... | collective-permute-start | bytes 196616 | tf_op jit(solution)/shard_map/ppermute | solution.py:55
  38.1 4.7 %collective-permute-start.13 = (bf16[128,256]{1,0:T(8,128)(2,1)S(1)}, bf16[128,256]{1,0:T(8,128)(2,1)S(1)}, u32[]{:S(2)}, u32[]{:S(2)}) collective-permute-start(bf16[128,256]{1,0:T(8,128)(2,1)S(1)} %shard_map.126.refs_0_), channel_id=1, source_target_pairs={{0,1},{1,0},{2,3},{3,2},{4,5},{5,4},{6,7},{7,6},{8,9},{9,8},{10,11... | collective-permute-start | bytes 196616 | tf_op jit(solution)/shard_map/ppermute | solution.py:55
  38.4 5.2 %collective-permute-start.14 = (bf16[128,256]{1,0:T(8,128)(2,1)S(1)}, bf16[128,256]{1,0:T(8,128)(2,1)S(1)}, u32[]{:S(2)}, u32[]{:S(2)}) collective-permute-start(bf16[128,256]{1,0:T(8,128)(2,1)S(1)} %shard_map.127.refs_0_), channel_id=1, source_target_pairs={{0,2},{1,3},{2,0},{3,1},{4,6},{5,7},{6,4},{7,5},{8,10},{9,11},{10,... | collective-permute-start | bytes 196616 | tf_op jit(solution)/shard_map/ppermute | solution.py:55
  41.0 4.4 %collective-permute-start.18 = (bf16[144,256]{1,0:T(8,128)(2,1)S(1)}, bf16[144,256]{1,0:T(8,128)(2,1)S(1)}, u32[]{:S(2)}, u32[]{:S(2)}) collective-permute-start(bf16[144,256]{1,0:T(8,128)(2,1)S(1)} %shard_map.132.refs_1_), channel_id=1, source_target_pairs={{0,16},{4,20},{8,24},{12,28},{16,0},{20,4},{24,8},{28,12},{1,17},{... | collective-permute-start | bytes 221192 | tf_op jit(solution)/shard_map/ppermute | solution.py:70
  45.5 1.4 %collective-permute-start.19 = (f32[128,256]{1,0:T(8,128)S(1)}, f32[128,256]{1,0:T(8,128)S(1)}, u32[]{:S(2)}, u32[]{:S(2)}) collective-permute-start(f32[128,256]{1,0:T(8,128)S(1)} %get-tuple-element.26.own_ref), channel_id=1, source_target_pairs={{0,4},{4,0},{8,12},{12,8},{16,20},{20,16},{24,28},{28,24},{1,5},{5... | collective-permute-start | bytes 393224 | tf_op jit(solution)/shard_map/ppermute | solution.py:60

commit v9 on v6

--- a/solution.py
+++ b/solution.py
@@ -13,6 +13,8 @@
 CUBIC = 0.044715
 VMEM_LIMIT = 48 * 1024 * 1024
 BIAS_ROWS = 16
+ROW_SUM_WEIGHT = 70
+FEATURES_WEIGHT = 150
 
 VMEM_SPEC = pl.BlockSpec(memory_space=pltpu.VMEM)
 HBM_SPEC = pl.BlockSpec(memory_space=pltpu.HBM)
@@ -58,20 +60,25 @@
     return lax.ppermute(block, "col", [(i, i ^ 1) for i in range(size)])
 
 
-def exchange_second(block, along, n_row, n_col):
-    count = n_row if along == "row" else n_col // 2
-    received = []
-    for k in far_first(count):
-        pairs = []
-        for row in range(n_row):
-            for col in range(1, n_col, 2):
-                if along == "row":
-                    target = col * n_row + partner(row, k, count)
-                else:
-                    target = (2 * partner(col // 2, k, count) + 1) * n_row + row
-                pairs.append((col * n_row + row, target))
-        received.append(lax.ppermute(block, ("col", "row"), pairs) if k else block)
-    return received
+def doubling(block, add, axes, count, pairs_at):
+    terms, step = [block], 1
+    while step < count:
+        block = add(terms) if len(terms) > 1 else block
+        terms = [lax.ppermute(block, axes, pairs_at(step)), block]
+        step *= 2
+    return terms
+
+
+def second_cores_along_row(step, n_row, n_col):
+    return [
+        (col * n_row + row, col * n_row + (row ^ step if col % 2 else row))
+        for col in range(n_col)
+        for row in range(n_row)
+    ]
+
+
+def second_cores_along_col(step, n_col):
+    return [(col, col ^ (2 * step) if col % 2 else col) for col in range(n_col)]
 
 
 def block_at(index, size):
@@ -326,15 +333,15 @@
     near = 1
     own_nodes = n_chip * tile
 
-    def add(terms, after=()):
+    def add(terms, flops=0):
         return call(
             functools.partial(add_terms_kernel, n_terms=len(terms)),
             like(width + BIAS_ROWS, hidden),
-            [VMEM_SPEC] * (len(terms) + len(after)),
-            [],
-            len(terms) * width * hidden,
+            [VMEM_SPEC] * len(terms),
+            [],
+            flops or len(terms) * width * hidden,
             len(terms) * width * hidden * 2,
-        )(*terms, *after)
+        )(*terms)
 
     is_dense = n_row * n_col <= 2 * slots
     if is_dense:
@@ -434,9 +441,10 @@
         matrix,
         6 * block_bytes,
     )(aggregated, grad)
-    first_term = lax.ppermute(term, "col", [(i - 1, i) for i in range(1, n_col, 2)])
-    chip_term = add([first_term, term])
-    row_terms = exchange_second(chip_term, "row", n_row, n_col)
+    chip_term = add([swap_cores(term, n_col), term])
+    along_row = functools.partial(second_cores_along_row, n_row=n_row, n_col=n_col)
+    row_terms = doubling(chip_term, add, ("col", "row"), n_row, along_row)
+    row_term = add(row_terms, flops=ROW_SUM_WEIGHT * matrix)
 
     own_grads = call(
         gather_kernel,
@@ -478,18 +486,17 @@
             2 * block_bytes,
         )(*piece_args, *before)
 
-    made = in_turn(n_row, back_piece)
-    backs = exchange(made, "row", n_row)
-    row_term = add(row_terms, [made[0]])
+    backs = exchange(in_turn(n_row, back_piece), "row", n_row)
     grad_features = call(
         features_kernel,
         like(tile, width),
         [VMEM_SPEC] * (1 + n_row),
         [],
-        matrix,
+        FEATURES_WEIGHT * matrix,
         n_row * block_bytes,
     )(weight, *backs)
-    all_terms = exchange_second(row_term, "col", n_row, n_col)
+    along_col = functools.partial(second_cores_along_col, n_col=n_col)
+    all_terms = doubling(row_term, add, "col", n_chip, along_col)
     factor = (tile * n_row * n_col) ** (-0.5)
     total = call(
         functools.partial(scale_kernel, factor=factor),
@@ -499,7 +506,6 @@
         len(all_terms) * width * hidden,
         len(all_terms) * width * hidden * 2,
     )(pltpu.with_memory_space_constraint(grad_features, pltpu.HBM), *all_terms)
-    second_total = lax.ppermute(total, "col", [(i, i - 1) for i in range(1, n_col, 2)])
     grad_weight, grad_bias = call(
         join_kernel,
         (like(width, hidden, F32), like(1, hidden, F32)),
@@ -507,7 +513,7 @@
         [],
         0,
         width * hidden * 8,
-    )(total, second_total)
+    )(total, swap_cores(total, n_col))
     return hidden_out, grad_features, grad_weight, grad_bias.reshape(hidden)
 
 

time: 66 us -> 53.8 us (0.82)
  waiting for transfers between devices: 34.6 us -> 13.9 us
  starting transfers between devices: 22.4 us -> 31.7 us
  Pallas kernels: 7.13 us -> 6.45 us
    ppermute x8 -> x4, waiting for transfers between devices: 15.8 us -> 0.01 us  [doubling(): terms = [lax.ppermute(block, axes, pairs_at(step)), block]]
    ppermute x2 -> x4, starting transfers between devices: 0.14 us -> 11.4 us  [swap_cores(): return lax.ppermute(block, 'col', [(i, i ^ 1) for i in range(size)])]
    ppermute x12, waiting for transfers between devices: 17.5 us -> 10.8 us  [exchange(): lax.ppermute(blocks[k], axis, pairs)]
    ppermute x8 -> x4, starting transfers between devices: 6.61 us -> 2.68 us  [doubling(): terms = [lax.ppermute(block, axes, pairs_at(step)), block]]
    ppermute x2 -> x4, waiting for transfers between devices: 1.23 us -> 3.11 us  [swap_cores(): return lax.ppermute(block, 'col', [(i, i ^ 1) for i in range(size)])]
    ppermute x12, starting transfers between devices: 15.7 us -> 17.6 us  [exchange(): lax.ppermute(blocks[k], axis, pairs)]
    pallas_call x1, Pallas kernels: 2.13 us -> 1.45 us  [local(): call(dense_kernel, (like(row_nodes, col_nodes), like(1, hidden, F32)), [S...]
  transfers between devices with their start and end apart: 22 -> 20, of which waited for: 13 -> 15; matrix products, arithmetic and copies ran while one was open for 0% -> 0% of each run, Pallas kernels for 8% -> 9%
where the time goes in v9:
time: 53.8 us; the launch traced here: 53.6 us
  starting transfers between devices  31.7 us (59%)
  waiting for transfers between devices  13.9 us (26%)
  Pallas kernels  6.45 us (12%)
  between operations  1.51 us (3%)
    ppermute x12, starting transfers between devices, exchange(): lax.ppermute(blocks[k], axis, pairs)  17.6 us
    ppermute x4, starting transfers between devices, swap_cores(): return lax.ppermute(block, 'col', [(i, i ^ 1) for i in range(size)])  11.4 us
    ppermute x12, waiting for transfers between devices, exchange(): lax.ppermute(blocks[k], axis, pairs)  10.8 us
    ppermute x4, waiting for transfers between devices, swap_cores(): return lax.ppermute(block, 'col', [(i, i ^ 1) for i in range(size)])  3.11 us
    ppermute x4, starting transfers between devices, doubling(): terms = [lax.ppermute(block, axes, pairs_at(step)), block]  2.68 us
    pallas_call x1, Pallas kernels, local(): call(dense_kernel, (like(row_nodes, col_nodes), like(1, hidden, F32)), [S...  1.45 us
  transfers between devices with their start and end apart: 20, of which 15 were waited for; matrix products, arithmetic and copies ran while one was open for 0% of the time, Pallas kernels for 9%

profile of v9, /device:TPU:0, one launch (start us, length us, event | category | flops | bytes accessed | tf_op | source)
XLA Modules:
  0.0 53.6 jit_solution(15127807822590217970)
XLA Ops:
  0.6 5.1 %collective-permute-start = (bf16[128,256]{1,0:T(8,128)(2,1)}, bf16[128,256]{1,0:T(8,128)(2,1)S(1)}, u32[]{:S(2)}, u32[]{:S(2)}) collective-permute-start(bf16[128,256]{1,0:T(8,128)(2,1)} %refs_3_.1), channel_id=1, source_target_pairs={{0,3},{1,2},{2,1},{3,0},{4,7},{5,6},{6,5},{7,4},{8,11},{9,10},{10,... | collective-permute-start | bytes 196616 | tf_op jit(solution)/shard_map/ppermute | solution.py:55
  5.8 0.6 %collective-permute-start.2 = (bf16[128,256]{1,0:T(8,128)(2,1)}, bf16[128,256]{1,0:T(8,128)(2,1)S(1)}, u32[]{:S(2)}, u32[]{:S(2)}) collective-permute-start(bf16[128,256]{1,0:T(8,128)(2,1)} %refs_3_.1), channel_id=1, source_target_pairs={{0,2},{1,3},{2,0},{3,1},{4,6},{5,7},{6,4},{7,5},{8,10},{9,11},{10,... | collective-permute-start | bytes 196616 | tf_op jit(solution)/shard_map/ppermute | solution.py:55
  7.1 1.5 %shard_map.111 = (bf16[1024,512]{1,0:T(8,128)(2,1)S(1)}, f32[1,256]{1,0:T(1,128)S(1)}) custom-call(s32[1,1]{1,0:T(1,128)S(6)} %copy.12.count_ref, s32[1,1,32]{2,1,0:T(1,128)} %row_hbm.1, s32[1,1,32]{2,1,0:T(1,128)} %col_hbm.1, bf16[1,1,32,128,128]{4,3,2,1,0:T(8,128)(2,1)} %tiles_hbm.1, f32[1,256]{1,0:T(1,128)} %bitcast.2), custom_call_target="tpu_custom_call" | custom-call | bytes 6291456 | tf_op jit(solution)/shard_map/pallas_call | solution.py:349
  8.9 1.8 %collective-permute-done.1.refs_1_ = bf16[128,256]{1,0:T(8,128)(2,1)S(1)} collective-permute-done((bf16[128,256]{1,0:T(8,128)(2,1)}, bf16[128,256]{1,0:T(8,128)(2,1)S(1)}, u32[]{:S(2)}, u32[]{:S(2)}) %collective-permute-start.1) | collective-permute-done | bytes 65568 | tf_op jit(solution)/shard_map/ppermute | solution.py:55
  10.6 1.0 %collective-permute-done.2.refs_2_ = bf16[128,256]{1,0:T(8,128)(2,1)S(1)} collective-permute-done((bf16[128,256]{1,0:T(8,128)(2,1)}, bf16[128,256]{1,0:T(8,128)(2,1)S(1)}, u32[]{:S(2)}, u32[]{:S(2)}) %collective-permute-start.2) | collective-permute-done | bytes 65568 | tf_op jit(solution)/shard_map/ppermute | solution.py:55
  12.3 1.2 %collective-permute-done.3.other_ref = bf16[512,256]{1,0:T(8,128)(2,1)S(1)} collective-permute-done((bf16[512,256]{1,0:T(8,128)(2,1)S(1)}, bf16[512,256]{1,0:T(8,128)(2,1)S(1)}, u32[]{:S(2)}, u32[]{:S(2)}) %collective-permute-start.3) | collective-permute-done | bytes 262176 | tf_op jit(solution)/shard_map/ppermute | solution.py:60
  13.5 2.5 %collective-permute-start.4 = (bf16[128,256]{1,0:T(8,128)(2,1)S(1)}, bf16[128,256]{1,0:T(8,128)(2,1)S(1)}, u32[]{:S(2)}, u32[]{:S(2)}) collective-permute-start(bf16[128,256]{1,0:T(8,128)(2,1)S(1)} %shard_map.114.refs_0_), channel_id=1, source_target_pairs={{0,24},{4,28},{8,16},{12,20},{16,8},{20,12},{24,0},{28,4},{1,25},{... | collective-permute-start | bytes 196616 | tf_op jit(solution)/shard_map/ppermute | solution.py:55
  16.1 0.6 %collective-permute-start.5 = (bf16[128,256]{1,0:T(8,128)(2,1)S(1)}, bf16[128,256]{1,0:T(8,128)(2,1)S(1)}, u32[]{:S(2)}, u32[]{:S(2)}) collective-permute-start(bf16[128,256]{1,0:T(8,128)(2,1)S(1)} %shard_map.115.refs_0_), channel_id=1, source_target_pairs={{0,8},{4,12},{8,0},{12,4},{16,24},{20,28},{24,16},{28,20},{1,9},{5... | collective-permute-start | bytes 196616 | tf_op jit(solution)/shard_map/ppermute | solution.py:55
  16.7 0.6 %collective-permute-start.6 = (bf16[128,256]{1,0:T(8,128)(2,1)S(1)}, bf16[128,256]{1,0:T(8,128)(2,1)S(1)}, u32[]{:S(2)}, u32[]{:S(2)}) collective-permute-start(bf16[128,256]{1,0:T(8,128)(2,1)S(1)} %shard_map.116.refs_0_), channel_id=1, source_target_pairs={{0,16},{4,20},{8,24},{12,28},{16,0},{20,4},{24,8},{28,12},{1,17},{... | collective-permute-start | bytes 196616 | tf_op jit(solution)/shard_map/ppermute | solution.py:55
  17.3 1.8 %collective-permute-done.4.refs_0_ = bf16[128,256]{1,0:T(8,128)(2,1)S(1)} collective-permute-done((bf16[128,256]{1,0:T(8,128)(2,1)S(1)}, bf16[128,256]{1,0:T(8,128)(2,1)S(1)}, u32[]{:S(2)}, u32[]{:S(2)}) %collective-permute-start.4) | collective-permute-done | bytes 65568 | tf_op jit(solution)/shard_map/ppermute | solution.py:55
  19.1 1.3 %collective-permute-done.5.refs_1_ = bf16[128,256]{1,0:T(8,128)(2,1)S(1)} collective-permute-done((bf16[128,256]{1,0:T(8,128)(2,1)S(1)}, bf16[128,256]{1,0:T(8,128)(2,1)S(1)}, u32[]{:S(2)}, u32[]{:S(2)}) %collective-permute-start.5) | collective-permute-done | bytes 65568 | tf_op jit(solution)/shard_map/ppermute | solution.py:55
  20.4 0.6 %collective-permute-done.6.refs_2_ = bf16[128,256]{1,0:T(8,128)(2,1)S(1)} collective-permute-done((bf16[128,256]{1,0:T(8,128)(2,1)S(1)}, bf16[128,256]{1,0:T(8,128)(2,1)S(1)}, u32[]{:S(2)}, u32[]{:S(2)}) %collective-permute-start.6) | collective-permute-done | bytes 65568 | tf_op jit(solution)/shard_map/ppermute | solution.py:55
  21.6 1.3 %collective-permute-done.7.refs_0_ = bf16[272,256]{1,0:T(8,128)(2,1)S(1)} collective-permute-done((bf16[272,256]{1,0:T(8,128)(2,1)S(1)}, bf16[272,256]{1,0:T(8,128)(2,1)S(1)}, u32[]{:S(2)}, u32[]{:S(2)}) %collective-permute-start.7) | collective-permute-done | bytes 139296 | tf_op jit(solution)/shard_map/ppermute | solution.py:60
  23.0 0.7 %collective-permute-start.15 = (bf16[272,256]{1,0:T(8,128)(2,1)S(1)}, bf16[272,256]{1,0:T(8,128)(2,1)S(1)}, u32[]{:S(2)}, u32[]{:S(2)}) collective-permute-start(bf16[272,256]{1,0:T(8,128)(2,1)S(1)} %shard_map.122.after_ref.refs_1_), channel_id=1, source_target_pairs={{0,0},{1,1},{2,2},{3,3},{4,5},{5,4},{6,7},{7,6},{8,8},{9,9},{10,10... | collective-permute-start | bytes 417800 | tf_op jit(solution)/shard_map/ppermute | solution.py:67
  23.7 1.5 %collective-permute-start.8 = (bf16[128,256]{1,0:T(8,128)(2,1)S(1)}, bf16[128,256]{1,0:T(8,128)(2,1)S(1)}, u32[]{:S(2)}, u32[]{:S(2)}) collective-permute-start(bf16[128,256]{1,0:T(8,128)(2,1)S(1)} %get-tuple-element.19.grad_ref.refs_3_), channel_id=1, source_target_pairs={{0,24},{4,28},{8,16},{12,20},{16,8},{20,12},{24,0},{28,4},{1,25},{... | collective-permute-start | bytes 196616 | tf_op jit(solution)/shard_map/ppermute | solution.py:55
  25.2 0.5 %collective-permute-start.9 = (bf16[128,256]{1,0:T(8,128)(2,1)S(1)}, bf16[128,256]{1,0:T(8,128)(2,1)S(1)}, u32[]{:S(2)}, u32[]{:S(2)}) collective-permute-start(bf16[128,256]{1,0:T(8,128)(2,1)S(1)} %get-tuple-element.19.grad_ref.refs_3_), channel_id=1, source_target_pairs={{0,8},{4,12},{8,0},{12,4},{16,24},{20,28},{24,16},{28,20},{1,9},{5... | collective-permute-start | bytes 196616 | tf_op jit(solution)/shard_map/ppermute | solution.py:55
  25.7 1.5 %collective-permute-start.10 = (bf16[128,256]{1,0:T(8,128)(2,1)S(1)}, bf16[128,256]{1,0:T(8,128)(2,1)S(1)}, u32[]{:S(2)}, u32[]{:S(2)}) collective-permute-start(bf16[128,256]{1,0:T(8,128)(2,1)S(1)} %get-tuple-element.19.grad_ref.refs_3_), channel_id=1, source_target_pairs={{0,16},{4,20},{8,24},{12,28},{16,0},{20,4},{24,8},{28,12},{1,17},{... | collective-permute-start | bytes 196616 | tf_op jit(solution)/shard_map/ppermute | solution.py:55
  27.3 0.7 %collective-permute-start.16 = (bf16[272,256]{1,0:T(8,128)(2,1)S(1)}, bf16[272,256]{1,0:T(8,128)(2,1)S(1)}, u32[]{:S(2)}, u32[]{:S(2)}) collective-permute-start(bf16[272,256]{1,0:T(8,128)(2,1)S(1)} %shard_map.130.refs_1_), channel_id=1, source_target_pairs={{0,0},{1,1},{2,2},{3,3},{4,6},{5,7},{6,4},{7,5},{8,8},{9,9},{10,10... | collective-permute-start | bytes 417800 | tf_op jit(solution)/shard_map/ppermute | solution.py:67
  28.0 0.9 %collective-permute-done.8.refs_0_ = bf16[128,256]{1,0:T(8,128)(2,1)S(1)} collective-permute-done((bf16[128,256]{1,0:T(8,128)(2,1)S(1)}, bf16[128,256]{1,0:T(8,128)(2,1)S(1)}, u32[]{:S(2)}, u32[]{:S(2)}) %collective-permute-start.8) | collective-permute-done | bytes 65568 | tf_op jit(solution)/shard_map/ppermute | solution.py:55
  28.9 1.0 %collective-permute-done.9.refs_1_ = bf16[128,256]{1,0:T(8,128)(2,1)S(1)} collective-permute-done((bf16[128,256]{1,0:T(8,128)(2,1)S(1)}, bf16[128,256]{1,0:T(8,128)(2,1)S(1)}, u32[]{:S(2)}, u32[]{:S(2)}) %collective-permute-start.9) | collective-permute-done | bytes 65568 | tf_op jit(solution)/shard_map/ppermute | solution.py:55
  30.1 2.9 %collective-permute-start.11 = (bf16[512,256]{1,0:T(8,128)(2,1)S(1)}, bf16[512,256]{1,0:T(8,128)(2,1)S(1)}, u32[]{:S(2)}, u32[]{:S(2)}) collective-permute-start(bf16[512,256]{1,0:T(8,128)(2,1)S(1)} %shard_map.123.source_ref), channel_id=1, source_target_pairs={{0,4},{4,0},{8,12},{12,8},{16,20},{20,16},{24,28},{28,24},{1,5},{5... | collective-permute-start | bytes 786440 | tf_op jit(solution)/shard_map/ppermute | solution.py:60
  33.1 0.7 %collective-permute-start.17 = (bf16[272,256]{1,0:T(8,128)(2,1)S(1)}, bf16[272,256]{1,0:T(8,128)(2,1)S(1)}, u32[]{:S(2)}, u32[]{:S(2)}) collective-permute-start(bf16[272,256]{1,0:T(8,128)(2,1)S(1)} %shard_map.131.refs_1_), channel_id=1, source_target_pairs={{0,0},{4,12},{8,8},{12,4},{16,16},{20,28},{24,24},{28,20},{1,1},{5... | collective-permute-start | bytes 417800 | tf_op jit(solution)/shard_map/ppermute | solution.py:67
  34.6 2.0 %collective-permute-start.12 = (bf16[128,256]{1,0:T(8,128)(2,1)S(1)}, bf16[128,256]{1,0:T(8,128)(2,1)S(1)}, u32[]{:S(2)}, u32[]{:S(2)}) collective-permute-start(bf16[128,256]{1,0:T(8,128)(2,1)S(1)} %shard_map.125.refs_0_), channel_id=1, source_target_pairs={{0,3},{1,2},{2,1},{3,0},{4,7},{5,6},{6,5},{7,4},{8,11},{9,10},{10,... | collective-permute-start | bytes 196616 | tf_op jit(solution)/shard_map/ppermute | solution.py:55
  37.1 2.5 %collective-permute-start.14 = (bf16[128,256]{1,0:T(8,128)(2,1)S(1)}, bf16[128,256]{1,0:T(8,128)(2,1)S(1)}, u32[]{:S(2)}, u32[]{:S(2)}) collective-permute-start(bf16[128,256]{1,0:T(8,128)(2,1)S(1)} %shard_map.127.refs_0_), channel_id=1, source_target_pairs={{0,2},{1,3},{2,0},{3,1},{4,6},{5,7},{6,4},{7,5},{8,10},{9,11},{10,... | collective-permute-start | bytes 196616 | tf_op jit(solution)/shard_map/ppermute | solution.py:55
  39.8 0.7 %collective-permute-start.18 = (bf16[272,256]{1,0:T(8,128)(2,1)S(1)}, bf16[272,256]{1,0:T(8,128)(2,1)S(1)}, u32[]{:S(2)}, u32[]{:S(2)}) collective-permute-start(bf16[272,256]{1,0:T(8,128)(2,1)S(1)} %shard_map.132.refs_1_), channel_id=1, source_target_pairs={{0,0},{4,20},{8,8},{12,28},{16,16},{20,4},{24,24},{28,12},{1,1},{5... | collective-permute-start | bytes 417800 | tf_op jit(solution)/shard_map/ppermute | solution.py:67
  40.8 0.7 %collective-permute-done.13.refs_1_ = bf16[128,256]{1,0:T(8,128)(2,1)S(1)} collective-permute-done((bf16[128,256]{1,0:T(8,128)(2,1)S(1)}, bf16[128,256]{1,0:T(8,128)(2,1)S(1)}, u32[]{:S(2)}, u32[]{:S(2)}) %collective-permute-start.13) | collective-permute-done | bytes 65568 | tf_op jit(solution)/shard_map/ppermute | solution.py:55
  41.4 0.9 %collective-permute-done.14.refs_2_ = bf16[128,256]{1,0:T(8,128)(2,1)S(1)} collective-permute-done((bf16[128,256]{1,0:T(8,128)(2,1)S(1)}, bf16[128,256]{1,0:T(8,128)(2,1)S(1)}, u32[]{:S(2)}, u32[]{:S(2)}) %collective-permute-start.14) | collective-permute-done | bytes 65568 | tf_op jit(solution)/shard_map/ppermute | solution.py:55
  42.3 0.8 %shard_map.129.after_ref = bf16[128,256]{1,0:T(8,128)(2,1)} custom-call(bf16[256,256]{1,0:T(8,128)(2,1)S(1)} %copy-done, bf16[128,256]{1,0:T(8,128)(2,1)S(1)} %collective-permute-done.12.refs_0_, bf16[128,256]{1,0:T(8,128)(2,1)S(1)} %collective-permute-done.13.refs_1_, bf16[128,256]{1,0:T(8,128)(2,1)S(1)} %collective-permute-done.14.refs_2_, ...), custom_call_target="tpu_custom_call" | custom-call | flops 2516582400 | bytes 262144 | tf_op jit(solution)/shard_map/pallas_call | solution.py:490
  43.2 8.4 %collective-permute-start.19 = (f32[264,256]{1,0:T(8,128)S(1)}, f32[264,256]{1,0:T(8,128)S(1)}, u32[]{:S(2)}, u32[]{:S(2)}) collective-permute-start(f32[264,256]{1,0:T(8,128)S(1)} %shard_map.133.own_ref), channel_id=1, source_target_pairs={{0,4},{4,0},{8,12},{12,8},{16,20},{20,16},{24,28},{28,24},{1,5},{5... | collective-permute-start | bytes 811016 | tf_op jit(solution)/shard_map/ppermute | solution.py:60
  51.6 0.6 %shard_map.119 = bf16[128,256]{1,0:T(8,128)(2,1)} custom-call(bf16[128,256]{1,0:T(8,128)(2,1)S(1)} %get-tuple-element.17.in_ref), custom_call_target="tpu_custom_call" | custom-call | bytes 131072 | tf_op jit(solution)/shard_map/pallas_call | solution.py:435
  52.3 0.5 %collective-permute-done.19.other_ref = f32[264,256]{1,0:T(8,128)S(1)} collective-permute-done((f32[264,256]{1,0:T(8,128)S(1)}, f32[264,256]{1,0:T(8,128)S(1)}, u32[]{:S(2)}, u32[]{:S(2)}) %collective-permute-start.19) | collective-permute-done | bytes 270368 | tf_op jit(solution)/shard_map/ppermute | solution.py:60
  52.8 0.7 %shard_map.134 = (f32[256,256]{1,0:T(8,128)}, f32[1,256]{1,0:T(1,128)}) custom-call(f32[264,256]{1,0:T(8,128)S(1)} %shard_map.133.own_ref, f32[264,256]{1,0:T(8,128)S(1)} %collective-permute-done.19.other_ref), custom_call_target="tpu_custom_call" | custom-call | bytes 524288 | tf_op jit(solution)/shard_map/pallas_call | solution.py:509
  (38 shorter events, 3.8 us)
Async XLA Ops:
  0.6 8.2 %collective-permute-start = (bf16[128,256]{1,0:T(8,128)(2,1)}, bf16[128,256]{1,0:T(8,128)(2,1)S(1)}, u32[]{:S(2)}, u32[]{:S(2)}) collective-permute-start(bf16[128,256]{1,0:T(8,128)(2,1)} %refs_3_.1), channel_id=1, source_target_pairs={{0,3},{1,2},{2,1},{3,0},{4,7},{5,6},{6,5},{7,4},{8,11},{9,10},{10,... | collective-permute-start | bytes 196616 | tf_op jit(solution)/shard_map/ppermute | solution.py:55
  5.7 4.9 %collective-permute-start.1 = (bf16[128,256]{1,0:T(8,128)(2,1)}, bf16[128,256]{1,0:T(8,128)(2,1)S(1)}, u32[]{:S(2)}, u32[]{:S(2)}) collective-permute-start(bf16[128,256]{1,0:T(8,128)(2,1)} %refs_3_.1), channel_id=1, source_target_pairs={{0,1},{1,0},{2,3},{3,2},{4,5},{5,4},{6,7},{7,6},{8,9},{9,8},{10,11... | collective-permute-start | bytes 196616 | tf_op jit(solution)/shard_map/ppermute | solution.py:55
  5.8 5.8 %collective-permute-start.2 = (bf16[128,256]{1,0:T(8,128)(2,1)}, bf16[128,256]{1,0:T(8,128)(2,1)S(1)}, u32[]{:S(2)}, u32[]{:S(2)}) collective-permute-start(bf16[128,256]{1,0:T(8,128)(2,1)} %refs_3_.1), channel_id=1, source_target_pairs={{0,2},{1,3},{2,0},{3,1},{4,6},{5,7},{6,4},{7,5},{8,10},{9,11},{10,... | collective-permute-start | bytes 196616 | tf_op jit(solution)/shard_map/ppermute | solution.py:55
  7.0 4.6 %copy-start.1 = (bf16[128,256]{1,0:T(8,128)(2,1)S(1)}, bf16[128,256]{1,0:T(8,128)(2,1)}, u32[]{:S(2)}) copy-start(bf16[128,256]{1,0:T(8,128)(2,1)} %refs_3_.1) | copy-start | bytes 196612
  11.9 1.6 %collective-permute-start.3 = (bf16[512,256]{1,0:T(8,128)(2,1)S(1)}, bf16[512,256]{1,0:T(8,128)(2,1)S(1)}, u32[]{:S(2)}, u32[]{:S(2)}) collective-permute-start(bf16[512,256]{1,0:T(8,128)(2,1)S(1)} %get-tuple-element.16), channel_id=1, source_target_pairs={{0,4},{4,0},{8,12},{12,8},{16,20},{20,16},{24,28},{28,24},{1,5},{5... | collective-permute-start | bytes 786440 | tf_op jit(solution)/shard_map/ppermute | solution.py:60
  13.5 5.5 %collective-permute-start.4 = (bf16[128,256]{1,0:T(8,128)(2,1)S(1)}, bf16[128,256]{1,0:T(8,128)(2,1)S(1)}, u32[]{:S(2)}, u32[]{:S(2)}) collective-permute-start(bf16[128,256]{1,0:T(8,128)(2,1)S(1)} %shard_map.114.refs_0_), channel_id=1, source_target_pairs={{0,24},{4,28},{8,16},{12,20},{16,8},{20,12},{24,0},{28,4},{1,25},{... | collective-permute-start | bytes 196616 | tf_op jit(solution)/shard_map/ppermute | solution.py:55
  16.1 4.3 %collective-permute-start.5 = (bf16[128,256]{1,0:T(8,128)(2,1)S(1)}, bf16[128,256]{1,0:T(8,128)(2,1)S(1)}, u32[]{:S(2)}, u32[]{:S(2)}) collective-permute-start(bf16[128,256]{1,0:T(8,128)(2,1)S(1)} %shard_map.115.refs_0_), channel_id=1, source_target_pairs={{0,8},{4,12},{8,0},{12,4},{16,24},{20,28},{24,16},{28,20},{1,9},{5... | collective-permute-start | bytes 196616 | tf_op jit(solution)/shard_map/ppermute | solution.py:55
  16.7 4.4 %copy-start = (bf16[256,256]{1,0:T(8,128)(2,1)S(1)}, bf16[256,256]{1,0:T(8,128)(2,1)}, u32[]{:S(2)}) copy-start(bf16[256,256]{1,0:T(8,128)(2,1)} %weight_ref.3) | copy-start | bytes 393220
  16.7 4.3 %copy-start.2 = (bf16[128,256]{1,0:T(8,128)(2,1)S(1)}, bf16[128,256]{1,0:T(8,128)(2,1)}, u32[]{:S(2)}) copy-start(bf16[128,256]{1,0:T(8,128)(2,1)} %cot_ref.1) | copy-start | bytes 196612
  16.7 4.3 %collective-permute-start.6 = (bf16[128,256]{1,0:T(8,128)(2,1)S(1)}, bf16[128,256]{1,0:T(8,128)(2,1)S(1)}, u32[]{:S(2)}, u32[]{:S(2)}) collective-permute-start(bf16[128,256]{1,0:T(8,128)(2,1)S(1)} %shard_map.116.refs_0_), channel_id=1, source_target_pairs={{0,16},{4,20},{8,24},{12,28},{16,0},{20,4},{24,8},{28,12},{1,17},{... | collective-permute-start | bytes 196616 | tf_op jit(solution)/shard_map/ppermute | solution.py:55
  21.5 1.4 %collective-permute-start.7 = (bf16[272,256]{1,0:T(8,128)(2,1)S(1)}, bf16[272,256]{1,0:T(8,128)(2,1)S(1)}, u32[]{:S(2)}, u32[]{:S(2)}) collective-permute-start(bf16[272,256]{1,0:T(8,128)(2,1)S(1)} %shard_map.121.refs_1_), channel_id=1, source_target_pairs={{0,4},{4,0},{8,12},{12,8},{16,20},{20,16},{24,28},{28,24},{1,5},{5... | collective-permute-start | bytes 417800 | tf_op jit(solution)/shard_map/ppermute | solution.py:60
  23.0 4.2 %collective-permute-start.15 = (bf16[272,256]{1,0:T(8,128)(2,1)S(1)}, bf16[272,256]{1,0:T(8,128)(2,1)S(1)}, u32[]{:S(2)}, u32[]{:S(2)}) collective-permute-start(bf16[272,256]{1,0:T(8,128)(2,1)S(1)} %shard_map.122.after_ref.refs_1_), channel_id=1, source_target_pairs={{0,0},{1,1},{2,2},{3,3},{4,5},{5,4},{6,7},{7,6},{8,8},{9,9},{10,10... | collective-permute-start | bytes 417800 | tf_op jit(solution)/shard_map/ppermute | solution.py:67
  23.7 5.2 %collective-permute-start.8 = (bf16[128,256]{1,0:T(8,128)(2,1)S(1)}, bf16[128,256]{1,0:T(8,128)(2,1)S(1)}, u32[]{:S(2)}, u32[]{:S(2)}) collective-permute-start(bf16[128,256]{1,0:T(8,128)(2,1)S(1)} %get-tuple-element.19.grad_ref.refs_3_), channel_id=1, source_target_pairs={{0,24},{4,28},{8,16},{12,20},{16,8},{20,12},{24,0},{28,4},{1,25},{... | collective-permute-start | bytes 196616 | tf_op jit(solution)/shard_map/ppermute | solution.py:55
  25.2 4.8 %collective-permute-start.9 = (bf16[128,256]{1,0:T(8,128)(2,1)S(1)}, bf16[128,256]{1,0:T(8,128)(2,1)S(1)}, u32[]{:S(2)}, u32[]{:S(2)}) collective-permute-start(bf16[128,256]{1,0:T(8,128)(2,1)S(1)} %get-tuple-element.19.grad_ref.refs_3_), channel_id=1, source_target_pairs={{0,8},{4,12},{8,0},{12,4},{16,24},{20,28},{24,16},{28,20},{1,9},{5... | collective-permute-start | bytes 196616 | tf_op jit(solution)/shard_map/ppermute | solution.py:55
  25.7 4.4 %collective-permute-start.10 = (bf16[128,256]{1,0:T(8,128)(2,1)S(1)}, bf16[128,256]{1,0:T(8,128)(2,1)S(1)}, u32[]{:S(2)}, u32[]{:S(2)}) collective-permute-start(bf16[128,256]{1,0:T(8,128)(2,1)S(1)} %get-tuple-element.19.grad_ref.refs_3_), channel_id=1, source_target_pairs={{0,16},{4,20},{8,24},{12,28},{16,0},{20,4},{24,8},{28,12},{1,17},{... | collective-permute-start | bytes 196616 | tf_op jit(solution)/shard_map/ppermute | solution.py:55
  27.3 5.7 %collective-permute-start.16 = (bf16[272,256]{1,0:T(8,128)(2,1)S(1)}, bf16[272,256]{1,0:T(8,128)(2,1)S(1)}, u32[]{:S(2)}, u32[]{:S(2)}) collective-permute-start(bf16[272,256]{1,0:T(8,128)(2,1)S(1)} %shard_map.130.refs_1_), channel_id=1, source_target_pairs={{0,0},{1,1},{2,2},{3,3},{4,6},{5,7},{6,4},{7,5},{8,8},{9,9},{10,10... | collective-permute-start | bytes 417800 | tf_op jit(solution)/shard_map/ppermute | solution.py:67
  30.1 4.3 %collective-permute-start.11 = (bf16[512,256]{1,0:T(8,128)(2,1)S(1)}, bf16[512,256]{1,0:T(8,128)(2,1)S(1)}, u32[]{:S(2)}, u32[]{:S(2)}) collective-permute-start(bf16[512,256]{1,0:T(8,128)(2,1)S(1)} %shard_map.123.source_ref), channel_id=1, source_target_pairs={{0,4},{4,0},{8,12},{12,8},{16,20},{20,16},{24,28},{28,24},{1,5},{5... | collective-permute-start | bytes 786440 | tf_op jit(solution)/shard_map/ppermute | solution.py:60
  33.1 6.7 %collective-permute-start.17 = (bf16[272,256]{1,0:T(8,128)(2,1)S(1)}, bf16[272,256]{1,0:T(8,128)(2,1)S(1)}, u32[]{:S(2)}, u32[]{:S(2)}) collective-permute-start(bf16[272,256]{1,0:T(8,128)(2,1)S(1)} %shard_map.131.refs_1_), channel_id=1, source_target_pairs={{0,0},{4,12},{8,8},{12,4},{16,16},{20,28},{24,24},{28,20},{1,1},{5... | collective-permute-start | bytes 417800 | tf_op jit(solution)/shard_map/ppermute | solution.py:67
  34.6 6.2 %collective-permute-start.12 = (bf16[128,256]{1,0:T(8,128)(2,1)S(1)}, bf16[128,256]{1,0:T(8,128)(2,1)S(1)}, u32[]{:S(2)}, u32[]{:S(2)}) collective-permute-start(bf16[128,256]{1,0:T(8,128)(2,1)S(1)} %shard_map.125.refs_0_), channel_id=1, source_target_pairs={{0,3},{1,2},{2,1},{3,0},{4,7},{5,6},{6,5},{7,4},{8,11},{9,10},{10,... | collective-permute-start | bytes 196616 | tf_op jit(solution)/shard_map/ppermute | solution.py:55
  36.8 4.6 %collective-permute-start.13 = (bf16[128,256]{1,0:T(8,128)(2,1)S(1)}, bf16[128,256]{1,0:T(8,128)(2,1)S(1)}, u32[]{:S(2)}, u32[]{:S(2)}) collective-permute-start(bf16[128,256]{1,0:T(8,128)(2,1)S(1)} %shard_map.126.refs_0_), channel_id=1, source_target_pairs={{0,1},{1,0},{2,3},{3,2},{4,5},{5,4},{6,7},{7,6},{8,9},{9,8},{10,11... | collective-permute-start | bytes 196616 | tf_op jit(solution)/shard_map/ppermute | solution.py:55
  37.1 5.2 %collective-permute-start.14 = (bf16[128,256]{1,0:T(8,128)(2,1)S(1)}, bf16[128,256]{1,0:T(8,128)(2,1)S(1)}, u32[]{:S(2)}, u32[]{:S(2)}) collective-permute-start(bf16[128,256]{1,0:T(8,128)(2,1)S(1)} %shard_map.127.refs_0_), channel_id=1, source_target_pairs={{0,2},{1,3},{2,0},{3,1},{4,6},{5,7},{6,4},{7,5},{8,10},{9,11},{10,... | collective-permute-start | bytes 196616 | tf_op jit(solution)/shard_map/ppermute | solution.py:55
  39.8 3.3 %collective-permute-start.18 = (bf16[272,256]{1,0:T(8,128)(2,1)S(1)}, bf16[272,256]{1,0:T(8,128)(2,1)S(1)}, u32[]{:S(2)}, u32[]{:S(2)}) collective-permute-start(bf16[272,256]{1,0:T(8,128)(2,1)S(1)} %shard_map.132.refs_1_), channel_id=1, source_target_pairs={{0,0},{4,20},{8,8},{12,28},{16,16},{20,4},{24,24},{28,12},{1,1},{5... | collective-permute-start | bytes 417800 | tf_op jit(solution)/shard_map/ppermute | solution.py:67
  43.2 9.6 %collective-permute-start.19 = (f32[264,256]{1,0:T(8,128)S(1)}, f32[264,256]{1,0:T(8,128)S(1)}, u32[]{:S(2)}, u32[]{:S(2)}) collective-permute-start(f32[264,256]{1,0:T(8,128)S(1)} %shard_map.133.own_ref), channel_id=1, source_target_pairs={{0,4},{4,0},{8,12},{12,8},{16,20},{20,16},{24,28},{28,24},{1,5},{5... | collective-permute-start | bytes 811016 | tf_op jit(solution)/shard_map/ppermute | solution.py:60

commit v10 on v8

--- a/solution.py
+++ b/solution.py
@@ -13,8 +13,9 @@
 CUBIC = 0.044715
 VMEM_LIMIT = 48 * 1024 * 1024
 BIAS_ROWS = 16
-ROW_SUM_WEIGHT = 250
-FEATURES_WEIGHT = 150
+BACK_SUM_WEIGHT = 30
+ROW_SUM_WEIGHT = 120
+FEATURES_WEIGHT = 100
 
 VMEM_SPEC = pl.BlockSpec(memory_space=pltpu.VMEM)
 HBM_SPEC = pl.BlockSpec(memory_space=pltpu.HBM)
@@ -40,7 +41,7 @@
 
 
 def far_first(count):
-    return list(dict.fromkeys([count - 1, *range(1, count), 0]))
+    return list(range(count - 1, -1, -1))
 
 
 def pairs_of(k, size, cores):
@@ -281,10 +282,16 @@
     out_ref[...] = back_ref[rows, :].astype(BF16)
 
 
-def features_kernel(weight_ref, *refs):
-    parts, out_ref = refs[:-1], refs[-1]
+def back_sum_kernel(*refs):
+    total = refs[0][...].astype(F32)
+    for ref in refs[1:-1]:
+        total += ref[...].astype(F32)
+    refs[-1][...] = total
+
+
+def features_kernel(weight_ref, most_ref, last_ref, out_ref):
     out_ref[...] = lax.dot_general(
-        summed(parts).astype(BF16),
+        (most_ref[...] + last_ref[...].astype(F32)).astype(BF16),
         weight_ref[...],
         (((1,), (1,)), ((), ())),
         preferred_element_type=F32,
@@ -478,24 +485,32 @@
         )(*piece_args, *before)
 
     backs = exchange(in_turn(n_row, back_piece), "row", n_row)
+    most = call(
+        back_sum_kernel,
+        like(tile, hidden, F32),
+        [VMEM_SPEC] * (n_row - 1),
+        [],
+        BACK_SUM_WEIGHT * matrix,
+        n_row * block_bytes,
+    )(*backs[:-2], backs[-1])
     grad_features = call(
         features_kernel,
         like(tile, width),
-        [VMEM_SPEC] * (1 + n_row),
+        [VMEM_SPEC] * 3,
         [],
         FEATURES_WEIGHT * matrix,
         n_row * block_bytes,
-    )(weight, *backs)
+    )(weight, most, backs[-2])
     all_terms = total_over(row_term, add, "col", n_col, 2)
     factor = (tile * n_row * n_col) ** (-0.5)
     own_half, bias_grad = call(
         functools.partial(scale_kernel, factor=factor),
         (like(half, hidden, F32), like(1, hidden, F32)),
-        [HBM_SPEC] + [VMEM_SPEC] * len(all_terms),
+        [VMEM_SPEC] * (1 + len(all_terms)),
         [],
         len(all_terms) * half * hidden,
         len(all_terms) * half * hidden * 2,
-    )(pltpu.with_memory_space_constraint(grad_features, pltpu.HBM), *all_terms)
+    )(most, *all_terms)
     other_half = swap_cores(own_half, n_col)
     grad_weight, grad_bias = call(
         join_kernel,

time: 47.8 us -> 46 us (0.962)
  waiting for transfers between devices: 16.6 us -> 14.9 us
    ppermute x4, waiting for transfers between devices: 3.18 us -> 2.48 us  [swap_cores(): return lax.ppermute(block, 'col', [(i, i ^ 1) for i in range(size)])]
    ppermute x4, starting transfers between devices: 5.08 us -> 5.62 us  [total_over(): terms = [lax.ppermute(block, axis, pairs_of(step, size, cores)), block]]
    ppermute x4, waiting for transfers between devices: 3.84 us -> 3.32 us  [total_over(): terms = [lax.ppermute(block, axis, pairs_of(step, size, cores)), block]]
    ppermute x12, waiting for transfers between devices: 9.62 us -> 9.13 us  [exchange(): lax.ppermute(blocks[k], axis, pairs)]
  transfers between devices with their start and end apart: 20 -> 20, of which waited for: 16 -> 13; matrix products, arithmetic and copies ran while one was open for 0% -> 0% of each run, Pallas kernels for 10% -> 11%
where the time goes in v10:
time: 46 us; the launch traced here: 45.8 us
  starting transfers between devices  22.9 us (50%)
  waiting for transfers between devices  14.9 us (32%)
  Pallas kernels  6.44 us (14%)
  between operations  1.5 us (3%)
    ppermute x12, starting transfers between devices, exchange(): lax.ppermute(blocks[k], axis, pairs)  17 us
    ppermute x12, waiting for transfers between devices, exchange(): lax.ppermute(blocks[k], axis, pairs)  9.13 us
    ppermute x4, starting transfers between devices, total_over(): terms = [lax.ppermute(block, axis, pairs_of(step, size, cores)), block]  5.62 us
    ppermute x4, waiting for transfers between devices, total_over(): terms = [lax.ppermute(block, axis, pairs_of(step, size, cores)), block]  3.32 us
    ppermute x4, waiting for transfers between devices, swap_cores(): return lax.ppermute(block, 'col', [(i, i ^ 1) for i in range(size)])  2.48 us
    pallas_call x1, Pallas kernels, local(): call(dense_kernel, (like(row_nodes, col_nodes), like(1, hidden, F32)), [S...  1.45 us
  transfers between devices with their start and end apart: 20, of which 13 were waited for; matrix products, arithmetic and copies ran while one was open for 0% of the time, Pallas kernels for 11%

profile of v10, /device:TPU:0, one launch (start us, length us, event | category | flops | bytes accessed | tf_op | source)
XLA Modules:
  0.0 45.8 jit_solution(1898268817529454985)
XLA Ops:
  0.6 5.1 %collective-permute-start = (bf16[128,256]{1,0:T(8,128)(2,1)}, bf16[128,256]{1,0:T(8,128)(2,1)S(1)}, u32[]{:S(2)}, u32[]{:S(2)}) collective-permute-start(bf16[128,256]{1,0:T(8,128)(2,1)} %refs_3_.1), channel_id=1, source_target_pairs={{0,3},{1,2},{2,1},{3,0},{4,7},{5,6},{6,5},{7,4},{8,11},{9,10},{10,... | collective-permute-start | bytes 196616 | tf_op jit(solution)/shard_map/ppermute | solution.py:56
  5.8 0.6 %collective-permute-start.2 = (bf16[128,256]{1,0:T(8,128)(2,1)}, bf16[128,256]{1,0:T(8,128)(2,1)S(1)}, u32[]{:S(2)}, u32[]{:S(2)}) collective-permute-start(bf16[128,256]{1,0:T(8,128)(2,1)} %refs_3_.1), channel_id=1, source_target_pairs={{0,1},{1,0},{2,3},{3,2},{4,5},{5,4},{6,7},{7,6},{8,9},{9,8},{10,11... | collective-permute-start | bytes 196616 | tf_op jit(solution)/shard_map/ppermute | solution.py:56
  7.1 1.5 %shard_map.111 = (bf16[1024,512]{1,0:T(8,128)(2,1)S(1)}, f32[1,256]{1,0:T(1,128)S(1)}) custom-call(s32[1,1]{1,0:T(1,128)S(6)} %copy.12.count_ref, s32[1,1,32]{2,1,0:T(1,128)} %row_hbm.1, s32[1,1,32]{2,1,0:T(1,128)} %col_hbm.1, bf16[1,1,32,128,128]{4,3,2,1,0:T(8,128)(2,1)} %tiles_hbm.1, f32[1,256]{1,0:T(1,128)} %bitcast.2), custom_call_target="tpu_custom_call" | custom-call | bytes 6291456 | tf_op jit(solution)/shard_map/pallas_call | solution.py:348
  8.6 3.0 %collective-permute-done.1.refs_1_ = bf16[128,256]{1,0:T(8,128)(2,1)S(1)} collective-permute-done((bf16[128,256]{1,0:T(8,128)(2,1)}, bf16[128,256]{1,0:T(8,128)(2,1)S(1)}, u32[]{:S(2)}, u32[]{:S(2)}) %collective-permute-start.1) | collective-permute-done | bytes 65568 | tf_op jit(solution)/shard_map/ppermute | solution.py:56
  11.6 0.3 shard_map.112
  12.3 1.2 %collective-permute-done.3.other_ref = bf16[512,256]{1,0:T(8,128)(2,1)S(1)} collective-permute-done((bf16[512,256]{1,0:T(8,128)(2,1)S(1)}, bf16[512,256]{1,0:T(8,128)(2,1)S(1)}, u32[]{:S(2)}, u32[]{:S(2)}) %collective-permute-start.3) | collective-permute-done | bytes 262176 | tf_op jit(solution)/shard_map/ppermute | solution.py:61
  13.5 2.5 %collective-permute-start.4 = (bf16[128,256]{1,0:T(8,128)(2,1)S(1)}, bf16[128,256]{1,0:T(8,128)(2,1)S(1)}, u32[]{:S(2)}, u32[]{:S(2)}) collective-permute-start(bf16[128,256]{1,0:T(8,128)(2,1)S(1)} %shard_map.114.refs_0_), channel_id=1, source_target_pairs={{0,24},{4,28},{8,16},{12,20},{16,8},{20,12},{24,0},{28,4},{1,25},{... | collective-permute-start | bytes 196616 | tf_op jit(solution)/shard_map/ppermute | solution.py:56
  16.1 0.6 %collective-permute-start.5 = (bf16[128,256]{1,0:T(8,128)(2,1)S(1)}, bf16[128,256]{1,0:T(8,128)(2,1)S(1)}, u32[]{:S(2)}, u32[]{:S(2)}) collective-permute-start(bf16[128,256]{1,0:T(8,128)(2,1)S(1)} %shard_map.115.refs_0_), channel_id=1, source_target_pairs={{0,16},{4,20},{8,24},{12,28},{16,0},{20,4},{24,8},{28,12},{1,17},{... | collective-permute-start | bytes 196616 | tf_op jit(solution)/shard_map/ppermute | solution.py:56
  16.7 0.6 %collective-permute-start.6 = (bf16[128,256]{1,0:T(8,128)(2,1)S(1)}, bf16[128,256]{1,0:T(8,128)(2,1)S(1)}, u32[]{:S(2)}, u32[]{:S(2)}) collective-permute-start(bf16[128,256]{1,0:T(8,128)(2,1)S(1)} %shard_map.116.refs_0_), channel_id=1, source_target_pairs={{0,8},{4,12},{8,0},{12,4},{16,24},{20,28},{24,16},{28,20},{1,9},{5... | collective-permute-start | bytes 196616 | tf_op jit(solution)/shard_map/ppermute | solution.py:56
  17.3 1.5 %collective-permute-done.4.refs_0_ = bf16[128,256]{1,0:T(8,128)(2,1)S(1)} collective-permute-done((bf16[128,256]{1,0:T(8,128)(2,1)S(1)}, bf16[128,256]{1,0:T(8,128)(2,1)S(1)}, u32[]{:S(2)}, u32[]{:S(2)}) %collective-permute-start.4) | collective-permute-done | bytes 65568 | tf_op jit(solution)/shard_map/ppermute | solution.py:56
  18.8 1.6 %collective-permute-done.5.refs_1_ = bf16[128,256]{1,0:T(8,128)(2,1)S(1)} collective-permute-done((bf16[128,256]{1,0:T(8,128)(2,1)S(1)}, bf16[128,256]{1,0:T(8,128)(2,1)S(1)}, u32[]{:S(2)}, u32[]{:S(2)}) %collective-permute-start.5) | collective-permute-done | bytes 65568 | tf_op jit(solution)/shard_map/ppermute | solution.py:56
  20.4 0.6 %collective-permute-done.6.refs_2_ = bf16[128,256]{1,0:T(8,128)(2,1)S(1)} collective-permute-done((bf16[128,256]{1,0:T(8,128)(2,1)S(1)}, bf16[128,256]{1,0:T(8,128)(2,1)S(1)}, u32[]{:S(2)}, u32[]{:S(2)}) %collective-permute-start.6) | collective-permute-done | bytes 65568 | tf_op jit(solution)/shard_map/ppermute | solution.py:56
  21.6 1.3 %collective-permute-done.7.refs_0_ = bf16[144,256]{1,0:T(8,128)(2,1)S(1)} collective-permute-done((bf16[144,256]{1,0:T(8,128)(2,1)S(1)}, bf16[144,256]{1,0:T(8,128)(2,1)S(1)}, u32[]{:S(2)}, u32[]{:S(2)}) %collective-permute-start.7) | collective-permute-done | bytes 73760 | tf_op jit(solution)/shard_map/ppermute | solution.py:61
  22.9 1.1 %collective-permute-start.15 = (bf16[144,256]{1,0:T(8,128)(2,1)S(1)}, bf16[144,256]{1,0:T(8,128)(2,1)S(1)}, u32[]{:S(2)}, u32[]{:S(2)}) collective-permute-start(bf16[144,256]{1,0:T(8,128)(2,1)S(1)} %shard_map.122.after_ref.refs_1_), channel_id=1, source_target_pairs={{0,1},{1,0},{2,3},{3,2},{4,5},{5,4},{6,7},{7,6},{8,9},{9,8},{10,11... | collective-permute-start | bytes 221192 | tf_op jit(solution)/shard_map/ppermute | solution.py:71
  24.0 1.5 %collective-permute-start.8 = (bf16[128,256]{1,0:T(8,128)(2,1)S(1)}, bf16[128,256]{1,0:T(8,128)(2,1)S(1)}, u32[]{:S(2)}, u32[]{:S(2)}) collective-permute-start(bf16[128,256]{1,0:T(8,128)(2,1)S(1)} %get-tuple-element.23.grad_ref.refs_3_), channel_id=1, source_target_pairs={{0,24},{4,28},{8,16},{12,20},{16,8},{20,12},{24,0},{28,4},{1,25},{... | collective-permute-start | bytes 196616 | tf_op jit(solution)/shard_map/ppermute | solution.py:56
  25.5 0.5 %collective-permute-start.9 = (bf16[128,256]{1,0:T(8,128)(2,1)S(1)}, bf16[128,256]{1,0:T(8,128)(2,1)S(1)}, u32[]{:S(2)}, u32[]{:S(2)}) collective-permute-start(bf16[128,256]{1,0:T(8,128)(2,1)S(1)} %get-tuple-element.23.grad_ref.refs_3_), channel_id=1, source_target_pairs={{0,16},{4,20},{8,24},{12,28},{16,0},{20,4},{24,8},{28,12},{1,17},{... | collective-permute-start | bytes 196616 | tf_op jit(solution)/shard_map/ppermute | solution.py:56
  26.1 1.5 %collective-permute-start.10 = (bf16[128,256]{1,0:T(8,128)(2,1)S(1)}, bf16[128,256]{1,0:T(8,128)(2,1)S(1)}, u32[]{:S(2)}, u32[]{:S(2)}) collective-permute-start(bf16[128,256]{1,0:T(8,128)(2,1)S(1)} %get-tuple-element.23.grad_ref.refs_3_), channel_id=1, source_target_pairs={{0,8},{4,12},{8,0},{12,4},{16,24},{20,28},{24,16},{28,20},{1,9},{5... | collective-permute-start | bytes 196616 | tf_op jit(solution)/shard_map/ppermute | solution.py:56
  27.6 2.3 %collective-permute-start.16 = (bf16[144,256]{1,0:T(8,128)(2,1)S(1)}, bf16[144,256]{1,0:T(8,128)(2,1)S(1)}, u32[]{:S(2)}, u32[]{:S(2)}) collective-permute-start(bf16[144,256]{1,0:T(8,128)(2,1)S(1)} %shard_map.131.refs_1_), channel_id=1, source_target_pairs={{0,2},{1,3},{2,0},{3,1},{4,6},{5,7},{6,4},{7,5},{8,10},{9,11},{10,... | collective-permute-start | bytes 221192 | tf_op jit(solution)/shard_map/ppermute | solution.py:71
  29.8 0.4 collective-permute-done.9.refs_1_
  30.4 0.3 shard_map.120.turned_ref
  30.8 2.9 %collective-permute-done.16.refs_0_ = bf16[144,256]{1,0:T(8,128)(2,1)S(1)} collective-permute-done((bf16[144,256]{1,0:T(8,128)(2,1)S(1)}, bf16[144,256]{1,0:T(8,128)(2,1)S(1)}, u32[]{:S(2)}, u32[]{:S(2)}) %collective-permute-start.16) | collective-permute-done | bytes 73760 | tf_op jit(solution)/shard_map/ppermute | solution.py:71
  33.7 0.6 %collective-permute-start.17 = (bf16[144,256]{1,0:T(8,128)(2,1)S(1)}, bf16[144,256]{1,0:T(8,128)(2,1)S(1)}, u32[]{:S(2)}, u32[]{:S(2)}) collective-permute-start(bf16[144,256]{1,0:T(8,128)(2,1)S(1)} %shard_map.132.refs_1_), channel_id=1, source_target_pairs={{0,8},{4,12},{8,0},{12,4},{16,24},{20,28},{24,16},{28,20},{1,9},{5... | collective-permute-start | bytes 221192 | tf_op jit(solution)/shard_map/ppermute | solution.py:71
  34.3 0.3 shard_map.124.own_ref
  34.8 2.6 %collective-permute-start.12 = (bf16[128,256]{1,0:T(8,128)(2,1)S(1)}, bf16[128,256]{1,0:T(8,128)(2,1)S(1)}, u32[]{:S(2)}, u32[]{:S(2)}) collective-permute-start(bf16[128,256]{1,0:T(8,128)(2,1)S(1)} %shard_map.125.refs_0_), channel_id=1, source_target_pairs={{0,3},{1,2},{2,1},{3,0},{4,7},{5,6},{6,5},{7,4},{8,11},{9,10},{10,... | collective-permute-start | bytes 196616 | tf_op jit(solution)/shard_map/ppermute | solution.py:56
  37.7 0.4 collective-permute-done.17.refs_0_
  38.1 1.6 %collective-permute-start.18 = (bf16[144,256]{1,0:T(8,128)(2,1)S(1)}, bf16[144,256]{1,0:T(8,128)(2,1)S(1)}, u32[]{:S(2)}, u32[]{:S(2)}) collective-permute-start(bf16[144,256]{1,0:T(8,128)(2,1)S(1)} %shard_map.133.refs_1_), channel_id=1, source_target_pairs={{0,16},{4,20},{8,24},{12,28},{16,0},{20,4},{24,8},{28,12},{1,17},{... | collective-permute-start | bytes 221192 | tf_op jit(solution)/shard_map/ppermute | solution.py:71
  39.9 1.5 %collective-permute-start.14 = (bf16[128,256]{1,0:T(8,128)(2,1)S(1)}, bf16[128,256]{1,0:T(8,128)(2,1)S(1)}, u32[]{:S(2)}, u32[]{:S(2)}) collective-permute-start(bf16[128,256]{1,0:T(8,128)(2,1)S(1)} %shard_map.127.refs_0_), channel_id=1, source_target_pairs={{0,1},{1,0},{2,3},{3,2},{4,5},{5,4},{6,7},{7,6},{8,9},{9,8},{10,11... | collective-permute-start | bytes 196616 | tf_op jit(solution)/shard_map/ppermute | solution.py:56
  41.4 0.6 %shard_map.119 = bf16[128,256]{1,0:T(8,128)(2,1)} custom-call(bf16[128,256]{1,0:T(8,128)(2,1)S(1)} %get-tuple-element.21.in_ref), custom_call_target="tpu_custom_call" | custom-call | bytes 131072 | tf_op jit(solution)/shard_map/pallas_call | solution.py:434
  42.2 0.7 %collective-permute-done.13.refs_1_ = bf16[128,256]{1,0:T(8,128)(2,1)S(1)} collective-permute-done((bf16[128,256]{1,0:T(8,128)(2,1)S(1)}, bf16[128,256]{1,0:T(8,128)(2,1)S(1)}, u32[]{:S(2)}, u32[]{:S(2)}) %collective-permute-start.13) | collective-permute-done | bytes 65568 | tf_op jit(solution)/shard_map/ppermute | solution.py:56
  43.1 1.2 %collective-permute-done.14.last_ref = bf16[128,256]{1,0:T(8,128)(2,1)S(1)} collective-permute-done((bf16[128,256]{1,0:T(8,128)(2,1)S(1)}, bf16[128,256]{1,0:T(8,128)(2,1)S(1)}, u32[]{:S(2)}, u32[]{:S(2)}) %collective-permute-start.14) | collective-permute-done | bytes 65568 | tf_op jit(solution)/shard_map/ppermute | solution.py:56
  44.3 0.8 %shard_map.130 = bf16[128,256]{1,0:T(8,128)(2,1)} custom-call(bf16[256,256]{1,0:T(8,128)(2,1)S(1)} %copy-done, f32[128,256]{1,0:T(8,128)S(1)} %shard_map.129.most_ref.after_ref, bf16[128,256]{1,0:T(8,128)(2,1)S(1)} %collective-permute-done.14.last_ref), custom_call_target="tpu_custom_call" | custom-call | flops 1677721600 | bytes 262144 | tf_op jit(solution)/shard_map/pallas_call | solution.py:496
  45.1 0.7 %shard_map.135 = (f32[256,256]{1,0:T(8,128)}, f32[1,256]{1,0:T(1,128)}) custom-call(f32[128,256]{1,0:T(8,128)S(1)} %get-tuple-element.26.own_ref, f32[128,256]{1,0:T(8,128)S(1)} %collective-permute-done.19.other_ref, f32[1,256]{1,0:T(1,128)S(1)} %get-tuple-element.27.bias_ref), custom_call_target="tpu_custom_call" | custom-call | bytes 524288 | tf_op jit(solution)/shard_map/pallas_call | solution.py:515
  (39 shorter events, 2.4 us)
Async XLA Ops:
  0.6 7.9 %collective-permute-start = (bf16[128,256]{1,0:T(8,128)(2,1)}, bf16[128,256]{1,0:T(8,128)(2,1)S(1)}, u32[]{:S(2)}, u32[]{:S(2)}) collective-permute-start(bf16[128,256]{1,0:T(8,128)(2,1)} %refs_3_.1), channel_id=1, source_target_pairs={{0,3},{1,2},{2,1},{3,0},{4,7},{5,6},{6,5},{7,4},{8,11},{9,10},{10,... | collective-permute-start | bytes 196616 | tf_op jit(solution)/shard_map/ppermute | solution.py:56
  5.7 5.8 %collective-permute-start.1 = (bf16[128,256]{1,0:T(8,128)(2,1)}, bf16[128,256]{1,0:T(8,128)(2,1)S(1)}, u32[]{:S(2)}, u32[]{:S(2)}) collective-permute-start(bf16[128,256]{1,0:T(8,128)(2,1)} %refs_3_.1), channel_id=1, source_target_pairs={{0,2},{1,3},{2,0},{3,1},{4,6},{5,7},{6,4},{7,5},{8,10},{9,11},{10,... | collective-permute-start | bytes 196616 | tf_op jit(solution)/shard_map/ppermute | solution.py:56
  5.8 5.8 %collective-permute-start.2 = (bf16[128,256]{1,0:T(8,128)(2,1)}, bf16[128,256]{1,0:T(8,128)(2,1)S(1)}, u32[]{:S(2)}, u32[]{:S(2)}) collective-permute-start(bf16[128,256]{1,0:T(8,128)(2,1)} %refs_3_.1), channel_id=1, source_target_pairs={{0,1},{1,0},{2,3},{3,2},{4,5},{5,4},{6,7},{7,6},{8,9},{9,8},{10,11... | collective-permute-start | bytes 196616 | tf_op jit(solution)/shard_map/ppermute | solution.py:56
  7.0 4.5 %copy-start.1 = (bf16[128,256]{1,0:T(8,128)(2,1)S(1)}, bf16[128,256]{1,0:T(8,128)(2,1)}, u32[]{:S(2)}) copy-start(bf16[128,256]{1,0:T(8,128)(2,1)} %refs_3_.1) | copy-start | bytes 196612
  11.9 1.6 %collective-permute-start.3 = (bf16[512,256]{1,0:T(8,128)(2,1)S(1)}, bf16[512,256]{1,0:T(8,128)(2,1)S(1)}, u32[]{:S(2)}, u32[]{:S(2)}) collective-permute-start(bf16[512,256]{1,0:T(8,128)(2,1)S(1)} %get-tuple-element.20), channel_id=1, source_target_pairs={{0,4},{4,0},{8,12},{12,8},{16,20},{20,16},{24,28},{28,24},{1,5},{5... | collective-permute-start | bytes 786440 | tf_op jit(solution)/shard_map/ppermute | solution.py:61
  13.5 5.2 %collective-permute-start.4 = (bf16[128,256]{1,0:T(8,128)(2,1)S(1)}, bf16[128,256]{1,0:T(8,128)(2,1)S(1)}, u32[]{:S(2)}, u32[]{:S(2)}) collective-permute-start(bf16[128,256]{1,0:T(8,128)(2,1)S(1)} %shard_map.114.refs_0_), channel_id=1, source_target_pairs={{0,24},{4,28},{8,16},{12,20},{16,8},{20,12},{24,0},{28,4},{1,25},{... | collective-permute-start | bytes 196616 | tf_op jit(solution)/shard_map/ppermute | solution.py:56
  16.1 4.3 %collective-permute-start.5 = (bf16[128,256]{1,0:T(8,128)(2,1)S(1)}, bf16[128,256]{1,0:T(8,128)(2,1)S(1)}, u32[]{:S(2)}, u32[]{:S(2)}) collective-permute-start(bf16[128,256]{1,0:T(8,128)(2,1)S(1)} %shard_map.115.refs_0_), channel_id=1, source_target_pairs={{0,16},{4,20},{8,24},{12,28},{16,0},{20,4},{24,8},{28,12},{1,17},{... | collective-permute-start | bytes 196616 | tf_op jit(solution)/shard_map/ppermute | solution.py:56
  16.6 4.4 %copy-start = (bf16[256,256]{1,0:T(8,128)(2,1)S(1)}, bf16[256,256]{1,0:T(8,128)(2,1)}, u32[]{:S(2)}) copy-start(bf16[256,256]{1,0:T(8,128)(2,1)} %weight_ref.3) | copy-start | bytes 393220
  16.7 4.3 %copy-start.2 = (bf16[128,256]{1,0:T(8,128)(2,1)S(1)}, bf16[128,256]{1,0:T(8,128)(2,1)}, u32[]{:S(2)}) copy-start(bf16[128,256]{1,0:T(8,128)(2,1)} %cot_ref.1) | copy-start | bytes 196612
  16.7 4.3 %collective-permute-start.6 = (bf16[128,256]{1,0:T(8,128)(2,1)S(1)}, bf16[128,256]{1,0:T(8,128)(2,1)S(1)}, u32[]{:S(2)}, u32[]{:S(2)}) collective-permute-start(bf16[128,256]{1,0:T(8,128)(2,1)S(1)} %shard_map.116.refs_0_), channel_id=1, source_target_pairs={{0,8},{4,12},{8,0},{12,4},{16,24},{20,28},{24,16},{28,20},{1,9},{5... | collective-permute-start | bytes 196616 | tf_op jit(solution)/shard_map/ppermute | solution.py:56
  21.5 1.3 %collective-permute-start.7 = (bf16[144,256]{1,0:T(8,128)(2,1)S(1)}, bf16[144,256]{1,0:T(8,128)(2,1)S(1)}, u32[]{:S(2)}, u32[]{:S(2)}) collective-permute-start(bf16[144,256]{1,0:T(8,128)(2,1)S(1)} %get-tuple-element.24), channel_id=1, source_target_pairs={{0,4},{4,0},{8,12},{12,8},{16,20},{20,16},{24,28},{28,24},{1,5},{5... | collective-permute-start | bytes 221192 | tf_op jit(solution)/shard_map/ppermute | solution.py:61
  22.9 4.6 %collective-permute-start.15 = (bf16[144,256]{1,0:T(8,128)(2,1)S(1)}, bf16[144,256]{1,0:T(8,128)(2,1)S(1)}, u32[]{:S(2)}, u32[]{:S(2)}) collective-permute-start(bf16[144,256]{1,0:T(8,128)(2,1)S(1)} %shard_map.122.after_ref.refs_1_), channel_id=1, source_target_pairs={{0,1},{1,0},{2,3},{3,2},{4,5},{5,4},{6,7},{7,6},{8,9},{9,8},{10,11... | collective-permute-start | bytes 221192 | tf_op jit(solution)/shard_map/ppermute | solution.py:71
  24.0 5.8 %collective-permute-start.8 = (bf16[128,256]{1,0:T(8,128)(2,1)S(1)}, bf16[128,256]{1,0:T(8,128)(2,1)S(1)}, u32[]{:S(2)}, u32[]{:S(2)}) collective-permute-start(bf16[128,256]{1,0:T(8,128)(2,1)S(1)} %get-tuple-element.23.grad_ref.refs_3_), channel_id=1, source_target_pairs={{0,24},{4,28},{8,16},{12,20},{16,8},{20,12},{24,0},{28,4},{1,25},{... | collective-permute-start | bytes 196616 | tf_op jit(solution)/shard_map/ppermute | solution.py:56
  25.5 4.7 %collective-permute-start.9 = (bf16[128,256]{1,0:T(8,128)(2,1)S(1)}, bf16[128,256]{1,0:T(8,128)(2,1)S(1)}, u32[]{:S(2)}, u32[]{:S(2)}) collective-permute-start(bf16[128,256]{1,0:T(8,128)(2,1)S(1)} %get-tuple-element.23.grad_ref.refs_3_), channel_id=1, source_target_pairs={{0,16},{4,20},{8,24},{12,28},{16,0},{20,4},{24,8},{28,12},{1,17},{... | collective-permute-start | bytes 196616 | tf_op jit(solution)/shard_map/ppermute | solution.py:56
  26.1 4.3 %collective-permute-start.10 = (bf16[128,256]{1,0:T(8,128)(2,1)S(1)}, bf16[128,256]{1,0:T(8,128)(2,1)S(1)}, u32[]{:S(2)}, u32[]{:S(2)}) collective-permute-start(bf16[128,256]{1,0:T(8,128)(2,1)S(1)} %get-tuple-element.23.grad_ref.refs_3_), channel_id=1, source_target_pairs={{0,8},{4,12},{8,0},{12,4},{16,24},{20,28},{24,16},{28,20},{1,9},{5... | collective-permute-start | bytes 196616 | tf_op jit(solution)/shard_map/ppermute | solution.py:56
  27.6 6.1 %collective-permute-start.16 = (bf16[144,256]{1,0:T(8,128)(2,1)S(1)}, bf16[144,256]{1,0:T(8,128)(2,1)S(1)}, u32[]{:S(2)}, u32[]{:S(2)}) collective-permute-start(bf16[144,256]{1,0:T(8,128)(2,1)S(1)} %shard_map.131.refs_1_), channel_id=1, source_target_pairs={{0,2},{1,3},{2,0},{3,1},{4,6},{5,7},{6,4},{7,5},{8,10},{9,11},{10,... | collective-permute-start | bytes 221192 | tf_op jit(solution)/shard_map/ppermute | solution.py:71
  30.4 4.3 %collective-permute-start.11 = (bf16[512,256]{1,0:T(8,128)(2,1)S(1)}, bf16[512,256]{1,0:T(8,128)(2,1)S(1)}, u32[]{:S(2)}, u32[]{:S(2)}) collective-permute-start(bf16[512,256]{1,0:T(8,128)(2,1)S(1)} %shard_map.123.source_ref), channel_id=1, source_target_pairs={{0,4},{4,0},{8,12},{12,8},{16,20},{20,16},{24,28},{28,24},{1,5},{5... | collective-permute-start | bytes 786440 | tf_op jit(solution)/shard_map/ppermute | solution.py:61
  33.7 4.4 %collective-permute-start.17 = (bf16[144,256]{1,0:T(8,128)(2,1)S(1)}, bf16[144,256]{1,0:T(8,128)(2,1)S(1)}, u32[]{:S(2)}, u32[]{:S(2)}) collective-permute-start(bf16[144,256]{1,0:T(8,128)(2,1)S(1)} %shard_map.132.refs_1_), channel_id=1, source_target_pairs={{0,8},{4,12},{8,0},{12,4},{16,24},{20,28},{24,16},{28,20},{1,9},{5... | collective-permute-start | bytes 221192 | tf_op jit(solution)/shard_map/ppermute | solution.py:71
  34.8 7.4 %collective-permute-start.12 = (bf16[128,256]{1,0:T(8,128)(2,1)S(1)}, bf16[128,256]{1,0:T(8,128)(2,1)S(1)}, u32[]{:S(2)}, u32[]{:S(2)}) collective-permute-start(bf16[128,256]{1,0:T(8,128)(2,1)S(1)} %shard_map.125.refs_0_), channel_id=1, source_target_pairs={{0,3},{1,2},{2,1},{3,0},{4,7},{5,6},{6,5},{7,4},{8,11},{9,10},{10,... | collective-permute-start | bytes 196616 | tf_op jit(solution)/shard_map/ppermute | solution.py:56
  37.6 5.3 %collective-permute-start.13 = (bf16[128,256]{1,0:T(8,128)(2,1)S(1)}, bf16[128,256]{1,0:T(8,128)(2,1)S(1)}, u32[]{:S(2)}, u32[]{:S(2)}) collective-permute-start(bf16[128,256]{1,0:T(8,128)(2,1)S(1)} %shard_map.126.refs_0_), channel_id=1, source_target_pairs={{0,2},{1,3},{2,0},{3,1},{4,6},{5,7},{6,4},{7,5},{8,10},{9,11},{10,... | collective-permute-start | bytes 196616 | tf_op jit(solution)/shard_map/ppermute | solution.py:56
  38.1 4.8 %collective-permute-start.18 = (bf16[144,256]{1,0:T(8,128)(2,1)S(1)}, bf16[144,256]{1,0:T(8,128)(2,1)S(1)}, u32[]{:S(2)}, u32[]{:S(2)}) collective-permute-start(bf16[144,256]{1,0:T(8,128)(2,1)S(1)} %shard_map.133.refs_1_), channel_id=1, source_target_pairs={{0,16},{4,20},{8,24},{12,28},{16,0},{20,4},{24,8},{28,12},{1,17},{... | collective-permute-start | bytes 221192 | tf_op jit(solution)/shard_map/ppermute | solution.py:71
  39.9 4.3 %collective-permute-start.14 = (bf16[128,256]{1,0:T(8,128)(2,1)S(1)}, bf16[128,256]{1,0:T(8,128)(2,1)S(1)}, u32[]{:S(2)}, u32[]{:S(2)}) collective-permute-start(bf16[128,256]{1,0:T(8,128)(2,1)S(1)} %shard_map.127.refs_0_), channel_id=1, source_target_pairs={{0,1},{1,0},{2,3},{3,2},{4,5},{5,4},{6,7},{7,6},{8,9},{9,8},{10,11... | collective-permute-start | bytes 196616 | tf_op jit(solution)/shard_map/ppermute | solution.py:56
  43.0 2.1 %collective-permute-start.19 = (f32[128,256]{1,0:T(8,128)S(1)}, f32[128,256]{1,0:T(8,128)S(1)}, u32[]{:S(2)}, u32[]{:S(2)}) collective-permute-start(f32[128,256]{1,0:T(8,128)S(1)} %get-tuple-element.26.own_ref), channel_id=1, source_target_pairs={{0,4},{4,0},{8,12},{12,8},{16,20},{20,16},{24,28},{28,24},{1,5},{5... | collective-permute-start | bytes 393224 | tf_op jit(solution)/shard_map/ppermute | solution.py:61

commit v11 on v10

--- a/solution.py
+++ b/solution.py
@@ -22,12 +22,12 @@
 SMEM_SPEC = pl.BlockSpec(memory_space=pltpu.SMEM)
 
 
-def call(kernel, out_shape, in_specs, scratch, flops, moved):
+def call(kernel, out_shape, in_specs, scratch, flops, moved, out_spec=VMEM_SPEC):
     return pl.pallas_call(
         kernel,
         out_shape=out_shape,
         in_specs=in_specs,
-        out_specs=jax.tree.map(lambda _: VMEM_SPEC, out_shape),
+        out_specs=jax.tree.map(lambda _: out_spec, out_shape),
         scratch_shapes=scratch,
         compiler_params=pltpu.CompilerParams(vmem_limit_bytes=VMEM_LIMIT),
         cost_estimate=pl.CostEstimate(flops=flops, bytes_accessed=moved, transcendentals=0),
@@ -262,24 +262,24 @@
     out_ref[...] = dense_dot(turned_ref[:, : source_ref.shape[0]], source_ref[...])
 
 
-def back_piece_kernel(turned_ref, own_ref, source_ref, *refs, k, n_row):
-    out_ref = refs[-1]
-    rows = block_at(partner(row_index(), k, n_row), out_ref.shape[0])
-    rest = dense_dot(turned_ref[rows, source_ref.shape[0] :], source_ref[...])
-    out_ref[...] = (own_ref[rows, :] + rest).astype(BF16)
-
-
-def slot_back_kernel(count_ref, row_ref, col_ref, tiles_ref, own_ref, other_ref, out_ref, source_ref):
+def back_pieces_kernel(turned_ref, own_ref, source_ref, *outs):
+    tile = outs[0].shape[0]
+    for k, out_ref in zip(far_first(len(outs)), outs):
+        rows = block_at(partner(row_index(), k, len(outs)), tile)
+        rest = dense_dot(turned_ref[rows, source_ref.shape[0] :], source_ref[...])
+        out_ref[...] = (own_ref[rows, :] + rest).astype(BF16)
+
+
+def slot_back_kernel(count_ref, row_ref, col_ref, tiles_ref, own_ref, other_ref, *refs):
+    outs, (source_ref, acc_ref) = refs[:-2], refs[-2:]
     half = own_ref.shape[0]
     source_ref[:half, :] = own_ref[...]
     source_ref[half:, :] = other_ref[...]
-    slot_product((count_ref, row_ref, col_ref, tiles_ref), source_ref, out_ref, True)
-
-
-def slot_piece_kernel(back_ref, *refs, k, n_row):
-    out_ref = refs[-1]
-    rows = block_at(partner(row_index(), k, n_row), out_ref.shape[0])
-    out_ref[...] = back_ref[rows, :].astype(BF16)
+    slot_product((count_ref, row_ref, col_ref, tiles_ref), source_ref, acc_ref, True)
+    tile = outs[0].shape[0]
+    for k, out_ref in zip(far_first(len(outs)), outs):
+        rows = block_at(partner(row_index(), k, len(outs)), tile)
+        out_ref[...] = acc_ref[rows, :].astype(BF16)
 
 
 def back_sum_kernel(*refs):
@@ -298,11 +298,20 @@
     ).astype(BF16)
 
 
-def join_kernel(own_ref, other_ref, bias_ref, weight_ref, bias_out):
+def write_kernel(
+    features_ref, own_ref, other_ref, bias_ref, features_hbm, grad_hbm, bias_hbm, sems
+):
     half = own_ref.shape[0]
-    weight_ref[block_at(core_index(), half), :] = own_ref[...]
-    weight_ref[block_at(1 - core_index(), half), :] = other_ref[...]
-    bias_out[...] = bias_ref[...]
+    copies = [
+        pltpu.make_async_copy(own_ref, grad_hbm.at[block_at(core_index(), half)], sems.at[0]),
+        pltpu.make_async_copy(other_ref, grad_hbm.at[block_at(1 - core_index(), half)], sems.at[1]),
+        pltpu.make_async_copy(features_ref, features_hbm, sems.at[2]),
+        pltpu.make_async_copy(bias_ref, bias_hbm, sems.at[3]),
+    ]
+    for copy in copies:
+        copy.start()
+    for copy in copies:
+        copy.wait()
 
 
 def in_turn(count, make):
@@ -332,15 +341,15 @@
     near = 1
     own_nodes = n_chip * tile
 
-    def add(terms, flops=0):
+    def add(terms, flops=0, after=()):
         return call(
             functools.partial(add_terms_kernel, n_terms=len(terms)),
             like(half + BIAS_ROWS, hidden),
-            [VMEM_SPEC] * len(terms),
+            [VMEM_SPEC] * (len(terms) + len(after)),
             [],
             flops or len(terms) * half * hidden,
             len(terms) * half * hidden * 2,
-        )(*terms)
+        )(*terms, *after)
 
     is_dense = n_row * n_col <= 2 * slots
     if is_dense:
@@ -442,7 +451,8 @@
     )(aggregated, grad)
     chip_term = add([swap_cores(theirs, n_col), mine])
     add_late = functools.partial(add, flops=ROW_SUM_WEIGHT * matrix)
-    row_term = add_late(total_over(chip_term, add, "row", n_row))
+    row_terms = total_over(chip_term, add, "row", n_row)
+    row_term = add_late(row_terms)
 
     own_grads = call(
         gather_kernel,
@@ -451,7 +461,7 @@
         [],
         0,
         own_nodes * hidden * 4,
-    )(chip_term, *grads)
+    )(row_terms[-1], *grads)
     other_grads = swap_cores(own_grads, n_col)
     if is_dense:
         back_own = call(
@@ -462,38 +472,37 @@
             slots * matrix // 2,
             row_nodes * hidden * 8,
         )(turned, own_grads)
-        piece_kernel, piece_args = back_piece_kernel, (turned, back_own, other_grads)
+        back_pieces = call(
+            back_pieces_kernel,
+            [like(tile, hidden)] * n_row,
+            [VMEM_SPEC] * 3,
+            [],
+            slots * matrix // 2,
+            row_nodes * hidden * 8,
+        )(turned, back_own, other_grads)
     else:
-        back = call(
+        back_pieces = call(
             slot_back_kernel,
-            like(col_nodes, hidden, F32),
+            [like(tile, hidden)] * n_row,
             slot_specs + [VMEM_SPEC] * 2,
-            [pltpu.VMEM((row_nodes, hidden), BF16)],
+            [pltpu.VMEM((row_nodes, hidden), BF16), pltpu.VMEM((col_nodes, hidden), F32)],
             slots * matrix // 2,
             row_nodes * hidden * 8,
         )(*slot_args, own_grads, other_grads)
-        piece_kernel, piece_args = slot_piece_kernel, (back,)
-
-    def back_piece(k, before):
+    backs = exchange(dict(zip(far_first(n_row), back_pieces)), "row", n_row)
+    def back_sum(*blocks):
         return call(
-            functools.partial(piece_kernel, k=k, n_row=n_row),
-            like(tile, hidden),
-            [VMEM_SPEC] * (len(piece_args) + len(before)),
-            [],
-            n_chip * matrix,
-            2 * block_bytes,
-        )(*piece_args, *before)
-
-    backs = exchange(in_turn(n_row, back_piece), "row", n_row)
-    most = call(
-        back_sum_kernel,
-        like(tile, hidden, F32),
-        [VMEM_SPEC] * (n_row - 1),
-        [],
-        BACK_SUM_WEIGHT * matrix,
-        n_row * block_bytes,
-    )(*backs[:-2], backs[-1])
-    grad_features = call(
+            back_sum_kernel,
+            like(tile, hidden, F32),
+            [VMEM_SPEC] * len(blocks),
+            [],
+            BACK_SUM_WEIGHT * matrix,
+            n_row * block_bytes,
+        )(*blocks)
+
+    first = back_sum(*backs[:1], backs[-1])
+    most = back_sum(first, *backs[1:-2])
+    own_features = call(
         features_kernel,
         like(tile, width),
         [VMEM_SPEC] * 3,
@@ -501,7 +510,7 @@
         FEATURES_WEIGHT * matrix,
         n_row * block_bytes,
     )(weight, most, backs[-2])
-    all_terms = total_over(row_term, add, "col", n_col, 2)
+    all_terms = total_over(row_term, functools.partial(add, after=[first]), "col", n_col, 2)
     factor = (tile * n_row * n_col) ** (-0.5)
     own_half, bias_grad = call(
         functools.partial(scale_kernel, factor=factor),
@@ -511,15 +520,15 @@
         len(all_terms) * half * hidden,
         len(all_terms) * half * hidden * 2,
     )(most, *all_terms)
-    other_half = swap_cores(own_half, n_col)
-    grad_weight, grad_bias = call(
-        join_kernel,
-        (like(width, hidden, F32), like(1, hidden, F32)),
-        [VMEM_SPEC] * 3,
-        [],
+    grad_features, grad_weight, grad_bias = call(
+        write_kernel,
+        (like(tile, width), like(width, hidden, F32), like(1, hidden, F32)),
+        [VMEM_SPEC] * 4,
+        [pltpu.SemaphoreType.DMA((4,))],
         0,
         width * hidden * 8,
-    )(own_half, other_half, bias_grad)
+        HBM_SPEC,
+    )(own_features, own_half, swap_cores(own_half, n_col), bias_grad)
     return hidden_out, grad_features, grad_weight, grad_bias.reshape(hidden)
 
 

time: 46 us -> 49.5 us (1.076)
  waiting for transfers between devices: 14.9 us -> 20.2 us
  Pallas kernels: 6.44 us -> 5.4 us
  starting transfers between devices: 22.9 us -> 22.2 us
    ppermute x4, waiting for transfers between devices: 3.32 us -> 6.92 us  [total_over(): terms = [lax.ppermute(block, axis, pairs_of(step, size, cores)), block]]
    ppermute x12, waiting for transfers between devices: 9.13 us -> 10.8 us  [exchange(): lax.ppermute(blocks[k], axis, pairs)]
    ppermute x12, starting transfers between devices: 17 us -> 15.4 us  [exchange(): lax.ppermute(blocks[k], axis, pairs)]
    ppermute x4, starting transfers between devices: 5.62 us -> 6.48 us  [total_over(): terms = [lax.ppermute(block, axis, pairs_of(step, size, cores)), block]]
    pallas_call x1, Pallas kernels: 0.83 us -> 0.2 us  [local(): call(features_kernel, like(tile, width), [VMEM_SPEC] * 3, [], FEATURES_WE...]
    pallas_call x6 -> x4, Pallas kernels: 1.51 us -> 1.11 us  [the longest x1 0.77 us: local(): call(write_kernel, (like(tile, width), like(width, hidden, F32), like(1,...]
  transfers between devices with their start and end apart: 20 -> 20, of which waited for: 13 -> 14; matrix products, arithmetic and copies ran while one was open for 0% -> 0% of each run, Pallas kernels for 11% -> 8%
where the time goes in v11:
time: 49.5 us; the launch traced here: 49.3 us
  starting transfers between devices  22.2 us (45%)
  waiting for transfers between devices  20.2 us (41%)
  Pallas kernels  5.4 us (11%)
  between operations  1.47 us (3%)
    ppermute x12, starting transfers between devices, exchange(): lax.ppermute(blocks[k], axis, pairs)  15.4 us
    ppermute x12, waiting for transfers between devices, exchange(): lax.ppermute(blocks[k], axis, pairs)  10.8 us
    ppermute x4, waiting for transfers between devices, total_over(): terms = [lax.ppermute(block, axis, pairs_of(step, size, cores)), block]  6.92 us
    ppermute x4, starting transfers between devices, total_over(): terms = [lax.ppermute(block, axis, pairs_of(step, size, cores)), block]  6.48 us
    ppermute x4, waiting for transfers between devices, swap_cores(): return lax.ppermute(block, 'col', [(i, i ^ 1) for i in range(size)])  2.48 us
    pallas_call x1, Pallas kernels, local(): call(dense_kernel, (like(row_nodes, col_nodes), like(1, hidden, F32)), [S...  1.45 us
  transfers between devices with their start and end apart: 20, of which 14 were waited for; matrix products, arithmetic and copies ran while one was open for 0% of the time, Pallas kernels for 8%

profile of v11, /device:TPU:0, one launch (start us, length us, event | category | flops | bytes accessed | tf_op | source)
XLA Modules:
  0.0 49.3 jit_solution(13891004264230607172)
XLA Ops:
  0.6 5.1 %collective-permute-start = (bf16[128,256]{1,0:T(8,128)(2,1)}, bf16[128,256]{1,0:T(8,128)(2,1)S(1)}, u32[]{:S(2)}, u32[]{:S(2)}) collective-permute-start(bf16[128,256]{1,0:T(8,128)(2,1)} %refs_3_.1), channel_id=1, source_target_pairs={{0,3},{1,2},{2,1},{3,0},{4,7},{5,6},{6,5},{7,4},{8,11},{9,10},{10,... | collective-permute-start | bytes 196616 | tf_op jit(solution)/shard_map/ppermute | solution.py:56
  5.8 0.6 %collective-permute-start.2 = (bf16[128,256]{1,0:T(8,128)(2,1)}, bf16[128,256]{1,0:T(8,128)(2,1)S(1)}, u32[]{:S(2)}, u32[]{:S(2)}) collective-permute-start(bf16[128,256]{1,0:T(8,128)(2,1)} %refs_3_.1), channel_id=1, source_target_pairs={{0,1},{1,0},{2,3},{3,2},{4,5},{5,4},{6,7},{7,6},{8,9},{9,8},{10,11... | collective-permute-start | bytes 196616 | tf_op jit(solution)/shard_map/ppermute | solution.py:56
  7.1 1.5 %shard_map.111 = (bf16[1024,512]{1,0:T(8,128)(2,1)S(1)}, f32[1,256]{1,0:T(1,128)S(1)}) custom-call(s32[1,1]{1,0:T(1,128)S(6)} %copy.12.count_ref, s32[1,1,32]{2,1,0:T(1,128)} %row_hbm.1, s32[1,1,32]{2,1,0:T(1,128)} %col_hbm.1, bf16[1,1,32,128,128]{4,3,2,1,0:T(8,128)(2,1)} %tiles_hbm.1, f32[1,256]{1,0:T(1,128)} %bitcast.2), custom_call_target="tpu_custom_call" | custom-call | bytes 6291456 | tf_op jit(solution)/shard_map/pallas_call | solution.py:357
  8.6 3.0 %collective-permute-done.1.refs_1_ = bf16[128,256]{1,0:T(8,128)(2,1)S(1)} collective-permute-done((bf16[128,256]{1,0:T(8,128)(2,1)}, bf16[128,256]{1,0:T(8,128)(2,1)S(1)}, u32[]{:S(2)}, u32[]{:S(2)}) %collective-permute-start.1) | collective-permute-done | bytes 65568 | tf_op jit(solution)/shard_map/ppermute | solution.py:56
  11.6 0.3 shard_map.112
  12.3 1.2 %collective-permute-done.3.other_ref = bf16[512,256]{1,0:T(8,128)(2,1)S(1)} collective-permute-done((bf16[512,256]{1,0:T(8,128)(2,1)S(1)}, bf16[512,256]{1,0:T(8,128)(2,1)S(1)}, u32[]{:S(2)}, u32[]{:S(2)}) %collective-permute-start.3) | collective-permute-done | bytes 262176 | tf_op jit(solution)/shard_map/ppermute | solution.py:61
  13.5 2.5 %collective-permute-start.4 = (bf16[128,256]{1,0:T(8,128)(2,1)S(1)}, bf16[128,256]{1,0:T(8,128)(2,1)S(1)}, u32[]{:S(2)}, u32[]{:S(2)}) collective-permute-start(bf16[128,256]{1,0:T(8,128)(2,1)S(1)} %shard_map.114.refs_0_), channel_id=1, source_target_pairs={{0,24},{4,28},{8,16},{12,20},{16,8},{20,12},{24,0},{28,4},{1,25},{... | collective-permute-start | bytes 196616 | tf_op jit(solution)/shard_map/ppermute | solution.py:56
  16.1 0.6 %collective-permute-start.5 = (bf16[128,256]{1,0:T(8,128)(2,1)S(1)}, bf16[128,256]{1,0:T(8,128)(2,1)S(1)}, u32[]{:S(2)}, u32[]{:S(2)}) collective-permute-start(bf16[128,256]{1,0:T(8,128)(2,1)S(1)} %shard_map.115.refs_0_), channel_id=1, source_target_pairs={{0,16},{4,20},{8,24},{12,28},{16,0},{20,4},{24,8},{28,12},{1,17},{... | collective-permute-start | bytes 196616 | tf_op jit(solution)/shard_map/ppermute | solution.py:56
  16.7 0.6 %collective-permute-start.6 = (bf16[128,256]{1,0:T(8,128)(2,1)S(1)}, bf16[128,256]{1,0:T(8,128)(2,1)S(1)}, u32[]{:S(2)}, u32[]{:S(2)}) collective-permute-start(bf16[128,256]{1,0:T(8,128)(2,1)S(1)} %shard_map.116.refs_0_), channel_id=1, source_target_pairs={{0,8},{4,12},{8,0},{12,4},{16,24},{20,28},{24,16},{28,20},{1,9},{5... | collective-permute-start | bytes 196616 | tf_op jit(solution)/shard_map/ppermute | solution.py:56
  17.3 1.5 %collective-permute-done.4.refs_0_ = bf16[128,256]{1,0:T(8,128)(2,1)S(1)} collective-permute-done((bf16[128,256]{1,0:T(8,128)(2,1)S(1)}, bf16[128,256]{1,0:T(8,128)(2,1)S(1)}, u32[]{:S(2)}, u32[]{:S(2)}) %collective-permute-start.4) | collective-permute-done | bytes 65568 | tf_op jit(solution)/shard_map/ppermute | solution.py:56
  18.8 1.6 %collective-permute-done.5.refs_1_ = bf16[128,256]{1,0:T(8,128)(2,1)S(1)} collective-permute-done((bf16[128,256]{1,0:T(8,128)(2,1)S(1)}, bf16[128,256]{1,0:T(8,128)(2,1)S(1)}, u32[]{:S(2)}, u32[]{:S(2)}) %collective-permute-start.5) | collective-permute-done | bytes 65568 | tf_op jit(solution)/shard_map/ppermute | solution.py:56
  20.4 0.6 %collective-permute-done.6.refs_2_ = bf16[128,256]{1,0:T(8,128)(2,1)S(1)} collective-permute-done((bf16[128,256]{1,0:T(8,128)(2,1)S(1)}, bf16[128,256]{1,0:T(8,128)(2,1)S(1)}, u32[]{:S(2)}, u32[]{:S(2)}) %collective-permute-start.6) | collective-permute-done | bytes 65568 | tf_op jit(solution)/shard_map/ppermute | solution.py:56
  21.6 1.3 %collective-permute-done.7.refs_0_ = bf16[144,256]{1,0:T(8,128)(2,1)S(1)} collective-permute-done((bf16[144,256]{1,0:T(8,128)(2,1)S(1)}, bf16[144,256]{1,0:T(8,128)(2,1)S(1)}, u32[]{:S(2)}, u32[]{:S(2)}) %collective-permute-start.7) | collective-permute-done | bytes 73760 | tf_op jit(solution)/shard_map/ppermute | solution.py:61
  22.9 1.1 %collective-permute-start.8 = (bf16[144,256]{1,0:T(8,128)(2,1)S(1)}, bf16[144,256]{1,0:T(8,128)(2,1)S(1)}, u32[]{:S(2)}, u32[]{:S(2)}) collective-permute-start(bf16[144,256]{1,0:T(8,128)(2,1)S(1)} %shard_map.122.refs_1_), channel_id=1, source_target_pairs={{0,1},{1,0},{2,3},{3,2},{4,5},{5,4},{6,7},{7,6},{8,9},{9,8},{10,11... | collective-permute-start | bytes 221192 | tf_op jit(solution)/shard_map/ppermute | solution.py:71
  24.0 1.5 %collective-permute-start.9 = (bf16[128,256]{1,0:T(8,128)(2,1)S(1)}, bf16[128,256]{1,0:T(8,128)(2,1)S(1)}, u32[]{:S(2)}, u32[]{:S(2)}) collective-permute-start(bf16[128,256]{1,0:T(8,128)(2,1)S(1)} %get-tuple-element.28.grad_ref.refs_3_), channel_id=1, source_target_pairs={{0,24},{4,28},{8,16},{12,20},{16,8},{20,12},{24,0},{28,4},{1,25},{... | collective-permute-start | bytes 196616 | tf_op jit(solution)/shard_map/ppermute | solution.py:56
  25.5 0.5 %collective-permute-start.10 = (bf16[128,256]{1,0:T(8,128)(2,1)S(1)}, bf16[128,256]{1,0:T(8,128)(2,1)S(1)}, u32[]{:S(2)}, u32[]{:S(2)}) collective-permute-start(bf16[128,256]{1,0:T(8,128)(2,1)S(1)} %get-tuple-element.28.grad_ref.refs_3_), channel_id=1, source_target_pairs={{0,16},{4,20},{8,24},{12,28},{16,0},{20,4},{24,8},{28,12},{1,17},{... | collective-permute-start | bytes 196616 | tf_op jit(solution)/shard_map/ppermute | solution.py:56
  26.1 1.5 %collective-permute-start.11 = (bf16[128,256]{1,0:T(8,128)(2,1)S(1)}, bf16[128,256]{1,0:T(8,128)(2,1)S(1)}, u32[]{:S(2)}, u32[]{:S(2)}) collective-permute-start(bf16[128,256]{1,0:T(8,128)(2,1)S(1)} %get-tuple-element.28.grad_ref.refs_3_), channel_id=1, source_target_pairs={{0,8},{4,12},{8,0},{12,4},{16,24},{20,28},{24,16},{28,20},{1,9},{5... | collective-permute-start | bytes 196616 | tf_op jit(solution)/shard_map/ppermute | solution.py:56
  27.6 2.0 %collective-permute-done.9.refs_0_ = bf16[128,256]{1,0:T(8,128)(2,1)S(1)} collective-permute-done((bf16[128,256]{1,0:T(8,128)(2,1)S(1)}, bf16[128,256]{1,0:T(8,128)(2,1)S(1)}, u32[]{:S(2)}, u32[]{:S(2)}) %collective-permute-start.9) | collective-permute-done | bytes 65568 | tf_op jit(solution)/shard_map/ppermute | solution.py:56
  29.6 0.6 %collective-permute-done.10.refs_1_ = bf16[128,256]{1,0:T(8,128)(2,1)S(1)} collective-permute-done((bf16[128,256]{1,0:T(8,128)(2,1)S(1)}, bf16[128,256]{1,0:T(8,128)(2,1)S(1)}, u32[]{:S(2)}, u32[]{:S(2)}) %collective-permute-start.10) | collective-permute-done | bytes 65568 | tf_op jit(solution)/shard_map/ppermute | solution.py:56
  30.5 2.3 %collective-permute-start.16 = (bf16[144,256]{1,0:T(8,128)(2,1)S(1)}, bf16[144,256]{1,0:T(8,128)(2,1)S(1)}, u32[]{:S(2)}, u32[]{:S(2)}) collective-permute-start(bf16[144,256]{1,0:T(8,128)(2,1)S(1)} %shard_map.123.after_ref.refs_1_), channel_id=1, source_target_pairs={{0,2},{1,3},{2,0},{3,1},{4,6},{5,7},{6,4},{7,5},{8,10},{9,11},{10,... | collective-permute-start | bytes 221192 | tf_op jit(solution)/shard_map/ppermute | solution.py:71
  32.7 0.3 shard_map.120.turned_ref
  33.4 0.3 shard_map.126
  33.7 1.2 %collective-permute-start.13 = (bf16[128,256]{1,0:T(8,128)(2,1)S(1)}, bf16[128,256]{1,0:T(8,128)(2,1)S(1)}, u32[]{:S(2)}, u32[]{:S(2)}) collective-permute-start(bf16[128,256]{1,0:T(8,128)(2,1)S(1)} %get-tuple-element.31), channel_id=1, source_target_pairs={{0,3},{1,2},{2,1},{3,0},{4,7},{5,6},{6,5},{7,4},{8,11},{9,10},{10,... | collective-permute-start | bytes 196616 | tf_op jit(solution)/shard_map/ppermute | solution.py:56
  34.9 3.2 %collective-permute-done.16.refs_0_ = bf16[144,256]{1,0:T(8,128)(2,1)S(1)} collective-permute-done((bf16[144,256]{1,0:T(8,128)(2,1)S(1)}, bf16[144,256]{1,0:T(8,128)(2,1)S(1)}, u32[]{:S(2)}, u32[]{:S(2)}) %collective-permute-start.16) | collective-permute-done | bytes 73760 | tf_op jit(solution)/shard_map/ppermute | solution.py:71
  38.1 1.5 %collective-permute-start.17 = (bf16[144,256]{1,0:T(8,128)(2,1)S(1)}, bf16[144,256]{1,0:T(8,128)(2,1)S(1)}, u32[]{:S(2)}, u32[]{:S(2)}) collective-permute-start(bf16[144,256]{1,0:T(8,128)(2,1)S(1)} %shard_map.130.refs_1_), channel_id=1, source_target_pairs={{0,8},{4,12},{8,0},{12,4},{16,24},{20,28},{24,16},{28,20},{1,9},{5... | collective-permute-start | bytes 221192 | tf_op jit(solution)/shard_map/ppermute | solution.py:71
  39.9 2.6 %collective-permute-done.17.refs_0_ = bf16[144,256]{1,0:T(8,128)(2,1)S(1)} collective-permute-done((bf16[144,256]{1,0:T(8,128)(2,1)S(1)}, bf16[144,256]{1,0:T(8,128)(2,1)S(1)}, u32[]{:S(2)}, u32[]{:S(2)}) %collective-permute-start.17) | collective-permute-done | bytes 73760 | tf_op jit(solution)/shard_map/ppermute | solution.py:71
  42.5 1.6 %collective-permute-start.18 = (bf16[144,256]{1,0:T(8,128)(2,1)S(1)}, bf16[144,256]{1,0:T(8,128)(2,1)S(1)}, u32[]{:S(2)}, u32[]{:S(2)}) collective-permute-start(bf16[144,256]{1,0:T(8,128)(2,1)S(1)} %shard_map.131.refs_1_), channel_id=1, source_target_pairs={{0,16},{4,20},{8,24},{12,28},{16,0},{20,4},{24,8},{28,12},{1,17},{... | collective-permute-start | bytes 221192 | tf_op jit(solution)/shard_map/ppermute | solution.py:71
  44.1 1.0 %collective-permute-start.15 = (bf16[128,256]{1,0:T(8,128)(2,1)S(1)}, bf16[128,256]{1,0:T(8,128)(2,1)S(1)}, u32[]{:S(2)}, u32[]{:S(2)}) collective-permute-start(bf16[128,256]{1,0:T(8,128)(2,1)S(1)} %get-tuple-element.34), channel_id=1, source_target_pairs={{0,1},{1,0},{2,3},{3,2},{4,5},{5,4},{6,7},{7,6},{8,9},{9,8},{10,11... | collective-permute-start | bytes 196616 | tf_op jit(solution)/shard_map/ppermute | solution.py:56
  45.1 0.6 %shard_map.119 = bf16[128,256]{1,0:T(8,128)(2,1)} custom-call(bf16[128,256]{1,0:T(8,128)(2,1)S(1)} %get-tuple-element.26.in_ref), custom_call_target="tpu_custom_call" | custom-call | bytes 131072 | tf_op jit(solution)/shard_map/pallas_call | solution.py:443
  45.7 1.2 %collective-permute-done.18.refs_0_ = bf16[144,256]{1,0:T(8,128)(2,1)S(1)} collective-permute-done((bf16[144,256]{1,0:T(8,128)(2,1)S(1)}, bf16[144,256]{1,0:T(8,128)(2,1)S(1)}, u32[]{:S(2)}, u32[]{:S(2)}) %collective-permute-start.18) | collective-permute-done | bytes 73760 | tf_op jit(solution)/shard_map/ppermute | solution.py:71
  47.0 1.3 %collective-permute-done.15.last_ref = bf16[128,256]{1,0:T(8,128)(2,1)S(1)} collective-permute-done((bf16[128,256]{1,0:T(8,128)(2,1)S(1)}, bf16[128,256]{1,0:T(8,128)(2,1)S(1)}, u32[]{:S(2)}, u32[]{:S(2)}) %collective-permute-start.15) | collective-permute-done | bytes 65568 | tf_op jit(solution)/shard_map/ppermute | solution.py:56
  48.5 0.8 %shard_map.133 = (bf16[128,256]{1,0:T(8,128)(2,1)}, f32[256,256]{1,0:T(8,128)}, f32[1,256]{1,0:T(1,128)}) custom-call(bf16[128,256]{1,0:T(8,128)(2,1)S(1)} %shard_map.129.features_ref, f32[128,256]{1,0:T(8,128)S(1)} %get-tuple-element.35.own_ref, f32[128,256]{1,0:T(8,128)S(1)} %collective-permute-done.19.other_ref, f32[1,256]{1,0:T(1,128)S(1)} %get-tuple-element.36.bias_ref), custom_call_target="tpu_custom_call" | custom-call | bytes 524288 | tf_op jit(solution)/shard_map/pallas_call | solution.py:523
  (37 shorter events, 2.4 us)
Async XLA Ops:
  0.6 7.9 %collective-permute-start = (bf16[128,256]{1,0:T(8,128)(2,1)}, bf16[128,256]{1,0:T(8,128)(2,1)S(1)}, u32[]{:S(2)}, u32[]{:S(2)}) collective-permute-start(bf16[128,256]{1,0:T(8,128)(2,1)} %refs_3_.1), channel_id=1, source_target_pairs={{0,3},{1,2},{2,1},{3,0},{4,7},{5,6},{6,5},{7,4},{8,11},{9,10},{10,... | collective-permute-start | bytes 196616 | tf_op jit(solution)/shard_map/ppermute | solution.py:56
  5.7 5.8 %collective-permute-start.1 = (bf16[128,256]{1,0:T(8,128)(2,1)}, bf16[128,256]{1,0:T(8,128)(2,1)S(1)}, u32[]{:S(2)}, u32[]{:S(2)}) collective-permute-start(bf16[128,256]{1,0:T(8,128)(2,1)} %refs_3_.1), channel_id=1, source_target_pairs={{0,2},{1,3},{2,0},{3,1},{4,6},{5,7},{6,4},{7,5},{8,10},{9,11},{10,... | collective-permute-start | bytes 196616 | tf_op jit(solution)/shard_map/ppermute | solution.py:56
  5.8 5.8 %collective-permute-start.2 = (bf16[128,256]{1,0:T(8,128)(2,1)}, bf16[128,256]{1,0:T(8,128)(2,1)S(1)}, u32[]{:S(2)}, u32[]{:S(2)}) collective-permute-start(bf16[128,256]{1,0:T(8,128)(2,1)} %refs_3_.1), channel_id=1, source_target_pairs={{0,1},{1,0},{2,3},{3,2},{4,5},{5,4},{6,7},{7,6},{8,9},{9,8},{10,11... | collective-permute-start | bytes 196616 | tf_op jit(solution)/shard_map/ppermute | solution.py:56
  7.0 4.5 %copy-start.1 = (bf16[128,256]{1,0:T(8,128)(2,1)S(1)}, bf16[128,256]{1,0:T(8,128)(2,1)}, u32[]{:S(2)}) copy-start(bf16[128,256]{1,0:T(8,128)(2,1)} %refs_3_.1) | copy-start | bytes 196612
  11.9 1.6 %collective-permute-start.3 = (bf16[512,256]{1,0:T(8,128)(2,1)S(1)}, bf16[512,256]{1,0:T(8,128)(2,1)S(1)}, u32[]{:S(2)}, u32[]{:S(2)}) collective-permute-start(bf16[512,256]{1,0:T(8,128)(2,1)S(1)} %get-tuple-element.25), channel_id=1, source_target_pairs={{0,4},{4,0},{8,12},{12,8},{16,20},{20,16},{24,28},{28,24},{1,5},{5... | collective-permute-start | bytes 786440 | tf_op jit(solution)/shard_map/ppermute | solution.py:61
  13.5 5.2 %collective-permute-start.4 = (bf16[128,256]{1,0:T(8,128)(2,1)S(1)}, bf16[128,256]{1,0:T(8,128)(2,1)S(1)}, u32[]{:S(2)}, u32[]{:S(2)}) collective-permute-start(bf16[128,256]{1,0:T(8,128)(2,1)S(1)} %shard_map.114.refs_0_), channel_id=1, source_target_pairs={{0,24},{4,28},{8,16},{12,20},{16,8},{20,12},{24,0},{28,4},{1,25},{... | collective-permute-start | bytes 196616 | tf_op jit(solution)/shard_map/ppermute | solution.py:56
  16.1 4.3 %collective-permute-start.5 = (bf16[128,256]{1,0:T(8,128)(2,1)S(1)}, bf16[128,256]{1,0:T(8,128)(2,1)S(1)}, u32[]{:S(2)}, u32[]{:S(2)}) collective-permute-start(bf16[128,256]{1,0:T(8,128)(2,1)S(1)} %shard_map.115.refs_0_), channel_id=1, source_target_pairs={{0,16},{4,20},{8,24},{12,28},{16,0},{20,4},{24,8},{28,12},{1,17},{... | collective-permute-start | bytes 196616 | tf_op jit(solution)/shard_map/ppermute | solution.py:56
  16.6 4.4 %copy-start = (bf16[256,256]{1,0:T(8,128)(2,1)S(1)}, bf16[256,256]{1,0:T(8,128)(2,1)}, u32[]{:S(2)}) copy-start(bf16[256,256]{1,0:T(8,128)(2,1)} %weight_ref.3) | copy-start | bytes 393220
  16.7 4.3 %copy-start.2 = (bf16[128,256]{1,0:T(8,128)(2,1)S(1)}, bf16[128,256]{1,0:T(8,128)(2,1)}, u32[]{:S(2)}) copy-start(bf16[128,256]{1,0:T(8,128)(2,1)} %cot_ref.1) | copy-start | bytes 196612
  16.7 4.3 %collective-permute-start.6 = (bf16[128,256]{1,0:T(8,128)(2,1)S(1)}, bf16[128,256]{1,0:T(8,128)(2,1)S(1)}, u32[]{:S(2)}, u32[]{:S(2)}) collective-permute-start(bf16[128,256]{1,0:T(8,128)(2,1)S(1)} %shard_map.116.refs_0_), channel_id=1, source_target_pairs={{0,8},{4,12},{8,0},{12,4},{16,24},{20,28},{24,16},{28,20},{1,9},{5... | collective-permute-start | bytes 196616 | tf_op jit(solution)/shard_map/ppermute | solution.py:56
  21.5 1.3 %collective-permute-start.7 = (bf16[144,256]{1,0:T(8,128)(2,1)S(1)}, bf16[144,256]{1,0:T(8,128)(2,1)S(1)}, u32[]{:S(2)}, u32[]{:S(2)}) collective-permute-start(bf16[144,256]{1,0:T(8,128)(2,1)S(1)} %get-tuple-element.29), channel_id=1, source_target_pairs={{0,4},{4,0},{8,12},{12,8},{16,20},{20,16},{24,28},{28,24},{1,5},{5... | collective-permute-start | bytes 221192 | tf_op jit(solution)/shard_map/ppermute | solution.py:61
  22.9 4.6 %collective-permute-start.8 = (bf16[144,256]{1,0:T(8,128)(2,1)S(1)}, bf16[144,256]{1,0:T(8,128)(2,1)S(1)}, u32[]{:S(2)}, u32[]{:S(2)}) collective-permute-start(bf16[144,256]{1,0:T(8,128)(2,1)S(1)} %shard_map.122.refs_1_), channel_id=1, source_target_pairs={{0,1},{1,0},{2,3},{3,2},{4,5},{5,4},{6,7},{7,6},{8,9},{9,8},{10,11... | collective-permute-start | bytes 221192 | tf_op jit(solution)/shard_map/ppermute | solution.py:71
  24.0 5.6 %collective-permute-start.9 = (bf16[128,256]{1,0:T(8,128)(2,1)S(1)}, bf16[128,256]{1,0:T(8,128)(2,1)S(1)}, u32[]{:S(2)}, u32[]{:S(2)}) collective-permute-start(bf16[128,256]{1,0:T(8,128)(2,1)S(1)} %get-tuple-element.28.grad_ref.refs_3_), channel_id=1, source_target_pairs={{0,24},{4,28},{8,16},{12,20},{16,8},{20,12},{24,0},{28,4},{1,25},{... | collective-permute-start | bytes 196616 | tf_op jit(solution)/shard_map/ppermute | solution.py:56
  25.5 4.7 %collective-permute-start.10 = (bf16[128,256]{1,0:T(8,128)(2,1)S(1)}, bf16[128,256]{1,0:T(8,128)(2,1)S(1)}, u32[]{:S(2)}, u32[]{:S(2)}) collective-permute-start(bf16[128,256]{1,0:T(8,128)(2,1)S(1)} %get-tuple-element.28.grad_ref.refs_3_), channel_id=1, source_target_pairs={{0,16},{4,20},{8,24},{12,28},{16,0},{20,4},{24,8},{28,12},{1,17},{... | collective-permute-start | bytes 196616 | tf_op jit(solution)/shard_map/ppermute | solution.py:56
  26.1 4.3 %collective-permute-start.11 = (bf16[128,256]{1,0:T(8,128)(2,1)S(1)}, bf16[128,256]{1,0:T(8,128)(2,1)S(1)}, u32[]{:S(2)}, u32[]{:S(2)}) collective-permute-start(bf16[128,256]{1,0:T(8,128)(2,1)S(1)} %get-tuple-element.28.grad_ref.refs_3_), channel_id=1, source_target_pairs={{0,8},{4,12},{8,0},{12,4},{16,24},{20,28},{24,16},{28,20},{1,9},{5... | collective-permute-start | bytes 196616 | tf_op jit(solution)/shard_map/ppermute | solution.py:56
  30.4 3.0 %collective-permute-start.12 = (bf16[512,256]{1,0:T(8,128)(2,1)S(1)}, bf16[512,256]{1,0:T(8,128)(2,1)S(1)}, u32[]{:S(2)}, u32[]{:S(2)}) collective-permute-start(bf16[512,256]{1,0:T(8,128)(2,1)S(1)} %shard_map.124.source_ref), channel_id=1, source_target_pairs={{0,4},{4,0},{8,12},{12,8},{16,20},{20,16},{24,28},{28,24},{1,5},{5... | collective-permute-start | bytes 786440 | tf_op jit(solution)/shard_map/ppermute | solution.py:61
  30.5 7.6 %collective-permute-start.16 = (bf16[144,256]{1,0:T(8,128)(2,1)S(1)}, bf16[144,256]{1,0:T(8,128)(2,1)S(1)}, u32[]{:S(2)}, u32[]{:S(2)}) collective-permute-start(bf16[144,256]{1,0:T(8,128)(2,1)S(1)} %shard_map.123.after_ref.refs_1_), channel_id=1, source_target_pairs={{0,2},{1,3},{2,0},{3,1},{4,6},{5,7},{6,4},{7,5},{8,10},{9,11},{10,... | collective-permute-start | bytes 221192 | tf_op jit(solution)/shard_map/ppermute | solution.py:71
  33.7 6.2 %collective-permute-start.13 = (bf16[128,256]{1,0:T(8,128)(2,1)S(1)}, bf16[128,256]{1,0:T(8,128)(2,1)S(1)}, u32[]{:S(2)}, u32[]{:S(2)}) collective-permute-start(bf16[128,256]{1,0:T(8,128)(2,1)S(1)} %get-tuple-element.31), channel_id=1, source_target_pairs={{0,3},{1,2},{2,1},{3,0},{4,7},{5,6},{6,5},{7,4},{8,11},{9,10},{10,... | collective-permute-start | bytes 196616 | tf_op jit(solution)/shard_map/ppermute | solution.py:56
  38.1 4.4 %collective-permute-start.17 = (bf16[144,256]{1,0:T(8,128)(2,1)S(1)}, bf16[144,256]{1,0:T(8,128)(2,1)S(1)}, u32[]{:S(2)}, u32[]{:S(2)}) collective-permute-start(bf16[144,256]{1,0:T(8,128)(2,1)S(1)} %shard_map.130.refs_1_), channel_id=1, source_target_pairs={{0,8},{4,12},{8,0},{12,4},{16,24},{20,28},{24,16},{28,20},{1,9},{5... | collective-permute-start | bytes 221192 | tf_op jit(solution)/shard_map/ppermute | solution.py:71
  39.6 6.1 %collective-permute-start.14 = (bf16[128,256]{1,0:T(8,128)(2,1)S(1)}, bf16[128,256]{1,0:T(8,128)(2,1)S(1)}, u32[]{:S(2)}, u32[]{:S(2)}) collective-permute-start(bf16[128,256]{1,0:T(8,128)(2,1)S(1)} %get-tuple-element.33), channel_id=1, source_target_pairs={{0,2},{1,3},{2,0},{3,1},{4,6},{5,7},{6,4},{7,5},{8,10},{9,11},{10,... | collective-permute-start | bytes 196616 | tf_op jit(solution)/shard_map/ppermute | solution.py:56
  42.5 4.4 %collective-permute-start.18 = (bf16[144,256]{1,0:T(8,128)(2,1)S(1)}, bf16[144,256]{1,0:T(8,128)(2,1)S(1)}, u32[]{:S(2)}, u32[]{:S(2)}) collective-permute-start(bf16[144,256]{1,0:T(8,128)(2,1)S(1)} %shard_map.131.refs_1_), channel_id=1, source_target_pairs={{0,16},{4,20},{8,24},{12,28},{16,0},{20,4},{24,8},{28,12},{1,17},{... | collective-permute-start | bytes 221192 | tf_op jit(solution)/shard_map/ppermute | solution.py:71
  44.1 4.3 %collective-permute-start.15 = (bf16[128,256]{1,0:T(8,128)(2,1)S(1)}, bf16[128,256]{1,0:T(8,128)(2,1)S(1)}, u32[]{:S(2)}, u32[]{:S(2)}) collective-permute-start(bf16[128,256]{1,0:T(8,128)(2,1)S(1)} %get-tuple-element.34), channel_id=1, source_target_pairs={{0,1},{1,0},{2,3},{3,2},{4,5},{5,4},{6,7},{7,6},{8,9},{9,8},{10,11... | collective-permute-start | bytes 196616 | tf_op jit(solution)/shard_map/ppermute | solution.py:56
  47.0 1.6 %collective-permute-start.19 = (f32[128,256]{1,0:T(8,128)S(1)}, f32[128,256]{1,0:T(8,128)S(1)}, u32[]{:S(2)}, u32[]{:S(2)}) collective-permute-start(f32[128,256]{1,0:T(8,128)S(1)} %get-tuple-element.35.own_ref), channel_id=1, source_target_pairs={{0,4},{4,0},{8,12},{12,8},{16,20},{20,16},{24,28},{28,24},{1,5},{5... | collective-permute-start | bytes 393224 | tf_op jit(solution)/shard_map/ppermute | solution.py:61

commit v12 on v11

--- a/solution.py
+++ b/solution.py
@@ -65,11 +65,11 @@
     count = size // cores
     if count & (count - 1):
         return exchange([block] * count, axis, size, cores)
-    terms, step = [block], 1
-    while step < count:
+    terms, step = [block], count // 2
+    while step:
         block = add(terms) if len(terms) > 1 else block
         terms = [lax.ppermute(block, axis, pairs_of(step, size, cores)), block]
-        step *= 2
+        step //= 2
     return terms
 
 
@@ -341,15 +341,15 @@
     near = 1
     own_nodes = n_chip * tile
 
-    def add(terms, flops=0, after=()):
+    def add(terms, flops=0):
         return call(
             functools.partial(add_terms_kernel, n_terms=len(terms)),
             like(half + BIAS_ROWS, hidden),
-            [VMEM_SPEC] * (len(terms) + len(after)),
+            [VMEM_SPEC] * len(terms),
             [],
             flops or len(terms) * half * hidden,
             len(terms) * half * hidden * 2,
-        )(*terms, *after)
+        )(*terms)
 
     is_dense = n_row * n_col <= 2 * slots
     if is_dense:
@@ -451,8 +451,7 @@
     )(aggregated, grad)
     chip_term = add([swap_cores(theirs, n_col), mine])
     add_late = functools.partial(add, flops=ROW_SUM_WEIGHT * matrix)
-    row_terms = total_over(chip_term, add, "row", n_row)
-    row_term = add_late(row_terms)
+    row_term = add_late(total_over(chip_term, add, "row", n_row))
 
     own_grads = call(
         gather_kernel,
@@ -461,7 +460,7 @@
         [],
         0,
         own_nodes * hidden * 4,
-    )(row_terms[-1], *grads)
+    )(chip_term, *grads)
     other_grads = swap_cores(own_grads, n_col)
     if is_dense:
         back_own = call(
@@ -490,18 +489,14 @@
             row_nodes * hidden * 8,
         )(*slot_args, own_grads, other_grads)
     backs = exchange(dict(zip(far_first(n_row), back_pieces)), "row", n_row)
-    def back_sum(*blocks):
-        return call(
-            back_sum_kernel,
-            like(tile, hidden, F32),
-            [VMEM_SPEC] * len(blocks),
-            [],
-            BACK_SUM_WEIGHT * matrix,
-            n_row * block_bytes,
-        )(*blocks)
-
-    first = back_sum(*backs[:1], backs[-1])
-    most = back_sum(first, *backs[1:-2])
+    most = call(
+        back_sum_kernel,
+        like(tile, hidden, F32),
+        [VMEM_SPEC] * (n_row - 1),
+        [],
+        BACK_SUM_WEIGHT * matrix,
+        n_row * block_bytes,
+    )(*backs[:-2], backs[-1])
     own_features = call(
         features_kernel,
         like(tile, width),
@@ -510,7 +505,7 @@
         FEATURES_WEIGHT * matrix,
         n_row * block_bytes,
     )(weight, most, backs[-2])
-    all_terms = total_over(row_term, functools.partial(add, after=[first]), "col", n_col, 2)
+    all_terms = total_over(row_term, add, "col", n_col, 2)
     factor = (tile * n_row * n_col) ** (-0.5)
     own_half, bias_grad = call(
         functools.partial(scale_kernel, factor=factor),

time: 49.5 us -> 47 us (0.949)
  waiting for transfers between devices: 20.2 us -> 18.4 us
  starting transfers between devices: 22.2 us -> 21.6 us
    ppermute x4, starting transfers between devices: 6.48 us -> 3.89 us  [total_over(): terms = [lax.ppermute(block, axis, pairs_of(step, size, cores)), block]]
    ppermute x4, waiting for transfers between devices: 6.92 us -> 4.65 us  [total_over(): terms = [lax.ppermute(block, axis, pairs_of(step, size, cores)), block]]
    ppermute x12, starting transfers between devices: 15.4 us -> 17.4 us  [exchange(): lax.ppermute(blocks[k], axis, pairs)]
    ppermute x4, waiting for transfers between devices: 2.48 us -> 3.6 us  [swap_cores(): return lax.ppermute(block, 'col', [(i, i ^ 1) for i in range(size)])]
    ppermute x12, waiting for transfers between devices: 10.8 us -> 10.1 us  [exchange(): lax.ppermute(blocks[k], axis, pairs)]
  transfers between devices with their start and end apart: 20 -> 20, of which waited for: 14 -> 15; matrix products, arithmetic and copies ran while one was open for 0% -> 0% of each run, Pallas kernels for 8% -> 8%
where the time goes in v12:
time: 47 us; the launch traced here: 46.8 us
  starting transfers between devices  21.6 us (46%)
  waiting for transfers between devices  18.4 us (39%)
  Pallas kernels  5.37 us (11%)
  between operations  1.49 us (3%)
    ppermute x12, starting transfers between devices, exchange(): lax.ppermute(blocks[k], axis, pairs)  17.4 us
    ppermute x12, waiting for transfers between devices, exchange(): lax.ppermute(blocks[k], axis, pairs)  10.1 us
    ppermute x4, waiting for transfers between devices, total_over(): terms = [lax.ppermute(block, axis, pairs_of(step, size, cores)), block]  4.65 us
    ppermute x4, starting transfers between devices, total_over(): terms = [lax.ppermute(block, axis, pairs_of(step, size, cores)), block]  3.89 us
    ppermute x4, waiting for transfers between devices, swap_cores(): return lax.ppermute(block, 'col', [(i, i ^ 1) for i in range(size)])  3.6 us
    pallas_call x1, Pallas kernels, local(): call(dense_kernel, (like(row_nodes, col_nodes), like(1, hidden, F32)), [S...  1.45 us
  transfers between devices with their start and end apart: 20, of which 15 were waited for; matrix products, arithmetic and copies ran while one was open for 0% of the time, Pallas kernels for 8%

profile of v12, /device:TPU:0, one launch (start us, length us, event | category | flops | bytes accessed | tf_op | source)
XLA Modules:
  0.0 46.8 jit_solution(2387354256528660620)
XLA Ops:
  0.6 5.1 %collective-permute-start = (bf16[128,256]{1,0:T(8,128)(2,1)}, bf16[128,256]{1,0:T(8,128)(2,1)S(1)}, u32[]{:S(2)}, u32[]{:S(2)}) collective-permute-start(bf16[128,256]{1,0:T(8,128)(2,1)} %refs_3_.1), channel_id=1, source_target_pairs={{0,3},{1,2},{2,1},{3,0},{4,7},{5,6},{6,5},{7,4},{8,11},{9,10},{10,... | collective-permute-start | bytes 196616 | tf_op jit(solution)/shard_map/ppermute | solution.py:56
  5.8 0.6 %collective-permute-start.2 = (bf16[128,256]{1,0:T(8,128)(2,1)}, bf16[128,256]{1,0:T(8,128)(2,1)S(1)}, u32[]{:S(2)}, u32[]{:S(2)}) collective-permute-start(bf16[128,256]{1,0:T(8,128)(2,1)} %refs_3_.1), channel_id=1, source_target_pairs={{0,1},{1,0},{2,3},{3,2},{4,5},{5,4},{6,7},{7,6},{8,9},{9,8},{10,11... | collective-permute-start | bytes 196616 | tf_op jit(solution)/shard_map/ppermute | solution.py:56
  7.1 1.5 %shard_map.111 = (bf16[1024,512]{1,0:T(8,128)(2,1)S(1)}, f32[1,256]{1,0:T(1,128)S(1)}) custom-call(s32[1,1]{1,0:T(1,128)S(6)} %copy.12.count_ref, s32[1,1,32]{2,1,0:T(1,128)} %row_hbm.1, s32[1,1,32]{2,1,0:T(1,128)} %col_hbm.1, bf16[1,1,32,128,128]{4,3,2,1,0:T(8,128)(2,1)} %tiles_hbm.1, f32[1,256]{1,0:T(1,128)} %bitcast.2), custom_call_target="tpu_custom_call" | custom-call | bytes 6291456 | tf_op jit(solution)/shard_map/pallas_call | solution.py:357
  8.6 3.0 %collective-permute-done.1.refs_1_ = bf16[128,256]{1,0:T(8,128)(2,1)S(1)} collective-permute-done((bf16[128,256]{1,0:T(8,128)(2,1)}, bf16[128,256]{1,0:T(8,128)(2,1)S(1)}, u32[]{:S(2)}, u32[]{:S(2)}) %collective-permute-start.1) | collective-permute-done | bytes 65568 | tf_op jit(solution)/shard_map/ppermute | solution.py:56
  11.6 0.3 shard_map.112
  12.0 0.3 shard_map.113.own_ref
  12.3 1.2 %collective-permute-done.3.other_ref = bf16[512,256]{1,0:T(8,128)(2,1)S(1)} collective-permute-done((bf16[512,256]{1,0:T(8,128)(2,1)S(1)}, bf16[512,256]{1,0:T(8,128)(2,1)S(1)}, u32[]{:S(2)}, u32[]{:S(2)}) %collective-permute-start.3) | collective-permute-done | bytes 262176 | tf_op jit(solution)/shard_map/ppermute | solution.py:61
  13.5 2.5 %collective-permute-start.4 = (bf16[128,256]{1,0:T(8,128)(2,1)S(1)}, bf16[128,256]{1,0:T(8,128)(2,1)S(1)}, u32[]{:S(2)}, u32[]{:S(2)}) collective-permute-start(bf16[128,256]{1,0:T(8,128)(2,1)S(1)} %shard_map.114.refs_0_), channel_id=1, source_target_pairs={{0,24},{4,28},{8,16},{12,20},{16,8},{20,12},{24,0},{28,4},{1,25},{... | collective-permute-start | bytes 196616 | tf_op jit(solution)/shard_map/ppermute | solution.py:56
  16.1 0.6 %collective-permute-start.5 = (bf16[128,256]{1,0:T(8,128)(2,1)S(1)}, bf16[128,256]{1,0:T(8,128)(2,1)S(1)}, u32[]{:S(2)}, u32[]{:S(2)}) collective-permute-start(bf16[128,256]{1,0:T(8,128)(2,1)S(1)} %shard_map.115.refs_0_), channel_id=1, source_target_pairs={{0,16},{4,20},{8,24},{12,28},{16,0},{20,4},{24,8},{28,12},{1,17},{... | collective-permute-start | bytes 196616 | tf_op jit(solution)/shard_map/ppermute | solution.py:56
  16.7 0.6 %collective-permute-start.6 = (bf16[128,256]{1,0:T(8,128)(2,1)S(1)}, bf16[128,256]{1,0:T(8,128)(2,1)S(1)}, u32[]{:S(2)}, u32[]{:S(2)}) collective-permute-start(bf16[128,256]{1,0:T(8,128)(2,1)S(1)} %shard_map.116.refs_0_), channel_id=1, source_target_pairs={{0,8},{4,12},{8,0},{12,4},{16,24},{20,28},{24,16},{28,20},{1,9},{5... | collective-permute-start | bytes 196616 | tf_op jit(solution)/shard_map/ppermute | solution.py:56
  17.3 1.5 %collective-permute-done.4.refs_0_ = bf16[128,256]{1,0:T(8,128)(2,1)S(1)} collective-permute-done((bf16[128,256]{1,0:T(8,128)(2,1)S(1)}, bf16[128,256]{1,0:T(8,128)(2,1)S(1)}, u32[]{:S(2)}, u32[]{:S(2)}) %collective-permute-start.4) | collective-permute-done | bytes 65568 | tf_op jit(solution)/shard_map/ppermute | solution.py:56
  18.8 1.6 %collective-permute-done.5.refs_1_ = bf16[128,256]{1,0:T(8,128)(2,1)S(1)} collective-permute-done((bf16[128,256]{1,0:T(8,128)(2,1)S(1)}, bf16[128,256]{1,0:T(8,128)(2,1)S(1)}, u32[]{:S(2)}, u32[]{:S(2)}) %collective-permute-start.5) | collective-permute-done | bytes 65568 | tf_op jit(solution)/shard_map/ppermute | solution.py:56
  20.4 0.6 %collective-permute-done.6.refs_2_ = bf16[128,256]{1,0:T(8,128)(2,1)S(1)} collective-permute-done((bf16[128,256]{1,0:T(8,128)(2,1)S(1)}, bf16[128,256]{1,0:T(8,128)(2,1)S(1)}, u32[]{:S(2)}, u32[]{:S(2)}) %collective-permute-start.6) | collective-permute-done | bytes 65568 | tf_op jit(solution)/shard_map/ppermute | solution.py:56
  21.6 1.3 %collective-permute-done.7.refs_0_ = bf16[144,256]{1,0:T(8,128)(2,1)S(1)} collective-permute-done((bf16[144,256]{1,0:T(8,128)(2,1)S(1)}, bf16[144,256]{1,0:T(8,128)(2,1)S(1)}, u32[]{:S(2)}, u32[]{:S(2)}) %collective-permute-start.7) | collective-permute-done | bytes 73760 | tf_op jit(solution)/shard_map/ppermute | solution.py:61
  22.9 1.6 %collective-permute-start.15 = (bf16[144,256]{1,0:T(8,128)(2,1)S(1)}, bf16[144,256]{1,0:T(8,128)(2,1)S(1)}, u32[]{:S(2)}, u32[]{:S(2)}) collective-permute-start(bf16[144,256]{1,0:T(8,128)(2,1)S(1)} %shard_map.122.after_ref.refs_1_), channel_id=1, source_target_pairs={{0,2},{1,3},{2,0},{3,1},{4,6},{5,7},{6,4},{7,5},{8,10},{9,11},{10,... | collective-permute-start | bytes 221192 | tf_op jit(solution)/shard_map/ppermute | solution.py:71
  24.5 1.5 %collective-permute-start.8 = (bf16[128,256]{1,0:T(8,128)(2,1)S(1)}, bf16[128,256]{1,0:T(8,128)(2,1)S(1)}, u32[]{:S(2)}, u32[]{:S(2)}) collective-permute-start(bf16[128,256]{1,0:T(8,128)(2,1)S(1)} %get-tuple-element.28.grad_ref.refs_3_), channel_id=1, source_target_pairs={{0,24},{4,28},{8,16},{12,20},{16,8},{20,12},{24,0},{28,4},{1,25},{... | collective-permute-start | bytes 196616 | tf_op jit(solution)/shard_map/ppermute | solution.py:56
  26.0 0.5 %collective-permute-start.9 = (bf16[128,256]{1,0:T(8,128)(2,1)S(1)}, bf16[128,256]{1,0:T(8,128)(2,1)S(1)}, u32[]{:S(2)}, u32[]{:S(2)}) collective-permute-start(bf16[128,256]{1,0:T(8,128)(2,1)S(1)} %get-tuple-element.28.grad_ref.refs_3_), channel_id=1, source_target_pairs={{0,16},{4,20},{8,24},{12,28},{16,0},{20,4},{24,8},{28,12},{1,17},{... | collective-permute-start | bytes 196616 | tf_op jit(solution)/shard_map/ppermute | solution.py:56
  26.6 1.5 %collective-permute-start.10 = (bf16[128,256]{1,0:T(8,128)(2,1)S(1)}, bf16[128,256]{1,0:T(8,128)(2,1)S(1)}, u32[]{:S(2)}, u32[]{:S(2)}) collective-permute-start(bf16[128,256]{1,0:T(8,128)(2,1)S(1)} %get-tuple-element.28.grad_ref.refs_3_), channel_id=1, source_target_pairs={{0,8},{4,12},{8,0},{12,4},{16,24},{20,28},{24,16},{28,20},{1,9},{5... | collective-permute-start | bytes 196616 | tf_op jit(solution)/shard_map/ppermute | solution.py:56
  28.0 1.7 %collective-permute-done.15.refs_0_ = bf16[144,256]{1,0:T(8,128)(2,1)S(1)} collective-permute-done((bf16[144,256]{1,0:T(8,128)(2,1)S(1)}, bf16[144,256]{1,0:T(8,128)(2,1)S(1)}, u32[]{:S(2)}, u32[]{:S(2)}) %collective-permute-start.15) | collective-permute-done | bytes 73760 | tf_op jit(solution)/shard_map/ppermute | solution.py:71
  30.1 0.6 %collective-permute-done.9.refs_1_ = bf16[128,256]{1,0:T(8,128)(2,1)S(1)} collective-permute-done((bf16[128,256]{1,0:T(8,128)(2,1)S(1)}, bf16[128,256]{1,0:T(8,128)(2,1)S(1)}, u32[]{:S(2)}, u32[]{:S(2)}) %collective-permute-start.9) | collective-permute-done | bytes 65568 | tf_op jit(solution)/shard_map/ppermute | solution.py:56
  31.0 0.3 shard_map.120.turned_ref
  31.3 2.9 %collective-permute-done.16.refs_0_ = bf16[144,256]{1,0:T(8,128)(2,1)S(1)} collective-permute-done((bf16[144,256]{1,0:T(8,128)(2,1)S(1)}, bf16[144,256]{1,0:T(8,128)(2,1)S(1)}, u32[]{:S(2)}, u32[]{:S(2)}) %collective-permute-start.16) | collective-permute-done | bytes 73760 | tf_op jit(solution)/shard_map/ppermute | solution.py:71
  34.2 1.6 %collective-permute-start.17 = (bf16[144,256]{1,0:T(8,128)(2,1)S(1)}, bf16[144,256]{1,0:T(8,128)(2,1)S(1)}, u32[]{:S(2)}, u32[]{:S(2)}) collective-permute-start(bf16[144,256]{1,0:T(8,128)(2,1)S(1)} %shard_map.129.refs_1_), channel_id=1, source_target_pairs={{0,16},{4,20},{8,24},{12,28},{16,0},{20,4},{24,8},{28,12},{1,17},{... | collective-permute-start | bytes 221192 | tf_op jit(solution)/shard_map/ppermute | solution.py:71
  36.1 0.3 shard_map.125
  36.5 2.5 %collective-permute-start.12 = (bf16[128,256]{1,0:T(8,128)(2,1)S(1)}, bf16[128,256]{1,0:T(8,128)(2,1)S(1)}, u32[]{:S(2)}, u32[]{:S(2)}) collective-permute-start(bf16[128,256]{1,0:T(8,128)(2,1)S(1)} %get-tuple-element.31), channel_id=1, source_target_pairs={{0,3},{1,2},{2,1},{3,0},{4,7},{5,6},{6,5},{7,4},{8,11},{9,10},{10,... | collective-permute-start | bytes 196616 | tf_op jit(solution)/shard_map/ppermute | solution.py:56
  39.0 0.6 %collective-permute-start.18 = (bf16[144,256]{1,0:T(8,128)(2,1)S(1)}, bf16[144,256]{1,0:T(8,128)(2,1)S(1)}, u32[]{:S(2)}, u32[]{:S(2)}) collective-permute-start(bf16[144,256]{1,0:T(8,128)(2,1)S(1)} %shard_map.130.refs_1_), channel_id=1, source_target_pairs={{0,8},{4,12},{8,0},{12,4},{16,24},{20,28},{24,16},{28,20},{1,9},{5... | collective-permute-start | bytes 221192 | tf_op jit(solution)/shard_map/ppermute | solution.py:71
  39.6 1.9 %collective-permute-start.14 = (bf16[128,256]{1,0:T(8,128)(2,1)S(1)}, bf16[128,256]{1,0:T(8,128)(2,1)S(1)}, u32[]{:S(2)}, u32[]{:S(2)}) collective-permute-start(bf16[128,256]{1,0:T(8,128)(2,1)S(1)} %get-tuple-element.34), channel_id=1, source_target_pairs={{0,1},{1,0},{2,3},{3,2},{4,5},{5,4},{6,7},{7,6},{8,9},{9,8},{10,11... | collective-permute-start | bytes 196616 | tf_op jit(solution)/shard_map/ppermute | solution.py:56
  41.5 0.6 %shard_map.119 = bf16[128,256]{1,0:T(8,128)(2,1)} custom-call(bf16[128,256]{1,0:T(8,128)(2,1)S(1)} %get-tuple-element.26.in_ref), custom_call_target="tpu_custom_call" | custom-call | bytes 131072 | tf_op jit(solution)/shard_map/pallas_call | solution.py:443
  42.2 0.7 %collective-permute-done.12.refs_0_ = bf16[128,256]{1,0:T(8,128)(2,1)S(1)} collective-permute-done((bf16[128,256]{1,0:T(8,128)(2,1)S(1)}, bf16[128,256]{1,0:T(8,128)(2,1)S(1)}, u32[]{:S(2)}, u32[]{:S(2)}) %collective-permute-start.12) | collective-permute-done | bytes 65568 | tf_op jit(solution)/shard_map/ppermute | solution.py:56
  42.9 1.7 %collective-permute-done.13.refs_1_ = bf16[128,256]{1,0:T(8,128)(2,1)S(1)} collective-permute-done((bf16[128,256]{1,0:T(8,128)(2,1)S(1)}, bf16[128,256]{1,0:T(8,128)(2,1)S(1)}, u32[]{:S(2)}, u32[]{:S(2)}) %collective-permute-start.13) | collective-permute-done | bytes 65568 | tf_op jit(solution)/shard_map/ppermute | solution.py:56
  45.0 1.1 %collective-permute-done.19.other_ref = f32[128,256]{1,0:T(8,128)S(1)} collective-permute-done((f32[128,256]{1,0:T(8,128)S(1)}, f32[128,256]{1,0:T(8,128)S(1)}, u32[]{:S(2)}, u32[]{:S(2)}) %collective-permute-start.19) | collective-permute-done | bytes 131104 | tf_op jit(solution)/shard_map/ppermute | solution.py:61
  46.1 0.8 %shard_map.132 = (bf16[128,256]{1,0:T(8,128)(2,1)}, f32[256,256]{1,0:T(8,128)}, f32[1,256]{1,0:T(1,128)}) custom-call(bf16[128,256]{1,0:T(8,128)(2,1)S(1)} %shard_map.127.features_ref, f32[128,256]{1,0:T(8,128)S(1)} %get-tuple-element.35.own_ref, f32[128,256]{1,0:T(8,128)S(1)} %collective-permute-done.19.other_ref, f32[1,256]{1,0:T(1,128)S(1)} %get-tuple-element.36.bias_ref), custom_call_target="tpu_custom_call" | custom-call | bytes 524288 | tf_op jit(solution)/shard_map/pallas_call | solution.py:518
  (36 shorter events, 2.0 us)
Async XLA Ops:
  0.6 7.9 %collective-permute-start = (bf16[128,256]{1,0:T(8,128)(2,1)}, bf16[128,256]{1,0:T(8,128)(2,1)S(1)}, u32[]{:S(2)}, u32[]{:S(2)}) collective-permute-start(bf16[128,256]{1,0:T(8,128)(2,1)} %refs_3_.1), channel_id=1, source_target_pairs={{0,3},{1,2},{2,1},{3,0},{4,7},{5,6},{6,5},{7,4},{8,11},{9,10},{10,... | collective-permute-start | bytes 196616 | tf_op jit(solution)/shard_map/ppermute | solution.py:56
  5.7 5.8 %collective-permute-start.1 = (bf16[128,256]{1,0:T(8,128)(2,1)}, bf16[128,256]{1,0:T(8,128)(2,1)S(1)}, u32[]{:S(2)}, u32[]{:S(2)}) collective-permute-start(bf16[128,256]{1,0:T(8,128)(2,1)} %refs_3_.1), channel_id=1, source_target_pairs={{0,2},{1,3},{2,0},{3,1},{4,6},{5,7},{6,4},{7,5},{8,10},{9,11},{10,... | collective-permute-start | bytes 196616 | tf_op jit(solution)/shard_map/ppermute | solution.py:56
  5.8 5.8 %collective-permute-start.2 = (bf16[128,256]{1,0:T(8,128)(2,1)}, bf16[128,256]{1,0:T(8,128)(2,1)S(1)}, u32[]{:S(2)}, u32[]{:S(2)}) collective-permute-start(bf16[128,256]{1,0:T(8,128)(2,1)} %refs_3_.1), channel_id=1, source_target_pairs={{0,1},{1,0},{2,3},{3,2},{4,5},{5,4},{6,7},{7,6},{8,9},{9,8},{10,11... | collective-permute-start | bytes 196616 | tf_op jit(solution)/shard_map/ppermute | solution.py:56
  7.0 4.5 %copy-start.1 = (bf16[128,256]{1,0:T(8,128)(2,1)S(1)}, bf16[128,256]{1,0:T(8,128)(2,1)}, u32[]{:S(2)}) copy-start(bf16[128,256]{1,0:T(8,128)(2,1)} %refs_3_.1) | copy-start | bytes 196612
  11.9 1.6 %collective-permute-start.3 = (bf16[512,256]{1,0:T(8,128)(2,1)S(1)}, bf16[512,256]{1,0:T(8,128)(2,1)S(1)}, u32[]{:S(2)}, u32[]{:S(2)}) collective-permute-start(bf16[512,256]{1,0:T(8,128)(2,1)S(1)} %get-tuple-element.25), channel_id=1, source_target_pairs={{0,4},{4,0},{8,12},{12,8},{16,20},{20,16},{24,28},{28,24},{1,5},{5... | collective-permute-start | bytes 786440 | tf_op jit(solution)/shard_map/ppermute | solution.py:61
  13.5 5.2 %collective-permute-start.4 = (bf16[128,256]{1,0:T(8,128)(2,1)S(1)}, bf16[128,256]{1,0:T(8,128)(2,1)S(1)}, u32[]{:S(2)}, u32[]{:S(2)}) collective-permute-start(bf16[128,256]{1,0:T(8,128)(2,1)S(1)} %shard_map.114.refs_0_), channel_id=1, source_target_pairs={{0,24},{4,28},{8,16},{12,20},{16,8},{20,12},{24,0},{28,4},{1,25},{... | collective-permute-start | bytes 196616 | tf_op jit(solution)/shard_map/ppermute | solution.py:56
  16.1 4.3 %collective-permute-start.5 = (bf16[128,256]{1,0:T(8,128)(2,1)S(1)}, bf16[128,256]{1,0:T(8,128)(2,1)S(1)}, u32[]{:S(2)}, u32[]{:S(2)}) collective-permute-start(bf16[128,256]{1,0:T(8,128)(2,1)S(1)} %shard_map.115.refs_0_), channel_id=1, source_target_pairs={{0,16},{4,20},{8,24},{12,28},{16,0},{20,4},{24,8},{28,12},{1,17},{... | collective-permute-start | bytes 196616 | tf_op jit(solution)/shard_map/ppermute | solution.py:56
  16.6 4.4 %copy-start = (bf16[256,256]{1,0:T(8,128)(2,1)S(1)}, bf16[256,256]{1,0:T(8,128)(2,1)}, u32[]{:S(2)}) copy-start(bf16[256,256]{1,0:T(8,128)(2,1)} %weight_ref.3) | copy-start | bytes 393220
  16.7 4.3 %copy-start.2 = (bf16[128,256]{1,0:T(8,128)(2,1)S(1)}, bf16[128,256]{1,0:T(8,128)(2,1)}, u32[]{:S(2)}) copy-start(bf16[128,256]{1,0:T(8,128)(2,1)} %cot_ref.1) | copy-start | bytes 196612
  16.7 4.3 %collective-permute-start.6 = (bf16[128,256]{1,0:T(8,128)(2,1)S(1)}, bf16[128,256]{1,0:T(8,128)(2,1)S(1)}, u32[]{:S(2)}, u32[]{:S(2)}) collective-permute-start(bf16[128,256]{1,0:T(8,128)(2,1)S(1)} %shard_map.116.refs_0_), channel_id=1, source_target_pairs={{0,8},{4,12},{8,0},{12,4},{16,24},{20,28},{24,16},{28,20},{1,9},{5... | collective-permute-start | bytes 196616 | tf_op jit(solution)/shard_map/ppermute | solution.py:56
  21.5 1.3 %collective-permute-start.7 = (bf16[144,256]{1,0:T(8,128)(2,1)S(1)}, bf16[144,256]{1,0:T(8,128)(2,1)S(1)}, u32[]{:S(2)}, u32[]{:S(2)}) collective-permute-start(bf16[144,256]{1,0:T(8,128)(2,1)S(1)} %get-tuple-element.29), channel_id=1, source_target_pairs={{0,4},{4,0},{8,12},{12,8},{16,20},{20,16},{24,28},{28,24},{1,5},{5... | collective-permute-start | bytes 221192 | tf_op jit(solution)/shard_map/ppermute | solution.py:61
  22.9 6.9 %collective-permute-start.15 = (bf16[144,256]{1,0:T(8,128)(2,1)S(1)}, bf16[144,256]{1,0:T(8,128)(2,1)S(1)}, u32[]{:S(2)}, u32[]{:S(2)}) collective-permute-start(bf16[144,256]{1,0:T(8,128)(2,1)S(1)} %shard_map.122.after_ref.refs_1_), channel_id=1, source_target_pairs={{0,2},{1,3},{2,0},{3,1},{4,6},{5,7},{6,4},{7,5},{8,10},{9,11},{10,... | collective-permute-start | bytes 221192 | tf_op jit(solution)/shard_map/ppermute | solution.py:71
  24.5 5.6 %collective-permute-start.8 = (bf16[128,256]{1,0:T(8,128)(2,1)S(1)}, bf16[128,256]{1,0:T(8,128)(2,1)S(1)}, u32[]{:S(2)}, u32[]{:S(2)}) collective-permute-start(bf16[128,256]{1,0:T(8,128)(2,1)S(1)} %get-tuple-element.28.grad_ref.refs_3_), channel_id=1, source_target_pairs={{0,24},{4,28},{8,16},{12,20},{16,8},{20,12},{24,0},{28,4},{1,25},{... | collective-permute-start | bytes 196616 | tf_op jit(solution)/shard_map/ppermute | solution.py:56
  26.0 4.7 %collective-permute-start.9 = (bf16[128,256]{1,0:T(8,128)(2,1)S(1)}, bf16[128,256]{1,0:T(8,128)(2,1)S(1)}, u32[]{:S(2)}, u32[]{:S(2)}) collective-permute-start(bf16[128,256]{1,0:T(8,128)(2,1)S(1)} %get-tuple-element.28.grad_ref.refs_3_), channel_id=1, source_target_pairs={{0,16},{4,20},{8,24},{12,28},{16,0},{20,4},{24,8},{28,12},{1,17},{... | collective-permute-start | bytes 196616 | tf_op jit(solution)/shard_map/ppermute | solution.py:56
  26.6 4.3 %collective-permute-start.10 = (bf16[128,256]{1,0:T(8,128)(2,1)S(1)}, bf16[128,256]{1,0:T(8,128)(2,1)S(1)}, u32[]{:S(2)}, u32[]{:S(2)}) collective-permute-start(bf16[128,256]{1,0:T(8,128)(2,1)S(1)} %get-tuple-element.28.grad_ref.refs_3_), channel_id=1, source_target_pairs={{0,8},{4,12},{8,0},{12,4},{16,24},{20,28},{24,16},{28,20},{1,9},{5... | collective-permute-start | bytes 196616 | tf_op jit(solution)/shard_map/ppermute | solution.py:56
  29.8 4.4 %collective-permute-start.16 = (bf16[144,256]{1,0:T(8,128)(2,1)S(1)}, bf16[144,256]{1,0:T(8,128)(2,1)S(1)}, u32[]{:S(2)}, u32[]{:S(2)}) collective-permute-start(bf16[144,256]{1,0:T(8,128)(2,1)S(1)} %shard_map.128.refs_1_), channel_id=1, source_target_pairs={{0,1},{1,0},{2,3},{3,2},{4,5},{5,4},{6,7},{7,6},{8,9},{9,8},{10,11... | collective-permute-start | bytes 221192 | tf_op jit(solution)/shard_map/ppermute | solution.py:71
  30.9 5.3 %collective-permute-start.11 = (bf16[512,256]{1,0:T(8,128)(2,1)S(1)}, bf16[512,256]{1,0:T(8,128)(2,1)S(1)}, u32[]{:S(2)}, u32[]{:S(2)}) collective-permute-start(bf16[512,256]{1,0:T(8,128)(2,1)S(1)} %shard_map.123.source_ref), channel_id=1, source_target_pairs={{0,4},{4,0},{8,12},{12,8},{16,20},{20,16},{24,28},{28,24},{1,5},{5... | collective-permute-start | bytes 786440 | tf_op jit(solution)/shard_map/ppermute | solution.py:61
  34.2 4.8 %collective-permute-start.17 = (bf16[144,256]{1,0:T(8,128)(2,1)S(1)}, bf16[144,256]{1,0:T(8,128)(2,1)S(1)}, u32[]{:S(2)}, u32[]{:S(2)}) collective-permute-start(bf16[144,256]{1,0:T(8,128)(2,1)S(1)} %shard_map.129.refs_1_), channel_id=1, source_target_pairs={{0,16},{4,20},{8,24},{12,28},{16,0},{20,4},{24,8},{28,12},{1,17},{... | collective-permute-start | bytes 221192 | tf_op jit(solution)/shard_map/ppermute | solution.py:71
  36.5 6.4 %collective-permute-start.12 = (bf16[128,256]{1,0:T(8,128)(2,1)S(1)}, bf16[128,256]{1,0:T(8,128)(2,1)S(1)}, u32[]{:S(2)}, u32[]{:S(2)}) collective-permute-start(bf16[128,256]{1,0:T(8,128)(2,1)S(1)} %get-tuple-element.31), channel_id=1, source_target_pairs={{0,3},{1,2},{2,1},{3,0},{4,7},{5,6},{6,5},{7,4},{8,11},{9,10},{10,... | collective-permute-start | bytes 196616 | tf_op jit(solution)/shard_map/ppermute | solution.py:56
  39.0 5.6 %collective-permute-start.13 = (bf16[128,256]{1,0:T(8,128)(2,1)S(1)}, bf16[128,256]{1,0:T(8,128)(2,1)S(1)}, u32[]{:S(2)}, u32[]{:S(2)}) collective-permute-start(bf16[128,256]{1,0:T(8,128)(2,1)S(1)} %get-tuple-element.32), channel_id=1, source_target_pairs={{0,2},{1,3},{2,0},{3,1},{4,6},{5,7},{6,4},{7,5},{8,10},{9,11},{10,... | collective-permute-start | bytes 196616 | tf_op jit(solution)/shard_map/ppermute | solution.py:56
  39.0 5.6 %collective-permute-start.18 = (bf16[144,256]{1,0:T(8,128)(2,1)S(1)}, bf16[144,256]{1,0:T(8,128)(2,1)S(1)}, u32[]{:S(2)}, u32[]{:S(2)}) collective-permute-start(bf16[144,256]{1,0:T(8,128)(2,1)S(1)} %shard_map.130.refs_1_), channel_id=1, source_target_pairs={{0,8},{4,12},{8,0},{12,4},{16,24},{20,28},{24,16},{28,20},{1,9},{5... | collective-permute-start | bytes 221192 | tf_op jit(solution)/shard_map/ppermute | solution.py:71
  39.6 5.1 %collective-permute-start.14 = (bf16[128,256]{1,0:T(8,128)(2,1)S(1)}, bf16[128,256]{1,0:T(8,128)(2,1)S(1)}, u32[]{:S(2)}, u32[]{:S(2)}) collective-permute-start(bf16[128,256]{1,0:T(8,128)(2,1)S(1)} %get-tuple-element.34), channel_id=1, source_target_pairs={{0,1},{1,0},{2,3},{3,2},{4,5},{5,4},{6,7},{7,6},{8,9},{9,8},{10,11... | collective-permute-start | bytes 196616 | tf_op jit(solution)/shard_map/ppermute | solution.py:56
  44.7 1.4 %collective-permute-start.19 = (f32[128,256]{1,0:T(8,128)S(1)}, f32[128,256]{1,0:T(8,128)S(1)}, u32[]{:S(2)}, u32[]{:S(2)}) collective-permute-start(f32[128,256]{1,0:T(8,128)S(1)} %get-tuple-element.35.own_ref), channel_id=1, source_target_pairs={{0,4},{4,0},{8,12},{12,8},{16,20},{20,16},{24,28},{28,24},{1,5},{5... | collective-permute-start | bytes 393224 | tf_op jit(solution)/shard_map/ppermute | solution.py:61

commit v13 on v12

--- a/solution.py
+++ b/solution.py
@@ -13,7 +13,6 @@
 CUBIC = 0.044715
 VMEM_LIMIT = 48 * 1024 * 1024
 BIAS_ROWS = 16
-BACK_SUM_WEIGHT = 30
 ROW_SUM_WEIGHT = 120
 FEATURES_WEIGHT = 100
 
@@ -65,11 +64,11 @@
     count = size // cores
     if count & (count - 1):
         return exchange([block] * count, axis, size, cores)
-    terms, step = [block], count // 2
-    while step:
+    terms, step = [block], 1
+    while step < count:
         block = add(terms) if len(terms) > 1 else block
         terms = [lax.ppermute(block, axis, pairs_of(step, size, cores)), block]
-        step //= 2
+        step *= 2
     return terms
 
 
@@ -262,12 +261,29 @@
     out_ref[...] = dense_dot(turned_ref[:, : source_ref.shape[0]], source_ref[...])
 
 
-def back_pieces_kernel(turned_ref, own_ref, source_ref, *outs):
-    tile = outs[0].shape[0]
-    for k, out_ref in zip(far_first(len(outs)), outs):
-        rows = block_at(partner(row_index(), k, len(outs)), tile)
+def back_pieces_kernel(turned_ref, own_ref, source_ref, near_ref, *far_refs):
+    tile = far_refs[0].shape[0]
+
+    def rows_for(k):
+        rows = block_at(row_index() ^ k, tile)
         rest = dense_dot(turned_ref[rows, source_ref.shape[0] :], source_ref[...])
-        out_ref[...] = (own_ref[rows, :] + rest).astype(BF16)
+        return own_ref[rows, :] + rest
+
+    write_pieces(rows_for, near_ref, far_refs)
+
+
+def write_pieces(rows_for, near_ref, far_refs):
+    tile = far_refs[0].shape[0]
+    for i in range(len(far_refs)):
+        near_ref[i * tile : (i + 1) * tile, :] = rows_for(2 * i or 1).astype(BF16)
+    for i, ref in enumerate(far_refs):
+        ref[...] = rows_for(2 * i + 1 if i else 0)
+
+
+def far_sum_kernel(near_ref, far_ref, out_ref, *, at):
+    tile = out_ref.shape[0]
+    near = near_ref[at * tile : (at + 1) * tile, :].astype(F32)
+    out_ref[...] = (near + far_ref[...]).astype(BF16)
 
 
 def slot_back_kernel(count_ref, row_ref, col_ref, tiles_ref, own_ref, other_ref, *refs):
@@ -276,22 +292,17 @@
     source_ref[:half, :] = own_ref[...]
     source_ref[half:, :] = other_ref[...]
     slot_product((count_ref, row_ref, col_ref, tiles_ref), source_ref, acc_ref, True)
-    tile = outs[0].shape[0]
-    for k, out_ref in zip(far_first(len(outs)), outs):
-        rows = block_at(partner(row_index(), k, len(outs)), tile)
-        out_ref[...] = acc_ref[rows, :].astype(BF16)
-
-
-def back_sum_kernel(*refs):
-    total = refs[0][...].astype(F32)
-    for ref in refs[1:-1]:
+    tile = outs[1].shape[0]
+    write_pieces(lambda k: acc_ref[block_at(row_index() ^ k, tile), :], outs[0], outs[1:])
+
+
+def features_kernel(weight_ref, near_ref, own_ref, *refs):
+    parts, out_ref = refs[:-1], refs[-1]
+    total = own_ref[...] + near_ref[: out_ref.shape[0], :].astype(F32)
+    for ref in parts:
         total += ref[...].astype(F32)
-    refs[-1][...] = total
-
-
-def features_kernel(weight_ref, most_ref, last_ref, out_ref):
     out_ref[...] = lax.dot_general(
-        (most_ref[...] + last_ref[...].astype(F32)).astype(BF16),
+        total.astype(BF16),
         weight_ref[...],
         (((1,), (1,)), ((), ())),
         preferred_element_type=F32,
@@ -471,41 +482,44 @@
             slots * matrix // 2,
             row_nodes * hidden * 8,
         )(turned, own_grads)
-        back_pieces = call(
+        near_piece, *far_pieces = call(
             back_pieces_kernel,
-            [like(tile, hidden)] * n_row,
+            [like(n_row // 2 * tile, hidden)] + [like(tile, hidden, F32)] * (n_row // 2),
             [VMEM_SPEC] * 3,
             [],
             slots * matrix // 2,
             row_nodes * hidden * 8,
         )(turned, back_own, other_grads)
     else:
-        back_pieces = call(
+        near_piece, *far_pieces = call(
             slot_back_kernel,
-            [like(tile, hidden)] * n_row,
+            [like(n_row // 2 * tile, hidden)] + [like(tile, hidden, F32)] * (n_row // 2),
             slot_specs + [VMEM_SPEC] * 2,
             [pltpu.VMEM((row_nodes, hidden), BF16), pltpu.VMEM((col_nodes, hidden), F32)],
             slots * matrix // 2,
             row_nodes * hidden * 8,
         )(*slot_args, own_grads, other_grads)
-    backs = exchange(dict(zip(far_first(n_row), back_pieces)), "row", n_row)
-    most = call(
-        back_sum_kernel,
-        like(tile, hidden, F32),
-        [VMEM_SPEC] * (n_row - 1),
-        [],
-        BACK_SUM_WEIGHT * matrix,
-        n_row * block_bytes,
-    )(*backs[:-2], backs[-1])
+    near = lax.ppermute(near_piece, "row", pairs_of(1, n_row, 1))
+    backs = []
+    for i in range(1, n_row // 2):
+        piece = call(
+            functools.partial(far_sum_kernel, at=i),
+            like(tile, hidden),
+            [VMEM_SPEC] * 2,
+            [],
+            tile * hidden,
+            4 * block_bytes,
+        )(near, far_pieces[i])
+        backs.append(lax.ppermute(piece, "row", pairs_of(2 * i + 1, n_row, 1)))
     own_features = call(
         features_kernel,
         like(tile, width),
-        [VMEM_SPEC] * 3,
+        [VMEM_SPEC] * (3 + len(backs)),
         [],
         FEATURES_WEIGHT * matrix,
         n_row * block_bytes,
-    )(weight, most, backs[-2])
-    all_terms = total_over(row_term, add, "col", n_col, 2)
+    )(weight, near, far_pieces[0], *backs)
+    all_terms = total_over(row_term, add_late, "col", n_col, 2)
     factor = (tile * n_row * n_col) ** (-0.5)
     own_half, bias_grad = call(
         functools.partial(scale_kernel, factor=factor),
@@ -514,7 +528,7 @@
         [],
         len(all_terms) * half * hidden,
         len(all_terms) * half * hidden * 2,
-    )(most, *all_terms)
+    )(near, *all_terms)
     grad_features, grad_weight, grad_bias = call(
         write_kernel,
         (like(tile, width), like(width, hidden, F32), like(1, hidden, F32)),

time: 47 us -> 47.6 us (1.013)
  waiting for transfers between devices: 18.4 us -> 18.9 us
    ppermute x12 -> x9, starting transfers between devices: 17.4 us -> 12.9 us  [exchange(): lax.ppermute(blocks[k], axis, pairs)]
    ppermute x0 -> x2, waiting for transfers between devices: none -> 3.45 us  [the longest x1 2.82 us: local(): backs.append(lax.ppermute(piece, 'row', pairs_of(2 * i + 1, n_row, 1)))]
    ppermute x0 -> x2, starting transfers between devices: none -> 2.88 us  [the longest x1 2.56 us: local(): backs.append(lax.ppermute(piece, 'row', pairs_of(2 * i + 1, n_row, 1)))]
    ppermute x12 -> x9, waiting for transfers between devices: 10.1 us -> 7.27 us  [exchange(): lax.ppermute(blocks[k], axis, pairs)]
    ppermute x4, starting transfers between devices: 3.89 us -> 5.62 us  [total_over(): terms = [lax.ppermute(block, axis, pairs_of(step, size, cores)), block]]
    ppermute x4, waiting for transfers between devices: 3.6 us -> 2.48 us  [swap_cores(): return lax.ppermute(block, 'col', [(i, i ^ 1) for i in range(size)])]
    ppermute x4, waiting for transfers between devices: 4.65 us -> 5.69 us  [total_over(): terms = [lax.ppermute(block, axis, pairs_of(step, size, cores)), block]]
  transfers between devices with their start and end apart: 20 -> 19, of which waited for: 15 -> 13; matrix products, arithmetic and copies ran while one was open for 0% -> 0% of each run, Pallas kernels for 8% -> 8%
where the time goes in v13:
time: 47.6 us; the launch traced here: 47.5 us
  starting transfers between devices  21.7 us (46%)
  waiting for transfers between devices  18.9 us (40%)
  Pallas kernels  5.39 us (11%)
  between operations  1.47 us (3%)
    ppermute x9, starting transfers between devices, exchange(): lax.ppermute(blocks[k], axis, pairs)  12.9 us
    ppermute x9, waiting for transfers between devices, exchange(): lax.ppermute(blocks[k], axis, pairs)  7.27 us
    ppermute x4, waiting for transfers between devices, total_over(): terms = [lax.ppermute(block, axis, pairs_of(step, size, cores)), block]  5.69 us
    ppermute x4, starting transfers between devices, total_over(): terms = [lax.ppermute(block, axis, pairs_of(step, size, cores)), block]  5.62 us
    ppermute x1, waiting for transfers between devices, local(): backs.append(lax.ppermute(piece, 'row', pairs_of(2 * i + 1, n_row, 1)))  2.82 us
    ppermute x1, starting transfers between devices, local(): backs.append(lax.ppermute(piece, 'row', pairs_of(2 * i + 1, n_row, 1)))  2.56 us
    ppermute x4, waiting for transfers between devices, swap_cores(): return lax.ppermute(block, 'col', [(i, i ^ 1) for i in range(size)])  2.48 us
    pallas_call x1, Pallas kernels, local(): call(dense_kernel, (like(row_nodes, col_nodes), like(1, hidden, F32)), [S...  1.45 us
  transfers between devices with their start and end apart: 19, of which 13 were waited for; matrix products, arithmetic and copies ran while one was open for 0% of the time, Pallas kernels for 8%

profile of v13, /device:TPU:0, one launch (start us, length us, event | category | flops | bytes accessed | tf_op | source)
XLA Modules:
  0.0 47.5 jit_solution(11907101069440817157)
XLA Ops:
  0.6 5.1 %collective-permute-start = (bf16[128,256]{1,0:T(8,128)(2,1)}, bf16[128,256]{1,0:T(8,128)(2,1)S(1)}, u32[]{:S(2)}, u32[]{:S(2)}) collective-permute-start(bf16[128,256]{1,0:T(8,128)(2,1)} %refs_3_.1), channel_id=1, source_target_pairs={{0,3},{1,2},{2,1},{3,0},{4,7},{5,6},{6,5},{7,4},{8,11},{9,10},{10,... | collective-permute-start | bytes 196616 | tf_op jit(solution)/shard_map/ppermute | solution.py:55
  5.8 0.6 %collective-permute-start.2 = (bf16[128,256]{1,0:T(8,128)(2,1)}, bf16[128,256]{1,0:T(8,128)(2,1)S(1)}, u32[]{:S(2)}, u32[]{:S(2)}) collective-permute-start(bf16[128,256]{1,0:T(8,128)(2,1)} %refs_3_.1), channel_id=1, source_target_pairs={{0,1},{1,0},{2,3},{3,2},{4,5},{5,4},{6,7},{7,6},{8,9},{9,8},{10,11... | collective-permute-start | bytes 196616 | tf_op jit(solution)/shard_map/ppermute | solution.py:55
  7.1 1.5 %shard_map.111 = (bf16[1024,512]{1,0:T(8,128)(2,1)S(1)}, f32[1,256]{1,0:T(1,128)S(1)}) custom-call(s32[1,1]{1,0:T(1,128)S(6)} %copy.12.count_ref, s32[1,1,32]{2,1,0:T(1,128)} %row_hbm.1, s32[1,1,32]{2,1,0:T(1,128)} %col_hbm.1, bf16[1,1,32,128,128]{4,3,2,1,0:T(8,128)(2,1)} %tiles_hbm.1, f32[1,256]{1,0:T(1,128)} %bitcast.2), custom_call_target="tpu_custom_call" | custom-call | bytes 6291456 | tf_op jit(solution)/shard_map/pallas_call | solution.py:368
  8.6 3.0 %collective-permute-done.1.refs_1_ = bf16[128,256]{1,0:T(8,128)(2,1)S(1)} collective-permute-done((bf16[128,256]{1,0:T(8,128)(2,1)}, bf16[128,256]{1,0:T(8,128)(2,1)S(1)}, u32[]{:S(2)}, u32[]{:S(2)}) %collective-permute-start.1) | collective-permute-done | bytes 65568 | tf_op jit(solution)/shard_map/ppermute | solution.py:55
  11.6 0.3 shard_map.112
  12.3 1.2 %collective-permute-done.3.other_ref = bf16[512,256]{1,0:T(8,128)(2,1)S(1)} collective-permute-done((bf16[512,256]{1,0:T(8,128)(2,1)S(1)}, bf16[512,256]{1,0:T(8,128)(2,1)S(1)}, u32[]{:S(2)}, u32[]{:S(2)}) %collective-permute-start.3) | collective-permute-done | bytes 262176 | tf_op jit(solution)/shard_map/ppermute | solution.py:60
  13.5 2.5 %collective-permute-start.4 = (bf16[128,256]{1,0:T(8,128)(2,1)S(1)}, bf16[128,256]{1,0:T(8,128)(2,1)S(1)}, u32[]{:S(2)}, u32[]{:S(2)}) collective-permute-start(bf16[128,256]{1,0:T(8,128)(2,1)S(1)} %shard_map.114.refs_0_), channel_id=1, source_target_pairs={{0,24},{4,28},{8,16},{12,20},{16,8},{20,12},{24,0},{28,4},{1,25},{... | collective-permute-start | bytes 196616 | tf_op jit(solution)/shard_map/ppermute | solution.py:55
  16.1 0.6 %collective-permute-start.5 = (bf16[128,256]{1,0:T(8,128)(2,1)S(1)}, bf16[128,256]{1,0:T(8,128)(2,1)S(1)}, u32[]{:S(2)}, u32[]{:S(2)}) collective-permute-start(bf16[128,256]{1,0:T(8,128)(2,1)S(1)} %shard_map.115.refs_0_), channel_id=1, source_target_pairs={{0,16},{4,20},{8,24},{12,28},{16,0},{20,4},{24,8},{28,12},{1,17},{... | collective-permute-start | bytes 196616 | tf_op jit(solution)/shard_map/ppermute | solution.py:55
  16.7 0.6 %collective-permute-start.6 = (bf16[128,256]{1,0:T(8,128)(2,1)S(1)}, bf16[128,256]{1,0:T(8,128)(2,1)S(1)}, u32[]{:S(2)}, u32[]{:S(2)}) collective-permute-start(bf16[128,256]{1,0:T(8,128)(2,1)S(1)} %shard_map.116.refs_0_), channel_id=1, source_target_pairs={{0,8},{4,12},{8,0},{12,4},{16,24},{20,28},{24,16},{28,20},{1,9},{5... | collective-permute-start | bytes 196616 | tf_op jit(solution)/shard_map/ppermute | solution.py:55
  17.3 1.5 %collective-permute-done.4.refs_0_ = bf16[128,256]{1,0:T(8,128)(2,1)S(1)} collective-permute-done((bf16[128,256]{1,0:T(8,128)(2,1)S(1)}, bf16[128,256]{1,0:T(8,128)(2,1)S(1)}, u32[]{:S(2)}, u32[]{:S(2)}) %collective-permute-start.4) | collective-permute-done | bytes 65568 | tf_op jit(solution)/shard_map/ppermute | solution.py:55
  18.8 1.6 %collective-permute-done.5.refs_1_ = bf16[128,256]{1,0:T(8,128)(2,1)S(1)} collective-permute-done((bf16[128,256]{1,0:T(8,128)(2,1)S(1)}, bf16[128,256]{1,0:T(8,128)(2,1)S(1)}, u32[]{:S(2)}, u32[]{:S(2)}) %collective-permute-start.5) | collective-permute-done | bytes 65568 | tf_op jit(solution)/shard_map/ppermute | solution.py:55
  20.4 0.6 %collective-permute-done.6.refs_2_ = bf16[128,256]{1,0:T(8,128)(2,1)S(1)} collective-permute-done((bf16[128,256]{1,0:T(8,128)(2,1)S(1)}, bf16[128,256]{1,0:T(8,128)(2,1)S(1)}, u32[]{:S(2)}, u32[]{:S(2)}) %collective-permute-start.6) | collective-permute-done | bytes 65568 | tf_op jit(solution)/shard_map/ppermute | solution.py:55
  21.6 1.3 %collective-permute-done.7.refs_0_ = bf16[144,256]{1,0:T(8,128)(2,1)S(1)} collective-permute-done((bf16[144,256]{1,0:T(8,128)(2,1)S(1)}, bf16[144,256]{1,0:T(8,128)(2,1)S(1)}, u32[]{:S(2)}, u32[]{:S(2)}) %collective-permute-start.7) | collective-permute-done | bytes 73760 | tf_op jit(solution)/shard_map/ppermute | solution.py:60
  22.9 1.1 %collective-permute-start.14 = (bf16[144,256]{1,0:T(8,128)(2,1)S(1)}, bf16[144,256]{1,0:T(8,128)(2,1)S(1)}, u32[]{:S(2)}, u32[]{:S(2)}) collective-permute-start(bf16[144,256]{1,0:T(8,128)(2,1)S(1)} %shard_map.122.after_ref.refs_1_), channel_id=1, source_target_pairs={{0,1},{1,0},{2,3},{3,2},{4,5},{5,4},{6,7},{7,6},{8,9},{9,8},{10,11... | collective-permute-start | bytes 221192 | tf_op jit(solution)/shard_map/ppermute | solution.py:70
  24.0 1.5 %collective-permute-start.8 = (bf16[128,256]{1,0:T(8,128)(2,1)S(1)}, bf16[128,256]{1,0:T(8,128)(2,1)S(1)}, u32[]{:S(2)}, u32[]{:S(2)}) collective-permute-start(bf16[128,256]{1,0:T(8,128)(2,1)S(1)} %get-tuple-element.27.grad_ref.refs_3_), channel_id=1, source_target_pairs={{0,24},{4,28},{8,16},{12,20},{16,8},{20,12},{24,0},{28,4},{1,25},{... | collective-permute-start | bytes 196616 | tf_op jit(solution)/shard_map/ppermute | solution.py:55
  25.5 0.5 %collective-permute-start.9 = (bf16[128,256]{1,0:T(8,128)(2,1)S(1)}, bf16[128,256]{1,0:T(8,128)(2,1)S(1)}, u32[]{:S(2)}, u32[]{:S(2)}) collective-permute-start(bf16[128,256]{1,0:T(8,128)(2,1)S(1)} %get-tuple-element.27.grad_ref.refs_3_), channel_id=1, source_target_pairs={{0,16},{4,20},{8,24},{12,28},{16,0},{20,4},{24,8},{28,12},{1,17},{... | collective-permute-start | bytes 196616 | tf_op jit(solution)/shard_map/ppermute | solution.py:55
  26.1 1.5 %collective-permute-start.10 = (bf16[128,256]{1,0:T(8,128)(2,1)S(1)}, bf16[128,256]{1,0:T(8,128)(2,1)S(1)}, u32[]{:S(2)}, u32[]{:S(2)}) collective-permute-start(bf16[128,256]{1,0:T(8,128)(2,1)S(1)} %get-tuple-element.27.grad_ref.refs_3_), channel_id=1, source_target_pairs={{0,8},{4,12},{8,0},{12,4},{16,24},{20,28},{24,16},{28,20},{1,9},{5... | collective-permute-start | bytes 196616 | tf_op jit(solution)/shard_map/ppermute | solution.py:55
  27.6 2.3 %collective-permute-start.15 = (bf16[144,256]{1,0:T(8,128)(2,1)S(1)}, bf16[144,256]{1,0:T(8,128)(2,1)S(1)}, u32[]{:S(2)}, u32[]{:S(2)}) collective-permute-start(bf16[144,256]{1,0:T(8,128)(2,1)S(1)} %shard_map.128.refs_1_), channel_id=1, source_target_pairs={{0,2},{1,3},{2,0},{3,1},{4,6},{5,7},{6,4},{7,5},{8,10},{9,11},{10,... | collective-permute-start | bytes 221192 | tf_op jit(solution)/shard_map/ppermute | solution.py:70
  29.8 0.4 collective-permute-done.9.refs_1_
  30.5 3.2 %collective-permute-done.15.refs_0_ = bf16[144,256]{1,0:T(8,128)(2,1)S(1)} collective-permute-done((bf16[144,256]{1,0:T(8,128)(2,1)S(1)}, bf16[144,256]{1,0:T(8,128)(2,1)S(1)}, u32[]{:S(2)}, u32[]{:S(2)}) %collective-permute-start.15) | collective-permute-done | bytes 73760 | tf_op jit(solution)/shard_map/ppermute | solution.py:70
  33.7 0.6 %collective-permute-start.16 = (bf16[144,256]{1,0:T(8,128)(2,1)S(1)}, bf16[144,256]{1,0:T(8,128)(2,1)S(1)}, u32[]{:S(2)}, u32[]{:S(2)}) collective-permute-start(bf16[144,256]{1,0:T(8,128)(2,1)S(1)} %shard_map.129.refs_1_), channel_id=1, source_target_pairs={{0,8},{4,12},{8,0},{12,4},{16,24},{20,28},{24,16},{28,20},{1,9},{5... | collective-permute-start | bytes 221192 | tf_op jit(solution)/shard_map/ppermute | solution.py:70
  34.3 0.3 shard_map.120.turned_ref
  34.7 0.3 shard_map.124.own_ref
  35.0 0.3 shard_map.125
  35.3 0.3 collective-permute-start.12
  35.7 2.5 %collective-permute-done.16.refs_0_ = bf16[144,256]{1,0:T(8,128)(2,1)S(1)} collective-permute-done((bf16[144,256]{1,0:T(8,128)(2,1)S(1)}, bf16[144,256]{1,0:T(8,128)(2,1)S(1)}, u32[]{:S(2)}, u32[]{:S(2)}) %collective-permute-start.16) | collective-permute-done | bytes 73760 | tf_op jit(solution)/shard_map/ppermute | solution.py:70
  38.1 1.6 %collective-permute-start.17 = (bf16[144,256]{1,0:T(8,128)(2,1)S(1)}, bf16[144,256]{1,0:T(8,128)(2,1)S(1)}, u32[]{:S(2)}, u32[]{:S(2)}) collective-permute-start(bf16[144,256]{1,0:T(8,128)(2,1)S(1)} %shard_map.130.refs_1_), channel_id=1, source_target_pairs={{0,16},{4,20},{8,24},{12,28},{16,0},{20,4},{24,8},{28,12},{1,17},{... | collective-permute-start | bytes 221192 | tf_op jit(solution)/shard_map/ppermute | solution.py:70
  39.7 0.6 %collective-permute-done.12.near_ref.after_ref = bf16[256,256]{1,0:T(8,128)(2,1)S(1)} collective-permute-done((bf16[256,256]{1,0:T(8,128)(2,1)S(1)}, bf16[256,256]{1,0:T(8,128)(2,1)S(1)}, u32[]{:S(2)}, u32[]{:S(2)}) %collective-permute-start.12) | collective-permute-done | bytes 131104 | tf_op jit(solution)/shard_map/ppermute | solution.py:502
  40.4 2.6 %collective-permute-start.13 = (bf16[128,256]{1,0:T(8,128)(2,1)S(1)}, bf16[128,256]{1,0:T(8,128)(2,1)S(1)}, u32[]{:S(2)}, u32[]{:S(2)}) collective-permute-start(bf16[128,256]{1,0:T(8,128)(2,1)S(1)} %shard_map.126), channel_id=1, source_target_pairs={{0,3},{1,2},{2,1},{3,0},{4,7},{5,6},{6,5},{7,4},{8,11},{9,10},{10,... | collective-permute-start | bytes 196616 | tf_op jit(solution)/shard_map/ppermute | solution.py:513
  42.9 0.6 %shard_map.119 = bf16[128,256]{1,0:T(8,128)(2,1)} custom-call(bf16[128,256]{1,0:T(8,128)(2,1)S(1)} %get-tuple-element.25.in_ref), custom_call_target="tpu_custom_call" | custom-call | bytes 131072 | tf_op jit(solution)/shard_map/pallas_call | solution.py:454
  43.7 2.8 %collective-permute-done.13.refs_0_ = bf16[128,256]{1,0:T(8,128)(2,1)S(1)} collective-permute-done((bf16[128,256]{1,0:T(8,128)(2,1)S(1)}, bf16[128,256]{1,0:T(8,128)(2,1)S(1)}, u32[]{:S(2)}, u32[]{:S(2)}) %collective-permute-start.13) | collective-permute-done | bytes 65568 | tf_op jit(solution)/shard_map/ppermute | solution.py:513
  46.7 0.8 %shard_map.132 = (bf16[128,256]{1,0:T(8,128)(2,1)}, f32[256,256]{1,0:T(8,128)}, f32[1,256]{1,0:T(1,128)}) custom-call(bf16[128,256]{1,0:T(8,128)(2,1)S(1)} %shard_map.127.features_ref, f32[128,256]{1,0:T(8,128)S(1)} %get-tuple-element.33.own_ref, f32[128,256]{1,0:T(8,128)S(1)} %collective-permute-done.18.other_ref, f32[1,256]{1,0:T(1,128)S(1)} %get-tuple-element.34.bias_ref), custom_call_target="tpu_custom_call" | custom-call | bytes 524288 | tf_op jit(solution)/shard_map/pallas_call | solution.py:532
  (34 shorter events, 1.7 us)
Async XLA Ops:
  0.6 7.9 %collective-permute-start = (bf16[128,256]{1,0:T(8,128)(2,1)}, bf16[128,256]{1,0:T(8,128)(2,1)S(1)}, u32[]{:S(2)}, u32[]{:S(2)}) collective-permute-start(bf16[128,256]{1,0:T(8,128)(2,1)} %refs_3_.1), channel_id=1, source_target_pairs={{0,3},{1,2},{2,1},{3,0},{4,7},{5,6},{6,5},{7,4},{8,11},{9,10},{10,... | collective-permute-start | bytes 196616 | tf_op jit(solution)/shard_map/ppermute | solution.py:55
  5.7 5.8 %collective-permute-start.1 = (bf16[128,256]{1,0:T(8,128)(2,1)}, bf16[128,256]{1,0:T(8,128)(2,1)S(1)}, u32[]{:S(2)}, u32[]{:S(2)}) collective-permute-start(bf16[128,256]{1,0:T(8,128)(2,1)} %refs_3_.1), channel_id=1, source_target_pairs={{0,2},{1,3},{2,0},{3,1},{4,6},{5,7},{6,4},{7,5},{8,10},{9,11},{10,... | collective-permute-start | bytes 196616 | tf_op jit(solution)/shard_map/ppermute | solution.py:55
  5.8 5.8 %collective-permute-start.2 = (bf16[128,256]{1,0:T(8,128)(2,1)}, bf16[128,256]{1,0:T(8,128)(2,1)S(1)}, u32[]{:S(2)}, u32[]{:S(2)}) collective-permute-start(bf16[128,256]{1,0:T(8,128)(2,1)} %refs_3_.1), channel_id=1, source_target_pairs={{0,1},{1,0},{2,3},{3,2},{4,5},{5,4},{6,7},{7,6},{8,9},{9,8},{10,11... | collective-permute-start | bytes 196616 | tf_op jit(solution)/shard_map/ppermute | solution.py:55
  7.0 4.5 %copy-start.1 = (bf16[128,256]{1,0:T(8,128)(2,1)S(1)}, bf16[128,256]{1,0:T(8,128)(2,1)}, u32[]{:S(2)}) copy-start(bf16[128,256]{1,0:T(8,128)(2,1)} %refs_3_.1) | copy-start | bytes 196612
  11.9 1.6 %collective-permute-start.3 = (bf16[512,256]{1,0:T(8,128)(2,1)S(1)}, bf16[512,256]{1,0:T(8,128)(2,1)S(1)}, u32[]{:S(2)}, u32[]{:S(2)}) collective-permute-start(bf16[512,256]{1,0:T(8,128)(2,1)S(1)} %get-tuple-element.24), channel_id=1, source_target_pairs={{0,4},{4,0},{8,12},{12,8},{16,20},{20,16},{24,28},{28,24},{1,5},{5... | collective-permute-start | bytes 786440 | tf_op jit(solution)/shard_map/ppermute | solution.py:60
  13.5 5.2 %collective-permute-start.4 = (bf16[128,256]{1,0:T(8,128)(2,1)S(1)}, bf16[128,256]{1,0:T(8,128)(2,1)S(1)}, u32[]{:S(2)}, u32[]{:S(2)}) collective-permute-start(bf16[128,256]{1,0:T(8,128)(2,1)S(1)} %shard_map.114.refs_0_), channel_id=1, source_target_pairs={{0,24},{4,28},{8,16},{12,20},{16,8},{20,12},{24,0},{28,4},{1,25},{... | collective-permute-start | bytes 196616 | tf_op jit(solution)/shard_map/ppermute | solution.py:55
  16.1 4.3 %collective-permute-start.5 = (bf16[128,256]{1,0:T(8,128)(2,1)S(1)}, bf16[128,256]{1,0:T(8,128)(2,1)S(1)}, u32[]{:S(2)}, u32[]{:S(2)}) collective-permute-start(bf16[128,256]{1,0:T(8,128)(2,1)S(1)} %shard_map.115.refs_0_), channel_id=1, source_target_pairs={{0,16},{4,20},{8,24},{12,28},{16,0},{20,4},{24,8},{28,12},{1,17},{... | collective-permute-start | bytes 196616 | tf_op jit(solution)/shard_map/ppermute | solution.py:55
  16.6 4.4 %copy-start = (bf16[256,256]{1,0:T(8,128)(2,1)S(1)}, bf16[256,256]{1,0:T(8,128)(2,1)}, u32[]{:S(2)}) copy-start(bf16[256,256]{1,0:T(8,128)(2,1)} %weight_ref.3) | copy-start | bytes 393220
  16.7 4.3 %copy-start.2 = (bf16[128,256]{1,0:T(8,128)(2,1)S(1)}, bf16[128,256]{1,0:T(8,128)(2,1)}, u32[]{:S(2)}) copy-start(bf16[128,256]{1,0:T(8,128)(2,1)} %cot_ref.1) | copy-start | bytes 196612
  16.7 4.3 %collective-permute-start.6 = (bf16[128,256]{1,0:T(8,128)(2,1)S(1)}, bf16[128,256]{1,0:T(8,128)(2,1)S(1)}, u32[]{:S(2)}, u32[]{:S(2)}) collective-permute-start(bf16[128,256]{1,0:T(8,128)(2,1)S(1)} %shard_map.116.refs_0_), channel_id=1, source_target_pairs={{0,8},{4,12},{8,0},{12,4},{16,24},{20,28},{24,16},{28,20},{1,9},{5... | collective-permute-start | bytes 196616 | tf_op jit(solution)/shard_map/ppermute | solution.py:55
  21.5 1.3 %collective-permute-start.7 = (bf16[144,256]{1,0:T(8,128)(2,1)S(1)}, bf16[144,256]{1,0:T(8,128)(2,1)S(1)}, u32[]{:S(2)}, u32[]{:S(2)}) collective-permute-start(bf16[144,256]{1,0:T(8,128)(2,1)S(1)} %get-tuple-element.28), channel_id=1, source_target_pairs={{0,4},{4,0},{8,12},{12,8},{16,20},{20,16},{24,28},{28,24},{1,5},{5... | collective-permute-start | bytes 221192 | tf_op jit(solution)/shard_map/ppermute | solution.py:60
  22.9 4.6 %collective-permute-start.14 = (bf16[144,256]{1,0:T(8,128)(2,1)S(1)}, bf16[144,256]{1,0:T(8,128)(2,1)S(1)}, u32[]{:S(2)}, u32[]{:S(2)}) collective-permute-start(bf16[144,256]{1,0:T(8,128)(2,1)S(1)} %shard_map.122.after_ref.refs_1_), channel_id=1, source_target_pairs={{0,1},{1,0},{2,3},{3,2},{4,5},{5,4},{6,7},{7,6},{8,9},{9,8},{10,11... | collective-permute-start | bytes 221192 | tf_op jit(solution)/shard_map/ppermute | solution.py:70
  24.0 5.8 %collective-permute-start.8 = (bf16[128,256]{1,0:T(8,128)(2,1)S(1)}, bf16[128,256]{1,0:T(8,128)(2,1)S(1)}, u32[]{:S(2)}, u32[]{:S(2)}) collective-permute-start(bf16[128,256]{1,0:T(8,128)(2,1)S(1)} %get-tuple-element.27.grad_ref.refs_3_), channel_id=1, source_target_pairs={{0,24},{4,28},{8,16},{12,20},{16,8},{20,12},{24,0},{28,4},{1,25},{... | collective-permute-start | bytes 196616 | tf_op jit(solution)/shard_map/ppermute | solution.py:55
  25.5 4.7 %collective-permute-start.9 = (bf16[128,256]{1,0:T(8,128)(2,1)S(1)}, bf16[128,256]{1,0:T(8,128)(2,1)S(1)}, u32[]{:S(2)}, u32[]{:S(2)}) collective-permute-start(bf16[128,256]{1,0:T(8,128)(2,1)S(1)} %get-tuple-element.27.grad_ref.refs_3_), channel_id=1, source_target_pairs={{0,16},{4,20},{8,24},{12,28},{16,0},{20,4},{24,8},{28,12},{1,17},{... | collective-permute-start | bytes 196616 | tf_op jit(solution)/shard_map/ppermute | solution.py:55
  26.1 4.3 %collective-permute-start.10 = (bf16[128,256]{1,0:T(8,128)(2,1)S(1)}, bf16[128,256]{1,0:T(8,128)(2,1)S(1)}, u32[]{:S(2)}, u32[]{:S(2)}) collective-permute-start(bf16[128,256]{1,0:T(8,128)(2,1)S(1)} %get-tuple-element.27.grad_ref.refs_3_), channel_id=1, source_target_pairs={{0,8},{4,12},{8,0},{12,4},{16,24},{20,28},{24,16},{28,20},{1,9},{5... | collective-permute-start | bytes 196616 | tf_op jit(solution)/shard_map/ppermute | solution.py:55
  27.6 6.1 %collective-permute-start.15 = (bf16[144,256]{1,0:T(8,128)(2,1)S(1)}, bf16[144,256]{1,0:T(8,128)(2,1)S(1)}, u32[]{:S(2)}, u32[]{:S(2)}) collective-permute-start(bf16[144,256]{1,0:T(8,128)(2,1)S(1)} %shard_map.128.refs_1_), channel_id=1, source_target_pairs={{0,2},{1,3},{2,0},{3,1},{4,6},{5,7},{6,4},{7,5},{8,10},{9,11},{10,... | collective-permute-start | bytes 221192 | tf_op jit(solution)/shard_map/ppermute | solution.py:70
  30.4 4.6 %collective-permute-start.11 = (bf16[512,256]{1,0:T(8,128)(2,1)S(1)}, bf16[512,256]{1,0:T(8,128)(2,1)S(1)}, u32[]{:S(2)}, u32[]{:S(2)}) collective-permute-start(bf16[512,256]{1,0:T(8,128)(2,1)S(1)} %shard_map.123.source_ref), channel_id=1, source_target_pairs={{0,4},{4,0},{8,12},{12,8},{16,20},{20,16},{24,28},{28,24},{1,5},{5... | collective-permute-start | bytes 786440 | tf_op jit(solution)/shard_map/ppermute | solution.py:60
  33.7 4.4 %collective-permute-start.16 = (bf16[144,256]{1,0:T(8,128)(2,1)S(1)}, bf16[144,256]{1,0:T(8,128)(2,1)S(1)}, u32[]{:S(2)}, u32[]{:S(2)}) collective-permute-start(bf16[144,256]{1,0:T(8,128)(2,1)S(1)} %shard_map.129.refs_1_), channel_id=1, source_target_pairs={{0,8},{4,12},{8,0},{12,4},{16,24},{20,28},{24,16},{28,20},{1,9},{5... | collective-permute-start | bytes 221192 | tf_op jit(solution)/shard_map/ppermute | solution.py:70
  35.3 5.0 %collective-permute-start.12 = (bf16[256,256]{1,0:T(8,128)(2,1)S(1)}, bf16[256,256]{1,0:T(8,128)(2,1)S(1)}, u32[]{:S(2)}, u32[]{:S(2)}) collective-permute-start(bf16[256,256]{1,0:T(8,128)(2,1)S(1)} %get-tuple-element.30), channel_id=1, source_target_pairs={{0,1},{1,0},{2,3},{3,2},{4,5},{5,4},{6,7},{7,6},{8,9},{9,8},{10,11... | collective-permute-start | bytes 393224 | tf_op jit(solution)/shard_map/ppermute | solution.py:502
  38.1 5.4 %collective-permute-start.17 = (bf16[144,256]{1,0:T(8,128)(2,1)S(1)}, bf16[144,256]{1,0:T(8,128)(2,1)S(1)}, u32[]{:S(2)}, u32[]{:S(2)}) collective-permute-start(bf16[144,256]{1,0:T(8,128)(2,1)S(1)} %shard_map.130.refs_1_), channel_id=1, source_target_pairs={{0,16},{4,20},{8,24},{12,28},{16,0},{20,4},{24,8},{28,12},{1,17},{... | collective-permute-start | bytes 221192 | tf_op jit(solution)/shard_map/ppermute | solution.py:70
  40.4 6.1 %collective-permute-start.13 = (bf16[128,256]{1,0:T(8,128)(2,1)S(1)}, bf16[128,256]{1,0:T(8,128)(2,1)S(1)}, u32[]{:S(2)}, u32[]{:S(2)}) collective-permute-start(bf16[128,256]{1,0:T(8,128)(2,1)S(1)} %shard_map.126), channel_id=1, source_target_pairs={{0,3},{1,2},{2,1},{3,0},{4,7},{5,6},{6,5},{7,4},{8,11},{9,10},{10,... | collective-permute-start | bytes 196616 | tf_op jit(solution)/shard_map/ppermute | solution.py:513
  43.6 3.1 %collective-permute-start.18 = (f32[128,256]{1,0:T(8,128)S(1)}, f32[128,256]{1,0:T(8,128)S(1)}, u32[]{:S(2)}, u32[]{:S(2)}) collective-permute-start(f32[128,256]{1,0:T(8,128)S(1)} %get-tuple-element.33.own_ref), channel_id=1, source_target_pairs={{0,4},{4,0},{8,12},{12,8},{16,20},{20,16},{24,28},{28,24},{1,5},{5... | collective-permute-start | bytes 393224 | tf_op jit(solution)/shard_map/ppermute | solution.py:60

commit v14 on v12

--- a/solution.py
+++ b/solution.py
@@ -65,11 +65,11 @@
     count = size // cores
     if count & (count - 1):
         return exchange([block] * count, axis, size, cores)
-    terms, step = [block], count // 2
-    while step:
+    terms, step = [block], 1
+    while step < count:
         block = add(terms) if len(terms) > 1 else block
         terms = [lax.ppermute(block, axis, pairs_of(step, size, cores)), block]
-        step //= 2
+        step *= 2
     return terms
 
 

time: 47 us -> 45.4 us (0.966)
  waiting for transfers between devices: 18.4 us -> 15.7 us
  starting transfers between devices: 21.6 us -> 22.7 us
    ppermute x4, starting transfers between devices: 3.89 us -> 5.62 us  [total_over(): terms = [lax.ppermute(block, axis, pairs_of(step, size, cores)), block]]
    ppermute x4, waiting for transfers between devices: 4.65 us -> 3.47 us  [total_over(): terms = [lax.ppermute(block, axis, pairs_of(step, size, cores)), block]]
    ppermute x4, waiting for transfers between devices: 3.6 us -> 2.79 us  [swap_cores(): return lax.ppermute(block, 'col', [(i, i ^ 1) for i in range(size)])]
    ppermute x12, waiting for transfers between devices: 10.1 us -> 9.48 us  [exchange(): lax.ppermute(blocks[k], axis, pairs)]
    ppermute x12, starting transfers between devices: 17.4 us -> 16.8 us  [exchange(): lax.ppermute(blocks[k], axis, pairs)]
  transfers between devices with their start and end apart: 20 -> 20, of which waited for: 15 -> 14; matrix products, arithmetic and copies ran while one was open for 0% -> 0% of each run, Pallas kernels for 8% -> 8%
where the time goes in v14:
time: 45.4 us; the launch traced here: 45.3 us
  starting transfers between devices  22.7 us (50%)
  waiting for transfers between devices  15.7 us (35%)
  Pallas kernels  5.38 us (12%)
  between operations  1.47 us (3%)
    ppermute x12, starting transfers between devices, exchange(): lax.ppermute(blocks[k], axis, pairs)  16.8 us
    ppermute x12, waiting for transfers between devices, exchange(): lax.ppermute(blocks[k], axis, pairs)  9.48 us
    ppermute x4, starting transfers between devices, total_over(): terms = [lax.ppermute(block, axis, pairs_of(step, size, cores)), block]  5.62 us
    ppermute x4, waiting for transfers between devices, total_over(): terms = [lax.ppermute(block, axis, pairs_of(step, size, cores)), block]  3.47 us
    ppermute x4, waiting for transfers between devices, swap_cores(): return lax.ppermute(block, 'col', [(i, i ^ 1) for i in range(size)])  2.79 us
    pallas_call x1, Pallas kernels, local(): call(dense_kernel, (like(row_nodes, col_nodes), like(1, hidden, F32)), [S...  1.45 us
  transfers between devices with their start and end apart: 20, of which 14 were waited for; matrix products, arithmetic and copies ran while one was open for 0% of the time, Pallas kernels for 8%

profile of v14, /device:TPU:0, one launch (start us, length us, event | category | flops | bytes accessed | tf_op | source)
XLA Modules:
  0.0 45.3 jit_solution(5553716516825192782)
XLA Ops:
  0.6 5.1 %collective-permute-start = (bf16[128,256]{1,0:T(8,128)(2,1)}, bf16[128,256]{1,0:T(8,128)(2,1)S(1)}, u32[]{:S(2)}, u32[]{:S(2)}) collective-permute-start(bf16[128,256]{1,0:T(8,128)(2,1)} %refs_3_.1), channel_id=1, source_target_pairs={{0,3},{1,2},{2,1},{3,0},{4,7},{5,6},{6,5},{7,4},{8,11},{9,10},{10,... | collective-permute-start | bytes 196616 | tf_op jit(solution)/shard_map/ppermute | solution.py:56
  5.8 0.6 %collective-permute-start.2 = (bf16[128,256]{1,0:T(8,128)(2,1)}, bf16[128,256]{1,0:T(8,128)(2,1)S(1)}, u32[]{:S(2)}, u32[]{:S(2)}) collective-permute-start(bf16[128,256]{1,0:T(8,128)(2,1)} %refs_3_.1), channel_id=1, source_target_pairs={{0,1},{1,0},{2,3},{3,2},{4,5},{5,4},{6,7},{7,6},{8,9},{9,8},{10,11... | collective-permute-start | bytes 196616 | tf_op jit(solution)/shard_map/ppermute | solution.py:56
  7.1 1.5 %shard_map.111 = (bf16[1024,512]{1,0:T(8,128)(2,1)S(1)}, f32[1,256]{1,0:T(1,128)S(1)}) custom-call(s32[1,1]{1,0:T(1,128)S(6)} %copy.12.count_ref, s32[1,1,32]{2,1,0:T(1,128)} %row_hbm.1, s32[1,1,32]{2,1,0:T(1,128)} %col_hbm.1, bf16[1,1,32,128,128]{4,3,2,1,0:T(8,128)(2,1)} %tiles_hbm.1, f32[1,256]{1,0:T(1,128)} %bitcast.2), custom_call_target="tpu_custom_call" | custom-call | bytes 6291456 | tf_op jit(solution)/shard_map/pallas_call | solution.py:357
  8.6 3.0 %collective-permute-done.1.refs_1_ = bf16[128,256]{1,0:T(8,128)(2,1)S(1)} collective-permute-done((bf16[128,256]{1,0:T(8,128)(2,1)}, bf16[128,256]{1,0:T(8,128)(2,1)S(1)}, u32[]{:S(2)}, u32[]{:S(2)}) %collective-permute-start.1) | collective-permute-done | bytes 65568 | tf_op jit(solution)/shard_map/ppermute | solution.py:56
  11.6 0.3 shard_map.112
  12.3 1.2 %collective-permute-done.3.other_ref = bf16[512,256]{1,0:T(8,128)(2,1)S(1)} collective-permute-done((bf16[512,256]{1,0:T(8,128)(2,1)S(1)}, bf16[512,256]{1,0:T(8,128)(2,1)S(1)}, u32[]{:S(2)}, u32[]{:S(2)}) %collective-permute-start.3) | collective-permute-done | bytes 262176 | tf_op jit(solution)/shard_map/ppermute | solution.py:61
  13.5 2.5 %collective-permute-start.4 = (bf16[128,256]{1,0:T(8,128)(2,1)S(1)}, bf16[128,256]{1,0:T(8,128)(2,1)S(1)}, u32[]{:S(2)}, u32[]{:S(2)}) collective-permute-start(bf16[128,256]{1,0:T(8,128)(2,1)S(1)} %shard_map.114.refs_0_), channel_id=1, source_target_pairs={{0,24},{4,28},{8,16},{12,20},{16,8},{20,12},{24,0},{28,4},{1,25},{... | collective-permute-start | bytes 196616 | tf_op jit(solution)/shard_map/ppermute | solution.py:56
  16.1 0.6 %collective-permute-start.5 = (bf16[128,256]{1,0:T(8,128)(2,1)S(1)}, bf16[128,256]{1,0:T(8,128)(2,1)S(1)}, u32[]{:S(2)}, u32[]{:S(2)}) collective-permute-start(bf16[128,256]{1,0:T(8,128)(2,1)S(1)} %shard_map.115.refs_0_), channel_id=1, source_target_pairs={{0,16},{4,20},{8,24},{12,28},{16,0},{20,4},{24,8},{28,12},{1,17},{... | collective-permute-start | bytes 196616 | tf_op jit(solution)/shard_map/ppermute | solution.py:56
  16.7 0.6 %collective-permute-start.6 = (bf16[128,256]{1,0:T(8,128)(2,1)S(1)}, bf16[128,256]{1,0:T(8,128)(2,1)S(1)}, u32[]{:S(2)}, u32[]{:S(2)}) collective-permute-start(bf16[128,256]{1,0:T(8,128)(2,1)S(1)} %shard_map.116.refs_0_), channel_id=1, source_target_pairs={{0,8},{4,12},{8,0},{12,4},{16,24},{20,28},{24,16},{28,20},{1,9},{5... | collective-permute-start | bytes 196616 | tf_op jit(solution)/shard_map/ppermute | solution.py:56
  17.3 1.5 %collective-permute-done.4.refs_0_ = bf16[128,256]{1,0:T(8,128)(2,1)S(1)} collective-permute-done((bf16[128,256]{1,0:T(8,128)(2,1)S(1)}, bf16[128,256]{1,0:T(8,128)(2,1)S(1)}, u32[]{:S(2)}, u32[]{:S(2)}) %collective-permute-start.4) | collective-permute-done | bytes 65568 | tf_op jit(solution)/shard_map/ppermute | solution.py:56
  18.8 1.6 %collective-permute-done.5.refs_1_ = bf16[128,256]{1,0:T(8,128)(2,1)S(1)} collective-permute-done((bf16[128,256]{1,0:T(8,128)(2,1)S(1)}, bf16[128,256]{1,0:T(8,128)(2,1)S(1)}, u32[]{:S(2)}, u32[]{:S(2)}) %collective-permute-start.5) | collective-permute-done | bytes 65568 | tf_op jit(solution)/shard_map/ppermute | solution.py:56
  20.4 0.6 %collective-permute-done.6.refs_2_ = bf16[128,256]{1,0:T(8,128)(2,1)S(1)} collective-permute-done((bf16[128,256]{1,0:T(8,128)(2,1)S(1)}, bf16[128,256]{1,0:T(8,128)(2,1)S(1)}, u32[]{:S(2)}, u32[]{:S(2)}) %collective-permute-start.6) | collective-permute-done | bytes 65568 | tf_op jit(solution)/shard_map/ppermute | solution.py:56
  21.6 1.3 %collective-permute-done.7.refs_0_ = bf16[144,256]{1,0:T(8,128)(2,1)S(1)} collective-permute-done((bf16[144,256]{1,0:T(8,128)(2,1)S(1)}, bf16[144,256]{1,0:T(8,128)(2,1)S(1)}, u32[]{:S(2)}, u32[]{:S(2)}) %collective-permute-start.7) | collective-permute-done | bytes 73760 | tf_op jit(solution)/shard_map/ppermute | solution.py:61
  22.9 1.1 %collective-permute-start.15 = (bf16[144,256]{1,0:T(8,128)(2,1)S(1)}, bf16[144,256]{1,0:T(8,128)(2,1)S(1)}, u32[]{:S(2)}, u32[]{:S(2)}) collective-permute-start(bf16[144,256]{1,0:T(8,128)(2,1)S(1)} %shard_map.122.after_ref.refs_1_), channel_id=1, source_target_pairs={{0,1},{1,0},{2,3},{3,2},{4,5},{5,4},{6,7},{7,6},{8,9},{9,8},{10,11... | collective-permute-start | bytes 221192 | tf_op jit(solution)/shard_map/ppermute | solution.py:71
  24.0 1.5 %collective-permute-start.8 = (bf16[128,256]{1,0:T(8,128)(2,1)S(1)}, bf16[128,256]{1,0:T(8,128)(2,1)S(1)}, u32[]{:S(2)}, u32[]{:S(2)}) collective-permute-start(bf16[128,256]{1,0:T(8,128)(2,1)S(1)} %get-tuple-element.28.grad_ref.refs_3_), channel_id=1, source_target_pairs={{0,24},{4,28},{8,16},{12,20},{16,8},{20,12},{24,0},{28,4},{1,25},{... | collective-permute-start | bytes 196616 | tf_op jit(solution)/shard_map/ppermute | solution.py:56
  25.5 0.5 %collective-permute-start.9 = (bf16[128,256]{1,0:T(8,128)(2,1)S(1)}, bf16[128,256]{1,0:T(8,128)(2,1)S(1)}, u32[]{:S(2)}, u32[]{:S(2)}) collective-permute-start(bf16[128,256]{1,0:T(8,128)(2,1)S(1)} %get-tuple-element.28.grad_ref.refs_3_), channel_id=1, source_target_pairs={{0,16},{4,20},{8,24},{12,28},{16,0},{20,4},{24,8},{28,12},{1,17},{... | collective-permute-start | bytes 196616 | tf_op jit(solution)/shard_map/ppermute | solution.py:56
  26.1 1.5 %collective-permute-start.10 = (bf16[128,256]{1,0:T(8,128)(2,1)S(1)}, bf16[128,256]{1,0:T(8,128)(2,1)S(1)}, u32[]{:S(2)}, u32[]{:S(2)}) collective-permute-start(bf16[128,256]{1,0:T(8,128)(2,1)S(1)} %get-tuple-element.28.grad_ref.refs_3_), channel_id=1, source_target_pairs={{0,8},{4,12},{8,0},{12,4},{16,24},{20,28},{24,16},{28,20},{1,9},{5... | collective-permute-start | bytes 196616 | tf_op jit(solution)/shard_map/ppermute | solution.py:56
  27.6 2.3 %collective-permute-start.16 = (bf16[144,256]{1,0:T(8,128)(2,1)S(1)}, bf16[144,256]{1,0:T(8,128)(2,1)S(1)}, u32[]{:S(2)}, u32[]{:S(2)}) collective-permute-start(bf16[144,256]{1,0:T(8,128)(2,1)S(1)} %shard_map.128.refs_1_), channel_id=1, source_target_pairs={{0,2},{1,3},{2,0},{3,1},{4,6},{5,7},{6,4},{7,5},{8,10},{9,11},{10,... | collective-permute-start | bytes 221192 | tf_op jit(solution)/shard_map/ppermute | solution.py:71
  29.8 0.4 collective-permute-done.9.refs_1_
  30.4 0.3 shard_map.120.turned_ref
  30.8 2.9 %collective-permute-done.16.refs_0_ = bf16[144,256]{1,0:T(8,128)(2,1)S(1)} collective-permute-done((bf16[144,256]{1,0:T(8,128)(2,1)S(1)}, bf16[144,256]{1,0:T(8,128)(2,1)S(1)}, u32[]{:S(2)}, u32[]{:S(2)}) %collective-permute-start.16) | collective-permute-done | bytes 73760 | tf_op jit(solution)/shard_map/ppermute | solution.py:71
  33.7 0.6 %collective-permute-start.17 = (bf16[144,256]{1,0:T(8,128)(2,1)S(1)}, bf16[144,256]{1,0:T(8,128)(2,1)S(1)}, u32[]{:S(2)}, u32[]{:S(2)}) collective-permute-start(bf16[144,256]{1,0:T(8,128)(2,1)S(1)} %shard_map.129.refs_1_), channel_id=1, source_target_pairs={{0,8},{4,12},{8,0},{12,4},{16,24},{20,28},{24,16},{28,20},{1,9},{5... | collective-permute-start | bytes 221192 | tf_op jit(solution)/shard_map/ppermute | solution.py:71
  34.6 0.3 shard_map.125
  35.0 2.6 %collective-permute-start.12 = (bf16[128,256]{1,0:T(8,128)(2,1)S(1)}, bf16[128,256]{1,0:T(8,128)(2,1)S(1)}, u32[]{:S(2)}, u32[]{:S(2)}) collective-permute-start(bf16[128,256]{1,0:T(8,128)(2,1)S(1)} %get-tuple-element.31), channel_id=1, source_target_pairs={{0,3},{1,2},{2,1},{3,0},{4,7},{5,6},{6,5},{7,4},{8,11},{9,10},{10,... | collective-permute-start | bytes 196616 | tf_op jit(solution)/shard_map/ppermute | solution.py:56
  37.5 0.6 %collective-permute-done.17.refs_0_ = bf16[144,256]{1,0:T(8,128)(2,1)S(1)} collective-permute-done((bf16[144,256]{1,0:T(8,128)(2,1)S(1)}, bf16[144,256]{1,0:T(8,128)(2,1)S(1)}, u32[]{:S(2)}, u32[]{:S(2)}) %collective-permute-start.17) | collective-permute-done | bytes 73760 | tf_op jit(solution)/shard_map/ppermute | solution.py:71
  38.1 1.6 %collective-permute-start.18 = (bf16[144,256]{1,0:T(8,128)(2,1)S(1)}, bf16[144,256]{1,0:T(8,128)(2,1)S(1)}, u32[]{:S(2)}, u32[]{:S(2)}) collective-permute-start(bf16[144,256]{1,0:T(8,128)(2,1)S(1)} %shard_map.130.refs_1_), channel_id=1, source_target_pairs={{0,16},{4,20},{8,24},{12,28},{16,0},{20,4},{24,8},{28,12},{1,17},{... | collective-permute-start | bytes 221192 | tf_op jit(solution)/shard_map/ppermute | solution.py:71
  39.7 1.3 %collective-permute-start.14 = (bf16[128,256]{1,0:T(8,128)(2,1)S(1)}, bf16[128,256]{1,0:T(8,128)(2,1)S(1)}, u32[]{:S(2)}, u32[]{:S(2)}) collective-permute-start(bf16[128,256]{1,0:T(8,128)(2,1)S(1)} %get-tuple-element.34), channel_id=1, source_target_pairs={{0,1},{1,0},{2,3},{3,2},{4,5},{5,4},{6,7},{7,6},{8,9},{9,8},{10,11... | collective-permute-start | bytes 196616 | tf_op jit(solution)/shard_map/ppermute | solution.py:56
  41.0 0.6 %shard_map.119 = bf16[128,256]{1,0:T(8,128)(2,1)} custom-call(bf16[128,256]{1,0:T(8,128)(2,1)S(1)} %get-tuple-element.26.in_ref), custom_call_target="tpu_custom_call" | custom-call | bytes 131072 | tf_op jit(solution)/shard_map/pallas_call | solution.py:443
  41.6 1.4 %collective-permute-done.13.refs_1_ = bf16[128,256]{1,0:T(8,128)(2,1)S(1)} collective-permute-done((bf16[128,256]{1,0:T(8,128)(2,1)S(1)}, bf16[128,256]{1,0:T(8,128)(2,1)S(1)}, u32[]{:S(2)}, u32[]{:S(2)}) %collective-permute-start.13) | collective-permute-done | bytes 65568 | tf_op jit(solution)/shard_map/ppermute | solution.py:56
  43.2 0.8 %collective-permute-done.14.last_ref = bf16[128,256]{1,0:T(8,128)(2,1)S(1)} collective-permute-done((bf16[128,256]{1,0:T(8,128)(2,1)S(1)}, bf16[128,256]{1,0:T(8,128)(2,1)S(1)}, u32[]{:S(2)}, u32[]{:S(2)}) %collective-permute-start.14) | collective-permute-done | bytes 65568 | tf_op jit(solution)/shard_map/ppermute | solution.py:56
  44.2 0.3 collective-permute-done.19.other_ref
  44.5 0.8 %shard_map.132 = (bf16[128,256]{1,0:T(8,128)(2,1)}, f32[256,256]{1,0:T(8,128)}, f32[1,256]{1,0:T(1,128)}) custom-call(bf16[128,256]{1,0:T(8,128)(2,1)S(1)} %shard_map.127.features_ref, f32[128,256]{1,0:T(8,128)S(1)} %get-tuple-element.35.own_ref, f32[128,256]{1,0:T(8,128)S(1)} %collective-permute-done.19.other_ref, f32[1,256]{1,0:T(1,128)S(1)} %get-tuple-element.36.bias_ref), custom_call_target="tpu_custom_call" | custom-call | bytes 524288 | tf_op jit(solution)/shard_map/pallas_call | solution.py:518
  (36 shorter events, 2.1 us)
Async XLA Ops:
  0.6 7.9 %collective-permute-start = (bf16[128,256]{1,0:T(8,128)(2,1)}, bf16[128,256]{1,0:T(8,128)(2,1)S(1)}, u32[]{:S(2)}, u32[]{:S(2)}) collective-permute-start(bf16[128,256]{1,0:T(8,128)(2,1)} %refs_3_.1), channel_id=1, source_target_pairs={{0,3},{1,2},{2,1},{3,0},{4,7},{5,6},{6,5},{7,4},{8,11},{9,10},{10,... | collective-permute-start | bytes 196616 | tf_op jit(solution)/shard_map/ppermute | solution.py:56
  5.7 5.8 %collective-permute-start.1 = (bf16[128,256]{1,0:T(8,128)(2,1)}, bf16[128,256]{1,0:T(8,128)(2,1)S(1)}, u32[]{:S(2)}, u32[]{:S(2)}) collective-permute-start(bf16[128,256]{1,0:T(8,128)(2,1)} %refs_3_.1), channel_id=1, source_target_pairs={{0,2},{1,3},{2,0},{3,1},{4,6},{5,7},{6,4},{7,5},{8,10},{9,11},{10,... | collective-permute-start | bytes 196616 | tf_op jit(solution)/shard_map/ppermute | solution.py:56
  5.8 5.8 %collective-permute-start.2 = (bf16[128,256]{1,0:T(8,128)(2,1)}, bf16[128,256]{1,0:T(8,128)(2,1)S(1)}, u32[]{:S(2)}, u32[]{:S(2)}) collective-permute-start(bf16[128,256]{1,0:T(8,128)(2,1)} %refs_3_.1), channel_id=1, source_target_pairs={{0,1},{1,0},{2,3},{3,2},{4,5},{5,4},{6,7},{7,6},{8,9},{9,8},{10,11... | collective-permute-start | bytes 196616 | tf_op jit(solution)/shard_map/ppermute | solution.py:56
  7.0 4.5 %copy-start.1 = (bf16[128,256]{1,0:T(8,128)(2,1)S(1)}, bf16[128,256]{1,0:T(8,128)(2,1)}, u32[]{:S(2)}) copy-start(bf16[128,256]{1,0:T(8,128)(2,1)} %refs_3_.1) | copy-start | bytes 196612
  11.9 1.6 %collective-permute-start.3 = (bf16[512,256]{1,0:T(8,128)(2,1)S(1)}, bf16[512,256]{1,0:T(8,128)(2,1)S(1)}, u32[]{:S(2)}, u32[]{:S(2)}) collective-permute-start(bf16[512,256]{1,0:T(8,128)(2,1)S(1)} %get-tuple-element.25), channel_id=1, source_target_pairs={{0,4},{4,0},{8,12},{12,8},{16,20},{20,16},{24,28},{28,24},{1,5},{5... | collective-permute-start | bytes 786440 | tf_op jit(solution)/shard_map/ppermute | solution.py:61
  13.5 5.2 %collective-permute-start.4 = (bf16[128,256]{1,0:T(8,128)(2,1)S(1)}, bf16[128,256]{1,0:T(8,128)(2,1)S(1)}, u32[]{:S(2)}, u32[]{:S(2)}) collective-permute-start(bf16[128,256]{1,0:T(8,128)(2,1)S(1)} %shard_map.114.refs_0_), channel_id=1, source_target_pairs={{0,24},{4,28},{8,16},{12,20},{16,8},{20,12},{24,0},{28,4},{1,25},{... | collective-permute-start | bytes 196616 | tf_op jit(solution)/shard_map/ppermute | solution.py:56
  16.1 4.3 %collective-permute-start.5 = (bf16[128,256]{1,0:T(8,128)(2,1)S(1)}, bf16[128,256]{1,0:T(8,128)(2,1)S(1)}, u32[]{:S(2)}, u32[]{:S(2)}) collective-permute-start(bf16[128,256]{1,0:T(8,128)(2,1)S(1)} %shard_map.115.refs_0_), channel_id=1, source_target_pairs={{0,16},{4,20},{8,24},{12,28},{16,0},{20,4},{24,8},{28,12},{1,17},{... | collective-permute-start | bytes 196616 | tf_op jit(solution)/shard_map/ppermute | solution.py:56
  16.6 4.4 %copy-start = (bf16[256,256]{1,0:T(8,128)(2,1)S(1)}, bf16[256,256]{1,0:T(8,128)(2,1)}, u32[]{:S(2)}) copy-start(bf16[256,256]{1,0:T(8,128)(2,1)} %weight_ref.3) | copy-start | bytes 393220
  16.7 4.3 %copy-start.2 = (bf16[128,256]{1,0:T(8,128)(2,1)S(1)}, bf16[128,256]{1,0:T(8,128)(2,1)}, u32[]{:S(2)}) copy-start(bf16[128,256]{1,0:T(8,128)(2,1)} %cot_ref.1) | copy-start | bytes 196612
  16.7 4.3 %collective-permute-start.6 = (bf16[128,256]{1,0:T(8,128)(2,1)S(1)}, bf16[128,256]{1,0:T(8,128)(2,1)S(1)}, u32[]{:S(2)}, u32[]{:S(2)}) collective-permute-start(bf16[128,256]{1,0:T(8,128)(2,1)S(1)} %shard_map.116.refs_0_), channel_id=1, source_target_pairs={{0,8},{4,12},{8,0},{12,4},{16,24},{20,28},{24,16},{28,20},{1,9},{5... | collective-permute-start | bytes 196616 | tf_op jit(solution)/shard_map/ppermute | solution.py:56
  21.5 1.3 %collective-permute-start.7 = (bf16[144,256]{1,0:T(8,128)(2,1)S(1)}, bf16[144,256]{1,0:T(8,128)(2,1)S(1)}, u32[]{:S(2)}, u32[]{:S(2)}) collective-permute-start(bf16[144,256]{1,0:T(8,128)(2,1)S(1)} %get-tuple-element.29), channel_id=1, source_target_pairs={{0,4},{4,0},{8,12},{12,8},{16,20},{20,16},{24,28},{28,24},{1,5},{5... | collective-permute-start | bytes 221192 | tf_op jit(solution)/shard_map/ppermute | solution.py:61
  22.9 4.6 %collective-permute-start.15 = (bf16[144,256]{1,0:T(8,128)(2,1)S(1)}, bf16[144,256]{1,0:T(8,128)(2,1)S(1)}, u32[]{:S(2)}, u32[]{:S(2)}) collective-permute-start(bf16[144,256]{1,0:T(8,128)(2,1)S(1)} %shard_map.122.after_ref.refs_1_), channel_id=1, source_target_pairs={{0,1},{1,0},{2,3},{3,2},{4,5},{5,4},{6,7},{7,6},{8,9},{9,8},{10,11... | collective-permute-start | bytes 221192 | tf_op jit(solution)/shard_map/ppermute | solution.py:71
  24.0 5.8 %collective-permute-start.8 = (bf16[128,256]{1,0:T(8,128)(2,1)S(1)}, bf16[128,256]{1,0:T(8,128)(2,1)S(1)}, u32[]{:S(2)}, u32[]{:S(2)}) collective-permute-start(bf16[128,256]{1,0:T(8,128)(2,1)S(1)} %get-tuple-element.28.grad_ref.refs_3_), channel_id=1, source_target_pairs={{0,24},{4,28},{8,16},{12,20},{16,8},{20,12},{24,0},{28,4},{1,25},{... | collective-permute-start | bytes 196616 | tf_op jit(solution)/shard_map/ppermute | solution.py:56
  25.5 4.7 %collective-permute-start.9 = (bf16[128,256]{1,0:T(8,128)(2,1)S(1)}, bf16[128,256]{1,0:T(8,128)(2,1)S(1)}, u32[]{:S(2)}, u32[]{:S(2)}) collective-permute-start(bf16[128,256]{1,0:T(8,128)(2,1)S(1)} %get-tuple-element.28.grad_ref.refs_3_), channel_id=1, source_target_pairs={{0,16},{4,20},{8,24},{12,28},{16,0},{20,4},{24,8},{28,12},{1,17},{... | collective-permute-start | bytes 196616 | tf_op jit(solution)/shard_map/ppermute | solution.py:56
  26.1 4.3 %collective-permute-start.10 = (bf16[128,256]{1,0:T(8,128)(2,1)S(1)}, bf16[128,256]{1,0:T(8,128)(2,1)S(1)}, u32[]{:S(2)}, u32[]{:S(2)}) collective-permute-start(bf16[128,256]{1,0:T(8,128)(2,1)S(1)} %get-tuple-element.28.grad_ref.refs_3_), channel_id=1, source_target_pairs={{0,8},{4,12},{8,0},{12,4},{16,24},{20,28},{24,16},{28,20},{1,9},{5... | collective-permute-start | bytes 196616 | tf_op jit(solution)/shard_map/ppermute | solution.py:56
  27.6 6.1 %collective-permute-start.16 = (bf16[144,256]{1,0:T(8,128)(2,1)S(1)}, bf16[144,256]{1,0:T(8,128)(2,1)S(1)}, u32[]{:S(2)}, u32[]{:S(2)}) collective-permute-start(bf16[144,256]{1,0:T(8,128)(2,1)S(1)} %shard_map.128.refs_1_), channel_id=1, source_target_pairs={{0,2},{1,3},{2,0},{3,1},{4,6},{5,7},{6,4},{7,5},{8,10},{9,11},{10,... | collective-permute-start | bytes 221192 | tf_op jit(solution)/shard_map/ppermute | solution.py:71
  30.4 4.3 %collective-permute-start.11 = (bf16[512,256]{1,0:T(8,128)(2,1)S(1)}, bf16[512,256]{1,0:T(8,128)(2,1)S(1)}, u32[]{:S(2)}, u32[]{:S(2)}) collective-permute-start(bf16[512,256]{1,0:T(8,128)(2,1)S(1)} %shard_map.123.source_ref), channel_id=1, source_target_pairs={{0,4},{4,0},{8,12},{12,8},{16,20},{20,16},{24,28},{28,24},{1,5},{5... | collective-permute-start | bytes 786440 | tf_op jit(solution)/shard_map/ppermute | solution.py:61
  33.7 4.4 %collective-permute-start.17 = (bf16[144,256]{1,0:T(8,128)(2,1)S(1)}, bf16[144,256]{1,0:T(8,128)(2,1)S(1)}, u32[]{:S(2)}, u32[]{:S(2)}) collective-permute-start(bf16[144,256]{1,0:T(8,128)(2,1)S(1)} %shard_map.129.refs_1_), channel_id=1, source_target_pairs={{0,8},{4,12},{8,0},{12,4},{16,24},{20,28},{24,16},{28,20},{1,9},{5... | collective-permute-start | bytes 221192 | tf_op jit(solution)/shard_map/ppermute | solution.py:71
  35.0 6.7 %collective-permute-start.12 = (bf16[128,256]{1,0:T(8,128)(2,1)S(1)}, bf16[128,256]{1,0:T(8,128)(2,1)S(1)}, u32[]{:S(2)}, u32[]{:S(2)}) collective-permute-start(bf16[128,256]{1,0:T(8,128)(2,1)S(1)} %get-tuple-element.31), channel_id=1, source_target_pairs={{0,3},{1,2},{2,1},{3,0},{4,7},{5,6},{6,5},{7,4},{8,11},{9,10},{10,... | collective-permute-start | bytes 196616 | tf_op jit(solution)/shard_map/ppermute | solution.py:56
  37.5 5.5 %collective-permute-start.13 = (bf16[128,256]{1,0:T(8,128)(2,1)S(1)}, bf16[128,256]{1,0:T(8,128)(2,1)S(1)}, u32[]{:S(2)}, u32[]{:S(2)}) collective-permute-start(bf16[128,256]{1,0:T(8,128)(2,1)S(1)} %get-tuple-element.32), channel_id=1, source_target_pairs={{0,2},{1,3},{2,0},{3,1},{4,6},{5,7},{6,4},{7,5},{8,10},{9,11},{10,... | collective-permute-start | bytes 196616 | tf_op jit(solution)/shard_map/ppermute | solution.py:56
  38.1 4.9 %collective-permute-start.18 = (bf16[144,256]{1,0:T(8,128)(2,1)S(1)}, bf16[144,256]{1,0:T(8,128)(2,1)S(1)}, u32[]{:S(2)}, u32[]{:S(2)}) collective-permute-start(bf16[144,256]{1,0:T(8,128)(2,1)S(1)} %shard_map.130.refs_1_), channel_id=1, source_target_pairs={{0,16},{4,20},{8,24},{12,28},{16,0},{20,4},{24,8},{28,12},{1,17},{... | collective-permute-start | bytes 221192 | tf_op jit(solution)/shard_map/ppermute | solution.py:71
  39.7 4.3 %collective-permute-start.14 = (bf16[128,256]{1,0:T(8,128)(2,1)S(1)}, bf16[128,256]{1,0:T(8,128)(2,1)S(1)}, u32[]{:S(2)}, u32[]{:S(2)}) collective-permute-start(bf16[128,256]{1,0:T(8,128)(2,1)S(1)} %get-tuple-element.34), channel_id=1, source_target_pairs={{0,1},{1,0},{2,3},{3,2},{4,5},{5,4},{6,7},{7,6},{8,9},{9,8},{10,11... | collective-permute-start | bytes 196616 | tf_op jit(solution)/shard_map/ppermute | solution.py:56
  43.1 1.4 %collective-permute-start.19 = (f32[128,256]{1,0:T(8,128)S(1)}, f32[128,256]{1,0:T(8,128)S(1)}, u32[]{:S(2)}, u32[]{:S(2)}) collective-permute-start(f32[128,256]{1,0:T(8,128)S(1)} %get-tuple-element.35.own_ref), channel_id=1, source_target_pairs={{0,4},{4,0},{8,12},{12,8},{16,20},{20,16},{24,28},{28,24},{1,5},{5... | collective-permute-start | bytes 393224 | tf_op jit(solution)/shard_map/ppermute | solution.py:61

commit v15 on v14

--- a/solution.py
+++ b/solution.py
@@ -40,20 +40,41 @@
     return (k - index) % count
 
 
-def far_first(count):
-    return list(range(count - 1, -1, -1))
-
-
-def pairs_of(k, size, cores):
-    return [(i, partner(i // cores, k, size // cores) * cores + i % cores) for i in range(size)]
-
-
-def exchange(blocks, axis, size, cores=1):
+def turns(count, core):
+    if core == 0:
+        return list(range(count - 1, -1, -1))
+    return list(dict.fromkeys([count - 1, *range(1, count), 0]))
+
+
+def steps(count, core):
+    powers = [1 << i for i in range(count.bit_length() - 1)]
+    return powers if core else powers[::-1]
+
+
+def turn(i, count):
+    return jnp.where(core_index() == 0, turns(count, 0)[i], turns(count, 1)[i])
+
+
+def permute(block, axis, sizes, distances):
+    n_col, n_row = sizes
+    pairs = []
+    for col in range(n_col):
+        chip, core = col // 2, col % 2
+        for row in range(n_row):
+            if axis == "row":
+                target = col, partner(row, distances[core], n_row)
+            else:
+                target = 2 * partner(chip, distances[core], n_col // 2) + core, row
+            pairs.append((col * n_row + row, target[0] * n_row + target[1]))
+    return lax.ppermute(block, ("col", "row"), pairs)
+
+
+def exchange(blocks, axis, sizes):
+    count = len(blocks)
     received = []
-    for k in far_first(size // cores):
-        pairs = pairs_of(k, size, cores)
-        moves = any(i != j for i, j in pairs)
-        received.append(lax.ppermute(blocks[k], axis, pairs) if moves else blocks[k])
+    for i, block in enumerate(blocks):
+        distances = [turns(count, core)[i] for core in range(2)]
+        received.append(permute(block, axis, sizes, distances) if any(distances) else block)
     return received
 
 
@@ -61,15 +82,14 @@
     return lax.ppermute(block, "col", [(i, i ^ 1) for i in range(size)])
 
 
-def total_over(block, add, axis, size, cores=1):
-    count = size // cores
+def total_over(block, add, axis, sizes):
+    count = sizes[1] if axis == "row" else sizes[0] // 2
     if count & (count - 1):
-        return exchange([block] * count, axis, size, cores)
-    terms, step = [block], 1
-    while step < count:
+        return exchange([block] * count, axis, sizes)
+    terms = [block]
+    for distances in zip(steps(count, 0), steps(count, 1)):
         block = add(terms) if len(terms) > 1 else block
-        terms = [lax.ppermute(block, axis, pairs_of(step, size, cores)), block]
-        step *= 2
+        terms = [permute(block, axis, sizes, distances), block]
     return terms
 
 
@@ -90,11 +110,10 @@
 
 
 def summed(refs):
-    by_partner = dict(zip(far_first(len(refs)), refs))
-    values = [by_partner[k][...].astype(F32) for k in sorted(by_partner)]
-    while len(values) > 1:
-        values = [sum(values[i + 1 : i + 2], values[i]) for i in range(0, len(values), 2)]
-    return values[0]
+    total = refs[0][...].astype(F32)
+    for ref in refs[1:]:
+        total += ref[...].astype(F32)
+    return total
 
 
 def bias_rows(bias):
@@ -158,8 +177,9 @@
 
 def gather_sources(sources, source_ref, index):
     tile = sources[0].shape[0]
-    for k, ref in zip(far_first(len(sources)), sources):
-        source_ref[block_at(partner(index, k, len(sources)), tile), :] = ref[...]
+    for i, ref in enumerate(sources):
+        place = partner(index, turn(i, len(sources)), len(sources))
+        source_ref[block_at(place, tile), :] = ref[...]
 
 
 def slot_product(refs, source_ref, acc_ref, turned):
@@ -203,9 +223,9 @@
     other_ref[...] = acc_ref[half:, :].astype(BF16)
 
 
-def chip_kernel(own_ref, other_ref, *refs, k, n_chip):
+def chip_kernel(own_ref, other_ref, *refs, i, n_chip):
     out_ref = refs[-1]
-    rows = block_at(partner(chip_index(), k, n_chip), out_ref.shape[0])
+    rows = block_at(partner(chip_index(), turn(i, n_chip), n_chip), out_ref.shape[0])
     out_ref[...] = (own_ref[rows, :].astype(F32) + other_ref[rows, :].astype(F32)).astype(BF16)
 
 
@@ -264,8 +284,8 @@
 
 def back_pieces_kernel(turned_ref, own_ref, source_ref, *outs):
     tile = outs[0].shape[0]
-    for k, out_ref in zip(far_first(len(outs)), outs):
-        rows = block_at(partner(row_index(), k, len(outs)), tile)
+    for i, out_ref in enumerate(outs):
+        rows = block_at(partner(row_index(), turn(i, len(outs)), len(outs)), tile)
         rest = dense_dot(turned_ref[rows, source_ref.shape[0] :], source_ref[...])
         out_ref[...] = (own_ref[rows, :] + rest).astype(BF16)
 
@@ -277,8 +297,8 @@
     source_ref[half:, :] = other_ref[...]
     slot_product((count_ref, row_ref, col_ref, tiles_ref), source_ref, acc_ref, True)
     tile = outs[0].shape[0]
-    for k, out_ref in zip(far_first(len(outs)), outs):
-        rows = block_at(partner(row_index(), k, len(outs)), tile)
+    for i, out_ref in enumerate(outs):
+        rows = block_at(partner(row_index(), turn(i, len(outs)), len(outs)), tile)
         out_ref[...] = acc_ref[rows, :].astype(BF16)
 
 
@@ -314,18 +334,11 @@
         copy.wait()
 
 
-def in_turn(count, make):
-    made, before = {}, []
-    for k in far_first(count):
-        made[k] = make(k, before)
-        before = [made[k]]
-    return made
-
-
 def local(features, weight, bias_term, cotangent, tile_values, tile_row, tile_col, tile_count):
     n_row = lax.axis_size("row")
     n_col = lax.axis_size("col")
     n_chip = n_col // 2
+    sizes = n_col, n_row
     tile, width = features.shape
     hidden = weight.shape[1]
     slots = tile_values.shape[2]
@@ -381,7 +394,7 @@
         )
         slot_specs = [SMEM_SPEC] * 3 + [VMEM_SPEC]
 
-    sources = exchange([features] * n_row, "row", n_row)
+    sources = exchange([features] * n_row, "row", sizes)
     if is_dense:
         other, source = call(
             forward_other_kernel,
@@ -410,9 +423,9 @@
         )(*slot_args, *sources)
     swapped = swap_cores(other, n_col)
 
-    def chip_piece(k, before):
+    def chip_piece(i, before):
         return call(
-            functools.partial(chip_kernel, k=k, n_chip=n_chip),
+            functools.partial(chip_kernel, i=i, n_chip=n_chip),
             like(tile, width),
             [VMEM_SPEC] * (2 + len(before)),
             [],
@@ -420,8 +433,10 @@
             3 * block_bytes,
         )(own, swapped, *before)
 
-    pieces = in_turn(n_chip, chip_piece)
-    parts = exchange(pieces, "col", n_col, 2)
+    pieces = []
+    for i in range(n_chip):
+        pieces.append(chip_piece(i, pieces[-1:]))
+    parts = exchange(pieces, "chip", sizes)
     if is_dense:
         turned = call(
             turn_kernel,
@@ -430,7 +445,7 @@
             [],
             0,
             4 * row_nodes * col_nodes,
-        )(dense, pieces[0])
+        )(dense, pieces[-1])
     hidden_own, grad, aggregated = call(
         middle_kernel,
         [like(tile, hidden), like(tile, hidden), like(tile, width)],
@@ -439,7 +454,7 @@
         matrix,
         n_chip * block_bytes,
     )(weight, bias_row, cotangent, *parts)
-    grads = exchange([grad] * n_chip, "col", n_col, 2)
+    grads = exchange([grad] * n_chip, "chip", sizes)
     hidden_out = call(copy_kernel, like(tile, hidden), [VMEM_SPEC], [], 0, 2 * block_bytes)(hidden_own)
     mine, theirs = call(
         term_kernel,
@@ -451,7 +466,7 @@
     )(aggregated, grad)
     chip_term = add([swap_cores(theirs, n_col), mine])
     add_late = functools.partial(add, flops=ROW_SUM_WEIGHT * matrix)
-    row_term = add_late(total_over(chip_term, add, "row", n_row))
+    row_term = add_late(total_over(chip_term, add, "row", sizes))
 
     own_grads = call(
         gather_kernel,
@@ -488,7 +503,7 @@
             slots * matrix // 2,
             row_nodes * hidden * 8,
         )(*slot_args, own_grads, other_grads)
-    backs = exchange(dict(zip(far_first(n_row), back_pieces)), "row", n_row)
+    backs = exchange(back_pieces, "row", sizes)
     most = call(
         back_sum_kernel,
         like(tile, hidden, F32),
@@ -505,7 +520,7 @@
         FEATURES_WEIGHT * matrix,
         n_row * block_bytes,
     )(weight, most, backs[-2])
-    all_terms = total_over(row_term, add, "col", n_col, 2)
+    all_terms = total_over(row_term, add, "chip", sizes)
     factor = (tile * n_row * n_col) ** (-0.5)
     own_half, bias_grad = call(
         functools.partial(scale_kernel, factor=factor),

time: 45.4 us -> 46.5 us (1.024)
  waiting for transfers between devices: 15.7 us -> 17.7 us
  starting transfers between devices: 22.7 us -> 21.9 us
    ppermute x16, waiting for transfers between devices: 12.9 us -> 14.1 us  [permute(): return lax.ppermute(block, ('col', 'row'), pairs)]
    ppermute x4, waiting for transfers between devices: 2.79 us -> 3.59 us  [swap_cores(): return lax.ppermute(block, 'col', [(i, i ^ 1) for i in range(size)])]
    ppermute x16, starting transfers between devices: 22.4 us -> 21.6 us  [permute(): return lax.ppermute(block, ('col', 'row'), pairs)]
where the time goes in v15:
time: 46.5 us; the launch traced here: 46.4 us
  starting transfers between devices  21.9 us (47%)
  waiting for transfers between devices  17.7 us (38%)
  Pallas kernels  5.32 us (11%)
  between operations  1.48 us (3%)
    ppermute x16, starting transfers between devices, permute(): return lax.ppermute(block, ('col', 'row'), pairs)  21.6 us
    ppermute x16, waiting for transfers between devices, permute(): return lax.ppermute(block, ('col', 'row'), pairs)  14.1 us
    ppermute x4, waiting for transfers between devices, swap_cores(): return lax.ppermute(block, 'col', [(i, i ^ 1) for i in range(size)])  3.59 us
    pallas_call x1, Pallas kernels, local(): call(dense_kernel, (like(row_nodes, col_nodes), like(1, hidden, F32)), [S...  1.4 us
  transfers between devices with their start and end apart: 20, of which 14 were waited for; matrix products, arithmetic and copies ran while one was open for 0% of the time, Pallas kernels for 8%

profile of v15, /device:TPU:0, one launch (start us, length us, event | category | flops | bytes accessed | tf_op | source)
XLA Modules:
  0.0 46.4 jit_solution(16738216553552816980)
XLA Ops:
  0.6 5.1 %collective-permute-start = (bf16[128,256]{1,0:T(8,128)(2,1)}, bf16[128,256]{1,0:T(8,128)(2,1)S(1)}, u32[]{:S(2)}, u32[]{:S(2)}) collective-permute-start(bf16[128,256]{1,0:T(8,128)(2,1)} %refs_3_.1), channel_id=1, source_target_pairs={{0,3},{1,2},{2,1},{3,0},{4,7},{5,6},{6,5},{7,4},{8,11},{9,10},{10,... | collective-permute-start | bytes 196616 | tf_op jit(solution)/shard_map/ppermute | solution.py:69
  5.8 0.6 %collective-permute-start.2 = (bf16[128,256]{1,0:T(8,128)(2,1)}, bf16[128,256]{1,0:T(8,128)(2,1)S(1)}, u32[]{:S(2)}, u32[]{:S(2)}) collective-permute-start(bf16[128,256]{1,0:T(8,128)(2,1)} %refs_3_.1), channel_id=1, source_target_pairs={{0,1},{1,0},{2,3},{3,2},{4,6},{5,7},{6,4},{7,5},{8,9},{9,8},{10,11... | collective-permute-start | bytes 196616 | tf_op jit(solution)/shard_map/ppermute | solution.py:69
  7.1 1.4 %shard_map.111 = (bf16[1024,512]{1,0:T(8,128)(2,1)S(1)}, f32[1,256]{1,0:T(1,128)S(1)}) custom-call(s32[1,1]{1,0:T(1,128)S(6)} %copy.12.count_ref, s32[1,1,32]{2,1,0:T(1,128)} %row_hbm.1, s32[1,1,32]{2,1,0:T(1,128)} %col_hbm.1, bf16[1,1,32,128,128]{4,3,2,1,0:T(8,128)(2,1)} %tiles_hbm.1, f32[1,256]{1,0:T(1,128)} %bitcast.2), custom_call_target="tpu_custom_call" | custom-call | bytes 6291456 | tf_op jit(solution)/shard_map/pallas_call | solution.py:370
  8.5 0.4 collective-permute-done.refs_0_
  8.9 3.0 %collective-permute-done.1.refs_1_ = bf16[128,256]{1,0:T(8,128)(2,1)S(1)} collective-permute-done((bf16[128,256]{1,0:T(8,128)(2,1)}, bf16[128,256]{1,0:T(8,128)(2,1)S(1)}, u32[]{:S(2)}, u32[]{:S(2)}) %collective-permute-start.1) | collective-permute-done | bytes 65568 | tf_op jit(solution)/shard_map/ppermute | solution.py:69
  11.8 0.3 shard_map.112
  12.5 1.2 %collective-permute-done.3.other_ref = bf16[512,256]{1,0:T(8,128)(2,1)S(1)} collective-permute-done((bf16[512,256]{1,0:T(8,128)(2,1)S(1)}, bf16[512,256]{1,0:T(8,128)(2,1)S(1)}, u32[]{:S(2)}, u32[]{:S(2)}) %collective-permute-start.3) | collective-permute-done | bytes 262176 | tf_op jit(solution)/shard_map/ppermute | solution.py:82
  13.8 2.5 %collective-permute-start.4 = (bf16[128,256]{1,0:T(8,128)(2,1)S(1)}, bf16[128,256]{1,0:T(8,128)(2,1)S(1)}, u32[]{:S(2)}, u32[]{:S(2)}) collective-permute-start(bf16[128,256]{1,0:T(8,128)(2,1)S(1)} %shard_map.114.refs_0_), channel_id=1, source_target_pairs={{0,24},{1,25},{2,26},{3,27},{4,28},{5,29},{6,30},{7,31},{8,16},{9,... | collective-permute-start | bytes 196616 | tf_op jit(solution)/shard_map/ppermute | solution.py:69
  16.3 0.6 %collective-permute-start.5 = (bf16[128,256]{1,0:T(8,128)(2,1)S(1)}, bf16[128,256]{1,0:T(8,128)(2,1)S(1)}, u32[]{:S(2)}, u32[]{:S(2)}) collective-permute-start(bf16[128,256]{1,0:T(8,128)(2,1)S(1)} %shard_map.115.refs_0_), channel_id=1, source_target_pairs={{0,16},{1,17},{2,18},{3,19},{4,12},{5,13},{6,14},{7,15},{8,24},{9,... | collective-permute-start | bytes 196616 | tf_op jit(solution)/shard_map/ppermute | solution.py:69
  16.9 0.6 %collective-permute-start.6 = (bf16[128,256]{1,0:T(8,128)(2,1)S(1)}, bf16[128,256]{1,0:T(8,128)(2,1)S(1)}, u32[]{:S(2)}, u32[]{:S(2)}) collective-permute-start(bf16[128,256]{1,0:T(8,128)(2,1)S(1)} %shard_map.116.refs_0_), channel_id=1, source_target_pairs={{0,8},{1,9},{2,10},{3,11},{4,20},{5,21},{6,22},{7,23},{8,0},{9,1},... | collective-permute-start | bytes 196616 | tf_op jit(solution)/shard_map/ppermute | solution.py:69
  17.5 1.8 %collective-permute-done.4.refs_0_ = bf16[128,256]{1,0:T(8,128)(2,1)S(1)} collective-permute-done((bf16[128,256]{1,0:T(8,128)(2,1)S(1)}, bf16[128,256]{1,0:T(8,128)(2,1)S(1)}, u32[]{:S(2)}, u32[]{:S(2)}) %collective-permute-start.4) | collective-permute-done | bytes 65568 | tf_op jit(solution)/shard_map/ppermute | solution.py:69
  19.3 1.3 %collective-permute-done.5.refs_1_ = bf16[128,256]{1,0:T(8,128)(2,1)S(1)} collective-permute-done((bf16[128,256]{1,0:T(8,128)(2,1)S(1)}, bf16[128,256]{1,0:T(8,128)(2,1)S(1)}, u32[]{:S(2)}, u32[]{:S(2)}) %collective-permute-start.5) | collective-permute-done | bytes 65568 | tf_op jit(solution)/shard_map/ppermute | solution.py:69
  20.7 0.6 %collective-permute-done.6.refs_2_ = bf16[128,256]{1,0:T(8,128)(2,1)S(1)} collective-permute-done((bf16[128,256]{1,0:T(8,128)(2,1)S(1)}, bf16[128,256]{1,0:T(8,128)(2,1)S(1)}, u32[]{:S(2)}, u32[]{:S(2)}) %collective-permute-start.6) | collective-permute-done | bytes 65568 | tf_op jit(solution)/shard_map/ppermute | solution.py:69
  21.9 1.3 %collective-permute-done.7.refs_0_ = bf16[144,256]{1,0:T(8,128)(2,1)S(1)} collective-permute-done((bf16[144,256]{1,0:T(8,128)(2,1)S(1)}, bf16[144,256]{1,0:T(8,128)(2,1)S(1)}, u32[]{:S(2)}, u32[]{:S(2)}) %collective-permute-start.7) | collective-permute-done | bytes 73760 | tf_op jit(solution)/shard_map/ppermute | solution.py:82
  23.1 1.4 %collective-permute-start.15 = (bf16[144,256]{1,0:T(8,128)(2,1)S(1)}, bf16[144,256]{1,0:T(8,128)(2,1)S(1)}, u32[]{:S(2)}, u32[]{:S(2)}) collective-permute-start(bf16[144,256]{1,0:T(8,128)(2,1)S(1)} %shard_map.122.after_ref.refs_1_), channel_id=1, source_target_pairs={{0,2},{1,3},{2,0},{3,1},{4,5},{5,4},{6,7},{7,6},{8,10},{9,11},{10,... | collective-permute-start | bytes 221192 | tf_op jit(solution)/shard_map/ppermute | solution.py:69
  24.5 1.5 %collective-permute-start.8 = (bf16[128,256]{1,0:T(8,128)(2,1)S(1)}, bf16[128,256]{1,0:T(8,128)(2,1)S(1)}, u32[]{:S(2)}, u32[]{:S(2)}) collective-permute-start(bf16[128,256]{1,0:T(8,128)(2,1)S(1)} %get-tuple-element.28.grad_ref.refs_3_), channel_id=1, source_target_pairs={{0,24},{1,25},{2,26},{3,27},{4,28},{5,29},{6,30},{7,31},{8,16},{9,... | collective-permute-start | bytes 196616 | tf_op jit(solution)/shard_map/ppermute | solution.py:69
  26.0 0.8 %collective-permute-start.9 = (bf16[128,256]{1,0:T(8,128)(2,1)S(1)}, bf16[128,256]{1,0:T(8,128)(2,1)S(1)}, u32[]{:S(2)}, u32[]{:S(2)}) collective-permute-start(bf16[128,256]{1,0:T(8,128)(2,1)S(1)} %get-tuple-element.28.grad_ref.refs_3_), channel_id=1, source_target_pairs={{0,16},{1,17},{2,18},{3,19},{4,12},{5,13},{6,14},{7,15},{8,24},{9,... | collective-permute-start | bytes 196616 | tf_op jit(solution)/shard_map/ppermute | solution.py:69
  26.9 1.2 %collective-permute-start.10 = (bf16[128,256]{1,0:T(8,128)(2,1)S(1)}, bf16[128,256]{1,0:T(8,128)(2,1)S(1)}, u32[]{:S(2)}, u32[]{:S(2)}) collective-permute-start(bf16[128,256]{1,0:T(8,128)(2,1)S(1)} %get-tuple-element.28.grad_ref.refs_3_), channel_id=1, source_target_pairs={{0,8},{1,9},{2,10},{3,11},{4,20},{5,21},{6,22},{7,23},{8,0},{9,1},... | collective-permute-start | bytes 196616 | tf_op jit(solution)/shard_map/ppermute | solution.py:69
  28.0 1.2 %collective-permute-done.15.refs_0_ = bf16[144,256]{1,0:T(8,128)(2,1)S(1)} collective-permute-done((bf16[144,256]{1,0:T(8,128)(2,1)S(1)}, bf16[144,256]{1,0:T(8,128)(2,1)S(1)}, u32[]{:S(2)}, u32[]{:S(2)}) %collective-permute-start.15) | collective-permute-done | bytes 73760 | tf_op jit(solution)/shard_map/ppermute | solution.py:69
  29.3 0.7 %collective-permute-start.16 = (bf16[144,256]{1,0:T(8,128)(2,1)S(1)}, bf16[144,256]{1,0:T(8,128)(2,1)S(1)}, u32[]{:S(2)}, u32[]{:S(2)}) collective-permute-start(bf16[144,256]{1,0:T(8,128)(2,1)S(1)} %shard_map.128.refs_1_), channel_id=1, source_target_pairs={{0,1},{1,0},{2,3},{3,2},{4,6},{5,7},{6,4},{7,5},{8,9},{9,8},{10,11... | collective-permute-start | bytes 221192 | tf_op jit(solution)/shard_map/ppermute | solution.py:69
  30.0 1.0 %collective-permute-done.9.refs_1_ = bf16[128,256]{1,0:T(8,128)(2,1)S(1)} collective-permute-done((bf16[128,256]{1,0:T(8,128)(2,1)S(1)}, bf16[128,256]{1,0:T(8,128)(2,1)S(1)}, u32[]{:S(2)}, u32[]{:S(2)}) %collective-permute-start.9) | collective-permute-done | bytes 65568 | tf_op jit(solution)/shard_map/ppermute | solution.py:69
  31.3 0.3 shard_map.120.turned_ref
  31.6 2.1 %collective-permute-done.16.refs_0_ = bf16[144,256]{1,0:T(8,128)(2,1)S(1)} collective-permute-done((bf16[144,256]{1,0:T(8,128)(2,1)S(1)}, bf16[144,256]{1,0:T(8,128)(2,1)S(1)}, u32[]{:S(2)}, u32[]{:S(2)}) %collective-permute-start.16) | collective-permute-done | bytes 73760 | tf_op jit(solution)/shard_map/ppermute | solution.py:69
  33.7 1.6 %collective-permute-start.17 = (bf16[144,256]{1,0:T(8,128)(2,1)S(1)}, bf16[144,256]{1,0:T(8,128)(2,1)S(1)}, u32[]{:S(2)}, u32[]{:S(2)}) collective-permute-start(bf16[144,256]{1,0:T(8,128)(2,1)S(1)} %shard_map.129.refs_1_), channel_id=1, source_target_pairs={{0,16},{1,17},{2,18},{3,19},{4,12},{5,13},{6,14},{7,15},{8,24},{9,... | collective-permute-start | bytes 221192 | tf_op jit(solution)/shard_map/ppermute | solution.py:69
  35.9 2.3 %collective-permute-start.12 = (bf16[128,256]{1,0:T(8,128)(2,1)S(1)}, bf16[128,256]{1,0:T(8,128)(2,1)S(1)}, u32[]{:S(2)}, u32[]{:S(2)}) collective-permute-start(bf16[128,256]{1,0:T(8,128)(2,1)S(1)} %get-tuple-element.31), channel_id=1, source_target_pairs={{0,3},{1,2},{2,1},{3,0},{4,7},{5,6},{6,5},{7,4},{8,11},{9,10},{10,... | collective-permute-start | bytes 196616 | tf_op jit(solution)/shard_map/ppermute | solution.py:69
  38.3 0.8 %collective-permute-start.18 = (bf16[144,256]{1,0:T(8,128)(2,1)S(1)}, bf16[144,256]{1,0:T(8,128)(2,1)S(1)}, u32[]{:S(2)}, u32[]{:S(2)}) collective-permute-start(bf16[144,256]{1,0:T(8,128)(2,1)S(1)} %shard_map.130.refs_1_), channel_id=1, source_target_pairs={{0,8},{1,9},{2,10},{3,11},{4,20},{5,21},{6,22},{7,23},{8,0},{9,1},... | collective-permute-start | bytes 221192 | tf_op jit(solution)/shard_map/ppermute | solution.py:69
  39.1 1.9 %collective-permute-start.14 = (bf16[128,256]{1,0:T(8,128)(2,1)S(1)}, bf16[128,256]{1,0:T(8,128)(2,1)S(1)}, u32[]{:S(2)}, u32[]{:S(2)}) collective-permute-start(bf16[128,256]{1,0:T(8,128)(2,1)S(1)} %get-tuple-element.34), channel_id=1, source_target_pairs={{0,1},{1,0},{2,3},{3,2},{4,6},{5,7},{6,4},{7,5},{8,9},{9,8},{10,11... | collective-permute-start | bytes 196616 | tf_op jit(solution)/shard_map/ppermute | solution.py:69
  41.0 0.6 %shard_map.119 = bf16[128,256]{1,0:T(8,128)(2,1)} custom-call(bf16[128,256]{1,0:T(8,128)(2,1)S(1)} %get-tuple-element.26.in_ref), custom_call_target="tpu_custom_call" | custom-call | bytes 131072 | tf_op jit(solution)/shard_map/pallas_call | solution.py:458
  41.7 1.1 %collective-permute-done.12.refs_0_ = bf16[128,256]{1,0:T(8,128)(2,1)S(1)} collective-permute-done((bf16[128,256]{1,0:T(8,128)(2,1)S(1)}, bf16[128,256]{1,0:T(8,128)(2,1)S(1)}, u32[]{:S(2)}, u32[]{:S(2)}) %collective-permute-start.12) | collective-permute-done | bytes 65568 | tf_op jit(solution)/shard_map/ppermute | solution.py:69
  42.7 1.4 %collective-permute-done.13.refs_1_ = bf16[128,256]{1,0:T(8,128)(2,1)S(1)} collective-permute-done((bf16[128,256]{1,0:T(8,128)(2,1)S(1)}, bf16[128,256]{1,0:T(8,128)(2,1)S(1)}, u32[]{:S(2)}, u32[]{:S(2)}) %collective-permute-start.13) | collective-permute-done | bytes 65568 | tf_op jit(solution)/shard_map/ppermute | solution.py:69
  44.5 1.1 %collective-permute-done.19.other_ref = f32[128,256]{1,0:T(8,128)S(1)} collective-permute-done((f32[128,256]{1,0:T(8,128)S(1)}, f32[128,256]{1,0:T(8,128)S(1)}, u32[]{:S(2)}, u32[]{:S(2)}) %collective-permute-start.19) | collective-permute-done | bytes 131104 | tf_op jit(solution)/shard_map/ppermute | solution.py:82
  45.6 0.8 %shard_map.132 = (bf16[128,256]{1,0:T(8,128)(2,1)}, f32[256,256]{1,0:T(8,128)}, f32[1,256]{1,0:T(1,128)}) custom-call(bf16[128,256]{1,0:T(8,128)(2,1)S(1)} %shard_map.127.features_ref, f32[128,256]{1,0:T(8,128)S(1)} %get-tuple-element.35.own_ref, f32[128,256]{1,0:T(8,128)S(1)} %collective-permute-done.19.other_ref, f32[1,256]{1,0:T(1,128)S(1)} %get-tuple-element.36.bias_ref), custom_call_target="tpu_custom_call" | custom-call | bytes 524288 | tf_op jit(solution)/shard_map/pallas_call | solution.py:533
  (36 shorter events, 2.3 us)
Async XLA Ops:
  0.6 8.2 %collective-permute-start = (bf16[128,256]{1,0:T(8,128)(2,1)}, bf16[128,256]{1,0:T(8,128)(2,1)S(1)}, u32[]{:S(2)}, u32[]{:S(2)}) collective-permute-start(bf16[128,256]{1,0:T(8,128)(2,1)} %refs_3_.1), channel_id=1, source_target_pairs={{0,3},{1,2},{2,1},{3,0},{4,7},{5,6},{6,5},{7,4},{8,11},{9,10},{10,... | collective-permute-start | bytes 196616 | tf_op jit(solution)/shard_map/ppermute | solution.py:69
  5.7 6.1 %collective-permute-start.1 = (bf16[128,256]{1,0:T(8,128)(2,1)}, bf16[128,256]{1,0:T(8,128)(2,1)S(1)}, u32[]{:S(2)}, u32[]{:S(2)}) collective-permute-start(bf16[128,256]{1,0:T(8,128)(2,1)} %refs_3_.1), channel_id=1, source_target_pairs={{0,2},{1,3},{2,0},{3,1},{4,5},{5,4},{6,7},{7,6},{8,10},{9,11},{10,... | collective-permute-start | bytes 196616 | tf_op jit(solution)/shard_map/ppermute | solution.py:69
  5.8 6.1 %collective-permute-start.2 = (bf16[128,256]{1,0:T(8,128)(2,1)}, bf16[128,256]{1,0:T(8,128)(2,1)S(1)}, u32[]{:S(2)}, u32[]{:S(2)}) collective-permute-start(bf16[128,256]{1,0:T(8,128)(2,1)} %refs_3_.1), channel_id=1, source_target_pairs={{0,1},{1,0},{2,3},{3,2},{4,6},{5,7},{6,4},{7,5},{8,9},{9,8},{10,11... | collective-permute-start | bytes 196616 | tf_op jit(solution)/shard_map/ppermute | solution.py:69
  7.0 4.8 %copy-start.1 = (bf16[128,256]{1,0:T(8,128)(2,1)S(1)}, bf16[128,256]{1,0:T(8,128)(2,1)}, u32[]{:S(2)}) copy-start(bf16[128,256]{1,0:T(8,128)(2,1)} %refs_3_.1) | copy-start | bytes 196612
  12.1 1.6 %collective-permute-start.3 = (bf16[512,256]{1,0:T(8,128)(2,1)S(1)}, bf16[512,256]{1,0:T(8,128)(2,1)S(1)}, u32[]{:S(2)}, u32[]{:S(2)}) collective-permute-start(bf16[512,256]{1,0:T(8,128)(2,1)S(1)} %get-tuple-element.25), channel_id=1, source_target_pairs={{0,4},{4,0},{8,12},{12,8},{16,20},{20,16},{24,28},{28,24},{1,5},{5... | collective-permute-start | bytes 786440 | tf_op jit(solution)/shard_map/ppermute | solution.py:82
  13.8 5.5 %collective-permute-start.4 = (bf16[128,256]{1,0:T(8,128)(2,1)S(1)}, bf16[128,256]{1,0:T(8,128)(2,1)S(1)}, u32[]{:S(2)}, u32[]{:S(2)}) collective-permute-start(bf16[128,256]{1,0:T(8,128)(2,1)S(1)} %shard_map.114.refs_0_), channel_id=1, source_target_pairs={{0,24},{1,25},{2,26},{3,27},{4,28},{5,29},{6,30},{7,31},{8,16},{9,... | collective-permute-start | bytes 196616 | tf_op jit(solution)/shard_map/ppermute | solution.py:69
  16.3 4.3 %collective-permute-start.5 = (bf16[128,256]{1,0:T(8,128)(2,1)S(1)}, bf16[128,256]{1,0:T(8,128)(2,1)S(1)}, u32[]{:S(2)}, u32[]{:S(2)}) collective-permute-start(bf16[128,256]{1,0:T(8,128)(2,1)S(1)} %shard_map.115.refs_0_), channel_id=1, source_target_pairs={{0,16},{1,17},{2,18},{3,19},{4,12},{5,13},{6,14},{7,15},{8,24},{9,... | collective-permute-start | bytes 196616 | tf_op jit(solution)/shard_map/ppermute | solution.py:69
  16.9 4.4 %copy-start = (bf16[256,256]{1,0:T(8,128)(2,1)S(1)}, bf16[256,256]{1,0:T(8,128)(2,1)}, u32[]{:S(2)}) copy-start(bf16[256,256]{1,0:T(8,128)(2,1)} %weight_ref.3) | copy-start | bytes 393220
  16.9 4.3 %copy-start.2 = (bf16[128,256]{1,0:T(8,128)(2,1)S(1)}, bf16[128,256]{1,0:T(8,128)(2,1)}, u32[]{:S(2)}) copy-start(bf16[128,256]{1,0:T(8,128)(2,1)} %cot_ref.1) | copy-start | bytes 196612
  16.9 4.3 %collective-permute-start.6 = (bf16[128,256]{1,0:T(8,128)(2,1)S(1)}, bf16[128,256]{1,0:T(8,128)(2,1)S(1)}, u32[]{:S(2)}, u32[]{:S(2)}) collective-permute-start(bf16[128,256]{1,0:T(8,128)(2,1)S(1)} %shard_map.116.refs_0_), channel_id=1, source_target_pairs={{0,8},{1,9},{2,10},{3,11},{4,20},{5,21},{6,22},{7,23},{8,0},{9,1},... | collective-permute-start | bytes 196616 | tf_op jit(solution)/shard_map/ppermute | solution.py:69
  21.8 1.3 %collective-permute-start.7 = (bf16[144,256]{1,0:T(8,128)(2,1)S(1)}, bf16[144,256]{1,0:T(8,128)(2,1)S(1)}, u32[]{:S(2)}, u32[]{:S(2)}) collective-permute-start(bf16[144,256]{1,0:T(8,128)(2,1)S(1)} %get-tuple-element.29), channel_id=1, source_target_pairs={{0,4},{4,0},{8,12},{12,8},{16,20},{20,16},{24,28},{28,24},{1,5},{5... | collective-permute-start | bytes 221192 | tf_op jit(solution)/shard_map/ppermute | solution.py:82
  23.1 6.1 %collective-permute-start.15 = (bf16[144,256]{1,0:T(8,128)(2,1)S(1)}, bf16[144,256]{1,0:T(8,128)(2,1)S(1)}, u32[]{:S(2)}, u32[]{:S(2)}) collective-permute-start(bf16[144,256]{1,0:T(8,128)(2,1)S(1)} %shard_map.122.after_ref.refs_1_), channel_id=1, source_target_pairs={{0,2},{1,3},{2,0},{3,1},{4,5},{5,4},{6,7},{7,6},{8,10},{9,11},{10,... | collective-permute-start | bytes 221192 | tf_op jit(solution)/shard_map/ppermute | solution.py:69
  24.5 5.4 %collective-permute-start.8 = (bf16[128,256]{1,0:T(8,128)(2,1)S(1)}, bf16[128,256]{1,0:T(8,128)(2,1)S(1)}, u32[]{:S(2)}, u32[]{:S(2)}) collective-permute-start(bf16[128,256]{1,0:T(8,128)(2,1)S(1)} %get-tuple-element.28.grad_ref.refs_3_), channel_id=1, source_target_pairs={{0,24},{1,25},{2,26},{3,27},{4,28},{5,29},{6,30},{7,31},{8,16},{9,... | collective-permute-start | bytes 196616 | tf_op jit(solution)/shard_map/ppermute | solution.py:69
  26.0 5.0 %collective-permute-start.9 = (bf16[128,256]{1,0:T(8,128)(2,1)S(1)}, bf16[128,256]{1,0:T(8,128)(2,1)S(1)}, u32[]{:S(2)}, u32[]{:S(2)}) collective-permute-start(bf16[128,256]{1,0:T(8,128)(2,1)S(1)} %get-tuple-element.28.grad_ref.refs_3_), channel_id=1, source_target_pairs={{0,16},{1,17},{2,18},{3,19},{4,12},{5,13},{6,14},{7,15},{8,24},{9,... | collective-permute-start | bytes 196616 | tf_op jit(solution)/shard_map/ppermute | solution.py:69
  26.9 4.3 %collective-permute-start.10 = (bf16[128,256]{1,0:T(8,128)(2,1)S(1)}, bf16[128,256]{1,0:T(8,128)(2,1)S(1)}, u32[]{:S(2)}, u32[]{:S(2)}) collective-permute-start(bf16[128,256]{1,0:T(8,128)(2,1)S(1)} %get-tuple-element.28.grad_ref.refs_3_), channel_id=1, source_target_pairs={{0,8},{1,9},{2,10},{3,11},{4,20},{5,21},{6,22},{7,23},{8,0},{9,1},... | collective-permute-start | bytes 196616 | tf_op jit(solution)/shard_map/ppermute | solution.py:69
  29.3 4.4 %collective-permute-start.16 = (bf16[144,256]{1,0:T(8,128)(2,1)S(1)}, bf16[144,256]{1,0:T(8,128)(2,1)S(1)}, u32[]{:S(2)}, u32[]{:S(2)}) collective-permute-start(bf16[144,256]{1,0:T(8,128)(2,1)S(1)} %shard_map.128.refs_1_), channel_id=1, source_target_pairs={{0,1},{1,0},{2,3},{3,2},{4,6},{5,7},{6,4},{7,5},{8,9},{9,8},{10,11... | collective-permute-start | bytes 221192 | tf_op jit(solution)/shard_map/ppermute | solution.py:69
  31.2 4.4 %collective-permute-start.11 = (bf16[512,256]{1,0:T(8,128)(2,1)S(1)}, bf16[512,256]{1,0:T(8,128)(2,1)S(1)}, u32[]{:S(2)}, u32[]{:S(2)}) collective-permute-start(bf16[512,256]{1,0:T(8,128)(2,1)S(1)} %shard_map.123.source_ref), channel_id=1, source_target_pairs={{0,4},{4,0},{8,12},{12,8},{16,20},{20,16},{24,28},{28,24},{1,5},{5... | collective-permute-start | bytes 786440 | tf_op jit(solution)/shard_map/ppermute | solution.py:82
  33.7 4.5 %collective-permute-start.17 = (bf16[144,256]{1,0:T(8,128)(2,1)S(1)}, bf16[144,256]{1,0:T(8,128)(2,1)S(1)}, u32[]{:S(2)}, u32[]{:S(2)}) collective-permute-start(bf16[144,256]{1,0:T(8,128)(2,1)S(1)} %shard_map.129.refs_1_), channel_id=1, source_target_pairs={{0,16},{1,17},{2,18},{3,19},{4,12},{5,13},{6,14},{7,15},{8,24},{9,... | collective-permute-start | bytes 221192 | tf_op jit(solution)/shard_map/ppermute | solution.py:69
  35.9 6.8 %collective-permute-start.12 = (bf16[128,256]{1,0:T(8,128)(2,1)S(1)}, bf16[128,256]{1,0:T(8,128)(2,1)S(1)}, u32[]{:S(2)}, u32[]{:S(2)}) collective-permute-start(bf16[128,256]{1,0:T(8,128)(2,1)S(1)} %get-tuple-element.31), channel_id=1, source_target_pairs={{0,3},{1,2},{2,1},{3,0},{4,7},{5,6},{6,5},{7,4},{8,11},{9,10},{10,... | collective-permute-start | bytes 196616 | tf_op jit(solution)/shard_map/ppermute | solution.py:69
  38.2 5.9 %collective-permute-start.13 = (bf16[128,256]{1,0:T(8,128)(2,1)S(1)}, bf16[128,256]{1,0:T(8,128)(2,1)S(1)}, u32[]{:S(2)}, u32[]{:S(2)}) collective-permute-start(bf16[128,256]{1,0:T(8,128)(2,1)S(1)} %get-tuple-element.32), channel_id=1, source_target_pairs={{0,2},{1,3},{2,0},{3,1},{4,5},{5,4},{6,7},{7,6},{8,10},{9,11},{10,... | collective-permute-start | bytes 196616 | tf_op jit(solution)/shard_map/ppermute | solution.py:69
  38.3 5.9 %collective-permute-start.18 = (bf16[144,256]{1,0:T(8,128)(2,1)S(1)}, bf16[144,256]{1,0:T(8,128)(2,1)S(1)}, u32[]{:S(2)}, u32[]{:S(2)}) collective-permute-start(bf16[144,256]{1,0:T(8,128)(2,1)S(1)} %shard_map.130.refs_1_), channel_id=1, source_target_pairs={{0,8},{1,9},{2,10},{3,11},{4,20},{5,21},{6,22},{7,23},{8,0},{9,1},... | collective-permute-start | bytes 221192 | tf_op jit(solution)/shard_map/ppermute | solution.py:69
  39.1 5.2 %collective-permute-start.14 = (bf16[128,256]{1,0:T(8,128)(2,1)S(1)}, bf16[128,256]{1,0:T(8,128)(2,1)S(1)}, u32[]{:S(2)}, u32[]{:S(2)}) collective-permute-start(bf16[128,256]{1,0:T(8,128)(2,1)S(1)} %get-tuple-element.34), channel_id=1, source_target_pairs={{0,1},{1,0},{2,3},{3,2},{4,6},{5,7},{6,4},{7,5},{8,9},{9,8},{10,11... | collective-permute-start | bytes 196616 | tf_op jit(solution)/shard_map/ppermute | solution.py:69
  44.2 1.4 %collective-permute-start.19 = (f32[128,256]{1,0:T(8,128)S(1)}, f32[128,256]{1,0:T(8,128)S(1)}, u32[]{:S(2)}, u32[]{:S(2)}) collective-permute-start(f32[128,256]{1,0:T(8,128)S(1)} %get-tuple-element.35.own_ref), channel_id=1, source_target_pairs={{0,4},{4,0},{8,12},{12,8},{16,20},{20,16},{24,28},{28,24},{1,5},{5... | collective-permute-start | bytes 393224 | tf_op jit(solution)/shard_map/ppermute | solution.py:82

commit v16 on v14

--- a/solution.py
+++ b/solution.py
@@ -226,16 +226,17 @@
     out_ref[...] = in_ref[...]
 
 
-def term_kernel(agg_ref, grad_ref, mine_ref, theirs_ref, acc_ref):
+def term_kernel(agg_ref, grad_ref, out_ref, *, own):
+    half = agg_ref.shape[1] // 2
+    core = core_index() if own else 1 - core_index()
     grad = grad_ref[...]
-    acc_ref[...] = lax.dot_general(
-        agg_ref[...], grad, (((0,), (0,)), ((), ())), preferred_element_type=F32
-    )
-    half = acc_ref.shape[0] // 2
-    bias = bias_rows(jnp.sum(grad.astype(F32), axis=0, keepdims=True)).astype(BF16)
-    for ref, core in ((mine_ref, core_index()), (theirs_ref, 1 - core_index())):
-        ref[:half, :] = acc_ref[block_at(core, half), :].astype(BF16)
-        ref[half:, :] = bias
+    out_ref[:half, :] = lax.dot_general(
+        agg_ref[:, block_at(core, half)],
+        grad,
+        (((0,), (0,)), ((), ())),
+        preferred_element_type=F32,
+    ).astype(BF16)
+    out_ref[half:, :] = bias_rows(jnp.sum(grad.astype(F32), axis=0, keepdims=True)).astype(BF16)
 
 
 def add_terms_kernel(*refs, n_terms):
@@ -341,15 +342,15 @@
     near = 1
     own_nodes = n_chip * tile
 
-    def add(terms, flops=0):
+    def add(terms, flops=0, after=()):
         return call(
             functools.partial(add_terms_kernel, n_terms=len(terms)),
             like(half + BIAS_ROWS, hidden),
-            [VMEM_SPEC] * len(terms),
+            [VMEM_SPEC] * (len(terms) + len(after)),
             [],
             flops or len(terms) * half * hidden,
             len(terms) * half * hidden * 2,
-        )(*terms)
+        )(*terms, *after)
 
     is_dense = n_row * n_col <= 2 * slots
     if is_dense:
@@ -441,17 +442,20 @@
     )(weight, bias_row, cotangent, *parts)
     grads = exchange([grad] * n_chip, "col", n_col, 2)
     hidden_out = call(copy_kernel, like(tile, hidden), [VMEM_SPEC], [], 0, 2 * block_bytes)(hidden_own)
-    mine, theirs = call(
-        term_kernel,
-        [like(half + BIAS_ROWS, hidden)] * 2,
-        [VMEM_SPEC] * 2,
-        [pltpu.VMEM((width, hidden), F32)],
-        matrix,
-        6 * block_bytes,
-    )(aggregated, grad)
+    mine, theirs = (
+        call(
+            functools.partial(term_kernel, own=own),
+            like(half + BIAS_ROWS, hidden),
+            [VMEM_SPEC] * 2,
+            [],
+            matrix // 2,
+            4 * block_bytes,
+        )(aggregated, grad)
+        for own in (True, False)
+    )
     chip_term = add([swap_cores(theirs, n_col), mine])
     add_late = functools.partial(add, flops=ROW_SUM_WEIGHT * matrix)
-    row_term = add_late(total_over(chip_term, add, "row", n_row))
+    row_terms = total_over(chip_term, add, "row", n_row)
 
     own_grads = call(
         gather_kernel,
@@ -471,6 +475,7 @@
             slots * matrix // 2,
             row_nodes * hidden * 8,
         )(turned, own_grads)
+        row_term = add_late(row_terms, after=[back_own])
         back_pieces = call(
             back_pieces_kernel,
             [like(tile, hidden)] * n_row,
@@ -480,6 +485,7 @@
             row_nodes * hidden * 8,
         )(turned, back_own, other_grads)
     else:
+        row_term = add_late(row_terms)
         back_pieces = call(
             slot_back_kernel,
             [like(tile, hidden)] * n_row,

time: 45.4 us -> 45.1 us (level)
    ppermute x4, waiting for transfers between devices: 2.79 us -> 2.27 us  [swap_cores(): return lax.ppermute(block, 'col', [(i, i ^ 1) for i in range(size)])]
  transfers between devices with their start and end apart: 20 -> 20, of which waited for: 14 -> 12; matrix products, arithmetic and copies ran while one was open for 0% -> 0% of each run, Pallas kernels for 8% -> 9%
where the time goes in v16:
time: 45.1 us; the launch traced here: 44.9 us
  starting transfers between devices  22.4 us (50%)
  waiting for transfers between devices  15.3 us (34%)
  Pallas kernels  5.74 us (13%)
  between operations  1.48 us (3%)
    ppermute x12, starting transfers between devices, exchange(): lax.ppermute(blocks[k], axis, pairs)  16.4 us
    ppermute x12, waiting for transfers between devices, exchange(): lax.ppermute(blocks[k], axis, pairs)  9.6 us
    ppermute x4, starting transfers between devices, total_over(): terms = [lax.ppermute(block, axis, pairs_of(step, size, cores)), block]  5.62 us
    ppermute x4, waiting for transfers between devices, total_over(): terms = [lax.ppermute(block, axis, pairs_of(step, size, cores)), block]  3.47 us
    ppermute x4, waiting for transfers between devices, swap_cores(): return lax.ppermute(block, 'col', [(i, i ^ 1) for i in range(size)])  2.27 us
    pallas_call x1, Pallas kernels, local(): call(dense_kernel, (like(row_nodes, col_nodes), like(1, hidden, F32)), [S...  1.64 us
  transfers between devices with their start and end apart: 20, of which 12 were waited for; matrix products, arithmetic and copies ran while one was open for 0% of the time, Pallas kernels for 9%

profile of v16, /device:TPU:0, one launch (start us, length us, event | category | flops | bytes accessed | tf_op | source)
XLA Modules:
  0.0 44.9 jit_solution(15568092102034370074)
XLA Ops:
  0.6 5.1 %collective-permute-start = (bf16[128,256]{1,0:T(8,128)(2,1)}, bf16[128,256]{1,0:T(8,128)(2,1)S(1)}, u32[]{:S(2)}, u32[]{:S(2)}) collective-permute-start(bf16[128,256]{1,0:T(8,128)(2,1)} %refs_3_.1), channel_id=1, source_target_pairs={{0,3},{1,2},{2,1},{3,0},{4,7},{5,6},{6,5},{7,4},{8,11},{9,10},{10,... | collective-permute-start | bytes 196616 | tf_op jit(solution)/shard_map/ppermute | solution.py:56
  5.8 0.6 %collective-permute-start.2 = (bf16[128,256]{1,0:T(8,128)(2,1)}, bf16[128,256]{1,0:T(8,128)(2,1)S(1)}, u32[]{:S(2)}, u32[]{:S(2)}) collective-permute-start(bf16[128,256]{1,0:T(8,128)(2,1)} %refs_3_.1), channel_id=1, source_target_pairs={{0,1},{1,0},{2,3},{3,2},{4,5},{5,4},{6,7},{7,6},{8,9},{9,8},{10,11... | collective-permute-start | bytes 196616 | tf_op jit(solution)/shard_map/ppermute | solution.py:56
  7.1 1.6 %shard_map.111 = (bf16[1024,512]{1,0:T(8,128)(2,1)S(1)}, f32[1,256]{1,0:T(1,128)S(1)}) custom-call(s32[1,1]{1,0:T(1,128)S(6)} %copy.12.count_ref, s32[1,1,32]{2,1,0:T(1,128)} %row_hbm.1, s32[1,1,32]{2,1,0:T(1,128)} %col_hbm.1, bf16[1,1,32,128,128]{4,3,2,1,0:T(8,128)(2,1)} %tiles_hbm.1, f32[1,256]{1,0:T(1,128)} %bitcast.2), custom_call_target="tpu_custom_call" | custom-call | bytes 6291456 | tf_op jit(solution)/shard_map/pallas_call | solution.py:358
  8.7 2.9 %collective-permute-done.1.refs_1_ = bf16[128,256]{1,0:T(8,128)(2,1)S(1)} collective-permute-done((bf16[128,256]{1,0:T(8,128)(2,1)}, bf16[128,256]{1,0:T(8,128)(2,1)S(1)}, u32[]{:S(2)}, u32[]{:S(2)}) %collective-permute-start.1) | collective-permute-done | bytes 65568 | tf_op jit(solution)/shard_map/ppermute | solution.py:56
  11.6 0.3 shard_map.112
  12.3 1.2 %collective-permute-done.3.other_ref = bf16[512,256]{1,0:T(8,128)(2,1)S(1)} collective-permute-done((bf16[512,256]{1,0:T(8,128)(2,1)S(1)}, bf16[512,256]{1,0:T(8,128)(2,1)S(1)}, u32[]{:S(2)}, u32[]{:S(2)}) %collective-permute-start.3) | collective-permute-done | bytes 262176 | tf_op jit(solution)/shard_map/ppermute | solution.py:61
  13.5 2.5 %collective-permute-start.4 = (bf16[128,256]{1,0:T(8,128)(2,1)S(1)}, bf16[128,256]{1,0:T(8,128)(2,1)S(1)}, u32[]{:S(2)}, u32[]{:S(2)}) collective-permute-start(bf16[128,256]{1,0:T(8,128)(2,1)S(1)} %shard_map.114.refs_0_), channel_id=1, source_target_pairs={{0,24},{4,28},{8,16},{12,20},{16,8},{20,12},{24,0},{28,4},{1,25},{... | collective-permute-start | bytes 196616 | tf_op jit(solution)/shard_map/ppermute | solution.py:56
  16.1 0.6 %collective-permute-start.5 = (bf16[128,256]{1,0:T(8,128)(2,1)S(1)}, bf16[128,256]{1,0:T(8,128)(2,1)S(1)}, u32[]{:S(2)}, u32[]{:S(2)}) collective-permute-start(bf16[128,256]{1,0:T(8,128)(2,1)S(1)} %shard_map.115.refs_0_), channel_id=1, source_target_pairs={{0,16},{4,20},{8,24},{12,28},{16,0},{20,4},{24,8},{28,12},{1,17},{... | collective-permute-start | bytes 196616 | tf_op jit(solution)/shard_map/ppermute | solution.py:56
  16.7 0.6 %collective-permute-start.6 = (bf16[128,256]{1,0:T(8,128)(2,1)S(1)}, bf16[128,256]{1,0:T(8,128)(2,1)S(1)}, u32[]{:S(2)}, u32[]{:S(2)}) collective-permute-start(bf16[128,256]{1,0:T(8,128)(2,1)S(1)} %shard_map.116.refs_0_), channel_id=1, source_target_pairs={{0,8},{4,12},{8,0},{12,4},{16,24},{20,28},{24,16},{28,20},{1,9},{5... | collective-permute-start | bytes 196616 | tf_op jit(solution)/shard_map/ppermute | solution.py:56
  17.3 1.5 %collective-permute-done.4.refs_0_ = bf16[128,256]{1,0:T(8,128)(2,1)S(1)} collective-permute-done((bf16[128,256]{1,0:T(8,128)(2,1)S(1)}, bf16[128,256]{1,0:T(8,128)(2,1)S(1)}, u32[]{:S(2)}, u32[]{:S(2)}) %collective-permute-start.4) | collective-permute-done | bytes 65568 | tf_op jit(solution)/shard_map/ppermute | solution.py:56
  18.8 1.6 %collective-permute-done.5.refs_1_ = bf16[128,256]{1,0:T(8,128)(2,1)S(1)} collective-permute-done((bf16[128,256]{1,0:T(8,128)(2,1)S(1)}, bf16[128,256]{1,0:T(8,128)(2,1)S(1)}, u32[]{:S(2)}, u32[]{:S(2)}) %collective-permute-start.5) | collective-permute-done | bytes 65568 | tf_op jit(solution)/shard_map/ppermute | solution.py:56
  20.4 0.6 %collective-permute-done.6.refs_2_ = bf16[128,256]{1,0:T(8,128)(2,1)S(1)} collective-permute-done((bf16[128,256]{1,0:T(8,128)(2,1)S(1)}, bf16[128,256]{1,0:T(8,128)(2,1)S(1)}, u32[]{:S(2)}, u32[]{:S(2)}) %collective-permute-start.6) | collective-permute-done | bytes 65568 | tf_op jit(solution)/shard_map/ppermute | solution.py:56
  21.8 1.0 %collective-permute-done.7.refs_0_ = bf16[144,256]{1,0:T(8,128)(2,1)S(1)} collective-permute-done((bf16[144,256]{1,0:T(8,128)(2,1)S(1)}, bf16[144,256]{1,0:T(8,128)(2,1)S(1)}, u32[]{:S(2)}, u32[]{:S(2)}) %collective-permute-start.7) | collective-permute-done | bytes 73760 | tf_op jit(solution)/shard_map/ppermute | solution.py:61
  22.8 1.1 %collective-permute-start.15 = (bf16[144,256]{1,0:T(8,128)(2,1)S(1)}, bf16[144,256]{1,0:T(8,128)(2,1)S(1)}, u32[]{:S(2)}, u32[]{:S(2)}) collective-permute-start(bf16[144,256]{1,0:T(8,128)(2,1)S(1)} %shard_map.123.after_ref.refs_1_), channel_id=1, source_target_pairs={{0,1},{1,0},{2,3},{3,2},{4,5},{5,4},{6,7},{7,6},{8,9},{9,8},{10,11... | collective-permute-start | bytes 221192 | tf_op jit(solution)/shard_map/ppermute | solution.py:71
  24.0 1.5 %collective-permute-start.8 = (bf16[128,256]{1,0:T(8,128)(2,1)S(1)}, bf16[128,256]{1,0:T(8,128)(2,1)S(1)}, u32[]{:S(2)}, u32[]{:S(2)}) collective-permute-start(bf16[128,256]{1,0:T(8,128)(2,1)S(1)} %get-tuple-element.26.grad_ref.refs_3_), channel_id=1, source_target_pairs={{0,24},{4,28},{8,16},{12,20},{16,8},{20,12},{24,0},{28,4},{1,25},{... | collective-permute-start | bytes 196616 | tf_op jit(solution)/shard_map/ppermute | solution.py:56
  25.5 0.5 %collective-permute-start.9 = (bf16[128,256]{1,0:T(8,128)(2,1)S(1)}, bf16[128,256]{1,0:T(8,128)(2,1)S(1)}, u32[]{:S(2)}, u32[]{:S(2)}) collective-permute-start(bf16[128,256]{1,0:T(8,128)(2,1)S(1)} %get-tuple-element.26.grad_ref.refs_3_), channel_id=1, source_target_pairs={{0,16},{4,20},{8,24},{12,28},{16,0},{20,4},{24,8},{28,12},{1,17},{... | collective-permute-start | bytes 196616 | tf_op jit(solution)/shard_map/ppermute | solution.py:56
  26.0 1.5 %collective-permute-start.10 = (bf16[128,256]{1,0:T(8,128)(2,1)S(1)}, bf16[128,256]{1,0:T(8,128)(2,1)S(1)}, u32[]{:S(2)}, u32[]{:S(2)}) collective-permute-start(bf16[128,256]{1,0:T(8,128)(2,1)S(1)} %get-tuple-element.26.grad_ref.refs_3_), channel_id=1, source_target_pairs={{0,8},{4,12},{8,0},{12,4},{16,24},{20,28},{24,16},{28,20},{1,9},{5... | collective-permute-start | bytes 196616 | tf_op jit(solution)/shard_map/ppermute | solution.py:56
  27.5 2.3 %collective-permute-start.16 = (bf16[144,256]{1,0:T(8,128)(2,1)S(1)}, bf16[144,256]{1,0:T(8,128)(2,1)S(1)}, u32[]{:S(2)}, u32[]{:S(2)}) collective-permute-start(bf16[144,256]{1,0:T(8,128)(2,1)S(1)} %shard_map.129.refs_1_), channel_id=1, source_target_pairs={{0,2},{1,3},{2,0},{3,1},{4,6},{5,7},{6,4},{7,5},{8,10},{9,11},{10,... | collective-permute-start | bytes 221192 | tf_op jit(solution)/shard_map/ppermute | solution.py:71
  29.8 0.4 collective-permute-done.9.refs_1_
  30.4 0.3 shard_map.120.turned_ref
  30.7 0.3 shard_map.125.own_ref.refs_2_
  31.1 2.6 %collective-permute-done.16.refs_0_ = bf16[144,256]{1,0:T(8,128)(2,1)S(1)} collective-permute-done((bf16[144,256]{1,0:T(8,128)(2,1)S(1)}, bf16[144,256]{1,0:T(8,128)(2,1)S(1)}, u32[]{:S(2)}, u32[]{:S(2)}) %collective-permute-start.16) | collective-permute-done | bytes 73760 | tf_op jit(solution)/shard_map/ppermute | solution.py:71
  33.6 0.6 %collective-permute-start.17 = (bf16[144,256]{1,0:T(8,128)(2,1)S(1)}, bf16[144,256]{1,0:T(8,128)(2,1)S(1)}, u32[]{:S(2)}, u32[]{:S(2)}) collective-permute-start(bf16[144,256]{1,0:T(8,128)(2,1)S(1)} %shard_map.130.refs_1_), channel_id=1, source_target_pairs={{0,8},{4,12},{8,0},{12,4},{16,24},{20,28},{24,16},{28,20},{1,9},{5... | collective-permute-start | bytes 221192 | tf_op jit(solution)/shard_map/ppermute | solution.py:71
  34.3 0.3 shard_map.126
  34.6 2.6 %collective-permute-start.12 = (bf16[128,256]{1,0:T(8,128)(2,1)S(1)}, bf16[128,256]{1,0:T(8,128)(2,1)S(1)}, u32[]{:S(2)}, u32[]{:S(2)}) collective-permute-start(bf16[128,256]{1,0:T(8,128)(2,1)S(1)} %get-tuple-element.27), channel_id=1, source_target_pairs={{0,3},{1,2},{2,1},{3,0},{4,7},{5,6},{6,5},{7,4},{8,11},{9,10},{10,... | collective-permute-start | bytes 196616 | tf_op jit(solution)/shard_map/ppermute | solution.py:56
  37.2 0.9 %collective-permute-done.17.refs_0_ = bf16[144,256]{1,0:T(8,128)(2,1)S(1)} collective-permute-done((bf16[144,256]{1,0:T(8,128)(2,1)S(1)}, bf16[144,256]{1,0:T(8,128)(2,1)S(1)}, u32[]{:S(2)}, u32[]{:S(2)}) %collective-permute-start.17) | collective-permute-done | bytes 73760 | tf_op jit(solution)/shard_map/ppermute | solution.py:71
  38.1 1.6 %collective-permute-start.18 = (bf16[144,256]{1,0:T(8,128)(2,1)S(1)}, bf16[144,256]{1,0:T(8,128)(2,1)S(1)}, u32[]{:S(2)}, u32[]{:S(2)}) collective-permute-start(bf16[144,256]{1,0:T(8,128)(2,1)S(1)} %shard_map.131.refs_1_), channel_id=1, source_target_pairs={{0,16},{4,20},{8,24},{12,28},{16,0},{20,4},{24,8},{28,12},{1,17},{... | collective-permute-start | bytes 221192 | tf_op jit(solution)/shard_map/ppermute | solution.py:71
  39.7 1.0 %collective-permute-start.14 = (bf16[128,256]{1,0:T(8,128)(2,1)S(1)}, bf16[128,256]{1,0:T(8,128)(2,1)S(1)}, u32[]{:S(2)}, u32[]{:S(2)}) collective-permute-start(bf16[128,256]{1,0:T(8,128)(2,1)S(1)} %get-tuple-element.30), channel_id=1, source_target_pairs={{0,1},{1,0},{2,3},{3,2},{4,5},{5,4},{6,7},{7,6},{8,9},{9,8},{10,11... | collective-permute-start | bytes 196616 | tf_op jit(solution)/shard_map/ppermute | solution.py:56
  40.6 0.6 %shard_map.119 = bf16[128,256]{1,0:T(8,128)(2,1)} custom-call(bf16[128,256]{1,0:T(8,128)(2,1)S(1)} %get-tuple-element.24.in_ref), custom_call_target="tpu_custom_call" | custom-call | bytes 131072 | tf_op jit(solution)/shard_map/pallas_call | solution.py:444
  41.3 1.3 %collective-permute-done.13.refs_1_ = bf16[128,256]{1,0:T(8,128)(2,1)S(1)} collective-permute-done((bf16[128,256]{1,0:T(8,128)(2,1)S(1)}, bf16[128,256]{1,0:T(8,128)(2,1)S(1)}, u32[]{:S(2)}, u32[]{:S(2)}) %collective-permute-start.13) | collective-permute-done | bytes 65568 | tf_op jit(solution)/shard_map/ppermute | solution.py:56
  42.7 1.3 %collective-permute-done.14.last_ref = bf16[128,256]{1,0:T(8,128)(2,1)S(1)} collective-permute-done((bf16[128,256]{1,0:T(8,128)(2,1)S(1)}, bf16[128,256]{1,0:T(8,128)(2,1)S(1)}, u32[]{:S(2)}, u32[]{:S(2)}) %collective-permute-start.14) | collective-permute-done | bytes 65568 | tf_op jit(solution)/shard_map/ppermute | solution.py:56
  44.2 0.8 %shard_map.133 = (bf16[128,256]{1,0:T(8,128)(2,1)}, f32[256,256]{1,0:T(8,128)}, f32[1,256]{1,0:T(1,128)}) custom-call(bf16[128,256]{1,0:T(8,128)(2,1)S(1)} %shard_map.128.features_ref, f32[128,256]{1,0:T(8,128)S(1)} %get-tuple-element.31.own_ref, f32[128,256]{1,0:T(8,128)S(1)} %collective-permute-done.19.other_ref, f32[1,256]{1,0:T(1,128)S(1)} %get-tuple-element.32.bias_ref), custom_call_target="tpu_custom_call" | custom-call | bytes 524288 | tf_op jit(solution)/shard_map/pallas_call | solution.py:524
  (37 shorter events, 1.9 us)
Async XLA Ops:
  0.6 8.1 %collective-permute-start = (bf16[128,256]{1,0:T(8,128)(2,1)}, bf16[128,256]{1,0:T(8,128)(2,1)S(1)}, u32[]{:S(2)}, u32[]{:S(2)}) collective-permute-start(bf16[128,256]{1,0:T(8,128)(2,1)} %refs_3_.1), channel_id=1, source_target_pairs={{0,3},{1,2},{2,1},{3,0},{4,7},{5,6},{6,5},{7,4},{8,11},{9,10},{10,... | collective-permute-start | bytes 196616 | tf_op jit(solution)/shard_map/ppermute | solution.py:56
  5.7 5.8 %collective-permute-start.1 = (bf16[128,256]{1,0:T(8,128)(2,1)}, bf16[128,256]{1,0:T(8,128)(2,1)S(1)}, u32[]{:S(2)}, u32[]{:S(2)}) collective-permute-start(bf16[128,256]{1,0:T(8,128)(2,1)} %refs_3_.1), channel_id=1, source_target_pairs={{0,2},{1,3},{2,0},{3,1},{4,6},{5,7},{6,4},{7,5},{8,10},{9,11},{10,... | collective-permute-start | bytes 196616 | tf_op jit(solution)/shard_map/ppermute | solution.py:56
  5.8 5.8 %collective-permute-start.2 = (bf16[128,256]{1,0:T(8,128)(2,1)}, bf16[128,256]{1,0:T(8,128)(2,1)S(1)}, u32[]{:S(2)}, u32[]{:S(2)}) collective-permute-start(bf16[128,256]{1,0:T(8,128)(2,1)} %refs_3_.1), channel_id=1, source_target_pairs={{0,1},{1,0},{2,3},{3,2},{4,5},{5,4},{6,7},{7,6},{8,9},{9,8},{10,11... | collective-permute-start | bytes 196616 | tf_op jit(solution)/shard_map/ppermute | solution.py:56
  7.0 4.5 %copy-start.1 = (bf16[128,256]{1,0:T(8,128)(2,1)S(1)}, bf16[128,256]{1,0:T(8,128)(2,1)}, u32[]{:S(2)}) copy-start(bf16[128,256]{1,0:T(8,128)(2,1)} %refs_3_.1) | copy-start | bytes 196612
  11.9 1.6 %collective-permute-start.3 = (bf16[512,256]{1,0:T(8,128)(2,1)S(1)}, bf16[512,256]{1,0:T(8,128)(2,1)S(1)}, u32[]{:S(2)}, u32[]{:S(2)}) collective-permute-start(bf16[512,256]{1,0:T(8,128)(2,1)S(1)} %get-tuple-element.23), channel_id=1, source_target_pairs={{0,4},{4,0},{8,12},{12,8},{16,20},{20,16},{24,28},{28,24},{1,5},{5... | collective-permute-start | bytes 786440 | tf_op jit(solution)/shard_map/ppermute | solution.py:61
  13.5 5.2 %collective-permute-start.4 = (bf16[128,256]{1,0:T(8,128)(2,1)S(1)}, bf16[128,256]{1,0:T(8,128)(2,1)S(1)}, u32[]{:S(2)}, u32[]{:S(2)}) collective-permute-start(bf16[128,256]{1,0:T(8,128)(2,1)S(1)} %shard_map.114.refs_0_), channel_id=1, source_target_pairs={{0,24},{4,28},{8,16},{12,20},{16,8},{20,12},{24,0},{28,4},{1,25},{... | collective-permute-start | bytes 196616 | tf_op jit(solution)/shard_map/ppermute | solution.py:56
  16.1 4.3 %collective-permute-start.5 = (bf16[128,256]{1,0:T(8,128)(2,1)S(1)}, bf16[128,256]{1,0:T(8,128)(2,1)S(1)}, u32[]{:S(2)}, u32[]{:S(2)}) collective-permute-start(bf16[128,256]{1,0:T(8,128)(2,1)S(1)} %shard_map.115.refs_0_), channel_id=1, source_target_pairs={{0,16},{4,20},{8,24},{12,28},{16,0},{20,4},{24,8},{28,12},{1,17},{... | collective-permute-start | bytes 196616 | tf_op jit(solution)/shard_map/ppermute | solution.py:56
  16.6 4.4 %copy-start = (bf16[256,256]{1,0:T(8,128)(2,1)S(1)}, bf16[256,256]{1,0:T(8,128)(2,1)}, u32[]{:S(2)}) copy-start(bf16[256,256]{1,0:T(8,128)(2,1)} %weight_ref.3) | copy-start | bytes 393220
  16.7 4.3 %copy-start.2 = (bf16[128,256]{1,0:T(8,128)(2,1)S(1)}, bf16[128,256]{1,0:T(8,128)(2,1)}, u32[]{:S(2)}) copy-start(bf16[128,256]{1,0:T(8,128)(2,1)} %cot_ref.1) | copy-start | bytes 196612
  16.7 4.3 %collective-permute-start.6 = (bf16[128,256]{1,0:T(8,128)(2,1)S(1)}, bf16[128,256]{1,0:T(8,128)(2,1)S(1)}, u32[]{:S(2)}, u32[]{:S(2)}) collective-permute-start(bf16[128,256]{1,0:T(8,128)(2,1)S(1)} %shard_map.116.refs_0_), channel_id=1, source_target_pairs={{0,8},{4,12},{8,0},{12,4},{16,24},{20,28},{24,16},{28,20},{1,9},{5... | collective-permute-start | bytes 196616 | tf_op jit(solution)/shard_map/ppermute | solution.py:56
  21.5 1.3 %collective-permute-start.7 = (bf16[144,256]{1,0:T(8,128)(2,1)S(1)}, bf16[144,256]{1,0:T(8,128)(2,1)S(1)}, u32[]{:S(2)}, u32[]{:S(2)}) collective-permute-start(bf16[144,256]{1,0:T(8,128)(2,1)S(1)} %shard_map.121), channel_id=1, source_target_pairs={{0,4},{4,0},{8,12},{12,8},{16,20},{20,16},{24,28},{28,24},{1,5},{5... | collective-permute-start | bytes 221192 | tf_op jit(solution)/shard_map/ppermute | solution.py:61
  22.8 4.6 %collective-permute-start.15 = (bf16[144,256]{1,0:T(8,128)(2,1)S(1)}, bf16[144,256]{1,0:T(8,128)(2,1)S(1)}, u32[]{:S(2)}, u32[]{:S(2)}) collective-permute-start(bf16[144,256]{1,0:T(8,128)(2,1)S(1)} %shard_map.123.after_ref.refs_1_), channel_id=1, source_target_pairs={{0,1},{1,0},{2,3},{3,2},{4,5},{5,4},{6,7},{7,6},{8,9},{9,8},{10,11... | collective-permute-start | bytes 221192 | tf_op jit(solution)/shard_map/ppermute | solution.py:71
  24.0 5.8 %collective-permute-start.8 = (bf16[128,256]{1,0:T(8,128)(2,1)S(1)}, bf16[128,256]{1,0:T(8,128)(2,1)S(1)}, u32[]{:S(2)}, u32[]{:S(2)}) collective-permute-start(bf16[128,256]{1,0:T(8,128)(2,1)S(1)} %get-tuple-element.26.grad_ref.refs_3_), channel_id=1, source_target_pairs={{0,24},{4,28},{8,16},{12,20},{16,8},{20,12},{24,0},{28,4},{1,25},{... | collective-permute-start | bytes 196616 | tf_op jit(solution)/shard_map/ppermute | solution.py:56
  25.5 4.7 %collective-permute-start.9 = (bf16[128,256]{1,0:T(8,128)(2,1)S(1)}, bf16[128,256]{1,0:T(8,128)(2,1)S(1)}, u32[]{:S(2)}, u32[]{:S(2)}) collective-permute-start(bf16[128,256]{1,0:T(8,128)(2,1)S(1)} %get-tuple-element.26.grad_ref.refs_3_), channel_id=1, source_target_pairs={{0,16},{4,20},{8,24},{12,28},{16,0},{20,4},{24,8},{28,12},{1,17},{... | collective-permute-start | bytes 196616 | tf_op jit(solution)/shard_map/ppermute | solution.py:56
  26.0 4.3 %collective-permute-start.10 = (bf16[128,256]{1,0:T(8,128)(2,1)S(1)}, bf16[128,256]{1,0:T(8,128)(2,1)S(1)}, u32[]{:S(2)}, u32[]{:S(2)}) collective-permute-start(bf16[128,256]{1,0:T(8,128)(2,1)S(1)} %get-tuple-element.26.grad_ref.refs_3_), channel_id=1, source_target_pairs={{0,8},{4,12},{8,0},{12,4},{16,24},{20,28},{24,16},{28,20},{1,9},{5... | collective-permute-start | bytes 196616 | tf_op jit(solution)/shard_map/ppermute | solution.py:56
  27.5 6.1 %collective-permute-start.16 = (bf16[144,256]{1,0:T(8,128)(2,1)S(1)}, bf16[144,256]{1,0:T(8,128)(2,1)S(1)}, u32[]{:S(2)}, u32[]{:S(2)}) collective-permute-start(bf16[144,256]{1,0:T(8,128)(2,1)S(1)} %shard_map.129.refs_1_), channel_id=1, source_target_pairs={{0,2},{1,3},{2,0},{3,1},{4,6},{5,7},{6,4},{7,5},{8,10},{9,11},{10,... | collective-permute-start | bytes 221192 | tf_op jit(solution)/shard_map/ppermute | solution.py:71
  30.3 4.0 %collective-permute-start.11 = (bf16[512,256]{1,0:T(8,128)(2,1)S(1)}, bf16[512,256]{1,0:T(8,128)(2,1)S(1)}, u32[]{:S(2)}, u32[]{:S(2)}) collective-permute-start(bf16[512,256]{1,0:T(8,128)(2,1)S(1)} %shard_map.124.source_ref), channel_id=1, source_target_pairs={{0,4},{4,0},{8,12},{12,8},{16,20},{20,16},{24,28},{28,24},{1,5},{5... | collective-permute-start | bytes 786440 | tf_op jit(solution)/shard_map/ppermute | solution.py:61
  33.6 4.4 %collective-permute-start.17 = (bf16[144,256]{1,0:T(8,128)(2,1)S(1)}, bf16[144,256]{1,0:T(8,128)(2,1)S(1)}, u32[]{:S(2)}, u32[]{:S(2)}) collective-permute-start(bf16[144,256]{1,0:T(8,128)(2,1)S(1)} %shard_map.130.refs_1_), channel_id=1, source_target_pairs={{0,8},{4,12},{8,0},{12,4},{16,24},{20,28},{24,16},{28,20},{1,9},{5... | collective-permute-start | bytes 221192 | tf_op jit(solution)/shard_map/ppermute | solution.py:71
  34.6 6.7 %collective-permute-start.12 = (bf16[128,256]{1,0:T(8,128)(2,1)S(1)}, bf16[128,256]{1,0:T(8,128)(2,1)S(1)}, u32[]{:S(2)}, u32[]{:S(2)}) collective-permute-start(bf16[128,256]{1,0:T(8,128)(2,1)S(1)} %get-tuple-element.27), channel_id=1, source_target_pairs={{0,3},{1,2},{2,1},{3,0},{4,7},{5,6},{6,5},{7,4},{8,11},{9,10},{10,... | collective-permute-start | bytes 196616 | tf_op jit(solution)/shard_map/ppermute | solution.py:56
  37.2 5.4 %collective-permute-start.13 = (bf16[128,256]{1,0:T(8,128)(2,1)S(1)}, bf16[128,256]{1,0:T(8,128)(2,1)S(1)}, u32[]{:S(2)}, u32[]{:S(2)}) collective-permute-start(bf16[128,256]{1,0:T(8,128)(2,1)S(1)} %get-tuple-element.28), channel_id=1, source_target_pairs={{0,2},{1,3},{2,0},{3,1},{4,6},{5,7},{6,4},{7,5},{8,10},{9,11},{10,... | collective-permute-start | bytes 196616 | tf_op jit(solution)/shard_map/ppermute | solution.py:56
  38.1 4.5 %collective-permute-start.18 = (bf16[144,256]{1,0:T(8,128)(2,1)S(1)}, bf16[144,256]{1,0:T(8,128)(2,1)S(1)}, u32[]{:S(2)}, u32[]{:S(2)}) collective-permute-start(bf16[144,256]{1,0:T(8,128)(2,1)S(1)} %shard_map.131.refs_1_), channel_id=1, source_target_pairs={{0,16},{4,20},{8,24},{12,28},{16,0},{20,4},{24,8},{28,12},{1,17},{... | collective-permute-start | bytes 221192 | tf_op jit(solution)/shard_map/ppermute | solution.py:71
  39.7 4.3 %collective-permute-start.14 = (bf16[128,256]{1,0:T(8,128)(2,1)S(1)}, bf16[128,256]{1,0:T(8,128)(2,1)S(1)}, u32[]{:S(2)}, u32[]{:S(2)}) collective-permute-start(bf16[128,256]{1,0:T(8,128)(2,1)S(1)} %get-tuple-element.30), channel_id=1, source_target_pairs={{0,1},{1,0},{2,3},{3,2},{4,5},{5,4},{6,7},{7,6},{8,9},{9,8},{10,11... | collective-permute-start | bytes 196616 | tf_op jit(solution)/shard_map/ppermute | solution.py:56
  42.6 1.5 %collective-permute-start.19 = (f32[128,256]{1,0:T(8,128)S(1)}, f32[128,256]{1,0:T(8,128)S(1)}, u32[]{:S(2)}, u32[]{:S(2)}) collective-permute-start(f32[128,256]{1,0:T(8,128)S(1)} %get-tuple-element.31.own_ref), channel_id=1, source_target_pairs={{0,4},{4,0},{8,12},{12,8},{16,20},{20,16},{24,28},{28,24},{1,5},{5... | collective-permute-start | bytes 393224 | tf_op jit(solution)/shard_map/ppermute | solution.py:61

commit v17 on v16

--- a/solution.py
+++ b/solution.py
@@ -48,9 +48,13 @@
     return [(i, partner(i // cores, k, size // cores) * cores + i % cores) for i in range(size)]
 
 
-def exchange(blocks, axis, size, cores=1):
+def half_first(count):
+    return [count // 2] + [k for k in far_first(count) if k != count // 2]
+
+
+def exchange(blocks, axis, size, cores=1, order=far_first):
     received = []
-    for k in far_first(size // cores):
+    for k in order(size // cores):
         pairs = pairs_of(k, size, cores)
         moves = any(i != j for i, j in pairs)
         received.append(lax.ppermute(blocks[k], axis, pairs) if moves else blocks[k])
@@ -156,9 +160,9 @@
     return jnp.dot(left, right, preferred_element_type=F32)
 
 
-def gather_sources(sources, source_ref, index):
+def gather_sources(sources, source_ref, index, order):
     tile = sources[0].shape[0]
-    for k, ref in zip(far_first(len(sources)), sources):
+    for k, ref in zip(order(len(sources)), sources):
         source_ref[block_at(partner(index, k, len(sources)), tile), :] = ref[...]
 
 
@@ -185,7 +189,7 @@
 
 def forward_other_kernel(dense_ref, *refs):
     sources, (other_ref, source_ref) = refs[:-2], refs[-2:]
-    gather_sources(sources, source_ref, row_index())
+    gather_sources(sources, source_ref, row_index(), half_first)
     half = other_ref.shape[0]
     other_ref[...] = dense_dot(dense_ref[half:, :], source_ref[...]).astype(BF16)
 
@@ -196,7 +200,7 @@
 
 def slot_forward_kernel(count_ref, row_ref, col_ref, tiles_ref, *refs):
     sources, (other_ref, own_ref, source_ref, acc_ref) = refs[:-4], refs[-4:]
-    gather_sources(sources, source_ref, row_index())
+    gather_sources(sources, source_ref, row_index(), half_first)
     slot_product((count_ref, row_ref, col_ref, tiles_ref), source_ref, acc_ref, False)
     half = own_ref.shape[0]
     own_ref[...] = acc_ref[:half, :].astype(BF16)
@@ -256,7 +260,7 @@
 
 
 def gather_kernel(after_ref, *refs):
-    gather_sources(refs[:-1], refs[-1], chip_index())
+    gather_sources(refs[:-1], refs[-1], chip_index(), far_first)
 
 
 def back_own_kernel(turned_ref, source_ref, out_ref):
@@ -382,7 +386,7 @@
         )
         slot_specs = [SMEM_SPEC] * 3 + [VMEM_SPEC]
 
-    sources = exchange([features] * n_row, "row", n_row)
+    sources = exchange([features] * n_row, "row", n_row, order=half_first)
     if is_dense:
         other, source = call(
             forward_other_kernel,

time: 45.1 us -> 45 us (level)
  starting transfers between devices: 22.4 us -> 23.3 us
  waiting for transfers between devices: 15.3 us -> 14.5 us
    ppermute x4, waiting for transfers between devices: 3.47 us -> 2.73 us  [total_over(): terms = [lax.ppermute(block, axis, pairs_of(step, size, cores)), block]]
    ppermute x12, starting transfers between devices: 16.4 us -> 17.1 us  [exchange(): lax.ppermute(blocks[k], axis, pairs)]
    ppermute x12, waiting for transfers between devices: 9.6 us -> 9.12 us  [exchange(): lax.ppermute(blocks[k], axis, pairs)]
  transfers between devices with their start and end apart: 20 -> 20, of which waited for: 12 -> 14; matrix products, arithmetic and copies ran while one was open for 0% -> 0% of each run, Pallas kernels for 9% -> 9%
where the time goes in v17:
time: 45 us; the launch traced here: 44.8 us
  starting transfers between devices  23.3 us (52%)
  waiting for transfers between devices  14.5 us (32%)
  Pallas kernels  5.53 us (12%)
  between operations  1.47 us (3%)
    ppermute x12, starting transfers between devices, exchange(): lax.ppermute(blocks[k], axis, pairs)  17.1 us
    ppermute x12, waiting for transfers between devices, exchange(): lax.ppermute(blocks[k], axis, pairs)  9.12 us
    ppermute x4, starting transfers between devices, total_over(): terms = [lax.ppermute(block, axis, pairs_of(step, size, cores)), block]  5.91 us
    ppermute x4, waiting for transfers between devices, total_over(): terms = [lax.ppermute(block, axis, pairs_of(step, size, cores)), block]  2.73 us
    ppermute x4, waiting for transfers between devices, swap_cores(): return lax.ppermute(block, 'col', [(i, i ^ 1) for i in range(size)])  2.66 us
    pallas_call x1, Pallas kernels, local(): call(dense_kernel, (like(row_nodes, col_nodes), like(1, hidden, F32)), [S...  1.45 us
  transfers between devices with their start and end apart: 20, of which 14 were waited for; matrix products, arithmetic and copies ran while one was open for 0% of the time, Pallas kernels for 9%

profile of v17, /device:TPU:0, one launch (start us, length us, event | category | flops | bytes accessed | tf_op | source)
XLA Modules:
  0.0 44.8 jit_solution(6216488275347479821)
XLA Ops:
  0.6 4.1 %collective-permute-start = (bf16[128,256]{1,0:T(8,128)(2,1)}, bf16[128,256]{1,0:T(8,128)(2,1)S(1)}, u32[]{:S(2)}, u32[]{:S(2)}) collective-permute-start(bf16[128,256]{1,0:T(8,128)(2,1)} %refs_3_.1), channel_id=1, source_target_pairs={{0,2},{1,3},{2,0},{3,1},{4,6},{5,7},{6,4},{7,5},{8,10},{9,11},{10,... | collective-permute-start | bytes 196616 | tf_op jit(solution)/shard_map/ppermute | solution.py:60
  4.7 1.3 %collective-permute-start.1 = (bf16[128,256]{1,0:T(8,128)(2,1)}, bf16[128,256]{1,0:T(8,128)(2,1)S(1)}, u32[]{:S(2)}, u32[]{:S(2)}) collective-permute-start(bf16[128,256]{1,0:T(8,128)(2,1)} %refs_3_.1), channel_id=1, source_target_pairs={{0,3},{1,2},{2,1},{3,0},{4,7},{5,6},{6,5},{7,4},{8,11},{9,10},{10,... | collective-permute-start | bytes 196616 | tf_op jit(solution)/shard_map/ppermute | solution.py:60
  7.0 1.5 %shard_map.111 = (bf16[1024,512]{1,0:T(8,128)(2,1)S(1)}, f32[1,256]{1,0:T(1,128)S(1)}) custom-call(s32[1,1]{1,0:T(1,128)S(6)} %copy.12.count_ref, s32[1,1,32]{2,1,0:T(1,128)} %row_hbm.1, s32[1,1,32]{2,1,0:T(1,128)} %col_hbm.1, bf16[1,1,32,128,128]{4,3,2,1,0:T(8,128)(2,1)} %tiles_hbm.1, f32[1,256]{1,0:T(1,128)} %bitcast.2), custom_call_target="tpu_custom_call" | custom-call | bytes 6291456 | tf_op jit(solution)/shard_map/pallas_call | solution.py:362
  8.7 2.5 %collective-permute-done.1.refs_1_ = bf16[128,256]{1,0:T(8,128)(2,1)S(1)} collective-permute-done((bf16[128,256]{1,0:T(8,128)(2,1)}, bf16[128,256]{1,0:T(8,128)(2,1)S(1)}, u32[]{:S(2)}, u32[]{:S(2)}) %collective-permute-start.1) | collective-permute-done | bytes 65568 | tf_op jit(solution)/shard_map/ppermute | solution.py:60
  11.3 0.3 shard_map.112
  11.7 0.3 shard_map.113.own_ref
  12.0 1.2 %collective-permute-done.3.other_ref = bf16[512,256]{1,0:T(8,128)(2,1)S(1)} collective-permute-done((bf16[512,256]{1,0:T(8,128)(2,1)S(1)}, bf16[512,256]{1,0:T(8,128)(2,1)S(1)}, u32[]{:S(2)}, u32[]{:S(2)}) %collective-permute-start.3) | collective-permute-done | bytes 262176 | tf_op jit(solution)/shard_map/ppermute | solution.py:65
  13.2 2.5 %collective-permute-start.4 = (bf16[128,256]{1,0:T(8,128)(2,1)S(1)}, bf16[128,256]{1,0:T(8,128)(2,1)S(1)}, u32[]{:S(2)}, u32[]{:S(2)}) collective-permute-start(bf16[128,256]{1,0:T(8,128)(2,1)S(1)} %shard_map.114.refs_0_), channel_id=1, source_target_pairs={{0,24},{4,28},{8,16},{12,20},{16,8},{20,12},{24,0},{28,4},{1,25},{... | collective-permute-start | bytes 196616 | tf_op jit(solution)/shard_map/ppermute | solution.py:60
  15.7 0.6 %collective-permute-start.5 = (bf16[128,256]{1,0:T(8,128)(2,1)S(1)}, bf16[128,256]{1,0:T(8,128)(2,1)S(1)}, u32[]{:S(2)}, u32[]{:S(2)}) collective-permute-start(bf16[128,256]{1,0:T(8,128)(2,1)S(1)} %shard_map.115.refs_0_), channel_id=1, source_target_pairs={{0,16},{4,20},{8,24},{12,28},{16,0},{20,4},{24,8},{28,12},{1,17},{... | collective-permute-start | bytes 196616 | tf_op jit(solution)/shard_map/ppermute | solution.py:60
  16.4 0.6 %collective-permute-start.6 = (bf16[128,256]{1,0:T(8,128)(2,1)S(1)}, bf16[128,256]{1,0:T(8,128)(2,1)S(1)}, u32[]{:S(2)}, u32[]{:S(2)}) collective-permute-start(bf16[128,256]{1,0:T(8,128)(2,1)S(1)} %shard_map.116.refs_0_), channel_id=1, source_target_pairs={{0,8},{4,12},{8,0},{12,4},{16,24},{20,28},{24,16},{28,20},{1,9},{5... | collective-permute-start | bytes 196616 | tf_op jit(solution)/shard_map/ppermute | solution.py:60
  17.0 1.5 %collective-permute-done.4.refs_0_ = bf16[128,256]{1,0:T(8,128)(2,1)S(1)} collective-permute-done((bf16[128,256]{1,0:T(8,128)(2,1)S(1)}, bf16[128,256]{1,0:T(8,128)(2,1)S(1)}, u32[]{:S(2)}, u32[]{:S(2)}) %collective-permute-start.4) | collective-permute-done | bytes 65568 | tf_op jit(solution)/shard_map/ppermute | solution.py:60
  18.5 1.6 %collective-permute-done.5.refs_1_ = bf16[128,256]{1,0:T(8,128)(2,1)S(1)} collective-permute-done((bf16[128,256]{1,0:T(8,128)(2,1)S(1)}, bf16[128,256]{1,0:T(8,128)(2,1)S(1)}, u32[]{:S(2)}, u32[]{:S(2)}) %collective-permute-start.5) | collective-permute-done | bytes 65568 | tf_op jit(solution)/shard_map/ppermute | solution.py:60
  20.1 0.6 %collective-permute-done.6.refs_2_ = bf16[128,256]{1,0:T(8,128)(2,1)S(1)} collective-permute-done((bf16[128,256]{1,0:T(8,128)(2,1)S(1)}, bf16[128,256]{1,0:T(8,128)(2,1)S(1)}, u32[]{:S(2)}, u32[]{:S(2)}) %collective-permute-start.6) | collective-permute-done | bytes 65568 | tf_op jit(solution)/shard_map/ppermute | solution.py:60
  21.5 1.0 %collective-permute-done.7.refs_0_ = bf16[144,256]{1,0:T(8,128)(2,1)S(1)} collective-permute-done((bf16[144,256]{1,0:T(8,128)(2,1)S(1)}, bf16[144,256]{1,0:T(8,128)(2,1)S(1)}, u32[]{:S(2)}, u32[]{:S(2)}) %collective-permute-start.7) | collective-permute-done | bytes 73760 | tf_op jit(solution)/shard_map/ppermute | solution.py:65
  22.5 1.0 %collective-permute-start.15 = (bf16[144,256]{1,0:T(8,128)(2,1)S(1)}, bf16[144,256]{1,0:T(8,128)(2,1)S(1)}, u32[]{:S(2)}, u32[]{:S(2)}) collective-permute-start(bf16[144,256]{1,0:T(8,128)(2,1)S(1)} %shard_map.123.after_ref.refs_1_), channel_id=1, source_target_pairs={{0,1},{1,0},{2,3},{3,2},{4,5},{5,4},{6,7},{7,6},{8,9},{9,8},{10,11... | collective-permute-start | bytes 221192 | tf_op jit(solution)/shard_map/ppermute | solution.py:75
  23.5 1.5 %collective-permute-start.8 = (bf16[128,256]{1,0:T(8,128)(2,1)S(1)}, bf16[128,256]{1,0:T(8,128)(2,1)S(1)}, u32[]{:S(2)}, u32[]{:S(2)}) collective-permute-start(bf16[128,256]{1,0:T(8,128)(2,1)S(1)} %get-tuple-element.26.grad_ref.refs_3_), channel_id=1, source_target_pairs={{0,24},{4,28},{8,16},{12,20},{16,8},{20,12},{24,0},{28,4},{1,25},{... | collective-permute-start | bytes 196616 | tf_op jit(solution)/shard_map/ppermute | solution.py:60
  25.0 0.5 %collective-permute-start.9 = (bf16[128,256]{1,0:T(8,128)(2,1)S(1)}, bf16[128,256]{1,0:T(8,128)(2,1)S(1)}, u32[]{:S(2)}, u32[]{:S(2)}) collective-permute-start(bf16[128,256]{1,0:T(8,128)(2,1)S(1)} %get-tuple-element.26.grad_ref.refs_3_), channel_id=1, source_target_pairs={{0,16},{4,20},{8,24},{12,28},{16,0},{20,4},{24,8},{28,12},{1,17},{... | collective-permute-start | bytes 196616 | tf_op jit(solution)/shard_map/ppermute | solution.py:60
  25.5 1.5 %collective-permute-start.10 = (bf16[128,256]{1,0:T(8,128)(2,1)S(1)}, bf16[128,256]{1,0:T(8,128)(2,1)S(1)}, u32[]{:S(2)}, u32[]{:S(2)}) collective-permute-start(bf16[128,256]{1,0:T(8,128)(2,1)S(1)} %get-tuple-element.26.grad_ref.refs_3_), channel_id=1, source_target_pairs={{0,8},{4,12},{8,0},{12,4},{16,24},{20,28},{24,16},{28,20},{1,9},{5... | collective-permute-start | bytes 196616 | tf_op jit(solution)/shard_map/ppermute | solution.py:60
  27.0 2.7 %collective-permute-start.16 = (bf16[144,256]{1,0:T(8,128)(2,1)S(1)}, bf16[144,256]{1,0:T(8,128)(2,1)S(1)}, u32[]{:S(2)}, u32[]{:S(2)}) collective-permute-start(bf16[144,256]{1,0:T(8,128)(2,1)S(1)} %shard_map.129.refs_1_), channel_id=1, source_target_pairs={{0,2},{1,3},{2,0},{3,1},{4,6},{5,7},{6,4},{7,5},{8,10},{9,11},{10,... | collective-permute-start | bytes 221192 | tf_op jit(solution)/shard_map/ppermute | solution.py:75
  29.9 0.3 shard_map.120.turned_ref
  30.3 0.3 shard_map.125.own_ref.refs_2_
  30.6 2.6 %collective-permute-done.16.refs_0_ = bf16[144,256]{1,0:T(8,128)(2,1)S(1)} collective-permute-done((bf16[144,256]{1,0:T(8,128)(2,1)S(1)}, bf16[144,256]{1,0:T(8,128)(2,1)S(1)}, u32[]{:S(2)}, u32[]{:S(2)}) %collective-permute-start.16) | collective-permute-done | bytes 73760 | tf_op jit(solution)/shard_map/ppermute | solution.py:75
  33.2 0.6 %collective-permute-start.17 = (bf16[144,256]{1,0:T(8,128)(2,1)S(1)}, bf16[144,256]{1,0:T(8,128)(2,1)S(1)}, u32[]{:S(2)}, u32[]{:S(2)}) collective-permute-start(bf16[144,256]{1,0:T(8,128)(2,1)S(1)} %shard_map.130.refs_1_), channel_id=1, source_target_pairs={{0,8},{4,12},{8,0},{12,4},{16,24},{20,28},{24,16},{28,20},{1,9},{5... | collective-permute-start | bytes 221192 | tf_op jit(solution)/shard_map/ppermute | solution.py:75
  33.8 0.3 shard_map.126
  34.1 3.3 %collective-permute-start.12 = (bf16[128,256]{1,0:T(8,128)(2,1)S(1)}, bf16[128,256]{1,0:T(8,128)(2,1)S(1)}, u32[]{:S(2)}, u32[]{:S(2)}) collective-permute-start(bf16[128,256]{1,0:T(8,128)(2,1)S(1)} %get-tuple-element.27), channel_id=1, source_target_pairs={{0,3},{1,2},{2,1},{3,0},{4,7},{5,6},{6,5},{7,4},{8,11},{9,10},{10,... | collective-permute-start | bytes 196616 | tf_op jit(solution)/shard_map/ppermute | solution.py:60
  37.6 1.6 %collective-permute-start.18 = (bf16[144,256]{1,0:T(8,128)(2,1)S(1)}, bf16[144,256]{1,0:T(8,128)(2,1)S(1)}, u32[]{:S(2)}, u32[]{:S(2)}) collective-permute-start(bf16[144,256]{1,0:T(8,128)(2,1)S(1)} %shard_map.131.refs_1_), channel_id=1, source_target_pairs={{0,16},{4,20},{8,24},{12,28},{16,0},{20,4},{24,8},{28,12},{1,17},{... | collective-permute-start | bytes 221192 | tf_op jit(solution)/shard_map/ppermute | solution.py:75
  39.2 1.0 %collective-permute-start.14 = (bf16[128,256]{1,0:T(8,128)(2,1)S(1)}, bf16[128,256]{1,0:T(8,128)(2,1)S(1)}, u32[]{:S(2)}, u32[]{:S(2)}) collective-permute-start(bf16[128,256]{1,0:T(8,128)(2,1)S(1)} %get-tuple-element.30), channel_id=1, source_target_pairs={{0,1},{1,0},{2,3},{3,2},{4,5},{5,4},{6,7},{7,6},{8,9},{9,8},{10,11... | collective-permute-start | bytes 196616 | tf_op jit(solution)/shard_map/ppermute | solution.py:60
  40.2 0.6 %shard_map.119 = bf16[128,256]{1,0:T(8,128)(2,1)} custom-call(bf16[128,256]{1,0:T(8,128)(2,1)S(1)} %get-tuple-element.24.in_ref), custom_call_target="tpu_custom_call" | custom-call | bytes 131072 | tf_op jit(solution)/shard_map/pallas_call | solution.py:448
  40.8 1.8 %collective-permute-done.13.refs_1_ = bf16[128,256]{1,0:T(8,128)(2,1)S(1)} collective-permute-done((bf16[128,256]{1,0:T(8,128)(2,1)S(1)}, bf16[128,256]{1,0:T(8,128)(2,1)S(1)}, u32[]{:S(2)}, u32[]{:S(2)}) %collective-permute-start.13) | collective-permute-done | bytes 65568 | tf_op jit(solution)/shard_map/ppermute | solution.py:60
  42.7 0.7 %collective-permute-done.14.last_ref = bf16[128,256]{1,0:T(8,128)(2,1)S(1)} collective-permute-done((bf16[128,256]{1,0:T(8,128)(2,1)S(1)}, bf16[128,256]{1,0:T(8,128)(2,1)S(1)}, u32[]{:S(2)}, u32[]{:S(2)}) %collective-permute-start.14) | collective-permute-done | bytes 65568 | tf_op jit(solution)/shard_map/ppermute | solution.py:60
  43.7 0.4 collective-permute-done.19.other_ref
  44.1 0.8 %shard_map.133 = (bf16[128,256]{1,0:T(8,128)(2,1)}, f32[256,256]{1,0:T(8,128)}, f32[1,256]{1,0:T(1,128)}) custom-call(bf16[128,256]{1,0:T(8,128)(2,1)S(1)} %shard_map.128.features_ref, f32[128,256]{1,0:T(8,128)S(1)} %get-tuple-element.31.own_ref, f32[128,256]{1,0:T(8,128)S(1)} %collective-permute-done.19.other_ref, f32[1,256]{1,0:T(1,128)S(1)} %get-tuple-element.32.bias_ref), custom_call_target="tpu_custom_call" | custom-call | bytes 524288 | tf_op jit(solution)/shard_map/pallas_call | solution.py:528
  (37 shorter events, 2.3 us)
Async XLA Ops:
  0.6 8.1 %collective-permute-start = (bf16[128,256]{1,0:T(8,128)(2,1)}, bf16[128,256]{1,0:T(8,128)(2,1)S(1)}, u32[]{:S(2)}, u32[]{:S(2)}) collective-permute-start(bf16[128,256]{1,0:T(8,128)(2,1)} %refs_3_.1), channel_id=1, source_target_pairs={{0,2},{1,3},{2,0},{3,1},{4,6},{5,7},{6,4},{7,5},{8,10},{9,11},{10,... | collective-permute-start | bytes 196616 | tf_op jit(solution)/shard_map/ppermute | solution.py:60
  4.7 6.4 %collective-permute-start.1 = (bf16[128,256]{1,0:T(8,128)(2,1)}, bf16[128,256]{1,0:T(8,128)(2,1)S(1)}, u32[]{:S(2)}, u32[]{:S(2)}) collective-permute-start(bf16[128,256]{1,0:T(8,128)(2,1)} %refs_3_.1), channel_id=1, source_target_pairs={{0,3},{1,2},{2,1},{3,0},{4,7},{5,6},{6,5},{7,4},{8,11},{9,10},{10,... | collective-permute-start | bytes 196616 | tf_op jit(solution)/shard_map/ppermute | solution.py:60
  6.1 5.2 %collective-permute-start.2 = (bf16[128,256]{1,0:T(8,128)(2,1)}, bf16[128,256]{1,0:T(8,128)(2,1)S(1)}, u32[]{:S(2)}, u32[]{:S(2)}) collective-permute-start(bf16[128,256]{1,0:T(8,128)(2,1)} %refs_3_.1), channel_id=1, source_target_pairs={{0,1},{1,0},{2,3},{3,2},{4,5},{5,4},{6,7},{7,6},{8,9},{9,8},{10,11... | collective-permute-start | bytes 196616 | tf_op jit(solution)/shard_map/ppermute | solution.py:60
  7.0 4.3 %copy-start.1 = (bf16[128,256]{1,0:T(8,128)(2,1)S(1)}, bf16[128,256]{1,0:T(8,128)(2,1)}, u32[]{:S(2)}) copy-start(bf16[128,256]{1,0:T(8,128)(2,1)} %refs_3_.1) | copy-start | bytes 196612
  11.6 1.6 %collective-permute-start.3 = (bf16[512,256]{1,0:T(8,128)(2,1)S(1)}, bf16[512,256]{1,0:T(8,128)(2,1)S(1)}, u32[]{:S(2)}, u32[]{:S(2)}) collective-permute-start(bf16[512,256]{1,0:T(8,128)(2,1)S(1)} %get-tuple-element.23), channel_id=1, source_target_pairs={{0,4},{4,0},{8,12},{12,8},{16,20},{20,16},{24,28},{28,24},{1,5},{5... | collective-permute-start | bytes 786440 | tf_op jit(solution)/shard_map/ppermute | solution.py:65
  13.2 5.2 %collective-permute-start.4 = (bf16[128,256]{1,0:T(8,128)(2,1)S(1)}, bf16[128,256]{1,0:T(8,128)(2,1)S(1)}, u32[]{:S(2)}, u32[]{:S(2)}) collective-permute-start(bf16[128,256]{1,0:T(8,128)(2,1)S(1)} %shard_map.114.refs_0_), channel_id=1, source_target_pairs={{0,24},{4,28},{8,16},{12,20},{16,8},{20,12},{24,0},{28,4},{1,25},{... | collective-permute-start | bytes 196616 | tf_op jit(solution)/shard_map/ppermute | solution.py:60
  15.7 4.3 %collective-permute-start.5 = (bf16[128,256]{1,0:T(8,128)(2,1)S(1)}, bf16[128,256]{1,0:T(8,128)(2,1)S(1)}, u32[]{:S(2)}, u32[]{:S(2)}) collective-permute-start(bf16[128,256]{1,0:T(8,128)(2,1)S(1)} %shard_map.115.refs_0_), channel_id=1, source_target_pairs={{0,16},{4,20},{8,24},{12,28},{16,0},{20,4},{24,8},{28,12},{1,17},{... | collective-permute-start | bytes 196616 | tf_op jit(solution)/shard_map/ppermute | solution.py:60
  16.3 4.4 %copy-start = (bf16[256,256]{1,0:T(8,128)(2,1)S(1)}, bf16[256,256]{1,0:T(8,128)(2,1)}, u32[]{:S(2)}) copy-start(bf16[256,256]{1,0:T(8,128)(2,1)} %weight_ref.3) | copy-start | bytes 393220
  16.4 4.3 %copy-start.2 = (bf16[128,256]{1,0:T(8,128)(2,1)S(1)}, bf16[128,256]{1,0:T(8,128)(2,1)}, u32[]{:S(2)}) copy-start(bf16[128,256]{1,0:T(8,128)(2,1)} %cot_ref.1) | copy-start | bytes 196612
  16.4 4.3 %collective-permute-start.6 = (bf16[128,256]{1,0:T(8,128)(2,1)S(1)}, bf16[128,256]{1,0:T(8,128)(2,1)S(1)}, u32[]{:S(2)}, u32[]{:S(2)}) collective-permute-start(bf16[128,256]{1,0:T(8,128)(2,1)S(1)} %shard_map.116.refs_0_), channel_id=1, source_target_pairs={{0,8},{4,12},{8,0},{12,4},{16,24},{20,28},{24,16},{28,20},{1,9},{5... | collective-permute-start | bytes 196616 | tf_op jit(solution)/shard_map/ppermute | solution.py:60
  21.2 1.3 %collective-permute-start.7 = (bf16[144,256]{1,0:T(8,128)(2,1)S(1)}, bf16[144,256]{1,0:T(8,128)(2,1)S(1)}, u32[]{:S(2)}, u32[]{:S(2)}) collective-permute-start(bf16[144,256]{1,0:T(8,128)(2,1)S(1)} %shard_map.121), channel_id=1, source_target_pairs={{0,4},{4,0},{8,12},{12,8},{16,20},{20,16},{24,28},{28,24},{1,5},{5... | collective-permute-start | bytes 221192 | tf_op jit(solution)/shard_map/ppermute | solution.py:65
  22.5 4.5 %collective-permute-start.15 = (bf16[144,256]{1,0:T(8,128)(2,1)S(1)}, bf16[144,256]{1,0:T(8,128)(2,1)S(1)}, u32[]{:S(2)}, u32[]{:S(2)}) collective-permute-start(bf16[144,256]{1,0:T(8,128)(2,1)S(1)} %shard_map.123.after_ref.refs_1_), channel_id=1, source_target_pairs={{0,1},{1,0},{2,3},{3,2},{4,5},{5,4},{6,7},{7,6},{8,9},{9,8},{10,11... | collective-permute-start | bytes 221192 | tf_op jit(solution)/shard_map/ppermute | solution.py:75
  23.5 6.2 %collective-permute-start.8 = (bf16[128,256]{1,0:T(8,128)(2,1)S(1)}, bf16[128,256]{1,0:T(8,128)(2,1)S(1)}, u32[]{:S(2)}, u32[]{:S(2)}) collective-permute-start(bf16[128,256]{1,0:T(8,128)(2,1)S(1)} %get-tuple-element.26.grad_ref.refs_3_), channel_id=1, source_target_pairs={{0,24},{4,28},{8,16},{12,20},{16,8},{20,12},{24,0},{28,4},{1,25},{... | collective-permute-start | bytes 196616 | tf_op jit(solution)/shard_map/ppermute | solution.py:60
  25.0 4.7 %collective-permute-start.9 = (bf16[128,256]{1,0:T(8,128)(2,1)S(1)}, bf16[128,256]{1,0:T(8,128)(2,1)S(1)}, u32[]{:S(2)}, u32[]{:S(2)}) collective-permute-start(bf16[128,256]{1,0:T(8,128)(2,1)S(1)} %get-tuple-element.26.grad_ref.refs_3_), channel_id=1, source_target_pairs={{0,16},{4,20},{8,24},{12,28},{16,0},{20,4},{24,8},{28,12},{1,17},{... | collective-permute-start | bytes 196616 | tf_op jit(solution)/shard_map/ppermute | solution.py:60
  25.5 4.3 %collective-permute-start.10 = (bf16[128,256]{1,0:T(8,128)(2,1)S(1)}, bf16[128,256]{1,0:T(8,128)(2,1)S(1)}, u32[]{:S(2)}, u32[]{:S(2)}) collective-permute-start(bf16[128,256]{1,0:T(8,128)(2,1)S(1)} %get-tuple-element.26.grad_ref.refs_3_), channel_id=1, source_target_pairs={{0,8},{4,12},{8,0},{12,4},{16,24},{20,28},{24,16},{28,20},{1,9},{5... | collective-permute-start | bytes 196616 | tf_op jit(solution)/shard_map/ppermute | solution.py:60
  27.0 6.1 %collective-permute-start.16 = (bf16[144,256]{1,0:T(8,128)(2,1)S(1)}, bf16[144,256]{1,0:T(8,128)(2,1)S(1)}, u32[]{:S(2)}, u32[]{:S(2)}) collective-permute-start(bf16[144,256]{1,0:T(8,128)(2,1)S(1)} %shard_map.129.refs_1_), channel_id=1, source_target_pairs={{0,2},{1,3},{2,0},{3,1},{4,6},{5,7},{6,4},{7,5},{8,10},{9,11},{10,... | collective-permute-start | bytes 221192 | tf_op jit(solution)/shard_map/ppermute | solution.py:75
  29.9 4.0 %collective-permute-start.11 = (bf16[512,256]{1,0:T(8,128)(2,1)S(1)}, bf16[512,256]{1,0:T(8,128)(2,1)S(1)}, u32[]{:S(2)}, u32[]{:S(2)}) collective-permute-start(bf16[512,256]{1,0:T(8,128)(2,1)S(1)} %shard_map.124.source_ref), channel_id=1, source_target_pairs={{0,4},{4,0},{8,12},{12,8},{16,20},{20,16},{24,28},{28,24},{1,5},{5... | collective-permute-start | bytes 786440 | tf_op jit(solution)/shard_map/ppermute | solution.py:65
  33.2 4.4 %collective-permute-start.17 = (bf16[144,256]{1,0:T(8,128)(2,1)S(1)}, bf16[144,256]{1,0:T(8,128)(2,1)S(1)}, u32[]{:S(2)}, u32[]{:S(2)}) collective-permute-start(bf16[144,256]{1,0:T(8,128)(2,1)S(1)} %shard_map.130.refs_1_), channel_id=1, source_target_pairs={{0,8},{4,12},{8,0},{12,4},{16,24},{20,28},{24,16},{28,20},{1,9},{5... | collective-permute-start | bytes 221192 | tf_op jit(solution)/shard_map/ppermute | solution.py:75
  34.1 6.7 %collective-permute-start.12 = (bf16[128,256]{1,0:T(8,128)(2,1)S(1)}, bf16[128,256]{1,0:T(8,128)(2,1)S(1)}, u32[]{:S(2)}, u32[]{:S(2)}) collective-permute-start(bf16[128,256]{1,0:T(8,128)(2,1)S(1)} %get-tuple-element.27), channel_id=1, source_target_pairs={{0,3},{1,2},{2,1},{3,0},{4,7},{5,6},{6,5},{7,4},{8,11},{9,10},{10,... | collective-permute-start | bytes 196616 | tf_op jit(solution)/shard_map/ppermute | solution.py:60
  37.4 5.2 %collective-permute-start.13 = (bf16[128,256]{1,0:T(8,128)(2,1)S(1)}, bf16[128,256]{1,0:T(8,128)(2,1)S(1)}, u32[]{:S(2)}, u32[]{:S(2)}) collective-permute-start(bf16[128,256]{1,0:T(8,128)(2,1)S(1)} %get-tuple-element.28), channel_id=1, source_target_pairs={{0,2},{1,3},{2,0},{3,1},{4,6},{5,7},{6,4},{7,5},{8,10},{9,11},{10,... | collective-permute-start | bytes 196616 | tf_op jit(solution)/shard_map/ppermute | solution.py:60
  37.6 5.0 %collective-permute-start.18 = (bf16[144,256]{1,0:T(8,128)(2,1)S(1)}, bf16[144,256]{1,0:T(8,128)(2,1)S(1)}, u32[]{:S(2)}, u32[]{:S(2)}) collective-permute-start(bf16[144,256]{1,0:T(8,128)(2,1)S(1)} %shard_map.131.refs_1_), channel_id=1, source_target_pairs={{0,16},{4,20},{8,24},{12,28},{16,0},{20,4},{24,8},{28,12},{1,17},{... | collective-permute-start | bytes 221192 | tf_op jit(solution)/shard_map/ppermute | solution.py:75
  39.2 4.3 %collective-permute-start.14 = (bf16[128,256]{1,0:T(8,128)(2,1)S(1)}, bf16[128,256]{1,0:T(8,128)(2,1)S(1)}, u32[]{:S(2)}, u32[]{:S(2)}) collective-permute-start(bf16[128,256]{1,0:T(8,128)(2,1)S(1)} %get-tuple-element.30), channel_id=1, source_target_pairs={{0,1},{1,0},{2,3},{3,2},{4,5},{5,4},{6,7},{7,6},{8,9},{9,8},{10,11... | collective-permute-start | bytes 196616 | tf_op jit(solution)/shard_map/ppermute | solution.py:60
  42.7 1.4 %collective-permute-start.19 = (f32[128,256]{1,0:T(8,128)S(1)}, f32[128,256]{1,0:T(8,128)S(1)}, u32[]{:S(2)}, u32[]{:S(2)}) collective-permute-start(f32[128,256]{1,0:T(8,128)S(1)} %get-tuple-element.31.own_ref), channel_id=1, source_target_pairs={{0,4},{4,0},{8,12},{12,8},{16,20},{20,16},{24,28},{28,24},{1,5},{5... | collective-permute-start | bytes 393224 | tf_op jit(solution)/shard_map/ppermute | solution.py:65

commit v18 on v17

--- a/solution.py
+++ b/solution.py
@@ -269,7 +269,7 @@
 
 def back_pieces_kernel(turned_ref, own_ref, source_ref, *outs):
     tile = outs[0].shape[0]
-    for k, out_ref in zip(far_first(len(outs)), outs):
+    for k, out_ref in zip(half_first(len(outs)), outs):
         rows = block_at(partner(row_index(), k, len(outs)), tile)
         rest = dense_dot(turned_ref[rows, source_ref.shape[0] :], source_ref[...])
         out_ref[...] = (own_ref[rows, :] + rest).astype(BF16)
@@ -282,7 +282,7 @@
     source_ref[half:, :] = other_ref[...]
     slot_product((count_ref, row_ref, col_ref, tiles_ref), source_ref, acc_ref, True)
     tile = outs[0].shape[0]
-    for k, out_ref in zip(far_first(len(outs)), outs):
+    for k, out_ref in zip(half_first(len(outs)), outs):
         rows = block_at(partner(row_index(), k, len(outs)), tile)
         out_ref[...] = acc_ref[rows, :].astype(BF16)
 
@@ -498,7 +498,8 @@
             slots * matrix // 2,
             row_nodes * hidden * 8,
         )(*slot_args, own_grads, other_grads)
-    backs = exchange(dict(zip(far_first(n_row), back_pieces)), "row", n_row)
+    by_partner = dict(zip(half_first(n_row), back_pieces))
+    backs = exchange(by_partner, "row", n_row, order=half_first)
     most = call(
         back_sum_kernel,
         like(tile, hidden, F32),

time: 45 us -> 44.7 us (level)
  Pallas kernels: 5.53 us -> 6.21 us
  waiting for transfers between devices: 14.5 us -> 14 us
    pallas_call x1, Pallas kernels: 1.45 us -> 2.13 us  [local(): call(dense_kernel, (like(row_nodes, col_nodes), like(1, hidden, F32)), [S...]
  transfers between devices with their start and end apart: 20 -> 20, of which waited for: 14 -> 14; matrix products, arithmetic and copies ran while one was open for 0% -> 0% of each run, Pallas kernels for 9% -> 10%
where the time goes in v18:
time: 44.7 us; the launch traced here: 44.6 us
  starting transfers between devices  22.9 us (51%)
  waiting for transfers between devices  14 us (31%)
  Pallas kernels  6.21 us (14%)
  between operations  1.47 us (3%)
    ppermute x12, starting transfers between devices, exchange(): lax.ppermute(blocks[k], axis, pairs)  16.7 us
    ppermute x12, waiting for transfers between devices, exchange(): lax.ppermute(blocks[k], axis, pairs)  8.96 us
    ppermute x4, starting transfers between devices, total_over(): terms = [lax.ppermute(block, axis, pairs_of(step, size, cores)), block]  5.91 us
    ppermute x4, waiting for transfers between devices, total_over(): terms = [lax.ppermute(block, axis, pairs_of(step, size, cores)), block]  2.66 us
    ppermute x4, waiting for transfers between devices, swap_cores(): return lax.ppermute(block, 'col', [(i, i ^ 1) for i in range(size)])  2.4 us
    pallas_call x1, Pallas kernels, local(): call(dense_kernel, (like(row_nodes, col_nodes), like(1, hidden, F32)), [S...  2.13 us
  transfers between devices with their start and end apart: 20, of which 14 were waited for; matrix products, arithmetic and copies ran while one was open for 0% of the time, Pallas kernels for 10%

profile of v18, /device:TPU:0, one launch (start us, length us, event | category | flops | bytes accessed | tf_op | source)
XLA Modules:
  0.0 44.6 jit_solution(9954535229315384958)
XLA Ops:
  0.6 4.1 %collective-permute-start = (bf16[128,256]{1,0:T(8,128)(2,1)}, bf16[128,256]{1,0:T(8,128)(2,1)S(1)}, u32[]{:S(2)}, u32[]{:S(2)}) collective-permute-start(bf16[128,256]{1,0:T(8,128)(2,1)} %refs_3_.1), channel_id=1, source_target_pairs={{0,2},{1,3},{2,0},{3,1},{4,6},{5,7},{6,4},{7,5},{8,10},{9,11},{10,... | collective-permute-start | bytes 196616 | tf_op jit(solution)/shard_map/ppermute | solution.py:60
  4.7 1.3 %collective-permute-start.1 = (bf16[128,256]{1,0:T(8,128)(2,1)}, bf16[128,256]{1,0:T(8,128)(2,1)S(1)}, u32[]{:S(2)}, u32[]{:S(2)}) collective-permute-start(bf16[128,256]{1,0:T(8,128)(2,1)} %refs_3_.1), channel_id=1, source_target_pairs={{0,3},{1,2},{2,1},{3,0},{4,7},{5,6},{6,5},{7,4},{8,11},{9,10},{10,... | collective-permute-start | bytes 196616 | tf_op jit(solution)/shard_map/ppermute | solution.py:60
  7.0 2.1 %shard_map.111 = (bf16[1024,512]{1,0:T(8,128)(2,1)S(1)}, f32[1,256]{1,0:T(1,128)S(1)}) custom-call(s32[1,1]{1,0:T(1,128)S(6)} %copy.12.count_ref, s32[1,1,32]{2,1,0:T(1,128)} %row_hbm.1, s32[1,1,32]{2,1,0:T(1,128)} %col_hbm.1, bf16[1,1,32,128,128]{4,3,2,1,0:T(8,128)(2,1)} %tiles_hbm.1, f32[1,256]{1,0:T(1,128)} %bitcast.2), custom_call_target="tpu_custom_call" | custom-call | bytes 6291456 | tf_op jit(solution)/shard_map/pallas_call | solution.py:362
  9.1 2.0 %collective-permute-done.1.refs_1_ = bf16[128,256]{1,0:T(8,128)(2,1)S(1)} collective-permute-done((bf16[128,256]{1,0:T(8,128)(2,1)}, bf16[128,256]{1,0:T(8,128)(2,1)S(1)}, u32[]{:S(2)}, u32[]{:S(2)}) %collective-permute-start.1) | collective-permute-done | bytes 65568 | tf_op jit(solution)/shard_map/ppermute | solution.py:60
  11.3 0.3 shard_map.112
  12.0 1.2 %collective-permute-done.3.other_ref = bf16[512,256]{1,0:T(8,128)(2,1)S(1)} collective-permute-done((bf16[512,256]{1,0:T(8,128)(2,1)S(1)}, bf16[512,256]{1,0:T(8,128)(2,1)S(1)}, u32[]{:S(2)}, u32[]{:S(2)}) %collective-permute-start.3) | collective-permute-done | bytes 262176 | tf_op jit(solution)/shard_map/ppermute | solution.py:65
  13.2 2.5 %collective-permute-start.4 = (bf16[128,256]{1,0:T(8,128)(2,1)S(1)}, bf16[128,256]{1,0:T(8,128)(2,1)S(1)}, u32[]{:S(2)}, u32[]{:S(2)}) collective-permute-start(bf16[128,256]{1,0:T(8,128)(2,1)S(1)} %shard_map.114.refs_0_), channel_id=1, source_target_pairs={{0,24},{4,28},{8,16},{12,20},{16,8},{20,12},{24,0},{28,4},{1,25},{... | collective-permute-start | bytes 196616 | tf_op jit(solution)/shard_map/ppermute | solution.py:60
  15.7 0.6 %collective-permute-start.5 = (bf16[128,256]{1,0:T(8,128)(2,1)S(1)}, bf16[128,256]{1,0:T(8,128)(2,1)S(1)}, u32[]{:S(2)}, u32[]{:S(2)}) collective-permute-start(bf16[128,256]{1,0:T(8,128)(2,1)S(1)} %shard_map.115.refs_0_), channel_id=1, source_target_pairs={{0,16},{4,20},{8,24},{12,28},{16,0},{20,4},{24,8},{28,12},{1,17},{... | collective-permute-start | bytes 196616 | tf_op jit(solution)/shard_map/ppermute | solution.py:60
  16.4 0.6 %collective-permute-start.6 = (bf16[128,256]{1,0:T(8,128)(2,1)S(1)}, bf16[128,256]{1,0:T(8,128)(2,1)S(1)}, u32[]{:S(2)}, u32[]{:S(2)}) collective-permute-start(bf16[128,256]{1,0:T(8,128)(2,1)S(1)} %shard_map.116.refs_0_), channel_id=1, source_target_pairs={{0,8},{4,12},{8,0},{12,4},{16,24},{20,28},{24,16},{28,20},{1,9},{5... | collective-permute-start | bytes 196616 | tf_op jit(solution)/shard_map/ppermute | solution.py:60
  17.0 1.5 %collective-permute-done.4.refs_0_ = bf16[128,256]{1,0:T(8,128)(2,1)S(1)} collective-permute-done((bf16[128,256]{1,0:T(8,128)(2,1)S(1)}, bf16[128,256]{1,0:T(8,128)(2,1)S(1)}, u32[]{:S(2)}, u32[]{:S(2)}) %collective-permute-start.4) | collective-permute-done | bytes 65568 | tf_op jit(solution)/shard_map/ppermute | solution.py:60
  18.5 1.6 %collective-permute-done.5.refs_1_ = bf16[128,256]{1,0:T(8,128)(2,1)S(1)} collective-permute-done((bf16[128,256]{1,0:T(8,128)(2,1)S(1)}, bf16[128,256]{1,0:T(8,128)(2,1)S(1)}, u32[]{:S(2)}, u32[]{:S(2)}) %collective-permute-start.5) | collective-permute-done | bytes 65568 | tf_op jit(solution)/shard_map/ppermute | solution.py:60
  20.1 0.6 %collective-permute-done.6.refs_2_ = bf16[128,256]{1,0:T(8,128)(2,1)S(1)} collective-permute-done((bf16[128,256]{1,0:T(8,128)(2,1)S(1)}, bf16[128,256]{1,0:T(8,128)(2,1)S(1)}, u32[]{:S(2)}, u32[]{:S(2)}) %collective-permute-start.6) | collective-permute-done | bytes 65568 | tf_op jit(solution)/shard_map/ppermute | solution.py:60
  21.5 1.0 %collective-permute-done.7.refs_0_ = bf16[144,256]{1,0:T(8,128)(2,1)S(1)} collective-permute-done((bf16[144,256]{1,0:T(8,128)(2,1)S(1)}, bf16[144,256]{1,0:T(8,128)(2,1)S(1)}, u32[]{:S(2)}, u32[]{:S(2)}) %collective-permute-start.7) | collective-permute-done | bytes 73760 | tf_op jit(solution)/shard_map/ppermute | solution.py:65
  22.5 1.0 %collective-permute-start.15 = (bf16[144,256]{1,0:T(8,128)(2,1)S(1)}, bf16[144,256]{1,0:T(8,128)(2,1)S(1)}, u32[]{:S(2)}, u32[]{:S(2)}) collective-permute-start(bf16[144,256]{1,0:T(8,128)(2,1)S(1)} %shard_map.123.after_ref.refs_1_), channel_id=1, source_target_pairs={{0,1},{1,0},{2,3},{3,2},{4,5},{5,4},{6,7},{7,6},{8,9},{9,8},{10,11... | collective-permute-start | bytes 221192 | tf_op jit(solution)/shard_map/ppermute | solution.py:75
  23.5 1.5 %collective-permute-start.8 = (bf16[128,256]{1,0:T(8,128)(2,1)S(1)}, bf16[128,256]{1,0:T(8,128)(2,1)S(1)}, u32[]{:S(2)}, u32[]{:S(2)}) collective-permute-start(bf16[128,256]{1,0:T(8,128)(2,1)S(1)} %get-tuple-element.26.grad_ref.refs_3_), channel_id=1, source_target_pairs={{0,24},{4,28},{8,16},{12,20},{16,8},{20,12},{24,0},{28,4},{1,25},{... | collective-permute-start | bytes 196616 | tf_op jit(solution)/shard_map/ppermute | solution.py:60
  25.0 0.5 %collective-permute-start.9 = (bf16[128,256]{1,0:T(8,128)(2,1)S(1)}, bf16[128,256]{1,0:T(8,128)(2,1)S(1)}, u32[]{:S(2)}, u32[]{:S(2)}) collective-permute-start(bf16[128,256]{1,0:T(8,128)(2,1)S(1)} %get-tuple-element.26.grad_ref.refs_3_), channel_id=1, source_target_pairs={{0,16},{4,20},{8,24},{12,28},{16,0},{20,4},{24,8},{28,12},{1,17},{... | collective-permute-start | bytes 196616 | tf_op jit(solution)/shard_map/ppermute | solution.py:60
  25.5 1.5 %collective-permute-start.10 = (bf16[128,256]{1,0:T(8,128)(2,1)S(1)}, bf16[128,256]{1,0:T(8,128)(2,1)S(1)}, u32[]{:S(2)}, u32[]{:S(2)}) collective-permute-start(bf16[128,256]{1,0:T(8,128)(2,1)S(1)} %get-tuple-element.26.grad_ref.refs_3_), channel_id=1, source_target_pairs={{0,8},{4,12},{8,0},{12,4},{16,24},{20,28},{24,16},{28,20},{1,9},{5... | collective-permute-start | bytes 196616 | tf_op jit(solution)/shard_map/ppermute | solution.py:60
  27.0 2.7 %collective-permute-start.16 = (bf16[144,256]{1,0:T(8,128)(2,1)S(1)}, bf16[144,256]{1,0:T(8,128)(2,1)S(1)}, u32[]{:S(2)}, u32[]{:S(2)}) collective-permute-start(bf16[144,256]{1,0:T(8,128)(2,1)S(1)} %shard_map.129.refs_1_), channel_id=1, source_target_pairs={{0,2},{1,3},{2,0},{3,1},{4,6},{5,7},{6,4},{7,5},{8,10},{9,11},{10,... | collective-permute-start | bytes 221192 | tf_op jit(solution)/shard_map/ppermute | solution.py:75
  29.9 0.3 shard_map.120.turned_ref
  30.3 0.3 shard_map.125.own_ref.refs_2_
  30.6 2.6 %collective-permute-done.16.refs_0_ = bf16[144,256]{1,0:T(8,128)(2,1)S(1)} collective-permute-done((bf16[144,256]{1,0:T(8,128)(2,1)S(1)}, bf16[144,256]{1,0:T(8,128)(2,1)S(1)}, u32[]{:S(2)}, u32[]{:S(2)}) %collective-permute-start.16) | collective-permute-done | bytes 73760 | tf_op jit(solution)/shard_map/ppermute | solution.py:75
  33.2 0.6 %collective-permute-start.17 = (bf16[144,256]{1,0:T(8,128)(2,1)S(1)}, bf16[144,256]{1,0:T(8,128)(2,1)S(1)}, u32[]{:S(2)}, u32[]{:S(2)}) collective-permute-start(bf16[144,256]{1,0:T(8,128)(2,1)S(1)} %shard_map.130.refs_1_), channel_id=1, source_target_pairs={{0,8},{4,12},{8,0},{12,4},{16,24},{20,28},{24,16},{28,20},{1,9},{5... | collective-permute-start | bytes 221192 | tf_op jit(solution)/shard_map/ppermute | solution.py:75
  33.8 0.3 shard_map.126
  34.1 2.0 %collective-permute-start.12 = (bf16[128,256]{1,0:T(8,128)(2,1)S(1)}, bf16[128,256]{1,0:T(8,128)(2,1)S(1)}, u32[]{:S(2)}, u32[]{:S(2)}) collective-permute-start(bf16[128,256]{1,0:T(8,128)(2,1)S(1)} %get-tuple-element.27), channel_id=1, source_target_pairs={{0,2},{1,3},{2,0},{3,1},{4,6},{5,7},{6,4},{7,5},{8,10},{9,11},{10,... | collective-permute-start | bytes 196616 | tf_op jit(solution)/shard_map/ppermute | solution.py:60
  36.1 1.4 %collective-permute-start.13 = (bf16[128,256]{1,0:T(8,128)(2,1)S(1)}, bf16[128,256]{1,0:T(8,128)(2,1)S(1)}, u32[]{:S(2)}, u32[]{:S(2)}) collective-permute-start(bf16[128,256]{1,0:T(8,128)(2,1)S(1)} %get-tuple-element.28), channel_id=1, source_target_pairs={{0,3},{1,2},{2,1},{3,0},{4,7},{5,6},{6,5},{7,4},{8,11},{9,10},{10,... | collective-permute-start | bytes 196616 | tf_op jit(solution)/shard_map/ppermute | solution.py:60
  37.6 1.6 %collective-permute-start.18 = (bf16[144,256]{1,0:T(8,128)(2,1)S(1)}, bf16[144,256]{1,0:T(8,128)(2,1)S(1)}, u32[]{:S(2)}, u32[]{:S(2)}) collective-permute-start(bf16[144,256]{1,0:T(8,128)(2,1)S(1)} %shard_map.131.refs_1_), channel_id=1, source_target_pairs={{0,16},{4,20},{8,24},{12,28},{16,0},{20,4},{24,8},{28,12},{1,17},{... | collective-permute-start | bytes 221192 | tf_op jit(solution)/shard_map/ppermute | solution.py:75
  39.2 0.4 collective-permute-start.14
  39.7 0.6 %shard_map.119 = bf16[128,256]{1,0:T(8,128)(2,1)} custom-call(bf16[128,256]{1,0:T(8,128)(2,1)S(1)} %get-tuple-element.24.in_ref), custom_call_target="tpu_custom_call" | custom-call | bytes 131072 | tf_op jit(solution)/shard_map/pallas_call | solution.py:448
  40.3 0.8 %collective-permute-done.12.refs_0_ = bf16[128,256]{1,0:T(8,128)(2,1)S(1)} collective-permute-done((bf16[128,256]{1,0:T(8,128)(2,1)S(1)}, bf16[128,256]{1,0:T(8,128)(2,1)S(1)}, u32[]{:S(2)}, u32[]{:S(2)}) %collective-permute-start.12) | collective-permute-done | bytes 65568 | tf_op jit(solution)/shard_map/ppermute | solution.py:60
  41.1 1.2 %collective-permute-done.13.refs_1_ = bf16[128,256]{1,0:T(8,128)(2,1)S(1)} collective-permute-done((bf16[128,256]{1,0:T(8,128)(2,1)S(1)}, bf16[128,256]{1,0:T(8,128)(2,1)S(1)}, u32[]{:S(2)}, u32[]{:S(2)}) %collective-permute-start.13) | collective-permute-done | bytes 65568 | tf_op jit(solution)/shard_map/ppermute | solution.py:60
  42.5 1.0 %collective-permute-done.14.last_ref = bf16[128,256]{1,0:T(8,128)(2,1)S(1)} collective-permute-done((bf16[128,256]{1,0:T(8,128)(2,1)S(1)}, bf16[128,256]{1,0:T(8,128)(2,1)S(1)}, u32[]{:S(2)}, u32[]{:S(2)}) %collective-permute-start.14) | collective-permute-done | bytes 65568 | tf_op jit(solution)/shard_map/ppermute | solution.py:60
  43.8 0.8 %shard_map.133 = (bf16[128,256]{1,0:T(8,128)(2,1)}, f32[256,256]{1,0:T(8,128)}, f32[1,256]{1,0:T(1,128)}) custom-call(bf16[128,256]{1,0:T(8,128)(2,1)S(1)} %shard_map.128.features_ref, f32[128,256]{1,0:T(8,128)S(1)} %get-tuple-element.31.own_ref, f32[128,256]{1,0:T(8,128)S(1)} %collective-permute-done.19.other_ref, f32[1,256]{1,0:T(1,128)S(1)} %get-tuple-element.32.bias_ref), custom_call_target="tpu_custom_call" | custom-call | bytes 524288 | tf_op jit(solution)/shard_map/pallas_call | solution.py:529
  (37 shorter events, 2.3 us)
Async XLA Ops:
  0.6 8.5 %collective-permute-start = (bf16[128,256]{1,0:T(8,128)(2,1)}, bf16[128,256]{1,0:T(8,128)(2,1)S(1)}, u32[]{:S(2)}, u32[]{:S(2)}) collective-permute-start(bf16[128,256]{1,0:T(8,128)(2,1)} %refs_3_.1), channel_id=1, source_target_pairs={{0,2},{1,3},{2,0},{3,1},{4,6},{5,7},{6,4},{7,5},{8,10},{9,11},{10,... | collective-permute-start | bytes 196616 | tf_op jit(solution)/shard_map/ppermute | solution.py:60
  4.7 6.4 %collective-permute-start.1 = (bf16[128,256]{1,0:T(8,128)(2,1)}, bf16[128,256]{1,0:T(8,128)(2,1)S(1)}, u32[]{:S(2)}, u32[]{:S(2)}) collective-permute-start(bf16[128,256]{1,0:T(8,128)(2,1)} %refs_3_.1), channel_id=1, source_target_pairs={{0,3},{1,2},{2,1},{3,0},{4,7},{5,6},{6,5},{7,4},{8,11},{9,10},{10,... | collective-permute-start | bytes 196616 | tf_op jit(solution)/shard_map/ppermute | solution.py:60
  6.1 5.2 %collective-permute-start.2 = (bf16[128,256]{1,0:T(8,128)(2,1)}, bf16[128,256]{1,0:T(8,128)(2,1)S(1)}, u32[]{:S(2)}, u32[]{:S(2)}) collective-permute-start(bf16[128,256]{1,0:T(8,128)(2,1)} %refs_3_.1), channel_id=1, source_target_pairs={{0,1},{1,0},{2,3},{3,2},{4,5},{5,4},{6,7},{7,6},{8,9},{9,8},{10,11... | collective-permute-start | bytes 196616 | tf_op jit(solution)/shard_map/ppermute | solution.py:60
  7.0 4.3 %copy-start.1 = (bf16[128,256]{1,0:T(8,128)(2,1)S(1)}, bf16[128,256]{1,0:T(8,128)(2,1)}, u32[]{:S(2)}) copy-start(bf16[128,256]{1,0:T(8,128)(2,1)} %refs_3_.1) | copy-start | bytes 196612
  11.6 1.6 %collective-permute-start.3 = (bf16[512,256]{1,0:T(8,128)(2,1)S(1)}, bf16[512,256]{1,0:T(8,128)(2,1)S(1)}, u32[]{:S(2)}, u32[]{:S(2)}) collective-permute-start(bf16[512,256]{1,0:T(8,128)(2,1)S(1)} %get-tuple-element.23), channel_id=1, source_target_pairs={{0,4},{4,0},{8,12},{12,8},{16,20},{20,16},{24,28},{28,24},{1,5},{5... | collective-permute-start | bytes 786440 | tf_op jit(solution)/shard_map/ppermute | solution.py:65
  13.2 5.2 %collective-permute-start.4 = (bf16[128,256]{1,0:T(8,128)(2,1)S(1)}, bf16[128,256]{1,0:T(8,128)(2,1)S(1)}, u32[]{:S(2)}, u32[]{:S(2)}) collective-permute-start(bf16[128,256]{1,0:T(8,128)(2,1)S(1)} %shard_map.114.refs_0_), channel_id=1, source_target_pairs={{0,24},{4,28},{8,16},{12,20},{16,8},{20,12},{24,0},{28,4},{1,25},{... | collective-permute-start | bytes 196616 | tf_op jit(solution)/shard_map/ppermute | solution.py:60
  15.7 4.3 %collective-permute-start.5 = (bf16[128,256]{1,0:T(8,128)(2,1)S(1)}, bf16[128,256]{1,0:T(8,128)(2,1)S(1)}, u32[]{:S(2)}, u32[]{:S(2)}) collective-permute-start(bf16[128,256]{1,0:T(8,128)(2,1)S(1)} %shard_map.115.refs_0_), channel_id=1, source_target_pairs={{0,16},{4,20},{8,24},{12,28},{16,0},{20,4},{24,8},{28,12},{1,17},{... | collective-permute-start | bytes 196616 | tf_op jit(solution)/shard_map/ppermute | solution.py:60
  16.3 4.4 %copy-start = (bf16[256,256]{1,0:T(8,128)(2,1)S(1)}, bf16[256,256]{1,0:T(8,128)(2,1)}, u32[]{:S(2)}) copy-start(bf16[256,256]{1,0:T(8,128)(2,1)} %weight_ref.3) | copy-start | bytes 393220
  16.4 4.3 %copy-start.2 = (bf16[128,256]{1,0:T(8,128)(2,1)S(1)}, bf16[128,256]{1,0:T(8,128)(2,1)}, u32[]{:S(2)}) copy-start(bf16[128,256]{1,0:T(8,128)(2,1)} %cot_ref.1) | copy-start | bytes 196612
  16.4 4.3 %collective-permute-start.6 = (bf16[128,256]{1,0:T(8,128)(2,1)S(1)}, bf16[128,256]{1,0:T(8,128)(2,1)S(1)}, u32[]{:S(2)}, u32[]{:S(2)}) collective-permute-start(bf16[128,256]{1,0:T(8,128)(2,1)S(1)} %shard_map.116.refs_0_), channel_id=1, source_target_pairs={{0,8},{4,12},{8,0},{12,4},{16,24},{20,28},{24,16},{28,20},{1,9},{5... | collective-permute-start | bytes 196616 | tf_op jit(solution)/shard_map/ppermute | solution.py:60
  21.2 1.3 %collective-permute-start.7 = (bf16[144,256]{1,0:T(8,128)(2,1)S(1)}, bf16[144,256]{1,0:T(8,128)(2,1)S(1)}, u32[]{:S(2)}, u32[]{:S(2)}) collective-permute-start(bf16[144,256]{1,0:T(8,128)(2,1)S(1)} %shard_map.121), channel_id=1, source_target_pairs={{0,4},{4,0},{8,12},{12,8},{16,20},{20,16},{24,28},{28,24},{1,5},{5... | collective-permute-start | bytes 221192 | tf_op jit(solution)/shard_map/ppermute | solution.py:65
  22.5 4.5 %collective-permute-start.15 = (bf16[144,256]{1,0:T(8,128)(2,1)S(1)}, bf16[144,256]{1,0:T(8,128)(2,1)S(1)}, u32[]{:S(2)}, u32[]{:S(2)}) collective-permute-start(bf16[144,256]{1,0:T(8,128)(2,1)S(1)} %shard_map.123.after_ref.refs_1_), channel_id=1, source_target_pairs={{0,1},{1,0},{2,3},{3,2},{4,5},{5,4},{6,7},{7,6},{8,9},{9,8},{10,11... | collective-permute-start | bytes 221192 | tf_op jit(solution)/shard_map/ppermute | solution.py:75
  23.5 6.2 %collective-permute-start.8 = (bf16[128,256]{1,0:T(8,128)(2,1)S(1)}, bf16[128,256]{1,0:T(8,128)(2,1)S(1)}, u32[]{:S(2)}, u32[]{:S(2)}) collective-permute-start(bf16[128,256]{1,0:T(8,128)(2,1)S(1)} %get-tuple-element.26.grad_ref.refs_3_), channel_id=1, source_target_pairs={{0,24},{4,28},{8,16},{12,20},{16,8},{20,12},{24,0},{28,4},{1,25},{... | collective-permute-start | bytes 196616 | tf_op jit(solution)/shard_map/ppermute | solution.py:60
  25.0 4.7 %collective-permute-start.9 = (bf16[128,256]{1,0:T(8,128)(2,1)S(1)}, bf16[128,256]{1,0:T(8,128)(2,1)S(1)}, u32[]{:S(2)}, u32[]{:S(2)}) collective-permute-start(bf16[128,256]{1,0:T(8,128)(2,1)S(1)} %get-tuple-element.26.grad_ref.refs_3_), channel_id=1, source_target_pairs={{0,16},{4,20},{8,24},{12,28},{16,0},{20,4},{24,8},{28,12},{1,17},{... | collective-permute-start | bytes 196616 | tf_op jit(solution)/shard_map/ppermute | solution.py:60
  25.5 4.3 %collective-permute-start.10 = (bf16[128,256]{1,0:T(8,128)(2,1)S(1)}, bf16[128,256]{1,0:T(8,128)(2,1)S(1)}, u32[]{:S(2)}, u32[]{:S(2)}) collective-permute-start(bf16[128,256]{1,0:T(8,128)(2,1)S(1)} %get-tuple-element.26.grad_ref.refs_3_), channel_id=1, source_target_pairs={{0,8},{4,12},{8,0},{12,4},{16,24},{20,28},{24,16},{28,20},{1,9},{5... | collective-permute-start | bytes 196616 | tf_op jit(solution)/shard_map/ppermute | solution.py:60
  27.0 6.1 %collective-permute-start.16 = (bf16[144,256]{1,0:T(8,128)(2,1)S(1)}, bf16[144,256]{1,0:T(8,128)(2,1)S(1)}, u32[]{:S(2)}, u32[]{:S(2)}) collective-permute-start(bf16[144,256]{1,0:T(8,128)(2,1)S(1)} %shard_map.129.refs_1_), channel_id=1, source_target_pairs={{0,2},{1,3},{2,0},{3,1},{4,6},{5,7},{6,4},{7,5},{8,10},{9,11},{10,... | collective-permute-start | bytes 221192 | tf_op jit(solution)/shard_map/ppermute | solution.py:75
  29.9 4.0 %collective-permute-start.11 = (bf16[512,256]{1,0:T(8,128)(2,1)S(1)}, bf16[512,256]{1,0:T(8,128)(2,1)S(1)}, u32[]{:S(2)}, u32[]{:S(2)}) collective-permute-start(bf16[512,256]{1,0:T(8,128)(2,1)S(1)} %shard_map.124.source_ref), channel_id=1, source_target_pairs={{0,4},{4,0},{8,12},{12,8},{16,20},{20,16},{24,28},{28,24},{1,5},{5... | collective-permute-start | bytes 786440 | tf_op jit(solution)/shard_map/ppermute | solution.py:65
  33.2 4.4 %collective-permute-start.17 = (bf16[144,256]{1,0:T(8,128)(2,1)S(1)}, bf16[144,256]{1,0:T(8,128)(2,1)S(1)}, u32[]{:S(2)}, u32[]{:S(2)}) collective-permute-start(bf16[144,256]{1,0:T(8,128)(2,1)S(1)} %shard_map.130.refs_1_), channel_id=1, source_target_pairs={{0,8},{4,12},{8,0},{12,4},{16,24},{20,28},{24,16},{28,20},{1,9},{5... | collective-permute-start | bytes 221192 | tf_op jit(solution)/shard_map/ppermute | solution.py:75
  34.1 7.0 %collective-permute-start.12 = (bf16[128,256]{1,0:T(8,128)(2,1)S(1)}, bf16[128,256]{1,0:T(8,128)(2,1)S(1)}, u32[]{:S(2)}, u32[]{:S(2)}) collective-permute-start(bf16[128,256]{1,0:T(8,128)(2,1)S(1)} %get-tuple-element.27), channel_id=1, source_target_pairs={{0,2},{1,3},{2,0},{3,1},{4,6},{5,7},{6,4},{7,5},{8,10},{9,11},{10,... | collective-permute-start | bytes 196616 | tf_op jit(solution)/shard_map/ppermute | solution.py:60
  36.1 6.2 %collective-permute-start.13 = (bf16[128,256]{1,0:T(8,128)(2,1)S(1)}, bf16[128,256]{1,0:T(8,128)(2,1)S(1)}, u32[]{:S(2)}, u32[]{:S(2)}) collective-permute-start(bf16[128,256]{1,0:T(8,128)(2,1)S(1)} %get-tuple-element.28), channel_id=1, source_target_pairs={{0,3},{1,2},{2,1},{3,0},{4,7},{5,6},{6,5},{7,4},{8,11},{9,10},{10,... | collective-permute-start | bytes 196616 | tf_op jit(solution)/shard_map/ppermute | solution.py:60
  37.6 4.7 %collective-permute-start.18 = (bf16[144,256]{1,0:T(8,128)(2,1)S(1)}, bf16[144,256]{1,0:T(8,128)(2,1)S(1)}, u32[]{:S(2)}, u32[]{:S(2)}) collective-permute-start(bf16[144,256]{1,0:T(8,128)(2,1)S(1)} %shard_map.131.refs_1_), channel_id=1, source_target_pairs={{0,16},{4,20},{8,24},{12,28},{16,0},{20,4},{24,8},{28,12},{1,17},{... | collective-permute-start | bytes 221192 | tf_op jit(solution)/shard_map/ppermute | solution.py:75
  39.2 4.3 %collective-permute-start.14 = (bf16[128,256]{1,0:T(8,128)(2,1)S(1)}, bf16[128,256]{1,0:T(8,128)(2,1)S(1)}, u32[]{:S(2)}, u32[]{:S(2)}) collective-permute-start(bf16[128,256]{1,0:T(8,128)(2,1)S(1)} %get-tuple-element.30), channel_id=1, source_target_pairs={{0,1},{1,0},{2,3},{3,2},{4,5},{5,4},{6,7},{7,6},{8,9},{9,8},{10,11... | collective-permute-start | bytes 196616 | tf_op jit(solution)/shard_map/ppermute | solution.py:60
  42.4 1.4 %collective-permute-start.19 = (f32[128,256]{1,0:T(8,128)S(1)}, f32[128,256]{1,0:T(8,128)S(1)}, u32[]{:S(2)}, u32[]{:S(2)}) collective-permute-start(f32[128,256]{1,0:T(8,128)S(1)} %get-tuple-element.31.own_ref), channel_id=1, source_target_pairs={{0,4},{4,0},{8,12},{12,8},{16,20},{20,16},{24,28},{28,24},{1,5},{5... | collective-permute-start | bytes 393224 | tf_op jit(solution)/shard_map/ppermute | solution.py:65

commit v19 on v16

--- a/solution.py
+++ b/solution.py
@@ -40,8 +40,8 @@
     return (k - index) % count
 
 
-def far_first(count):
-    return list(range(count - 1, -1, -1))
+def order(count):
+    return [count // 2] + [k for k in range(count - 1, -1, -1) if k != count // 2]
 
 
 def pairs_of(k, size, cores):
@@ -50,7 +50,7 @@
 
 def exchange(blocks, axis, size, cores=1):
     received = []
-    for k in far_first(size // cores):
+    for k in order(size // cores):
         pairs = pairs_of(k, size, cores)
         moves = any(i != j for i, j in pairs)
         received.append(lax.ppermute(blocks[k], axis, pairs) if moves else blocks[k])
@@ -90,7 +90,7 @@
 
 
 def summed(refs):
-    by_partner = dict(zip(far_first(len(refs)), refs))
+    by_partner = dict(zip(order(len(refs)), refs))
     values = [by_partner[k][...].astype(F32) for k in sorted(by_partner)]
     while len(values) > 1:
         values = [sum(values[i + 1 : i + 2], values[i]) for i in range(0, len(values), 2)]
@@ -158,7 +158,7 @@
 
 def gather_sources(sources, source_ref, index):
     tile = sources[0].shape[0]
-    for k, ref in zip(far_first(len(sources)), sources):
+    for k, ref in zip(order(len(sources)), sources):
         source_ref[block_at(partner(index, k, len(sources)), tile), :] = ref[...]
 
 
@@ -265,7 +265,7 @@
 
 def back_pieces_kernel(turned_ref, own_ref, source_ref, *outs):
     tile = outs[0].shape[0]
-    for k, out_ref in zip(far_first(len(outs)), outs):
+    for k, out_ref in zip(order(len(outs)), outs):
         rows = block_at(partner(row_index(), k, len(outs)), tile)
         rest = dense_dot(turned_ref[rows, source_ref.shape[0] :], source_ref[...])
         out_ref[...] = (own_ref[rows, :] + rest).astype(BF16)
@@ -278,7 +278,7 @@
     source_ref[half:, :] = other_ref[...]
     slot_product((count_ref, row_ref, col_ref, tiles_ref), source_ref, acc_ref, True)
     tile = outs[0].shape[0]
-    for k, out_ref in zip(far_first(len(outs)), outs):
+    for k, out_ref in zip(order(len(outs)), outs):
         rows = block_at(partner(row_index(), k, len(outs)), tile)
         out_ref[...] = acc_ref[rows, :].astype(BF16)
 
@@ -317,7 +317,7 @@
 
 def in_turn(count, make):
     made, before = {}, []
-    for k in far_first(count):
+    for k in order(count):
         made[k] = make(k, before)
         before = [made[k]]
     return made
@@ -494,7 +494,8 @@
             slots * matrix // 2,
             row_nodes * hidden * 8,
         )(*slot_args, own_grads, other_grads)
-    backs = exchange(dict(zip(far_first(n_row), back_pieces)), "row", n_row)
+    by_partner = dict(zip(order(n_row), back_pieces))
+    backs = exchange(by_partner, "row", n_row)
     most = call(
         back_sum_kernel,
         like(tile, hidden, F32),

time: 45.1 us -> 45.3 us (level)
  waiting for transfers between devices: 15.3 us -> 14.2 us
  starting transfers between devices: 22.4 us -> 23.2 us
  Pallas kernels: 5.74 us -> 6.2 us
    ppermute x4, waiting for transfers between devices: 3.47 us -> 2 us  [total_over(): terms = [lax.ppermute(block, axis, pairs_of(step, size, cores)), block]]
    ppermute x4, starting transfers between devices: 5.62 us -> 6.22 us  [total_over(): terms = [lax.ppermute(block, axis, pairs_of(step, size, cores)), block]]
    pallas_call x1, Pallas kernels: 1.64 us -> 2.13 us  [local(): call(dense_kernel, (like(row_nodes, col_nodes), like(1, hidden, F32)), [S...]
    ppermute x4, waiting for transfers between devices: 2.27 us -> 2.75 us  [swap_cores(): return lax.ppermute(block, 'col', [(i, i ^ 1) for i in range(size)])]
  transfers between devices with their start and end apart: 20 -> 20, of which waited for: 12 -> 14; matrix products, arithmetic and copies ran while one was open for 0% -> 0% of each run, Pallas kernels for 9% -> 10%
where the time goes in v19:
time: 45.3 us; the launch traced here: 45.1 us
  starting transfers between devices  23.2 us (51%)
  waiting for transfers between devices  14.2 us (31%)
  Pallas kernels  6.2 us (14%)
  between operations  1.47 us (3%)
    ppermute x12, starting transfers between devices, exchange(): lax.ppermute(blocks[k], axis, pairs)  16.7 us
    ppermute x12, waiting for transfers between devices, exchange(): lax.ppermute(blocks[k], axis, pairs)  9.48 us
    ppermute x4, starting transfers between devices, total_over(): terms = [lax.ppermute(block, axis, pairs_of(step, size, cores)), block]  6.22 us
    ppermute x4, waiting for transfers between devices, swap_cores(): return lax.ppermute(block, 'col', [(i, i ^ 1) for i in range(size)])  2.75 us
    pallas_call x1, Pallas kernels, local(): call(dense_kernel, (like(row_nodes, col_nodes), like(1, hidden, F32)), [S...  2.13 us
    ppermute x4, waiting for transfers between devices, total_over(): terms = [lax.ppermute(block, axis, pairs_of(step, size, cores)), block]  2 us
  transfers between devices with their start and end apart: 20, of which 14 were waited for; matrix products, arithmetic and copies ran while one was open for 0% of the time, Pallas kernels for 10%

profile of v19, /device:TPU:0, one launch (start us, length us, event | category | flops | bytes accessed | tf_op | source)
XLA Modules:
  0.0 45.1 jit_solution(7949343750829245026)
XLA Ops:
  0.6 4.1 %collective-permute-start = (bf16[128,256]{1,0:T(8,128)(2,1)}, bf16[128,256]{1,0:T(8,128)(2,1)S(1)}, u32[]{:S(2)}, u32[]{:S(2)}) collective-permute-start(bf16[128,256]{1,0:T(8,128)(2,1)} %refs_3_.1), channel_id=1, source_target_pairs={{0,2},{1,3},{2,0},{3,1},{4,6},{5,7},{6,4},{7,5},{8,10},{9,11},{10,... | collective-permute-start | bytes 196616 | tf_op jit(solution)/shard_map/ppermute | solution.py:56
  4.7 1.3 %collective-permute-start.1 = (bf16[128,256]{1,0:T(8,128)(2,1)}, bf16[128,256]{1,0:T(8,128)(2,1)S(1)}, u32[]{:S(2)}, u32[]{:S(2)}) collective-permute-start(bf16[128,256]{1,0:T(8,128)(2,1)} %refs_3_.1), channel_id=1, source_target_pairs={{0,3},{1,2},{2,1},{3,0},{4,7},{5,6},{6,5},{7,4},{8,11},{9,10},{10,... | collective-permute-start | bytes 196616 | tf_op jit(solution)/shard_map/ppermute | solution.py:56
  7.0 2.1 %shard_map.111 = (bf16[1024,512]{1,0:T(8,128)(2,1)S(1)}, f32[1,256]{1,0:T(1,128)S(1)}) custom-call(s32[1,1]{1,0:T(1,128)S(6)} %copy.12.count_ref, s32[1,1,32]{2,1,0:T(1,128)} %row_hbm.1, s32[1,1,32]{2,1,0:T(1,128)} %col_hbm.1, bf16[1,1,32,128,128]{4,3,2,1,0:T(8,128)(2,1)} %tiles_hbm.1, f32[1,256]{1,0:T(1,128)} %bitcast.2), custom_call_target="tpu_custom_call" | custom-call | bytes 6291456 | tf_op jit(solution)/shard_map/pallas_call | solution.py:358
  9.1 2.0 %collective-permute-done.1.refs_1_ = bf16[128,256]{1,0:T(8,128)(2,1)S(1)} collective-permute-done((bf16[128,256]{1,0:T(8,128)(2,1)}, bf16[128,256]{1,0:T(8,128)(2,1)S(1)}, u32[]{:S(2)}, u32[]{:S(2)}) %collective-permute-start.1) | collective-permute-done | bytes 65568 | tf_op jit(solution)/shard_map/ppermute | solution.py:56
  11.3 0.3 shard_map.112
  12.0 1.2 %collective-permute-done.3.other_ref = bf16[512,256]{1,0:T(8,128)(2,1)S(1)} collective-permute-done((bf16[512,256]{1,0:T(8,128)(2,1)S(1)}, bf16[512,256]{1,0:T(8,128)(2,1)S(1)}, u32[]{:S(2)}, u32[]{:S(2)}) %collective-permute-start.3) | collective-permute-done | bytes 262176 | tf_op jit(solution)/shard_map/ppermute | solution.py:61
  13.2 1.6 %collective-permute-start.4 = (bf16[128,256]{1,0:T(8,128)(2,1)S(1)}, bf16[128,256]{1,0:T(8,128)(2,1)S(1)}, u32[]{:S(2)}, u32[]{:S(2)}) collective-permute-start(bf16[128,256]{1,0:T(8,128)(2,1)S(1)} %shard_map.114.refs_0_), channel_id=1, source_target_pairs={{0,16},{4,20},{8,24},{12,28},{16,0},{20,4},{24,8},{28,12},{1,17},{... | collective-permute-start | bytes 196616 | tf_op jit(solution)/shard_map/ppermute | solution.py:56
  14.8 1.5 %collective-permute-start.5 = (bf16[128,256]{1,0:T(8,128)(2,1)S(1)}, bf16[128,256]{1,0:T(8,128)(2,1)S(1)}, u32[]{:S(2)}, u32[]{:S(2)}) collective-permute-start(bf16[128,256]{1,0:T(8,128)(2,1)S(1)} %shard_map.115.refs_0_), channel_id=1, source_target_pairs={{0,24},{4,28},{8,16},{12,20},{16,8},{20,12},{24,0},{28,4},{1,25},{... | collective-permute-start | bytes 196616 | tf_op jit(solution)/shard_map/ppermute | solution.py:56
  16.4 0.6 %collective-permute-start.6 = (bf16[128,256]{1,0:T(8,128)(2,1)S(1)}, bf16[128,256]{1,0:T(8,128)(2,1)S(1)}, u32[]{:S(2)}, u32[]{:S(2)}) collective-permute-start(bf16[128,256]{1,0:T(8,128)(2,1)S(1)} %shard_map.116.refs_0_), channel_id=1, source_target_pairs={{0,8},{4,12},{8,0},{12,4},{16,24},{20,28},{24,16},{28,20},{1,9},{5... | collective-permute-start | bytes 196616 | tf_op jit(solution)/shard_map/ppermute | solution.py:56
  17.0 0.6 %collective-permute-done.4.refs_0_ = bf16[128,256]{1,0:T(8,128)(2,1)S(1)} collective-permute-done((bf16[128,256]{1,0:T(8,128)(2,1)S(1)}, bf16[128,256]{1,0:T(8,128)(2,1)S(1)}, u32[]{:S(2)}, u32[]{:S(2)}) %collective-permute-start.4) | collective-permute-done | bytes 65568 | tf_op jit(solution)/shard_map/ppermute | solution.py:56
  17.5 3.0 %collective-permute-done.5.refs_1_ = bf16[128,256]{1,0:T(8,128)(2,1)S(1)} collective-permute-done((bf16[128,256]{1,0:T(8,128)(2,1)S(1)}, bf16[128,256]{1,0:T(8,128)(2,1)S(1)}, u32[]{:S(2)}, u32[]{:S(2)}) %collective-permute-start.5) | collective-permute-done | bytes 65568 | tf_op jit(solution)/shard_map/ppermute | solution.py:56
  21.5 1.0 %collective-permute-done.7.refs_0_ = bf16[144,256]{1,0:T(8,128)(2,1)S(1)} collective-permute-done((bf16[144,256]{1,0:T(8,128)(2,1)S(1)}, bf16[144,256]{1,0:T(8,128)(2,1)S(1)}, u32[]{:S(2)}, u32[]{:S(2)}) %collective-permute-start.7) | collective-permute-done | bytes 73760 | tf_op jit(solution)/shard_map/ppermute | solution.py:61
  22.5 1.0 %collective-permute-start.15 = (bf16[144,256]{1,0:T(8,128)(2,1)S(1)}, bf16[144,256]{1,0:T(8,128)(2,1)S(1)}, u32[]{:S(2)}, u32[]{:S(2)}) collective-permute-start(bf16[144,256]{1,0:T(8,128)(2,1)S(1)} %shard_map.123.after_ref.refs_1_), channel_id=1, source_target_pairs={{0,1},{1,0},{2,3},{3,2},{4,5},{5,4},{6,7},{7,6},{8,9},{9,8},{10,11... | collective-permute-start | bytes 221192 | tf_op jit(solution)/shard_map/ppermute | solution.py:71
  23.5 1.5 %collective-permute-start.8 = (bf16[128,256]{1,0:T(8,128)(2,1)S(1)}, bf16[128,256]{1,0:T(8,128)(2,1)S(1)}, u32[]{:S(2)}, u32[]{:S(2)}) collective-permute-start(bf16[128,256]{1,0:T(8,128)(2,1)S(1)} %get-tuple-element.26.grad_ref.refs_3_), channel_id=1, source_target_pairs={{0,16},{4,20},{8,24},{12,28},{16,0},{20,4},{24,8},{28,12},{1,17},{... | collective-permute-start | bytes 196616 | tf_op jit(solution)/shard_map/ppermute | solution.py:56
  25.0 1.1 %collective-permute-start.9 = (bf16[128,256]{1,0:T(8,128)(2,1)S(1)}, bf16[128,256]{1,0:T(8,128)(2,1)S(1)}, u32[]{:S(2)}, u32[]{:S(2)}) collective-permute-start(bf16[128,256]{1,0:T(8,128)(2,1)S(1)} %get-tuple-element.26.grad_ref.refs_3_), channel_id=1, source_target_pairs={{0,24},{4,28},{8,16},{12,20},{16,8},{20,12},{24,0},{28,4},{1,25},{... | collective-permute-start | bytes 196616 | tf_op jit(solution)/shard_map/ppermute | solution.py:56
  26.1 0.9 %collective-permute-start.10 = (bf16[128,256]{1,0:T(8,128)(2,1)S(1)}, bf16[128,256]{1,0:T(8,128)(2,1)S(1)}, u32[]{:S(2)}, u32[]{:S(2)}) collective-permute-start(bf16[128,256]{1,0:T(8,128)(2,1)S(1)} %get-tuple-element.26.grad_ref.refs_3_), channel_id=1, source_target_pairs={{0,8},{4,12},{8,0},{12,4},{16,24},{20,28},{24,16},{28,20},{1,9},{5... | collective-permute-start | bytes 196616 | tf_op jit(solution)/shard_map/ppermute | solution.py:56
  27.0 2.7 %collective-permute-start.16 = (bf16[144,256]{1,0:T(8,128)(2,1)S(1)}, bf16[144,256]{1,0:T(8,128)(2,1)S(1)}, u32[]{:S(2)}, u32[]{:S(2)}) collective-permute-start(bf16[144,256]{1,0:T(8,128)(2,1)S(1)} %shard_map.129.refs_1_), channel_id=1, source_target_pairs={{0,2},{1,3},{2,0},{3,1},{4,6},{5,7},{6,4},{7,5},{8,10},{9,11},{10,... | collective-permute-start | bytes 221192 | tf_op jit(solution)/shard_map/ppermute | solution.py:71
  29.7 0.5 %collective-permute-done.9.refs_1_ = bf16[128,256]{1,0:T(8,128)(2,1)S(1)} collective-permute-done((bf16[128,256]{1,0:T(8,128)(2,1)S(1)}, bf16[128,256]{1,0:T(8,128)(2,1)S(1)}, u32[]{:S(2)}, u32[]{:S(2)}) %collective-permute-start.9) | collective-permute-done | bytes 65568 | tf_op jit(solution)/shard_map/ppermute | solution.py:56
  30.5 0.3 shard_map.120.turned_ref
  31.2 2.0 %collective-permute-done.16.refs_0_ = bf16[144,256]{1,0:T(8,128)(2,1)S(1)} collective-permute-done((bf16[144,256]{1,0:T(8,128)(2,1)S(1)}, bf16[144,256]{1,0:T(8,128)(2,1)S(1)}, u32[]{:S(2)}, u32[]{:S(2)}) %collective-permute-start.16) | collective-permute-done | bytes 73760 | tf_op jit(solution)/shard_map/ppermute | solution.py:71
  33.2 1.2 %collective-permute-start.17 = (bf16[144,256]{1,0:T(8,128)(2,1)S(1)}, bf16[144,256]{1,0:T(8,128)(2,1)S(1)}, u32[]{:S(2)}, u32[]{:S(2)}) collective-permute-start(bf16[144,256]{1,0:T(8,128)(2,1)S(1)} %shard_map.130.refs_1_), channel_id=1, source_target_pairs={{0,8},{4,12},{8,0},{12,4},{16,24},{20,28},{24,16},{28,20},{1,9},{5... | collective-permute-start | bytes 221192 | tf_op jit(solution)/shard_map/ppermute | solution.py:71
  34.4 0.3 shard_map.126
  34.7 2.0 %collective-permute-start.12 = (bf16[128,256]{1,0:T(8,128)(2,1)S(1)}, bf16[128,256]{1,0:T(8,128)(2,1)S(1)}, u32[]{:S(2)}, u32[]{:S(2)}) collective-permute-start(bf16[128,256]{1,0:T(8,128)(2,1)S(1)} %get-tuple-element.27), channel_id=1, source_target_pairs={{0,2},{1,3},{2,0},{3,1},{4,6},{5,7},{6,4},{7,5},{8,10},{9,11},{10,... | collective-permute-start | bytes 196616 | tf_op jit(solution)/shard_map/ppermute | solution.py:56
  36.7 1.4 %collective-permute-start.13 = (bf16[128,256]{1,0:T(8,128)(2,1)S(1)}, bf16[128,256]{1,0:T(8,128)(2,1)S(1)}, u32[]{:S(2)}, u32[]{:S(2)}) collective-permute-start(bf16[128,256]{1,0:T(8,128)(2,1)S(1)} %get-tuple-element.28), channel_id=1, source_target_pairs={{0,3},{1,2},{2,1},{3,0},{4,7},{5,6},{6,5},{7,4},{8,11},{9,10},{10,... | collective-permute-start | bytes 196616 | tf_op jit(solution)/shard_map/ppermute | solution.py:56
  38.1 1.3 %collective-permute-start.18 = (bf16[144,256]{1,0:T(8,128)(2,1)S(1)}, bf16[144,256]{1,0:T(8,128)(2,1)S(1)}, u32[]{:S(2)}, u32[]{:S(2)}) collective-permute-start(bf16[144,256]{1,0:T(8,128)(2,1)S(1)} %shard_map.131.refs_1_), channel_id=1, source_target_pairs={{0,16},{4,20},{8,24},{12,28},{16,0},{20,4},{24,8},{28,12},{1,17},{... | collective-permute-start | bytes 221192 | tf_op jit(solution)/shard_map/ppermute | solution.py:71
  39.4 0.5 %collective-permute-start.14 = (bf16[128,256]{1,0:T(8,128)(2,1)S(1)}, bf16[128,256]{1,0:T(8,128)(2,1)S(1)}, u32[]{:S(2)}, u32[]{:S(2)}) collective-permute-start(bf16[128,256]{1,0:T(8,128)(2,1)S(1)} %get-tuple-element.30), channel_id=1, source_target_pairs={{0,1},{1,0},{2,3},{3,2},{4,5},{5,4},{6,7},{7,6},{8,9},{9,8},{10,11... | collective-permute-start | bytes 196616 | tf_op jit(solution)/shard_map/ppermute | solution.py:56
  39.9 0.6 %shard_map.119 = bf16[128,256]{1,0:T(8,128)(2,1)} custom-call(bf16[128,256]{1,0:T(8,128)(2,1)S(1)} %get-tuple-element.24.in_ref), custom_call_target="tpu_custom_call" | custom-call | bytes 131072 | tf_op jit(solution)/shard_map/pallas_call | solution.py:444
  40.6 0.8 %collective-permute-done.12.refs_0_ = bf16[128,256]{1,0:T(8,128)(2,1)S(1)} collective-permute-done((bf16[128,256]{1,0:T(8,128)(2,1)S(1)}, bf16[128,256]{1,0:T(8,128)(2,1)S(1)}, u32[]{:S(2)}, u32[]{:S(2)}) %collective-permute-start.12) | collective-permute-done | bytes 65568 | tf_op jit(solution)/shard_map/ppermute | solution.py:56
  41.4 1.5 %collective-permute-done.13.refs_1_ = bf16[128,256]{1,0:T(8,128)(2,1)S(1)} collective-permute-done((bf16[128,256]{1,0:T(8,128)(2,1)S(1)}, bf16[128,256]{1,0:T(8,128)(2,1)S(1)}, u32[]{:S(2)}, u32[]{:S(2)}) %collective-permute-start.13) | collective-permute-done | bytes 65568 | tf_op jit(solution)/shard_map/ppermute | solution.py:56
  43.0 0.7 %collective-permute-done.14.last_ref = bf16[128,256]{1,0:T(8,128)(2,1)S(1)} collective-permute-done((bf16[128,256]{1,0:T(8,128)(2,1)S(1)}, bf16[128,256]{1,0:T(8,128)(2,1)S(1)}, u32[]{:S(2)}, u32[]{:S(2)}) %collective-permute-start.14) | collective-permute-done | bytes 65568 | tf_op jit(solution)/shard_map/ppermute | solution.py:56
  43.9 0.5 %collective-permute-done.19.other_ref = f32[128,256]{1,0:T(8,128)S(1)} collective-permute-done((f32[128,256]{1,0:T(8,128)S(1)}, f32[128,256]{1,0:T(8,128)S(1)}, u32[]{:S(2)}, u32[]{:S(2)}) %collective-permute-start.19) | collective-permute-done | bytes 131104 | tf_op jit(solution)/shard_map/ppermute | solution.py:61
  44.4 0.8 %shard_map.133 = (bf16[128,256]{1,0:T(8,128)(2,1)}, f32[256,256]{1,0:T(8,128)}, f32[1,256]{1,0:T(1,128)}) custom-call(bf16[128,256]{1,0:T(8,128)(2,1)S(1)} %shard_map.128.features_ref, f32[128,256]{1,0:T(8,128)S(1)} %get-tuple-element.31.own_ref, f32[128,256]{1,0:T(8,128)S(1)} %collective-permute-done.19.other_ref, f32[1,256]{1,0:T(1,128)S(1)} %get-tuple-element.32.bias_ref), custom_call_target="tpu_custom_call" | custom-call | bytes 524288 | tf_op jit(solution)/shard_map/pallas_call | solution.py:525
  (37 shorter events, 2.7 us)
Async XLA Ops:
  0.6 8.5 %collective-permute-start = (bf16[128,256]{1,0:T(8,128)(2,1)}, bf16[128,256]{1,0:T(8,128)(2,1)S(1)}, u32[]{:S(2)}, u32[]{:S(2)}) collective-permute-start(bf16[128,256]{1,0:T(8,128)(2,1)} %refs_3_.1), channel_id=1, source_target_pairs={{0,2},{1,3},{2,0},{3,1},{4,6},{5,7},{6,4},{7,5},{8,10},{9,11},{10,... | collective-permute-start | bytes 196616 | tf_op jit(solution)/shard_map/ppermute | solution.py:56
  4.7 6.4 %collective-permute-start.1 = (bf16[128,256]{1,0:T(8,128)(2,1)}, bf16[128,256]{1,0:T(8,128)(2,1)S(1)}, u32[]{:S(2)}, u32[]{:S(2)}) collective-permute-start(bf16[128,256]{1,0:T(8,128)(2,1)} %refs_3_.1), channel_id=1, source_target_pairs={{0,3},{1,2},{2,1},{3,0},{4,7},{5,6},{6,5},{7,4},{8,11},{9,10},{10,... | collective-permute-start | bytes 196616 | tf_op jit(solution)/shard_map/ppermute | solution.py:56
  6.1 5.2 %collective-permute-start.2 = (bf16[128,256]{1,0:T(8,128)(2,1)}, bf16[128,256]{1,0:T(8,128)(2,1)S(1)}, u32[]{:S(2)}, u32[]{:S(2)}) collective-permute-start(bf16[128,256]{1,0:T(8,128)(2,1)} %refs_3_.1), channel_id=1, source_target_pairs={{0,1},{1,0},{2,3},{3,2},{4,5},{5,4},{6,7},{7,6},{8,9},{9,8},{10,11... | collective-permute-start | bytes 196616 | tf_op jit(solution)/shard_map/ppermute | solution.py:56
  7.0 4.3 %copy-start.1 = (bf16[128,256]{1,0:T(8,128)(2,1)S(1)}, bf16[128,256]{1,0:T(8,128)(2,1)}, u32[]{:S(2)}) copy-start(bf16[128,256]{1,0:T(8,128)(2,1)} %refs_3_.1) | copy-start | bytes 196612
  11.6 1.6 %collective-permute-start.3 = (bf16[512,256]{1,0:T(8,128)(2,1)S(1)}, bf16[512,256]{1,0:T(8,128)(2,1)S(1)}, u32[]{:S(2)}, u32[]{:S(2)}) collective-permute-start(bf16[512,256]{1,0:T(8,128)(2,1)S(1)} %get-tuple-element.23), channel_id=1, source_target_pairs={{0,4},{4,0},{8,12},{12,8},{16,20},{20,16},{24,28},{28,24},{1,5},{5... | collective-permute-start | bytes 786440 | tf_op jit(solution)/shard_map/ppermute | solution.py:61
  13.2 4.3 %collective-permute-start.4 = (bf16[128,256]{1,0:T(8,128)(2,1)S(1)}, bf16[128,256]{1,0:T(8,128)(2,1)S(1)}, u32[]{:S(2)}, u32[]{:S(2)}) collective-permute-start(bf16[128,256]{1,0:T(8,128)(2,1)S(1)} %shard_map.114.refs_0_), channel_id=1, source_target_pairs={{0,16},{4,20},{8,24},{12,28},{16,0},{20,4},{24,8},{28,12},{1,17},{... | collective-permute-start | bytes 196616 | tf_op jit(solution)/shard_map/ppermute | solution.py:56
  14.8 5.7 %collective-permute-start.5 = (bf16[128,256]{1,0:T(8,128)(2,1)S(1)}, bf16[128,256]{1,0:T(8,128)(2,1)S(1)}, u32[]{:S(2)}, u32[]{:S(2)}) collective-permute-start(bf16[128,256]{1,0:T(8,128)(2,1)S(1)} %shard_map.115.refs_0_), channel_id=1, source_target_pairs={{0,24},{4,28},{8,16},{12,20},{16,8},{20,12},{24,0},{28,4},{1,25},{... | collective-permute-start | bytes 196616 | tf_op jit(solution)/shard_map/ppermute | solution.py:56
  16.3 4.4 %copy-start = (bf16[256,256]{1,0:T(8,128)(2,1)S(1)}, bf16[256,256]{1,0:T(8,128)(2,1)}, u32[]{:S(2)}) copy-start(bf16[256,256]{1,0:T(8,128)(2,1)} %weight_ref.3) | copy-start | bytes 393220
  16.4 4.3 %copy-start.2 = (bf16[128,256]{1,0:T(8,128)(2,1)S(1)}, bf16[128,256]{1,0:T(8,128)(2,1)}, u32[]{:S(2)}) copy-start(bf16[128,256]{1,0:T(8,128)(2,1)} %cot_ref.1) | copy-start | bytes 196612
  16.4 4.3 %collective-permute-start.6 = (bf16[128,256]{1,0:T(8,128)(2,1)S(1)}, bf16[128,256]{1,0:T(8,128)(2,1)S(1)}, u32[]{:S(2)}, u32[]{:S(2)}) collective-permute-start(bf16[128,256]{1,0:T(8,128)(2,1)S(1)} %shard_map.116.refs_0_), channel_id=1, source_target_pairs={{0,8},{4,12},{8,0},{12,4},{16,24},{20,28},{24,16},{28,20},{1,9},{5... | collective-permute-start | bytes 196616 | tf_op jit(solution)/shard_map/ppermute | solution.py:56
  21.2 1.3 %collective-permute-start.7 = (bf16[144,256]{1,0:T(8,128)(2,1)S(1)}, bf16[144,256]{1,0:T(8,128)(2,1)S(1)}, u32[]{:S(2)}, u32[]{:S(2)}) collective-permute-start(bf16[144,256]{1,0:T(8,128)(2,1)S(1)} %shard_map.121), channel_id=1, source_target_pairs={{0,4},{4,0},{8,12},{12,8},{16,20},{20,16},{24,28},{28,24},{1,5},{5... | collective-permute-start | bytes 221192 | tf_op jit(solution)/shard_map/ppermute | solution.py:61
  22.5 4.5 %collective-permute-start.15 = (bf16[144,256]{1,0:T(8,128)(2,1)S(1)}, bf16[144,256]{1,0:T(8,128)(2,1)S(1)}, u32[]{:S(2)}, u32[]{:S(2)}) collective-permute-start(bf16[144,256]{1,0:T(8,128)(2,1)S(1)} %shard_map.123.after_ref.refs_1_), channel_id=1, source_target_pairs={{0,1},{1,0},{2,3},{3,2},{4,5},{5,4},{6,7},{7,6},{8,9},{9,8},{10,11... | collective-permute-start | bytes 221192 | tf_op jit(solution)/shard_map/ppermute | solution.py:71
  23.5 6.2 %collective-permute-start.8 = (bf16[128,256]{1,0:T(8,128)(2,1)S(1)}, bf16[128,256]{1,0:T(8,128)(2,1)S(1)}, u32[]{:S(2)}, u32[]{:S(2)}) collective-permute-start(bf16[128,256]{1,0:T(8,128)(2,1)S(1)} %get-tuple-element.26.grad_ref.refs_3_), channel_id=1, source_target_pairs={{0,16},{4,20},{8,24},{12,28},{16,0},{20,4},{24,8},{28,12},{1,17},{... | collective-permute-start | bytes 196616 | tf_op jit(solution)/shard_map/ppermute | solution.py:56
  25.0 5.2 %collective-permute-start.9 = (bf16[128,256]{1,0:T(8,128)(2,1)S(1)}, bf16[128,256]{1,0:T(8,128)(2,1)S(1)}, u32[]{:S(2)}, u32[]{:S(2)}) collective-permute-start(bf16[128,256]{1,0:T(8,128)(2,1)S(1)} %get-tuple-element.26.grad_ref.refs_3_), channel_id=1, source_target_pairs={{0,24},{4,28},{8,16},{12,20},{16,8},{20,12},{24,0},{28,4},{1,25},{... | collective-permute-start | bytes 196616 | tf_op jit(solution)/shard_map/ppermute | solution.py:56
  26.1 4.3 %collective-permute-start.10 = (bf16[128,256]{1,0:T(8,128)(2,1)S(1)}, bf16[128,256]{1,0:T(8,128)(2,1)S(1)}, u32[]{:S(2)}, u32[]{:S(2)}) collective-permute-start(bf16[128,256]{1,0:T(8,128)(2,1)S(1)} %get-tuple-element.26.grad_ref.refs_3_), channel_id=1, source_target_pairs={{0,8},{4,12},{8,0},{12,4},{16,24},{20,28},{24,16},{28,20},{1,9},{5... | collective-permute-start | bytes 196616 | tf_op jit(solution)/shard_map/ppermute | solution.py:56
  27.0 6.1 %collective-permute-start.16 = (bf16[144,256]{1,0:T(8,128)(2,1)S(1)}, bf16[144,256]{1,0:T(8,128)(2,1)S(1)}, u32[]{:S(2)}, u32[]{:S(2)}) collective-permute-start(bf16[144,256]{1,0:T(8,128)(2,1)S(1)} %shard_map.129.refs_1_), channel_id=1, source_target_pairs={{0,2},{1,3},{2,0},{3,1},{4,6},{5,7},{6,4},{7,5},{8,10},{9,11},{10,... | collective-permute-start | bytes 221192 | tf_op jit(solution)/shard_map/ppermute | solution.py:71
  30.4 4.0 %collective-permute-start.11 = (bf16[512,256]{1,0:T(8,128)(2,1)S(1)}, bf16[512,256]{1,0:T(8,128)(2,1)S(1)}, u32[]{:S(2)}, u32[]{:S(2)}) collective-permute-start(bf16[512,256]{1,0:T(8,128)(2,1)S(1)} %shard_map.124.source_ref), channel_id=1, source_target_pairs={{0,4},{4,0},{8,12},{12,8},{16,20},{20,16},{24,28},{28,24},{1,5},{5... | collective-permute-start | bytes 786440 | tf_op jit(solution)/shard_map/ppermute | solution.py:61
  33.2 4.9 %collective-permute-start.17 = (bf16[144,256]{1,0:T(8,128)(2,1)S(1)}, bf16[144,256]{1,0:T(8,128)(2,1)S(1)}, u32[]{:S(2)}, u32[]{:S(2)}) collective-permute-start(bf16[144,256]{1,0:T(8,128)(2,1)S(1)} %shard_map.130.refs_1_), channel_id=1, source_target_pairs={{0,8},{4,12},{8,0},{12,4},{16,24},{20,28},{24,16},{28,20},{1,9},{5... | collective-permute-start | bytes 221192 | tf_op jit(solution)/shard_map/ppermute | solution.py:71
  34.7 6.7 %collective-permute-start.12 = (bf16[128,256]{1,0:T(8,128)(2,1)S(1)}, bf16[128,256]{1,0:T(8,128)(2,1)S(1)}, u32[]{:S(2)}, u32[]{:S(2)}) collective-permute-start(bf16[128,256]{1,0:T(8,128)(2,1)S(1)} %get-tuple-element.27), channel_id=1, source_target_pairs={{0,2},{1,3},{2,0},{3,1},{4,6},{5,7},{6,4},{7,5},{8,10},{9,11},{10,... | collective-permute-start | bytes 196616 | tf_op jit(solution)/shard_map/ppermute | solution.py:56
  36.7 6.2 %collective-permute-start.13 = (bf16[128,256]{1,0:T(8,128)(2,1)S(1)}, bf16[128,256]{1,0:T(8,128)(2,1)S(1)}, u32[]{:S(2)}, u32[]{:S(2)}) collective-permute-start(bf16[128,256]{1,0:T(8,128)(2,1)S(1)} %get-tuple-element.28), channel_id=1, source_target_pairs={{0,3},{1,2},{2,1},{3,0},{4,7},{5,6},{6,5},{7,4},{8,11},{9,10},{10,... | collective-permute-start | bytes 196616 | tf_op jit(solution)/shard_map/ppermute | solution.py:56
  38.1 4.8 %collective-permute-start.18 = (bf16[144,256]{1,0:T(8,128)(2,1)S(1)}, bf16[144,256]{1,0:T(8,128)(2,1)S(1)}, u32[]{:S(2)}, u32[]{:S(2)}) collective-permute-start(bf16[144,256]{1,0:T(8,128)(2,1)S(1)} %shard_map.131.refs_1_), channel_id=1, source_target_pairs={{0,16},{4,20},{8,24},{12,28},{16,0},{20,4},{24,8},{28,12},{1,17},{... | collective-permute-start | bytes 221192 | tf_op jit(solution)/shard_map/ppermute | solution.py:71
  39.4 4.3 %collective-permute-start.14 = (bf16[128,256]{1,0:T(8,128)(2,1)S(1)}, bf16[128,256]{1,0:T(8,128)(2,1)S(1)}, u32[]{:S(2)}, u32[]{:S(2)}) collective-permute-start(bf16[128,256]{1,0:T(8,128)(2,1)S(1)} %get-tuple-element.30), channel_id=1, source_target_pairs={{0,1},{1,0},{2,3},{3,2},{4,5},{5,4},{6,7},{7,6},{8,9},{9,8},{10,11... | collective-permute-start | bytes 196616 | tf_op jit(solution)/shard_map/ppermute | solution.py:56
  43.0 1.4 %collective-permute-start.19 = (f32[128,256]{1,0:T(8,128)S(1)}, f32[128,256]{1,0:T(8,128)S(1)}, u32[]{:S(2)}, u32[]{:S(2)}) collective-permute-start(f32[128,256]{1,0:T(8,128)S(1)} %get-tuple-element.31.own_ref), channel_id=1, source_target_pairs={{0,4},{4,0},{8,12},{12,8},{16,20},{20,16},{24,28},{28,24},{1,5},{5... | collective-permute-start | bytes 393224 | tf_op jit(solution)/shard_map/ppermute | solution.py:61

commit v20 on v18

--- a/solution.py
+++ b/solution.py
@@ -14,7 +14,8 @@
 VMEM_LIMIT = 48 * 1024 * 1024
 BIAS_ROWS = 16
 BACK_SUM_WEIGHT = 30
-ROW_SUM_WEIGHT = 120
+EARLY_WEIGHT = 40
+ROW_SUM_WEIGHT = 140
 FEATURES_WEIGHT = 100
 
 VMEM_SPEC = pl.BlockSpec(memory_space=pltpu.VMEM)
@@ -461,6 +462,12 @@
     add_late = functools.partial(add, flops=ROW_SUM_WEIGHT * matrix)
     row_terms = total_over(chip_term, add, "row", n_row)
 
+    early = [
+        call(copy_kernel, like(tile, hidden), [VMEM_SPEC], [], EARLY_WEIGHT * matrix, 2 * block_bytes)(
+            received
+        )
+        for received in grads[:-2]
+    ]
     own_grads = call(
         gather_kernel,
         like(own_nodes, hidden),
@@ -468,7 +475,7 @@
         [],
         0,
         own_nodes * hidden * 4,
-    )(chip_term, *grads)
+    )(chip_term, *early, *grads[-2:])
     other_grads = swap_cores(own_grads, n_col)
     if is_dense:
         back_own = call(

time: 44.7 us -> 46.1 us (1.031)
  waiting for transfers between devices: 14 us -> 16.1 us
  Pallas kernels: 6.21 us -> 5.73 us
    ppermute x12, waiting for transfers between devices: 8.96 us -> 10.7 us  [exchange(): lax.ppermute(blocks[k], axis, pairs)]
    ppermute x4, waiting for transfers between devices: 2.66 us -> 3.38 us  [total_over(): terms = [lax.ppermute(block, axis, pairs_of(step, size, cores)), block]]
    pallas_call x1, Pallas kernels: 2.13 us -> 1.64 us  [local(): call(dense_kernel, (like(row_nodes, col_nodes), like(1, hidden, F32)), [S...]
  transfers between devices with their start and end apart: 20 -> 20, of which waited for: 14 -> 14; matrix products, arithmetic and copies ran while one was open for 0% -> 0% of each run, Pallas kernels for 10% -> 9%
where the time goes in v20:
time: 46.1 us; the launch traced here: 46 us
  starting transfers between devices  22.7 us (49%)
  waiting for transfers between devices  16.1 us (35%)
  Pallas kernels  5.73 us (12%)
  between operations  1.49 us (3%)
    ppermute x12, starting transfers between devices, exchange(): lax.ppermute(blocks[k], axis, pairs)  16.5 us
    ppermute x12, waiting for transfers between devices, exchange(): lax.ppermute(blocks[k], axis, pairs)  10.7 us
    ppermute x4, starting transfers between devices, total_over(): terms = [lax.ppermute(block, axis, pairs_of(step, size, cores)), block]  5.84 us
    ppermute x4, waiting for transfers between devices, total_over(): terms = [lax.ppermute(block, axis, pairs_of(step, size, cores)), block]  3.38 us
    ppermute x4, waiting for transfers between devices, swap_cores(): return lax.ppermute(block, 'col', [(i, i ^ 1) for i in range(size)])  2.03 us
    pallas_call x1, Pallas kernels, local(): call(dense_kernel, (like(row_nodes, col_nodes), like(1, hidden, F32)), [S...  1.64 us
  transfers between devices with their start and end apart: 20, of which 14 were waited for; matrix products, arithmetic and copies ran while one was open for 0% of the time, Pallas kernels for 9%

profile of v20, /device:TPU:0, one launch (start us, length us, event | category | flops | bytes accessed | tf_op | source)
XLA Modules:
  0.0 46.0 jit_solution(12200131618378853749)
XLA Ops:
  0.6 4.1 %collective-permute-start = (bf16[128,256]{1,0:T(8,128)(2,1)}, bf16[128,256]{1,0:T(8,128)(2,1)S(1)}, u32[]{:S(2)}, u32[]{:S(2)}) collective-permute-start(bf16[128,256]{1,0:T(8,128)(2,1)} %refs_3_.1), channel_id=1, source_target_pairs={{0,2},{1,3},{2,0},{3,1},{4,6},{5,7},{6,4},{7,5},{8,10},{9,11},{10,... | collective-permute-start | bytes 196616 | tf_op jit(solution)/shard_map/ppermute | solution.py:61
  4.7 1.3 %collective-permute-start.1 = (bf16[128,256]{1,0:T(8,128)(2,1)}, bf16[128,256]{1,0:T(8,128)(2,1)S(1)}, u32[]{:S(2)}, u32[]{:S(2)}) collective-permute-start(bf16[128,256]{1,0:T(8,128)(2,1)} %refs_3_.1), channel_id=1, source_target_pairs={{0,3},{1,2},{2,1},{3,0},{4,7},{5,6},{6,5},{7,4},{8,11},{9,10},{10,... | collective-permute-start | bytes 196616 | tf_op jit(solution)/shard_map/ppermute | solution.py:61
  7.0 1.6 %shard_map.111 = (bf16[1024,512]{1,0:T(8,128)(2,1)S(1)}, f32[1,256]{1,0:T(1,128)S(1)}) custom-call(s32[1,1]{1,0:T(1,128)S(6)} %copy.12.count_ref, s32[1,1,32]{2,1,0:T(1,128)} %row_hbm.1, s32[1,1,32]{2,1,0:T(1,128)} %col_hbm.1, bf16[1,1,32,128,128]{4,3,2,1,0:T(8,128)(2,1)} %tiles_hbm.1, f32[1,256]{1,0:T(1,128)} %bitcast.2), custom_call_target="tpu_custom_call" | custom-call | bytes 6291456 | tf_op jit(solution)/shard_map/pallas_call | solution.py:363
  8.7 2.5 %collective-permute-done.1.refs_1_ = bf16[128,256]{1,0:T(8,128)(2,1)S(1)} collective-permute-done((bf16[128,256]{1,0:T(8,128)(2,1)}, bf16[128,256]{1,0:T(8,128)(2,1)S(1)}, u32[]{:S(2)}, u32[]{:S(2)}) %collective-permute-start.1) | collective-permute-done | bytes 65568 | tf_op jit(solution)/shard_map/ppermute | solution.py:61
  11.3 0.3 shard_map.112
  12.0 1.2 %collective-permute-done.3.other_ref = bf16[512,256]{1,0:T(8,128)(2,1)S(1)} collective-permute-done((bf16[512,256]{1,0:T(8,128)(2,1)S(1)}, bf16[512,256]{1,0:T(8,128)(2,1)S(1)}, u32[]{:S(2)}, u32[]{:S(2)}) %collective-permute-start.3) | collective-permute-done | bytes 262176 | tf_op jit(solution)/shard_map/ppermute | solution.py:66
  13.2 2.5 %collective-permute-start.4 = (bf16[128,256]{1,0:T(8,128)(2,1)S(1)}, bf16[128,256]{1,0:T(8,128)(2,1)S(1)}, u32[]{:S(2)}, u32[]{:S(2)}) collective-permute-start(bf16[128,256]{1,0:T(8,128)(2,1)S(1)} %shard_map.114.refs_0_), channel_id=1, source_target_pairs={{0,24},{4,28},{8,16},{12,20},{16,8},{20,12},{24,0},{28,4},{1,25},{... | collective-permute-start | bytes 196616 | tf_op jit(solution)/shard_map/ppermute | solution.py:61
  15.7 0.6 %collective-permute-start.5 = (bf16[128,256]{1,0:T(8,128)(2,1)S(1)}, bf16[128,256]{1,0:T(8,128)(2,1)S(1)}, u32[]{:S(2)}, u32[]{:S(2)}) collective-permute-start(bf16[128,256]{1,0:T(8,128)(2,1)S(1)} %shard_map.115.refs_0_), channel_id=1, source_target_pairs={{0,16},{4,20},{8,24},{12,28},{16,0},{20,4},{24,8},{28,12},{1,17},{... | collective-permute-start | bytes 196616 | tf_op jit(solution)/shard_map/ppermute | solution.py:61
  16.4 0.6 %collective-permute-start.6 = (bf16[128,256]{1,0:T(8,128)(2,1)S(1)}, bf16[128,256]{1,0:T(8,128)(2,1)S(1)}, u32[]{:S(2)}, u32[]{:S(2)}) collective-permute-start(bf16[128,256]{1,0:T(8,128)(2,1)S(1)} %shard_map.116.refs_0_), channel_id=1, source_target_pairs={{0,8},{4,12},{8,0},{12,4},{16,24},{20,28},{24,16},{28,20},{1,9},{5... | collective-permute-start | bytes 196616 | tf_op jit(solution)/shard_map/ppermute | solution.py:61
  17.0 1.5 %collective-permute-done.4.refs_0_ = bf16[128,256]{1,0:T(8,128)(2,1)S(1)} collective-permute-done((bf16[128,256]{1,0:T(8,128)(2,1)S(1)}, bf16[128,256]{1,0:T(8,128)(2,1)S(1)}, u32[]{:S(2)}, u32[]{:S(2)}) %collective-permute-start.4) | collective-permute-done | bytes 65568 | tf_op jit(solution)/shard_map/ppermute | solution.py:61
  18.5 1.6 %collective-permute-done.5.refs_1_ = bf16[128,256]{1,0:T(8,128)(2,1)S(1)} collective-permute-done((bf16[128,256]{1,0:T(8,128)(2,1)S(1)}, bf16[128,256]{1,0:T(8,128)(2,1)S(1)}, u32[]{:S(2)}, u32[]{:S(2)}) %collective-permute-start.5) | collective-permute-done | bytes 65568 | tf_op jit(solution)/shard_map/ppermute | solution.py:61
  20.1 0.6 %collective-permute-done.6.refs_2_ = bf16[128,256]{1,0:T(8,128)(2,1)S(1)} collective-permute-done((bf16[128,256]{1,0:T(8,128)(2,1)S(1)}, bf16[128,256]{1,0:T(8,128)(2,1)S(1)}, u32[]{:S(2)}, u32[]{:S(2)}) %collective-permute-start.6) | collective-permute-done | bytes 65568 | tf_op jit(solution)/shard_map/ppermute | solution.py:61
  21.3 1.6 %collective-permute-start.8 = (bf16[128,256]{1,0:T(8,128)(2,1)S(1)}, bf16[128,256]{1,0:T(8,128)(2,1)S(1)}, u32[]{:S(2)}, u32[]{:S(2)}) collective-permute-start(bf16[128,256]{1,0:T(8,128)(2,1)S(1)} %get-tuple-element.26.grad_ref.refs_3_), channel_id=1, source_target_pairs={{0,24},{4,28},{8,16},{12,20},{16,8},{20,12},{24,0},{28,4},{1,25},{... | collective-permute-start | bytes 196616 | tf_op jit(solution)/shard_map/ppermute | solution.py:61
  23.1 1.0 %collective-permute-start.15 = (bf16[144,256]{1,0:T(8,128)(2,1)S(1)}, bf16[144,256]{1,0:T(8,128)(2,1)S(1)}, u32[]{:S(2)}, u32[]{:S(2)}) collective-permute-start(bf16[144,256]{1,0:T(8,128)(2,1)S(1)} %shard_map.123.after_ref.refs_1_), channel_id=1, source_target_pairs={{0,1},{1,0},{2,3},{3,2},{4,5},{5,4},{6,7},{7,6},{8,9},{9,8},{10,11... | collective-permute-start | bytes 221192 | tf_op jit(solution)/shard_map/ppermute | solution.py:76
  24.0 1.0 %collective-permute-start.9 = (bf16[128,256]{1,0:T(8,128)(2,1)S(1)}, bf16[128,256]{1,0:T(8,128)(2,1)S(1)}, u32[]{:S(2)}, u32[]{:S(2)}) collective-permute-start(bf16[128,256]{1,0:T(8,128)(2,1)S(1)} %get-tuple-element.26.grad_ref.refs_3_), channel_id=1, source_target_pairs={{0,16},{4,20},{8,24},{12,28},{16,0},{20,4},{24,8},{28,12},{1,17},{... | collective-permute-start | bytes 196616 | tf_op jit(solution)/shard_map/ppermute | solution.py:61
  25.0 1.0 %collective-permute-start.10 = (bf16[128,256]{1,0:T(8,128)(2,1)S(1)}, bf16[128,256]{1,0:T(8,128)(2,1)S(1)}, u32[]{:S(2)}, u32[]{:S(2)}) collective-permute-start(bf16[128,256]{1,0:T(8,128)(2,1)S(1)} %get-tuple-element.26.grad_ref.refs_3_), channel_id=1, source_target_pairs={{0,8},{4,12},{8,0},{12,4},{16,24},{20,28},{24,16},{28,20},{1,9},{5... | collective-permute-start | bytes 196616 | tf_op jit(solution)/shard_map/ppermute | solution.py:61
  26.0 0.6 %collective-permute-done.8.in_ref = bf16[128,256]{1,0:T(8,128)(2,1)S(1)} collective-permute-done((bf16[128,256]{1,0:T(8,128)(2,1)S(1)}, bf16[128,256]{1,0:T(8,128)(2,1)S(1)}, u32[]{:S(2)}, u32[]{:S(2)}) %collective-permute-start.8) | collective-permute-done | bytes 65568 | tf_op jit(solution)/shard_map/ppermute | solution.py:61
  26.7 0.8 %collective-permute-done.15.refs_0_ = bf16[144,256]{1,0:T(8,128)(2,1)S(1)} collective-permute-done((bf16[144,256]{1,0:T(8,128)(2,1)S(1)}, bf16[144,256]{1,0:T(8,128)(2,1)S(1)}, u32[]{:S(2)}, u32[]{:S(2)}) %collective-permute-start.15) | collective-permute-done | bytes 73760 | tf_op jit(solution)/shard_map/ppermute | solution.py:76
  27.5 2.7 %collective-permute-start.16 = (bf16[144,256]{1,0:T(8,128)(2,1)S(1)}, bf16[144,256]{1,0:T(8,128)(2,1)S(1)}, u32[]{:S(2)}, u32[]{:S(2)}) collective-permute-start(bf16[144,256]{1,0:T(8,128)(2,1)S(1)} %shard_map.131.refs_1_), channel_id=1, source_target_pairs={{0,2},{1,3},{2,0},{3,1},{4,6},{5,7},{6,4},{7,5},{8,10},{9,11},{10,... | collective-permute-start | bytes 221192 | tf_op jit(solution)/shard_map/ppermute | solution.py:76
  30.4 0.3 shard_map.120.turned_ref
  31.1 2.6 %collective-permute-done.16.refs_0_ = bf16[144,256]{1,0:T(8,128)(2,1)S(1)} collective-permute-done((bf16[144,256]{1,0:T(8,128)(2,1)S(1)}, bf16[144,256]{1,0:T(8,128)(2,1)S(1)}, u32[]{:S(2)}, u32[]{:S(2)}) %collective-permute-start.16) | collective-permute-done | bytes 73760 | tf_op jit(solution)/shard_map/ppermute | solution.py:76
  33.7 1.6 %collective-permute-start.17 = (bf16[144,256]{1,0:T(8,128)(2,1)S(1)}, bf16[144,256]{1,0:T(8,128)(2,1)S(1)}, u32[]{:S(2)}, u32[]{:S(2)}) collective-permute-start(bf16[144,256]{1,0:T(8,128)(2,1)S(1)} %shard_map.132.refs_1_), channel_id=1, source_target_pairs={{0,8},{4,12},{8,0},{12,4},{16,24},{20,28},{24,16},{28,20},{1,9},{5... | collective-permute-start | bytes 221192 | tf_op jit(solution)/shard_map/ppermute | solution.py:76
  35.5 2.1 %collective-permute-start.12 = (bf16[128,256]{1,0:T(8,128)(2,1)S(1)}, bf16[128,256]{1,0:T(8,128)(2,1)S(1)}, u32[]{:S(2)}, u32[]{:S(2)}) collective-permute-start(bf16[128,256]{1,0:T(8,128)(2,1)S(1)} %get-tuple-element.27), channel_id=1, source_target_pairs={{0,2},{1,3},{2,0},{3,1},{4,6},{5,7},{6,4},{7,5},{8,10},{9,11},{10,... | collective-permute-start | bytes 196616 | tf_op jit(solution)/shard_map/ppermute | solution.py:61
  37.6 1.1 %collective-permute-start.13 = (bf16[128,256]{1,0:T(8,128)(2,1)S(1)}, bf16[128,256]{1,0:T(8,128)(2,1)S(1)}, u32[]{:S(2)}, u32[]{:S(2)}) collective-permute-start(bf16[128,256]{1,0:T(8,128)(2,1)S(1)} %get-tuple-element.28), channel_id=1, source_target_pairs={{0,3},{1,2},{2,1},{3,0},{4,7},{5,6},{6,5},{7,4},{8,11},{9,10},{10,... | collective-permute-start | bytes 196616 | tf_op jit(solution)/shard_map/ppermute | solution.py:61
  38.7 0.6 %collective-permute-start.18 = (bf16[144,256]{1,0:T(8,128)(2,1)S(1)}, bf16[144,256]{1,0:T(8,128)(2,1)S(1)}, u32[]{:S(2)}, u32[]{:S(2)}) collective-permute-start(bf16[144,256]{1,0:T(8,128)(2,1)S(1)} %shard_map.133.refs_1_), channel_id=1, source_target_pairs={{0,16},{4,20},{8,24},{12,28},{16,0},{20,4},{24,8},{28,12},{1,17},{... | collective-permute-start | bytes 221192 | tf_op jit(solution)/shard_map/ppermute | solution.py:76
  39.3 0.5 %collective-permute-start.14 = (bf16[128,256]{1,0:T(8,128)(2,1)S(1)}, bf16[128,256]{1,0:T(8,128)(2,1)S(1)}, u32[]{:S(2)}, u32[]{:S(2)}) collective-permute-start(bf16[128,256]{1,0:T(8,128)(2,1)S(1)} %get-tuple-element.30), channel_id=1, source_target_pairs={{0,1},{1,0},{2,3},{3,2},{4,5},{5,4},{6,7},{7,6},{8,9},{9,8},{10,11... | collective-permute-start | bytes 196616 | tf_op jit(solution)/shard_map/ppermute | solution.py:61
  39.8 0.6 %shard_map.119 = bf16[128,256]{1,0:T(8,128)(2,1)} custom-call(bf16[128,256]{1,0:T(8,128)(2,1)S(1)} %get-tuple-element.24.in_ref), custom_call_target="tpu_custom_call" | custom-call | bytes 131072 | tf_op jit(solution)/shard_map/pallas_call | solution.py:449
  40.4 1.1 %collective-permute-done.12.refs_0_ = bf16[128,256]{1,0:T(8,128)(2,1)S(1)} collective-permute-done((bf16[128,256]{1,0:T(8,128)(2,1)S(1)}, bf16[128,256]{1,0:T(8,128)(2,1)S(1)}, u32[]{:S(2)}, u32[]{:S(2)}) %collective-permute-start.12) | collective-permute-done | bytes 65568 | tf_op jit(solution)/shard_map/ppermute | solution.py:61
  41.5 2.3 %collective-permute-done.13.refs_1_ = bf16[128,256]{1,0:T(8,128)(2,1)S(1)} collective-permute-done((bf16[128,256]{1,0:T(8,128)(2,1)S(1)}, bf16[128,256]{1,0:T(8,128)(2,1)S(1)}, u32[]{:S(2)}, u32[]{:S(2)}) %collective-permute-start.13) | collective-permute-done | bytes 65568 | tf_op jit(solution)/shard_map/ppermute | solution.py:61
  43.9 0.3 collective-permute-done.14.last_ref
  44.4 0.8 %collective-permute-done.19.other_ref = f32[128,256]{1,0:T(8,128)S(1)} collective-permute-done((f32[128,256]{1,0:T(8,128)S(1)}, f32[128,256]{1,0:T(8,128)S(1)}, u32[]{:S(2)}, u32[]{:S(2)}) %collective-permute-start.19) | collective-permute-done | bytes 131104 | tf_op jit(solution)/shard_map/ppermute | solution.py:66
  45.2 0.8 %shard_map.135 = (bf16[128,256]{1,0:T(8,128)(2,1)}, f32[256,256]{1,0:T(8,128)}, f32[1,256]{1,0:T(1,128)}) custom-call(bf16[128,256]{1,0:T(8,128)(2,1)S(1)} %shard_map.130.features_ref, f32[128,256]{1,0:T(8,128)S(1)} %get-tuple-element.31.own_ref, f32[128,256]{1,0:T(8,128)S(1)} %collective-permute-done.19.other_ref, f32[1,256]{1,0:T(1,128)S(1)} %get-tuple-element.32.bias_ref), custom_call_target="tpu_custom_call" | custom-call | bytes 524288 | tf_op jit(solution)/shard_map/pallas_call | solution.py:536
  (39 shorter events, 2.8 us)
Async XLA Ops:
  0.6 8.1 %collective-permute-start = (bf16[128,256]{1,0:T(8,128)(2,1)}, bf16[128,256]{1,0:T(8,128)(2,1)S(1)}, u32[]{:S(2)}, u32[]{:S(2)}) collective-permute-start(bf16[128,256]{1,0:T(8,128)(2,1)} %refs_3_.1), channel_id=1, source_target_pairs={{0,2},{1,3},{2,0},{3,1},{4,6},{5,7},{6,4},{7,5},{8,10},{9,11},{10,... | collective-permute-start | bytes 196616 | tf_op jit(solution)/shard_map/ppermute | solution.py:61
  4.7 6.4 %collective-permute-start.1 = (bf16[128,256]{1,0:T(8,128)(2,1)}, bf16[128,256]{1,0:T(8,128)(2,1)S(1)}, u32[]{:S(2)}, u32[]{:S(2)}) collective-permute-start(bf16[128,256]{1,0:T(8,128)(2,1)} %refs_3_.1), channel_id=1, source_target_pairs={{0,3},{1,2},{2,1},{3,0},{4,7},{5,6},{6,5},{7,4},{8,11},{9,10},{10,... | collective-permute-start | bytes 196616 | tf_op jit(solution)/shard_map/ppermute | solution.py:61
  6.1 5.2 %collective-permute-start.2 = (bf16[128,256]{1,0:T(8,128)(2,1)}, bf16[128,256]{1,0:T(8,128)(2,1)S(1)}, u32[]{:S(2)}, u32[]{:S(2)}) collective-permute-start(bf16[128,256]{1,0:T(8,128)(2,1)} %refs_3_.1), channel_id=1, source_target_pairs={{0,1},{1,0},{2,3},{3,2},{4,5},{5,4},{6,7},{7,6},{8,9},{9,8},{10,11... | collective-permute-start | bytes 196616 | tf_op jit(solution)/shard_map/ppermute | solution.py:61
  7.0 4.3 %copy-start.1 = (bf16[128,256]{1,0:T(8,128)(2,1)S(1)}, bf16[128,256]{1,0:T(8,128)(2,1)}, u32[]{:S(2)}) copy-start(bf16[128,256]{1,0:T(8,128)(2,1)} %refs_3_.1) | copy-start | bytes 196612
  11.6 1.6 %collective-permute-start.3 = (bf16[512,256]{1,0:T(8,128)(2,1)S(1)}, bf16[512,256]{1,0:T(8,128)(2,1)S(1)}, u32[]{:S(2)}, u32[]{:S(2)}) collective-permute-start(bf16[512,256]{1,0:T(8,128)(2,1)S(1)} %get-tuple-element.23), channel_id=1, source_target_pairs={{0,4},{4,0},{8,12},{12,8},{16,20},{20,16},{24,28},{28,24},{1,5},{5... | collective-permute-start | bytes 786440 | tf_op jit(solution)/shard_map/ppermute | solution.py:66
  13.2 5.2 %collective-permute-start.4 = (bf16[128,256]{1,0:T(8,128)(2,1)S(1)}, bf16[128,256]{1,0:T(8,128)(2,1)S(1)}, u32[]{:S(2)}, u32[]{:S(2)}) collective-permute-start(bf16[128,256]{1,0:T(8,128)(2,1)S(1)} %shard_map.114.refs_0_), channel_id=1, source_target_pairs={{0,24},{4,28},{8,16},{12,20},{16,8},{20,12},{24,0},{28,4},{1,25},{... | collective-permute-start | bytes 196616 | tf_op jit(solution)/shard_map/ppermute | solution.py:61
  15.7 4.3 %collective-permute-start.5 = (bf16[128,256]{1,0:T(8,128)(2,1)S(1)}, bf16[128,256]{1,0:T(8,128)(2,1)S(1)}, u32[]{:S(2)}, u32[]{:S(2)}) collective-permute-start(bf16[128,256]{1,0:T(8,128)(2,1)S(1)} %shard_map.115.refs_0_), channel_id=1, source_target_pairs={{0,16},{4,20},{8,24},{12,28},{16,0},{20,4},{24,8},{28,12},{1,17},{... | collective-permute-start | bytes 196616 | tf_op jit(solution)/shard_map/ppermute | solution.py:61
  16.3 4.4 %copy-start = (bf16[256,256]{1,0:T(8,128)(2,1)S(1)}, bf16[256,256]{1,0:T(8,128)(2,1)}, u32[]{:S(2)}) copy-start(bf16[256,256]{1,0:T(8,128)(2,1)} %weight_ref.3) | copy-start | bytes 393220
  16.4 4.3 %copy-start.2 = (bf16[128,256]{1,0:T(8,128)(2,1)S(1)}, bf16[128,256]{1,0:T(8,128)(2,1)}, u32[]{:S(2)}) copy-start(bf16[128,256]{1,0:T(8,128)(2,1)} %cot_ref.1) | copy-start | bytes 196612
  16.4 4.3 %collective-permute-start.6 = (bf16[128,256]{1,0:T(8,128)(2,1)S(1)}, bf16[128,256]{1,0:T(8,128)(2,1)S(1)}, u32[]{:S(2)}, u32[]{:S(2)}) collective-permute-start(bf16[128,256]{1,0:T(8,128)(2,1)S(1)} %shard_map.116.refs_0_), channel_id=1, source_target_pairs={{0,8},{4,12},{8,0},{12,4},{16,24},{20,28},{24,16},{28,20},{1,9},{5... | collective-permute-start | bytes 196616 | tf_op jit(solution)/shard_map/ppermute | solution.py:61
  21.2 1.8 %collective-permute-start.7 = (bf16[144,256]{1,0:T(8,128)(2,1)S(1)}, bf16[144,256]{1,0:T(8,128)(2,1)S(1)}, u32[]{:S(2)}, u32[]{:S(2)}) collective-permute-start(bf16[144,256]{1,0:T(8,128)(2,1)S(1)} %shard_map.121), channel_id=1, source_target_pairs={{0,4},{4,0},{8,12},{12,8},{16,20},{20,16},{24,28},{28,24},{1,5},{5... | collective-permute-start | bytes 221192 | tf_op jit(solution)/shard_map/ppermute | solution.py:66
  21.3 5.4 %collective-permute-start.8 = (bf16[128,256]{1,0:T(8,128)(2,1)S(1)}, bf16[128,256]{1,0:T(8,128)(2,1)S(1)}, u32[]{:S(2)}, u32[]{:S(2)}) collective-permute-start(bf16[128,256]{1,0:T(8,128)(2,1)S(1)} %get-tuple-element.26.grad_ref.refs_3_), channel_id=1, source_target_pairs={{0,24},{4,28},{8,16},{12,20},{16,8},{20,12},{24,0},{28,4},{1,25},{... | collective-permute-start | bytes 196616 | tf_op jit(solution)/shard_map/ppermute | solution.py:61
  23.1 4.4 %collective-permute-start.15 = (bf16[144,256]{1,0:T(8,128)(2,1)S(1)}, bf16[144,256]{1,0:T(8,128)(2,1)S(1)}, u32[]{:S(2)}, u32[]{:S(2)}) collective-permute-start(bf16[144,256]{1,0:T(8,128)(2,1)S(1)} %shard_map.123.after_ref.refs_1_), channel_id=1, source_target_pairs={{0,1},{1,0},{2,3},{3,2},{4,5},{5,4},{6,7},{7,6},{8,9},{9,8},{10,11... | collective-permute-start | bytes 221192 | tf_op jit(solution)/shard_map/ppermute | solution.py:76
  24.0 6.2 %collective-permute-start.9 = (bf16[128,256]{1,0:T(8,128)(2,1)S(1)}, bf16[128,256]{1,0:T(8,128)(2,1)S(1)}, u32[]{:S(2)}, u32[]{:S(2)}) collective-permute-start(bf16[128,256]{1,0:T(8,128)(2,1)S(1)} %get-tuple-element.26.grad_ref.refs_3_), channel_id=1, source_target_pairs={{0,16},{4,20},{8,24},{12,28},{16,0},{20,4},{24,8},{28,12},{1,17},{... | collective-permute-start | bytes 196616 | tf_op jit(solution)/shard_map/ppermute | solution.py:61
  25.0 5.2 %collective-permute-start.10 = (bf16[128,256]{1,0:T(8,128)(2,1)S(1)}, bf16[128,256]{1,0:T(8,128)(2,1)S(1)}, u32[]{:S(2)}, u32[]{:S(2)}) collective-permute-start(bf16[128,256]{1,0:T(8,128)(2,1)S(1)} %get-tuple-element.26.grad_ref.refs_3_), channel_id=1, source_target_pairs={{0,8},{4,12},{8,0},{12,4},{16,24},{20,28},{24,16},{28,20},{1,9},{5... | collective-permute-start | bytes 196616 | tf_op jit(solution)/shard_map/ppermute | solution.py:61
  27.5 6.1 %collective-permute-start.16 = (bf16[144,256]{1,0:T(8,128)(2,1)S(1)}, bf16[144,256]{1,0:T(8,128)(2,1)S(1)}, u32[]{:S(2)}, u32[]{:S(2)}) collective-permute-start(bf16[144,256]{1,0:T(8,128)(2,1)S(1)} %shard_map.131.refs_1_), channel_id=1, source_target_pairs={{0,2},{1,3},{2,0},{3,1},{4,6},{5,7},{6,4},{7,5},{8,10},{9,11},{10,... | collective-permute-start | bytes 221192 | tf_op jit(solution)/shard_map/ppermute | solution.py:76
  30.3 4.9 %collective-permute-start.11 = (bf16[512,256]{1,0:T(8,128)(2,1)S(1)}, bf16[512,256]{1,0:T(8,128)(2,1)S(1)}, u32[]{:S(2)}, u32[]{:S(2)}) collective-permute-start(bf16[512,256]{1,0:T(8,128)(2,1)S(1)} %shard_map.126.source_ref), channel_id=1, source_target_pairs={{0,4},{4,0},{8,12},{12,8},{16,20},{20,16},{24,28},{28,24},{1,5},{5... | collective-permute-start | bytes 786440 | tf_op jit(solution)/shard_map/ppermute | solution.py:66
  33.7 5.0 %collective-permute-start.17 = (bf16[144,256]{1,0:T(8,128)(2,1)S(1)}, bf16[144,256]{1,0:T(8,128)(2,1)S(1)}, u32[]{:S(2)}, u32[]{:S(2)}) collective-permute-start(bf16[144,256]{1,0:T(8,128)(2,1)S(1)} %shard_map.132.refs_1_), channel_id=1, source_target_pairs={{0,8},{4,12},{8,0},{12,4},{16,24},{20,28},{24,16},{28,20},{1,9},{5... | collective-permute-start | bytes 221192 | tf_op jit(solution)/shard_map/ppermute | solution.py:76
  35.5 5.9 %collective-permute-start.12 = (bf16[128,256]{1,0:T(8,128)(2,1)S(1)}, bf16[128,256]{1,0:T(8,128)(2,1)S(1)}, u32[]{:S(2)}, u32[]{:S(2)}) collective-permute-start(bf16[128,256]{1,0:T(8,128)(2,1)S(1)} %get-tuple-element.27), channel_id=1, source_target_pairs={{0,2},{1,3},{2,0},{3,1},{4,6},{5,7},{6,4},{7,5},{8,10},{9,11},{10,... | collective-permute-start | bytes 196616 | tf_op jit(solution)/shard_map/ppermute | solution.py:61
  37.6 6.2 %collective-permute-start.13 = (bf16[128,256]{1,0:T(8,128)(2,1)S(1)}, bf16[128,256]{1,0:T(8,128)(2,1)S(1)}, u32[]{:S(2)}, u32[]{:S(2)}) collective-permute-start(bf16[128,256]{1,0:T(8,128)(2,1)S(1)} %get-tuple-element.28), channel_id=1, source_target_pairs={{0,3},{1,2},{2,1},{3,0},{4,7},{5,6},{6,5},{7,4},{8,11},{9,10},{10,... | collective-permute-start | bytes 196616 | tf_op jit(solution)/shard_map/ppermute | solution.py:61
  38.7 5.1 %collective-permute-start.18 = (bf16[144,256]{1,0:T(8,128)(2,1)S(1)}, bf16[144,256]{1,0:T(8,128)(2,1)S(1)}, u32[]{:S(2)}, u32[]{:S(2)}) collective-permute-start(bf16[144,256]{1,0:T(8,128)(2,1)S(1)} %shard_map.133.refs_1_), channel_id=1, source_target_pairs={{0,16},{4,20},{8,24},{12,28},{16,0},{20,4},{24,8},{28,12},{1,17},{... | collective-permute-start | bytes 221192 | tf_op jit(solution)/shard_map/ppermute | solution.py:76
  39.3 5.0 %collective-permute-start.14 = (bf16[128,256]{1,0:T(8,128)(2,1)S(1)}, bf16[128,256]{1,0:T(8,128)(2,1)S(1)}, u32[]{:S(2)}, u32[]{:S(2)}) collective-permute-start(bf16[128,256]{1,0:T(8,128)(2,1)S(1)} %get-tuple-element.30), channel_id=1, source_target_pairs={{0,1},{1,0},{2,3},{3,2},{4,5},{5,4},{6,7},{7,6},{8,9},{9,8},{10,11... | collective-permute-start | bytes 196616 | tf_op jit(solution)/shard_map/ppermute | solution.py:61
  43.8 1.4 %collective-permute-start.19 = (f32[128,256]{1,0:T(8,128)S(1)}, f32[128,256]{1,0:T(8,128)S(1)}, u32[]{:S(2)}, u32[]{:S(2)}) collective-permute-start(f32[128,256]{1,0:T(8,128)S(1)} %get-tuple-element.31.own_ref), channel_id=1, source_target_pairs={{0,4},{4,0},{8,12},{12,8},{16,20},{20,16},{24,28},{28,24},{1,5},{5... | collective-permute-start | bytes 393224 | tf_op jit(solution)/shard_map/ppermute | solution.py:66

commit v21 on v18

--- a/solution.py
+++ b/solution.py
@@ -267,10 +267,10 @@
     out_ref[...] = dense_dot(turned_ref[:, : source_ref.shape[0]], source_ref[...])
 
 
-def back_pieces_kernel(turned_ref, own_ref, source_ref, *outs):
+def back_pieces_kernel(turned_ref, own_ref, source_ref, *outs, partners, n_row):
     tile = outs[0].shape[0]
-    for k, out_ref in zip(half_first(len(outs)), outs):
-        rows = block_at(partner(row_index(), k, len(outs)), tile)
+    for k, out_ref in zip(partners, outs):
+        rows = block_at(partner(row_index(), k, n_row), tile)
         rest = dense_dot(turned_ref[rows, source_ref.shape[0] :], source_ref[...])
         out_ref[...] = (own_ref[rows, :] + rest).astype(BF16)
 
@@ -480,14 +480,16 @@
             row_nodes * hidden * 8,
         )(turned, own_grads)
         row_term = add_late(row_terms, after=[back_own])
-        back_pieces = call(
-            back_pieces_kernel,
-            [like(tile, hidden)] * n_row,
-            [VMEM_SPEC] * 3,
-            [],
-            slots * matrix // 2,
-            row_nodes * hidden * 8,
-        )(turned, back_own, other_grads)
+        back_pieces = []
+        for partners in (half_first(n_row)[:1], half_first(n_row)[1:]):
+            back_pieces += call(
+                functools.partial(back_pieces_kernel, partners=partners, n_row=n_row),
+                [like(tile, hidden)] * len(partners),
+                [VMEM_SPEC] * 3,
+                [],
+                len(partners) * n_chip * matrix,
+                row_nodes * hidden * 2,
+            )(turned, back_own, other_grads)
     else:
         row_term = add_late(row_terms)
         back_pieces = call(

time: 44.7 us -> 45 us (level)
  transfers between devices with their start and end apart: 20 -> 20, of which waited for: 14 -> 13; matrix products, arithmetic and copies ran while one was open for 0% -> 0% of each run, Pallas kernels for 10% -> 11%
where the time goes in v21:
time: 45 us; the launch traced here: 44.8 us
  starting transfers between devices  22.9 us (51%)
  waiting for transfers between devices  14 us (31%)
  Pallas kernels  6.36 us (14%)
  between operations  1.48 us (3%)
    ppermute x12, starting transfers between devices, exchange(): lax.ppermute(blocks[k], axis, pairs)  16.8 us
    ppermute x12, waiting for transfers between devices, exchange(): lax.ppermute(blocks[k], axis, pairs)  8.81 us
    ppermute x4, starting transfers between devices, total_over(): terms = [lax.ppermute(block, axis, pairs_of(step, size, cores)), block]  5.87 us
    ppermute x4, waiting for transfers between devices, swap_cores(): return lax.ppermute(block, 'col', [(i, i ^ 1) for i in range(size)])  2.6 us
    ppermute x4, waiting for transfers between devices, total_over(): terms = [lax.ppermute(block, axis, pairs_of(step, size, cores)), block]  2.57 us
    pallas_call x1, Pallas kernels, local(): call(dense_kernel, (like(row_nodes, col_nodes), like(1, hidden, F32)), [S...  2.13 us
  transfers between devices with their start and end apart: 20, of which 13 were waited for; matrix products, arithmetic and copies ran while one was open for 0% of the time, Pallas kernels for 11%

profile of v21, /device:TPU:0, one launch (start us, length us, event | category | flops | bytes accessed | tf_op | source)
XLA Modules:
  0.0 44.8 jit_solution(14036919277005350658)
XLA Ops:
  0.6 4.1 %collective-permute-start = (bf16[128,256]{1,0:T(8,128)(2,1)}, bf16[128,256]{1,0:T(8,128)(2,1)S(1)}, u32[]{:S(2)}, u32[]{:S(2)}) collective-permute-start(bf16[128,256]{1,0:T(8,128)(2,1)} %refs_3_.1), channel_id=1, source_target_pairs={{0,2},{1,3},{2,0},{3,1},{4,6},{5,7},{6,4},{7,5},{8,10},{9,11},{10,... | collective-permute-start | bytes 196616 | tf_op jit(solution)/shard_map/ppermute | solution.py:60
  4.7 1.3 %collective-permute-start.1 = (bf16[128,256]{1,0:T(8,128)(2,1)}, bf16[128,256]{1,0:T(8,128)(2,1)S(1)}, u32[]{:S(2)}, u32[]{:S(2)}) collective-permute-start(bf16[128,256]{1,0:T(8,128)(2,1)} %refs_3_.1), channel_id=1, source_target_pairs={{0,3},{1,2},{2,1},{3,0},{4,7},{5,6},{6,5},{7,4},{8,11},{9,10},{10,... | collective-permute-start | bytes 196616 | tf_op jit(solution)/shard_map/ppermute | solution.py:60
  7.0 2.1 %shard_map.111 = (bf16[1024,512]{1,0:T(8,128)(2,1)S(1)}, f32[1,256]{1,0:T(1,128)S(1)}) custom-call(s32[1,1]{1,0:T(1,128)S(6)} %copy.12.count_ref, s32[1,1,32]{2,1,0:T(1,128)} %row_hbm.1, s32[1,1,32]{2,1,0:T(1,128)} %col_hbm.1, bf16[1,1,32,128,128]{4,3,2,1,0:T(8,128)(2,1)} %tiles_hbm.1, f32[1,256]{1,0:T(1,128)} %bitcast.2), custom_call_target="tpu_custom_call" | custom-call | bytes 6291456 | tf_op jit(solution)/shard_map/pallas_call | solution.py:362
  9.1 2.0 %collective-permute-done.1.refs_1_ = bf16[128,256]{1,0:T(8,128)(2,1)S(1)} collective-permute-done((bf16[128,256]{1,0:T(8,128)(2,1)}, bf16[128,256]{1,0:T(8,128)(2,1)S(1)}, u32[]{:S(2)}, u32[]{:S(2)}) %collective-permute-start.1) | collective-permute-done | bytes 65568 | tf_op jit(solution)/shard_map/ppermute | solution.py:60
  11.3 0.3 shard_map.112
  12.0 1.2 %collective-permute-done.3.other_ref = bf16[512,256]{1,0:T(8,128)(2,1)S(1)} collective-permute-done((bf16[512,256]{1,0:T(8,128)(2,1)S(1)}, bf16[512,256]{1,0:T(8,128)(2,1)S(1)}, u32[]{:S(2)}, u32[]{:S(2)}) %collective-permute-start.3) | collective-permute-done | bytes 262176 | tf_op jit(solution)/shard_map/ppermute | solution.py:65
  13.2 2.5 %collective-permute-start.4 = (bf16[128,256]{1,0:T(8,128)(2,1)S(1)}, bf16[128,256]{1,0:T(8,128)(2,1)S(1)}, u32[]{:S(2)}, u32[]{:S(2)}) collective-permute-start(bf16[128,256]{1,0:T(8,128)(2,1)S(1)} %shard_map.114.refs_0_), channel_id=1, source_target_pairs={{0,24},{4,28},{8,16},{12,20},{16,8},{20,12},{24,0},{28,4},{1,25},{... | collective-permute-start | bytes 196616 | tf_op jit(solution)/shard_map/ppermute | solution.py:60
  15.7 0.6 %collective-permute-start.5 = (bf16[128,256]{1,0:T(8,128)(2,1)S(1)}, bf16[128,256]{1,0:T(8,128)(2,1)S(1)}, u32[]{:S(2)}, u32[]{:S(2)}) collective-permute-start(bf16[128,256]{1,0:T(8,128)(2,1)S(1)} %shard_map.115.refs_0_), channel_id=1, source_target_pairs={{0,16},{4,20},{8,24},{12,28},{16,0},{20,4},{24,8},{28,12},{1,17},{... | collective-permute-start | bytes 196616 | tf_op jit(solution)/shard_map/ppermute | solution.py:60
  16.4 0.6 %collective-permute-start.6 = (bf16[128,256]{1,0:T(8,128)(2,1)S(1)}, bf16[128,256]{1,0:T(8,128)(2,1)S(1)}, u32[]{:S(2)}, u32[]{:S(2)}) collective-permute-start(bf16[128,256]{1,0:T(8,128)(2,1)S(1)} %shard_map.116.refs_0_), channel_id=1, source_target_pairs={{0,8},{4,12},{8,0},{12,4},{16,24},{20,28},{24,16},{28,20},{1,9},{5... | collective-permute-start | bytes 196616 | tf_op jit(solution)/shard_map/ppermute | solution.py:60
  17.0 1.5 %collective-permute-done.4.refs_0_ = bf16[128,256]{1,0:T(8,128)(2,1)S(1)} collective-permute-done((bf16[128,256]{1,0:T(8,128)(2,1)S(1)}, bf16[128,256]{1,0:T(8,128)(2,1)S(1)}, u32[]{:S(2)}, u32[]{:S(2)}) %collective-permute-start.4) | collective-permute-done | bytes 65568 | tf_op jit(solution)/shard_map/ppermute | solution.py:60
  18.5 1.6 %collective-permute-done.5.refs_1_ = bf16[128,256]{1,0:T(8,128)(2,1)S(1)} collective-permute-done((bf16[128,256]{1,0:T(8,128)(2,1)S(1)}, bf16[128,256]{1,0:T(8,128)(2,1)S(1)}, u32[]{:S(2)}, u32[]{:S(2)}) %collective-permute-start.5) | collective-permute-done | bytes 65568 | tf_op jit(solution)/shard_map/ppermute | solution.py:60
  20.1 0.6 %collective-permute-done.6.refs_2_ = bf16[128,256]{1,0:T(8,128)(2,1)S(1)} collective-permute-done((bf16[128,256]{1,0:T(8,128)(2,1)S(1)}, bf16[128,256]{1,0:T(8,128)(2,1)S(1)}, u32[]{:S(2)}, u32[]{:S(2)}) %collective-permute-start.6) | collective-permute-done | bytes 65568 | tf_op jit(solution)/shard_map/ppermute | solution.py:60
  21.5 1.0 %collective-permute-done.7.refs_0_ = bf16[144,256]{1,0:T(8,128)(2,1)S(1)} collective-permute-done((bf16[144,256]{1,0:T(8,128)(2,1)S(1)}, bf16[144,256]{1,0:T(8,128)(2,1)S(1)}, u32[]{:S(2)}, u32[]{:S(2)}) %collective-permute-start.7) | collective-permute-done | bytes 73760 | tf_op jit(solution)/shard_map/ppermute | solution.py:65
  22.5 1.0 %collective-permute-start.15 = (bf16[144,256]{1,0:T(8,128)(2,1)S(1)}, bf16[144,256]{1,0:T(8,128)(2,1)S(1)}, u32[]{:S(2)}, u32[]{:S(2)}) collective-permute-start(bf16[144,256]{1,0:T(8,128)(2,1)S(1)} %shard_map.123.after_ref.refs_1_), channel_id=1, source_target_pairs={{0,1},{1,0},{2,3},{3,2},{4,5},{5,4},{6,7},{7,6},{8,9},{9,8},{10,11... | collective-permute-start | bytes 221192 | tf_op jit(solution)/shard_map/ppermute | solution.py:75
  23.5 1.5 %collective-permute-start.8 = (bf16[128,256]{1,0:T(8,128)(2,1)S(1)}, bf16[128,256]{1,0:T(8,128)(2,1)S(1)}, u32[]{:S(2)}, u32[]{:S(2)}) collective-permute-start(bf16[128,256]{1,0:T(8,128)(2,1)S(1)} %get-tuple-element.25.grad_ref.refs_3_), channel_id=1, source_target_pairs={{0,24},{4,28},{8,16},{12,20},{16,8},{20,12},{24,0},{28,4},{1,25},{... | collective-permute-start | bytes 196616 | tf_op jit(solution)/shard_map/ppermute | solution.py:60
  25.0 0.5 %collective-permute-start.9 = (bf16[128,256]{1,0:T(8,128)(2,1)S(1)}, bf16[128,256]{1,0:T(8,128)(2,1)S(1)}, u32[]{:S(2)}, u32[]{:S(2)}) collective-permute-start(bf16[128,256]{1,0:T(8,128)(2,1)S(1)} %get-tuple-element.25.grad_ref.refs_3_), channel_id=1, source_target_pairs={{0,16},{4,20},{8,24},{12,28},{16,0},{20,4},{24,8},{28,12},{1,17},{... | collective-permute-start | bytes 196616 | tf_op jit(solution)/shard_map/ppermute | solution.py:60
  25.5 1.5 %collective-permute-start.10 = (bf16[128,256]{1,0:T(8,128)(2,1)S(1)}, bf16[128,256]{1,0:T(8,128)(2,1)S(1)}, u32[]{:S(2)}, u32[]{:S(2)}) collective-permute-start(bf16[128,256]{1,0:T(8,128)(2,1)S(1)} %get-tuple-element.25.grad_ref.refs_3_), channel_id=1, source_target_pairs={{0,8},{4,12},{8,0},{12,4},{16,24},{20,28},{24,16},{28,20},{1,9},{5... | collective-permute-start | bytes 196616 | tf_op jit(solution)/shard_map/ppermute | solution.py:60
  27.0 2.7 %collective-permute-start.16 = (bf16[144,256]{1,0:T(8,128)(2,1)S(1)}, bf16[144,256]{1,0:T(8,128)(2,1)S(1)}, u32[]{:S(2)}, u32[]{:S(2)}) collective-permute-start(bf16[144,256]{1,0:T(8,128)(2,1)S(1)} %shard_map.130.refs_1_), channel_id=1, source_target_pairs={{0,2},{1,3},{2,0},{3,1},{4,6},{5,7},{6,4},{7,5},{8,10},{9,11},{10,... | collective-permute-start | bytes 221192 | tf_op jit(solution)/shard_map/ppermute | solution.py:75
  29.9 0.3 shard_map.120.turned_ref
  30.3 0.3 shard_map.125.own_ref.refs_2_
  30.6 2.6 %collective-permute-done.16.refs_0_ = bf16[144,256]{1,0:T(8,128)(2,1)S(1)} collective-permute-done((bf16[144,256]{1,0:T(8,128)(2,1)S(1)}, bf16[144,256]{1,0:T(8,128)(2,1)S(1)}, u32[]{:S(2)}, u32[]{:S(2)}) %collective-permute-start.16) | collective-permute-done | bytes 73760 | tf_op jit(solution)/shard_map/ppermute | solution.py:75
  33.2 0.6 %collective-permute-start.17 = (bf16[144,256]{1,0:T(8,128)(2,1)S(1)}, bf16[144,256]{1,0:T(8,128)(2,1)S(1)}, u32[]{:S(2)}, u32[]{:S(2)}) collective-permute-start(bf16[144,256]{1,0:T(8,128)(2,1)S(1)} %shard_map.131.refs_1_), channel_id=1, source_target_pairs={{0,8},{4,12},{8,0},{12,4},{16,24},{20,28},{24,16},{28,20},{1,9},{5... | collective-permute-start | bytes 221192 | tf_op jit(solution)/shard_map/ppermute | solution.py:75
  34.0 2.0 %collective-permute-start.12 = (bf16[128,256]{1,0:T(8,128)(2,1)S(1)}, bf16[128,256]{1,0:T(8,128)(2,1)S(1)}, u32[]{:S(2)}, u32[]{:S(2)}) collective-permute-start(bf16[128,256]{1,0:T(8,128)(2,1)S(1)} %shard_map.126), channel_id=1, source_target_pairs={{0,2},{1,3},{2,0},{3,1},{4,6},{5,7},{6,4},{7,5},{8,10},{9,11},{10,... | collective-permute-start | bytes 196616 | tf_op jit(solution)/shard_map/ppermute | solution.py:60
  36.3 1.3 %collective-permute-start.13 = (bf16[128,256]{1,0:T(8,128)(2,1)S(1)}, bf16[128,256]{1,0:T(8,128)(2,1)S(1)}, u32[]{:S(2)}, u32[]{:S(2)}) collective-permute-start(bf16[128,256]{1,0:T(8,128)(2,1)S(1)} %get-tuple-element.26), channel_id=1, source_target_pairs={{0,3},{1,2},{2,1},{3,0},{4,7},{5,6},{6,5},{7,4},{8,11},{9,10},{10,... | collective-permute-start | bytes 196616 | tf_op jit(solution)/shard_map/ppermute | solution.py:60
  37.7 1.6 %collective-permute-start.18 = (bf16[144,256]{1,0:T(8,128)(2,1)S(1)}, bf16[144,256]{1,0:T(8,128)(2,1)S(1)}, u32[]{:S(2)}, u32[]{:S(2)}) collective-permute-start(bf16[144,256]{1,0:T(8,128)(2,1)S(1)} %shard_map.132.refs_1_), channel_id=1, source_target_pairs={{0,16},{4,20},{8,24},{12,28},{16,0},{20,4},{24,8},{28,12},{1,17},{... | collective-permute-start | bytes 221192 | tf_op jit(solution)/shard_map/ppermute | solution.py:75
  39.2 0.6 %collective-permute-start.14 = (bf16[128,256]{1,0:T(8,128)(2,1)S(1)}, bf16[128,256]{1,0:T(8,128)(2,1)S(1)}, u32[]{:S(2)}, u32[]{:S(2)}) collective-permute-start(bf16[128,256]{1,0:T(8,128)(2,1)S(1)} %get-tuple-element.28), channel_id=1, source_target_pairs={{0,1},{1,0},{2,3},{3,2},{4,5},{5,4},{6,7},{7,6},{8,9},{9,8},{10,11... | collective-permute-start | bytes 196616 | tf_op jit(solution)/shard_map/ppermute | solution.py:60
  39.8 0.6 %shard_map.119 = bf16[128,256]{1,0:T(8,128)(2,1)} custom-call(bf16[128,256]{1,0:T(8,128)(2,1)S(1)} %get-tuple-element.23.in_ref), custom_call_target="tpu_custom_call" | custom-call | bytes 131072 | tf_op jit(solution)/shard_map/pallas_call | solution.py:448
  40.5 0.9 %collective-permute-done.12.refs_0_ = bf16[128,256]{1,0:T(8,128)(2,1)S(1)} collective-permute-done((bf16[128,256]{1,0:T(8,128)(2,1)S(1)}, bf16[128,256]{1,0:T(8,128)(2,1)S(1)}, u32[]{:S(2)}, u32[]{:S(2)}) %collective-permute-start.12) | collective-permute-done | bytes 65568 | tf_op jit(solution)/shard_map/ppermute | solution.py:60
  41.3 1.2 %collective-permute-done.13.refs_1_ = bf16[128,256]{1,0:T(8,128)(2,1)S(1)} collective-permute-done((bf16[128,256]{1,0:T(8,128)(2,1)S(1)}, bf16[128,256]{1,0:T(8,128)(2,1)S(1)}, u32[]{:S(2)}, u32[]{:S(2)}) %collective-permute-start.13) | collective-permute-done | bytes 65568 | tf_op jit(solution)/shard_map/ppermute | solution.py:60
  42.7 0.8 %collective-permute-done.14.last_ref = bf16[128,256]{1,0:T(8,128)(2,1)S(1)} collective-permute-done((bf16[128,256]{1,0:T(8,128)(2,1)S(1)}, bf16[128,256]{1,0:T(8,128)(2,1)S(1)}, u32[]{:S(2)}, u32[]{:S(2)}) %collective-permute-start.14) | collective-permute-done | bytes 65568 | tf_op jit(solution)/shard_map/ppermute | solution.py:60
  43.7 0.3 collective-permute-done.19.other_ref
  44.0 0.8 %shard_map.134 = (bf16[128,256]{1,0:T(8,128)(2,1)}, f32[256,256]{1,0:T(8,128)}, f32[1,256]{1,0:T(1,128)}) custom-call(bf16[128,256]{1,0:T(8,128)(2,1)S(1)} %shard_map.129.features_ref, f32[128,256]{1,0:T(8,128)S(1)} %get-tuple-element.29.own_ref, f32[128,256]{1,0:T(8,128)S(1)} %collective-permute-done.19.other_ref, f32[1,256]{1,0:T(1,128)S(1)} %get-tuple-element.30.bias_ref), custom_call_target="tpu_custom_call" | custom-call | bytes 524288 | tf_op jit(solution)/shard_map/pallas_call | solution.py:531
  (38 shorter events, 2.6 us)
Async XLA Ops:
  0.6 8.5 %collective-permute-start = (bf16[128,256]{1,0:T(8,128)(2,1)}, bf16[128,256]{1,0:T(8,128)(2,1)S(1)}, u32[]{:S(2)}, u32[]{:S(2)}) collective-permute-start(bf16[128,256]{1,0:T(8,128)(2,1)} %refs_3_.1), channel_id=1, source_target_pairs={{0,2},{1,3},{2,0},{3,1},{4,6},{5,7},{6,4},{7,5},{8,10},{9,11},{10,... | collective-permute-start | bytes 196616 | tf_op jit(solution)/shard_map/ppermute | solution.py:60
  4.7 6.4 %collective-permute-start.1 = (bf16[128,256]{1,0:T(8,128)(2,1)}, bf16[128,256]{1,0:T(8,128)(2,1)S(1)}, u32[]{:S(2)}, u32[]{:S(2)}) collective-permute-start(bf16[128,256]{1,0:T(8,128)(2,1)} %refs_3_.1), channel_id=1, source_target_pairs={{0,3},{1,2},{2,1},{3,0},{4,7},{5,6},{6,5},{7,4},{8,11},{9,10},{10,... | collective-permute-start | bytes 196616 | tf_op jit(solution)/shard_map/ppermute | solution.py:60
  6.1 5.2 %collective-permute-start.2 = (bf16[128,256]{1,0:T(8,128)(2,1)}, bf16[128,256]{1,0:T(8,128)(2,1)S(1)}, u32[]{:S(2)}, u32[]{:S(2)}) collective-permute-start(bf16[128,256]{1,0:T(8,128)(2,1)} %refs_3_.1), channel_id=1, source_target_pairs={{0,1},{1,0},{2,3},{3,2},{4,5},{5,4},{6,7},{7,6},{8,9},{9,8},{10,11... | collective-permute-start | bytes 196616 | tf_op jit(solution)/shard_map/ppermute | solution.py:60
  7.0 4.3 %copy-start.1 = (bf16[128,256]{1,0:T(8,128)(2,1)S(1)}, bf16[128,256]{1,0:T(8,128)(2,1)}, u32[]{:S(2)}) copy-start(bf16[128,256]{1,0:T(8,128)(2,1)} %refs_3_.1) | copy-start | bytes 196612
  11.6 1.6 %collective-permute-start.3 = (bf16[512,256]{1,0:T(8,128)(2,1)S(1)}, bf16[512,256]{1,0:T(8,128)(2,1)S(1)}, u32[]{:S(2)}, u32[]{:S(2)}) collective-permute-start(bf16[512,256]{1,0:T(8,128)(2,1)S(1)} %get-tuple-element.22), channel_id=1, source_target_pairs={{0,4},{4,0},{8,12},{12,8},{16,20},{20,16},{24,28},{28,24},{1,5},{5... | collective-permute-start | bytes 786440 | tf_op jit(solution)/shard_map/ppermute | solution.py:65
  13.2 5.2 %collective-permute-start.4 = (bf16[128,256]{1,0:T(8,128)(2,1)S(1)}, bf16[128,256]{1,0:T(8,128)(2,1)S(1)}, u32[]{:S(2)}, u32[]{:S(2)}) collective-permute-start(bf16[128,256]{1,0:T(8,128)(2,1)S(1)} %shard_map.114.refs_0_), channel_id=1, source_target_pairs={{0,24},{4,28},{8,16},{12,20},{16,8},{20,12},{24,0},{28,4},{1,25},{... | collective-permute-start | bytes 196616 | tf_op jit(solution)/shard_map/ppermute | solution.py:60
  15.7 4.3 %collective-permute-start.5 = (bf16[128,256]{1,0:T(8,128)(2,1)S(1)}, bf16[128,256]{1,0:T(8,128)(2,1)S(1)}, u32[]{:S(2)}, u32[]{:S(2)}) collective-permute-start(bf16[128,256]{1,0:T(8,128)(2,1)S(1)} %shard_map.115.refs_0_), channel_id=1, source_target_pairs={{0,16},{4,20},{8,24},{12,28},{16,0},{20,4},{24,8},{28,12},{1,17},{... | collective-permute-start | bytes 196616 | tf_op jit(solution)/shard_map/ppermute | solution.py:60
  16.3 4.4 %copy-start = (bf16[256,256]{1,0:T(8,128)(2,1)S(1)}, bf16[256,256]{1,0:T(8,128)(2,1)}, u32[]{:S(2)}) copy-start(bf16[256,256]{1,0:T(8,128)(2,1)} %weight_ref.3) | copy-start | bytes 393220
  16.4 4.3 %copy-start.2 = (bf16[128,256]{1,0:T(8,128)(2,1)S(1)}, bf16[128,256]{1,0:T(8,128)(2,1)}, u32[]{:S(2)}) copy-start(bf16[128,256]{1,0:T(8,128)(2,1)} %cot_ref.1) | copy-start | bytes 196612
  16.4 4.3 %collective-permute-start.6 = (bf16[128,256]{1,0:T(8,128)(2,1)S(1)}, bf16[128,256]{1,0:T(8,128)(2,1)S(1)}, u32[]{:S(2)}, u32[]{:S(2)}) collective-permute-start(bf16[128,256]{1,0:T(8,128)(2,1)S(1)} %shard_map.116.refs_0_), channel_id=1, source_target_pairs={{0,8},{4,12},{8,0},{12,4},{16,24},{20,28},{24,16},{28,20},{1,9},{5... | collective-permute-start | bytes 196616 | tf_op jit(solution)/shard_map/ppermute | solution.py:60
  21.2 1.3 %collective-permute-start.7 = (bf16[144,256]{1,0:T(8,128)(2,1)S(1)}, bf16[144,256]{1,0:T(8,128)(2,1)S(1)}, u32[]{:S(2)}, u32[]{:S(2)}) collective-permute-start(bf16[144,256]{1,0:T(8,128)(2,1)S(1)} %shard_map.121), channel_id=1, source_target_pairs={{0,4},{4,0},{8,12},{12,8},{16,20},{20,16},{24,28},{28,24},{1,5},{5... | collective-permute-start | bytes 221192 | tf_op jit(solution)/shard_map/ppermute | solution.py:65
  22.5 4.5 %collective-permute-start.15 = (bf16[144,256]{1,0:T(8,128)(2,1)S(1)}, bf16[144,256]{1,0:T(8,128)(2,1)S(1)}, u32[]{:S(2)}, u32[]{:S(2)}) collective-permute-start(bf16[144,256]{1,0:T(8,128)(2,1)S(1)} %shard_map.123.after_ref.refs_1_), channel_id=1, source_target_pairs={{0,1},{1,0},{2,3},{3,2},{4,5},{5,4},{6,7},{7,6},{8,9},{9,8},{10,11... | collective-permute-start | bytes 221192 | tf_op jit(solution)/shard_map/ppermute | solution.py:75
  23.5 6.2 %collective-permute-start.8 = (bf16[128,256]{1,0:T(8,128)(2,1)S(1)}, bf16[128,256]{1,0:T(8,128)(2,1)S(1)}, u32[]{:S(2)}, u32[]{:S(2)}) collective-permute-start(bf16[128,256]{1,0:T(8,128)(2,1)S(1)} %get-tuple-element.25.grad_ref.refs_3_), channel_id=1, source_target_pairs={{0,24},{4,28},{8,16},{12,20},{16,8},{20,12},{24,0},{28,4},{1,25},{... | collective-permute-start | bytes 196616 | tf_op jit(solution)/shard_map/ppermute | solution.py:60
  25.0 4.7 %collective-permute-start.9 = (bf16[128,256]{1,0:T(8,128)(2,1)S(1)}, bf16[128,256]{1,0:T(8,128)(2,1)S(1)}, u32[]{:S(2)}, u32[]{:S(2)}) collective-permute-start(bf16[128,256]{1,0:T(8,128)(2,1)S(1)} %get-tuple-element.25.grad_ref.refs_3_), channel_id=1, source_target_pairs={{0,16},{4,20},{8,24},{12,28},{16,0},{20,4},{24,8},{28,12},{1,17},{... | collective-permute-start | bytes 196616 | tf_op jit(solution)/shard_map/ppermute | solution.py:60
  25.5 4.3 %collective-permute-start.10 = (bf16[128,256]{1,0:T(8,128)(2,1)S(1)}, bf16[128,256]{1,0:T(8,128)(2,1)S(1)}, u32[]{:S(2)}, u32[]{:S(2)}) collective-permute-start(bf16[128,256]{1,0:T(8,128)(2,1)S(1)} %get-tuple-element.25.grad_ref.refs_3_), channel_id=1, source_target_pairs={{0,8},{4,12},{8,0},{12,4},{16,24},{20,28},{24,16},{28,20},{1,9},{5... | collective-permute-start | bytes 196616 | tf_op jit(solution)/shard_map/ppermute | solution.py:60
  27.0 6.1 %collective-permute-start.16 = (bf16[144,256]{1,0:T(8,128)(2,1)S(1)}, bf16[144,256]{1,0:T(8,128)(2,1)S(1)}, u32[]{:S(2)}, u32[]{:S(2)}) collective-permute-start(bf16[144,256]{1,0:T(8,128)(2,1)S(1)} %shard_map.130.refs_1_), channel_id=1, source_target_pairs={{0,2},{1,3},{2,0},{3,1},{4,6},{5,7},{6,4},{7,5},{8,10},{9,11},{10,... | collective-permute-start | bytes 221192 | tf_op jit(solution)/shard_map/ppermute | solution.py:75
  29.9 4.0 %collective-permute-start.11 = (bf16[512,256]{1,0:T(8,128)(2,1)S(1)}, bf16[512,256]{1,0:T(8,128)(2,1)S(1)}, u32[]{:S(2)}, u32[]{:S(2)}) collective-permute-start(bf16[512,256]{1,0:T(8,128)(2,1)S(1)} %shard_map.124.source_ref), channel_id=1, source_target_pairs={{0,4},{4,0},{8,12},{12,8},{16,20},{20,16},{24,28},{28,24},{1,5},{5... | collective-permute-start | bytes 786440 | tf_op jit(solution)/shard_map/ppermute | solution.py:65
  33.2 4.5 %collective-permute-start.17 = (bf16[144,256]{1,0:T(8,128)(2,1)S(1)}, bf16[144,256]{1,0:T(8,128)(2,1)S(1)}, u32[]{:S(2)}, u32[]{:S(2)}) collective-permute-start(bf16[144,256]{1,0:T(8,128)(2,1)S(1)} %shard_map.131.refs_1_), channel_id=1, source_target_pairs={{0,8},{4,12},{8,0},{12,4},{16,24},{20,28},{24,16},{28,20},{1,9},{5... | collective-permute-start | bytes 221192 | tf_op jit(solution)/shard_map/ppermute | solution.py:75
  34.0 7.3 %collective-permute-start.12 = (bf16[128,256]{1,0:T(8,128)(2,1)S(1)}, bf16[128,256]{1,0:T(8,128)(2,1)S(1)}, u32[]{:S(2)}, u32[]{:S(2)}) collective-permute-start(bf16[128,256]{1,0:T(8,128)(2,1)S(1)} %shard_map.126), channel_id=1, source_target_pairs={{0,2},{1,3},{2,0},{3,1},{4,6},{5,7},{6,4},{7,5},{8,10},{9,11},{10,... | collective-permute-start | bytes 196616 | tf_op jit(solution)/shard_map/ppermute | solution.py:60
  36.3 6.2 %collective-permute-start.13 = (bf16[128,256]{1,0:T(8,128)(2,1)S(1)}, bf16[128,256]{1,0:T(8,128)(2,1)S(1)}, u32[]{:S(2)}, u32[]{:S(2)}) collective-permute-start(bf16[128,256]{1,0:T(8,128)(2,1)S(1)} %get-tuple-element.26), channel_id=1, source_target_pairs={{0,3},{1,2},{2,1},{3,0},{4,7},{5,6},{6,5},{7,4},{8,11},{9,10},{10,... | collective-permute-start | bytes 196616 | tf_op jit(solution)/shard_map/ppermute | solution.py:60
  37.7 4.9 %collective-permute-start.18 = (bf16[144,256]{1,0:T(8,128)(2,1)S(1)}, bf16[144,256]{1,0:T(8,128)(2,1)S(1)}, u32[]{:S(2)}, u32[]{:S(2)}) collective-permute-start(bf16[144,256]{1,0:T(8,128)(2,1)S(1)} %shard_map.132.refs_1_), channel_id=1, source_target_pairs={{0,16},{4,20},{8,24},{12,28},{16,0},{20,4},{24,8},{28,12},{1,17},{... | collective-permute-start | bytes 221192 | tf_op jit(solution)/shard_map/ppermute | solution.py:75
  39.2 4.3 %collective-permute-start.14 = (bf16[128,256]{1,0:T(8,128)(2,1)S(1)}, bf16[128,256]{1,0:T(8,128)(2,1)S(1)}, u32[]{:S(2)}, u32[]{:S(2)}) collective-permute-start(bf16[128,256]{1,0:T(8,128)(2,1)S(1)} %get-tuple-element.28), channel_id=1, source_target_pairs={{0,1},{1,0},{2,3},{3,2},{4,5},{5,4},{6,7},{7,6},{8,9},{9,8},{10,11... | collective-permute-start | bytes 196616 | tf_op jit(solution)/shard_map/ppermute | solution.py:60
  42.6 1.4 %collective-permute-start.19 = (f32[128,256]{1,0:T(8,128)S(1)}, f32[128,256]{1,0:T(8,128)S(1)}, u32[]{:S(2)}, u32[]{:S(2)}) collective-permute-start(f32[128,256]{1,0:T(8,128)S(1)} %get-tuple-element.29.own_ref), channel_id=1, source_target_pairs={{0,4},{4,0},{8,12},{12,8},{16,20},{20,16},{24,28},{28,24},{1,5},{5... | collective-permute-start | bytes 393224 | tf_op jit(solution)/shard_map/ppermute | solution.py:65

commit v22 on v18

--- a/solution.py
+++ b/solution.py
@@ -41,7 +41,7 @@
 
 
 def far_first(count):
-    return list(range(count - 1, -1, -1))
+    return list(dict.fromkeys([count - 1, *range(1, count), 0]))
 
 
 def pairs_of(k, size, cores):
@@ -49,7 +49,7 @@
 
 
 def half_first(count):
-    return [count // 2] + [k for k in far_first(count) if k != count // 2]
+    return [count // 2] + [k for k in range(count - 1, -1, -1) if k != count // 2]
 
 
 def exchange(blocks, axis, size, cores=1, order=far_first):

time: 44.7 us -> 45.7 us (1.022)
  waiting for transfers between devices: 14 us -> 15.6 us
  Pallas kernels: 6.21 us -> 5.72 us
    ppermute x12, waiting for transfers between devices: 8.96 us -> 10.1 us  [exchange(): lax.ppermute(blocks[k], axis, pairs)]
    ppermute x4, waiting for transfers between devices: 2.4 us -> 2.92 us  [swap_cores(): return lax.ppermute(block, 'col', [(i, i ^ 1) for i in range(size)])]
    pallas_call x1, Pallas kernels: 2.13 us -> 1.64 us  [local(): call(dense_kernel, (like(row_nodes, col_nodes), like(1, hidden, F32)), [S...]
  transfers between devices with their start and end apart: 20 -> 20, of which waited for: 14 -> 14; matrix products, arithmetic and copies ran while one was open for 0% -> 0% of each run, Pallas kernels for 10% -> 9%
where the time goes in v22:
time: 45.7 us; the launch traced here: 45.6 us
  starting transfers between devices  22.8 us (50%)
  waiting for transfers between devices  15.6 us (34%)
  Pallas kernels  5.72 us (13%)
  between operations  1.47 us (3%)
    ppermute x12, starting transfers between devices, exchange(): lax.ppermute(blocks[k], axis, pairs)  16.7 us
    ppermute x12, waiting for transfers between devices, exchange(): lax.ppermute(blocks[k], axis, pairs)  10.1 us
    ppermute x4, starting transfers between devices, total_over(): terms = [lax.ppermute(block, axis, pairs_of(step, size, cores)), block]  5.82 us
    ppermute x4, waiting for transfers between devices, swap_cores(): return lax.ppermute(block, 'col', [(i, i ^ 1) for i in range(size)])  2.92 us
    ppermute x4, waiting for transfers between devices, total_over(): terms = [lax.ppermute(block, axis, pairs_of(step, size, cores)), block]  2.52 us
    pallas_call x1, Pallas kernels, local(): call(dense_kernel, (like(row_nodes, col_nodes), like(1, hidden, F32)), [S...  1.64 us
  transfers between devices with their start and end apart: 20, of which 14 were waited for; matrix products, arithmetic and copies ran while one was open for 0% of the time, Pallas kernels for 9%

profile of v22, /device:TPU:0, one launch (start us, length us, event | category | flops | bytes accessed | tf_op | source)
XLA Modules:
  0.0 45.6 jit_solution(8947572886276440577)
XLA Ops:
  0.6 4.1 %collective-permute-start = (bf16[128,256]{1,0:T(8,128)(2,1)}, bf16[128,256]{1,0:T(8,128)(2,1)S(1)}, u32[]{:S(2)}, u32[]{:S(2)}) collective-permute-start(bf16[128,256]{1,0:T(8,128)(2,1)} %refs_3_.1), channel_id=1, source_target_pairs={{0,2},{1,3},{2,0},{3,1},{4,6},{5,7},{6,4},{7,5},{8,10},{9,11},{10,... | collective-permute-start | bytes 196616 | tf_op jit(solution)/shard_map/ppermute | solution.py:60
  4.7 1.3 %collective-permute-start.1 = (bf16[128,256]{1,0:T(8,128)(2,1)}, bf16[128,256]{1,0:T(8,128)(2,1)S(1)}, u32[]{:S(2)}, u32[]{:S(2)}) collective-permute-start(bf16[128,256]{1,0:T(8,128)(2,1)} %refs_3_.1), channel_id=1, source_target_pairs={{0,3},{1,2},{2,1},{3,0},{4,7},{5,6},{6,5},{7,4},{8,11},{9,10},{10,... | collective-permute-start | bytes 196616 | tf_op jit(solution)/shard_map/ppermute | solution.py:60
  7.0 1.6 %shard_map.111 = (bf16[1024,512]{1,0:T(8,128)(2,1)S(1)}, f32[1,256]{1,0:T(1,128)S(1)}) custom-call(s32[1,1]{1,0:T(1,128)S(6)} %copy.12.count_ref, s32[1,1,32]{2,1,0:T(1,128)} %row_hbm.1, s32[1,1,32]{2,1,0:T(1,128)} %col_hbm.1, bf16[1,1,32,128,128]{4,3,2,1,0:T(8,128)(2,1)} %tiles_hbm.1, f32[1,256]{1,0:T(1,128)} %bitcast.2), custom_call_target="tpu_custom_call" | custom-call | bytes 6291456 | tf_op jit(solution)/shard_map/pallas_call | solution.py:362
  8.7 2.5 %collective-permute-done.1.refs_1_ = bf16[128,256]{1,0:T(8,128)(2,1)S(1)} collective-permute-done((bf16[128,256]{1,0:T(8,128)(2,1)}, bf16[128,256]{1,0:T(8,128)(2,1)S(1)}, u32[]{:S(2)}, u32[]{:S(2)}) %collective-permute-start.1) | collective-permute-done | bytes 65568 | tf_op jit(solution)/shard_map/ppermute | solution.py:60
  11.3 0.3 shard_map.112
  12.0 1.2 %collective-permute-done.3.other_ref = bf16[512,256]{1,0:T(8,128)(2,1)S(1)} collective-permute-done((bf16[512,256]{1,0:T(8,128)(2,1)S(1)}, bf16[512,256]{1,0:T(8,128)(2,1)S(1)}, u32[]{:S(2)}, u32[]{:S(2)}) %collective-permute-start.3) | collective-permute-done | bytes 262176 | tf_op jit(solution)/shard_map/ppermute | solution.py:65
  13.2 2.5 %collective-permute-start.4 = (bf16[128,256]{1,0:T(8,128)(2,1)S(1)}, bf16[128,256]{1,0:T(8,128)(2,1)S(1)}, u32[]{:S(2)}, u32[]{:S(2)}) collective-permute-start(bf16[128,256]{1,0:T(8,128)(2,1)S(1)} %shard_map.114.refs_0_), channel_id=1, source_target_pairs={{0,24},{4,28},{8,16},{12,20},{16,8},{20,12},{24,0},{28,4},{1,25},{... | collective-permute-start | bytes 196616 | tf_op jit(solution)/shard_map/ppermute | solution.py:60
  15.7 0.6 %collective-permute-start.5 = (bf16[128,256]{1,0:T(8,128)(2,1)S(1)}, bf16[128,256]{1,0:T(8,128)(2,1)S(1)}, u32[]{:S(2)}, u32[]{:S(2)}) collective-permute-start(bf16[128,256]{1,0:T(8,128)(2,1)S(1)} %shard_map.115.refs_0_), channel_id=1, source_target_pairs={{0,8},{4,12},{8,0},{12,4},{16,24},{20,28},{24,16},{28,20},{1,9},{5... | collective-permute-start | bytes 196616 | tf_op jit(solution)/shard_map/ppermute | solution.py:60
  16.4 0.6 %collective-permute-start.6 = (bf16[128,256]{1,0:T(8,128)(2,1)S(1)}, bf16[128,256]{1,0:T(8,128)(2,1)S(1)}, u32[]{:S(2)}, u32[]{:S(2)}) collective-permute-start(bf16[128,256]{1,0:T(8,128)(2,1)S(1)} %shard_map.116.refs_0_), channel_id=1, source_target_pairs={{0,16},{4,20},{8,24},{12,28},{16,0},{20,4},{24,8},{28,12},{1,17},{... | collective-permute-start | bytes 196616 | tf_op jit(solution)/shard_map/ppermute | solution.py:60
  17.0 1.8 %collective-permute-done.4.refs_0_ = bf16[128,256]{1,0:T(8,128)(2,1)S(1)} collective-permute-done((bf16[128,256]{1,0:T(8,128)(2,1)S(1)}, bf16[128,256]{1,0:T(8,128)(2,1)S(1)}, u32[]{:S(2)}, u32[]{:S(2)}) %collective-permute-start.4) | collective-permute-done | bytes 65568 | tf_op jit(solution)/shard_map/ppermute | solution.py:60
  18.8 1.3 %collective-permute-done.5.refs_1_ = bf16[128,256]{1,0:T(8,128)(2,1)S(1)} collective-permute-done((bf16[128,256]{1,0:T(8,128)(2,1)S(1)}, bf16[128,256]{1,0:T(8,128)(2,1)S(1)}, u32[]{:S(2)}, u32[]{:S(2)}) %collective-permute-start.5) | collective-permute-done | bytes 65568 | tf_op jit(solution)/shard_map/ppermute | solution.py:60
  20.1 0.6 %collective-permute-done.6.refs_2_ = bf16[128,256]{1,0:T(8,128)(2,1)S(1)} collective-permute-done((bf16[128,256]{1,0:T(8,128)(2,1)S(1)}, bf16[128,256]{1,0:T(8,128)(2,1)S(1)}, u32[]{:S(2)}, u32[]{:S(2)}) %collective-permute-start.6) | collective-permute-done | bytes 65568 | tf_op jit(solution)/shard_map/ppermute | solution.py:60
  21.5 1.0 %collective-permute-done.7.refs_0_ = bf16[144,256]{1,0:T(8,128)(2,1)S(1)} collective-permute-done((bf16[144,256]{1,0:T(8,128)(2,1)S(1)}, bf16[144,256]{1,0:T(8,128)(2,1)S(1)}, u32[]{:S(2)}, u32[]{:S(2)}) %collective-permute-start.7) | collective-permute-done | bytes 73760 | tf_op jit(solution)/shard_map/ppermute | solution.py:65
  22.6 1.0 %collective-permute-start.15 = (bf16[144,256]{1,0:T(8,128)(2,1)S(1)}, bf16[144,256]{1,0:T(8,128)(2,1)S(1)}, u32[]{:S(2)}, u32[]{:S(2)}) collective-permute-start(bf16[144,256]{1,0:T(8,128)(2,1)S(1)} %shard_map.123.after_ref.refs_1_), channel_id=1, source_target_pairs={{0,1},{1,0},{2,3},{3,2},{4,5},{5,4},{6,7},{7,6},{8,9},{9,8},{10,11... | collective-permute-start | bytes 221192 | tf_op jit(solution)/shard_map/ppermute | solution.py:75
  23.5 1.4 %collective-permute-start.8 = (bf16[128,256]{1,0:T(8,128)(2,1)S(1)}, bf16[128,256]{1,0:T(8,128)(2,1)S(1)}, u32[]{:S(2)}, u32[]{:S(2)}) collective-permute-start(bf16[128,256]{1,0:T(8,128)(2,1)S(1)} %get-tuple-element.26.grad_ref.refs_3_), channel_id=1, source_target_pairs={{0,24},{4,28},{8,16},{12,20},{16,8},{20,12},{24,0},{28,4},{1,25},{... | collective-permute-start | bytes 196616 | tf_op jit(solution)/shard_map/ppermute | solution.py:60
  25.0 0.5 %collective-permute-start.9 = (bf16[128,256]{1,0:T(8,128)(2,1)S(1)}, bf16[128,256]{1,0:T(8,128)(2,1)S(1)}, u32[]{:S(2)}, u32[]{:S(2)}) collective-permute-start(bf16[128,256]{1,0:T(8,128)(2,1)S(1)} %get-tuple-element.26.grad_ref.refs_3_), channel_id=1, source_target_pairs={{0,8},{4,12},{8,0},{12,4},{16,24},{20,28},{24,16},{28,20},{1,9},{5... | collective-permute-start | bytes 196616 | tf_op jit(solution)/shard_map/ppermute | solution.py:60
  25.5 1.5 %collective-permute-start.10 = (bf16[128,256]{1,0:T(8,128)(2,1)S(1)}, bf16[128,256]{1,0:T(8,128)(2,1)S(1)}, u32[]{:S(2)}, u32[]{:S(2)}) collective-permute-start(bf16[128,256]{1,0:T(8,128)(2,1)S(1)} %get-tuple-element.26.grad_ref.refs_3_), channel_id=1, source_target_pairs={{0,16},{4,20},{8,24},{12,28},{16,0},{20,4},{24,8},{28,12},{1,17},{... | collective-permute-start | bytes 196616 | tf_op jit(solution)/shard_map/ppermute | solution.py:60
  27.1 2.7 %collective-permute-start.16 = (bf16[144,256]{1,0:T(8,128)(2,1)S(1)}, bf16[144,256]{1,0:T(8,128)(2,1)S(1)}, u32[]{:S(2)}, u32[]{:S(2)}) collective-permute-start(bf16[144,256]{1,0:T(8,128)(2,1)S(1)} %shard_map.129.refs_1_), channel_id=1, source_target_pairs={{0,2},{1,3},{2,0},{3,1},{4,6},{5,7},{6,4},{7,5},{8,10},{9,11},{10,... | collective-permute-start | bytes 221192 | tf_op jit(solution)/shard_map/ppermute | solution.py:75
  30.0 0.3 shard_map.120.turned_ref
  30.7 2.5 %collective-permute-done.16.refs_0_ = bf16[144,256]{1,0:T(8,128)(2,1)S(1)} collective-permute-done((bf16[144,256]{1,0:T(8,128)(2,1)S(1)}, bf16[144,256]{1,0:T(8,128)(2,1)S(1)}, u32[]{:S(2)}, u32[]{:S(2)}) %collective-permute-start.16) | collective-permute-done | bytes 73760 | tf_op jit(solution)/shard_map/ppermute | solution.py:75
  33.2 1.6 %collective-permute-start.17 = (bf16[144,256]{1,0:T(8,128)(2,1)S(1)}, bf16[144,256]{1,0:T(8,128)(2,1)S(1)}, u32[]{:S(2)}, u32[]{:S(2)}) collective-permute-start(bf16[144,256]{1,0:T(8,128)(2,1)S(1)} %shard_map.130.refs_1_), channel_id=1, source_target_pairs={{0,8},{4,12},{8,0},{12,4},{16,24},{20,28},{24,16},{28,20},{1,9},{5... | collective-permute-start | bytes 221192 | tf_op jit(solution)/shard_map/ppermute | solution.py:75
  34.8 0.3 shard_map.126
  35.1 2.0 %collective-permute-start.12 = (bf16[128,256]{1,0:T(8,128)(2,1)S(1)}, bf16[128,256]{1,0:T(8,128)(2,1)S(1)}, u32[]{:S(2)}, u32[]{:S(2)}) collective-permute-start(bf16[128,256]{1,0:T(8,128)(2,1)S(1)} %get-tuple-element.27), channel_id=1, source_target_pairs={{0,2},{1,3},{2,0},{3,1},{4,6},{5,7},{6,4},{7,5},{8,10},{9,11},{10,... | collective-permute-start | bytes 196616 | tf_op jit(solution)/shard_map/ppermute | solution.py:60
  37.1 1.4 %collective-permute-start.13 = (bf16[128,256]{1,0:T(8,128)(2,1)S(1)}, bf16[128,256]{1,0:T(8,128)(2,1)S(1)}, u32[]{:S(2)}, u32[]{:S(2)}) collective-permute-start(bf16[128,256]{1,0:T(8,128)(2,1)S(1)} %get-tuple-element.28), channel_id=1, source_target_pairs={{0,3},{1,2},{2,1},{3,0},{4,7},{5,6},{6,5},{7,4},{8,11},{9,10},{10,... | collective-permute-start | bytes 196616 | tf_op jit(solution)/shard_map/ppermute | solution.py:60
  38.5 0.6 %collective-permute-start.18 = (bf16[144,256]{1,0:T(8,128)(2,1)S(1)}, bf16[144,256]{1,0:T(8,128)(2,1)S(1)}, u32[]{:S(2)}, u32[]{:S(2)}) collective-permute-start(bf16[144,256]{1,0:T(8,128)(2,1)S(1)} %shard_map.131.refs_1_), channel_id=1, source_target_pairs={{0,16},{4,20},{8,24},{12,28},{16,0},{20,4},{24,8},{28,12},{1,17},{... | collective-permute-start | bytes 221192 | tf_op jit(solution)/shard_map/ppermute | solution.py:75
  39.1 0.5 %collective-permute-start.14 = (bf16[128,256]{1,0:T(8,128)(2,1)S(1)}, bf16[128,256]{1,0:T(8,128)(2,1)S(1)}, u32[]{:S(2)}, u32[]{:S(2)}) collective-permute-start(bf16[128,256]{1,0:T(8,128)(2,1)S(1)} %get-tuple-element.30), channel_id=1, source_target_pairs={{0,1},{1,0},{2,3},{3,2},{4,5},{5,4},{6,7},{7,6},{8,9},{9,8},{10,11... | collective-permute-start | bytes 196616 | tf_op jit(solution)/shard_map/ppermute | solution.py:60
  39.6 0.6 %shard_map.119 = bf16[128,256]{1,0:T(8,128)(2,1)} custom-call(bf16[128,256]{1,0:T(8,128)(2,1)S(1)} %get-tuple-element.24.in_ref), custom_call_target="tpu_custom_call" | custom-call | bytes 131072 | tf_op jit(solution)/shard_map/pallas_call | solution.py:448
  40.2 1.4 %collective-permute-done.12.refs_0_ = bf16[128,256]{1,0:T(8,128)(2,1)S(1)} collective-permute-done((bf16[128,256]{1,0:T(8,128)(2,1)S(1)}, bf16[128,256]{1,0:T(8,128)(2,1)S(1)}, u32[]{:S(2)}, u32[]{:S(2)}) %collective-permute-start.12) | collective-permute-done | bytes 65568 | tf_op jit(solution)/shard_map/ppermute | solution.py:60
  41.6 1.7 %collective-permute-done.13.refs_1_ = bf16[128,256]{1,0:T(8,128)(2,1)S(1)} collective-permute-done((bf16[128,256]{1,0:T(8,128)(2,1)S(1)}, bf16[128,256]{1,0:T(8,128)(2,1)S(1)}, u32[]{:S(2)}, u32[]{:S(2)}) %collective-permute-start.13) | collective-permute-done | bytes 65568 | tf_op jit(solution)/shard_map/ppermute | solution.py:60
  43.5 0.5 %collective-permute-done.14.last_ref = bf16[128,256]{1,0:T(8,128)(2,1)S(1)} collective-permute-done((bf16[128,256]{1,0:T(8,128)(2,1)S(1)}, bf16[128,256]{1,0:T(8,128)(2,1)S(1)}, u32[]{:S(2)}, u32[]{:S(2)}) %collective-permute-start.14) | collective-permute-done | bytes 65568 | tf_op jit(solution)/shard_map/ppermute | solution.py:60
  44.2 0.6 %collective-permute-done.19.other_ref = f32[128,256]{1,0:T(8,128)S(1)} collective-permute-done((f32[128,256]{1,0:T(8,128)S(1)}, f32[128,256]{1,0:T(8,128)S(1)}, u32[]{:S(2)}, u32[]{:S(2)}) %collective-permute-start.19) | collective-permute-done | bytes 131104 | tf_op jit(solution)/shard_map/ppermute | solution.py:65
  44.8 0.8 %shard_map.133 = (bf16[128,256]{1,0:T(8,128)(2,1)}, f32[256,256]{1,0:T(8,128)}, f32[1,256]{1,0:T(1,128)}) custom-call(bf16[128,256]{1,0:T(8,128)(2,1)S(1)} %shard_map.128.features_ref, f32[128,256]{1,0:T(8,128)S(1)} %get-tuple-element.31.own_ref, f32[128,256]{1,0:T(8,128)S(1)} %collective-permute-done.19.other_ref, f32[1,256]{1,0:T(1,128)S(1)} %get-tuple-element.32.bias_ref), custom_call_target="tpu_custom_call" | custom-call | bytes 524288 | tf_op jit(solution)/shard_map/pallas_call | solution.py:529
  (37 shorter events, 2.5 us)
Async XLA Ops:
  0.6 8.1 %collective-permute-start = (bf16[128,256]{1,0:T(8,128)(2,1)}, bf16[128,256]{1,0:T(8,128)(2,1)S(1)}, u32[]{:S(2)}, u32[]{:S(2)}) collective-permute-start(bf16[128,256]{1,0:T(8,128)(2,1)} %refs_3_.1), channel_id=1, source_target_pairs={{0,2},{1,3},{2,0},{3,1},{4,6},{5,7},{6,4},{7,5},{8,10},{9,11},{10,... | collective-permute-start | bytes 196616 | tf_op jit(solution)/shard_map/ppermute | solution.py:60
  4.7 6.4 %collective-permute-start.1 = (bf16[128,256]{1,0:T(8,128)(2,1)}, bf16[128,256]{1,0:T(8,128)(2,1)S(1)}, u32[]{:S(2)}, u32[]{:S(2)}) collective-permute-start(bf16[128,256]{1,0:T(8,128)(2,1)} %refs_3_.1), channel_id=1, source_target_pairs={{0,3},{1,2},{2,1},{3,0},{4,7},{5,6},{6,5},{7,4},{8,11},{9,10},{10,... | collective-permute-start | bytes 196616 | tf_op jit(solution)/shard_map/ppermute | solution.py:60
  6.1 5.2 %collective-permute-start.2 = (bf16[128,256]{1,0:T(8,128)(2,1)}, bf16[128,256]{1,0:T(8,128)(2,1)S(1)}, u32[]{:S(2)}, u32[]{:S(2)}) collective-permute-start(bf16[128,256]{1,0:T(8,128)(2,1)} %refs_3_.1), channel_id=1, source_target_pairs={{0,1},{1,0},{2,3},{3,2},{4,5},{5,4},{6,7},{7,6},{8,9},{9,8},{10,11... | collective-permute-start | bytes 196616 | tf_op jit(solution)/shard_map/ppermute | solution.py:60
  7.0 4.3 %copy-start.1 = (bf16[128,256]{1,0:T(8,128)(2,1)S(1)}, bf16[128,256]{1,0:T(8,128)(2,1)}, u32[]{:S(2)}) copy-start(bf16[128,256]{1,0:T(8,128)(2,1)} %refs_3_.1) | copy-start | bytes 196612
  11.6 1.6 %collective-permute-start.3 = (bf16[512,256]{1,0:T(8,128)(2,1)S(1)}, bf16[512,256]{1,0:T(8,128)(2,1)S(1)}, u32[]{:S(2)}, u32[]{:S(2)}) collective-permute-start(bf16[512,256]{1,0:T(8,128)(2,1)S(1)} %get-tuple-element.23), channel_id=1, source_target_pairs={{0,4},{4,0},{8,12},{12,8},{16,20},{20,16},{24,28},{28,24},{1,5},{5... | collective-permute-start | bytes 786440 | tf_op jit(solution)/shard_map/ppermute | solution.py:65
  13.2 5.5 %collective-permute-start.4 = (bf16[128,256]{1,0:T(8,128)(2,1)S(1)}, bf16[128,256]{1,0:T(8,128)(2,1)S(1)}, u32[]{:S(2)}, u32[]{:S(2)}) collective-permute-start(bf16[128,256]{1,0:T(8,128)(2,1)S(1)} %shard_map.114.refs_0_), channel_id=1, source_target_pairs={{0,24},{4,28},{8,16},{12,20},{16,8},{20,12},{24,0},{28,4},{1,25},{... | collective-permute-start | bytes 196616 | tf_op jit(solution)/shard_map/ppermute | solution.py:60
  15.7 4.3 %collective-permute-start.5 = (bf16[128,256]{1,0:T(8,128)(2,1)S(1)}, bf16[128,256]{1,0:T(8,128)(2,1)S(1)}, u32[]{:S(2)}, u32[]{:S(2)}) collective-permute-start(bf16[128,256]{1,0:T(8,128)(2,1)S(1)} %shard_map.115.refs_0_), channel_id=1, source_target_pairs={{0,8},{4,12},{8,0},{12,4},{16,24},{20,28},{24,16},{28,20},{1,9},{5... | collective-permute-start | bytes 196616 | tf_op jit(solution)/shard_map/ppermute | solution.py:60
  16.4 4.4 %copy-start = (bf16[256,256]{1,0:T(8,128)(2,1)S(1)}, bf16[256,256]{1,0:T(8,128)(2,1)}, u32[]{:S(2)}) copy-start(bf16[256,256]{1,0:T(8,128)(2,1)} %weight_ref.3) | copy-start | bytes 393220
  16.4 4.3 %copy-start.2 = (bf16[128,256]{1,0:T(8,128)(2,1)S(1)}, bf16[128,256]{1,0:T(8,128)(2,1)}, u32[]{:S(2)}) copy-start(bf16[128,256]{1,0:T(8,128)(2,1)} %cot_ref.1) | copy-start | bytes 196612
  16.4 4.3 %collective-permute-start.6 = (bf16[128,256]{1,0:T(8,128)(2,1)S(1)}, bf16[128,256]{1,0:T(8,128)(2,1)S(1)}, u32[]{:S(2)}, u32[]{:S(2)}) collective-permute-start(bf16[128,256]{1,0:T(8,128)(2,1)S(1)} %shard_map.116.refs_0_), channel_id=1, source_target_pairs={{0,16},{4,20},{8,24},{12,28},{16,0},{20,4},{24,8},{28,12},{1,17},{... | collective-permute-start | bytes 196616 | tf_op jit(solution)/shard_map/ppermute | solution.py:60
  21.2 1.3 %collective-permute-start.7 = (bf16[144,256]{1,0:T(8,128)(2,1)S(1)}, bf16[144,256]{1,0:T(8,128)(2,1)S(1)}, u32[]{:S(2)}, u32[]{:S(2)}) collective-permute-start(bf16[144,256]{1,0:T(8,128)(2,1)S(1)} %shard_map.121), channel_id=1, source_target_pairs={{0,4},{4,0},{8,12},{12,8},{16,20},{20,16},{24,28},{28,24},{1,5},{5... | collective-permute-start | bytes 221192 | tf_op jit(solution)/shard_map/ppermute | solution.py:65
  22.6 4.5 %collective-permute-start.15 = (bf16[144,256]{1,0:T(8,128)(2,1)S(1)}, bf16[144,256]{1,0:T(8,128)(2,1)S(1)}, u32[]{:S(2)}, u32[]{:S(2)}) collective-permute-start(bf16[144,256]{1,0:T(8,128)(2,1)S(1)} %shard_map.123.after_ref.refs_1_), channel_id=1, source_target_pairs={{0,1},{1,0},{2,3},{3,2},{4,5},{5,4},{6,7},{7,6},{8,9},{9,8},{10,11... | collective-permute-start | bytes 221192 | tf_op jit(solution)/shard_map/ppermute | solution.py:75
  23.5 6.2 %collective-permute-start.8 = (bf16[128,256]{1,0:T(8,128)(2,1)S(1)}, bf16[128,256]{1,0:T(8,128)(2,1)S(1)}, u32[]{:S(2)}, u32[]{:S(2)}) collective-permute-start(bf16[128,256]{1,0:T(8,128)(2,1)S(1)} %get-tuple-element.26.grad_ref.refs_3_), channel_id=1, source_target_pairs={{0,24},{4,28},{8,16},{12,20},{16,8},{20,12},{24,0},{28,4},{1,25},{... | collective-permute-start | bytes 196616 | tf_op jit(solution)/shard_map/ppermute | solution.py:60
  25.0 4.8 %collective-permute-start.9 = (bf16[128,256]{1,0:T(8,128)(2,1)S(1)}, bf16[128,256]{1,0:T(8,128)(2,1)S(1)}, u32[]{:S(2)}, u32[]{:S(2)}) collective-permute-start(bf16[128,256]{1,0:T(8,128)(2,1)S(1)} %get-tuple-element.26.grad_ref.refs_3_), channel_id=1, source_target_pairs={{0,8},{4,12},{8,0},{12,4},{16,24},{20,28},{24,16},{28,20},{1,9},{5... | collective-permute-start | bytes 196616 | tf_op jit(solution)/shard_map/ppermute | solution.py:60
  25.5 4.4 %collective-permute-start.10 = (bf16[128,256]{1,0:T(8,128)(2,1)S(1)}, bf16[128,256]{1,0:T(8,128)(2,1)S(1)}, u32[]{:S(2)}, u32[]{:S(2)}) collective-permute-start(bf16[128,256]{1,0:T(8,128)(2,1)S(1)} %get-tuple-element.26.grad_ref.refs_3_), channel_id=1, source_target_pairs={{0,16},{4,20},{8,24},{12,28},{16,0},{20,4},{24,8},{28,12},{1,17},{... | collective-permute-start | bytes 196616 | tf_op jit(solution)/shard_map/ppermute | solution.py:60
  27.1 6.1 %collective-permute-start.16 = (bf16[144,256]{1,0:T(8,128)(2,1)S(1)}, bf16[144,256]{1,0:T(8,128)(2,1)S(1)}, u32[]{:S(2)}, u32[]{:S(2)}) collective-permute-start(bf16[144,256]{1,0:T(8,128)(2,1)S(1)} %shard_map.129.refs_1_), channel_id=1, source_target_pairs={{0,2},{1,3},{2,0},{3,1},{4,6},{5,7},{6,4},{7,5},{8,10},{9,11},{10,... | collective-permute-start | bytes 221192 | tf_op jit(solution)/shard_map/ppermute | solution.py:75
  29.9 4.8 %collective-permute-start.11 = (bf16[512,256]{1,0:T(8,128)(2,1)S(1)}, bf16[512,256]{1,0:T(8,128)(2,1)S(1)}, u32[]{:S(2)}, u32[]{:S(2)}) collective-permute-start(bf16[512,256]{1,0:T(8,128)(2,1)S(1)} %shard_map.124.source_ref), channel_id=1, source_target_pairs={{0,4},{4,0},{8,12},{12,8},{16,20},{20,16},{24,28},{28,24},{1,5},{5... | collective-permute-start | bytes 786440 | tf_op jit(solution)/shard_map/ppermute | solution.py:65
  33.2 5.3 %collective-permute-start.17 = (bf16[144,256]{1,0:T(8,128)(2,1)S(1)}, bf16[144,256]{1,0:T(8,128)(2,1)S(1)}, u32[]{:S(2)}, u32[]{:S(2)}) collective-permute-start(bf16[144,256]{1,0:T(8,128)(2,1)S(1)} %shard_map.130.refs_1_), channel_id=1, source_target_pairs={{0,8},{4,12},{8,0},{12,4},{16,24},{20,28},{24,16},{28,20},{1,9},{5... | collective-permute-start | bytes 221192 | tf_op jit(solution)/shard_map/ppermute | solution.py:75
  35.1 6.5 %collective-permute-start.12 = (bf16[128,256]{1,0:T(8,128)(2,1)S(1)}, bf16[128,256]{1,0:T(8,128)(2,1)S(1)}, u32[]{:S(2)}, u32[]{:S(2)}) collective-permute-start(bf16[128,256]{1,0:T(8,128)(2,1)S(1)} %get-tuple-element.27), channel_id=1, source_target_pairs={{0,2},{1,3},{2,0},{3,1},{4,6},{5,7},{6,4},{7,5},{8,10},{9,11},{10,... | collective-permute-start | bytes 196616 | tf_op jit(solution)/shard_map/ppermute | solution.py:60
  37.1 6.2 %collective-permute-start.13 = (bf16[128,256]{1,0:T(8,128)(2,1)S(1)}, bf16[128,256]{1,0:T(8,128)(2,1)S(1)}, u32[]{:S(2)}, u32[]{:S(2)}) collective-permute-start(bf16[128,256]{1,0:T(8,128)(2,1)S(1)} %get-tuple-element.28), channel_id=1, source_target_pairs={{0,3},{1,2},{2,1},{3,0},{4,7},{5,6},{6,5},{7,4},{8,11},{9,10},{10,... | collective-permute-start | bytes 196616 | tf_op jit(solution)/shard_map/ppermute | solution.py:60
  38.5 4.9 %collective-permute-start.18 = (bf16[144,256]{1,0:T(8,128)(2,1)S(1)}, bf16[144,256]{1,0:T(8,128)(2,1)S(1)}, u32[]{:S(2)}, u32[]{:S(2)}) collective-permute-start(bf16[144,256]{1,0:T(8,128)(2,1)S(1)} %shard_map.131.refs_1_), channel_id=1, source_target_pairs={{0,16},{4,20},{8,24},{12,28},{16,0},{20,4},{24,8},{28,12},{1,17},{... | collective-permute-start | bytes 221192 | tf_op jit(solution)/shard_map/ppermute | solution.py:75
  39.1 4.9 %collective-permute-start.14 = (bf16[128,256]{1,0:T(8,128)(2,1)S(1)}, bf16[128,256]{1,0:T(8,128)(2,1)S(1)}, u32[]{:S(2)}, u32[]{:S(2)}) collective-permute-start(bf16[128,256]{1,0:T(8,128)(2,1)S(1)} %get-tuple-element.30), channel_id=1, source_target_pairs={{0,1},{1,0},{2,3},{3,2},{4,5},{5,4},{6,7},{7,6},{8,9},{9,8},{10,11... | collective-permute-start | bytes 196616 | tf_op jit(solution)/shard_map/ppermute | solution.py:60
  43.4 1.4 %collective-permute-start.19 = (f32[128,256]{1,0:T(8,128)S(1)}, f32[128,256]{1,0:T(8,128)S(1)}, u32[]{:S(2)}, u32[]{:S(2)}) collective-permute-start(f32[128,256]{1,0:T(8,128)S(1)} %get-tuple-element.31.own_ref), channel_id=1, source_target_pairs={{0,4},{4,0},{8,12},{12,8},{16,20},{20,16},{24,28},{28,24},{1,5},{5... | collective-permute-start | bytes 393224 | tf_op jit(solution)/shard_map/ppermute | solution.py:65

commit v23 on v18

--- a/solution.py
+++ b/solution.py
@@ -189,7 +189,7 @@
 
 def forward_other_kernel(dense_ref, *refs):
     sources, (other_ref, source_ref) = refs[:-2], refs[-2:]
-    gather_sources(sources, source_ref, row_index(), half_first)
+    gather_sources(sources, source_ref, row_index(), far_first)
     half = other_ref.shape[0]
     other_ref[...] = dense_dot(dense_ref[half:, :], source_ref[...]).astype(BF16)
 
@@ -200,7 +200,7 @@
 
 def slot_forward_kernel(count_ref, row_ref, col_ref, tiles_ref, *refs):
     sources, (other_ref, own_ref, source_ref, acc_ref) = refs[:-4], refs[-4:]
-    gather_sources(sources, source_ref, row_index(), half_first)
+    gather_sources(sources, source_ref, row_index(), far_first)
     slot_product((count_ref, row_ref, col_ref, tiles_ref), source_ref, acc_ref, False)
     half = own_ref.shape[0]
     own_ref[...] = acc_ref[:half, :].astype(BF16)
@@ -386,7 +386,7 @@
         )
         slot_specs = [SMEM_SPEC] * 3 + [VMEM_SPEC]
 
-    sources = exchange([features] * n_row, "row", n_row, order=half_first)
+    sources = exchange([features] * n_row, "row", n_row)
     if is_dense:
         other, source = call(
             forward_other_kernel,

time: 44.7 us -> 45.1 us (level)
  waiting for transfers between devices: 14 us -> 16.1 us
  starting transfers between devices: 22.9 us -> 21.8 us
  Pallas kernels: 6.21 us -> 5.55 us
    ppermute x12, waiting for transfers between devices: 8.96 us -> 10.4 us  [exchange(): lax.ppermute(blocks[k], axis, pairs)]
    ppermute x4, waiting for transfers between devices: 2.66 us -> 3.49 us  [total_over(): terms = [lax.ppermute(block, axis, pairs_of(step, size, cores)), block]]
    ppermute x12, starting transfers between devices: 16.7 us -> 15.9 us  [exchange(): lax.ppermute(blocks[k], axis, pairs)]
    pallas_call x1, Pallas kernels: 2.13 us -> 1.45 us  [local(): call(dense_kernel, (like(row_nodes, col_nodes), like(1, hidden, F32)), [S...]
  transfers between devices with their start and end apart: 20 -> 20, of which waited for: 14 -> 15; matrix products, arithmetic and copies ran while one was open for 0% -> 0% of each run, Pallas kernels for 10% -> 9%
where the time goes in v23:
time: 45.1 us; the launch traced here: 44.9 us
  starting transfers between devices  21.8 us (48%)
  waiting for transfers between devices  16.1 us (36%)
  Pallas kernels  5.55 us (12%)
  between operations  1.46 us (3%)
    ppermute x12, starting transfers between devices, exchange(): lax.ppermute(blocks[k], axis, pairs)  15.9 us
    ppermute x12, waiting for transfers between devices, exchange(): lax.ppermute(blocks[k], axis, pairs)  10.4 us
    ppermute x4, starting transfers between devices, total_over(): terms = [lax.ppermute(block, axis, pairs_of(step, size, cores)), block]  5.62 us
    ppermute x4, waiting for transfers between devices, total_over(): terms = [lax.ppermute(block, axis, pairs_of(step, size, cores)), block]  3.49 us
    ppermute x4, waiting for transfers between devices, swap_cores(): return lax.ppermute(block, 'col', [(i, i ^ 1) for i in range(size)])  2.27 us
    pallas_call x1, Pallas kernels, local(): call(dense_kernel, (like(row_nodes, col_nodes), like(1, hidden, F32)), [S...  1.45 us
  transfers between devices with their start and end apart: 20, of which 15 were waited for; matrix products, arithmetic and copies ran while one was open for 0% of the time, Pallas kernels for 9%

profile of v23, /device:TPU:0, one launch (start us, length us, event | category | flops | bytes accessed | tf_op | source)
XLA Modules:
  0.0 44.9 jit_solution(10092720529330789978)
XLA Ops:
  0.6 5.1 %collective-permute-start = (bf16[128,256]{1,0:T(8,128)(2,1)}, bf16[128,256]{1,0:T(8,128)(2,1)S(1)}, u32[]{:S(2)}, u32[]{:S(2)}) collective-permute-start(bf16[128,256]{1,0:T(8,128)(2,1)} %refs_3_.1), channel_id=1, source_target_pairs={{0,3},{1,2},{2,1},{3,0},{4,7},{5,6},{6,5},{7,4},{8,11},{9,10},{10,... | collective-permute-start | bytes 196616 | tf_op jit(solution)/shard_map/ppermute | solution.py:60
  5.8 0.6 %collective-permute-start.2 = (bf16[128,256]{1,0:T(8,128)(2,1)}, bf16[128,256]{1,0:T(8,128)(2,1)S(1)}, u32[]{:S(2)}, u32[]{:S(2)}) collective-permute-start(bf16[128,256]{1,0:T(8,128)(2,1)} %refs_3_.1), channel_id=1, source_target_pairs={{0,1},{1,0},{2,3},{3,2},{4,5},{5,4},{6,7},{7,6},{8,9},{9,8},{10,11... | collective-permute-start | bytes 196616 | tf_op jit(solution)/shard_map/ppermute | solution.py:60
  7.1 1.5 %shard_map.111 = (bf16[1024,512]{1,0:T(8,128)(2,1)S(1)}, f32[1,256]{1,0:T(1,128)S(1)}) custom-call(s32[1,1]{1,0:T(1,128)S(6)} %copy.12.count_ref, s32[1,1,32]{2,1,0:T(1,128)} %row_hbm.1, s32[1,1,32]{2,1,0:T(1,128)} %col_hbm.1, bf16[1,1,32,128,128]{4,3,2,1,0:T(8,128)(2,1)} %tiles_hbm.1, f32[1,256]{1,0:T(1,128)} %bitcast.2), custom_call_target="tpu_custom_call" | custom-call | bytes 6291456 | tf_op jit(solution)/shard_map/pallas_call | solution.py:362
  8.6 3.0 %collective-permute-done.1.refs_1_ = bf16[128,256]{1,0:T(8,128)(2,1)S(1)} collective-permute-done((bf16[128,256]{1,0:T(8,128)(2,1)}, bf16[128,256]{1,0:T(8,128)(2,1)S(1)}, u32[]{:S(2)}, u32[]{:S(2)}) %collective-permute-start.1) | collective-permute-done | bytes 65568 | tf_op jit(solution)/shard_map/ppermute | solution.py:60
  11.6 0.3 shard_map.112
  12.3 1.2 %collective-permute-done.3.other_ref = bf16[512,256]{1,0:T(8,128)(2,1)S(1)} collective-permute-done((bf16[512,256]{1,0:T(8,128)(2,1)S(1)}, bf16[512,256]{1,0:T(8,128)(2,1)S(1)}, u32[]{:S(2)}, u32[]{:S(2)}) %collective-permute-start.3) | collective-permute-done | bytes 262176 | tf_op jit(solution)/shard_map/ppermute | solution.py:65
  13.5 2.5 %collective-permute-start.4 = (bf16[128,256]{1,0:T(8,128)(2,1)S(1)}, bf16[128,256]{1,0:T(8,128)(2,1)S(1)}, u32[]{:S(2)}, u32[]{:S(2)}) collective-permute-start(bf16[128,256]{1,0:T(8,128)(2,1)S(1)} %shard_map.114.refs_0_), channel_id=1, source_target_pairs={{0,24},{4,28},{8,16},{12,20},{16,8},{20,12},{24,0},{28,4},{1,25},{... | collective-permute-start | bytes 196616 | tf_op jit(solution)/shard_map/ppermute | solution.py:60
  16.1 0.6 %collective-permute-start.5 = (bf16[128,256]{1,0:T(8,128)(2,1)S(1)}, bf16[128,256]{1,0:T(8,128)(2,1)S(1)}, u32[]{:S(2)}, u32[]{:S(2)}) collective-permute-start(bf16[128,256]{1,0:T(8,128)(2,1)S(1)} %shard_map.115.refs_0_), channel_id=1, source_target_pairs={{0,16},{4,20},{8,24},{12,28},{16,0},{20,4},{24,8},{28,12},{1,17},{... | collective-permute-start | bytes 196616 | tf_op jit(solution)/shard_map/ppermute | solution.py:60
  16.7 0.6 %collective-permute-start.6 = (bf16[128,256]{1,0:T(8,128)(2,1)S(1)}, bf16[128,256]{1,0:T(8,128)(2,1)S(1)}, u32[]{:S(2)}, u32[]{:S(2)}) collective-permute-start(bf16[128,256]{1,0:T(8,128)(2,1)S(1)} %shard_map.116.refs_0_), channel_id=1, source_target_pairs={{0,8},{4,12},{8,0},{12,4},{16,24},{20,28},{24,16},{28,20},{1,9},{5... | collective-permute-start | bytes 196616 | tf_op jit(solution)/shard_map/ppermute | solution.py:60
  17.3 1.5 %collective-permute-done.4.refs_0_ = bf16[128,256]{1,0:T(8,128)(2,1)S(1)} collective-permute-done((bf16[128,256]{1,0:T(8,128)(2,1)S(1)}, bf16[128,256]{1,0:T(8,128)(2,1)S(1)}, u32[]{:S(2)}, u32[]{:S(2)}) %collective-permute-start.4) | collective-permute-done | bytes 65568 | tf_op jit(solution)/shard_map/ppermute | solution.py:60
  18.8 1.6 %collective-permute-done.5.refs_1_ = bf16[128,256]{1,0:T(8,128)(2,1)S(1)} collective-permute-done((bf16[128,256]{1,0:T(8,128)(2,1)S(1)}, bf16[128,256]{1,0:T(8,128)(2,1)S(1)}, u32[]{:S(2)}, u32[]{:S(2)}) %collective-permute-start.5) | collective-permute-done | bytes 65568 | tf_op jit(solution)/shard_map/ppermute | solution.py:60
  20.4 0.6 %collective-permute-done.6.refs_2_ = bf16[128,256]{1,0:T(8,128)(2,1)S(1)} collective-permute-done((bf16[128,256]{1,0:T(8,128)(2,1)S(1)}, bf16[128,256]{1,0:T(8,128)(2,1)S(1)}, u32[]{:S(2)}, u32[]{:S(2)}) %collective-permute-start.6) | collective-permute-done | bytes 65568 | tf_op jit(solution)/shard_map/ppermute | solution.py:60
  21.8 1.0 %collective-permute-done.7.refs_0_ = bf16[144,256]{1,0:T(8,128)(2,1)S(1)} collective-permute-done((bf16[144,256]{1,0:T(8,128)(2,1)S(1)}, bf16[144,256]{1,0:T(8,128)(2,1)S(1)}, u32[]{:S(2)}, u32[]{:S(2)}) %collective-permute-start.7) | collective-permute-done | bytes 73760 | tf_op jit(solution)/shard_map/ppermute | solution.py:65
  22.8 1.1 %collective-permute-start.15 = (bf16[144,256]{1,0:T(8,128)(2,1)S(1)}, bf16[144,256]{1,0:T(8,128)(2,1)S(1)}, u32[]{:S(2)}, u32[]{:S(2)}) collective-permute-start(bf16[144,256]{1,0:T(8,128)(2,1)S(1)} %shard_map.123.after_ref.refs_1_), channel_id=1, source_target_pairs={{0,1},{1,0},{2,3},{3,2},{4,5},{5,4},{6,7},{7,6},{8,9},{9,8},{10,11... | collective-permute-start | bytes 221192 | tf_op jit(solution)/shard_map/ppermute | solution.py:75
  24.0 1.5 %collective-permute-start.8 = (bf16[128,256]{1,0:T(8,128)(2,1)S(1)}, bf16[128,256]{1,0:T(8,128)(2,1)S(1)}, u32[]{:S(2)}, u32[]{:S(2)}) collective-permute-start(bf16[128,256]{1,0:T(8,128)(2,1)S(1)} %get-tuple-element.26.grad_ref.refs_3_), channel_id=1, source_target_pairs={{0,24},{4,28},{8,16},{12,20},{16,8},{20,12},{24,0},{28,4},{1,25},{... | collective-permute-start | bytes 196616 | tf_op jit(solution)/shard_map/ppermute | solution.py:60
  25.5 0.5 %collective-permute-start.9 = (bf16[128,256]{1,0:T(8,128)(2,1)S(1)}, bf16[128,256]{1,0:T(8,128)(2,1)S(1)}, u32[]{:S(2)}, u32[]{:S(2)}) collective-permute-start(bf16[128,256]{1,0:T(8,128)(2,1)S(1)} %get-tuple-element.26.grad_ref.refs_3_), channel_id=1, source_target_pairs={{0,16},{4,20},{8,24},{12,28},{16,0},{20,4},{24,8},{28,12},{1,17},{... | collective-permute-start | bytes 196616 | tf_op jit(solution)/shard_map/ppermute | solution.py:60
  26.0 1.5 %collective-permute-start.10 = (bf16[128,256]{1,0:T(8,128)(2,1)S(1)}, bf16[128,256]{1,0:T(8,128)(2,1)S(1)}, u32[]{:S(2)}, u32[]{:S(2)}) collective-permute-start(bf16[128,256]{1,0:T(8,128)(2,1)S(1)} %get-tuple-element.26.grad_ref.refs_3_), channel_id=1, source_target_pairs={{0,8},{4,12},{8,0},{12,4},{16,24},{20,28},{24,16},{28,20},{1,9},{5... | collective-permute-start | bytes 196616 | tf_op jit(solution)/shard_map/ppermute | solution.py:60
  27.5 2.3 %collective-permute-start.16 = (bf16[144,256]{1,0:T(8,128)(2,1)S(1)}, bf16[144,256]{1,0:T(8,128)(2,1)S(1)}, u32[]{:S(2)}, u32[]{:S(2)}) collective-permute-start(bf16[144,256]{1,0:T(8,128)(2,1)S(1)} %shard_map.129.refs_1_), channel_id=1, source_target_pairs={{0,2},{1,3},{2,0},{3,1},{4,6},{5,7},{6,4},{7,5},{8,10},{9,11},{10,... | collective-permute-start | bytes 221192 | tf_op jit(solution)/shard_map/ppermute | solution.py:75
  29.8 0.4 collective-permute-done.9.refs_1_
  30.4 0.3 shard_map.120.turned_ref
  31.1 2.6 %collective-permute-done.16.refs_0_ = bf16[144,256]{1,0:T(8,128)(2,1)S(1)} collective-permute-done((bf16[144,256]{1,0:T(8,128)(2,1)S(1)}, bf16[144,256]{1,0:T(8,128)(2,1)S(1)}, u32[]{:S(2)}, u32[]{:S(2)}) %collective-permute-start.16) | collective-permute-done | bytes 73760 | tf_op jit(solution)/shard_map/ppermute | solution.py:75
  33.6 0.6 %collective-permute-start.17 = (bf16[144,256]{1,0:T(8,128)(2,1)S(1)}, bf16[144,256]{1,0:T(8,128)(2,1)S(1)}, u32[]{:S(2)}, u32[]{:S(2)}) collective-permute-start(bf16[144,256]{1,0:T(8,128)(2,1)S(1)} %shard_map.130.refs_1_), channel_id=1, source_target_pairs={{0,8},{4,12},{8,0},{12,4},{16,24},{20,28},{24,16},{28,20},{1,9},{5... | collective-permute-start | bytes 221192 | tf_op jit(solution)/shard_map/ppermute | solution.py:75
  34.3 0.3 shard_map.126
  34.6 1.6 %collective-permute-start.12 = (bf16[128,256]{1,0:T(8,128)(2,1)S(1)}, bf16[128,256]{1,0:T(8,128)(2,1)S(1)}, u32[]{:S(2)}, u32[]{:S(2)}) collective-permute-start(bf16[128,256]{1,0:T(8,128)(2,1)S(1)} %get-tuple-element.27), channel_id=1, source_target_pairs={{0,2},{1,3},{2,0},{3,1},{4,6},{5,7},{6,4},{7,5},{8,10},{9,11},{10,... | collective-permute-start | bytes 196616 | tf_op jit(solution)/shard_map/ppermute | solution.py:60
  36.2 1.1 %collective-permute-start.13 = (bf16[128,256]{1,0:T(8,128)(2,1)S(1)}, bf16[128,256]{1,0:T(8,128)(2,1)S(1)}, u32[]{:S(2)}, u32[]{:S(2)}) collective-permute-start(bf16[128,256]{1,0:T(8,128)(2,1)S(1)} %get-tuple-element.28), channel_id=1, source_target_pairs={{0,3},{1,2},{2,1},{3,0},{4,7},{5,6},{6,5},{7,4},{8,11},{9,10},{10,... | collective-permute-start | bytes 196616 | tf_op jit(solution)/shard_map/ppermute | solution.py:60
  37.3 0.8 %collective-permute-done.17.refs_0_ = bf16[144,256]{1,0:T(8,128)(2,1)S(1)} collective-permute-done((bf16[144,256]{1,0:T(8,128)(2,1)S(1)}, bf16[144,256]{1,0:T(8,128)(2,1)S(1)}, u32[]{:S(2)}, u32[]{:S(2)}) %collective-permute-start.17) | collective-permute-done | bytes 73760 | tf_op jit(solution)/shard_map/ppermute | solution.py:75
  38.1 1.6 %collective-permute-start.18 = (bf16[144,256]{1,0:T(8,128)(2,1)S(1)}, bf16[144,256]{1,0:T(8,128)(2,1)S(1)}, u32[]{:S(2)}, u32[]{:S(2)}) collective-permute-start(bf16[144,256]{1,0:T(8,128)(2,1)S(1)} %shard_map.131.refs_1_), channel_id=1, source_target_pairs={{0,16},{4,20},{8,24},{12,28},{16,0},{20,4},{24,8},{28,12},{1,17},{... | collective-permute-start | bytes 221192 | tf_op jit(solution)/shard_map/ppermute | solution.py:75
  39.9 0.6 %shard_map.119 = bf16[128,256]{1,0:T(8,128)(2,1)} custom-call(bf16[128,256]{1,0:T(8,128)(2,1)S(1)} %get-tuple-element.24.in_ref), custom_call_target="tpu_custom_call" | custom-call | bytes 131072 | tf_op jit(solution)/shard_map/pallas_call | solution.py:448
  40.6 0.5 %collective-permute-done.12.refs_0_ = bf16[128,256]{1,0:T(8,128)(2,1)S(1)} collective-permute-done((bf16[128,256]{1,0:T(8,128)(2,1)S(1)}, bf16[128,256]{1,0:T(8,128)(2,1)S(1)}, u32[]{:S(2)}, u32[]{:S(2)}) %collective-permute-start.12) | collective-permute-done | bytes 65568 | tf_op jit(solution)/shard_map/ppermute | solution.py:60
  41.0 1.3 %collective-permute-done.13.refs_1_ = bf16[128,256]{1,0:T(8,128)(2,1)S(1)} collective-permute-done((bf16[128,256]{1,0:T(8,128)(2,1)S(1)}, bf16[128,256]{1,0:T(8,128)(2,1)S(1)}, u32[]{:S(2)}, u32[]{:S(2)}) %collective-permute-start.13) | collective-permute-done | bytes 65568 | tf_op jit(solution)/shard_map/ppermute | solution.py:60
  42.6 1.3 %collective-permute-done.14.last_ref = bf16[128,256]{1,0:T(8,128)(2,1)S(1)} collective-permute-done((bf16[128,256]{1,0:T(8,128)(2,1)S(1)}, bf16[128,256]{1,0:T(8,128)(2,1)S(1)}, u32[]{:S(2)}, u32[]{:S(2)}) %collective-permute-start.14) | collective-permute-done | bytes 65568 | tf_op jit(solution)/shard_map/ppermute | solution.py:60
  44.2 0.8 %shard_map.133 = (bf16[128,256]{1,0:T(8,128)(2,1)}, f32[256,256]{1,0:T(8,128)}, f32[1,256]{1,0:T(1,128)}) custom-call(bf16[128,256]{1,0:T(8,128)(2,1)S(1)} %shard_map.128.features_ref, f32[128,256]{1,0:T(8,128)S(1)} %get-tuple-element.31.own_ref, f32[128,256]{1,0:T(8,128)S(1)} %collective-permute-done.19.other_ref, f32[1,256]{1,0:T(1,128)S(1)} %get-tuple-element.32.bias_ref), custom_call_target="tpu_custom_call" | custom-call | bytes 524288 | tf_op jit(solution)/shard_map/pallas_call | solution.py:529
  (37 shorter events, 2.6 us)
Async XLA Ops:
  0.6 7.9 %collective-permute-start = (bf16[128,256]{1,0:T(8,128)(2,1)}, bf16[128,256]{1,0:T(8,128)(2,1)S(1)}, u32[]{:S(2)}, u32[]{:S(2)}) collective-permute-start(bf16[128,256]{1,0:T(8,128)(2,1)} %refs_3_.1), channel_id=1, source_target_pairs={{0,3},{1,2},{2,1},{3,0},{4,7},{5,6},{6,5},{7,4},{8,11},{9,10},{10,... | collective-permute-start | bytes 196616 | tf_op jit(solution)/shard_map/ppermute | solution.py:60
  5.7 5.8 %collective-permute-start.1 = (bf16[128,256]{1,0:T(8,128)(2,1)}, bf16[128,256]{1,0:T(8,128)(2,1)S(1)}, u32[]{:S(2)}, u32[]{:S(2)}) collective-permute-start(bf16[128,256]{1,0:T(8,128)(2,1)} %refs_3_.1), channel_id=1, source_target_pairs={{0,2},{1,3},{2,0},{3,1},{4,6},{5,7},{6,4},{7,5},{8,10},{9,11},{10,... | collective-permute-start | bytes 196616 | tf_op jit(solution)/shard_map/ppermute | solution.py:60
  5.8 5.8 %collective-permute-start.2 = (bf16[128,256]{1,0:T(8,128)(2,1)}, bf16[128,256]{1,0:T(8,128)(2,1)S(1)}, u32[]{:S(2)}, u32[]{:S(2)}) collective-permute-start(bf16[128,256]{1,0:T(8,128)(2,1)} %refs_3_.1), channel_id=1, source_target_pairs={{0,1},{1,0},{2,3},{3,2},{4,5},{5,4},{6,7},{7,6},{8,9},{9,8},{10,11... | collective-permute-start | bytes 196616 | tf_op jit(solution)/shard_map/ppermute | solution.py:60
  7.0 4.5 %copy-start.1 = (bf16[128,256]{1,0:T(8,128)(2,1)S(1)}, bf16[128,256]{1,0:T(8,128)(2,1)}, u32[]{:S(2)}) copy-start(bf16[128,256]{1,0:T(8,128)(2,1)} %refs_3_.1) | copy-start | bytes 196612
  11.9 1.6 %collective-permute-start.3 = (bf16[512,256]{1,0:T(8,128)(2,1)S(1)}, bf16[512,256]{1,0:T(8,128)(2,1)S(1)}, u32[]{:S(2)}, u32[]{:S(2)}) collective-permute-start(bf16[512,256]{1,0:T(8,128)(2,1)S(1)} %get-tuple-element.23), channel_id=1, source_target_pairs={{0,4},{4,0},{8,12},{12,8},{16,20},{20,16},{24,28},{28,24},{1,5},{5... | collective-permute-start | bytes 786440 | tf_op jit(solution)/shard_map/ppermute | solution.py:65
  13.5 5.2 %collective-permute-start.4 = (bf16[128,256]{1,0:T(8,128)(2,1)S(1)}, bf16[128,256]{1,0:T(8,128)(2,1)S(1)}, u32[]{:S(2)}, u32[]{:S(2)}) collective-permute-start(bf16[128,256]{1,0:T(8,128)(2,1)S(1)} %shard_map.114.refs_0_), channel_id=1, source_target_pairs={{0,24},{4,28},{8,16},{12,20},{16,8},{20,12},{24,0},{28,4},{1,25},{... | collective-permute-start | bytes 196616 | tf_op jit(solution)/shard_map/ppermute | solution.py:60
  16.1 4.3 %collective-permute-start.5 = (bf16[128,256]{1,0:T(8,128)(2,1)S(1)}, bf16[128,256]{1,0:T(8,128)(2,1)S(1)}, u32[]{:S(2)}, u32[]{:S(2)}) collective-permute-start(bf16[128,256]{1,0:T(8,128)(2,1)S(1)} %shard_map.115.refs_0_), channel_id=1, source_target_pairs={{0,16},{4,20},{8,24},{12,28},{16,0},{20,4},{24,8},{28,12},{1,17},{... | collective-permute-start | bytes 196616 | tf_op jit(solution)/shard_map/ppermute | solution.py:60
  16.6 4.4 %copy-start = (bf16[256,256]{1,0:T(8,128)(2,1)S(1)}, bf16[256,256]{1,0:T(8,128)(2,1)}, u32[]{:S(2)}) copy-start(bf16[256,256]{1,0:T(8,128)(2,1)} %weight_ref.3) | copy-start | bytes 393220
  16.7 4.3 %copy-start.2 = (bf16[128,256]{1,0:T(8,128)(2,1)S(1)}, bf16[128,256]{1,0:T(8,128)(2,1)}, u32[]{:S(2)}) copy-start(bf16[128,256]{1,0:T(8,128)(2,1)} %cot_ref.1) | copy-start | bytes 196612
  16.7 4.3 %collective-permute-start.6 = (bf16[128,256]{1,0:T(8,128)(2,1)S(1)}, bf16[128,256]{1,0:T(8,128)(2,1)S(1)}, u32[]{:S(2)}, u32[]{:S(2)}) collective-permute-start(bf16[128,256]{1,0:T(8,128)(2,1)S(1)} %shard_map.116.refs_0_), channel_id=1, source_target_pairs={{0,8},{4,12},{8,0},{12,4},{16,24},{20,28},{24,16},{28,20},{1,9},{5... | collective-permute-start | bytes 196616 | tf_op jit(solution)/shard_map/ppermute | solution.py:60
  21.5 1.3 %collective-permute-start.7 = (bf16[144,256]{1,0:T(8,128)(2,1)S(1)}, bf16[144,256]{1,0:T(8,128)(2,1)S(1)}, u32[]{:S(2)}, u32[]{:S(2)}) collective-permute-start(bf16[144,256]{1,0:T(8,128)(2,1)S(1)} %shard_map.121), channel_id=1, source_target_pairs={{0,4},{4,0},{8,12},{12,8},{16,20},{20,16},{24,28},{28,24},{1,5},{5... | collective-permute-start | bytes 221192 | tf_op jit(solution)/shard_map/ppermute | solution.py:65
  22.8 4.6 %collective-permute-start.15 = (bf16[144,256]{1,0:T(8,128)(2,1)S(1)}, bf16[144,256]{1,0:T(8,128)(2,1)S(1)}, u32[]{:S(2)}, u32[]{:S(2)}) collective-permute-start(bf16[144,256]{1,0:T(8,128)(2,1)S(1)} %shard_map.123.after_ref.refs_1_), channel_id=1, source_target_pairs={{0,1},{1,0},{2,3},{3,2},{4,5},{5,4},{6,7},{7,6},{8,9},{9,8},{10,11... | collective-permute-start | bytes 221192 | tf_op jit(solution)/shard_map/ppermute | solution.py:75
  24.0 5.8 %collective-permute-start.8 = (bf16[128,256]{1,0:T(8,128)(2,1)S(1)}, bf16[128,256]{1,0:T(8,128)(2,1)S(1)}, u32[]{:S(2)}, u32[]{:S(2)}) collective-permute-start(bf16[128,256]{1,0:T(8,128)(2,1)S(1)} %get-tuple-element.26.grad_ref.refs_3_), channel_id=1, source_target_pairs={{0,24},{4,28},{8,16},{12,20},{16,8},{20,12},{24,0},{28,4},{1,25},{... | collective-permute-start | bytes 196616 | tf_op jit(solution)/shard_map/ppermute | solution.py:60
  25.5 4.7 %collective-permute-start.9 = (bf16[128,256]{1,0:T(8,128)(2,1)S(1)}, bf16[128,256]{1,0:T(8,128)(2,1)S(1)}, u32[]{:S(2)}, u32[]{:S(2)}) collective-permute-start(bf16[128,256]{1,0:T(8,128)(2,1)S(1)} %get-tuple-element.26.grad_ref.refs_3_), channel_id=1, source_target_pairs={{0,16},{4,20},{8,24},{12,28},{16,0},{20,4},{24,8},{28,12},{1,17},{... | collective-permute-start | bytes 196616 | tf_op jit(solution)/shard_map/ppermute | solution.py:60
  26.0 4.3 %collective-permute-start.10 = (bf16[128,256]{1,0:T(8,128)(2,1)S(1)}, bf16[128,256]{1,0:T(8,128)(2,1)S(1)}, u32[]{:S(2)}, u32[]{:S(2)}) collective-permute-start(bf16[128,256]{1,0:T(8,128)(2,1)S(1)} %get-tuple-element.26.grad_ref.refs_3_), channel_id=1, source_target_pairs={{0,8},{4,12},{8,0},{12,4},{16,24},{20,28},{24,16},{28,20},{1,9},{5... | collective-permute-start | bytes 196616 | tf_op jit(solution)/shard_map/ppermute | solution.py:60
  27.5 6.1 %collective-permute-start.16 = (bf16[144,256]{1,0:T(8,128)(2,1)S(1)}, bf16[144,256]{1,0:T(8,128)(2,1)S(1)}, u32[]{:S(2)}, u32[]{:S(2)}) collective-permute-start(bf16[144,256]{1,0:T(8,128)(2,1)S(1)} %shard_map.129.refs_1_), channel_id=1, source_target_pairs={{0,2},{1,3},{2,0},{3,1},{4,6},{5,7},{6,4},{7,5},{8,10},{9,11},{10,... | collective-permute-start | bytes 221192 | tf_op jit(solution)/shard_map/ppermute | solution.py:75
  30.3 4.0 %collective-permute-start.11 = (bf16[512,256]{1,0:T(8,128)(2,1)S(1)}, bf16[512,256]{1,0:T(8,128)(2,1)S(1)}, u32[]{:S(2)}, u32[]{:S(2)}) collective-permute-start(bf16[512,256]{1,0:T(8,128)(2,1)S(1)} %shard_map.124.source_ref), channel_id=1, source_target_pairs={{0,4},{4,0},{8,12},{12,8},{16,20},{20,16},{24,28},{28,24},{1,5},{5... | collective-permute-start | bytes 786440 | tf_op jit(solution)/shard_map/ppermute | solution.py:65
  33.6 4.4 %collective-permute-start.17 = (bf16[144,256]{1,0:T(8,128)(2,1)S(1)}, bf16[144,256]{1,0:T(8,128)(2,1)S(1)}, u32[]{:S(2)}, u32[]{:S(2)}) collective-permute-start(bf16[144,256]{1,0:T(8,128)(2,1)S(1)} %shard_map.130.refs_1_), channel_id=1, source_target_pairs={{0,8},{4,12},{8,0},{12,4},{16,24},{20,28},{24,16},{28,20},{1,9},{5... | collective-permute-start | bytes 221192 | tf_op jit(solution)/shard_map/ppermute | solution.py:75
  34.6 6.4 %collective-permute-start.12 = (bf16[128,256]{1,0:T(8,128)(2,1)S(1)}, bf16[128,256]{1,0:T(8,128)(2,1)S(1)}, u32[]{:S(2)}, u32[]{:S(2)}) collective-permute-start(bf16[128,256]{1,0:T(8,128)(2,1)S(1)} %get-tuple-element.27), channel_id=1, source_target_pairs={{0,2},{1,3},{2,0},{3,1},{4,6},{5,7},{6,4},{7,5},{8,10},{9,11},{10,... | collective-permute-start | bytes 196616 | tf_op jit(solution)/shard_map/ppermute | solution.py:60
  36.2 6.2 %collective-permute-start.13 = (bf16[128,256]{1,0:T(8,128)(2,1)S(1)}, bf16[128,256]{1,0:T(8,128)(2,1)S(1)}, u32[]{:S(2)}, u32[]{:S(2)}) collective-permute-start(bf16[128,256]{1,0:T(8,128)(2,1)S(1)} %get-tuple-element.28), channel_id=1, source_target_pairs={{0,3},{1,2},{2,1},{3,0},{4,7},{5,6},{6,5},{7,4},{8,11},{9,10},{10,... | collective-permute-start | bytes 196616 | tf_op jit(solution)/shard_map/ppermute | solution.py:60
  38.1 4.4 %collective-permute-start.18 = (bf16[144,256]{1,0:T(8,128)(2,1)S(1)}, bf16[144,256]{1,0:T(8,128)(2,1)S(1)}, u32[]{:S(2)}, u32[]{:S(2)}) collective-permute-start(bf16[144,256]{1,0:T(8,128)(2,1)S(1)} %shard_map.131.refs_1_), channel_id=1, source_target_pairs={{0,16},{4,20},{8,24},{12,28},{16,0},{20,4},{24,8},{28,12},{1,17},{... | collective-permute-start | bytes 221192 | tf_op jit(solution)/shard_map/ppermute | solution.py:75
  39.7 4.3 %collective-permute-start.14 = (bf16[128,256]{1,0:T(8,128)(2,1)S(1)}, bf16[128,256]{1,0:T(8,128)(2,1)S(1)}, u32[]{:S(2)}, u32[]{:S(2)}) collective-permute-start(bf16[128,256]{1,0:T(8,128)(2,1)S(1)} %get-tuple-element.30), channel_id=1, source_target_pairs={{0,1},{1,0},{2,3},{3,2},{4,5},{5,4},{6,7},{7,6},{8,9},{9,8},{10,11... | collective-permute-start | bytes 196616 | tf_op jit(solution)/shard_map/ppermute | solution.py:60
  42.5 1.6 %collective-permute-start.19 = (f32[128,256]{1,0:T(8,128)S(1)}, f32[128,256]{1,0:T(8,128)S(1)}, u32[]{:S(2)}, u32[]{:S(2)}) collective-permute-start(f32[128,256]{1,0:T(8,128)S(1)} %get-tuple-element.31.own_ref), channel_id=1, source_target_pairs={{0,4},{4,0},{8,12},{12,8},{16,20},{20,16},{24,28},{28,24},{1,5},{5... | collective-permute-start | bytes 393224 | tf_op jit(solution)/shard_map/ppermute | solution.py:65
